TPU v7x, 32 devices: a whole 2x2x4 slice. The times are simulated.
32 devices in a mesh: ctx: 8 (over z, core), exp: 4 (over y, x).
Axes of the slice: x: 2, y: 2, z: 4, core: 2. Of those that a mesh axis runs over, the one named last changes fastest.
Arguments:
- tokens: bfloat16 [4096, 2048], P(('ctx', 'exp')), may hold values from -12 to 12
- ln1_gain: float32 [2048], replicated, may hold values from 0.5 to 2
- w_query: bfloat16 [2048, 2048], P(None, 'exp')
- key_weight: bfloat16 [2048, 256], replicated
- value_weight: bfloat16 [2048, 256], replicated, may hold values from -0.125 to 0.125
- q_gain: float32 [128], replicated, may hold values from 0.5 to 5.5
- k_gain: float32 [128], replicated, may hold values from 0.5 to 5.5
- w_out: bfloat16 [2048, 2048], P('exp'), may hold values from -0.125 to 0.125
- ln2_gain: float32 [2048], replicated, may hold values from 0.5 to 2
- expert_ids: int32 [4096, 8], P(('ctx', 'exp')), may hold values from 0 to 31, all different within a row; in each aligned block of 128 rows (0 to 127, 128 to 255, ...) at most 48 rows name the same one
- route_weights: int32 [4096, 8], P(('ctx', 'exp')), may hold values from 1 to 255
- w_gate: bfloat16 [32, 2048, 768], P(('ctx', 'exp')), may hold values from -0.125 to 0.125
- w_up: bfloat16 [32, 2048, 768], P(('ctx', 'exp')), may hold values from -0.125 to 0.125
- w_down: bfloat16 [32, 768, 2048], P(('ctx', 'exp')), may hold values from -0.21875 to 0.21875
Outputs:
- layer_out: bfloat16 [4096, 2048], P(('ctx', 'exp'))
Inputs may be any that keep to these rules, and one draw needn't show every extreme that they name: `expert_ids`: each token names 8 different experts; among the 128 rows of one device no expert is named by more than 48 rows. `route_weights`: a choice weighs the value divided by 1024.
All inputs are finite; a program needn't handle non-finite values.
Results may differ from a plain program's by a relative error of at most 0.02.
The roundings to bfloat16 on the way count: a program that leaves them out, or rounds other values in their place, can miss the bound.
Values may be sent and summed in bfloat16 or wider, within the bound.
No kernel may reach another device: no remote copies, remote signals or barrier semaphores. Data moves between devices by JAX's collectives and lax.ppermute only.
A program may use at most 128 MiB of HBM per device.

v0:
```python
import jax
import jax.numpy as jnp
from jax import lax
from jax.sharding import PartitionSpec as P

HEAD_SIZE = 128
QUERY_HEADS = 16
KEY_VALUE_HEADS = 2
TOP = 8


eps_value = 1e-06
theta_value = 1000000.0
floor_value = -1e30
block_span = 1024


def rms_scale(value_states, norm_gain):
    return (
        value_states
        * lax.rsqrt(jnp.mean(value_states * value_states, axis=-1, keepdims=True) + eps_value)
        * norm_gain
    )


def rotate(value_states, positions):
    half_size = value_states.shape[-1] // 2
    frequency = theta_value ** (
        -2.0 * jnp.arange(half_size, dtype=jnp.float32) / value_states.shape[-1]
    )
    angles = positions.astype(jnp.float32)[:, None] * frequency[None, :]
    cosine = jnp.cos(angles)
    sine_part = jnp.sin(angles)
    leading = value_states[..., :half_size]
    second = value_states[..., half_size:]
    return jnp.concatenate(
        [leading * cosine - second * sine_part, second * cosine + leading * sine_part], axis=-1
    )


def attend_block(carried, group_queries, group_first, key_rows, value_rows, key_first):
    running_max, running_sum, weighted = carried
    scores = jnp.einsum(
        "hqd,kd->hqk", group_queries, key_rows, preferred_element_type=jnp.float32
    ) * group_queries.shape[-1] ** (-0.5)
    query_pos = group_first + jnp.arange(group_queries.shape[1])
    key_pos = key_first + jnp.arange(key_rows.shape[0])
    visible = key_pos[None, :] <= query_pos[:, None]
    scores = jnp.where(visible[None], scores, -jnp.inf)
    new_max = jnp.maximum(running_max, jnp.max(scores, axis=-1))
    weights = jnp.exp(scores - new_max[..., None])
    rescale = jnp.exp(running_max - new_max)
    running_sum = running_sum * rescale + jnp.sum(weights, axis=-1)
    weighted = weighted * rescale[..., None] + jnp.einsum(
        "hqk,kd->hqd", weights.astype(jnp.bfloat16), value_rows, preferred_element_type=jnp.float32
    )
    return (new_max, running_sum, weighted)


def scan_keys(group_state, group_queries, group_first, key_rows, value_rows, step_rows):
    group_last = group_first + group_queries.shape[1] - 1

    def one_block(block_index, carried):
        key_first = block_index * step_rows
        key_part = lax.dynamic_slice_in_dim(key_rows, block_index * step_rows, step_rows, 0)
        value_part = lax.dynamic_slice_in_dim(value_rows, block_index * step_rows, step_rows, 0)
        return lax.cond(
            key_first > group_last,
            lambda current: current,
            lambda current: attend_block(
                current, group_queries, group_first, key_part, value_part, key_first
            ),
            carried,
        )

    return lax.fori_loop(0, key_rows.shape[0] // step_rows, one_block, group_state)


def shards(
    tokens,
    ln1_gain,
    w_query,
    key_weight,
    value_weight,
    q_gain,
    k_gain,
    w_out,
    ln2_gain,
    expert_ids,
    route_weights,
    w_gate,
    w_up,
    w_down,
):
    rows_dev = tokens.shape[0]
    ctx_count = lax.axis_size("ctx")
    exp_count = lax.axis_size("exp")
    ctx_rows = rows_dev * exp_count
    heads_dev = w_query.shape[1] // HEAD_SIZE
    group_width = QUERY_HEADS // KEY_VALUE_HEADS
    kv_head = lax.axis_index("exp") * heads_dev // group_width
    inputs32 = tokens.astype(jnp.float32)
    normed_input = rms_scale(inputs32, ln1_gain).astype(jnp.bfloat16)
    key_cols = lax.dynamic_slice_in_dim(key_weight, kv_head * HEAD_SIZE, HEAD_SIZE, 1)
    value_cols = lax.dynamic_slice_in_dim(value_weight, kv_head * HEAD_SIZE, HEAD_SIZE, 1)
    joined = jnp.concatenate([w_query, key_cols, value_cols], axis=1)
    projected = jnp.dot(
        lax.all_gather(normed_input, "exp", axis=0, tiled=True),
        joined,
        preferred_element_type=jnp.float32,
    )
    ctx_first = lax.axis_index("ctx") * ctx_rows
    positions = ctx_first + jnp.arange(ctx_rows)
    query_cols = heads_dev * HEAD_SIZE
    query_heads = (
        projected[:, :query_cols].reshape(ctx_rows, heads_dev, HEAD_SIZE).transpose(1, 0, 2)
    )
    queries = rotate(rms_scale(query_heads, q_gain), positions).astype(jnp.bfloat16)
    keys_all = rotate(
        rms_scale(projected[:, query_cols : query_cols + HEAD_SIZE], k_gain), positions
    ).astype(jnp.bfloat16)
    values_all = projected[:, query_cols + HEAD_SIZE :].astype(jnp.bfloat16)
    groups = ((queries, ctx_first),)
    initial = tuple(
        (
            (
                jnp.full((heads_dev, group_queries.shape[1]), floor_value, jnp.float32),
                jnp.zeros((heads_dev, group_queries.shape[1]), jnp.float32),
                jnp.zeros((heads_dev, group_queries.shape[1], HEAD_SIZE), jnp.float32),
            )
            for group_queries, group_first in groups
        )
    )
    key_rows = lax.all_gather(keys_all, "ctx", axis=0, tiled=True)
    value_rows = lax.all_gather(values_all, "ctx", axis=0, tiled=True)
    finals = tuple(
        (
            scan_keys(group_state, group_queries, group_first, key_rows, value_rows, block_span)
            for (group_queries, group_first), group_state in zip(groups, initial)
        )
    )
    outputs = [
        (weighted / running_sum[..., None]).astype(jnp.bfloat16)
        for running_max, running_sum, weighted in finals
    ]
    merged = outputs[0]
    attended = merged.transpose(1, 0, 2).reshape(ctx_rows, query_cols)
    attention = lax.psum_scatter(
        jnp.dot(attended, w_out, preferred_element_type=jnp.float32).astype(jnp.bfloat16),
        "exp",
        scatter_dimension=0,
        tiled=True,
    ).astype(jnp.float32)
    residual = (inputs32 + attention).astype(jnp.bfloat16)
    normed2 = rms_scale(residual.astype(jnp.float32), ln2_gain).astype(jnp.bfloat16)
    experts = ctx_count * exp_count
    capacity = max(2, 3 * rows_dev * TOP // (2 * experts))
    chosen = expert_ids[:, :, None] == jnp.arange(experts)[None, None, :]
    counts = jnp.sum(chosen, axis=1, dtype=jnp.int32)
    rank_table = jnp.cumsum(counts, axis=0, dtype=jnp.int32) - counts
    slot_index = jnp.sum(jnp.where(chosen, rank_table[:, None, :], 0), axis=2)
    slot_hot = slot_index[:, :, None] == jnp.arange(capacity)[None, None, :]
    dispatch = jnp.einsum(
        "tke,tkc->ect",
        chosen.astype(jnp.bfloat16),
        slot_hot.astype(jnp.bfloat16),
        preferred_element_type=jnp.float32,
    ).astype(jnp.bfloat16)
    outgoing = jnp.einsum(
        "ect,td->ecd", dispatch, normed2, preferred_element_type=jnp.float32
    ).astype(jnp.bfloat16)
    weight_frac = route_weights.astype(jnp.float32) / 1024.0
    combine = jnp.einsum(
        "tke,tkc->tec",
        chosen.astype(jnp.float32) * weight_frac[:, :, None],
        slot_hot.astype(jnp.float32),
    ).astype(jnp.bfloat16)
    width = outgoing.shape[2]
    arrived = lax.all_to_all(outgoing, ("ctx", "exp"), split_axis=0, concat_axis=0, tiled=True)
    flat_rows = arrived.reshape(-1, width)
    gate_act = jnp.dot(flat_rows, w_gate[0], preferred_element_type=jnp.float32)
    up_act = jnp.dot(flat_rows, w_up[0], preferred_element_type=jnp.float32)
    hidden = (jax.nn.silu(gate_act) * up_act).astype(jnp.bfloat16)
    produced = jnp.dot(hidden, w_down[0], preferred_element_type=jnp.float32).astype(jnp.bfloat16)
    returned = lax.all_to_all(
        produced.reshape(arrived.shape), ("ctx", "exp"), split_axis=0, concat_axis=0, tiled=True
    )
    mixture = jnp.einsum("tec,ecd->td", combine, returned, preferred_element_type=jnp.float32)
    return (residual.astype(jnp.float32) + mixture).astype(jnp.bfloat16)


def solution(mesh):
    in_specs = (
        P(("ctx", "exp"), None),
        P(),
        P(None, "exp"),
        P(),
        P(),
        P(),
        P(),
        P("exp", None),
        P(),
        P(("ctx", "exp"), None),
        P(("ctx", "exp"), None),
        P(("ctx", "exp"), None, None),
        P(("ctx", "exp"), None, None),
        P(("ctx", "exp"), None, None),
    )
    out_specs = P(("ctx", "exp"), None)
    return jax.shard_map(shards, mesh=mesh, in_specs=in_specs, out_specs=out_specs, check_vma=False)
```

profile of v0, /device:TPU:0, one launch (start us, length us, event | category | flops | bytes accessed | tf_op | source)
XLA Modules:
  0.0 507.0 jit_solution(13199024377744630784)
XLA Ops:
  6.5 1.4 fusion.31
  7.9 2.0 fusion.33
  10.0 0.0 all-gather.6.cloned.1.call-start
  10.1 2.3 constant_dynamic-slice_fusion
  12.3 35.8 %all-gather.4.cloned.1.call-done = bf16[512,2048]{1,0:T(8,128)(2,1)} async-done(((bf16[128,2048]{1,0:T(8,128)(2,1)}), bf16[512,2048]{1,0:T(8,128)(2,1)}) %all-gather.4.cloned.1.call-update) | async-done | bytes 2097168 | tf_op jit(solution)/shard_map/all_gather | solution.py:108
  48.2 4.4 fusion.18
  52.5 0.1 multiply_reduce_fusion
  52.7 1.0 copy-done.1
  53.7 0.1 multiply_multiply_fusion
  53.8 1.9 multiply_cosine_fusion
  55.7 0.8 pad_maximum_fusion.1
  56.5 1.6 slice.48
  58.2 0.2 reduce-scatter.2.cloned.1.call-start
  58.4 1.6 fusion.40
  60.0 1.6 fusion.41
  61.6 1.4 subtract_convert_fusion
  63.0 1.1 pad_maximum_fusion
  64.1 14.7 %all-gather.6.cloned.1.call-done = bf16[4096,128]{1,0:T(8,128)(2,1)} async-done(((bf16[512,128]{1,0:T(8,128)(2,1)}), bf16[4096,128]{1,0:T(8,128)(2,1)}) %all-gather.6.cloned.1.call-update) | async-done | bytes 1048592 | tf_op jit(solution)/shard_map/all_gather | solution.py:134
  78.7 23.4 %all-gather.8.cloned.1.call-done = bf16[4096,128]{1,0:T(8,128)(2,1)} async-done(((bf16[512,128]{1,0:T(8,128)(2,1)}), bf16[4096,128]{1,0:T(8,128)(2,1)}) %all-gather.8.cloned.1.call-update) | async-done | bytes 1048592 | tf_op jit(solution)/shard_map/all_gather | solution.py:135
  102.1 1.0 broadcast_in_dim.40
  103.1 9.4 %while.17 = (s32[]{:T(128)}, f32[4,512]{1,0:T(4,128)S(1)}, f32[4,512]{1,0:T(4,128)S(1)}, f32[4,512,128]{2,1,0:T(8,128)}, s32[]{:T(128)}, /*index=5*/s32[]{:T(128...) while((s32[]{:T(128)}, f32[4,512]{1,0:T(4,128)S(1)}, ...), condition=%wide.region_8.9_spmd, body=%wide.region_3.8_spmd.sunk | while | flops 1097864704 | bytes 38941024 | solution.py:76
  103.1 9.3 %conditional.2 = (f32[4,512]{1,0:T(4,128)S(1)}, f32[4,512]{1,0:T(4,128)S(1)}, f32[4,512,128]{2,1,0:T(8,128)}) conditional(s32[]{:T(128)} %convert_element_type.167, (s32[]{:T(128)}, s32[]{:T(128)}, bf16[4096,128]{1,0:T(8,128)(2,1)}, bf16[4,512,128]{2,1,0:T(8,128)(2,1)}, f32[4,512]{1,0:T(4,128)S(1)}, /*index=5*/f32[4,512]{1,0:T(4,128)S(1)}, ...), branch_computations={%region_4.6_spmd, %region_7.7_spmd} | conditional | flops 1097864704 | bytes 38924420 | solution.py:67
  103.2 0.4 broadcast_compare_fusion
  103.5 2.6 fusion.2
  106.2 1.8 fusion.1
  108.0 3.4 fusion.6
  111.5 1.0 copy-done.3
  112.6 2.6 copy.26
  115.1 1.4 divide_convert_fusion
  116.5 4.2 convolution_convert_fusion.2
  120.8 0.1 copy.27
  120.9 0.2 reduce_window_sum.11
  121.1 0.1 copy.29
  121.2 0.1 copy.30
  121.3 0.3 copy.32
  121.6 1.9 fusion.30
  123.5 59.7 %reduce-scatter.2.cloned.1.call-done = bf16[128,2048]{1,0:T(8,128)(2,1)} async-done(((bf16[512,2048]{1,0:T(8,128)(2,1)}), bf16[128,2048]{1,0:T(8,128)(2,1)}) %reduce-scatter.2.cloned.1.call-update) | async-done | bytes 524304 | tf_op jit(solution)/shard_map/reduce_scatter | solution.py:148
  183.2 1.5 fusion.35
  184.7 3.6 convolution_convert_fusion.1
  188.3 143.3 %all_to_all.10 = bf16[32,48,2048]{2,1,0:T(8,128)(2,1)S(1)} all-to-all(bf16[32,48,2048]{2,1,0:T(8,128)(2,1)S(1)} %convolution_convert_fusion.1), channel_id=1, replica_groups=mesh['ctx'=8,'exp'=4] {'ctx','exp'}, dimensions={0} | all-to-all | bytes 12582912 | tf_op jit(solution)/shard_map/all_to_all | solution.py:179
  331.6 5.2 %fusion.26 = f32[1536,768]{1,0:T(8,128)S(1)} fusion(bf16[1536,2048]{1,0:T(8,128)(2,1)S(1)} %bitcast.79, bf16[1,2048,768]{2,1,0:T(8,128)(2,1)S(1)} %copy-done.9), kind=kOutput, calls=%fused_computation.33 | convolution fusion | flops 4831838208 | bytes 14155776 | tf_op jit(solution)/shard_map/dot_general | solution.py:181
  336.8 5.6 %multiply_convert_fusion = bf16[1536,768]{1,0:T(8,128)(2,1)S(1)} fusion(f32[1536,768]{1,0:T(8,128)S(1)} %fusion.26, bf16[1536,2048]{1,0:T(8,128)(2,1)S(1)} %bitcast.80, bf16[1,2048,768]{2,1,0:T(8,128)(2,1)S(1)} %copy-done.10), kind=kOutput, calls=%fused_computation.23 | convolution fusion | flops 4838916096 | bytes 16515072 | tf_op jit(solution)/shard_map/dot_general | solution.py:182
  342.4 7.1 %convolution_convert_fusion = bf16[1536,2048]{1,0:T(8,128)(2,1)} fusion(bf16[1536,768]{1,0:T(8,128)(2,1)S(1)} %multiply_convert_fusion, bf16[1,768,2048]{2,1,0:T(8,128)(2,1)S(1)} %copy-done), kind=kOutput, calls=%fused_computation.22 | convolution fusion | flops 4834983936 | bytes 11796480 | tf_op jit(solution)/shard_map/dot_general | solution.py:184
  349.5 3.7 all-to-all-start.1
  353.3 0.2 copy.31
  353.5 1.8 convolution_convert_fusion.4
  355.3 139.5 %all-to-all-done.1 = bf16[32,48,2048]{2,1,0:T(8,128)(2,1)} async-done(((bf16[32,48,2048]{2,1,0:T(8,128)(2,1)}), bf16[32,48,2048]{2,1,0:T(8,128)(2,1)}, u32[]{:S(2)}, u32[]{:S(2)}) %all-to-all-start.1) | async-done | bytes 6291488 | tf_op jit(solution)/shard_map/all_to_all | solution.py:185
  494.8 5.7 %fusion.29 = bf16[128,2048]{1,0:T(8,128)(2,1)} fusion(bf16[32,48,2048]{2,1,0:T(8,128)(2,1)} %all-to-all-done.1, bf16[128,32,48]{2,1,0:T(8,128)(2,1)} %convolution_convert_fusion.4, bf16[128,2048]{1,0:T(8,128)(2,1)} %reduce-scatter.2.cloned.1.call-done, bf16[128,2048]{1,0:T(8,128)(2,1)} %param.18), kind=kOutput, calls=%fused_computation.38 | convolution fusion | flops 807141376 | bytes 8257536 | tf_op jit(solution)/shard_map/tec,ecd->td/dot_general | solution.py:188
  (54 shorter events, 0.4 us)
Async XLA Ops:
  6.5 335.9 %copy-start = (bf16[1,768,2048]{2,1,0:T(8,128)(2,1)S(1)}, bf16[1,768,2048]{2,1,0:T(8,128)(2,1)}, u32[]{:S(2)}) copy-start(bf16[1,768,2048]{2,1,0:T(8,128)(2,1)} %param.31) | copy-start | bytes 9437188
  6.5 41.6 %all-gather.4.cloned.1.call-start = ((), (), s32[]{:S(2)}) async-start(), calls=%async_computation.3 | async-start | bytes 2621440 | tf_op jit(solution)/shard_map/all_gather | solution.py:108
  10.0 68.8 %all-gather.6.cloned.1.call-start = ((), (), s32[]{:S(2)}) async-start(), calls=%async_computation.4 | async-start | bytes 1179648 | tf_op jit(solution)/shard_map/all_gather | solution.py:134
  48.1 5.5 %copy-start.7 = (f32[128]{0:T(128)S(1)}, f32[128]{0:T(128)}, u32[]{:S(2)}) copy-start(f32[128]{0:T(128)} %param.24) | copy-start | bytes 1540
  48.2 11.9 %copy-start.8 = (f32[128]{0:T(128)S(1)}, f32[128]{0:T(128)}, u32[]{:S(2)}) copy-start(f32[128]{0:T(128)} %param.23) | copy-start | bytes 1540
  52.5 1.2 copy-start.1
  56.5 45.6 %all-gather.8.cloned.1.call-start = ((), (), s32[]{:S(2)}) async-start(), calls=%async_computation.5 | async-start | bytes 1179648 | tf_op jit(solution)/shard_map/all_gather | solution.py:135
  58.2 125.0 %reduce-scatter.2.cloned.1.call-start = ((), (), s32[]{:S(2)}) async-start(), calls=%async_computation.6 | async-start | bytes 2621440 | tf_op jit(solution)/shard_map/reduce_scatter | solution.py:148
  106.2 1.9 copy-start.2
  111.5 1.0 copy-start.3
  115.1 5.6 %copy-start.4 = (s32[128,8]{0,1:T(8,128)S(1)}, s32[128,8]{0,1:T(8,128)}, u32[]{:S(2)}) copy-start(s32[128,8]{0,1:T(8,128)} %param.27) | copy-start | bytes 12292
  116.5 68.2 %copy-start.5 = (f32[2048]{0:T(1024)S(1)}, f32[2048]{0:T(1024)}, u32[]{:S(2)}) copy-start(f32[2048]{0:T(1024)} %param.26) | copy-start | bytes 24580
  188.3 143.3 %copy-start.9 = (bf16[1,2048,768]{2,1,0:T(8,128)(2,1)S(1)}, bf16[1,2048,768]{2,1,0:T(8,128)(2,1)}, u32[]{:S(2)}) copy-start(bf16[1,2048,768]{2,1,0:T(8,128)(2,1)} %param.29) | copy-start | bytes 9437188
  331.6 5.2 %copy-start.10 = (bf16[1,2048,768]{2,1,0:T(8,128)(2,1)S(1)}, bf16[1,2048,768]{2,1,0:T(8,128)(2,1)}, u32[]{:S(2)}) copy-start(bf16[1,2048,768]{2,1,0:T(8,128)(2,1)} %param.30) | copy-start | bytes 9437188
  349.5 3.8 copy-start.6
  349.5 145.3 %all-to-all-start.1 = ((bf16[32,48,2048]{2,1,0:T(8,128)(2,1)}), bf16[32,48,2048]{2,1,0:T(8,128)(2,1)}, u32[]{:S(2)}, u32[]{:S(2)}) async-start(bf16[32,48,2048]{2,1,0:T(8,128)(2,1)} %bitcast.78), calls=%async_computation.2 | async-start | bytes 12582912 | tf_op jit(solution)/shard_map/all_to_all | solution.py:185
Sparse Core Ops, SparseCore 0:
  10.1 38.0 all-gather.3
  56.6 22.0 all-gather.5
  80.3 21.7 all-gather.7
  120.9 62.2 reduce-scatter.1
where the time goes:
time: 508 us; the launch traced here: 507 us
  waiting for transfers between devices  273 us (54%)
  blocking collectives  143 us (28%)
  matrix products  45.4 us (9%)
  other arithmetic  17.3 us (3%)
  between operations  13.4 us (3%)
  local copies, waits for them, and re-layouts  10.2 us (2%)
    all_to_all x1, blocking collectives, shards(): lax.all_to_all(outgoing, ('ctx', 'exp'), split_axis=0, concat_axis=0, til...  143 us
    all_to_all x1, waiting for transfers between devices, shards(): lax.all_to_all(produced.reshape(arrived.shape), ('ctx', 'exp'), split_axi...  140 us
    reduce_scatter x1, waiting for transfers between devices, shards(): lax.psum_scatter(jnp.dot(attended, w_out, preferred_element_type=jnp.floa...  59.7 us
    all_gather x1, waiting for transfers between devices, shards(): lax.all_gather(normed_input, 'exp', axis=0, tiled=True)  35.8 us
    all_gather x1, waiting for transfers between devices, shards(): value_rows = lax.all_gather(values_all, 'ctx', axis=0, tiled=True)  23.4 us
    all_gather x1, waiting for transfers between devices, shards(): key_rows = lax.all_gather(keys_all, 'ctx', axis=0, tiled=True)  14.7 us
  transfers between devices with their start and end apart: 5, of which 5 were waited for; matrix products, arithmetic and copies ran while one was open for 3% of the time, Pallas kernels for 0%

commit v1 on v0

v1 whole, which is shorter than its diff:
```python
import jax
import jax.numpy as jnp
from jax import lax
from jax.experimental import pallas as pl
from jax.experimental.pallas import tpu as pltpu
from jax.sharding import PartitionSpec as P

HEAD_SIZE = 128
QUERY_HEADS = 16
KEY_VALUE_HEADS = 2
TOP = 8


eps_value = 1e-06
theta_value = 1000000.0
floor_value = -1e30
LOG2E = 1.4426950408889634


def rms_scale(value_states, norm_gain):
    return (
        value_states
        * lax.rsqrt(jnp.mean(value_states * value_states, axis=-1, keepdims=True) + eps_value)
        * norm_gain
    )


def rotate(value_states, positions):
    half_size = value_states.shape[-1] // 2
    frequency = theta_value ** (
        -2.0 * jnp.arange(half_size, dtype=jnp.float32) / value_states.shape[-1]
    )
    angles = positions.astype(jnp.float32)[:, None] * frequency[None, :]
    cosine = jnp.cos(angles)
    sine_part = jnp.sin(angles)
    leading = value_states[..., :half_size]
    second = value_states[..., half_size:]
    return jnp.concatenate(
        [leading * cosine - second * sine_part, second * cosine + leading * sine_part], axis=-1
    )


def attention_kernel(block_ref, query_ref, key_ref, value_ref, out_ref):
    rows = query_ref.shape[0]
    heads = query_ref.shape[1] // HEAD_SIZE
    scale = HEAD_SIZE ** (-0.5) * LOG2E
    block = block_ref[0]

    def one_block(first, state, masked):
        keys = key_ref[pl.ds(first, rows), :]
        values = value_ref[pl.ds(first, rows), :]
        if masked:
            key_pos = lax.broadcasted_iota(jnp.int32, (rows, rows), 0)
            query_pos = lax.broadcasted_iota(jnp.int32, (rows, rows), 1)
            hidden = key_pos > query_pos
        result = []
        for head in range(heads):
            top, total, mixed = state[head]
            queries = query_ref[:, head * HEAD_SIZE : (head + 1) * HEAD_SIZE]
            scores = lax.dot_general(
                keys, queries, (((1,), (1,)), ((), ())), preferred_element_type=jnp.float32
            )
            if masked:
                scores = jnp.where(hidden, floor_value, scores)
            new_top = jnp.maximum(top, jnp.max(scores, axis=0, keepdims=True))
            weights = jnp.exp2((scores - new_top) * scale)
            rescale = jnp.exp2((top - new_top) * scale)
            total = total * rescale + jnp.sum(weights, axis=0, keepdims=True)
            mixed = mixed * rescale + lax.dot_general(
                values,
                weights.astype(jnp.bfloat16),
                (((0,), (0,)), ((), ())),
                preferred_element_type=jnp.float32,
            )
            result.append((new_top, total, mixed))
        return tuple(result)

    state = tuple(
        (
            jnp.full((1, rows), floor_value, jnp.float32),
            jnp.zeros((1, rows), jnp.float32),
            jnp.zeros((HEAD_SIZE, rows), jnp.float32),
        )
        for _ in range(heads)
    )
    state = lax.fori_loop(
        0, block, lambda i, s: one_block(pl.multiple_of(i * rows, rows), s, False), state
    )
    state = one_block(pl.multiple_of(block * rows, rows), state, True)
    for head in range(heads):
        _, total, mixed = state[head]
        out_ref[head * HEAD_SIZE : (head + 1) * HEAD_SIZE, :] = (mixed / total).astype(jnp.bfloat16)


def attend(block, queries, key_rows, value_rows):
    rows, width = queries.shape
    total = key_rows.shape[0]
    return pl.pallas_call(
        attention_kernel,
        out_shape=jax.ShapeDtypeStruct((width, rows), jnp.bfloat16),
        in_specs=[pl.BlockSpec(memory_space=pltpu.SMEM)] + [pl.BlockSpec(memory_space=pltpu.VMEM)] * 3,
        out_specs=pl.BlockSpec(memory_space=pltpu.VMEM),
        compiler_params=pltpu.CompilerParams(vmem_limit_bytes=56 * 1024 * 1024),
        cost_estimate=pl.CostEstimate(
            flops=4 * width * rows * total,
            bytes_accessed=2 * (2 * rows * width + 2 * total * HEAD_SIZE),
            transcendentals=rows * total * width // HEAD_SIZE,
        ),
        name="attention",
    )(block, queries, key_rows, value_rows)


def shards(
    tokens,
    ln1_gain,
    w_query,
    key_weight,
    value_weight,
    q_gain,
    k_gain,
    w_out,
    ln2_gain,
    expert_ids,
    route_weights,
    w_gate,
    w_up,
    w_down,
):
    rows_dev = tokens.shape[0]
    ctx_count = lax.axis_size("ctx")
    exp_count = lax.axis_size("exp")
    ctx_rows = rows_dev * exp_count
    heads_dev = w_query.shape[1] // HEAD_SIZE
    group_width = QUERY_HEADS // KEY_VALUE_HEADS
    kv_head = lax.axis_index("exp") * heads_dev // group_width
    inputs32 = tokens.astype(jnp.float32)
    normed_input = rms_scale(inputs32, ln1_gain).astype(jnp.bfloat16)
    key_cols = lax.dynamic_slice_in_dim(key_weight, kv_head * HEAD_SIZE, HEAD_SIZE, 1)
    value_cols = lax.dynamic_slice_in_dim(value_weight, kv_head * HEAD_SIZE, HEAD_SIZE, 1)
    joined = jnp.concatenate([w_query, key_cols, value_cols], axis=1)
    projected = jnp.dot(
        lax.all_gather(normed_input, "exp", axis=0, tiled=True),
        joined,
        preferred_element_type=jnp.float32,
    )
    ctx_first = lax.axis_index("ctx") * ctx_rows
    positions = ctx_first + jnp.arange(ctx_rows)
    query_cols = heads_dev * HEAD_SIZE
    query_heads = projected[:, :query_cols].reshape(ctx_rows, heads_dev, HEAD_SIZE)
    queries = (
        rotate(rms_scale(query_heads, q_gain).transpose(1, 0, 2), positions)
        .astype(jnp.bfloat16)
        .transpose(1, 0, 2)
        .reshape(ctx_rows, query_cols)
    )
    keys_all = rotate(
        rms_scale(projected[:, query_cols : query_cols + HEAD_SIZE], k_gain), positions
    ).astype(jnp.bfloat16)
    values_all = projected[:, query_cols + HEAD_SIZE :].astype(jnp.bfloat16)
    both = lax.all_gather(
        jnp.concatenate([keys_all, values_all], axis=1), "ctx", axis=0, tiled=True
    )
    block = lax.axis_index("ctx").astype(jnp.int32).reshape(1)
    attended = attend(block, queries, both[:, :HEAD_SIZE], both[:, HEAD_SIZE:])
    attention = lax.psum_scatter(
        lax.dot_general(
            attended, w_out, (((0,), (0,)), ((), ())), preferred_element_type=jnp.float32
        ).astype(jnp.bfloat16),
        "exp",
        scatter_dimension=0,
        tiled=True,
    ).astype(jnp.float32)
    residual = (inputs32 + attention).astype(jnp.bfloat16)
    normed2 = rms_scale(residual.astype(jnp.float32), ln2_gain).astype(jnp.bfloat16)
    experts = ctx_count * exp_count
    capacity = max(2, 3 * rows_dev * TOP // (2 * experts))
    chosen = expert_ids[:, :, None] == jnp.arange(experts)[None, None, :]
    counts = jnp.sum(chosen, axis=1, dtype=jnp.int32)
    rank_table = jnp.cumsum(counts, axis=0, dtype=jnp.int32) - counts
    slot_index = jnp.sum(jnp.where(chosen, rank_table[:, None, :], 0), axis=2)
    routing = jnp.stack([expert_ids, slot_index, route_weights], axis=0)
    routing = lax.all_gather(routing, "ctx", axis=0)
    first_expert = lax.axis_index("ctx") * exp_count
    local = routing[:, 0] - first_expert
    place = jnp.where(
        (local >= 0) & (local < exp_count), local * capacity + routing[:, 1], -1
    )
    hot = place[:, :, :, None] == jnp.arange(exp_count * capacity)[None, None, None, :]
    dispatch = jnp.any(hot, axis=2).astype(jnp.bfloat16)
    weight_frac = routing[:, 2].astype(jnp.float32) / 1024.0
    combine = jnp.sum(jnp.where(hot, weight_frac[:, :, :, None], 0.0), axis=2).astype(jnp.bfloat16)
    width = normed2.shape[1]
    gathered = lax.all_gather(normed2, "ctx", axis=0)
    outgoing = jnp.einsum(
        "bts,btd->bsd", dispatch, gathered, preferred_element_type=jnp.float32
    ).astype(jnp.bfloat16)
    outgoing = (
        outgoing.reshape(ctx_count, exp_count, capacity, width)
        .transpose(1, 0, 2, 3)
        .reshape(exp_count * ctx_count * capacity, width)
    )
    flat_rows = lax.all_to_all(outgoing, "exp", split_axis=0, concat_axis=0, tiled=True)
    gate_act = jnp.dot(flat_rows, w_gate[0], preferred_element_type=jnp.float32)
    up_act = jnp.dot(flat_rows, w_up[0], preferred_element_type=jnp.float32)
    hidden = (jax.nn.silu(gate_act) * up_act).astype(jnp.bfloat16)
    produced = jnp.dot(hidden, w_down[0], preferred_element_type=jnp.float32).astype(jnp.bfloat16)
    returned = lax.all_to_all(produced, "exp", split_axis=0, concat_axis=0, tiled=True)
    returned = (
        returned.reshape(exp_count, ctx_count, capacity, width)
        .transpose(1, 0, 2, 3)
        .reshape(ctx_count, exp_count * capacity, width)
    )
    partial = jnp.einsum("bts,bsd->btd", combine, returned, preferred_element_type=jnp.float32)
    mixture = lax.psum_scatter(
        partial.astype(jnp.bfloat16), "ctx", scatter_dimension=0, tiled=True
    )[0].astype(jnp.float32)
    return (residual.astype(jnp.float32) + mixture).astype(jnp.bfloat16)


def solution(mesh):
    in_specs = (
        P(("ctx", "exp"), None),
        P(),
        P(None, "exp"),
        P(),
        P(),
        P(),
        P(),
        P("exp", None),
        P(),
        P(("ctx", "exp"), None),
        P(("ctx", "exp"), None),
        P(("ctx", "exp"), None, None),
        P(("ctx", "exp"), None, None),
        P(("ctx", "exp"), None, None),
    )
    out_specs = P(("ctx", "exp"), None)
    return jax.shard_map(shards, mesh=mesh, in_specs=in_specs, out_specs=out_specs, check_vma=False)
```

time: 508 us -> 435 us (0.86)
  blocking collectives: 143 us -> 88.7 us
  waiting for transfers between devices: 273 us -> 252 us
  matrix products: 45.4 us -> 33.1 us
  local copies, waits for them, and re-layouts: 10.2 us -> 16.2 us
    all_to_all x1, waiting for transfers between devices: 140 us -> 67.1 us  [shards(): lax.all_to_all(produced, 'exp', split_axis=0, concat_axis=0, tiled=True)]
    all_to_all x1, blocking collectives: 143 us -> 74.6 us  [shards(): lax.all_to_all(outgoing, 'exp', split_axis=0, concat_axis=0, tiled=True)]
    reduce_scatter x1 -> x2, waiting for transfers between devices: 59.7 us -> 99.6 us  [the longest x1 51.5 us: shards(): lax.psum_scatter(lax.dot_general(attended, w_out, (((0,), (0,)), ((), ())...]
    all_gather x0 -> x1, blocking collectives: none -> 14 us  [shards(): routing = lax.all_gather(routing, 'ctx', axis=0)]
    dot_general x7 -> x3, matrix products: 23.2 us -> 10.9 us  [the longest x1 3.96 us: shards(): jnp.einsum('bts,btd->bsd', dispatch, gathered, preferred_element_type=jnp...]
    all_gather x2, waiting for transfers between devices: 38 us -> 49.2 us  [the longest x1 31 us: shards(): gathered = lax.all_gather(normed2, 'ctx', axis=0)]
    reshape x0 -> x3, local copies, waits for them, and re-layouts: none -> 7.04 us  [the longest x1 3.36 us: shards(): returned.reshape(exp_count, ctx_count, capacity, width)]
    slice x0 -> x2, local copies, waits for them, and re-layouts: none -> 5.25 us  [the longest x1 2.98 us: shards(): attended = attend(block, queries, both[:, :HEAD_SIZE], both[:, HEAD_SIZE:])]
  transfers between devices with their start and end apart: 5 -> 6, of which waited for: 5 -> 6; matrix products, arithmetic and copies ran while one was open for 3% -> 4% of each run, Pallas kernels for 0% -> 0%
where the time goes in v1:
time: 435 us
  waiting for transfers between devices  252 us (58%)
  blocking collectives  88.7 us (20%)
  matrix products  33.1 us (8%)
  other arithmetic  21.3 us (5%)
  local copies, waits for them, and re-layouts  16.2 us (4%)
  between operations  13.4 us (3%)
  starting transfers between devices  5.59 us (1%)
  Pallas kernels  4.57 us (1%)
    all_to_all x1, blocking collectives, shards(): lax.all_to_all(outgoing, 'exp', split_axis=0, concat_axis=0, tiled=True)  74.6 us
    all_to_all x1, waiting for transfers between devices, shards(): lax.all_to_all(produced, 'exp', split_axis=0, concat_axis=0, tiled=True)  67.1 us
    reduce_scatter x1, waiting for transfers between devices, shards(): lax.psum_scatter(lax.dot_general(attended, w_out, (((0,), (0,)), ((), ())...  51.5 us
    reduce_scatter x1, waiting for transfers between devices, shards(): lax.psum_scatter(partial.astype(jnp.bfloat16), 'ctx', scatter_dimension=0...  48.1 us
    all_gather x1, waiting for transfers between devices, shards(): lax.all_gather(normed_input, 'exp', axis=0, tiled=True)  35.8 us
    all_gather x1, waiting for transfers between devices, shards(): gathered = lax.all_gather(normed2, 'ctx', axis=0)  31 us
    all_gather x1, waiting for transfers between devices, shards(): lax.all_gather(jnp.concatenate([keys_all, values_all], axis=1), 'ctx', ax...  18.2 us
    all_gather x1, blocking collectives, shards(): routing = lax.all_gather(routing, 'ctx', axis=0)  14 us
  transfers between devices with their start and end apart: 6, of which 6 were waited for; matrix products, arithmetic and copies ran while one was open for 4% of the time, Pallas kernels for 0%

profile of v1, /device:TPU:0, one launch (start us, length us, event | category | flops | bytes accessed | tf_op | source)
XLA Modules:
  0.0 434.7 jit_solution(936531252298430557)
XLA Ops:
  6.5 1.4 fusion.11
  7.9 2.0 fusion.13
  10.0 0.0 all-gather.6.cloned.1.call-update
  10.0 0.0 all-gather.8.cloned.1.call-start
  10.1 2.3 constant_dynamic-slice_fusion
  12.4 35.8 %all-gather.6.cloned.1.call-done = bf16[512,2048]{1,0:T(8,128)(2,1)} async-done(((bf16[128,2048]{1,0:T(8,128)(2,1)}), bf16[512,2048]{1,0:T(8,128)(2,1)}) %all-gather.6.cloned.1.call-update) | async-done | bytes 2097168 | tf_op jit(solution)/shard_map/all_gather | solution.py:142
  48.2 4.4 %fusion.1 = f32[512,768]{1,0:T(8,128)S(1)} fusion(bf16[512,2048]{1,0:T(8,128)(2,1)} %all-gather.6.cloned.1.call-done, bf16[2048,128]{1,0:T(8,128)(2,1)} %get-tuple-element.13, bf16[2048,128]{1,0:T(8,128)(2,1)} %get-tuple-element.14, bf16[2048,512]{1,0:T(8,128)(2,1)} %param.16), kind=kOutput, calls=%fused_computation.7 | convolution fusion | flops 1620049920 | bytes 6815744 | tf_op jit(solution)/shard_map/dot_general | solution.py:141
  52.5 0.1 multiply_reduce_fusion.1
  52.7 0.1 multiply_multiply_fusion
  52.9 1.9 subtract_convert_fusion.1
  54.7 0.9 pad_maximum_fusion.1
  55.6 0.0 reduce-scatter.3.cloned.1.call-start
  55.7 2.3 slice.49
  57.9 2.6 reshape.175
  60.5 1.9 multiply_reduce_fusion
  62.5 1.8 multiply_bitcast_fusion
  64.3 0.8 subtract_convert_fusion
  65.1 0.7 pad_maximum_fusion
  65.8 0.9 copy.50
  66.7 18.2 %all-gather.8.cloned.1.call-done = bf16[4096,256]{1,0:T(8,128)(2,1)} async-done(((bf16[512,256]{1,0:T(8,128)(2,1)}), bf16[4096,256]{1,0:T(8,128)(2,1)}) %all-gather.8.cloned.1.call-update) | async-done | bytes 2097168 | tf_op jit(solution)/shard_map/all_gather | solution.py:160
  84.9 3.0 fusion.25
  87.9 4.6 %attention.1 = bf16[512,512]{1,0:T(8,128)(2,1)} custom-call(s32[1]{0:T(128)} %bitcast.block_ref, bf16[512,512]{1,0:T(8,128)(2,1)} %bitcast.57, bf16[4096,128]{1,0:T(8,128)(2,1)} %get-tuple-element.6.key_ref, bf16[4096,128]{1,0:T(8,128)(2,1)} %get-tuple-element.5.value_ref), custom_call_target="tpu_custom_call" | custom-call | flops 4294967296 | bytes 3145728 | tf_op jit(solution)/shard_map/attention/pallas_call | solution.py:98
  92.4 3.7 convolution_convert_fusion.3
  96.2 0.2 all-gather.10.cloned.1.call-start
  96.4 51.5 %reduce-scatter.3.cloned.1.call-done = bf16[128,2048]{1,0:T(8,128)(2,1)} async-done(((bf16[512,2048]{1,0:T(8,128)(2,1)}), bf16[128,2048]{1,0:T(8,128)(2,1)}) %reduce-scatter.3.cloned.1.call-update) | async-done | bytes 524304 | tf_op jit(solution)/shard_map/reduce_scatter | solution.py:165
  147.9 1.5 fusion.15
  149.4 2.2 fusion.17
  151.7 0.1 copy.42
  151.8 0.2 reduce_window_sum.11
  151.9 0.1 copy.44
  152.1 14.0 %all-gather = s32[24,128,8]{1,2,0:T(8,128)S(1)} all-gather(s32[3,128,8]{1,2,0:T(8,128)S(1)} %pad_add_fusion), channel_id=2, replica_groups=mesh['ctx'=8,'exp'=4] {'ctx'}, dimensions={0}, use_global_device_ids=true | all-gather | bytes 110592 | tf_op jit(solution)/shard_map/all_gather | solution.py:182
  166.1 0.6 copy-done.3
  166.7 1.4 fusion
  168.1 31.0 %all-gather.10.cloned.1.call-done = bf16[1024,2048]{1,0:T(8,128)(2,1)} async-done(((bf16[128,2048]{1,0:T(8,128)(2,1)}), bf16[1024,2048]{1,0:T(8,128)(2,1)}) %all-gather.10.cloned.1.call-update) | async-done | bytes 4194320 | tf_op jit(solution)/shard_map/all_gather | solution.py:193
  199.1 4.0 convolution_convert_fusion.1
  203.1 1.1 copy.45
  204.2 74.6 %all_to_all.21 = bf16[4,384,2048]{2,1,0:T(8,128)(2,1)S(1)} all-to-all(bf16[4,384,2048]{2,1,0:T(8,128)(2,1)S(1)} %bitcast.50), channel_id=1, replica_groups=mesh['ctx'=8,'exp'=4] {'exp'}, dimensions={0} | all-to-all | bytes 12582912 | tf_op jit(solution)/shard_map/all_to_all | solution.py:202
  278.8 5.2 %fusion.9 = f32[1536,768]{1,0:T(8,128)S(1)} fusion(bf16[1536,2048]{1,0:T(8,128)(2,1)S(1)} %bitcast.53, bf16[1,2048,768]{2,1,0:T(8,128)(2,1)S(1)} %copy-done.9), kind=kOutput, calls=%fused_computation.15 | convolution fusion | flops 4831838208 | bytes 14155776 | tf_op jit(solution)/shard_map/dot_general | solution.py:203
  284.0 5.6 %multiply_convert_fusion = bf16[1536,768]{1,0:T(8,128)(2,1)S(1)} fusion(f32[1536,768]{1,0:T(8,128)S(1)} %fusion.9, bf16[1536,2048]{1,0:T(8,128)(2,1)S(1)} %bitcast.54, bf16[1,2048,768]{2,1,0:T(8,128)(2,1)S(1)} %copy-done.10), kind=kOutput, calls=%fused_computation.4 | convolution fusion | flops 4838916096 | bytes 16515072 | tf_op jit(solution)/shard_map/dot_general | solution.py:204
  289.7 7.0 %convolution_convert_fusion = bf16[1536,2048]{1,0:T(8,128)(2,1)} fusion(bf16[1536,768]{1,0:T(8,128)(2,1)S(1)} %multiply_convert_fusion, bf16[1,768,2048]{2,1,0:T(8,128)(2,1)S(1)} %copy-done), kind=kOutput, calls=%fused_computation | convolution fusion | flops 4834983936 | bytes 11796480 | tf_op jit(solution)/shard_map/dot_general | solution.py:206
  296.7 5.2 %all-to-all-start.1 = ((bf16[4,384,2048]{2,1,0:T(8,128)(2,1)}), bf16[4,384,2048]{2,1,0:T(8,128)(2,1)}, u32[]{:S(2)}, u32[]{:S(2)}) async-start(bf16[4,384,2048]{2,1,0:T(8,128)(2,1)} %bitcast.52), calls=%async_computation.2 | async-start | bytes 12582912 | tf_op jit(solution)/shard_map/all_to_all | solution.py:207
  302.0 0.0 reduce-scatter.5.cloned.1.call-start
  302.0 1.9 select_reduce_fusion
  303.9 67.1 %all-to-all-done.1 = bf16[4,384,2048]{2,1,0:T(8,128)(2,1)} async-done(((bf16[4,384,2048]{2,1,0:T(8,128)(2,1)}), bf16[4,384,2048]{2,1,0:T(8,128)(2,1)}, u32[]{:S(2)}, u32[]{:S(2)}) %all-to-all-start.1) | async-done | bytes 6291488 | tf_op jit(solution)/shard_map/all_to_all | solution.py:207
  371.0 3.4 copy.46
  374.4 3.2 convolution_convert_fusion.2
  377.7 48.1 %reduce-scatter.5.cloned.1.call-done = bf16[1,128,2048]{2,1,0:T(8,128)(2,1)} async-done(((bf16[8,128,2048]{2,1,0:T(8,128)(2,1)}), bf16[1,128,2048]{2,1,0:T(8,128)(2,1)}) %reduce-scatter.5.cloned.1.call-update) | async-done | bytes 524304 | tf_op jit(solution)/shard_map/reduce_scatter | solution.py:214
  425.7 2.4 fusion.18
  (41 shorter events, 0.3 us)
Async XLA Ops:
  6.5 283.1 %copy-start = (bf16[1,768,2048]{2,1,0:T(8,128)(2,1)S(1)}, bf16[1,768,2048]{2,1,0:T(8,128)(2,1)}, u32[]{:S(2)}) copy-start(bf16[1,768,2048]{2,1,0:T(8,128)(2,1)} %param.27) | copy-start | bytes 9437188
  6.5 41.6 %all-gather.6.cloned.1.call-start = ((), (), s32[]{:S(2)}) async-start(), calls=%async_computation.4 | async-start | bytes 2621440 | tf_op jit(solution)/shard_map/all_gather | solution.py:142
  10.0 74.9 %all-gather.8.cloned.1.call-start = ((), (), s32[]{:S(2)}) async-start(), calls=%async_computation.5 | async-start | bytes 2359296 | tf_op jit(solution)/shard_map/all_gather | solution.py:160
  48.1 4.6 %copy-start.7 = (f32[128]{0:T(128)S(1)}, f32[128]{0:T(128)}, u32[]{:S(2)}) copy-start(f32[128]{0:T(128)} %param.20) | copy-start | bytes 1540
  52.5 2.2 copy-start.1
  52.9 9.6 %copy-start.8 = (f32[128]{0:T(128)S(1)}, f32[128]{0:T(128)}, u32[]{:S(2)}) copy-start(f32[128]{0:T(128)} %param.19) | copy-start | bytes 1540
  55.6 92.3 %reduce-scatter.3.cloned.1.call-start = ((), (), s32[]{:S(2)}) async-start(), calls=%async_computation.6 | async-start | bytes 2621440 | tf_op jit(solution)/shard_map/reduce_scatter | solution.py:165
  60.5 3.8 copy-start.2
  87.9 4.6 %copy-start.11 = (bf16[512,2048]{1,0:T(8,128)(2,1)S(1)}, bf16[512,2048]{1,0:T(8,128)(2,1)}, u32[]{:S(2)}) copy-start(bf16[512,2048]{1,0:T(8,128)(2,1)} %param.21) | copy-start | bytes 6291460
  92.4 57.0 %copy-start.5 = (f32[2048]{0:T(1024)S(1)}, f32[2048]{0:T(1024)}, u32[]{:S(2)}) copy-start(f32[2048]{0:T(1024)} %param.22) | copy-start | bytes 24580
  92.4 59.2 %copy-start.4 = (s32[128,8]{0,1:T(8,128)S(1)}, s32[128,8]{0,1:T(8,128)}, u32[]{:S(2)}) copy-start(s32[128,8]{0,1:T(8,128)} %param.23) | copy-start | bytes 12292
  96.1 55.9 %copy-start.6 = (s32[128,8]{0,1:T(8,128)S(1)}, s32[128,8]{0,1:T(8,128)}, u32[]{:S(2)}) copy-start(s32[128,8]{0,1:T(8,128)} %param.24) | copy-start | bytes 12292
  96.2 102.9 %all-gather.10.cloned.1.call-start = ((), (), s32[]{:S(2)}) async-start(), calls=%async_computation.8 | async-start | bytes 4718592 | tf_op jit(solution)/shard_map/all_gather | solution.py:193
  166.1 0.6 copy-start.3
  204.2 74.6 %copy-start.9 = (bf16[1,2048,768]{2,1,0:T(8,128)(2,1)S(1)}, bf16[1,2048,768]{2,1,0:T(8,128)(2,1)}, u32[]{:S(2)}) copy-start(bf16[1,2048,768]{2,1,0:T(8,128)(2,1)} %param.25) | copy-start | bytes 9437188
  278.8 5.2 %copy-start.10 = (bf16[1,2048,768]{2,1,0:T(8,128)(2,1)S(1)}, bf16[1,2048,768]{2,1,0:T(8,128)(2,1)}, u32[]{:S(2)}) copy-start(bf16[1,2048,768]{2,1,0:T(8,128)(2,1)} %param.26) | copy-start | bytes 9437188
  296.7 74.3 %all-to-all-start.1 = ((bf16[4,384,2048]{2,1,0:T(8,128)(2,1)}), bf16[4,384,2048]{2,1,0:T(8,128)(2,1)}, u32[]{:S(2)}, u32[]{:S(2)}) async-start(bf16[4,384,2048]{2,1,0:T(8,128)(2,1)} %bitcast.52), calls=%async_computation.2 | async-start | bytes 12582912 | tf_op jit(solution)/shard_map/all_to_all | solution.py:207
  302.0 123.8 %reduce-scatter.5.cloned.1.call-start = ((), (), s32[]{:S(2)}) async-start(), calls=%async_computation.7 | async-start | bytes 4718592 | tf_op jit(solution)/shard_map/reduce_scatter | solution.py:214
Sparse Core Ops, SparseCore 0:
  10.1 38.0 all-gather.5
  55.7 29.0 all-gather.7
  96.3 51.5 reduce-scatter.2
  151.7 47.3 all-gather.9
  377.8 47.9 reduce-scatter.4

commit v2 on v0

v2 whole, which is shorter than its diff:
```python
import functools

import jax
import jax.numpy as jnp
from jax import lax
from jax.experimental import pallas as pl
from jax.experimental.pallas import tpu as pltpu
from jax.sharding import PartitionSpec as P

HEAD_SIZE = 128
QUERY_HEADS = 16
KEY_VALUE_HEADS = 2
TOP = 8
LOG2E = 1.4426950408889634

eps_value = 1e-06
theta_value = 1000000.0
floor_value = -1e30

VMEM = pl.BlockSpec(memory_space=pltpu.VMEM)
SMEM = pl.BlockSpec(memory_space=pltpu.SMEM)
PARAMS = pltpu.CompilerParams(vmem_limit_bytes=48 * 1024 * 1024)


def rms_scale(value_states, norm_gain):
    return (
        value_states
        * lax.rsqrt(jnp.mean(value_states * value_states, axis=-1, keepdims=True) + eps_value)
        * norm_gain
    )


def swap(array, axis, distance):
    pairs = [(i, i ^ distance) for i in range(lax.axis_size(axis))]
    return lax.ppermute(array, axis, pairs)


def tie(array, *others):
    if not others:
        return array
    return lax.optimization_barrier((array, *others))[0]


def rope_tables(positions):
    half = HEAD_SIZE // 2
    frequency = theta_value ** (-2.0 * jnp.arange(half, dtype=jnp.float32) / HEAD_SIZE)
    angles = positions.astype(jnp.float32)[:, None] * frequency[None, :]
    cosine, sine = jnp.cos(angles), jnp.sin(angles)
    return jnp.concatenate([cosine, cosine], axis=1), jnp.concatenate([-sine, sine], axis=1)


def normed_rotated(states, gain, cosine, sine):
    states = rms_scale(states, gain)
    return states * cosine + pltpu.roll(states, HEAD_SIZE // 2, 1) * sine


def key_value_kernel(tokens, gain, key_weight, value_weight, k_gain, cosine, sine, out):
    normed = rms_scale(tokens[...].astype(jnp.float32), gain[...]).astype(jnp.bfloat16)
    keys = jnp.dot(normed, key_weight[...], preferred_element_type=jnp.float32)
    values = jnp.dot(normed, value_weight[...], preferred_element_type=jnp.float32)
    for head in range(out.shape[0]):
        cols = slice(head * HEAD_SIZE, (head + 1) * HEAD_SIZE)
        rotated = normed_rotated(keys[:, cols], k_gain[...], cosine[...], sine[...])
        out[head, :, :HEAD_SIZE] = rotated.astype(jnp.bfloat16)
        out[head, :, HEAD_SIZE:] = values[:, cols].astype(jnp.bfloat16)


def query_kernel(*refs):
    *pieces, gain, w_query, q_gain, cosine, sine, out = refs
    rows = pieces[0].shape[0]
    heads = w_query.shape[1] // HEAD_SIZE
    for at, piece in enumerate(pieces):
        normed = rms_scale(piece[...].astype(jnp.float32), gain[...]).astype(jnp.bfloat16)
        queries = jnp.dot(normed, w_query[...], preferred_element_type=jnp.float32)
        here = pl.ds(at * rows, rows)
        for head in range(heads):
            cols = slice(head * HEAD_SIZE, (head + 1) * HEAD_SIZE)
            rotated = normed_rotated(queries[:, cols], q_gain[...], cosine[here, :], sine[here, :])
            out[at, pl.ds(head * rows, rows), :] = rotated.astype(jnp.bfloat16)


def attention_kernel(distance, rows, place, queries, both, w_out, out):
    block, me = place[0], place[1]
    heads = w_out.shape[0] // HEAD_SIZE
    width = heads * rows
    span = rows * (place.shape[0] - 2)
    scale = HEAD_SIZE ** (-0.5) * LOG2E
    asked = queries[0]

    def step(first, state, masked):
        keys = both[pl.ds(first, span), :HEAD_SIZE]
        values = both[pl.ds(first, span), HEAD_SIZE:]
        scores = lax.dot_general(
            keys, asked, (((1,), (1,)), ((), ())), preferred_element_type=jnp.float32
        )
        if masked:
            at = lax.broadcasted_iota(jnp.int32, (span, width), 0)
            key_pos = (me ^ (at // rows)) * rows + at % rows
            query = lax.broadcasted_iota(jnp.int32, (span, width), 1)
            scores = jnp.where(
                key_pos <= (me ^ distance) * rows + query % rows, scores, floor_value
            )
        top, total, mixed = state
        new_top = jnp.maximum(top, jnp.max(scores, axis=0, keepdims=True))
        weights = jnp.exp2((scores - new_top) * scale)
        rescale = jnp.exp2((top - new_top) * scale)
        total = total * rescale + jnp.sum(weights, axis=0, keepdims=True)
        mixed = mixed * rescale + lax.dot_general(
            values,
            weights.astype(jnp.bfloat16),
            (((0,), (0,)), ((), ())),
            preferred_element_type=jnp.float32,
        )
        return new_top, total, mixed

    state = (
        jnp.full((1, width), floor_value, jnp.float32),
        jnp.zeros((1, width), jnp.float32),
        jnp.zeros((HEAD_SIZE, width), jnp.float32),
    )
    state = step(pl.multiple_of(block * span, span), state, True)
    state = lax.fori_loop(
        0, block, lambda i, s: step(pl.multiple_of(i * span, span), s, False), state
    )
    _, total, mixed = state
    attended = (mixed / total).astype(jnp.bfloat16)
    attended = jnp.concatenate(
        [attended[:, head * rows : (head + 1) * rows] for head in range(heads)], axis=0
    )
    out[...] = lax.dot_general(
        attended, w_out[...], (((0,), (0,)), ((), ())), preferred_element_type=jnp.float32
    ).astype(jnp.bfloat16)


def residual_kernel(*refs):
    tokens, *partials, gain, residual, normed = refs
    attention = partials[0][...].astype(jnp.float32)
    for partial in partials[1:]:
        attention = attention + partial[...].astype(jnp.float32)
    rounded = (tokens[...].astype(jnp.float32) + attention).astype(jnp.bfloat16)
    residual[...] = rounded
    normed[...] = rms_scale(rounded.astype(jnp.float32), gain[...]).astype(jnp.bfloat16)


def slot_targets(routing, block, expert):
    table = routing[block].astype(jnp.float32)
    named = table[:TOP] == expert.astype(jnp.float32)
    slot = jnp.max(jnp.where(named, table[TOP : 2 * TOP], -1.0), axis=0, keepdims=True)
    weight = jnp.sum(jnp.where(named, table[2 * TOP :], 0.0), axis=0, keepdims=True)
    return slot.astype(jnp.int32), weight * (1.0 / 1024.0)


def dispatch_kernel(group, capacity, place, routing, same, other, *outs):
    block, me = place[0], place[1]
    count = len(outs)
    rows = same.shape[0]
    slots = lax.broadcasted_iota(jnp.int32, (capacity, rows), 0)
    for at, source in enumerate((same, other)):
        parts = []
        for distance in range(count):
            slot, _ = slot_targets(routing, block ^ (2 * group + at), block * count + (me ^ distance))
            parts.append(jnp.where(slots == slot, 1.0, 0.0))
        hot = jnp.concatenate(parts, axis=0).astype(jnp.bfloat16)
        picked = jnp.dot(hot, source[...], preferred_element_type=jnp.float32)
        picked = picked.astype(jnp.bfloat16)
        for distance in range(count):
            outs[distance][at * capacity : (at + 1) * capacity, :] = picked[
                distance * capacity : (distance + 1) * capacity
            ]


def combine_kernel(group, capacity, place, routing, *refs):
    *returned, same, other = refs
    block, me = place[0], place[1]
    count = len(returned)
    rows = same.shape[0]
    slots = lax.broadcasted_iota(jnp.int32, (capacity, rows), 0)
    for at, out in enumerate((same, other)):
        parts = []
        for distance in range(count):
            slot, weight = slot_targets(
                routing, block ^ (2 * group + at), block * count + (me ^ distance)
            )
            parts.append(jnp.where(slots == slot, weight, 0.0))
        shares = jnp.concatenate(parts, axis=0).astype(jnp.bfloat16)
        produced = jnp.concatenate(
            [ref[at * capacity : (at + 1) * capacity, :] for ref in returned], axis=0
        )
        out[...] = lax.dot_general(
            shares, produced, (((0,), (0,)), ((), ())), preferred_element_type=jnp.float32
        ).astype(jnp.bfloat16)


def call(kernel, out_shape, specs, flops, *args, name):
    outs = out_shape if isinstance(out_shape, list) else [out_shape]
    moved = sum(a.size * a.dtype.itemsize for a in [*args, *outs])
    return pl.pallas_call(
        kernel,
        out_shape=out_shape,
        in_specs=specs,
        out_specs=jax.tree.map(lambda _: VMEM, out_shape),
        compiler_params=PARAMS,
        cost_estimate=pl.CostEstimate(flops=flops, bytes_accessed=moved, transcendentals=0),
        name=name,
    )(*args)


def shards(
    tokens,
    ln1_gain,
    w_query,
    key_weight,
    value_weight,
    q_gain,
    k_gain,
    w_out,
    ln2_gain,
    expert_ids,
    route_weights,
    w_gate,
    w_up,
    w_down,
):
    rows, width = tokens.shape
    ctx_count = lax.axis_size("ctx")
    exp_count = lax.axis_size("exp")
    ctx_rows = rows * exp_count
    heads_dev = w_query.shape[1] // HEAD_SIZE
    group_width = QUERY_HEADS // KEY_VALUE_HEADS
    me_ctx = lax.axis_index("ctx").astype(jnp.int32)
    me_exp = lax.axis_index("exp").astype(jnp.int32)
    place = jnp.stack([me_ctx, me_exp] + [jnp.int32(0)] * exp_count)
    peers = list(range(exp_count))
    bf16 = functools.partial(jax.ShapeDtypeStruct, dtype=jnp.bfloat16)

    pieces = [tokens] + [swap(tokens, "exp", d) for d in peers[1:]]

    ln1_row = ln1_gain.reshape(1, width)
    own_first = me_ctx * ctx_rows + me_exp * rows
    cosine, sine = rope_tables(own_first + jnp.arange(rows))
    own_kv = call(
        key_value_kernel,
        bf16((KEY_VALUE_HEADS, rows, 2 * HEAD_SIZE)),
        [VMEM] * 7,
        4 * rows * width * KEY_VALUE_HEADS * HEAD_SIZE,
        tokens,
        ln1_row,
        key_weight,
        value_weight,
        k_gain.reshape(1, HEAD_SIZE),
        cosine,
        sine,
        name="own_kv",
    )

    def head_kv(distance):
        head = (me_exp ^ distance) * heads_dev // group_width
        return lax.dynamic_index_in_dim(own_kv, head, 0, keepdims=False)

    block_kv = jnp.concatenate(
        [head_kv(0)] + [swap(head_kv(d), "exp", d) for d in peers[1:]], axis=0
    )
    both = lax.all_gather(block_kv, "ctx", axis=0, tiled=True)

    experts = ctx_count * exp_count
    capacity = max(2, 3 * rows * TOP // (2 * experts))
    capacity = -(-capacity // 16) * 16
    chosen = expert_ids[:, :, None] == jnp.arange(experts)[None, None, :]
    counts = jnp.sum(chosen, axis=1, dtype=jnp.int32)
    rank_table = jnp.cumsum(counts, axis=0, dtype=jnp.int32) - counts
    slot_index = jnp.sum(jnp.where(chosen, rank_table[:, None, :], 0), axis=2)
    routing = jnp.concatenate([expert_ids, slot_index, route_weights], axis=1).T
    routing = lax.all_gather(tie(routing.astype(jnp.bfloat16), both), "ctx", axis=0)

    positions = jnp.concatenate(
        [me_ctx * ctx_rows + (me_exp ^ d) * rows + jnp.arange(rows) for d in peers]
    )
    cosine, sine = rope_tables(positions)
    queries = call(
        query_kernel,
        bf16((exp_count, heads_dev * rows, HEAD_SIZE)),
        [VMEM] * (exp_count + 5),
        2 * ctx_rows * width * w_query.shape[1],
        *pieces,
        ln1_row,
        w_query,
        q_gain.reshape(1, HEAD_SIZE),
        cosine,
        sine,
        name="queries",
    )

    order = sorted(peers, key=lambda d: -bin(d).count("1"))
    partials, last = {}, ()
    for d in order:
        partials[d] = call(
            functools.partial(attention_kernel, d, rows),
            bf16((rows, width)),
            [SMEM, VMEM, VMEM, VMEM],
            4 * rows * w_query.shape[1] * both.shape[0] + 2 * rows * w_out.size,
            place,
            tie(queries[d : d + 1], *last),
            both,
            w_out,
            name="attention",
        )
        last = (partials[d],)
    parts = [partials[0]] + [swap(partials[d], "exp", d) for d in order if d]
    residual, normed = call(
        residual_kernel,
        [bf16((rows, width)), bf16((rows, width))],
        [VMEM] * (exp_count + 2),
        10 * rows * width,
        tokens,
        *parts,
        ln2_gain.reshape(1, width),
        name="residual",
    )

    groups = ctx_count // 2
    far = [normed]
    for g in range(1, groups):
        far.append(swap(tie(normed, *([far[g - 1]] if g > 2 else [])), "ctx", 2 * g))
    in_flight = {d: () for d in peers[1:]}
    arrived = []
    for g in range(groups):
        mate = swap(far[g], "ctx", 1)
        outgoing = call(
            functools.partial(dispatch_kernel, g, capacity),
            [bf16((2 * capacity, width)) for _ in peers],
            [SMEM, VMEM, VMEM, VMEM],
            4 * exp_count * capacity * rows * width,
            place,
            routing,
            far[g],
            mate,
            name="dispatch",
        )
        came = [outgoing[0]]
        for d in peers[1:]:
            came.append(swap(tie(outgoing[d], *in_flight[d]), "exp", d))
            in_flight[d] = (came[d],)
        arrived.append(came)

    turns = [g for g in range(2, groups)] + [g for g in (1, 0) if g < groups]
    mixture = residual.astype(jnp.float32)
    produced = {}
    for g in range(groups):
        flat_rows = jnp.concatenate(arrived[g], axis=0)
        gate_act = jnp.dot(flat_rows, w_gate[0], preferred_element_type=jnp.float32)
        up_act = jnp.dot(flat_rows, w_up[0], preferred_element_type=jnp.float32)
        hidden = (jax.nn.silu(gate_act) * up_act).astype(jnp.bfloat16)
        made = jnp.dot(hidden, w_down[0], preferred_element_type=jnp.float32)
        made = made.astype(jnp.bfloat16)
        produced[g] = [made[d * 2 * capacity : (d + 1) * 2 * capacity] for d in peers]
    for g in turns:
        back = [produced[g][0]]
        for d in peers[1:]:
            back.append(swap(tie(produced[g][d], *in_flight[d]), "exp", d))
            in_flight[d] = (back[d],)
        same, other = call(
            functools.partial(combine_kernel, g, capacity),
            [bf16((rows, width)), bf16((rows, width))],
            [SMEM, VMEM] + [VMEM] * exp_count,
            4 * exp_count * capacity * rows * width,
            place,
            routing,
            *back,
            name="combine",
        )
        total = same.astype(jnp.float32) + swap(other, "ctx", 1).astype(jnp.float32)
        if g:
            total = swap(total.astype(jnp.bfloat16), "ctx", 2 * g).astype(jnp.float32)
        mixture = mixture + total
    return mixture.astype(jnp.bfloat16)


def solution(mesh):
    in_specs = (
        P(("ctx", "exp"), None),
        P(),
        P(None, "exp"),
        P(),
        P(),
        P(),
        P(),
        P("exp", None),
        P(),
        P(("ctx", "exp"), None),
        P(("ctx", "exp"), None),
        P(("ctx", "exp"), None, None),
        P(("ctx", "exp"), None, None),
        P(("ctx", "exp"), None, None),
    )
    out_specs = P(("ctx", "exp"), None)
    return jax.shard_map(shards, mesh=mesh, in_specs=in_specs, out_specs=out_specs, check_vma=False)
```

time: 508 us -> 349 us (0.69)
  waiting for transfers between devices: 273 us -> 138 us
  blocking collectives: 143 us -> 30.6 us
  starting transfers between devices: 4.05 us -> 64.7 us
  Pallas kernels: 0 us -> 26.4 us
  local copies, waits for them, and re-layouts: 10.2 us -> 30 us
  other arithmetic: 17.3 us -> 4.5 us
  matrix products: 45.4 us -> 39.5 us
    all_to_all x1 -> x0, blocking collectives: 143 us -> none  [shards(): lax.all_to_all(outgoing, ('ctx', 'exp'), split_axis=0, concat_axis=0, til...]
    all_to_all x1 -> x0, waiting for transfers between devices: 140 us -> none  [shards(): lax.all_to_all(produced.reshape(arrived.shape), ('ctx', 'exp'), split_axi...]
    ppermute x0 -> x47, waiting for transfers between devices: none -> 138 us  [swap(): return lax.ppermute(array, axis, pairs)]
    all_gather x3 -> x1, waiting for transfers between devices: 73.8 us -> 0.01 us  [shards(): both = lax.all_gather(block_kv, 'ctx', axis=0, tiled=True)]
    ppermute x0 -> x47, starting transfers between devices: none -> 64.7 us  [swap(): return lax.ppermute(array, axis, pairs)]
    reduce_scatter x1 -> x0, waiting for transfers between devices: 59.7 us -> none  [shards(): lax.psum_scatter(jnp.dot(attended, w_out, preferred_element_type=jnp.floa...]
    all_gather x0 -> x1, blocking collectives: none -> 30.6 us  [shards(): lax.all_gather(tie(routing.astype(jnp.bfloat16), both), 'ctx', axis=0)]
    pallas_call x0 -> x15, Pallas kernels: none -> 26.4 us  [call(): pl.pallas_call(kernel, out_shape=out_shape, in_specs=specs, out_specs=jax...]
  transfers between devices with their start and end apart: 5 -> 48, of which waited for: 5 -> 21; matrix products, arithmetic and copies ran while one was open for 3% -> 16% of each run, Pallas kernels for 0% -> 6%
where the time goes in v2:
time: 349 us; the launch traced here: 348 us
  waiting for transfers between devices  138 us (40%)
  starting transfers between devices  64.7 us (19%)
  matrix products  39.5 us (11%)
  blocking collectives  30.6 us (9%)
  local copies, waits for them, and re-layouts  30 us (9%)
  Pallas kernels  26.4 us (8%)
  between operations  14 us (4%)
  other arithmetic  4.5 us (1%)
    ppermute x47, waiting for transfers between devices, swap(): return lax.ppermute(array, axis, pairs)  138 us
    ppermute x47, starting transfers between devices, swap(): return lax.ppermute(array, axis, pairs)  64.7 us
    all_gather x1, blocking collectives, shards(): lax.all_gather(tie(routing.astype(jnp.bfloat16), both), 'ctx', axis=0)  30.6 us
    dot_general x4, matrix products, shards(): made = jnp.dot(hidden, w_down[0], preferred_element_type=jnp.float32)  27.6 us
    pallas_call x15, Pallas kernels, call(): pl.pallas_call(kernel, out_shape=out_shape, in_specs=specs, out_specs=jax...  26.4 us
    unnamed x74, local copies, waits for them, and re-layouts  22.3 us
    dot_general x4, matrix products, shards(): up_act = jnp.dot(flat_rows, w_up[0], preferred_element_type=jnp.float32)  11.9 us
  transfers between devices with their start and end apart: 48, of which 21 were waited for; matrix products, arithmetic and copies ran while one was open for 16% of the time, Pallas kernels for 6%

profile of v2, /device:TPU:0, one launch (start us, length us, event | category | flops | bytes accessed | tf_op | source)
XLA Modules:
  0.0 347.9 jit_solution(15523649104269462016)
XLA Ops:
  13.0 4.0 %collective-permute-start.5 = (bf16[128,256]{1,0:T(8,128)(2,1)S(1)}, bf16[128,256]{1,0:T(8,128)(2,1)S(1)}, u32[]{:S(2)}, u32[]{:S(2)}) collective-permute-start(bf16[128,256]{1,0:T(8,128)(2,1)S(1)} %get-tuple-element.130), channel_id=1, source_target_pairs={{0,3},{1,2},{2,1},{3,0},{4,7},{5,6},{6,5},{7,4},{8,11},{9,10},{10,... | collective-permute-start | bytes 196616 | tf_op jit(solution)/shard_map/ppermute | solution.py:35
  17.6 1.6 collective-permute-done.5
  19.2 2.0 collective-permute-done.4
  27.5 11.2 %collective-permute-done.2.refs_3_ = bf16[128,2048]{1,0:T(8,128)(2,1)} collective-permute-done((bf16[128,2048]{1,0:T(8,128)(2,1)}, bf16[128,2048]{1,0:T(8,128)(2,1)}, u32[]{:S(2)}, u32[]{:S(2)}) %collective-permute-start.2) | collective-permute-done | bytes 524320 | tf_op jit(solution)/shard_map/ppermute | solution.py:35
  38.6 8.7 %collective-permute-done.1.refs_2_ = bf16[128,2048]{1,0:T(8,128)(2,1)} collective-permute-done((bf16[128,2048]{1,0:T(8,128)(2,1)}, bf16[128,2048]{1,0:T(8,128)(2,1)}, u32[]{:S(2)}, u32[]{:S(2)}) %collective-permute-start.1) | collective-permute-done | bytes 524320 | tf_op jit(solution)/shard_map/ppermute | solution.py:35
  47.4 1.6 copy-done.4
  49.0 3.4 queries.1
  54.0 1.6 copy-done.16
  57.2 1.7 attention.4
  58.9 1.7 attention.5
  60.6 1.7 attention.6
  65.9 1.7 attention.7.refs_1_
  67.6 8.3 %collective-permute-done.8.refs_4_ = bf16[128,2048]{1,0:T(8,128)(2,1)S(1)} collective-permute-done((bf16[128,2048]{1,0:T(8,128)(2,1)S(1)}, bf16[128,2048]{1,0:T(8,128)(2,1)S(1)}, u32[]{:S(2)}, u32[]{:S(2)}) %collective-permute-start.8) | collective-permute-done | bytes 524320 | tf_op jit(solution)/shard_map/ppermute | solution.py:35
  75.9 1.7 collective-permute-done.7.refs_3_
  77.6 11.3 %collective-permute-done.6.refs_2_ = bf16[128,2048]{1,0:T(8,128)(2,1)S(1)} collective-permute-done((bf16[128,2048]{1,0:T(8,128)(2,1)S(1)}, bf16[128,2048]{1,0:T(8,128)(2,1)S(1)}, u32[]{:S(2)}, u32[]{:S(2)}) %collective-permute-start.6) | collective-permute-done | bytes 524320 | tf_op jit(solution)/shard_map/ppermute | solution.py:35
  91.9 11.3 %collective-permute-start.9 = (bf16[128,2048]{1,0:T(8,128)(2,1)}, bf16[128,2048]{1,0:T(8,128)(2,1)}, u32[]{:S(2)}, u32[]{:S(2)}) collective-permute-start(bf16[128,2048]{1,0:T(8,128)(2,1)} %get-tuple-element.79.same), channel_id=1, source_target_pairs={{0,16},{4,20},{8,24},{12,28},{16,0},{20,4},{24,8},{28,12},{1,17},{... | collective-permute-start | bytes 1572872 | tf_op jit(solution)/shard_map/ppermute | solution.py:35
  103.5 5.9 %collective-permute-start.11 = (bf16[128,2048]{1,0:T(8,128)(2,1)}, bf16[128,2048]{1,0:T(8,128)(2,1)}, u32[]{:S(2)}, u32[]{:S(2)}) collective-permute-start(bf16[128,2048]{1,0:T(8,128)(2,1)} %get-tuple-element.79.same), channel_id=1, source_target_pairs={{0,8},{4,12},{8,0},{12,4},{16,24},{20,28},{24,16},{28,20},{1,9},{5... | collective-permute-start | bytes 1572872 | tf_op jit(solution)/shard_map/ppermute | solution.py:35
  109.5 30.6 %all-gather = bf16[192,128]{1,0:T(8,128)(2,1)S(1)} all-gather(bf16[24,128]{1,0:T(8,128)(2,1)S(1)} %maximum_bitcast_fusion), channel_id=2, replica_groups=mesh['ctx'=8,'exp'=4] {'ctx'}, dimensions={0}, use_global_device_ids=true | all-gather | bytes 55296 | tf_op jit(solution)/shard_map/all_gather | solution.py:273
  140.0 1.8 dispatch.6
  143.1 2.3 collective-permute-start.23
  147.8 6.0 %collective-permute-done.14 = bf16[96,2048]{1,0:T(8,128)(2,1)S(1)} collective-permute-done((bf16[96,2048]{1,0:T(8,128)(2,1)S(1)}, bf16[96,2048]{1,0:T(8,128)(2,1)S(1)}, u32[]{:S(2)}, u32[]{:S(2)}) %collective-permute-start.14) | collective-permute-done | bytes 393248 | tf_op jit(solution)/shard_map/ppermute | solution.py:35
  153.8 10.8 %collective-permute-done.17 = bf16[96,2048]{1,0:T(8,128)(2,1)S(1)} collective-permute-done((bf16[96,2048]{1,0:T(8,128)(2,1)S(1)}, bf16[96,2048]{1,0:T(8,128)(2,1)S(1)}, u32[]{:S(2)}, u32[]{:S(2)}) %collective-permute-start.17) | collective-permute-done | bytes 393248 | tf_op jit(solution)/shard_map/ppermute | solution.py:35
  165.9 2.5 fusion.8
  168.5 6.9 %fusion.33 = bf16[384,2048]{1,0:T(8,128)(2,1)} fusion(bf16[1,768,2048]{2,1,0:T(8,128)(2,1)S(1)} %copy-done, f32[384,768]{1,0:T(8,128)} %fusion.8, bf16[384,2048]{1,0:T(8,128)(2,1)} %copy-done.25, bf16[1,2048,768]{2,1,0:T(8,128)(2,1)} %param.25), kind=kOutput, calls=%fused_computation.27 | convolution fusion | flops 2418475008 | bytes 10616832 | tf_op jit(solution)/shard_map/dot_general | solution.py:353
  175.3 1.8 dispatch.5
  180.7 2.8 dispatch.4
  184.4 4.9 %collective-permute-done.15 = bf16[96,2048]{1,0:T(8,128)(2,1)S(1)} collective-permute-done((bf16[96,2048]{1,0:T(8,128)(2,1)S(1)}, bf16[96,2048]{1,0:T(8,128)(2,1)S(1)}, u32[]{:S(2)}, u32[]{:S(2)}) %collective-permute-start.15) | collective-permute-done | bytes 393248 | tf_op jit(solution)/shard_map/ppermute | solution.py:35
  190.0 5.1 %collective-permute-done.18 = bf16[96,2048]{1,0:T(8,128)(2,1)S(1)} collective-permute-done((bf16[96,2048]{1,0:T(8,128)(2,1)S(1)}, bf16[96,2048]{1,0:T(8,128)(2,1)S(1)}, u32[]{:S(2)}, u32[]{:S(2)}) %collective-permute-start.18) | collective-permute-done | bytes 393248 | tf_op jit(solution)/shard_map/ppermute | solution.py:35
  195.2 2.2 collective-permute-start.19
  200.7 2.4 fusion.10
  203.1 6.9 %fusion.30 = bf16[384,2048]{1,0:T(8,128)(2,1)} fusion(bf16[1,768,2048]{2,1,0:T(8,128)(2,1)S(1)} %copy-done, f32[384,768]{1,0:T(8,128)} %fusion.10, bf16[384,2048]{1,0:T(8,128)(2,1)} %copy-done.24, bf16[1,2048,768]{2,1,0:T(8,128)(2,1)} %param.25), kind=kOutput, calls=%fused_computation.26 | convolution fusion | flops 2418475008 | bytes 10616832 | tf_op jit(solution)/shard_map/dot_general | solution.py:353
  210.0 2.9 dispatch.7
  221.5 4.5 %fusion.14 = f32[384,768]{1,0:T(8,128)} fusion(bf16[384,2048]{1,0:T(8,128)(2,1)S(1)} %constant_dynamic-update-slice_fusion, bf16[1,2048,768]{2,1,0:T(8,128)(2,1)} %param.26), kind=kOutput, calls=%fused_computation.14 | convolution fusion | flops 1207959552 | bytes 5898240 | tf_op jit(solution)/shard_map/dot_general | solution.py:351
  226.0 6.9 %fusion.24 = bf16[384,2048]{1,0:T(8,128)(2,1)} fusion(bf16[1,768,2048]{2,1,0:T(8,128)(2,1)S(1)} %copy-done, f32[384,768]{1,0:T(8,128)} %fusion.14, bf16[384,2048]{1,0:T(8,128)(2,1)} %copy-done.21, bf16[1,2048,768]{2,1,0:T(8,128)(2,1)} %param.25), kind=kOutput, calls=%fused_computation.24 | convolution fusion | flops 2418475008 | bytes 10616832 | tf_op jit(solution)/shard_map/dot_general | solution.py:353
  232.9 2.7 fusion.63
  243.5 2.5 fusion.12
  246.0 6.9 %fusion.27 = bf16[384,2048]{1,0:T(8,128)(2,1)} fusion(bf16[1,768,2048]{2,1,0:T(8,128)(2,1)S(1)} %copy-done, f32[384,768]{1,0:T(8,128)} %fusion.12, bf16[384,2048]{1,0:T(8,128)(2,1)} %copy-done.23, bf16[1,2048,768]{2,1,0:T(8,128)(2,1)} %param.25), kind=kOutput, calls=%fused_computation.25 | convolution fusion | flops 2418475008 | bytes 10616832 | tf_op jit(solution)/shard_map/dot_general | solution.py:353
  252.9 1.6 fusion.64
  258.3 1.8 combine.4
  260.3 3.6 %collective-permute-done.33.refs_1_ = bf16[96,2048]{1,0:T(8,128)(2,1)S(1)} collective-permute-done((bf16[96,2048]{1,0:T(8,128)(2,1)S(1)}, bf16[96,2048]{1,0:T(8,128)(2,1)S(1)}, u32[]{:S(2)}, u32[]{:S(2)}) %collective-permute-start.33) | collective-permute-done | bytes 393248 | tf_op jit(solution)/shard_map/ppermute | solution.py:35
  263.8 5.2 %collective-permute-done.34.refs_2_ = bf16[96,2048]{1,0:T(8,128)(2,1)S(1)} collective-permute-done((bf16[96,2048]{1,0:T(8,128)(2,1)S(1)}, bf16[96,2048]{1,0:T(8,128)(2,1)S(1)}, u32[]{:S(2)}, u32[]{:S(2)}) %collective-permute-start.34) | collective-permute-done | bytes 393248 | tf_op jit(solution)/shard_map/ppermute | solution.py:35
  273.8 8.3 %collective-permute-done.38.refs_1_ = bf16[96,2048]{1,0:T(8,128)(2,1)S(1)} collective-permute-done((bf16[96,2048]{1,0:T(8,128)(2,1)S(1)}, bf16[96,2048]{1,0:T(8,128)(2,1)S(1)}, u32[]{:S(2)}, u32[]{:S(2)}) %collective-permute-start.38) | collective-permute-done | bytes 393248 | tf_op jit(solution)/shard_map/ppermute | solution.py:35
  282.1 8.5 %collective-permute-done.39.refs_2_ = bf16[96,2048]{1,0:T(8,128)(2,1)S(1)} collective-permute-done((bf16[96,2048]{1,0:T(8,128)(2,1)S(1)}, bf16[96,2048]{1,0:T(8,128)(2,1)S(1)}, u32[]{:S(2)}, u32[]{:S(2)}) %collective-permute-start.39) | collective-permute-done | bytes 393248 | tf_op jit(solution)/shard_map/ppermute | solution.py:35
  295.6 8.3 %collective-permute-done.43.refs_1_ = bf16[96,2048]{1,0:T(8,128)(2,1)S(1)} collective-permute-done((bf16[96,2048]{1,0:T(8,128)(2,1)S(1)}, bf16[96,2048]{1,0:T(8,128)(2,1)S(1)}, u32[]{:S(2)}, u32[]{:S(2)}) %collective-permute-start.43) | collective-permute-done | bytes 393248 | tf_op jit(solution)/shard_map/ppermute | solution.py:35
  305.4 7.5 %collective-permute-done.44.refs_2_ = bf16[96,2048]{1,0:T(8,128)(2,1)S(1)} collective-permute-done((bf16[96,2048]{1,0:T(8,128)(2,1)S(1)}, bf16[96,2048]{1,0:T(8,128)(2,1)S(1)}, u32[]{:S(2)}, u32[]{:S(2)}) %collective-permute-start.44) | collective-permute-done | bytes 393248 | tf_op jit(solution)/shard_map/ppermute | solution.py:35
  314.2 1.7 collective-permute-start.42
  315.9 12.7 %collective-permute-done.32 = bf16[128,2048]{1,0:T(8,128)(2,1)S(1)} collective-permute-done((bf16[128,2048]{1,0:T(8,128)(2,1)S(1)}, bf16[128,2048]{1,0:T(8,128)(2,1)S(1)}, u32[]{:S(2)}, u32[]{:S(2)}) %collective-permute-start.32) | collective-permute-done | bytes 524320 | tf_op jit(solution)/shard_map/ppermute | solution.py:35
  328.6 11.1 %collective-permute-done.42 = bf16[128,2048]{1,0:T(8,128)(2,1)S(1)} collective-permute-done((bf16[128,2048]{1,0:T(8,128)(2,1)S(1)}, bf16[128,2048]{1,0:T(8,128)(2,1)S(1)}, u32[]{:S(2)}, u32[]{:S(2)}) %collective-permute-start.42) | collective-permute-done | bytes 524320 | tf_op jit(solution)/shard_map/ppermute | solution.py:35
  (185 shorter events, 70.8 us)
Async XLA Ops:
  6.5 46.5 %all-gather.3.cloned.1.call-start = ((), (), s32[]{:S(2)}) async-start(), calls=%async_computation | async-start | bytes 2359296 | tf_op jit(solution)/shard_map/all_gather | solution.py:263
  13.0 6.2 %collective-permute-start.5 = (bf16[128,256]{1,0:T(8,128)(2,1)S(1)}, bf16[128,256]{1,0:T(8,128)(2,1)S(1)}, u32[]{:S(2)}, u32[]{:S(2)}) collective-permute-start(bf16[128,256]{1,0:T(8,128)(2,1)S(1)} %get-tuple-element.130), channel_id=1, source_target_pairs={{0,3},{1,2},{2,1},{3,0},{4,7},{5,6},{6,5},{7,4},{8,11},{9,10},{10,... | collective-permute-start | bytes 196616 | tf_op jit(solution)/shard_map/ppermute | solution.py:35
  17.0 4.3 %collective-permute-start.4 = (bf16[128,256]{1,0:T(8,128)(2,1)S(1)}, bf16[128,256]{1,0:T(8,128)(2,1)S(1)}, u32[]{:S(2)}, u32[]{:S(2)}) collective-permute-start(bf16[128,256]{1,0:T(8,128)(2,1)S(1)} %get-tuple-element.131), channel_id=1, source_target_pairs={{0,2},{1,3},{2,0},{3,1},{4,6},{5,7},{6,4},{7,5},{8,10},{9,11},{10,... | collective-permute-start | bytes 196616 | tf_op jit(solution)/shard_map/ppermute | solution.py:35
  17.5 4.3 %collective-permute-start.3 = (bf16[128,256]{1,0:T(8,128)(2,1)S(1)}, bf16[128,256]{1,0:T(8,128)(2,1)S(1)}, u32[]{:S(2)}, u32[]{:S(2)}) collective-permute-start(bf16[128,256]{1,0:T(8,128)(2,1)S(1)} %get-tuple-element.132), channel_id=1, source_target_pairs={{0,1},{1,0},{2,3},{3,2},{4,5},{5,4},{6,7},{7,6},{8,9},{9,8},{10,11... | collective-permute-start | bytes 196616 | tf_op jit(solution)/shard_map/ppermute | solution.py:35
  22.5 16.1 %collective-permute-start.2 = (bf16[128,2048]{1,0:T(8,128)(2,1)}, bf16[128,2048]{1,0:T(8,128)(2,1)}, u32[]{:S(2)}, u32[]{:S(2)}) collective-permute-start(bf16[128,2048]{1,0:T(8,128)(2,1)} %refs_0_.3), channel_id=1, source_target_pairs={{0,3},{1,2},{2,1},{3,0},{4,7},{5,6},{6,5},{7,4},{8,11},{9,10},{10,... | collective-permute-start | bytes 1572872 | tf_op jit(solution)/shard_map/ppermute | solution.py:35
  24.1 23.3 %collective-permute-start.1 = (bf16[128,2048]{1,0:T(8,128)(2,1)}, bf16[128,2048]{1,0:T(8,128)(2,1)}, u32[]{:S(2)}, u32[]{:S(2)}) collective-permute-start(bf16[128,2048]{1,0:T(8,128)(2,1)} %refs_0_.3), channel_id=1, source_target_pairs={{0,2},{1,3},{2,0},{3,1},{4,6},{5,7},{6,4},{7,5},{8,10},{9,11},{10,... | collective-permute-start | bytes 1572872 | tf_op jit(solution)/shard_map/ppermute | solution.py:35
  24.5 22.9 %collective-permute-start = (bf16[128,2048]{1,0:T(8,128)(2,1)}, bf16[128,2048]{1,0:T(8,128)(2,1)}, u32[]{:S(2)}, u32[]{:S(2)}) collective-permute-start(bf16[128,2048]{1,0:T(8,128)(2,1)} %refs_0_.3), channel_id=1, source_target_pairs={{0,1},{1,0},{2,3},{3,2},{4,5},{5,4},{6,7},{7,6},{8,9},{9,8},{10,11... | collective-permute-start | bytes 1572872 | tf_op jit(solution)/shard_map/ppermute | solution.py:35
  62.3 13.6 %collective-permute-start.8 = (bf16[128,2048]{1,0:T(8,128)(2,1)S(1)}, bf16[128,2048]{1,0:T(8,128)(2,1)S(1)}, u32[]{:S(2)}, u32[]{:S(2)}) collective-permute-start(bf16[128,2048]{1,0:T(8,128)(2,1)S(1)} %attention.6), channel_id=1, source_target_pairs={{0,2},{1,3},{2,0},{3,1},{4,6},{5,7},{6,4},{7,5},{8,10},{9,11},{10,... | collective-permute-start | bytes 1572872 | tf_op jit(solution)/shard_map/ppermute | solution.py:35
  63.8 13.8 %collective-permute-start.7 = (bf16[128,2048]{1,0:T(8,128)(2,1)S(1)}, bf16[128,2048]{1,0:T(8,128)(2,1)S(1)}, u32[]{:S(2)}, u32[]{:S(2)}) collective-permute-start(bf16[128,2048]{1,0:T(8,128)(2,1)S(1)} %attention.5), channel_id=1, source_target_pairs={{0,1},{1,0},{2,3},{3,2},{4,5},{5,4},{6,7},{7,6},{8,9},{9,8},{10,11... | collective-permute-start | bytes 1572872 | tf_op jit(solution)/shard_map/ppermute | solution.py:35
  64.7 24.2 %collective-permute-start.6 = (bf16[128,2048]{1,0:T(8,128)(2,1)S(1)}, bf16[128,2048]{1,0:T(8,128)(2,1)S(1)}, u32[]{:S(2)}, u32[]{:S(2)}) collective-permute-start(bf16[128,2048]{1,0:T(8,128)(2,1)S(1)} %attention.4), channel_id=1, source_target_pairs={{0,3},{1,2},{2,1},{3,0},{4,7},{5,6},{6,5},{7,4},{8,11},{9,10},{10,... | collective-permute-start | bytes 1572872 | tf_op jit(solution)/shard_map/ppermute | solution.py:35
  91.0 49.0 %collective-permute-start.13 = (bf16[128,2048]{1,0:T(8,128)(2,1)}, bf16[128,2048]{1,0:T(8,128)(2,1)}, u32[]{:S(2)}, u32[]{:S(2)}) collective-permute-start(bf16[128,2048]{1,0:T(8,128)(2,1)} %get-tuple-element.79.same), channel_id=1, source_target_pairs={{0,4},{4,0},{8,12},{12,8},{16,20},{20,16},{24,28},{28,24},{1,5},{5... | collective-permute-start | bytes 1572872 | tf_op jit(solution)/shard_map/ppermute | solution.py:35
  91.9 51.2 %collective-permute-start.9 = (bf16[128,2048]{1,0:T(8,128)(2,1)}, bf16[128,2048]{1,0:T(8,128)(2,1)}, u32[]{:S(2)}, u32[]{:S(2)}) collective-permute-start(bf16[128,2048]{1,0:T(8,128)(2,1)} %get-tuple-element.79.same), channel_id=1, source_target_pairs={{0,16},{4,20},{8,24},{12,28},{16,0},{20,4},{24,8},{28,12},{1,17},{... | collective-permute-start | bytes 1572872 | tf_op jit(solution)/shard_map/ppermute | solution.py:35
  103.5 44.2 %collective-permute-start.11 = (bf16[128,2048]{1,0:T(8,128)(2,1)}, bf16[128,2048]{1,0:T(8,128)(2,1)}, u32[]{:S(2)}, u32[]{:S(2)}) collective-permute-start(bf16[128,2048]{1,0:T(8,128)(2,1)} %get-tuple-element.79.same), channel_id=1, source_target_pairs={{0,8},{4,12},{8,0},{12,4},{16,24},{20,28},{24,16},{28,20},{1,9},{5... | collective-permute-start | bytes 1572872 | tf_op jit(solution)/shard_map/ppermute | solution.py:35
  141.8 12.0 %collective-permute-start.14 = (bf16[96,2048]{1,0:T(8,128)(2,1)S(1)}, bf16[96,2048]{1,0:T(8,128)(2,1)S(1)}, u32[]{:S(2)}, u32[]{:S(2)}) collective-permute-start(bf16[96,2048]{1,0:T(8,128)(2,1)S(1)} %get-tuple-element.66), channel_id=1, source_target_pairs={{0,1},{1,0},{2,3},{3,2},{4,5},{5,4},{6,7},{7,6},{8,9},{9,8},{10,11... | collective-permute-start | bytes 1179656 | tf_op jit(solution)/shard_map/ppermute | solution.py:35
  143.1 37.6 %collective-permute-start.23 = (bf16[128,2048]{1,0:T(8,128)(2,1)}, bf16[128,2048]{1,0:T(8,128)(2,1)}, u32[]{:S(2)}, u32[]{:S(2)}) collective-permute-start(bf16[128,2048]{1,0:T(8,128)(2,1)} %get-tuple-element.79.same), channel_id=1, source_target_pairs={{0,24},{4,28},{8,16},{12,20},{16,8},{20,12},{24,0},{28,4},{1,25},{... | collective-permute-start | bytes 1572872 | tf_op jit(solution)/shard_map/ppermute | solution.py:35
  145.4 19.2 %collective-permute-start.17 = (bf16[96,2048]{1,0:T(8,128)(2,1)S(1)}, bf16[96,2048]{1,0:T(8,128)(2,1)S(1)}, u32[]{:S(2)}, u32[]{:S(2)}) collective-permute-start(bf16[96,2048]{1,0:T(8,128)(2,1)S(1)} %get-tuple-element.71), channel_id=1, source_target_pairs={{0,2},{1,3},{2,0},{3,1},{4,6},{5,7},{6,4},{7,5},{8,10},{9,11},{10,... | collective-permute-start | bytes 1179656 | tf_op jit(solution)/shard_map/ppermute | solution.py:35
  146.5 18.2 %collective-permute-start.20 = (bf16[96,2048]{1,0:T(8,128)(2,1)S(1)}, bf16[96,2048]{1,0:T(8,128)(2,1)S(1)}, u32[]{:S(2)}, u32[]{:S(2)}) collective-permute-start(bf16[96,2048]{1,0:T(8,128)(2,1)S(1)} %get-tuple-element.76), channel_id=1, source_target_pairs={{0,3},{1,2},{2,1},{3,0},{4,7},{5,6},{6,5},{7,4},{8,11},{9,10},{10,... | collective-permute-start | bytes 1179656 | tf_op jit(solution)/shard_map/ppermute | solution.py:35
  147.7 32.9 %collective-permute-start.10 = (bf16[128,2048]{1,0:T(8,128)(2,1)}, bf16[128,2048]{1,0:T(8,128)(2,1)}, u32[]{:S(2)}, u32[]{:S(2)}) collective-permute-start(bf16[128,2048]{1,0:T(8,128)(2,1)} %collective-permute-done.9.same), channel_id=1, source_target_pairs={{0,4},{4,0},{8,12},{12,8},{16,20},{20,16},{24,28},{28,24},{1,5},{5... | collective-permute-start | bytes 1572872 | tf_op jit(solution)/shard_map/ppermute | solution.py:35
  153.8 21.5 %collective-permute-start.12 = (bf16[128,2048]{1,0:T(8,128)(2,1)}, bf16[128,2048]{1,0:T(8,128)(2,1)}, u32[]{:S(2)}, u32[]{:S(2)}) collective-permute-start(bf16[128,2048]{1,0:T(8,128)(2,1)} %collective-permute-done.11.same), channel_id=1, source_target_pairs={{0,4},{4,0},{8,12},{12,8},{16,20},{20,16},{24,28},{28,24},{1,5},{5... | collective-permute-start | bytes 1572872 | tf_op jit(solution)/shard_map/ppermute | solution.py:35
  177.1 12.1 %collective-permute-start.15 = (bf16[96,2048]{1,0:T(8,128)(2,1)S(1)}, bf16[96,2048]{1,0:T(8,128)(2,1)S(1)}, u32[]{:S(2)}, u32[]{:S(2)}) collective-permute-start(bf16[96,2048]{1,0:T(8,128)(2,1)S(1)} %get-tuple-element.67), channel_id=1, source_target_pairs={{0,1},{1,0},{2,3},{3,2},{4,5},{5,4},{6,7},{7,6},{8,9},{9,8},{10,11... | collective-permute-start | bytes 1179656 | tf_op jit(solution)/shard_map/ppermute | solution.py:35
  178.0 17.2 %collective-permute-start.18 = (bf16[96,2048]{1,0:T(8,128)(2,1)S(1)}, bf16[96,2048]{1,0:T(8,128)(2,1)S(1)}, u32[]{:S(2)}, u32[]{:S(2)}) collective-permute-start(bf16[96,2048]{1,0:T(8,128)(2,1)S(1)} %get-tuple-element.72), channel_id=1, source_target_pairs={{0,2},{1,3},{2,0},{3,1},{4,6},{5,7},{6,4},{7,5},{8,10},{9,11},{10,... | collective-permute-start | bytes 1179656 | tf_op jit(solution)/shard_map/ppermute | solution.py:35
  179.4 18.8 %collective-permute-start.21 = (bf16[96,2048]{1,0:T(8,128)(2,1)S(1)}, bf16[96,2048]{1,0:T(8,128)(2,1)S(1)}, u32[]{:S(2)}, u32[]{:S(2)}) collective-permute-start(bf16[96,2048]{1,0:T(8,128)(2,1)S(1)} %get-tuple-element.77), channel_id=1, source_target_pairs={{0,3},{1,2},{2,1},{3,0},{4,7},{5,6},{6,5},{7,4},{8,11},{9,10},{10,... | collective-permute-start | bytes 1179656 | tf_op jit(solution)/shard_map/ppermute | solution.py:35
  180.7 29.4 %collective-permute-start.24 = (bf16[128,2048]{1,0:T(8,128)(2,1)}, bf16[128,2048]{1,0:T(8,128)(2,1)}, u32[]{:S(2)}, u32[]{:S(2)}) collective-permute-start(bf16[128,2048]{1,0:T(8,128)(2,1)} %collective-permute-done.23.same), channel_id=1, source_target_pairs={{0,4},{4,0},{8,12},{12,8},{16,20},{20,16},{24,28},{28,24},{1,5},{5... | collective-permute-start | bytes 1572872 | tf_op jit(solution)/shard_map/ppermute | solution.py:35
  189.2 24.5 %collective-permute-start.16 = (bf16[96,2048]{1,0:T(8,128)(2,1)}, bf16[96,2048]{1,0:T(8,128)(2,1)}, u32[]{:S(2)}, u32[]{:S(2)}) collective-permute-start(bf16[96,2048]{1,0:T(8,128)(2,1)} %get-tuple-element.68), channel_id=1, source_target_pairs={{0,1},{1,0},{2,3},{3,2},{4,5},{5,4},{6,7},{7,6},{8,9},{9,8},{10,11... | collective-permute-start | bytes 1179656 | tf_op jit(solution)/shard_map/ppermute | solution.py:35
  195.2 19.7 %collective-permute-start.19 = (bf16[96,2048]{1,0:T(8,128)(2,1)}, bf16[96,2048]{1,0:T(8,128)(2,1)}, u32[]{:S(2)}, u32[]{:S(2)}) collective-permute-start(bf16[96,2048]{1,0:T(8,128)(2,1)} %get-tuple-element.73), channel_id=1, source_target_pairs={{0,2},{1,3},{2,0},{3,1},{4,6},{5,7},{6,4},{7,5},{8,10},{9,11},{10,... | collective-permute-start | bytes 1179656 | tf_op jit(solution)/shard_map/ppermute | solution.py:35
  198.2 17.8 %collective-permute-start.22 = (bf16[96,2048]{1,0:T(8,128)(2,1)}, bf16[96,2048]{1,0:T(8,128)(2,1)}, u32[]{:S(2)}, u32[]{:S(2)}) collective-permute-start(bf16[96,2048]{1,0:T(8,128)(2,1)} %get-tuple-element.78), channel_id=1, source_target_pairs={{0,3},{1,2},{2,1},{3,0},{4,7},{5,6},{6,5},{7,4},{8,11},{9,10},{10,... | collective-permute-start | bytes 1179656 | tf_op jit(solution)/shard_map/ppermute | solution.py:35
  213.7 22.0 %collective-permute-start.25 = (bf16[96,2048]{1,0:T(8,128)(2,1)}, bf16[96,2048]{1,0:T(8,128)(2,1)}, u32[]{:S(2)}, u32[]{:S(2)}) collective-permute-start(bf16[96,2048]{1,0:T(8,128)(2,1)} %get-tuple-element.81), channel_id=1, source_target_pairs={{0,1},{1,0},{2,3},{3,2},{4,5},{5,4},{6,7},{7,6},{8,9},{9,8},{10,11... | collective-permute-start | bytes 1179656 | tf_op jit(solution)/shard_map/ppermute | solution.py:35
  214.9 20.8 %collective-permute-start.27 = (bf16[96,2048]{1,0:T(8,128)(2,1)}, bf16[96,2048]{1,0:T(8,128)(2,1)}, u32[]{:S(2)}, u32[]{:S(2)}) collective-permute-start(bf16[96,2048]{1,0:T(8,128)(2,1)} %get-tuple-element.84), channel_id=1, source_target_pairs={{0,2},{1,3},{2,0},{3,1},{4,6},{5,7},{6,4},{7,5},{8,10},{9,11},{10,... | collective-permute-start | bytes 1179656 | tf_op jit(solution)/shard_map/ppermute | solution.py:35
  216.0 19.7 %collective-permute-start.29 = (bf16[96,2048]{1,0:T(8,128)(2,1)}, bf16[96,2048]{1,0:T(8,128)(2,1)}, u32[]{:S(2)}, u32[]{:S(2)}) collective-permute-start(bf16[96,2048]{1,0:T(8,128)(2,1)} %get-tuple-element.87), channel_id=1, source_target_pairs={{0,3},{1,2},{2,1},{3,0},{4,7},{5,6},{6,5},{7,4},{8,11},{9,10},{10,... | collective-permute-start | bytes 1179656 | tf_op jit(solution)/shard_map/ppermute | solution.py:35
  235.7 18.9 %collective-permute-start.26 = (bf16[96,2048]{1,0:T(8,128)(2,1)}, bf16[96,2048]{1,0:T(8,128)(2,1)}, u32[]{:S(2)}, u32[]{:S(2)}) collective-permute-start(bf16[96,2048]{1,0:T(8,128)(2,1)} %get-tuple-element.82), channel_id=1, source_target_pairs={{0,1},{1,0},{2,3},{3,2},{4,5},{5,4},{6,7},{7,6},{8,9},{9,8},{10,11... | collective-permute-start | bytes 1179656 | tf_op jit(solution)/shard_map/ppermute | solution.py:35
  237.0 17.6 %collective-permute-start.28 = (bf16[96,2048]{1,0:T(8,128)(2,1)}, bf16[96,2048]{1,0:T(8,128)(2,1)}, u32[]{:S(2)}, u32[]{:S(2)}) collective-permute-start(bf16[96,2048]{1,0:T(8,128)(2,1)} %get-tuple-element.85), channel_id=1, source_target_pairs={{0,2},{1,3},{2,0},{3,1},{4,6},{5,7},{6,4},{7,5},{8,10},{9,11},{10,... | collective-permute-start | bytes 1179656 | tf_op jit(solution)/shard_map/ppermute | solution.py:35
  238.0 16.5 %collective-permute-start.30 = (bf16[96,2048]{1,0:T(8,128)(2,1)}, bf16[96,2048]{1,0:T(8,128)(2,1)}, u32[]{:S(2)}, u32[]{:S(2)}) collective-permute-start(bf16[96,2048]{1,0:T(8,128)(2,1)} %get-tuple-element.88), channel_id=1, source_target_pairs={{0,3},{1,2},{2,1},{3,0},{4,7},{5,6},{6,5},{7,4},{8,11},{9,10},{10,... | collective-permute-start | bytes 1179656 | tf_op jit(solution)/shard_map/ppermute | solution.py:35
  254.6 9.2 %collective-permute-start.33 = (bf16[96,2048]{1,0:T(8,128)(2,1)S(1)}, bf16[96,2048]{1,0:T(8,128)(2,1)S(1)}, u32[]{:S(2)}, u32[]{:S(2)}) collective-permute-start(bf16[96,2048]{1,0:T(8,128)(2,1)S(1)} %get-tuple-element.92), channel_id=1, source_target_pairs={{0,1},{1,0},{2,3},{3,2},{4,5},{5,4},{6,7},{7,6},{8,9},{9,8},{10,11... | collective-permute-start | bytes 1179656 | tf_op jit(solution)/shard_map/ppermute | solution.py:35
  255.9 13.1 %collective-permute-start.34 = (bf16[96,2048]{1,0:T(8,128)(2,1)S(1)}, bf16[96,2048]{1,0:T(8,128)(2,1)S(1)}, u32[]{:S(2)}, u32[]{:S(2)}) collective-permute-start(bf16[96,2048]{1,0:T(8,128)(2,1)S(1)} %get-tuple-element.93), channel_id=1, source_target_pairs={{0,2},{1,3},{2,0},{3,1},{4,6},{5,7},{6,4},{7,5},{8,10},{9,11},{10,... | collective-permute-start | bytes 1179656 | tf_op jit(solution)/shard_map/ppermute | solution.py:35
  256.9 12.1 %collective-permute-start.35 = (bf16[96,2048]{1,0:T(8,128)(2,1)S(1)}, bf16[96,2048]{1,0:T(8,128)(2,1)S(1)}, u32[]{:S(2)}, u32[]{:S(2)}) collective-permute-start(bf16[96,2048]{1,0:T(8,128)(2,1)S(1)} %get-tuple-element.94), channel_id=1, source_target_pairs={{0,3},{1,2},{2,1},{3,0},{4,7},{5,6},{6,5},{7,4},{8,11},{9,10},{10,... | collective-permute-start | bytes 1179656 | tf_op jit(solution)/shard_map/ppermute | solution.py:35
  260.2 31.5 %collective-permute-start.31 = (bf16[128,2048]{1,0:T(8,128)(2,1)S(1)}, bf16[128,2048]{1,0:T(8,128)(2,1)S(1)}, u32[]{:S(2)}, u32[]{:S(2)}) collective-permute-start(bf16[128,2048]{1,0:T(8,128)(2,1)S(1)} %get-tuple-element.90), channel_id=1, source_target_pairs={{0,4},{4,0},{8,12},{12,8},{16,20},{20,16},{24,28},{28,24},{1,5},{5... | collective-permute-start | bytes 1572872 | tf_op jit(solution)/shard_map/ppermute | solution.py:35
  270.0 24.1 %collective-permute-start.36 = (bf16[128,2048]{1,0:T(8,128)(2,1)S(1)}, bf16[128,2048]{1,0:T(8,128)(2,1)S(1)}, u32[]{:S(2)}, u32[]{:S(2)}) collective-permute-start(bf16[128,2048]{1,0:T(8,128)(2,1)S(1)} %get-tuple-element.96), channel_id=1, source_target_pairs={{0,4},{4,0},{8,12},{12,8},{16,20},{20,16},{24,28},{28,24},{1,5},{5... | collective-permute-start | bytes 1572872 | tf_op jit(solution)/shard_map/ppermute | solution.py:35
  270.1 12.0 %collective-permute-start.38 = (bf16[96,2048]{1,0:T(8,128)(2,1)S(1)}, bf16[96,2048]{1,0:T(8,128)(2,1)S(1)}, u32[]{:S(2)}, u32[]{:S(2)}) collective-permute-start(bf16[96,2048]{1,0:T(8,128)(2,1)S(1)} %get-tuple-element.98), channel_id=1, source_target_pairs={{0,1},{1,0},{2,3},{3,2},{4,5},{5,4},{6,7},{7,6},{8,9},{9,8},{10,11... | collective-permute-start | bytes 1179656 | tf_op jit(solution)/shard_map/ppermute | solution.py:35
  271.0 19.6 %collective-permute-start.39 = (bf16[96,2048]{1,0:T(8,128)(2,1)S(1)}, bf16[96,2048]{1,0:T(8,128)(2,1)S(1)}, u32[]{:S(2)}, u32[]{:S(2)}) collective-permute-start(bf16[96,2048]{1,0:T(8,128)(2,1)S(1)} %get-tuple-element.99), channel_id=1, source_target_pairs={{0,2},{1,3},{2,0},{3,1},{4,6},{5,7},{6,4},{7,5},{8,10},{9,11},{10,... | collective-permute-start | bytes 1179656 | tf_op jit(solution)/shard_map/ppermute | solution.py:35
  272.3 18.3 %collective-permute-start.40 = (bf16[96,2048]{1,0:T(8,128)(2,1)S(1)}, bf16[96,2048]{1,0:T(8,128)(2,1)S(1)}, u32[]{:S(2)}, u32[]{:S(2)}) collective-permute-start(bf16[96,2048]{1,0:T(8,128)(2,1)S(1)} %get-tuple-element.100), channel_id=1, source_target_pairs={{0,3},{1,2},{2,1},{3,0},{4,7},{5,6},{6,5},{7,4},{8,11},{9,10},{10,... | collective-permute-start | bytes 1179656 | tf_op jit(solution)/shard_map/ppermute | solution.py:35
  291.7 22.4 %collective-permute-start.41 = (bf16[128,2048]{1,0:T(8,128)(2,1)S(1)}, bf16[128,2048]{1,0:T(8,128)(2,1)S(1)}, u32[]{:S(2)}, u32[]{:S(2)}) collective-permute-start(bf16[128,2048]{1,0:T(8,128)(2,1)S(1)} %get-tuple-element.102), channel_id=1, source_target_pairs={{0,4},{4,0},{8,12},{12,8},{16,20},{20,16},{24,28},{28,24},{1,5},{5... | collective-permute-start | bytes 1572872 | tf_op jit(solution)/shard_map/ppermute | solution.py:35
  291.9 36.7 %collective-permute-start.32 = (bf16[128,2048]{1,0:T(8,128)(2,1)S(1)}, bf16[128,2048]{1,0:T(8,128)(2,1)S(1)}, u32[]{:S(2)}, u32[]{:S(2)}) collective-permute-start(bf16[128,2048]{1,0:T(8,128)(2,1)S(1)} %add_convert_fusion.3), channel_id=1, source_target_pairs={{0,16},{4,20},{8,24},{12,28},{16,0},{20,4},{24,8},{28,12},{1,17},{... | collective-permute-start | bytes 1572872 | tf_op jit(solution)/shard_map/ppermute | solution.py:35
  292.0 12.0 %collective-permute-start.43 = (bf16[96,2048]{1,0:T(8,128)(2,1)S(1)}, bf16[96,2048]{1,0:T(8,128)(2,1)S(1)}, u32[]{:S(2)}, u32[]{:S(2)}) collective-permute-start(bf16[96,2048]{1,0:T(8,128)(2,1)S(1)} %get-tuple-element.104), channel_id=1, source_target_pairs={{0,1},{1,0},{2,3},{3,2},{4,5},{5,4},{6,7},{7,6},{8,9},{9,8},{10,11... | collective-permute-start | bytes 1179656 | tf_op jit(solution)/shard_map/ppermute | solution.py:35
  293.2 19.7 %collective-permute-start.44 = (bf16[96,2048]{1,0:T(8,128)(2,1)S(1)}, bf16[96,2048]{1,0:T(8,128)(2,1)S(1)}, u32[]{:S(2)}, u32[]{:S(2)}) collective-permute-start(bf16[96,2048]{1,0:T(8,128)(2,1)S(1)} %get-tuple-element.105), channel_id=1, source_target_pairs={{0,2},{1,3},{2,0},{3,1},{4,6},{5,7},{6,4},{7,5},{8,10},{9,11},{10,... | collective-permute-start | bytes 1179656 | tf_op jit(solution)/shard_map/ppermute | solution.py:35
  294.2 18.7 %collective-permute-start.45 = (bf16[96,2048]{1,0:T(8,128)(2,1)S(1)}, bf16[96,2048]{1,0:T(8,128)(2,1)S(1)}, u32[]{:S(2)}, u32[]{:S(2)}) collective-permute-start(bf16[96,2048]{1,0:T(8,128)(2,1)S(1)} %get-tuple-element.106), channel_id=1, source_target_pairs={{0,3},{1,2},{2,1},{3,0},{4,7},{5,6},{6,5},{7,4},{8,11},{9,10},{10,... | collective-permute-start | bytes 1179656 | tf_op jit(solution)/shard_map/ppermute | solution.py:35
  303.9 24.6 %collective-permute-start.37 = (bf16[128,2048]{1,0:T(8,128)(2,1)S(1)}, bf16[128,2048]{1,0:T(8,128)(2,1)S(1)}, u32[]{:S(2)}, u32[]{:S(2)}) collective-permute-start(bf16[128,2048]{1,0:T(8,128)(2,1)S(1)} %add_convert_fusion.2), channel_id=1, source_target_pairs={{0,24},{4,28},{8,16},{12,20},{16,8},{20,12},{24,0},{28,4},{1,25},{... | collective-permute-start | bytes 1572872 | tf_op jit(solution)/shard_map/ppermute | solution.py:35
  313.9 14.7 %collective-permute-start.46 = (bf16[128,2048]{1,0:T(8,128)(2,1)S(1)}, bf16[128,2048]{1,0:T(8,128)(2,1)S(1)}, u32[]{:S(2)}, u32[]{:S(2)}) collective-permute-start(bf16[128,2048]{1,0:T(8,128)(2,1)S(1)} %get-tuple-element.108), channel_id=1, source_target_pairs={{0,4},{4,0},{8,12},{12,8},{16,20},{20,16},{24,28},{28,24},{1,5},{5... | collective-permute-start | bytes 1572872 | tf_op jit(solution)/shard_map/ppermute | solution.py:35
  314.2 25.6 %collective-permute-start.42 = (bf16[128,2048]{1,0:T(8,128)(2,1)S(1)}, bf16[128,2048]{1,0:T(8,128)(2,1)S(1)}, u32[]{:S(2)}, u32[]{:S(2)}) collective-permute-start(bf16[128,2048]{1,0:T(8,128)(2,1)S(1)} %add_convert_fusion.1), channel_id=1, source_target_pairs={{0,8},{4,12},{8,0},{12,4},{16,24},{20,28},{24,16},{28,20},{1,9},{5... | collective-permute-start | bytes 1572872 | tf_op jit(solution)/shard_map/ppermute | solution.py:35
  (31 other events, 472.8 us)
Sparse Core Ops, SparseCore 0:
  22.6 29.4 all-gather.2

commit v3 on v2

--- a/solution.py
+++ b/solution.py
@@ -19,7 +19,8 @@
 
 VMEM = pl.BlockSpec(memory_space=pltpu.VMEM)
 SMEM = pl.BlockSpec(memory_space=pltpu.SMEM)
-PARAMS = pltpu.CompilerParams(vmem_limit_bytes=48 * 1024 * 1024)
+ANY = pl.BlockSpec(memory_space=pl.ANY)
+PARAMS = pltpu.CompilerParams(vmem_limit_bytes=24 * 1024 * 1024)
 
 
 def rms_scale(value_states, norm_gain):
@@ -54,10 +55,52 @@
     return states * cosine + pltpu.roll(states, HEAD_SIZE // 2, 1) * sine
 
 
-def key_value_kernel(tokens, gain, key_weight, value_weight, k_gain, cosine, sine, out):
-    normed = rms_scale(tokens[...].astype(jnp.float32), gain[...]).astype(jnp.bfloat16)
-    keys = jnp.dot(normed, key_weight[...], preferred_element_type=jnp.float32)
-    values = jnp.dot(normed, value_weight[...], preferred_element_type=jnp.float32)
+def load_all(pairs, sems):
+    copies = []
+    for source, target in pairs:
+        part = max(16, source.shape[0] // 4)
+        for first in range(0, source.shape[0], part):
+            here = pl.ds(first, part)
+            copies.append(
+                pltpu.make_async_copy(source.at[here], target.at[here], sems.at[len(copies)])
+            )
+    for copy in copies:
+        copy.start()
+    return copies
+
+
+def own_rows_kernel(
+    experts, tokens, key_weight, value_weight, gain, k_gain, cosine, sine, ids, shares, out, table,
+    rows_in, key_in, value_in, sems,
+):
+    copies = load_all([(tokens, rows_in), (key_weight, key_in), (value_weight, value_in)], sems)
+    rows = tokens.shape[0]
+    chosen_ids = ids[...]
+    lanes = lax.broadcasted_iota(jnp.int32, (experts, rows), 0)
+    chosen = jnp.zeros((experts, rows), jnp.float32)
+    for k in range(TOP):
+        chosen = chosen + jnp.where(lanes == chosen_ids[k : k + 1], 1.0, 0.0)
+    earlier = lax.broadcasted_iota(jnp.int32, (rows, rows), 0) < lax.broadcasted_iota(
+        jnp.int32, (rows, rows), 1
+    )
+    rank = jnp.dot(
+        chosen.astype(jnp.bfloat16),
+        jnp.where(earlier, 1.0, 0.0).astype(jnp.bfloat16),
+        preferred_element_type=jnp.float32,
+    )
+    slots = [
+        jnp.sum(jnp.where(lanes == chosen_ids[k : k + 1], rank, 0.0), axis=0, keepdims=True)
+        for k in range(TOP)
+    ]
+    slots = jnp.concatenate(slots, axis=0)
+    left = jnp.concatenate([chosen_ids, shares[...]], axis=0).astype(jnp.float32)
+    table[:, :rows] = left.astype(jnp.bfloat16)
+    table[:, rows:] = jnp.concatenate([slots, jnp.zeros_like(slots)], axis=0).astype(jnp.bfloat16)
+    for copy in copies:
+        copy.wait()
+    normed = rms_scale(rows_in[...].astype(jnp.float32), gain[...]).astype(jnp.bfloat16)
+    keys = jnp.dot(normed, key_in[...], preferred_element_type=jnp.float32)
+    values = jnp.dot(normed, value_in[...], preferred_element_type=jnp.float32)
     for head in range(out.shape[0]):
         cols = slice(head * HEAD_SIZE, (head + 1) * HEAD_SIZE)
         rotated = normed_rotated(keys[:, cols], k_gain[...], cosine[...], sine[...])
@@ -84,6 +127,7 @@
     heads = w_out.shape[0] // HEAD_SIZE
     width = heads * rows
     span = rows * (place.shape[0] - 2)
+    stride = span + 2 * TOP
     scale = HEAD_SIZE ** (-0.5) * LOG2E
     asked = queries[0]
 
@@ -118,9 +162,9 @@
         jnp.zeros((1, width), jnp.float32),
         jnp.zeros((HEAD_SIZE, width), jnp.float32),
     )
-    state = step(pl.multiple_of(block * span, span), state, True)
+    state = step(pl.multiple_of(block * stride, 2 * TOP), state, True)
     state = lax.fori_loop(
-        0, block, lambda i, s: step(pl.multiple_of(i * span, span), s, False), state
+        0, block, lambda i, s: step(pl.multiple_of(i * stride, 2 * TOP), s, False), state
     )
     _, total, mixed = state
     attended = (mixed / total).astype(jnp.bfloat16)
@@ -144,9 +188,10 @@
 
 def slot_targets(routing, block, expert):
     table = routing[block].astype(jnp.float32)
-    named = table[:TOP] == expert.astype(jnp.float32)
-    slot = jnp.max(jnp.where(named, table[TOP : 2 * TOP], -1.0), axis=0, keepdims=True)
-    weight = jnp.sum(jnp.where(named, table[2 * TOP :], 0.0), axis=0, keepdims=True)
+    rows = table.shape[1] // 2
+    named = table[:TOP, :rows] == expert.astype(jnp.float32)
+    slot = jnp.max(jnp.where(named, table[:TOP, rows:], -1.0), axis=0, keepdims=True)
+    weight = jnp.sum(jnp.where(named, table[TOP:, :rows], 0.0), axis=0, keepdims=True)
     return slot.astype(jnp.int32), weight * (1.0 / 1024.0)
 
 
@@ -191,16 +236,33 @@
         ).astype(jnp.bfloat16)
 
 
-def call(kernel, out_shape, specs, flops, *args, name):
-    outs = out_shape if isinstance(out_shape, list) else [out_shape]
-    moved = sum(a.size * a.dtype.itemsize for a in [*args, *outs])
+def expert_kernel(*refs):
+    count = (len(refs) - 4) // 2
+    came, (w_gate, w_up, w_down), made, hidden = refs[:count], refs[count : count + 3], refs[count + 3 : -1], refs[-1]
+    part = came[0].shape[0]
+    rows = jnp.concatenate([ref[...] for ref in came], axis=0)
+    for first in range(0, hidden.shape[1], 256):
+        cols = slice(first, first + 256)
+        gate = jnp.dot(rows, w_gate[:, cols], preferred_element_type=jnp.float32)
+        up = jnp.dot(rows, w_up[:, cols], preferred_element_type=jnp.float32)
+        hidden[:, cols] = (gate / (1.0 + jnp.exp(-gate)) * up).astype(jnp.bfloat16)
+    for first in range(0, w_down.shape[1], 512):
+        cols = slice(first, first + 512)
+        product = jnp.dot(hidden[...], w_down[:, cols], preferred_element_type=jnp.float32)
+        product = product.astype(jnp.bfloat16)
+        for at, ref in enumerate(made):
+            ref[:, cols] = product[at * part : (at + 1) * part]
+
+
+def call(kernel, out_shape, specs, *args, name, scratch=()):
     return pl.pallas_call(
         kernel,
         out_shape=out_shape,
         in_specs=specs,
         out_specs=jax.tree.map(lambda _: VMEM, out_shape),
+        scratch_shapes=scratch,
         compiler_params=PARAMS,
-        cost_estimate=pl.CostEstimate(flops=flops, bytes_accessed=moved, transcendentals=0),
+        cost_estimate=pl.CostEstimate(flops=1000, bytes_accessed=1000, transcendentals=0),
         name=name,
     )(*args)
 
@@ -233,44 +295,50 @@
     peers = list(range(exp_count))
     bf16 = functools.partial(jax.ShapeDtypeStruct, dtype=jnp.bfloat16)
 
-    pieces = [tokens] + [swap(tokens, "exp", d) for d in peers[1:]]
-
+    pieces = {0: tokens}
+    for d in peers[1:]:
+        if d & (d - 1) == 0:
+            pieces[d] = swap(tokens, "exp", d)
+
+    experts = ctx_count * exp_count
+    capacity = max(2, 3 * rows * TOP // (2 * experts))
+    capacity = -(-capacity // 16) * 16
     ln1_row = ln1_gain.reshape(1, width)
     own_first = me_ctx * ctx_rows + me_exp * rows
     cosine, sine = rope_tables(own_first + jnp.arange(rows))
-    own_kv = call(
-        key_value_kernel,
-        bf16((KEY_VALUE_HEADS, rows, 2 * HEAD_SIZE)),
-        [VMEM] * 7,
-        4 * rows * width * KEY_VALUE_HEADS * HEAD_SIZE,
+    kv_width = key_weight.shape[1]
+    own_kv, table = call(
+        functools.partial(own_rows_kernel, experts),
+        [bf16((KEY_VALUE_HEADS, rows, 2 * HEAD_SIZE)), bf16((2 * TOP, 2 * rows))],
+        [ANY] * 3 + [VMEM] * 6,
         tokens,
-        ln1_row,
         key_weight,
         value_weight,
+        ln1_row,
         k_gain.reshape(1, HEAD_SIZE),
         cosine,
         sine,
-        name="own_kv",
+        expert_ids.T,
+        route_weights.T,
+        name="own_rows",
+        scratch=[
+            pltpu.VMEM((rows, width), jnp.bfloat16),
+            pltpu.VMEM((width, kv_width), jnp.bfloat16),
+            pltpu.VMEM((width, kv_width), jnp.bfloat16),
+            pltpu.SemaphoreType.DMA((12,)),
+        ],
     )
 
     def head_kv(distance):
         head = (me_exp ^ distance) * heads_dev // group_width
         return lax.dynamic_index_in_dim(own_kv, head, 0, keepdims=False)
 
-    block_kv = jnp.concatenate(
-        [head_kv(0)] + [swap(head_kv(d), "exp", d) for d in peers[1:]], axis=0
-    )
-    both = lax.all_gather(block_kv, "ctx", axis=0, tiled=True)
-
-    experts = ctx_count * exp_count
-    capacity = max(2, 3 * rows * TOP // (2 * experts))
-    capacity = -(-capacity // 16) * 16
-    chosen = expert_ids[:, :, None] == jnp.arange(experts)[None, None, :]
-    counts = jnp.sum(chosen, axis=1, dtype=jnp.int32)
-    rank_table = jnp.cumsum(counts, axis=0, dtype=jnp.int32) - counts
-    slot_index = jnp.sum(jnp.where(chosen, rank_table[:, None, :], 0), axis=2)
-    routing = jnp.concatenate([expert_ids, slot_index, route_weights], axis=1).T
-    routing = lax.all_gather(tie(routing.astype(jnp.bfloat16), both), "ctx", axis=0)
+    block_kv = [head_kv(0)] + [swap(head_kv(d), "exp", d) for d in peers[1:]]
+    for d in peers[1:]:
+        if d not in pieces:
+            pieces[d] = swap(tie(tokens, *block_kv[1:]), "exp", d)
+    both = lax.all_gather(jnp.concatenate(block_kv + [table], axis=0), "ctx", axis=0, tiled=True)
+    routing = both.reshape(ctx_count, ctx_rows + 2 * TOP, 2 * HEAD_SIZE)[:, ctx_rows:]
 
     positions = jnp.concatenate(
         [me_ctx * ctx_rows + (me_exp ^ d) * rows + jnp.arange(rows) for d in peers]
@@ -280,8 +348,7 @@
         query_kernel,
         bf16((exp_count, heads_dev * rows, HEAD_SIZE)),
         [VMEM] * (exp_count + 5),
-        2 * ctx_rows * width * w_query.shape[1],
-        *pieces,
+        *[pieces[d] for d in peers],
         ln1_row,
         w_query,
         q_gain.reshape(1, HEAD_SIZE),
@@ -297,7 +364,6 @@
             functools.partial(attention_kernel, d, rows),
             bf16((rows, width)),
             [SMEM, VMEM, VMEM, VMEM],
-            4 * rows * w_query.shape[1] * both.shape[0] + 2 * rows * w_out.size,
             place,
             tie(queries[d : d + 1], *last),
             both,
@@ -310,7 +376,6 @@
         residual_kernel,
         [bf16((rows, width)), bf16((rows, width))],
         [VMEM] * (exp_count + 2),
-        10 * rows * width,
         tokens,
         *parts,
         ln2_gain.reshape(1, width),
@@ -329,7 +394,6 @@
             functools.partial(dispatch_kernel, g, capacity),
             [bf16((2 * capacity, width)) for _ in peers],
             [SMEM, VMEM, VMEM, VMEM],
-            4 * exp_count * capacity * rows * width,
             place,
             routing,
             far[g],
@@ -346,13 +410,17 @@
     mixture = residual.astype(jnp.float32)
     produced = {}
     for g in range(groups):
-        flat_rows = jnp.concatenate(arrived[g], axis=0)
-        gate_act = jnp.dot(flat_rows, w_gate[0], preferred_element_type=jnp.float32)
-        up_act = jnp.dot(flat_rows, w_up[0], preferred_element_type=jnp.float32)
-        hidden = (jax.nn.silu(gate_act) * up_act).astype(jnp.bfloat16)
-        made = jnp.dot(hidden, w_down[0], preferred_element_type=jnp.float32)
-        made = made.astype(jnp.bfloat16)
-        produced[g] = [made[d * 2 * capacity : (d + 1) * 2 * capacity] for d in peers]
+        produced[g] = call(
+            expert_kernel,
+            [bf16((2 * capacity, width)) for _ in peers],
+            [VMEM] * (exp_count + 3),
+            *arrived[g],
+            w_gate[0],
+            w_up[0],
+            w_down[0],
+            name="expert",
+            scratch=[pltpu.VMEM((2 * capacity * exp_count, w_gate.shape[2]), jnp.bfloat16)],
+        )
     for g in turns:
         back = [produced[g][0]]
         for d in peers[1:]:
@@ -362,7 +430,6 @@
             functools.partial(combine_kernel, g, capacity),
             [bf16((rows, width)), bf16((rows, width))],
             [SMEM, VMEM] + [VMEM] * exp_count,
-            4 * exp_count * capacity * rows * width,
             place,
             routing,
             *back,

time: 349 us -> 300 us (0.86)
  matrix products: 39.5 us -> 0 us
  starting transfers between devices: 64.7 us -> 98 us
  blocking collectives: 30.6 us -> 0 us
  local copies, waits for them, and re-layouts: 30 us -> 12.1 us
  Pallas kernels: 26.4 us -> 35.3 us
    dot_general x8 -> x0, matrix products: 39.5 us -> none  [the longest x4 27.6 us: shards(): made = jnp.dot(hidden, w_down[0], preferred_element_type=jnp.float32)]
    ppermute x47, starting transfers between devices: 64.7 us -> 98 us  [swap(): return lax.ppermute(array, axis, pairs)]
    all_gather x1 -> x0, blocking collectives: 30.6 us -> none  [shards(): lax.all_gather(tie(routing.astype(jnp.bfloat16), both), 'ctx', axis=0)]
    unnamed x74 -> x46, local copies, waits for them, and re-layouts: 22.3 us -> 12 us
    pallas_call x15 -> x19, Pallas kernels: 26.4 us -> 35.3 us  [call(): pl.pallas_call(kernel, out_shape=out_shape, in_specs=specs, out_specs=jax...]
    slice x4 -> x1, local copies, waits for them, and re-layouts: 4.71 us -> 0.01 us  [shards(): both.reshape(ctx_count, ctx_rows + 2 * TOP, 2 * HEAD_SIZE)[:, ctx_rows:]]
  transfers between devices with their start and end apart: 48 -> 48, of which waited for: 21 -> 27; matrix products, arithmetic and copies ran while one was open for 16% -> 1% of each run, Pallas kernels for 6% -> 9%
where the time goes in v3:
time: 300 us
  waiting for transfers between devices  137 us (46%)
  starting transfers between devices  98 us (33%)
  Pallas kernels  35.3 us (12%)
  between operations  13.9 us (5%)
  local copies, waits for them, and re-layouts  12.1 us (4%)
  other arithmetic  3.54 us (1%)
    ppermute x47, waiting for transfers between devices, swap(): return lax.ppermute(array, axis, pairs)  136 us
    ppermute x47, starting transfers between devices, swap(): return lax.ppermute(array, axis, pairs)  98 us
    pallas_call x19, Pallas kernels, call(): pl.pallas_call(kernel, out_shape=out_shape, in_specs=specs, out_specs=jax...  35.3 us
    unnamed x46, local copies, waits for them, and re-layouts  12 us
  transfers between devices with their start and end apart: 48, of which 27 were waited for; matrix products, arithmetic and copies ran while one was open for 1% of the time, Pallas kernels for 9%

profile of v3, /device:TPU:0, one launch (start us, length us, event | category | flops | bytes accessed | tf_op | source)
XLA Modules:
  0.0 299.7 jit_solution(6041527864303879729)
XLA Ops:
  15.2 4.0 %collective-permute-start.4 = (bf16[128,256]{1,0:T(8,128)(2,1)S(1)}, bf16[128,256]{1,0:T(8,128)(2,1)S(1)}, u32[]{:S(2)}, u32[]{:S(2)}) collective-permute-start(bf16[128,256]{1,0:T(8,128)(2,1)S(1)} %get-tuple-element.149), channel_id=1, source_target_pairs={{0,3},{1,2},{2,1},{3,0},{4,7},{5,6},{6,5},{7,4},{8,11},{9,10},{10,... | collective-permute-start | bytes 196616 | tf_op jit(solution)/shard_map/ppermute | solution.py:36
  19.8 4.1 %collective-permute-done.2 = bf16[128,256]{1,0:T(8,128)(2,1)S(1)} collective-permute-done((bf16[128,256]{1,0:T(8,128)(2,1)S(1)}, bf16[128,256]{1,0:T(8,128)(2,1)S(1)}, u32[]{:S(2)}, u32[]{:S(2)}) %collective-permute-start.2) | collective-permute-done | bytes 65568 | tf_op jit(solution)/shard_map/ppermute | solution.py:36
  29.7 9.0 %collective-permute-done.1.refs_2_ = bf16[128,2048]{1,0:T(8,128)(2,1)S(1)} collective-permute-done((bf16[128,2048]{1,0:T(8,128)(2,1)S(1)}, bf16[128,2048]{1,0:T(8,128)(2,1)S(1)}, u32[]{:S(2)}, u32[]{:S(2)}) %collective-permute-start.1) | collective-permute-done | bytes 524320 | tf_op jit(solution)/shard_map/ppermute | solution.py:36
  38.8 2.4 collective-permute-done.refs_1_
  42.0 7.6 %collective-permute-done.5.refs_3_ = bf16[128,2048]{1,0:T(8,128)(2,1)S(1)} collective-permute-done((bf16[128,2048]{1,0:T(8,128)(2,1)S(1)}, bf16[128,2048]{1,0:T(8,128)(2,1)S(1)}, u32[]{:S(2)}, u32[]{:S(2)}) %collective-permute-start.5) | collective-permute-done | bytes 524320 | tf_op jit(solution)/shard_map/ppermute | solution.py:36
  65.2 1.9 attention.7.refs_1_
  67.1 7.9 %collective-permute-done.8.refs_4_ = bf16[128,2048]{1,0:T(8,128)(2,1)S(1)} collective-permute-done((bf16[128,2048]{1,0:T(8,128)(2,1)S(1)}, bf16[128,2048]{1,0:T(8,128)(2,1)S(1)}, u32[]{:S(2)}, u32[]{:S(2)}) %collective-permute-start.8) | collective-permute-done | bytes 524320 | tf_op jit(solution)/shard_map/ppermute | solution.py:36
  76.7 11.2 %collective-permute-done.6.refs_2_ = bf16[128,2048]{1,0:T(8,128)(2,1)S(1)} collective-permute-done((bf16[128,2048]{1,0:T(8,128)(2,1)S(1)}, bf16[128,2048]{1,0:T(8,128)(2,1)S(1)}, u32[]{:S(2)}, u32[]{:S(2)}) %collective-permute-start.6) | collective-permute-done | bytes 524320 | tf_op jit(solution)/shard_map/ppermute | solution.py:36
  88.5 5.9 %collective-permute-start.11 = (bf16[128,2048]{1,0:T(8,128)(2,1)S(1)}, bf16[128,2048]{1,0:T(8,128)(2,1)S(1)}, u32[]{:S(2)}, u32[]{:S(2)}) collective-permute-start(bf16[128,2048]{1,0:T(8,128)(2,1)S(1)} %get-tuple-element.101.same), channel_id=1, source_target_pairs={{0,8},{4,12},{8,0},{12,4},{16,24},{20,28},{24,16},{28,20},{1,9},{5... | collective-permute-start | bytes 1572872 | tf_op jit(solution)/shard_map/ppermute | solution.py:36
  95.1 10.7 %collective-permute-start.9 = (bf16[128,2048]{1,0:T(8,128)(2,1)S(1)}, bf16[128,2048]{1,0:T(8,128)(2,1)S(1)}, u32[]{:S(2)}, u32[]{:S(2)}) collective-permute-start(bf16[128,2048]{1,0:T(8,128)(2,1)S(1)} %get-tuple-element.101.same), channel_id=1, source_target_pairs={{0,16},{4,20},{8,24},{12,28},{16,0},{20,4},{24,8},{28,12},{1,17},{... | collective-permute-start | bytes 1572872 | tf_op jit(solution)/shard_map/ppermute | solution.py:36
  108.2 11.6 %collective-permute-start.17 = (bf16[96,2048]{1,0:T(8,128)(2,1)S(1)}, bf16[96,2048]{1,0:T(8,128)(2,1)S(1)}, u32[]{:S(2)}, u32[]{:S(2)}) collective-permute-start(bf16[96,2048]{1,0:T(8,128)(2,1)S(1)} %get-tuple-element.91), channel_id=1, source_target_pairs={{0,2},{1,3},{2,0},{3,1},{4,6},{5,7},{6,4},{7,5},{8,10},{9,11},{10,... | collective-permute-start | bytes 1179656 | tf_op jit(solution)/shard_map/ppermute | solution.py:36
  119.8 2.4 collective-permute-start.14
  122.2 7.4 %collective-permute-done.9.same = bf16[128,2048]{1,0:T(8,128)(2,1)S(1)} collective-permute-done((bf16[128,2048]{1,0:T(8,128)(2,1)S(1)}, bf16[128,2048]{1,0:T(8,128)(2,1)S(1)}, u32[]{:S(2)}, u32[]{:S(2)}) %collective-permute-start.9) | collective-permute-done | bytes 524320 | tf_op jit(solution)/shard_map/ppermute | solution.py:36
  129.7 2.2 collective-permute-start.23
  134.9 5.3 %collective-permute-done.20.refs_3_ = bf16[96,2048]{1,0:T(8,128)(2,1)S(1)} collective-permute-done((bf16[96,2048]{1,0:T(8,128)(2,1)S(1)}, bf16[96,2048]{1,0:T(8,128)(2,1)S(1)}, u32[]{:S(2)}, u32[]{:S(2)}) %collective-permute-start.20) | collective-permute-done | bytes 393248 | tf_op jit(solution)/shard_map/ppermute | solution.py:36
  140.2 3.4 %collective-permute-start.21 = (bf16[96,2048]{1,0:T(8,128)(2,1)S(1)}, bf16[96,2048]{1,0:T(8,128)(2,1)S(1)}, u32[]{:S(2)}, u32[]{:S(2)}) collective-permute-start(bf16[96,2048]{1,0:T(8,128)(2,1)S(1)} %get-tuple-element.97), channel_id=1, source_target_pairs={{0,3},{1,2},{2,1},{3,0},{4,7},{5,6},{6,5},{7,4},{8,11},{9,10},{10,... | collective-permute-start | bytes 1179656 | tf_op jit(solution)/shard_map/ppermute | solution.py:36
  146.4 2.0 collective-permute-done.18.refs_2_
  148.4 2.0 collective-permute-start.19
  150.4 2.1 collective-permute-start.16
  152.5 4.6 %collective-permute-done.21.refs_3_ = bf16[96,2048]{1,0:T(8,128)(2,1)S(1)} collective-permute-done((bf16[96,2048]{1,0:T(8,128)(2,1)S(1)}, bf16[96,2048]{1,0:T(8,128)(2,1)S(1)}, u32[]{:S(2)}, u32[]{:S(2)}) %collective-permute-start.21) | collective-permute-done | bytes 393248 | tf_op jit(solution)/shard_map/ppermute | solution.py:36
  157.1 3.4 %collective-permute-start.22 = (bf16[96,2048]{1,0:T(8,128)(2,1)S(1)}, bf16[96,2048]{1,0:T(8,128)(2,1)S(1)}, u32[]{:S(2)}, u32[]{:S(2)}) collective-permute-start(bf16[96,2048]{1,0:T(8,128)(2,1)S(1)} %get-tuple-element.98), channel_id=1, source_target_pairs={{0,3},{1,2},{2,1},{3,0},{4,7},{5,6},{6,5},{7,4},{8,11},{9,10},{10,... | collective-permute-start | bytes 1179656 | tf_op jit(solution)/shard_map/ppermute | solution.py:36
  161.6 3.8 %collective-permute-done.19.refs_2_ = bf16[96,2048]{1,0:T(8,128)(2,1)S(1)} collective-permute-done((bf16[96,2048]{1,0:T(8,128)(2,1)S(1)}, bf16[96,2048]{1,0:T(8,128)(2,1)S(1)}, u32[]{:S(2)}, u32[]{:S(2)}) %collective-permute-start.19) | collective-permute-done | bytes 393248 | tf_op jit(solution)/shard_map/ppermute | solution.py:36
  165.3 2.0 collective-permute-start.27
  167.3 2.1 collective-permute-start.25
  169.4 4.6 %collective-permute-done.22.refs_3_ = bf16[96,2048]{1,0:T(8,128)(2,1)S(1)} collective-permute-done((bf16[96,2048]{1,0:T(8,128)(2,1)S(1)}, bf16[96,2048]{1,0:T(8,128)(2,1)S(1)}, u32[]{:S(2)}, u32[]{:S(2)}) %collective-permute-start.22) | collective-permute-done | bytes 393248 | tf_op jit(solution)/shard_map/ppermute | solution.py:36
  174.0 3.4 %collective-permute-start.29 = (bf16[96,2048]{1,0:T(8,128)(2,1)S(1)}, bf16[96,2048]{1,0:T(8,128)(2,1)S(1)}, u32[]{:S(2)}, u32[]{:S(2)}) collective-permute-start(bf16[96,2048]{1,0:T(8,128)(2,1)S(1)} %get-tuple-element.111), channel_id=1, source_target_pairs={{0,3},{1,2},{2,1},{3,0},{4,7},{5,6},{6,5},{7,4},{8,11},{9,10},{10,... | collective-permute-start | bytes 1179656 | tf_op jit(solution)/shard_map/ppermute | solution.py:36
  177.4 3.8 %expert.4 = (bf16[96,2048]{1,0:T(8,128)(2,1)S(1)}, bf16[96,2048]{1,0:T(8,128)(2,1)S(1)}, bf16[96,2048]{1,0:T(8,128)(2,1)S(1)}, bf16[96,2048]{1,0:T(8,128)(2,1)S(1)}) custom-call(bf16[96,2048]{1,0:T(8,128)(2,1)S(1)} %get-tuple-element.83.refs_0_, bf16[96,2048]{1,0:T(8,128)(2,1)S(1)} %collective-permute-done.16.refs_1_, ...), custom_call_target="tpu_custom_call" | custom-call | flops 1000 | bytes 1000 | tf_op jit(solution)/shard_map/expert/pallas_call | solution.py:258
  182.2 2.0 collective-permute-start.28
  184.2 2.1 collective-permute-start.26
  186.3 4.6 %collective-permute-done.29.refs_3_ = bf16[96,2048]{1,0:T(8,128)(2,1)S(1)} collective-permute-done((bf16[96,2048]{1,0:T(8,128)(2,1)S(1)}, bf16[96,2048]{1,0:T(8,128)(2,1)S(1)}, u32[]{:S(2)}, u32[]{:S(2)}) %collective-permute-start.29) | collective-permute-done | bytes 393248 | tf_op jit(solution)/shard_map/ppermute | solution.py:36
  190.9 3.4 %collective-permute-start.30 = (bf16[96,2048]{1,0:T(8,128)(2,1)S(1)}, bf16[96,2048]{1,0:T(8,128)(2,1)S(1)}, u32[]{:S(2)}, u32[]{:S(2)}) collective-permute-start(bf16[96,2048]{1,0:T(8,128)(2,1)S(1)} %get-tuple-element.112), channel_id=1, source_target_pairs={{0,3},{1,2},{2,1},{3,0},{4,7},{5,6},{6,5},{7,4},{8,11},{9,10},{10,... | collective-permute-start | bytes 1179656 | tf_op jit(solution)/shard_map/ppermute | solution.py:36
  194.3 3.9 %expert.5 = (bf16[96,2048]{1,0:T(8,128)(2,1)S(1)}, bf16[96,2048]{1,0:T(8,128)(2,1)S(1)}, bf16[96,2048]{1,0:T(8,128)(2,1)S(1)}, bf16[96,2048]{1,0:T(8,128)(2,1)S(1)}) custom-call(bf16[96,2048]{1,0:T(8,128)(2,1)S(1)} %get-tuple-element.115.refs_0_, bf16[96,2048]{1,0:T(8,128)(2,1)S(1)} %collective-permute-done.25.refs_1_, ...), custom_call_target="tpu_custom_call" | custom-call | flops 1000 | bytes 1000 | tf_op jit(solution)/shard_map/expert/pallas_call | solution.py:258
  199.1 2.0 collective-permute-start.34
  201.1 2.1 collective-permute-start.33
  203.2 4.6 %collective-permute-done.30.refs_3_ = bf16[96,2048]{1,0:T(8,128)(2,1)S(1)} collective-permute-done((bf16[96,2048]{1,0:T(8,128)(2,1)S(1)}, bf16[96,2048]{1,0:T(8,128)(2,1)S(1)}, u32[]{:S(2)}, u32[]{:S(2)}) %collective-permute-start.30) | collective-permute-done | bytes 393248 | tf_op jit(solution)/shard_map/ppermute | solution.py:36
  207.8 3.4 %collective-permute-start.35 = (bf16[96,2048]{1,0:T(8,128)(2,1)S(1)}, bf16[96,2048]{1,0:T(8,128)(2,1)S(1)}, u32[]{:S(2)}, u32[]{:S(2)}) collective-permute-start(bf16[96,2048]{1,0:T(8,128)(2,1)S(1)} %get-tuple-element.122), channel_id=1, source_target_pairs={{0,3},{1,2},{2,1},{3,0},{4,7},{5,6},{6,5},{7,4},{8,11},{9,10},{10,... | collective-permute-start | bytes 1179656 | tf_op jit(solution)/shard_map/ppermute | solution.py:36
  212.3 4.1 %expert.6 = (bf16[96,2048]{1,0:T(8,128)(2,1)S(1)}, bf16[96,2048]{1,0:T(8,128)(2,1)S(1)}, bf16[96,2048]{1,0:T(8,128)(2,1)S(1)}, bf16[96,2048]{1,0:T(8,128)(2,1)S(1)}) custom-call(bf16[96,2048]{1,0:T(8,128)(2,1)S(1)} %get-tuple-element.125.refs_0_, bf16[96,2048]{1,0:T(8,128)(2,1)S(1)} %collective-permute-done.15.refs_1_, ...), custom_call_target="tpu_custom_call" | custom-call | flops 1000 | bytes 1000 | tf_op jit(solution)/shard_map/expert/pallas_call | solution.py:258
  218.0 2.1 collective-permute-start.38
  220.1 4.6 %collective-permute-done.35.refs_3_ = bf16[96,2048]{1,0:T(8,128)(2,1)S(1)} collective-permute-done((bf16[96,2048]{1,0:T(8,128)(2,1)S(1)}, bf16[96,2048]{1,0:T(8,128)(2,1)S(1)}, u32[]{:S(2)}, u32[]{:S(2)}) %collective-permute-start.35) | collective-permute-done | bytes 393248 | tf_op jit(solution)/shard_map/ppermute | solution.py:36
  224.7 3.4 %collective-permute-start.40 = (bf16[96,2048]{1,0:T(8,128)(2,1)S(1)}, bf16[96,2048]{1,0:T(8,128)(2,1)S(1)}, u32[]{:S(2)}, u32[]{:S(2)}) collective-permute-start(bf16[96,2048]{1,0:T(8,128)(2,1)S(1)} %get-tuple-element.132), channel_id=1, source_target_pairs={{0,3},{1,2},{2,1},{3,0},{4,7},{5,6},{6,5},{7,4},{8,11},{9,10},{10,... | collective-permute-start | bytes 1179656 | tf_op jit(solution)/shard_map/ppermute | solution.py:36
  229.2 3.8 %expert.7 = (bf16[96,2048]{1,0:T(8,128)(2,1)S(1)}, bf16[96,2048]{1,0:T(8,128)(2,1)S(1)}, bf16[96,2048]{1,0:T(8,128)(2,1)S(1)}, bf16[96,2048]{1,0:T(8,128)(2,1)S(1)}) custom-call(bf16[96,2048]{1,0:T(8,128)(2,1)S(1)} %get-tuple-element.135.refs_0_, bf16[96,2048]{1,0:T(8,128)(2,1)S(1)} %collective-permute-done.14.refs_1_, ...), custom_call_target="tpu_custom_call" | custom-call | flops 1000 | bytes 1000 | tf_op jit(solution)/shard_map/expert/pallas_call | solution.py:258
  233.5 7.4 %collective-permute-done.40.refs_3_ = bf16[96,2048]{1,0:T(8,128)(2,1)S(1)} collective-permute-done((bf16[96,2048]{1,0:T(8,128)(2,1)S(1)}, bf16[96,2048]{1,0:T(8,128)(2,1)S(1)}, u32[]{:S(2)}, u32[]{:S(2)}) %collective-permute-start.40) | collective-permute-done | bytes 393248 | tf_op jit(solution)/shard_map/ppermute | solution.py:36
  242.2 3.1 %collective-permute-start.32 = (bf16[128,2048]{1,0:T(8,128)(2,1)S(1)}, bf16[128,2048]{1,0:T(8,128)(2,1)S(1)}, u32[]{:S(2)}, u32[]{:S(2)}) collective-permute-start(bf16[128,2048]{1,0:T(8,128)(2,1)S(1)} %add_convert_fusion.3), channel_id=1, source_target_pairs={{0,16},{4,20},{8,24},{12,28},{16,0},{20,4},{24,8},{28,12},{1,17},{... | collective-permute-start | bytes 1572872 | tf_op jit(solution)/shard_map/ppermute | solution.py:36
  248.9 7.6 %collective-permute-done.44.refs_2_ = bf16[96,2048]{1,0:T(8,128)(2,1)S(1)} collective-permute-done((bf16[96,2048]{1,0:T(8,128)(2,1)S(1)}, bf16[96,2048]{1,0:T(8,128)(2,1)S(1)}, u32[]{:S(2)}, u32[]{:S(2)}) %collective-permute-start.44) | collective-permute-done | bytes 393248 | tf_op jit(solution)/shard_map/ppermute | solution.py:36
  256.5 2.3 collective-permute-start.37
  258.8 7.3 %collective-permute-done.45.refs_3_ = bf16[96,2048]{1,0:T(8,128)(2,1)S(1)} collective-permute-done((bf16[96,2048]{1,0:T(8,128)(2,1)S(1)}, bf16[96,2048]{1,0:T(8,128)(2,1)S(1)}, u32[]{:S(2)}, u32[]{:S(2)}) %collective-permute-start.45) | collective-permute-done | bytes 393248 | tf_op jit(solution)/shard_map/ppermute | solution.py:36
  268.7 11.9 %collective-permute-done.32 = bf16[128,2048]{1,0:T(8,128)(2,1)S(1)} collective-permute-done((bf16[128,2048]{1,0:T(8,128)(2,1)S(1)}, bf16[128,2048]{1,0:T(8,128)(2,1)S(1)}, u32[]{:S(2)}, u32[]{:S(2)}) %collective-permute-start.32) | collective-permute-done | bytes 524320 | tf_op jit(solution)/shard_map/ppermute | solution.py:36
  280.6 11.0 %collective-permute-done.42 = bf16[128,2048]{1,0:T(8,128)(2,1)S(1)} collective-permute-done((bf16[128,2048]{1,0:T(8,128)(2,1)S(1)}, bf16[128,2048]{1,0:T(8,128)(2,1)S(1)}, u32[]{:S(2)}, u32[]{:S(2)}) %collective-permute-start.42) | collective-permute-done | bytes 524320 | tf_op jit(solution)/shard_map/ppermute | solution.py:36
  (135 shorter events, 58.6 us)
Async XLA Ops:
  6.5 48.3 %all-gather.2.cloned.1.call-start = ((), (), s32[]{:S(2)}) async-start(), calls=%async_computation | async-start | bytes 2433024 | tf_op jit(solution)/shard_map/all_gather | solution.py:340
  15.2 8.8 %collective-permute-start.4 = (bf16[128,256]{1,0:T(8,128)(2,1)S(1)}, bf16[128,256]{1,0:T(8,128)(2,1)S(1)}, u32[]{:S(2)}, u32[]{:S(2)}) collective-permute-start(bf16[128,256]{1,0:T(8,128)(2,1)S(1)} %get-tuple-element.149), channel_id=1, source_target_pairs={{0,3},{1,2},{2,1},{3,0},{4,7},{5,6},{6,5},{7,4},{8,11},{9,10},{10,... | collective-permute-start | bytes 196616 | tf_op jit(solution)/shard_map/ppermute | solution.py:36
  19.2 4.8 %collective-permute-start.3 = (bf16[128,256]{1,0:T(8,128)(2,1)S(1)}, bf16[128,256]{1,0:T(8,128)(2,1)S(1)}, u32[]{:S(2)}, u32[]{:S(2)}) collective-permute-start(bf16[128,256]{1,0:T(8,128)(2,1)S(1)} %get-tuple-element.150), channel_id=1, source_target_pairs={{0,2},{1,3},{2,0},{3,1},{4,6},{5,7},{6,4},{7,5},{8,10},{9,11},{10,... | collective-permute-start | bytes 196616 | tf_op jit(solution)/shard_map/ppermute | solution.py:36
  19.7 4.3 %collective-permute-start.2 = (bf16[128,256]{1,0:T(8,128)(2,1)S(1)}, bf16[128,256]{1,0:T(8,128)(2,1)S(1)}, u32[]{:S(2)}, u32[]{:S(2)}) collective-permute-start(bf16[128,256]{1,0:T(8,128)(2,1)S(1)} %get-tuple-element.151), channel_id=1, source_target_pairs={{0,1},{1,0},{2,3},{3,2},{4,5},{5,4},{6,7},{7,6},{8,9},{9,8},{10,11... | collective-permute-start | bytes 196616 | tf_op jit(solution)/shard_map/ppermute | solution.py:36
  24.7 14.0 %collective-permute-start.1 = (bf16[128,2048]{1,0:T(8,128)(2,1)S(1)}, bf16[128,2048]{1,0:T(8,128)(2,1)S(1)}, u32[]{:S(2)}, u32[]{:S(2)}) collective-permute-start(bf16[128,2048]{1,0:T(8,128)(2,1)S(1)} %copy-done.7), channel_id=1, source_target_pairs={{0,2},{1,3},{2,0},{3,1},{4,6},{5,7},{6,4},{7,5},{8,10},{9,11},{10,... | collective-permute-start | bytes 1572872 | tf_op jit(solution)/shard_map/ppermute | solution.py:36
  26.3 14.9 %collective-permute-start = (bf16[128,2048]{1,0:T(8,128)(2,1)S(1)}, bf16[128,2048]{1,0:T(8,128)(2,1)S(1)}, u32[]{:S(2)}, u32[]{:S(2)}) collective-permute-start(bf16[128,2048]{1,0:T(8,128)(2,1)S(1)} %copy-done.7), channel_id=1, source_target_pairs={{0,1},{1,0},{2,3},{3,2},{4,5},{5,4},{6,7},{7,6},{8,9},{9,8},{10,11... | collective-permute-start | bytes 1572872 | tf_op jit(solution)/shard_map/ppermute | solution.py:36
  26.9 22.7 %collective-permute-start.5 = (bf16[128,2048]{1,0:T(8,128)(2,1)S(1)}, bf16[128,2048]{1,0:T(8,128)(2,1)S(1)}, u32[]{:S(2)}, u32[]{:S(2)}) collective-permute-start(bf16[128,2048]{1,0:T(8,128)(2,1)S(1)} %copy-done.7), channel_id=1, source_target_pairs={{0,3},{1,2},{2,1},{3,0},{4,7},{5,6},{6,5},{7,4},{8,11},{9,10},{10,... | collective-permute-start | bytes 1572872 | tf_op jit(solution)/shard_map/ppermute | solution.py:36
  61.6 13.3 %collective-permute-start.8 = (bf16[128,2048]{1,0:T(8,128)(2,1)S(1)}, bf16[128,2048]{1,0:T(8,128)(2,1)S(1)}, u32[]{:S(2)}, u32[]{:S(2)}) collective-permute-start(bf16[128,2048]{1,0:T(8,128)(2,1)S(1)} %attention.6), channel_id=1, source_target_pairs={{0,2},{1,3},{2,0},{3,1},{4,6},{5,7},{6,4},{7,5},{8,10},{9,11},{10,... | collective-permute-start | bytes 1572872 | tf_op jit(solution)/shard_map/ppermute | solution.py:36
  63.2 13.6 %collective-permute-start.7 = (bf16[128,2048]{1,0:T(8,128)(2,1)S(1)}, bf16[128,2048]{1,0:T(8,128)(2,1)S(1)}, u32[]{:S(2)}, u32[]{:S(2)}) collective-permute-start(bf16[128,2048]{1,0:T(8,128)(2,1)S(1)} %attention.5), channel_id=1, source_target_pairs={{0,1},{1,0},{2,3},{3,2},{4,5},{5,4},{6,7},{7,6},{8,9},{9,8},{10,11... | collective-permute-start | bytes 1572872 | tf_op jit(solution)/shard_map/ppermute | solution.py:36
  64.6 23.3 %collective-permute-start.6 = (bf16[128,2048]{1,0:T(8,128)(2,1)S(1)}, bf16[128,2048]{1,0:T(8,128)(2,1)S(1)}, u32[]{:S(2)}, u32[]{:S(2)}) collective-permute-start(bf16[128,2048]{1,0:T(8,128)(2,1)S(1)} %attention.4), channel_id=1, source_target_pairs={{0,3},{1,2},{2,1},{3,0},{4,7},{5,6},{6,5},{7,4},{8,11},{9,10},{10,... | collective-permute-start | bytes 1572872 | tf_op jit(solution)/shard_map/ppermute | solution.py:36
  88.5 18.5 %collective-permute-start.11 = (bf16[128,2048]{1,0:T(8,128)(2,1)S(1)}, bf16[128,2048]{1,0:T(8,128)(2,1)S(1)}, u32[]{:S(2)}, u32[]{:S(2)}) collective-permute-start(bf16[128,2048]{1,0:T(8,128)(2,1)S(1)} %get-tuple-element.101.same), channel_id=1, source_target_pairs={{0,8},{4,12},{8,0},{12,4},{16,24},{20,28},{24,16},{28,20},{1,9},{5... | collective-permute-start | bytes 1572872 | tf_op jit(solution)/shard_map/ppermute | solution.py:36
  94.4 12.6 %collective-permute-start.13 = (bf16[128,2048]{1,0:T(8,128)(2,1)S(1)}, bf16[128,2048]{1,0:T(8,128)(2,1)S(1)}, u32[]{:S(2)}, u32[]{:S(2)}) collective-permute-start(bf16[128,2048]{1,0:T(8,128)(2,1)S(1)} %get-tuple-element.101.same), channel_id=1, source_target_pairs={{0,4},{4,0},{8,12},{12,8},{16,20},{20,16},{24,28},{28,24},{1,5},{5... | collective-permute-start | bytes 1572872 | tf_op jit(solution)/shard_map/ppermute | solution.py:36
  95.1 34.5 %collective-permute-start.9 = (bf16[128,2048]{1,0:T(8,128)(2,1)S(1)}, bf16[128,2048]{1,0:T(8,128)(2,1)S(1)}, u32[]{:S(2)}, u32[]{:S(2)}) collective-permute-start(bf16[128,2048]{1,0:T(8,128)(2,1)S(1)} %get-tuple-element.101.same), channel_id=1, source_target_pairs={{0,16},{4,20},{8,24},{12,28},{16,0},{20,4},{24,8},{28,12},{1,17},{... | collective-permute-start | bytes 1572872 | tf_op jit(solution)/shard_map/ppermute | solution.py:36
  107.0 24.9 %collective-permute-start.12 = (bf16[128,2048]{1,0:T(8,128)(2,1)S(1)}, bf16[128,2048]{1,0:T(8,128)(2,1)S(1)}, u32[]{:S(2)}, u32[]{:S(2)}) collective-permute-start(bf16[128,2048]{1,0:T(8,128)(2,1)S(1)} %collective-permute-done.11.same), channel_id=1, source_target_pairs={{0,4},{4,0},{8,12},{12,8},{16,20},{20,16},{24,28},{28,24},{1,5},{5... | collective-permute-start | bytes 1572872 | tf_op jit(solution)/shard_map/ppermute | solution.py:36
  108.2 24.8 %collective-permute-start.17 = (bf16[96,2048]{1,0:T(8,128)(2,1)S(1)}, bf16[96,2048]{1,0:T(8,128)(2,1)S(1)}, u32[]{:S(2)}, u32[]{:S(2)}) collective-permute-start(bf16[96,2048]{1,0:T(8,128)(2,1)S(1)} %get-tuple-element.91), channel_id=1, source_target_pairs={{0,2},{1,3},{2,0},{3,1},{4,6},{5,7},{6,4},{7,5},{8,10},{9,11},{10,... | collective-permute-start | bytes 1179656 | tf_op jit(solution)/shard_map/ppermute | solution.py:36
  119.8 14.7 %collective-permute-start.14 = (bf16[96,2048]{1,0:T(8,128)(2,1)S(1)}, bf16[96,2048]{1,0:T(8,128)(2,1)S(1)}, u32[]{:S(2)}, u32[]{:S(2)}) collective-permute-start(bf16[96,2048]{1,0:T(8,128)(2,1)S(1)} %get-tuple-element.86), channel_id=1, source_target_pairs={{0,1},{1,0},{2,3},{3,2},{4,5},{5,4},{6,7},{7,6},{8,9},{9,8},{10,11... | collective-permute-start | bytes 1179656 | tf_op jit(solution)/shard_map/ppermute | solution.py:36
  122.2 18.0 %collective-permute-start.20 = (bf16[96,2048]{1,0:T(8,128)(2,1)S(1)}, bf16[96,2048]{1,0:T(8,128)(2,1)S(1)}, u32[]{:S(2)}, u32[]{:S(2)}) collective-permute-start(bf16[96,2048]{1,0:T(8,128)(2,1)S(1)} %get-tuple-element.96), channel_id=1, source_target_pairs={{0,3},{1,2},{2,1},{3,0},{4,7},{5,6},{6,5},{7,4},{8,11},{9,10},{10,... | collective-permute-start | bytes 1179656 | tf_op jit(solution)/shard_map/ppermute | solution.py:36
  129.7 15.7 %collective-permute-start.23 = (bf16[128,2048]{1,0:T(8,128)(2,1)S(1)}, bf16[128,2048]{1,0:T(8,128)(2,1)S(1)}, u32[]{:S(2)}, u32[]{:S(2)}) collective-permute-start(bf16[128,2048]{1,0:T(8,128)(2,1)S(1)} %get-tuple-element.101.same), channel_id=1, source_target_pairs={{0,24},{4,28},{8,16},{12,20},{16,8},{20,12},{24,0},{28,4},{1,25},{... | collective-permute-start | bytes 1572872 | tf_op jit(solution)/shard_map/ppermute | solution.py:36
  131.9 13.5 %collective-permute-start.10 = (bf16[128,2048]{1,0:T(8,128)(2,1)S(1)}, bf16[128,2048]{1,0:T(8,128)(2,1)S(1)}, u32[]{:S(2)}, u32[]{:S(2)}) collective-permute-start(bf16[128,2048]{1,0:T(8,128)(2,1)S(1)} %collective-permute-done.9.same), channel_id=1, source_target_pairs={{0,4},{4,0},{8,12},{12,8},{16,20},{20,16},{24,28},{28,24},{1,5},{5... | collective-permute-start | bytes 1572872 | tf_op jit(solution)/shard_map/ppermute | solution.py:36
  133.0 15.5 %collective-permute-start.18 = (bf16[96,2048]{1,0:T(8,128)(2,1)S(1)}, bf16[96,2048]{1,0:T(8,128)(2,1)S(1)}, u32[]{:S(2)}, u32[]{:S(2)}) collective-permute-start(bf16[96,2048]{1,0:T(8,128)(2,1)S(1)} %get-tuple-element.92), channel_id=1, source_target_pairs={{0,2},{1,3},{2,0},{3,1},{4,6},{5,7},{6,4},{7,5},{8,10},{9,11},{10,... | collective-permute-start | bytes 1179656 | tf_op jit(solution)/shard_map/ppermute | solution.py:36
  134.5 16.0 %collective-permute-start.15 = (bf16[96,2048]{1,0:T(8,128)(2,1)S(1)}, bf16[96,2048]{1,0:T(8,128)(2,1)S(1)}, u32[]{:S(2)}, u32[]{:S(2)}) collective-permute-start(bf16[96,2048]{1,0:T(8,128)(2,1)S(1)} %get-tuple-element.87), channel_id=1, source_target_pairs={{0,1},{1,0},{2,3},{3,2},{4,5},{5,4},{6,7},{7,6},{8,9},{9,8},{10,11... | collective-permute-start | bytes 1179656 | tf_op jit(solution)/shard_map/ppermute | solution.py:36
  140.2 16.9 %collective-permute-start.21 = (bf16[96,2048]{1,0:T(8,128)(2,1)S(1)}, bf16[96,2048]{1,0:T(8,128)(2,1)S(1)}, u32[]{:S(2)}, u32[]{:S(2)}) collective-permute-start(bf16[96,2048]{1,0:T(8,128)(2,1)S(1)} %get-tuple-element.97), channel_id=1, source_target_pairs={{0,3},{1,2},{2,1},{3,0},{4,7},{5,6},{6,5},{7,4},{8,11},{9,10},{10,... | collective-permute-start | bytes 1179656 | tf_op jit(solution)/shard_map/ppermute | solution.py:36
  145.3 15.2 %collective-permute-start.24 = (bf16[128,2048]{1,0:T(8,128)(2,1)S(1)}, bf16[128,2048]{1,0:T(8,128)(2,1)S(1)}, u32[]{:S(2)}, u32[]{:S(2)}) collective-permute-start(bf16[128,2048]{1,0:T(8,128)(2,1)S(1)} %collective-permute-done.23.same), channel_id=1, source_target_pairs={{0,4},{4,0},{8,12},{12,8},{16,20},{20,16},{24,28},{28,24},{1,5},{5... | collective-permute-start | bytes 1572872 | tf_op jit(solution)/shard_map/ppermute | solution.py:36
  148.4 16.9 %collective-permute-start.19 = (bf16[96,2048]{1,0:T(8,128)(2,1)S(1)}, bf16[96,2048]{1,0:T(8,128)(2,1)S(1)}, u32[]{:S(2)}, u32[]{:S(2)}) collective-permute-start(bf16[96,2048]{1,0:T(8,128)(2,1)S(1)} %get-tuple-element.93), channel_id=1, source_target_pairs={{0,2},{1,3},{2,0},{3,1},{4,6},{5,7},{6,4},{7,5},{8,10},{9,11},{10,... | collective-permute-start | bytes 1179656 | tf_op jit(solution)/shard_map/ppermute | solution.py:36
  150.4 16.9 %collective-permute-start.16 = (bf16[96,2048]{1,0:T(8,128)(2,1)S(1)}, bf16[96,2048]{1,0:T(8,128)(2,1)S(1)}, u32[]{:S(2)}, u32[]{:S(2)}) collective-permute-start(bf16[96,2048]{1,0:T(8,128)(2,1)S(1)} %get-tuple-element.88), channel_id=1, source_target_pairs={{0,1},{1,0},{2,3},{3,2},{4,5},{5,4},{6,7},{7,6},{8,9},{9,8},{10,11... | collective-permute-start | bytes 1179656 | tf_op jit(solution)/shard_map/ppermute | solution.py:36
  157.1 16.9 %collective-permute-start.22 = (bf16[96,2048]{1,0:T(8,128)(2,1)S(1)}, bf16[96,2048]{1,0:T(8,128)(2,1)S(1)}, u32[]{:S(2)}, u32[]{:S(2)}) collective-permute-start(bf16[96,2048]{1,0:T(8,128)(2,1)S(1)} %get-tuple-element.98), channel_id=1, source_target_pairs={{0,3},{1,2},{2,1},{3,0},{4,7},{5,6},{6,5},{7,4},{8,11},{9,10},{10,... | collective-permute-start | bytes 1179656 | tf_op jit(solution)/shard_map/ppermute | solution.py:36
  165.3 16.9 %collective-permute-start.27 = (bf16[96,2048]{1,0:T(8,128)(2,1)S(1)}, bf16[96,2048]{1,0:T(8,128)(2,1)S(1)}, u32[]{:S(2)}, u32[]{:S(2)}) collective-permute-start(bf16[96,2048]{1,0:T(8,128)(2,1)S(1)} %get-tuple-element.107), channel_id=1, source_target_pairs={{0,2},{1,3},{2,0},{3,1},{4,6},{5,7},{6,4},{7,5},{8,10},{9,11},{10,... | collective-permute-start | bytes 1179656 | tf_op jit(solution)/shard_map/ppermute | solution.py:36
  167.3 16.9 %collective-permute-start.25 = (bf16[96,2048]{1,0:T(8,128)(2,1)S(1)}, bf16[96,2048]{1,0:T(8,128)(2,1)S(1)}, u32[]{:S(2)}, u32[]{:S(2)}) collective-permute-start(bf16[96,2048]{1,0:T(8,128)(2,1)S(1)} %get-tuple-element.103), channel_id=1, source_target_pairs={{0,1},{1,0},{2,3},{3,2},{4,5},{5,4},{6,7},{7,6},{8,9},{9,8},{10,11... | collective-permute-start | bytes 1179656 | tf_op jit(solution)/shard_map/ppermute | solution.py:36
  174.0 16.9 %collective-permute-start.29 = (bf16[96,2048]{1,0:T(8,128)(2,1)S(1)}, bf16[96,2048]{1,0:T(8,128)(2,1)S(1)}, u32[]{:S(2)}, u32[]{:S(2)}) collective-permute-start(bf16[96,2048]{1,0:T(8,128)(2,1)S(1)} %get-tuple-element.111), channel_id=1, source_target_pairs={{0,3},{1,2},{2,1},{3,0},{4,7},{5,6},{6,5},{7,4},{8,11},{9,10},{10,... | collective-permute-start | bytes 1179656 | tf_op jit(solution)/shard_map/ppermute | solution.py:36
  182.2 16.9 %collective-permute-start.28 = (bf16[96,2048]{1,0:T(8,128)(2,1)S(1)}, bf16[96,2048]{1,0:T(8,128)(2,1)S(1)}, u32[]{:S(2)}, u32[]{:S(2)}) collective-permute-start(bf16[96,2048]{1,0:T(8,128)(2,1)S(1)} %get-tuple-element.108), channel_id=1, source_target_pairs={{0,2},{1,3},{2,0},{3,1},{4,6},{5,7},{6,4},{7,5},{8,10},{9,11},{10,... | collective-permute-start | bytes 1179656 | tf_op jit(solution)/shard_map/ppermute | solution.py:36
  184.2 16.9 %collective-permute-start.26 = (bf16[96,2048]{1,0:T(8,128)(2,1)S(1)}, bf16[96,2048]{1,0:T(8,128)(2,1)S(1)}, u32[]{:S(2)}, u32[]{:S(2)}) collective-permute-start(bf16[96,2048]{1,0:T(8,128)(2,1)S(1)} %get-tuple-element.104), channel_id=1, source_target_pairs={{0,1},{1,0},{2,3},{3,2},{4,5},{5,4},{6,7},{7,6},{8,9},{9,8},{10,11... | collective-permute-start | bytes 1179656 | tf_op jit(solution)/shard_map/ppermute | solution.py:36
  190.9 16.9 %collective-permute-start.30 = (bf16[96,2048]{1,0:T(8,128)(2,1)S(1)}, bf16[96,2048]{1,0:T(8,128)(2,1)S(1)}, u32[]{:S(2)}, u32[]{:S(2)}) collective-permute-start(bf16[96,2048]{1,0:T(8,128)(2,1)S(1)} %get-tuple-element.112), channel_id=1, source_target_pairs={{0,3},{1,2},{2,1},{3,0},{4,7},{5,6},{6,5},{7,4},{8,11},{9,10},{10,... | collective-permute-start | bytes 1179656 | tf_op jit(solution)/shard_map/ppermute | solution.py:36
  199.1 17.2 %collective-permute-start.34 = (bf16[96,2048]{1,0:T(8,128)(2,1)S(1)}, bf16[96,2048]{1,0:T(8,128)(2,1)S(1)}, u32[]{:S(2)}, u32[]{:S(2)}) collective-permute-start(bf16[96,2048]{1,0:T(8,128)(2,1)S(1)} %get-tuple-element.120), channel_id=1, source_target_pairs={{0,2},{1,3},{2,0},{3,1},{4,6},{5,7},{6,4},{7,5},{8,10},{9,11},{10,... | collective-permute-start | bytes 1179656 | tf_op jit(solution)/shard_map/ppermute | solution.py:36
  201.1 16.9 %collective-permute-start.33 = (bf16[96,2048]{1,0:T(8,128)(2,1)S(1)}, bf16[96,2048]{1,0:T(8,128)(2,1)S(1)}, u32[]{:S(2)}, u32[]{:S(2)}) collective-permute-start(bf16[96,2048]{1,0:T(8,128)(2,1)S(1)} %get-tuple-element.118), channel_id=1, source_target_pairs={{0,1},{1,0},{2,3},{3,2},{4,5},{5,4},{6,7},{7,6},{8,9},{9,8},{10,11... | collective-permute-start | bytes 1179656 | tf_op jit(solution)/shard_map/ppermute | solution.py:36
  207.8 16.9 %collective-permute-start.35 = (bf16[96,2048]{1,0:T(8,128)(2,1)S(1)}, bf16[96,2048]{1,0:T(8,128)(2,1)S(1)}, u32[]{:S(2)}, u32[]{:S(2)}) collective-permute-start(bf16[96,2048]{1,0:T(8,128)(2,1)S(1)} %get-tuple-element.122), channel_id=1, source_target_pairs={{0,3},{1,2},{2,1},{3,0},{4,7},{5,6},{6,5},{7,4},{8,11},{9,10},{10,... | collective-permute-start | bytes 1179656 | tf_op jit(solution)/shard_map/ppermute | solution.py:36
  212.2 29.8 %collective-permute-start.31 = (bf16[128,2048]{1,0:T(8,128)(2,1)S(1)}, bf16[128,2048]{1,0:T(8,128)(2,1)S(1)}, u32[]{:S(2)}, u32[]{:S(2)}) collective-permute-start(bf16[128,2048]{1,0:T(8,128)(2,1)S(1)} %get-tuple-element.114), channel_id=1, source_target_pairs={{0,4},{4,0},{8,12},{12,8},{16,20},{20,16},{24,28},{28,24},{1,5},{5... | collective-permute-start | bytes 1572872 | tf_op jit(solution)/shard_map/ppermute | solution.py:36
  216.4 16.6 %collective-permute-start.39 = (bf16[96,2048]{1,0:T(8,128)(2,1)S(1)}, bf16[96,2048]{1,0:T(8,128)(2,1)S(1)}, u32[]{:S(2)}, u32[]{:S(2)}) collective-permute-start(bf16[96,2048]{1,0:T(8,128)(2,1)S(1)} %get-tuple-element.130), channel_id=1, source_target_pairs={{0,2},{1,3},{2,0},{3,1},{4,6},{5,7},{6,4},{7,5},{8,10},{9,11},{10,... | collective-permute-start | bytes 1179656 | tf_op jit(solution)/shard_map/ppermute | solution.py:36
  218.0 15.5 %collective-permute-start.38 = (bf16[96,2048]{1,0:T(8,128)(2,1)S(1)}, bf16[96,2048]{1,0:T(8,128)(2,1)S(1)}, u32[]{:S(2)}, u32[]{:S(2)}) collective-permute-start(bf16[96,2048]{1,0:T(8,128)(2,1)S(1)} %get-tuple-element.128), channel_id=1, source_target_pairs={{0,1},{1,0},{2,3},{3,2},{4,5},{5,4},{6,7},{7,6},{8,9},{9,8},{10,11... | collective-permute-start | bytes 1179656 | tf_op jit(solution)/shard_map/ppermute | solution.py:36
  224.7 16.2 %collective-permute-start.40 = (bf16[96,2048]{1,0:T(8,128)(2,1)S(1)}, bf16[96,2048]{1,0:T(8,128)(2,1)S(1)}, u32[]{:S(2)}, u32[]{:S(2)}) collective-permute-start(bf16[96,2048]{1,0:T(8,128)(2,1)S(1)} %get-tuple-element.132), channel_id=1, source_target_pairs={{0,3},{1,2},{2,1},{3,0},{4,7},{5,6},{6,5},{7,4},{8,11},{9,10},{10,... | collective-permute-start | bytes 1179656 | tf_op jit(solution)/shard_map/ppermute | solution.py:36
  229.1 18.4 %collective-permute-start.36 = (bf16[128,2048]{1,0:T(8,128)(2,1)S(1)}, bf16[128,2048]{1,0:T(8,128)(2,1)S(1)}, u32[]{:S(2)}, u32[]{:S(2)}) collective-permute-start(bf16[128,2048]{1,0:T(8,128)(2,1)S(1)} %get-tuple-element.124), channel_id=1, source_target_pairs={{0,4},{4,0},{8,12},{12,8},{16,20},{20,16},{24,28},{28,24},{1,5},{5... | collective-permute-start | bytes 1572872 | tf_op jit(solution)/shard_map/ppermute | solution.py:36
  241.9 25.3 %collective-permute-start.41 = (bf16[128,2048]{1,0:T(8,128)(2,1)S(1)}, bf16[128,2048]{1,0:T(8,128)(2,1)S(1)}, u32[]{:S(2)}, u32[]{:S(2)}) collective-permute-start(bf16[128,2048]{1,0:T(8,128)(2,1)S(1)} %get-tuple-element.134), channel_id=1, source_target_pairs={{0,4},{4,0},{8,12},{12,8},{16,20},{20,16},{24,28},{28,24},{1,5},{5... | collective-permute-start | bytes 1572872 | tf_op jit(solution)/shard_map/ppermute | solution.py:36
  242.2 38.4 %collective-permute-start.32 = (bf16[128,2048]{1,0:T(8,128)(2,1)S(1)}, bf16[128,2048]{1,0:T(8,128)(2,1)S(1)}, u32[]{:S(2)}, u32[]{:S(2)}) collective-permute-start(bf16[128,2048]{1,0:T(8,128)(2,1)S(1)} %add_convert_fusion.3), channel_id=1, source_target_pairs={{0,16},{4,20},{8,24},{12,28},{16,0},{20,4},{24,8},{28,12},{1,17},{... | collective-permute-start | bytes 1572872 | tf_op jit(solution)/shard_map/ppermute | solution.py:36
  245.3 11.2 %collective-permute-start.44 = (bf16[96,2048]{1,0:T(8,128)(2,1)S(1)}, bf16[96,2048]{1,0:T(8,128)(2,1)S(1)}, u32[]{:S(2)}, u32[]{:S(2)}) collective-permute-start(bf16[96,2048]{1,0:T(8,128)(2,1)S(1)} %get-tuple-element.140), channel_id=1, source_target_pairs={{0,2},{1,3},{2,0},{3,1},{4,6},{5,7},{6,4},{7,5},{8,10},{9,11},{10,... | collective-permute-start | bytes 1179656 | tf_op jit(solution)/shard_map/ppermute | solution.py:36
  246.8 12.0 %collective-permute-start.43 = (bf16[96,2048]{1,0:T(8,128)(2,1)S(1)}, bf16[96,2048]{1,0:T(8,128)(2,1)S(1)}, u32[]{:S(2)}, u32[]{:S(2)}) collective-permute-start(bf16[96,2048]{1,0:T(8,128)(2,1)S(1)} %get-tuple-element.138), channel_id=1, source_target_pairs={{0,1},{1,0},{2,3},{3,2},{4,5},{5,4},{6,7},{7,6},{8,9},{9,8},{10,11... | collective-permute-start | bytes 1179656 | tf_op jit(solution)/shard_map/ppermute | solution.py:36
  247.5 18.6 %collective-permute-start.45 = (bf16[96,2048]{1,0:T(8,128)(2,1)S(1)}, bf16[96,2048]{1,0:T(8,128)(2,1)S(1)}, u32[]{:S(2)}, u32[]{:S(2)}) collective-permute-start(bf16[96,2048]{1,0:T(8,128)(2,1)S(1)} %get-tuple-element.142), channel_id=1, source_target_pairs={{0,3},{1,2},{2,1},{3,0},{4,7},{5,6},{6,5},{7,4},{8,11},{9,10},{10,... | collective-permute-start | bytes 1179656 | tf_op jit(solution)/shard_map/ppermute | solution.py:36
  256.5 24.1 %collective-permute-start.37 = (bf16[128,2048]{1,0:T(8,128)(2,1)S(1)}, bf16[128,2048]{1,0:T(8,128)(2,1)S(1)}, u32[]{:S(2)}, u32[]{:S(2)}) collective-permute-start(bf16[128,2048]{1,0:T(8,128)(2,1)S(1)} %add_convert_fusion.2), channel_id=1, source_target_pairs={{0,24},{4,28},{8,16},{12,20},{16,8},{20,12},{24,0},{28,4},{1,25},{... | collective-permute-start | bytes 1572872 | tf_op jit(solution)/shard_map/ppermute | solution.py:36
  267.2 13.4 %collective-permute-start.46 = (bf16[128,2048]{1,0:T(8,128)(2,1)S(1)}, bf16[128,2048]{1,0:T(8,128)(2,1)S(1)}, u32[]{:S(2)}, u32[]{:S(2)}) collective-permute-start(bf16[128,2048]{1,0:T(8,128)(2,1)S(1)} %get-tuple-element.144), channel_id=1, source_target_pairs={{0,4},{4,0},{8,12},{12,8},{16,20},{20,16},{24,28},{28,24},{1,5},{5... | collective-permute-start | bytes 1572872 | tf_op jit(solution)/shard_map/ppermute | solution.py:36
  267.4 24.2 %collective-permute-start.42 = (bf16[128,2048]{1,0:T(8,128)(2,1)S(1)}, bf16[128,2048]{1,0:T(8,128)(2,1)S(1)}, u32[]{:S(2)}, u32[]{:S(2)}) collective-permute-start(bf16[128,2048]{1,0:T(8,128)(2,1)S(1)} %add_convert_fusion.1), channel_id=1, source_target_pairs={{0,8},{4,12},{8,0},{12,4},{16,24},{20,28},{24,16},{28,20},{1,9},{5... | collective-permute-start | bytes 1572872 | tf_op jit(solution)/shard_map/ppermute | solution.py:36
  (21 other events, 440.6 us)
Sparse Core Ops, SparseCore 0:
  24.8 29.9 all-gather.1

commit v4 on v3

--- a/solution.py
+++ b/solution.py
@@ -20,7 +20,6 @@
 VMEM = pl.BlockSpec(memory_space=pltpu.VMEM)
 SMEM = pl.BlockSpec(memory_space=pltpu.SMEM)
 ANY = pl.BlockSpec(memory_space=pl.ANY)
-PARAMS = pltpu.CompilerParams(vmem_limit_bytes=24 * 1024 * 1024)
 
 
 def rms_scale(value_states, norm_gain):
@@ -58,7 +57,7 @@
 def load_all(pairs, sems):
     copies = []
     for source, target in pairs:
-        part = max(16, source.shape[0] // 4)
+        part = source.shape[0] // 4 if source.shape[0] >= 128 and source.shape[1] > 128 else source.shape[0]
         for first in range(0, source.shape[0], part):
             here = pl.ds(first, part)
             copies.append(
@@ -69,11 +68,12 @@
     return copies
 
 
-def own_rows_kernel(
-    experts, tokens, key_weight, value_weight, gain, k_gain, cosine, sine, ids, shares, out, table,
-    rows_in, key_in, value_in, sems,
-):
-    copies = load_all([(tokens, rows_in), (key_weight, key_in), (value_weight, value_in)], sems)
+def own_rows_kernel(experts, *refs):
+    sources, (out, table), targets, sems = refs[:9], refs[9:11], refs[11:20], refs[20]
+    copies = load_all(list(zip(sources, targets)), sems)
+    ids, shares, tokens, gain, key_weight, value_weight, k_gain, cosine, sine = targets
+    copies[0].wait()
+    copies[1].wait()
     rows = tokens.shape[0]
     chosen_ids = ids[...]
     lanes = lax.broadcasted_iota(jnp.int32, (experts, rows), 0)
@@ -96,11 +96,11 @@
     left = jnp.concatenate([chosen_ids, shares[...]], axis=0).astype(jnp.float32)
     table[:, :rows] = left.astype(jnp.bfloat16)
     table[:, rows:] = jnp.concatenate([slots, jnp.zeros_like(slots)], axis=0).astype(jnp.bfloat16)
-    for copy in copies:
+    for copy in copies[2:]:
         copy.wait()
-    normed = rms_scale(rows_in[...].astype(jnp.float32), gain[...]).astype(jnp.bfloat16)
-    keys = jnp.dot(normed, key_in[...], preferred_element_type=jnp.float32)
-    values = jnp.dot(normed, value_in[...], preferred_element_type=jnp.float32)
+    normed = rms_scale(tokens[...].astype(jnp.float32), gain[...]).astype(jnp.bfloat16)
+    keys = jnp.dot(normed, key_weight[...], preferred_element_type=jnp.float32)
+    values = jnp.dot(normed, value_weight[...], preferred_element_type=jnp.float32)
     for head in range(out.shape[0]):
         cols = slice(head * HEAD_SIZE, (head + 1) * HEAD_SIZE)
         rotated = normed_rotated(keys[:, cols], k_gain[...], cosine[...], sine[...])
@@ -122,66 +122,70 @@
             out[at, pl.ds(head * rows, rows), :] = rotated.astype(jnp.bfloat16)
 
 
-def attention_kernel(distance, rows, place, queries, both, w_out, out):
+def attention_kernel(distances, rows, place, queries, both, w_out, *outs):
     block, me = place[0], place[1]
     heads = w_out.shape[0] // HEAD_SIZE
     width = heads * rows
     span = rows * (place.shape[0] - 2)
     stride = span + 2 * TOP
     scale = HEAD_SIZE ** (-0.5) * LOG2E
-    asked = queries[0]
-
-    def step(first, state, masked):
+
+    def step(first, states, masked):
         keys = both[pl.ds(first, span), :HEAD_SIZE]
         values = both[pl.ds(first, span), HEAD_SIZE:]
-        scores = lax.dot_general(
-            keys, asked, (((1,), (1,)), ((), ())), preferred_element_type=jnp.float32
-        )
-        if masked:
-            at = lax.broadcasted_iota(jnp.int32, (span, width), 0)
-            key_pos = (me ^ (at // rows)) * rows + at % rows
-            query = lax.broadcasted_iota(jnp.int32, (span, width), 1)
-            scores = jnp.where(
-                key_pos <= (me ^ distance) * rows + query % rows, scores, floor_value
+        result = []
+        for at, (top, total, mixed) in enumerate(states):
+            scores = lax.dot_general(
+                keys, queries[at], (((1,), (1,)), ((), ())), preferred_element_type=jnp.float32
             )
-        top, total, mixed = state
-        new_top = jnp.maximum(top, jnp.max(scores, axis=0, keepdims=True))
-        weights = jnp.exp2((scores - new_top) * scale)
-        rescale = jnp.exp2((top - new_top) * scale)
-        total = total * rescale + jnp.sum(weights, axis=0, keepdims=True)
-        mixed = mixed * rescale + lax.dot_general(
-            values,
-            weights.astype(jnp.bfloat16),
-            (((0,), (0,)), ((), ())),
-            preferred_element_type=jnp.float32,
-        )
-        return new_top, total, mixed
-
-    state = (
-        jnp.full((1, width), floor_value, jnp.float32),
-        jnp.zeros((1, width), jnp.float32),
-        jnp.zeros((HEAD_SIZE, width), jnp.float32),
-    )
-    state = step(pl.multiple_of(block * stride, 2 * TOP), state, True)
-    state = lax.fori_loop(
-        0, block, lambda i, s: step(pl.multiple_of(i * stride, 2 * TOP), s, False), state
-    )
-    _, total, mixed = state
-    attended = (mixed / total).astype(jnp.bfloat16)
-    attended = jnp.concatenate(
-        [attended[:, head * rows : (head + 1) * rows] for head in range(heads)], axis=0
-    )
-    out[...] = lax.dot_general(
-        attended, w_out[...], (((0,), (0,)), ((), ())), preferred_element_type=jnp.float32
-    ).astype(jnp.bfloat16)
-
-
-def residual_kernel(*refs):
-    tokens, *partials, gain, residual, normed = refs
-    attention = partials[0][...].astype(jnp.float32)
-    for partial in partials[1:]:
-        attention = attention + partial[...].astype(jnp.float32)
-    rounded = (tokens[...].astype(jnp.float32) + attention).astype(jnp.bfloat16)
+            if masked:
+                row = lax.broadcasted_iota(jnp.int32, (span, width), 0)
+                key_pos = (me ^ (row // rows)) * rows + row % rows
+                query = lax.broadcasted_iota(jnp.int32, (span, width), 1) % rows
+                query_pos = (me ^ distances[at]) * rows + query
+                scores = jnp.where(key_pos <= query_pos, scores, floor_value)
+            new_top = jnp.maximum(top, jnp.max(scores, axis=0, keepdims=True))
+            weights = jnp.exp2((scores - new_top) * scale)
+            rescale = jnp.exp2((top - new_top) * scale)
+            total = total * rescale + jnp.sum(weights, axis=0, keepdims=True)
+            mixed = mixed * rescale + lax.dot_general(
+                values,
+                weights.astype(jnp.bfloat16),
+                (((0,), (0,)), ((), ())),
+                preferred_element_type=jnp.float32,
+            )
+            result.append((new_top, total, mixed))
+        return tuple(result)
+
+    states = tuple(
+        (
+            jnp.full((1, width), floor_value, jnp.float32),
+            jnp.zeros((1, width), jnp.float32),
+            jnp.zeros((HEAD_SIZE, width), jnp.float32),
+        )
+        for _ in distances
+    )
+    states = step(pl.multiple_of(block * stride, 2 * TOP), states, True)
+    states = lax.fori_loop(
+        0, block, lambda i, s: step(pl.multiple_of(i * stride, 2 * TOP), s, False), states
+    )
+    for (_, total, mixed), out in zip(states, outs):
+        attended = (mixed / total).astype(jnp.bfloat16)
+        attended = jnp.concatenate(
+            [attended[:, head * rows : (head + 1) * rows] for head in range(heads)], axis=0
+        )
+        out[...] = lax.dot_general(
+            attended, w_out[...], (((0,), (0,)), ((), ())), preferred_element_type=jnp.float32
+        ).astype(jnp.bfloat16)
+
+
+def add_kernel(total, partial, out):
+    out[...] = total[...].astype(jnp.float32) + partial[...].astype(jnp.float32)
+
+
+def residual_kernel(tokens, attention, partial, gain, residual, normed):
+    summed = attention[...].astype(jnp.float32) + partial[...].astype(jnp.float32)
+    rounded = (tokens[...].astype(jnp.float32) + summed).astype(jnp.bfloat16)
     residual[...] = rounded
     normed[...] = rms_scale(rounded.astype(jnp.float32), gain[...]).astype(jnp.bfloat16)
 
@@ -254,15 +258,15 @@
             ref[:, cols] = product[at * part : (at + 1) * part]
 
 
-def call(kernel, out_shape, specs, *args, name, scratch=()):
+def call(kernel, out_shape, specs, *args, name, scratch=(), limit=24, flops=1000):
     return pl.pallas_call(
         kernel,
         out_shape=out_shape,
         in_specs=specs,
         out_specs=jax.tree.map(lambda _: VMEM, out_shape),
         scratch_shapes=scratch,
-        compiler_params=PARAMS,
-        cost_estimate=pl.CostEstimate(flops=1000, bytes_accessed=1000, transcendentals=0),
+        compiler_params=pltpu.CompilerParams(vmem_limit_bytes=limit * 1024 * 1024),
+        cost_estimate=pl.CostEstimate(flops=flops, bytes_accessed=1000, transcendentals=0),
         name=name,
     )(*args)
 
@@ -306,27 +310,25 @@
     ln1_row = ln1_gain.reshape(1, width)
     own_first = me_ctx * ctx_rows + me_exp * rows
     cosine, sine = rope_tables(own_first + jnp.arange(rows))
-    kv_width = key_weight.shape[1]
+    own_args = [
+        expert_ids.T,
+        route_weights.T,
+        tokens,
+        ln1_row,
+        key_weight,
+        value_weight,
+        k_gain.reshape(1, HEAD_SIZE),
+        cosine,
+        sine,
+    ]
     own_kv, table = call(
         functools.partial(own_rows_kernel, experts),
         [bf16((KEY_VALUE_HEADS, rows, 2 * HEAD_SIZE)), bf16((2 * TOP, 2 * rows))],
-        [ANY] * 3 + [VMEM] * 6,
-        tokens,
-        key_weight,
-        value_weight,
-        ln1_row,
-        k_gain.reshape(1, HEAD_SIZE),
-        cosine,
-        sine,
-        expert_ids.T,
-        route_weights.T,
+        [ANY] * 9,
+        *own_args,
         name="own_rows",
-        scratch=[
-            pltpu.VMEM((rows, width), jnp.bfloat16),
-            pltpu.VMEM((width, kv_width), jnp.bfloat16),
-            pltpu.VMEM((width, kv_width), jnp.bfloat16),
-            pltpu.SemaphoreType.DMA((12,)),
-        ],
+        scratch=[pltpu.VMEM(a.shape, a.dtype) for a in own_args] + [pltpu.SemaphoreType.DMA((18,))],
+        limit=60,
     )
 
     def head_kv(distance):
@@ -337,7 +339,9 @@
     for d in peers[1:]:
         if d not in pieces:
             pieces[d] = swap(tie(tokens, *block_kv[1:]), "exp", d)
-    both = lax.all_gather(jnp.concatenate(block_kv + [table], axis=0), "ctx", axis=0, tiled=True)
+    both = jnp.concatenate(block_kv + [table], axis=0)
+    both = tie(both, *[pieces[d] for d in peers[1:] if d & (d - 1) == 0])
+    both = lax.all_gather(both, "ctx", axis=0, tiled=True)
     routing = both.reshape(ctx_count, ctx_rows + 2 * TOP, 2 * HEAD_SIZE)[:, ctx_rows:]
 
     positions = jnp.concatenate(
@@ -359,25 +363,39 @@
 
     order = sorted(peers, key=lambda d: -bin(d).count("1"))
     partials, last = {}, ()
-    for d in order:
-        partials[d] = call(
-            functools.partial(attention_kernel, d, rows),
-            bf16((rows, width)),
+    for some in [[d] for d in order]:
+        asked = queries[some[0] : some[0] + 1]
+        made = call(
+            functools.partial(attention_kernel, some, rows),
+            [bf16((rows, width)) for _ in some],
             [SMEM, VMEM, VMEM, VMEM],
             place,
-            tie(queries[d : d + 1], *last),
+            tie(asked, *last),
             both,
             w_out,
             name="attention",
         )
-        last = (partials[d],)
-    parts = [partials[0]] + [swap(partials[d], "exp", d) for d in order if d]
+        partials.update(zip(some, made))
+        last = tuple(made)
+    attention = partials[0]
+    parts = [swap(partials[d], "exp", d) for d in order if d]
+    for part in parts[:-1]:
+        attention = call(
+            add_kernel,
+            jax.ShapeDtypeStruct((rows, width), jnp.float32),
+            [VMEM] * 2,
+            attention,
+            part,
+            name="add",
+            flops=3_000_000_000,
+        )
     residual, normed = call(
         residual_kernel,
         [bf16((rows, width)), bf16((rows, width))],
-        [VMEM] * (exp_count + 2),
+        [VMEM] * 4,
         tokens,
-        *parts,
+        attention,
+        parts[-1],
         ln2_gain.reshape(1, width),
         name="residual",
     )
@@ -387,9 +405,9 @@
     for g in range(1, groups):
         far.append(swap(tie(normed, *([far[g - 1]] if g > 2 else [])), "ctx", 2 * g))
     in_flight = {d: () for d in peers[1:]}
-    arrived = []
+    arrived, sent = [], ()
     for g in range(groups):
-        mate = swap(far[g], "ctx", 1)
+        mate = swap(tie(far[g], *sent), "ctx", 1)
         outgoing = call(
             functools.partial(dispatch_kernel, g, capacity),
             [bf16((2 * capacity, width)) for _ in peers],
@@ -404,11 +422,12 @@
         for d in peers[1:]:
             came.append(swap(tie(outgoing[d], *in_flight[d]), "exp", d))
             in_flight[d] = (came[d],)
+        sent = tuple(came[1:]) if g == 0 else ()
         arrived.append(came)
 
     turns = [g for g in range(2, groups)] + [g for g in (1, 0) if g < groups]
     mixture = residual.astype(jnp.float32)
-    produced = {}
+    produced, sums, hop = {}, (), ()
     for g in range(groups):
         produced[g] = call(
             expert_kernel,
@@ -422,7 +441,7 @@
             scratch=[pltpu.VMEM((2 * capacity * exp_count, w_gate.shape[2]), jnp.bfloat16)],
         )
     for g in turns:
-        back = [produced[g][0]]
+        back = [tie(produced[g][0], *sums)]
         for d in peers[1:]:
             back.append(swap(tie(produced[g][d], *in_flight[d]), "exp", d))
             in_flight[d] = (back[d],)
@@ -437,7 +456,11 @@
         )
         total = same.astype(jnp.float32) + swap(other, "ctx", 1).astype(jnp.float32)
         if g:
-            total = swap(total.astype(jnp.bfloat16), "ctx", 2 * g).astype(jnp.float32)
+            total = total.astype(jnp.bfloat16)
+            sums = (total,)
+            total = swap(tie(total, *(hop if g > 1 else ())), "ctx", 2 * g)
+            hop = (total,)
+            total = total.astype(jnp.float32)
         mixture = mixture + total
     return mixture.astype(jnp.bfloat16)
 

time: 300 us -> 310 us (1.033)
  waiting for transfers between devices: 137 us -> 182 us
  starting transfers between devices: 98 us -> 64.3 us
  local copies, waits for them, and re-layouts: 12.1 us -> 7.55 us
    ppermute x47, waiting for transfers between devices: 136 us -> 170 us  [swap(): return lax.ppermute(array, axis, pairs)]
    ppermute x47, starting transfers between devices: 98 us -> 64.3 us  [swap(): return lax.ppermute(array, axis, pairs)]
    all_gather x1, waiting for transfers between devices: 0.76 us -> 12.2 us  [shards(): both = lax.all_gather(both, 'ctx', axis=0, tiled=True)]
    unnamed x46 -> x32, local copies, waits for them, and re-layouts: 12 us -> 5.87 us
    pallas_call x19 -> x21, Pallas kernels: 35.3 us -> 36.9 us  [call(): pl.pallas_call(kernel, out_shape=out_shape, in_specs=specs, out_specs=jax...]
  transfers between devices with their start and end apart: 48 -> 48, of which waited for: 27 -> 22; matrix products, arithmetic and copies ran while one was open for 1% -> 2% of each run, Pallas kernels for 9% -> 11%
where the time goes in v4:
time: 310 us
  waiting for transfers between devices  182 us (59%)
  starting transfers between devices  64.3 us (21%)
  Pallas kernels  36.9 us (12%)
  between operations  13.8 us (4%)
  local copies, waits for them, and re-layouts  7.55 us (2%)
  other arithmetic  4.79 us (2%)
    ppermute x47, waiting for transfers between devices, swap(): return lax.ppermute(array, axis, pairs)  170 us
    ppermute x47, starting transfers between devices, swap(): return lax.ppermute(array, axis, pairs)  64.3 us
    pallas_call x21, Pallas kernels, call(): pl.pallas_call(kernel, out_shape=out_shape, in_specs=specs, out_specs=jax...  36.9 us
    all_gather x1, waiting for transfers between devices, shards(): both = lax.all_gather(both, 'ctx', axis=0, tiled=True)  12.2 us
  transfers between devices with their start and end apart: 48, of which 22 were waited for; matrix products, arithmetic and copies ran while one was open for 2% of the time, Pallas kernels for 11%

profile of v4, /device:TPU:0, one launch (start us, length us, event | category | flops | bytes accessed | tf_op | source)
XLA Modules:
  0.0 309.6 jit_solution(867567152182237144)
XLA Ops:
  6.5 3.0 collective-permute-start.1
  12.8 3.4 %own_rows.1 = (bf16[2,128,256]{2,1,0:T(8,128)(2,1)}, bf16[16,256]{1,0:T(8,128)(2,1)}) custom-call(s32[8,128]{1,0:T(8,128)} %bitcast.37, s32[8,128]{1,0:T(8,128)} %bitcast.38, bf16[128,2048]{1,0:T(8,128)(2,1)} %tokens.1, f32[1,2048]{1,0:T(1,128)} %bitcast.33, bf16[2048,256]{1,0:T(8,128)(2,1)} %refs_4_.1, bf16[2048,256]{1,0:T(8,128)(2,1)} %refs_5_.2, ...), custom_call_target="tpu_custom_call" | custom-call | flops 1000 | bytes 1000 | tf_op jit(solution)/shard_map/own_rows/pallas_call | solution.py:262
  17.2 2.0 collective-permute-start.3
  21.5 4.4 %collective-permute-done.2 = bf16[128,256]{1,0:T(8,128)(2,1)S(1)} collective-permute-done((bf16[128,256]{1,0:T(8,128)(2,1)S(1)}, bf16[128,256]{1,0:T(8,128)(2,1)S(1)}, u32[]{:S(2)}, u32[]{:S(2)}) %collective-permute-start.2) | collective-permute-done | bytes 65568 | tf_op jit(solution)/shard_map/ppermute | solution.py:35
  27.5 1.7 collective-permute-start.5
  30.5 10.4 %collective-permute-done.5.refs_3_ = bf16[128,2048]{1,0:T(8,128)(2,1)S(1)} collective-permute-done((bf16[128,2048]{1,0:T(8,128)(2,1)S(1)}, bf16[128,2048]{1,0:T(8,128)(2,1)S(1)}, u32[]{:S(2)}, u32[]{:S(2)}) %collective-permute-start.5) | collective-permute-done | bytes 524320 | tf_op jit(solution)/shard_map/ppermute | solution.py:35
  43.6 1.8 queries.1
  45.4 12.2 %all-gather.2.cloned.1.call-done.both = bf16[4224,256]{1,0:T(8,128)(2,1)} async-done(((bf16[528,256]{1,0:T(8,128)(2,1)}), bf16[4224,256]{1,0:T(8,128)(2,1)}) %all-gather.2.cloned.1.call-update) | async-done | bytes 2162704 | tf_op jit(solution)/shard_map/all_gather | solution.py:344
  59.2 1.7 attention.4
  61.0 2.5 collective-permute-start.6
  63.4 1.7 attention.5
  65.8 1.7 attention.6
  68.1 1.9 attention.7.total
  70.0 6.8 %collective-permute-done.6.partial = bf16[128,2048]{1,0:T(8,128)(2,1)S(1)} collective-permute-done((bf16[128,2048]{1,0:T(8,128)(2,1)S(1)}, bf16[128,2048]{1,0:T(8,128)(2,1)S(1)}, u32[]{:S(2)}, u32[]{:S(2)}) %collective-permute-start.6) | collective-permute-done | bytes 524320 | tf_op jit(solution)/shard_map/ppermute | solution.py:35
  76.9 11.1 %collective-permute-done.7.partial = bf16[128,2048]{1,0:T(8,128)(2,1)S(1)} collective-permute-done((bf16[128,2048]{1,0:T(8,128)(2,1)S(1)}, bf16[128,2048]{1,0:T(8,128)(2,1)S(1)}, u32[]{:S(2)}, u32[]{:S(2)}) %collective-permute-start.7) | collective-permute-done | bytes 524320 | tf_op jit(solution)/shard_map/ppermute | solution.py:35
  88.7 2.9 collective-permute-start.11
  96.3 6.3 %collective-permute-start.9 = (bf16[128,2048]{1,0:T(8,128)(2,1)S(1)}, bf16[128,2048]{1,0:T(8,128)(2,1)S(1)}, u32[]{:S(2)}, u32[]{:S(2)}) collective-permute-start(bf16[128,2048]{1,0:T(8,128)(2,1)S(1)} %get-tuple-element.109.same), channel_id=1, source_target_pairs={{0,16},{4,20},{8,24},{12,28},{16,0},{20,4},{24,8},{28,12},{1,17},{... | collective-permute-start | bytes 1572872 | tf_op jit(solution)/shard_map/ppermute | solution.py:35
  102.6 8.7 %collective-permute-done.11.same = bf16[128,2048]{1,0:T(8,128)(2,1)S(1)} collective-permute-done((bf16[128,2048]{1,0:T(8,128)(2,1)S(1)}, bf16[128,2048]{1,0:T(8,128)(2,1)S(1)}, u32[]{:S(2)}, u32[]{:S(2)}) %collective-permute-start.11) | collective-permute-done | bytes 524320 | tf_op jit(solution)/shard_map/ppermute | solution.py:35
  111.3 2.3 collective-permute-done.14.refs_2_
  113.6 11.3 %collective-permute-done.9.same = bf16[128,2048]{1,0:T(8,128)(2,1)S(1)} collective-permute-done((bf16[128,2048]{1,0:T(8,128)(2,1)S(1)}, bf16[128,2048]{1,0:T(8,128)(2,1)S(1)}, u32[]{:S(2)}, u32[]{:S(2)}) %collective-permute-start.9) | collective-permute-done | bytes 524320 | tf_op jit(solution)/shard_map/ppermute | solution.py:35
  124.9 4.7 %collective-permute-start.23 = (bf16[128,2048]{1,0:T(8,128)(2,1)S(1)}, bf16[128,2048]{1,0:T(8,128)(2,1)S(1)}, u32[]{:S(2)}, u32[]{:S(2)}) collective-permute-start(bf16[128,2048]{1,0:T(8,128)(2,1)S(1)} %get-tuple-element.109.same), channel_id=1, source_target_pairs={{0,24},{4,28},{8,16},{12,20},{16,8},{20,12},{24,0},{28,4},{1,25},{... | collective-permute-start | bytes 1572872 | tf_op jit(solution)/shard_map/ppermute | solution.py:35
  131.6 2.0 collective-permute-start.21
  134.2 6.0 %collective-permute-done.23.same = bf16[128,2048]{1,0:T(8,128)(2,1)S(1)} collective-permute-done((bf16[128,2048]{1,0:T(8,128)(2,1)S(1)}, bf16[128,2048]{1,0:T(8,128)(2,1)S(1)}, u32[]{:S(2)}, u32[]{:S(2)}) %collective-permute-start.23) | collective-permute-done | bytes 524320 | tf_op jit(solution)/shard_map/ppermute | solution.py:35
  141.3 9.3 %collective-permute-done.19.refs_2_ = bf16[96,2048]{1,0:T(8,128)(2,1)S(1)} collective-permute-done((bf16[96,2048]{1,0:T(8,128)(2,1)S(1)}, bf16[96,2048]{1,0:T(8,128)(2,1)S(1)}, u32[]{:S(2)}, u32[]{:S(2)}) %collective-permute-start.19) | collective-permute-done | bytes 393248 | tf_op jit(solution)/shard_map/ppermute | solution.py:35
  151.5 2.0 collective-permute-start.22
  155.3 14.6 %collective-permute-done.20.refs_2_ = bf16[96,2048]{1,0:T(8,128)(2,1)S(1)} collective-permute-done((bf16[96,2048]{1,0:T(8,128)(2,1)S(1)}, bf16[96,2048]{1,0:T(8,128)(2,1)S(1)}, u32[]{:S(2)}, u32[]{:S(2)}) %collective-permute-start.20) | collective-permute-done | bytes 393248 | tf_op jit(solution)/shard_map/ppermute | solution.py:35
  170.7 2.0 collective-permute-start.29
  173.4 3.8 %expert.4 = (bf16[96,2048]{1,0:T(8,128)(2,1)S(1)}, bf16[96,2048]{1,0:T(8,128)(2,1)S(1)}, bf16[96,2048]{1,0:T(8,128)(2,1)S(1)}, bf16[96,2048]{1,0:T(8,128)(2,1)S(1)}) custom-call(bf16[96,2048]{1,0:T(8,128)(2,1)S(1)} %get-tuple-element.90.refs_0_, bf16[96,2048]{1,0:T(8,128)(2,1)S(1)} %collective-permute-done.18.refs_1_, ...), custom_call_target="tpu_custom_call" | custom-call | flops 1000 | bytes 1000 | tf_op jit(solution)/shard_map/expert/pallas_call | solution.py:262
  177.2 10.9 %collective-permute-done.27.refs_2_ = bf16[96,2048]{1,0:T(8,128)(2,1)S(1)} collective-permute-done((bf16[96,2048]{1,0:T(8,128)(2,1)S(1)}, bf16[96,2048]{1,0:T(8,128)(2,1)S(1)}, u32[]{:S(2)}, u32[]{:S(2)}) %collective-permute-start.27) | collective-permute-done | bytes 393248 | tf_op jit(solution)/shard_map/ppermute | solution.py:35
  188.1 1.7 collective-permute-start.30
  191.6 9.5 %collective-permute-done.30.refs_3_ = bf16[96,2048]{1,0:T(8,128)(2,1)S(1)} collective-permute-done((bf16[96,2048]{1,0:T(8,128)(2,1)S(1)}, bf16[96,2048]{1,0:T(8,128)(2,1)S(1)}, u32[]{:S(2)}, u32[]{:S(2)}) %collective-permute-start.30) | collective-permute-done | bytes 393248 | tf_op jit(solution)/shard_map/ppermute | solution.py:35
  201.1 5.9 %collective-permute-done.28.refs_2_ = bf16[96,2048]{1,0:T(8,128)(2,1)S(1)} collective-permute-done((bf16[96,2048]{1,0:T(8,128)(2,1)S(1)}, bf16[96,2048]{1,0:T(8,128)(2,1)S(1)}, u32[]{:S(2)}, u32[]{:S(2)}) %collective-permute-start.28) | collective-permute-done | bytes 393248 | tf_op jit(solution)/shard_map/ppermute | solution.py:35
  208.1 3.9 %expert.5 = (bf16[96,2048]{1,0:T(8,128)(2,1)S(1)}, bf16[96,2048]{1,0:T(8,128)(2,1)S(1)}, bf16[96,2048]{1,0:T(8,128)(2,1)S(1)}, bf16[96,2048]{1,0:T(8,128)(2,1)S(1)}) custom-call(bf16[96,2048]{1,0:T(8,128)(2,1)S(1)} %get-tuple-element.123.refs_0_, bf16[96,2048]{1,0:T(8,128)(2,1)S(1)} %collective-permute-done.25.refs_1_, ...), custom_call_target="tpu_custom_call" | custom-call | flops 1000 | bytes 1000 | tf_op jit(solution)/shard_map/expert/pallas_call | solution.py:262
  211.9 1.7 collective-permute-start.35
  215.6 9.2 %collective-permute-done.35.refs_3_ = bf16[96,2048]{1,0:T(8,128)(2,1)S(1)} collective-permute-done((bf16[96,2048]{1,0:T(8,128)(2,1)S(1)}, bf16[96,2048]{1,0:T(8,128)(2,1)S(1)}, u32[]{:S(2)}, u32[]{:S(2)}) %collective-permute-start.35) | collective-permute-done | bytes 393248 | tf_op jit(solution)/shard_map/ppermute | solution.py:35
  224.9 8.0 %collective-permute-done.34.refs_2_ = bf16[96,2048]{1,0:T(8,128)(2,1)S(1)} collective-permute-done((bf16[96,2048]{1,0:T(8,128)(2,1)S(1)}, bf16[96,2048]{1,0:T(8,128)(2,1)S(1)}, u32[]{:S(2)}, u32[]{:S(2)}) %collective-permute-start.34) | collective-permute-done | bytes 393248 | tf_op jit(solution)/shard_map/ppermute | solution.py:35
  234.0 4.1 %expert.6 = (bf16[96,2048]{1,0:T(8,128)(2,1)S(1)}, bf16[96,2048]{1,0:T(8,128)(2,1)S(1)}, bf16[96,2048]{1,0:T(8,128)(2,1)S(1)}, bf16[96,2048]{1,0:T(8,128)(2,1)S(1)}) custom-call(bf16[96,2048]{1,0:T(8,128)(2,1)S(1)} %get-tuple-element.135.refs_0_, bf16[96,2048]{1,0:T(8,128)(2,1)S(1)} %collective-permute-done.17.refs_1_, ...), custom_call_target="tpu_custom_call" | custom-call | flops 1000 | bytes 1000 | tf_op jit(solution)/shard_map/expert/pallas_call | solution.py:262
  238.1 1.6 collective-permute-start.40
  241.6 3.1 %collective-permute-start.32 = (bf16[128,2048]{1,0:T(8,128)(2,1)S(1)}, bf16[128,2048]{1,0:T(8,128)(2,1)S(1)}, u32[]{:S(2)}, u32[]{:S(2)}) collective-permute-start(bf16[128,2048]{1,0:T(8,128)(2,1)S(1)} %add_convert_fusion.3), channel_id=1, source_target_pairs={{0,16},{4,20},{8,24},{12,28},{16,0},{20,4},{24,8},{28,12},{1,17},{... | collective-permute-start | bytes 1572872 | tf_op jit(solution)/shard_map/ppermute | solution.py:35
  244.9 6.1 %collective-permute-done.40.refs_3_ = bf16[96,2048]{1,0:T(8,128)(2,1)S(1)} collective-permute-done((bf16[96,2048]{1,0:T(8,128)(2,1)S(1)}, bf16[96,2048]{1,0:T(8,128)(2,1)S(1)}, u32[]{:S(2)}, u32[]{:S(2)}) %collective-permute-start.40) | collective-permute-done | bytes 393248 | tf_op jit(solution)/shard_map/ppermute | solution.py:35
  251.0 8.0 %collective-permute-done.39.refs_2_ = bf16[96,2048]{1,0:T(8,128)(2,1)S(1)} collective-permute-done((bf16[96,2048]{1,0:T(8,128)(2,1)S(1)}, bf16[96,2048]{1,0:T(8,128)(2,1)S(1)}, u32[]{:S(2)}, u32[]{:S(2)}) %collective-permute-start.39) | collective-permute-done | bytes 393248 | tf_op jit(solution)/shard_map/ppermute | solution.py:35
  260.1 3.8 %expert.7 = (bf16[96,2048]{1,0:T(8,128)(2,1)S(1)}, bf16[96,2048]{1,0:T(8,128)(2,1)S(1)}, bf16[96,2048]{1,0:T(8,128)(2,1)S(1)}, bf16[96,2048]{1,0:T(8,128)(2,1)S(1)}) custom-call(bf16[96,2048]{1,0:T(8,128)(2,1)S(1)} %get-tuple-element.146.refs_0_, bf16[96,2048]{1,0:T(8,128)(2,1)S(1)} %collective-permute-done.13.refs_1_, ...), custom_call_target="tpu_custom_call" | custom-call | flops 1000 | bytes 1000 | tf_op jit(solution)/shard_map/expert/pallas_call | solution.py:262
  264.0 1.6 collective-permute-start.45
  267.7 2.2 collective-permute-start.37
  270.0 6.9 %collective-permute-done.45.refs_3_ = bf16[96,2048]{1,0:T(8,128)(2,1)S(1)} collective-permute-done((bf16[96,2048]{1,0:T(8,128)(2,1)S(1)}, bf16[96,2048]{1,0:T(8,128)(2,1)S(1)}, u32[]{:S(2)}, u32[]{:S(2)}) %collective-permute-start.45) | collective-permute-done | bytes 393248 | tf_op jit(solution)/shard_map/ppermute | solution.py:35
  276.9 7.9 %collective-permute-done.44.refs_2_ = bf16[96,2048]{1,0:T(8,128)(2,1)S(1)} collective-permute-done((bf16[96,2048]{1,0:T(8,128)(2,1)S(1)}, bf16[96,2048]{1,0:T(8,128)(2,1)S(1)}, u32[]{:S(2)}, u32[]{:S(2)}) %collective-permute-start.44) | collective-permute-done | bytes 393248 | tf_op jit(solution)/shard_map/ppermute | solution.py:35
  286.0 3.0 collective-permute-start.42
  289.0 12.5 %collective-permute-done.42 = bf16[128,2048]{1,0:T(8,128)(2,1)S(1)} collective-permute-done((bf16[128,2048]{1,0:T(8,128)(2,1)S(1)}, bf16[128,2048]{1,0:T(8,128)(2,1)S(1)}, u32[]{:S(2)}, u32[]{:S(2)}) %collective-permute-start.42) | collective-permute-done | bytes 524320 | tf_op jit(solution)/shard_map/ppermute | solution.py:35
  (123 shorter events, 42.0 us)
Async XLA Ops:
  6.5 51.1 %all-gather.2.cloned.1.call-start = ((), (), s32[]{:S(2)}) async-start(), calls=%async_computation | async-start | bytes 2433024 | tf_op jit(solution)/shard_map/all_gather | solution.py:344
  6.5 20.1 %collective-permute-start.1 = (bf16[128,2048]{1,0:T(8,128)(2,1)}, bf16[128,2048]{1,0:T(8,128)(2,1)S(1)}, u32[]{:S(2)}, u32[]{:S(2)}) collective-permute-start(bf16[128,2048]{1,0:T(8,128)(2,1)} %tokens.1), channel_id=1, source_target_pairs={{0,2},{1,3},{2,0},{3,1},{4,6},{5,7},{6,4},{7,5},{8,10},{9,11},{10,... | collective-permute-start | bytes 1572872 | tf_op jit(solution)/shard_map/ppermute | solution.py:35
  9.5 17.2 %collective-permute-start = (bf16[128,2048]{1,0:T(8,128)(2,1)}, bf16[128,2048]{1,0:T(8,128)(2,1)S(1)}, u32[]{:S(2)}, u32[]{:S(2)}) collective-permute-start(bf16[128,2048]{1,0:T(8,128)(2,1)} %tokens.1), channel_id=1, source_target_pairs={{0,1},{1,0},{2,3},{3,2},{4,5},{5,4},{6,7},{7,6},{8,9},{9,8},{10,11... | collective-permute-start | bytes 1572872 | tf_op jit(solution)/shard_map/ppermute | solution.py:35
  17.1 8.9 %collective-permute-start.4 = (bf16[128,256]{1,0:T(8,128)(2,1)S(1)}, bf16[128,256]{1,0:T(8,128)(2,1)S(1)}, u32[]{:S(2)}, u32[]{:S(2)}) collective-permute-start(bf16[128,256]{1,0:T(8,128)(2,1)S(1)} %get-tuple-element.161), channel_id=1, source_target_pairs={{0,3},{1,2},{2,1},{3,0},{4,7},{5,6},{6,5},{7,4},{8,11},{9,10},{10,... | collective-permute-start | bytes 196616 | tf_op jit(solution)/shard_map/ppermute | solution.py:35
  17.2 8.8 %collective-permute-start.3 = (bf16[128,256]{1,0:T(8,128)(2,1)S(1)}, bf16[128,256]{1,0:T(8,128)(2,1)S(1)}, u32[]{:S(2)}, u32[]{:S(2)}) collective-permute-start(bf16[128,256]{1,0:T(8,128)(2,1)S(1)} %get-tuple-element.162), channel_id=1, source_target_pairs={{0,2},{1,3},{2,0},{3,1},{4,6},{5,7},{6,4},{7,5},{8,10},{9,11},{10,... | collective-permute-start | bytes 196616 | tf_op jit(solution)/shard_map/ppermute | solution.py:35
  19.1 6.8 %collective-permute-start.2 = (bf16[128,256]{1,0:T(8,128)(2,1)S(1)}, bf16[128,256]{1,0:T(8,128)(2,1)S(1)}, u32[]{:S(2)}, u32[]{:S(2)}) collective-permute-start(bf16[128,256]{1,0:T(8,128)(2,1)S(1)} %get-tuple-element.163), channel_id=1, source_target_pairs={{0,1},{1,0},{2,3},{3,2},{4,5},{5,4},{6,7},{7,6},{8,9},{9,8},{10,11... | collective-permute-start | bytes 196616 | tf_op jit(solution)/shard_map/ppermute | solution.py:35
  27.5 13.4 %collective-permute-start.5 = (bf16[128,2048]{1,0:T(8,128)(2,1)S(1)}, bf16[128,2048]{1,0:T(8,128)(2,1)S(1)}, u32[]{:S(2)}, u32[]{:S(2)}) collective-permute-start(bf16[128,2048]{1,0:T(8,128)(2,1)S(1)} %copy-done.6), channel_id=1, source_target_pairs={{0,3},{1,2},{2,1},{3,0},{4,7},{5,6},{6,5},{7,4},{8,11},{9,10},{10,... | collective-permute-start | bytes 1572872 | tf_op jit(solution)/shard_map/ppermute | solution.py:35
  61.0 15.9 %collective-permute-start.6 = (bf16[128,2048]{1,0:T(8,128)(2,1)S(1)}, bf16[128,2048]{1,0:T(8,128)(2,1)S(1)}, u32[]{:S(2)}, u32[]{:S(2)}) collective-permute-start(bf16[128,2048]{1,0:T(8,128)(2,1)S(1)} %attention.4), channel_id=1, source_target_pairs={{0,3},{1,2},{2,1},{3,0},{4,7},{5,6},{6,5},{7,4},{8,11},{9,10},{10,... | collective-permute-start | bytes 1572872 | tf_op jit(solution)/shard_map/ppermute | solution.py:35
  65.1 22.9 %collective-permute-start.7 = (bf16[128,2048]{1,0:T(8,128)(2,1)S(1)}, bf16[128,2048]{1,0:T(8,128)(2,1)S(1)}, u32[]{:S(2)}, u32[]{:S(2)}) collective-permute-start(bf16[128,2048]{1,0:T(8,128)(2,1)S(1)} %attention.5), channel_id=1, source_target_pairs={{0,1},{1,0},{2,3},{3,2},{4,5},{5,4},{6,7},{7,6},{8,9},{9,8},{10,11... | collective-permute-start | bytes 1572872 | tf_op jit(solution)/shard_map/ppermute | solution.py:35
  67.5 20.6 %collective-permute-start.8 = (bf16[128,2048]{1,0:T(8,128)(2,1)S(1)}, bf16[128,2048]{1,0:T(8,128)(2,1)S(1)}, u32[]{:S(2)}, u32[]{:S(2)}) collective-permute-start(bf16[128,2048]{1,0:T(8,128)(2,1)S(1)} %attention.6), channel_id=1, source_target_pairs={{0,2},{1,3},{2,0},{3,1},{4,6},{5,7},{6,4},{7,5},{8,10},{9,11},{10,... | collective-permute-start | bytes 1572872 | tf_op jit(solution)/shard_map/ppermute | solution.py:35
  88.6 3.1 collective-permute-start.12
  88.7 22.5 %collective-permute-start.11 = (bf16[128,2048]{1,0:T(8,128)(2,1)S(1)}, bf16[128,2048]{1,0:T(8,128)(2,1)S(1)}, u32[]{:S(2)}, u32[]{:S(2)}) collective-permute-start(bf16[128,2048]{1,0:T(8,128)(2,1)S(1)} %get-tuple-element.109.same), channel_id=1, source_target_pairs={{0,8},{4,12},{8,0},{12,4},{16,24},{20,28},{24,16},{28,20},{1,9},{5... | collective-permute-start | bytes 1572872 | tf_op jit(solution)/shard_map/ppermute | solution.py:35
  92.7 18.6 %collective-permute-start.13 = (bf16[96,2048]{1,0:T(8,128)(2,1)S(1)}, bf16[96,2048]{1,0:T(8,128)(2,1)S(1)}, u32[]{:S(2)}, u32[]{:S(2)}) collective-permute-start(bf16[96,2048]{1,0:T(8,128)(2,1)S(1)} %get-tuple-element.92), channel_id=1, source_target_pairs={{0,1},{1,0},{2,3},{3,2},{4,5},{5,4},{6,7},{7,6},{8,9},{9,8},{10,11... | collective-permute-start | bytes 1179656 | tf_op jit(solution)/shard_map/ppermute | solution.py:35
  94.3 19.2 %collective-permute-start.14 = (bf16[96,2048]{1,0:T(8,128)(2,1)S(1)}, bf16[96,2048]{1,0:T(8,128)(2,1)S(1)}, u32[]{:S(2)}, u32[]{:S(2)}) collective-permute-start(bf16[96,2048]{1,0:T(8,128)(2,1)S(1)} %get-tuple-element.93), channel_id=1, source_target_pairs={{0,2},{1,3},{2,0},{3,1},{4,6},{5,7},{6,4},{7,5},{8,10},{9,11},{10,... | collective-permute-start | bytes 1179656 | tf_op jit(solution)/shard_map/ppermute | solution.py:35
  95.5 18.0 %collective-permute-start.15 = (bf16[96,2048]{1,0:T(8,128)(2,1)S(1)}, bf16[96,2048]{1,0:T(8,128)(2,1)S(1)}, u32[]{:S(2)}, u32[]{:S(2)}) collective-permute-start(bf16[96,2048]{1,0:T(8,128)(2,1)S(1)} %get-tuple-element.94), channel_id=1, source_target_pairs={{0,3},{1,2},{2,1},{3,0},{4,7},{5,6},{6,5},{7,4},{8,11},{9,10},{10,... | collective-permute-start | bytes 1179656 | tf_op jit(solution)/shard_map/ppermute | solution.py:35
  96.3 28.6 %collective-permute-start.9 = (bf16[128,2048]{1,0:T(8,128)(2,1)S(1)}, bf16[128,2048]{1,0:T(8,128)(2,1)S(1)}, u32[]{:S(2)}, u32[]{:S(2)}) collective-permute-start(bf16[128,2048]{1,0:T(8,128)(2,1)S(1)} %get-tuple-element.109.same), channel_id=1, source_target_pairs={{0,16},{4,20},{8,24},{12,28},{16,0},{20,4},{24,8},{28,12},{1,17},{... | collective-permute-start | bytes 1572872 | tf_op jit(solution)/shard_map/ppermute | solution.py:35
  113.5 16.0 %collective-permute-start.16 = (bf16[128,2048]{1,0:T(8,128)(2,1)S(1)}, bf16[128,2048]{1,0:T(8,128)(2,1)S(1)}, u32[]{:S(2)}, u32[]{:S(2)}) collective-permute-start(bf16[128,2048]{1,0:T(8,128)(2,1)S(1)} %collective-permute-done.11.same), channel_id=1, source_target_pairs={{0,4},{4,0},{8,12},{12,8},{16,20},{20,16},{24,28},{28,24},{1,5},{5... | collective-permute-start | bytes 1572872 | tf_op jit(solution)/shard_map/ppermute | solution.py:35
  124.9 15.3 %collective-permute-start.23 = (bf16[128,2048]{1,0:T(8,128)(2,1)S(1)}, bf16[128,2048]{1,0:T(8,128)(2,1)S(1)}, u32[]{:S(2)}, u32[]{:S(2)}) collective-permute-start(bf16[128,2048]{1,0:T(8,128)(2,1)S(1)} %get-tuple-element.109.same), channel_id=1, source_target_pairs={{0,24},{4,28},{8,16},{12,20},{16,8},{20,12},{24,0},{28,4},{1,25},{... | collective-permute-start | bytes 1572872 | tf_op jit(solution)/shard_map/ppermute | solution.py:35
  129.5 10.7 %collective-permute-start.10 = (bf16[128,2048]{1,0:T(8,128)(2,1)S(1)}, bf16[128,2048]{1,0:T(8,128)(2,1)S(1)}, u32[]{:S(2)}, u32[]{:S(2)}) collective-permute-start(bf16[128,2048]{1,0:T(8,128)(2,1)S(1)} %collective-permute-done.9.same), channel_id=1, source_target_pairs={{0,4},{4,0},{8,12},{12,8},{16,20},{20,16},{24,28},{28,24},{1,5},{5... | collective-permute-start | bytes 1572872 | tf_op jit(solution)/shard_map/ppermute | solution.py:35
  130.6 20.0 %collective-permute-start.19 = (bf16[96,2048]{1,0:T(8,128)(2,1)S(1)}, bf16[96,2048]{1,0:T(8,128)(2,1)S(1)}, u32[]{:S(2)}, u32[]{:S(2)}) collective-permute-start(bf16[96,2048]{1,0:T(8,128)(2,1)S(1)} %get-tuple-element.101), channel_id=1, source_target_pairs={{0,2},{1,3},{2,0},{3,1},{4,6},{5,7},{6,4},{7,5},{8,10},{9,11},{10,... | collective-permute-start | bytes 1179656 | tf_op jit(solution)/shard_map/ppermute | solution.py:35
  131.6 20.0 %collective-permute-start.21 = (bf16[96,2048]{1,0:T(8,128)(2,1)S(1)}, bf16[96,2048]{1,0:T(8,128)(2,1)S(1)}, u32[]{:S(2)}, u32[]{:S(2)}) collective-permute-start(bf16[96,2048]{1,0:T(8,128)(2,1)S(1)} %get-tuple-element.105), channel_id=1, source_target_pairs={{0,3},{1,2},{2,1},{3,0},{4,7},{5,6},{6,5},{7,4},{8,11},{9,10},{10,... | collective-permute-start | bytes 1179656 | tf_op jit(solution)/shard_map/ppermute | solution.py:35
  133.6 20.0 %collective-permute-start.17 = (bf16[96,2048]{1,0:T(8,128)(2,1)S(1)}, bf16[96,2048]{1,0:T(8,128)(2,1)S(1)}, u32[]{:S(2)}, u32[]{:S(2)}) collective-permute-start(bf16[96,2048]{1,0:T(8,128)(2,1)S(1)} %get-tuple-element.97), channel_id=1, source_target_pairs={{0,1},{1,0},{2,3},{3,2},{4,5},{5,4},{6,7},{7,6},{8,9},{9,8},{10,11... | collective-permute-start | bytes 1179656 | tf_op jit(solution)/shard_map/ppermute | solution.py:35
  140.2 13.9 %collective-permute-start.24 = (bf16[128,2048]{1,0:T(8,128)(2,1)S(1)}, bf16[128,2048]{1,0:T(8,128)(2,1)S(1)}, u32[]{:S(2)}, u32[]{:S(2)}) collective-permute-start(bf16[128,2048]{1,0:T(8,128)(2,1)S(1)} %collective-permute-done.23.same), channel_id=1, source_target_pairs={{0,4},{4,0},{8,12},{12,8},{16,20},{20,16},{24,28},{28,24},{1,5},{5... | collective-permute-start | bytes 1572872 | tf_op jit(solution)/shard_map/ppermute | solution.py:35
  150.7 19.2 %collective-permute-start.20 = (bf16[96,2048]{1,0:T(8,128)(2,1)S(1)}, bf16[96,2048]{1,0:T(8,128)(2,1)S(1)}, u32[]{:S(2)}, u32[]{:S(2)}) collective-permute-start(bf16[96,2048]{1,0:T(8,128)(2,1)S(1)} %get-tuple-element.102), channel_id=1, source_target_pairs={{0,2},{1,3},{2,0},{3,1},{4,6},{5,7},{6,4},{7,5},{8,10},{9,11},{10,... | collective-permute-start | bytes 1179656 | tf_op jit(solution)/shard_map/ppermute | solution.py:35
  151.5 19.2 %collective-permute-start.22 = (bf16[96,2048]{1,0:T(8,128)(2,1)S(1)}, bf16[96,2048]{1,0:T(8,128)(2,1)S(1)}, u32[]{:S(2)}, u32[]{:S(2)}) collective-permute-start(bf16[96,2048]{1,0:T(8,128)(2,1)S(1)} %get-tuple-element.106), channel_id=1, source_target_pairs={{0,3},{1,2},{2,1},{3,0},{4,7},{5,6},{6,5},{7,4},{8,11},{9,10},{10,... | collective-permute-start | bytes 1179656 | tf_op jit(solution)/shard_map/ppermute | solution.py:35
  153.6 19.2 %collective-permute-start.18 = (bf16[96,2048]{1,0:T(8,128)(2,1)S(1)}, bf16[96,2048]{1,0:T(8,128)(2,1)S(1)}, u32[]{:S(2)}, u32[]{:S(2)}) collective-permute-start(bf16[96,2048]{1,0:T(8,128)(2,1)S(1)} %get-tuple-element.98), channel_id=1, source_target_pairs={{0,1},{1,0},{2,3},{3,2},{4,5},{5,4},{6,7},{7,6},{8,9},{9,8},{10,11... | collective-permute-start | bytes 1179656 | tf_op jit(solution)/shard_map/ppermute | solution.py:35
  169.8 18.3 %collective-permute-start.27 = (bf16[96,2048]{1,0:T(8,128)(2,1)S(1)}, bf16[96,2048]{1,0:T(8,128)(2,1)S(1)}, u32[]{:S(2)}, u32[]{:S(2)}) collective-permute-start(bf16[96,2048]{1,0:T(8,128)(2,1)S(1)} %get-tuple-element.115), channel_id=1, source_target_pairs={{0,2},{1,3},{2,0},{3,1},{4,6},{5,7},{6,4},{7,5},{8,10},{9,11},{10,... | collective-permute-start | bytes 1179656 | tf_op jit(solution)/shard_map/ppermute | solution.py:35
  170.7 17.4 %collective-permute-start.29 = (bf16[96,2048]{1,0:T(8,128)(2,1)S(1)}, bf16[96,2048]{1,0:T(8,128)(2,1)S(1)}, u32[]{:S(2)}, u32[]{:S(2)}) collective-permute-start(bf16[96,2048]{1,0:T(8,128)(2,1)S(1)} %get-tuple-element.119), channel_id=1, source_target_pairs={{0,3},{1,2},{2,1},{3,0},{4,7},{5,6},{6,5},{7,4},{8,11},{9,10},{10,... | collective-permute-start | bytes 1179656 | tf_op jit(solution)/shard_map/ppermute | solution.py:35
  172.7 18.3 %collective-permute-start.25 = (bf16[96,2048]{1,0:T(8,128)(2,1)S(1)}, bf16[96,2048]{1,0:T(8,128)(2,1)S(1)}, u32[]{:S(2)}, u32[]{:S(2)}) collective-permute-start(bf16[96,2048]{1,0:T(8,128)(2,1)S(1)} %get-tuple-element.111), channel_id=1, source_target_pairs={{0,1},{1,0},{2,3},{3,2},{4,5},{5,4},{6,7},{7,6},{8,9},{9,8},{10,11... | collective-permute-start | bytes 1179656 | tf_op jit(solution)/shard_map/ppermute | solution.py:35
  188.1 13.0 %collective-permute-start.30 = (bf16[96,2048]{1,0:T(8,128)(2,1)S(1)}, bf16[96,2048]{1,0:T(8,128)(2,1)S(1)}, u32[]{:S(2)}, u32[]{:S(2)}) collective-permute-start(bf16[96,2048]{1,0:T(8,128)(2,1)S(1)} %get-tuple-element.120), channel_id=1, source_target_pairs={{0,3},{1,2},{2,1},{3,0},{4,7},{5,6},{6,5},{7,4},{8,11},{9,10},{10,... | collective-permute-start | bytes 1179656 | tf_op jit(solution)/shard_map/ppermute | solution.py:35
  189.9 17.1 %collective-permute-start.28 = (bf16[96,2048]{1,0:T(8,128)(2,1)S(1)}, bf16[96,2048]{1,0:T(8,128)(2,1)S(1)}, u32[]{:S(2)}, u32[]{:S(2)}) collective-permute-start(bf16[96,2048]{1,0:T(8,128)(2,1)S(1)} %get-tuple-element.116), channel_id=1, source_target_pairs={{0,2},{1,3},{2,0},{3,1},{4,6},{5,7},{6,4},{7,5},{8,10},{9,11},{10,... | collective-permute-start | bytes 1179656 | tf_op jit(solution)/shard_map/ppermute | solution.py:35
  191.0 15.9 %collective-permute-start.26 = (bf16[96,2048]{1,0:T(8,128)(2,1)S(1)}, bf16[96,2048]{1,0:T(8,128)(2,1)S(1)}, u32[]{:S(2)}, u32[]{:S(2)}) collective-permute-start(bf16[96,2048]{1,0:T(8,128)(2,1)S(1)} %get-tuple-element.112), channel_id=1, source_target_pairs={{0,1},{1,0},{2,3},{3,2},{4,5},{5,4},{6,7},{7,6},{8,9},{9,8},{10,11... | collective-permute-start | bytes 1179656 | tf_op jit(solution)/shard_map/ppermute | solution.py:35
  208.0 7.5 %collective-permute-start.31 = (bf16[128,2048]{1,0:T(8,128)(2,1)S(1)}, bf16[128,2048]{1,0:T(8,128)(2,1)S(1)}, u32[]{:S(2)}, u32[]{:S(2)}) collective-permute-start(bf16[128,2048]{1,0:T(8,128)(2,1)S(1)} %get-tuple-element.122), channel_id=1, source_target_pairs={{0,4},{4,0},{8,12},{12,8},{16,20},{20,16},{24,28},{28,24},{1,5},{5... | collective-permute-start | bytes 1572872 | tf_op jit(solution)/shard_map/ppermute | solution.py:35
  211.9 12.9 %collective-permute-start.35 = (bf16[96,2048]{1,0:T(8,128)(2,1)S(1)}, bf16[96,2048]{1,0:T(8,128)(2,1)S(1)}, u32[]{:S(2)}, u32[]{:S(2)}) collective-permute-start(bf16[96,2048]{1,0:T(8,128)(2,1)S(1)} %get-tuple-element.131), channel_id=1, source_target_pairs={{0,3},{1,2},{2,1},{3,0},{4,7},{5,6},{6,5},{7,4},{8,11},{9,10},{10,... | collective-permute-start | bytes 1179656 | tf_op jit(solution)/shard_map/ppermute | solution.py:35
  213.6 19.2 %collective-permute-start.34 = (bf16[96,2048]{1,0:T(8,128)(2,1)S(1)}, bf16[96,2048]{1,0:T(8,128)(2,1)S(1)}, u32[]{:S(2)}, u32[]{:S(2)}) collective-permute-start(bf16[96,2048]{1,0:T(8,128)(2,1)S(1)} %get-tuple-element.129), channel_id=1, source_target_pairs={{0,2},{1,3},{2,0},{3,1},{4,6},{5,7},{6,4},{7,5},{8,10},{9,11},{10,... | collective-permute-start | bytes 1179656 | tf_op jit(solution)/shard_map/ppermute | solution.py:35
  214.3 18.6 %collective-permute-start.33 = (bf16[96,2048]{1,0:T(8,128)(2,1)S(1)}, bf16[96,2048]{1,0:T(8,128)(2,1)S(1)}, u32[]{:S(2)}, u32[]{:S(2)}) collective-permute-start(bf16[96,2048]{1,0:T(8,128)(2,1)S(1)} %get-tuple-element.127), channel_id=1, source_target_pairs={{0,1},{1,0},{2,3},{3,2},{4,5},{5,4},{6,7},{7,6},{8,9},{9,8},{10,11... | collective-permute-start | bytes 1179656 | tf_op jit(solution)/shard_map/ppermute | solution.py:35
  233.9 10.9 %collective-permute-start.36 = (bf16[128,2048]{1,0:T(8,128)(2,1)S(1)}, bf16[128,2048]{1,0:T(8,128)(2,1)S(1)}, u32[]{:S(2)}, u32[]{:S(2)}) collective-permute-start(bf16[128,2048]{1,0:T(8,128)(2,1)S(1)} %get-tuple-element.133), channel_id=1, source_target_pairs={{0,4},{4,0},{8,12},{12,8},{16,20},{20,16},{24,28},{28,24},{1,5},{5... | collective-permute-start | bytes 1572872 | tf_op jit(solution)/shard_map/ppermute | solution.py:35
  238.1 12.9 %collective-permute-start.40 = (bf16[96,2048]{1,0:T(8,128)(2,1)S(1)}, bf16[96,2048]{1,0:T(8,128)(2,1)S(1)}, u32[]{:S(2)}, u32[]{:S(2)}) collective-permute-start(bf16[96,2048]{1,0:T(8,128)(2,1)S(1)} %get-tuple-element.143), channel_id=1, source_target_pairs={{0,3},{1,2},{2,1},{3,0},{4,7},{5,6},{6,5},{7,4},{8,11},{9,10},{10,... | collective-permute-start | bytes 1179656 | tf_op jit(solution)/shard_map/ppermute | solution.py:35
  239.7 19.2 %collective-permute-start.39 = (bf16[96,2048]{1,0:T(8,128)(2,1)S(1)}, bf16[96,2048]{1,0:T(8,128)(2,1)S(1)}, u32[]{:S(2)}, u32[]{:S(2)}) collective-permute-start(bf16[96,2048]{1,0:T(8,128)(2,1)S(1)} %get-tuple-element.141), channel_id=1, source_target_pairs={{0,2},{1,3},{2,0},{3,1},{4,6},{5,7},{6,4},{7,5},{8,10},{9,11},{10,... | collective-permute-start | bytes 1179656 | tf_op jit(solution)/shard_map/ppermute | solution.py:35
  240.4 18.5 %collective-permute-start.38 = (bf16[96,2048]{1,0:T(8,128)(2,1)S(1)}, bf16[96,2048]{1,0:T(8,128)(2,1)S(1)}, u32[]{:S(2)}, u32[]{:S(2)}) collective-permute-start(bf16[96,2048]{1,0:T(8,128)(2,1)S(1)} %get-tuple-element.139), channel_id=1, source_target_pairs={{0,1},{1,0},{2,3},{3,2},{4,5},{5,4},{6,7},{7,6},{8,9},{9,8},{10,11... | collective-permute-start | bytes 1179656 | tf_op jit(solution)/shard_map/ppermute | solution.py:35
  241.6 26.1 %collective-permute-start.32 = (bf16[128,2048]{1,0:T(8,128)(2,1)S(1)}, bf16[128,2048]{1,0:T(8,128)(2,1)S(1)}, u32[]{:S(2)}, u32[]{:S(2)}) collective-permute-start(bf16[128,2048]{1,0:T(8,128)(2,1)S(1)} %add_convert_fusion.3), channel_id=1, source_target_pairs={{0,16},{4,20},{8,24},{12,28},{16,0},{20,4},{24,8},{28,12},{1,17},{... | collective-permute-start | bytes 1572872 | tf_op jit(solution)/shard_map/ppermute | solution.py:35
  260.0 9.9 %collective-permute-start.41 = (bf16[128,2048]{1,0:T(8,128)(2,1)S(1)}, bf16[128,2048]{1,0:T(8,128)(2,1)S(1)}, u32[]{:S(2)}, u32[]{:S(2)}) collective-permute-start(bf16[128,2048]{1,0:T(8,128)(2,1)S(1)} %get-tuple-element.145), channel_id=1, source_target_pairs={{0,4},{4,0},{8,12},{12,8},{16,20},{20,16},{24,28},{28,24},{1,5},{5... | collective-permute-start | bytes 1572872 | tf_op jit(solution)/shard_map/ppermute | solution.py:35
  264.0 12.9 %collective-permute-start.45 = (bf16[96,2048]{1,0:T(8,128)(2,1)S(1)}, bf16[96,2048]{1,0:T(8,128)(2,1)S(1)}, u32[]{:S(2)}, u32[]{:S(2)}) collective-permute-start(bf16[96,2048]{1,0:T(8,128)(2,1)S(1)} %get-tuple-element.154), channel_id=1, source_target_pairs={{0,3},{1,2},{2,1},{3,0},{4,7},{5,6},{6,5},{7,4},{8,11},{9,10},{10,... | collective-permute-start | bytes 1179656 | tf_op jit(solution)/shard_map/ppermute | solution.py:35
  265.6 19.2 %collective-permute-start.44 = (bf16[96,2048]{1,0:T(8,128)(2,1)S(1)}, bf16[96,2048]{1,0:T(8,128)(2,1)S(1)}, u32[]{:S(2)}, u32[]{:S(2)}) collective-permute-start(bf16[96,2048]{1,0:T(8,128)(2,1)S(1)} %get-tuple-element.152), channel_id=1, source_target_pairs={{0,2},{1,3},{2,0},{3,1},{4,6},{5,7},{6,4},{7,5},{8,10},{9,11},{10,... | collective-permute-start | bytes 1179656 | tf_op jit(solution)/shard_map/ppermute | solution.py:35
  266.3 18.5 %collective-permute-start.43 = (bf16[96,2048]{1,0:T(8,128)(2,1)S(1)}, bf16[96,2048]{1,0:T(8,128)(2,1)S(1)}, u32[]{:S(2)}, u32[]{:S(2)}) collective-permute-start(bf16[96,2048]{1,0:T(8,128)(2,1)S(1)} %get-tuple-element.150), channel_id=1, source_target_pairs={{0,1},{1,0},{2,3},{3,2},{4,5},{5,4},{6,7},{7,6},{8,9},{9,8},{10,11... | collective-permute-start | bytes 1179656 | tf_op jit(solution)/shard_map/ppermute | solution.py:35
  267.7 21.2 %collective-permute-start.37 = (bf16[128,2048]{1,0:T(8,128)(2,1)S(1)}, bf16[128,2048]{1,0:T(8,128)(2,1)S(1)}, u32[]{:S(2)}, u32[]{:S(2)}) collective-permute-start(bf16[128,2048]{1,0:T(8,128)(2,1)S(1)} %add_convert_fusion.2), channel_id=1, source_target_pairs={{0,24},{4,28},{8,16},{12,20},{16,8},{20,12},{24,0},{28,4},{1,25},{... | collective-permute-start | bytes 1572872 | tf_op jit(solution)/shard_map/ppermute | solution.py:35
  285.9 3.1 collective-permute-start.46
  286.0 15.5 %collective-permute-start.42 = (bf16[128,2048]{1,0:T(8,128)(2,1)S(1)}, bf16[128,2048]{1,0:T(8,128)(2,1)S(1)}, u32[]{:S(2)}, u32[]{:S(2)}) collective-permute-start(bf16[128,2048]{1,0:T(8,128)(2,1)S(1)} %add_convert_fusion.1), channel_id=1, source_target_pairs={{0,8},{4,12},{8,0},{12,4},{16,24},{20,28},{24,16},{28,20},{1,9},{5... | collective-permute-start | bytes 1572872 | tf_op jit(solution)/shard_map/ppermute | solution.py:35
  (14 other events, 381.8 us)
Sparse Core Ops, SparseCore 0:
  27.5 30.0 all-gather.1

commit v5 on v4

--- a/solution.py
+++ b/solution.py
@@ -45,7 +45,10 @@
     half = HEAD_SIZE // 2
     frequency = theta_value ** (-2.0 * jnp.arange(half, dtype=jnp.float32) / HEAD_SIZE)
     angles = positions.astype(jnp.float32)[:, None] * frequency[None, :]
-    cosine, sine = jnp.cos(angles), jnp.sin(angles)
+    return jnp.cos(angles), jnp.sin(angles)
+
+
+def both_halves(cosine, sine):
     return jnp.concatenate([cosine, cosine], axis=1), jnp.concatenate([-sine, sine], axis=1)
 
 
@@ -68,8 +71,9 @@
     return copies
 
 
-def own_rows_kernel(experts, *refs):
-    sources, (out, table), targets, sems = refs[:9], refs[9:11], refs[11:20], refs[20]
+def own_rows_kernel(experts, heads_dev, place, *refs):
+    peers = len(refs) - 20
+    sources, outs, table, targets, sems = refs[:9], refs[9:-11], refs[-11], refs[-10:-1], refs[-1]
     copies = load_all(list(zip(sources, targets)), sems)
     ids, shares, tokens, gain, key_weight, value_weight, k_gain, cosine, sine = targets
     copies[0].wait()
@@ -101,11 +105,17 @@
     normed = rms_scale(tokens[...].astype(jnp.float32), gain[...]).astype(jnp.bfloat16)
     keys = jnp.dot(normed, key_weight[...], preferred_element_type=jnp.float32)
     values = jnp.dot(normed, value_weight[...], preferred_element_type=jnp.float32)
-    for head in range(out.shape[0]):
+    cosine, sine = both_halves(cosine[...], sine[...])
+    for head in range(KEY_VALUE_HEADS):
         cols = slice(head * HEAD_SIZE, (head + 1) * HEAD_SIZE)
-        rotated = normed_rotated(keys[:, cols], k_gain[...], cosine[...], sine[...])
-        out[head, :, :HEAD_SIZE] = rotated.astype(jnp.bfloat16)
-        out[head, :, HEAD_SIZE:] = values[:, cols].astype(jnp.bfloat16)
+        rotated = normed_rotated(keys[:, cols], k_gain[...], cosine, sine)
+        pair = jnp.concatenate([rotated, values[:, cols]], axis=1).astype(jnp.bfloat16)
+        for distance in range(peers):
+            asked = (place[1] ^ distance) * heads_dev // (QUERY_HEADS // KEY_VALUE_HEADS)
+
+            @pl.when(asked == head)
+            def _(out=outs[distance], pair=pair):
+                out[...] = pair
 
 
 def query_kernel(*refs):
@@ -116,9 +126,10 @@
         normed = rms_scale(piece[...].astype(jnp.float32), gain[...]).astype(jnp.bfloat16)
         queries = jnp.dot(normed, w_query[...], preferred_element_type=jnp.float32)
         here = pl.ds(at * rows, rows)
+        turn = both_halves(cosine[here, :], sine[here, :])
         for head in range(heads):
             cols = slice(head * HEAD_SIZE, (head + 1) * HEAD_SIZE)
-            rotated = normed_rotated(queries[:, cols], q_gain[...], cosine[here, :], sine[here, :])
+            rotated = normed_rotated(queries[:, cols], q_gain[...], *turn)
             out[at, pl.ds(head * rows, rows), :] = rotated.astype(jnp.bfloat16)
 
 
@@ -179,10 +190,6 @@
         ).astype(jnp.bfloat16)
 
 
-def add_kernel(total, partial, out):
-    out[...] = total[...].astype(jnp.float32) + partial[...].astype(jnp.float32)
-
-
 def residual_kernel(tokens, attention, partial, gain, residual, normed):
     summed = attention[...].astype(jnp.float32) + partial[...].astype(jnp.float32)
     rounded = (tokens[...].astype(jnp.float32) + summed).astype(jnp.bfloat16)
@@ -199,52 +206,47 @@
     return slot.astype(jnp.int32), weight * (1.0 / 1024.0)
 
 
-def dispatch_kernel(group, capacity, place, routing, same, other, *outs):
+def plane_targets(place, routing, count, distance, group):
     block, me = place[0], place[1]
+    return [
+        slot_targets(routing, block ^ (2 * group), (block ^ core) * count + (me ^ distance))
+        for core in (0, 1)
+    ]
+
+
+def dispatch_kernel(group, capacity, place, routing, source, *outs):
     count = len(outs)
-    rows = same.shape[0]
-    slots = lax.broadcasted_iota(jnp.int32, (capacity, rows), 0)
-    for at, source in enumerate((same, other)):
-        parts = []
-        for distance in range(count):
-            slot, _ = slot_targets(routing, block ^ (2 * group + at), block * count + (me ^ distance))
+    slots = lax.broadcasted_iota(jnp.int32, (capacity, source.shape[0]), 0)
+    parts = []
+    for distance in range(count):
+        for slot, _ in plane_targets(place, routing, count, distance, group):
             parts.append(jnp.where(slots == slot, 1.0, 0.0))
-        hot = jnp.concatenate(parts, axis=0).astype(jnp.bfloat16)
-        picked = jnp.dot(hot, source[...], preferred_element_type=jnp.float32)
-        picked = picked.astype(jnp.bfloat16)
-        for distance in range(count):
-            outs[distance][at * capacity : (at + 1) * capacity, :] = picked[
-                distance * capacity : (distance + 1) * capacity
-            ]
+    hot = jnp.concatenate(parts, axis=0).astype(jnp.bfloat16)
+    picked = jnp.dot(hot, source[...], preferred_element_type=jnp.float32).astype(jnp.bfloat16)
+    for distance, out in enumerate(outs):
+        out[...] = picked[2 * distance * capacity : 2 * (distance + 1) * capacity]
 
 
 def combine_kernel(group, capacity, place, routing, *refs):
-    *returned, same, other = refs
-    block, me = place[0], place[1]
+    *returned, out = refs
     count = len(returned)
-    rows = same.shape[0]
-    slots = lax.broadcasted_iota(jnp.int32, (capacity, rows), 0)
-    for at, out in enumerate((same, other)):
-        parts = []
-        for distance in range(count):
-            slot, weight = slot_targets(
-                routing, block ^ (2 * group + at), block * count + (me ^ distance)
-            )
+    slots = lax.broadcasted_iota(jnp.int32, (capacity, out.shape[0]), 0)
+    parts = []
+    for distance in range(count):
+        for slot, weight in plane_targets(place, routing, count, distance, group):
             parts.append(jnp.where(slots == slot, weight, 0.0))
-        shares = jnp.concatenate(parts, axis=0).astype(jnp.bfloat16)
-        produced = jnp.concatenate(
-            [ref[at * capacity : (at + 1) * capacity, :] for ref in returned], axis=0
-        )
-        out[...] = lax.dot_general(
-            shares, produced, (((0,), (0,)), ((), ())), preferred_element_type=jnp.float32
-        ).astype(jnp.bfloat16)
+    shares = jnp.concatenate(parts, axis=0).astype(jnp.bfloat16)
+    produced = jnp.concatenate([ref[...] for ref in returned], axis=0)
+    out[...] = lax.dot_general(
+        shares, produced, (((0,), (0,)), ((), ())), preferred_element_type=jnp.float32
+    ).astype(jnp.bfloat16)
 
 
 def expert_kernel(*refs):
-    count = (len(refs) - 4) // 2
-    came, (w_gate, w_up, w_down), made, hidden = refs[:count], refs[count : count + 3], refs[count + 3 : -1], refs[-1]
-    part = came[0].shape[0]
-    rows = jnp.concatenate([ref[...] for ref in came], axis=0)
+    *came, mate, w_gate, w_up, w_down, own, other, hidden = refs
+    capacity = came[0].shape[0] // 2
+    half = own.shape[0]
+    rows = jnp.concatenate([ref[:capacity, :] for ref in came] + [mate[...]], axis=0)
     for first in range(0, hidden.shape[1], 256):
         cols = slice(first, first + 256)
         gate = jnp.dot(rows, w_gate[:, cols], preferred_element_type=jnp.float32)
@@ -254,8 +256,16 @@
         cols = slice(first, first + 512)
         product = jnp.dot(hidden[...], w_down[:, cols], preferred_element_type=jnp.float32)
         product = product.astype(jnp.bfloat16)
-        for at, ref in enumerate(made):
-            ref[:, cols] = product[at * part : (at + 1) * part]
+        own[:, cols] = product[:half]
+        other[:, cols] = product[half:]
+
+
+def sum_kernel(*refs):
+    *parts, out = refs
+    total = parts[0][...].astype(jnp.float32)
+    for part in parts[1:]:
+        total = total + part[...].astype(jnp.float32)
+    out[...] = total.astype(out.dtype)
 
 
 def call(kernel, out_shape, specs, *args, name, scratch=(), limit=24, flops=1000):
@@ -299,11 +309,6 @@
     peers = list(range(exp_count))
     bf16 = functools.partial(jax.ShapeDtypeStruct, dtype=jnp.bfloat16)
 
-    pieces = {0: tokens}
-    for d in peers[1:]:
-        if d & (d - 1) == 0:
-            pieces[d] = swap(tokens, "exp", d)
-
     experts = ctx_count * exp_count
     capacity = max(2, 3 * rows * TOP // (2 * experts))
     capacity = -(-capacity // 16) * 16
@@ -321,27 +326,20 @@
         cosine,
         sine,
     ]
-    own_kv, table = call(
-        functools.partial(own_rows_kernel, experts),
-        [bf16((KEY_VALUE_HEADS, rows, 2 * HEAD_SIZE)), bf16((2 * TOP, 2 * rows))],
-        [ANY] * 9,
+    *own_kv, table = call(
+        functools.partial(own_rows_kernel, experts, heads_dev),
+        [bf16((rows, 2 * HEAD_SIZE)) for _ in peers] + [bf16((2 * TOP, 2 * rows))],
+        [SMEM] + [ANY] * 9,
+        place,
         *own_args,
         name="own_rows",
         scratch=[pltpu.VMEM(a.shape, a.dtype) for a in own_args] + [pltpu.SemaphoreType.DMA((18,))],
         limit=60,
     )
-
-    def head_kv(distance):
-        head = (me_exp ^ distance) * heads_dev // group_width
-        return lax.dynamic_index_in_dim(own_kv, head, 0, keepdims=False)
-
-    block_kv = [head_kv(0)] + [swap(head_kv(d), "exp", d) for d in peers[1:]]
-    for d in peers[1:]:
-        if d not in pieces:
-            pieces[d] = swap(tie(tokens, *block_kv[1:]), "exp", d)
-    both = jnp.concatenate(block_kv + [table], axis=0)
-    both = tie(both, *[pieces[d] for d in peers[1:] if d & (d - 1) == 0])
-    both = lax.all_gather(both, "ctx", axis=0, tiled=True)
+    block_kv = [own_kv[0]] + [swap(own_kv[d], "exp", d) for d in peers[1:]]
+    both = lax.all_gather(jnp.concatenate(block_kv + [table], axis=0), "ctx", axis=0, tiled=True)
+    sent = tie(tokens, *block_kv[1:])
+    pieces = [tokens] + [swap(sent, "exp", d) for d in peers[1:]]
     routing = both.reshape(ctx_count, ctx_rows + 2 * TOP, 2 * HEAD_SIZE)[:, ctx_rows:]
 
     positions = jnp.concatenate(
@@ -352,7 +350,7 @@
         query_kernel,
         bf16((exp_count, heads_dev * rows, HEAD_SIZE)),
         [VMEM] * (exp_count + 5),
-        *[pieces[d] for d in peers],
+        *pieces,
         ln1_row,
         w_query,
         q_gain.reshape(1, HEAD_SIZE),
@@ -381,7 +379,7 @@
     parts = [swap(partials[d], "exp", d) for d in order if d]
     for part in parts[:-1]:
         attention = call(
-            add_kernel,
+            sum_kernel,
             jax.ShapeDtypeStruct((rows, width), jnp.float32),
             [VMEM] * 2,
             attention,
@@ -405,64 +403,75 @@
     for g in range(1, groups):
         far.append(swap(tie(normed, *([far[g - 1]] if g > 2 else [])), "ctx", 2 * g))
     in_flight = {d: () for d in peers[1:]}
-    arrived, sent = [], ()
+
+    def send(array, d):
+        came = swap(tie(array, *in_flight[d]), "exp", d)
+        in_flight[d] = (came,)
+        return came
+
+    arrived = []
     for g in range(groups):
-        mate = swap(tie(far[g], *sent), "ctx", 1)
         outgoing = call(
             functools.partial(dispatch_kernel, g, capacity),
             [bf16((2 * capacity, width)) for _ in peers],
-            [SMEM, VMEM, VMEM, VMEM],
+            [SMEM, VMEM, VMEM],
             place,
             routing,
             far[g],
+            name="dispatch",
+        )
+        arrived.append([outgoing[0]] + [send(outgoing[d], d) for d in peers[1:]])
+
+    produced = []
+    half = exp_count * capacity
+    for came in arrived:
+        mate = swap(jnp.concatenate([rows_in[capacity:] for rows_in in came], axis=0), "ctx", 1)
+        own, other = call(
+            expert_kernel,
+            [bf16((half, width)), bf16((half, width))],
+            [VMEM] * (exp_count + 4),
+            *came,
             mate,
-            name="dispatch",
-        )
-        came = [outgoing[0]]
-        for d in peers[1:]:
-            came.append(swap(tie(outgoing[d], *in_flight[d]), "exp", d))
-            in_flight[d] = (came[d],)
-        sent = tuple(came[1:]) if g == 0 else ()
-        arrived.append(came)
-
-    turns = [g for g in range(2, groups)] + [g for g in (1, 0) if g < groups]
-    mixture = residual.astype(jnp.float32)
-    produced, sums, hop = {}, (), ()
-    for g in range(groups):
-        produced[g] = call(
-            expert_kernel,
-            [bf16((2 * capacity, width)) for _ in peers],
-            [VMEM] * (exp_count + 3),
-            *arrived[g],
             w_gate[0],
             w_up[0],
             w_down[0],
             name="expert",
-            scratch=[pltpu.VMEM((2 * capacity * exp_count, w_gate.shape[2]), jnp.bfloat16)],
-        )
-    for g in turns:
-        back = [tie(produced[g][0], *sums)]
-        for d in peers[1:]:
-            back.append(swap(tie(produced[g][d], *in_flight[d]), "exp", d))
-            in_flight[d] = (back[d],)
-        same, other = call(
+            scratch=[pltpu.VMEM((2 * half, w_gate.shape[2]), jnp.bfloat16)],
+        )
+        produced.append((own, swap(other, "ctx", 1)))
+
+    totals, hop = [], ()
+    for g in [*range(2, groups), *(g for g in (1, 0) if g < groups)]:
+        back = []
+        for d in peers:
+            mine = slice(d * capacity, (d + 1) * capacity)
+            back.append(jnp.concatenate([part[mine] for part in produced[g]], axis=0))
+        back = [back[0]] + [send(back[d], d) for d in peers[1:]]
+        total = call(
             functools.partial(combine_kernel, g, capacity),
-            [bf16((rows, width)), bf16((rows, width))],
+            bf16((rows, width)),
             [SMEM, VMEM] + [VMEM] * exp_count,
             place,
             routing,
             *back,
             name="combine",
         )
-        total = same.astype(jnp.float32) + swap(other, "ctx", 1).astype(jnp.float32)
         if g:
-            total = total.astype(jnp.bfloat16)
-            sums = (total,)
             total = swap(tie(total, *(hop if g > 1 else ())), "ctx", 2 * g)
             hop = (total,)
-            total = total.astype(jnp.float32)
-        mixture = mixture + total
-    return mixture.astype(jnp.bfloat16)
+        totals.append(total)
+    early = call(
+        sum_kernel,
+        jax.ShapeDtypeStruct((rows, width), jnp.float32),
+        [VMEM] * groups,
+        residual,
+        *totals[:-1],
+        name="add",
+        flops=10_000_000_000,
+    )
+    return call(
+        sum_kernel, bf16((rows, width)), [VMEM] * 2, early, totals[-1], name="add"
+    )
 
 
 def solution(mesh):

time: 310 us -> 271 us (0.87)
  waiting for transfers between devices: 182 us -> 153 us
  starting transfers between devices: 64.3 us -> 54.8 us
    ppermute x47, waiting for transfers between devices: 170 us -> 152 us  [swap(): return lax.ppermute(array, axis, pairs)]
    all_gather x1, waiting for transfers between devices: 12.2 us -> 1.71 us  [shards(): lax.all_gather(jnp.concatenate(block_kv + [table], axis=0), 'ctx', axis=0...]
    ppermute x47, starting transfers between devices: 64.3 us -> 54.8 us  [swap(): return lax.ppermute(array, axis, pairs)]
    pallas_call x21 -> x23, Pallas kernels: 36.9 us -> 39.1 us  [call(): pl.pallas_call(kernel, out_shape=out_shape, in_specs=specs, out_specs=jax...]
  transfers between devices with their start and end apart: 48 -> 48, of which waited for: 22 -> 25; matrix products, arithmetic and copies ran while one was open for 2% -> 1% of each run, Pallas kernels for 11% -> 11%
where the time goes in v5:
time: 271 us
  waiting for transfers between devices  153 us (56%)
  starting transfers between devices  54.8 us (20%)
  Pallas kernels  39.1 us (14%)
  between operations  14.1 us (5%)
  local copies, waits for them, and re-layouts  6.35 us (2%)
  other arithmetic  3.27 us (1%)
    ppermute x47, waiting for transfers between devices, swap(): return lax.ppermute(array, axis, pairs)  152 us
    ppermute x47, starting transfers between devices, swap(): return lax.ppermute(array, axis, pairs)  54.8 us
    pallas_call x23, Pallas kernels, call(): pl.pallas_call(kernel, out_shape=out_shape, in_specs=specs, out_specs=jax...  39.1 us
  transfers between devices with their start and end apart: 48, of which 25 were waited for; matrix products, arithmetic and copies ran while one was open for 1% of the time, Pallas kernels for 11%

profile of v5, /device:TPU:0, one launch (start us, length us, event | category | flops | bytes accessed | tf_op | source)
XLA Modules:
  0.0 271.0 jit_solution(5469984339943589627)
XLA Ops:
  8.1 4.5 %own_rows.1 = (bf16[128,256]{1,0:T(8,128)(2,1)}, bf16[128,256]{1,0:T(8,128)(2,1)}, bf16[128,256]{1,0:T(8,128)(2,1)}, bf16[128,256]{1,0:T(8,128)(2,1)}, bf16[16,256]{1,0:T(8,128)(2,1)}) custom-call(s32[6]{0:T(128)} %pad_add_fusion.place, s32[8,128]{1,0:T(8,128)} %bitcast.29, s32[8,128]{1,0:T(8,128)} %bitcast.30, bf16[128,2048]{1,0:T(8,128)(2,1)} %tokens.1, ...), custom_call_target="tpu_custom_call" | custom-call | flops 1000 | bytes 1000 | tf_op jit(solution)/shard_map/own_rows/pallas_call | solution.py:272
  12.6 3.0 %collective-permute-start = (bf16[128,256]{1,0:T(8,128)(2,1)}, bf16[128,256]{1,0:T(8,128)(2,1)S(1)}, u32[]{:S(2)}, u32[]{:S(2)}) collective-permute-start(bf16[128,256]{1,0:T(8,128)(2,1)} %get-tuple-element.63), channel_id=1, source_target_pairs={{0,1},{1,0},{2,3},{3,2},{4,5},{5,4},{6,7},{7,6},{8,9},{9,8},{10,11... | collective-permute-start | bytes 196616 | tf_op jit(solution)/shard_map/ppermute | solution.py:35
  18.3 1.8 collective-permute-done.1
  20.1 2.4 collective-permute-done.2
  24.8 2.7 collective-permute-start.5
  28.5 10.4 %collective-permute-done.3.refs_1_ = bf16[128,2048]{1,0:T(8,128)(2,1)S(1)} collective-permute-done((bf16[128,2048]{1,0:T(8,128)(2,1)S(1)}, bf16[128,2048]{1,0:T(8,128)(2,1)S(1)}, u32[]{:S(2)}, u32[]{:S(2)}) %collective-permute-start.3) | collective-permute-done | bytes 524320 | tf_op jit(solution)/shard_map/ppermute | solution.py:35
  38.9 9.0 %collective-permute-done.4.refs_2_ = bf16[128,2048]{1,0:T(8,128)(2,1)S(1)} collective-permute-done((bf16[128,2048]{1,0:T(8,128)(2,1)S(1)}, bf16[128,2048]{1,0:T(8,128)(2,1)S(1)}, u32[]{:S(2)}, u32[]{:S(2)}) %collective-permute-start.4) | collective-permute-done | bytes 524320 | tf_op jit(solution)/shard_map/ppermute | solution.py:35
  47.9 1.6 copy-done.7
  49.5 1.8 queries.1
  51.4 1.7 all-gather.2.cloned.1.call-done.both
  53.1 1.6 copy-done.3
  54.7 1.7 attention.4
  56.4 2.4 collective-permute-start.6
  58.9 1.7 attention.5
  61.2 1.7 attention.6
  63.6 1.9 attention.7.refs_0_
  65.5 6.8 %collective-permute-done.6.refs_1_ = bf16[128,2048]{1,0:T(8,128)(2,1)S(1)} collective-permute-done((bf16[128,2048]{1,0:T(8,128)(2,1)S(1)}, bf16[128,2048]{1,0:T(8,128)(2,1)S(1)}, u32[]{:S(2)}, u32[]{:S(2)}) %collective-permute-start.6) | collective-permute-done | bytes 524320 | tf_op jit(solution)/shard_map/ppermute | solution.py:35
  72.4 11.1 %collective-permute-done.7.refs_1_ = bf16[128,2048]{1,0:T(8,128)(2,1)S(1)} collective-permute-done((bf16[128,2048]{1,0:T(8,128)(2,1)S(1)}, bf16[128,2048]{1,0:T(8,128)(2,1)S(1)}, u32[]{:S(2)}, u32[]{:S(2)}) %collective-permute-start.7) | collective-permute-done | bytes 524320 | tf_op jit(solution)/shard_map/ppermute | solution.py:35
  85.1 2.2 collective-permute-start.17
  88.7 2.9 %collective-permute-start.10 = (bf16[128,2048]{1,0:T(8,128)(2,1)S(1)}, bf16[128,2048]{1,0:T(8,128)(2,1)S(1)}, u32[]{:S(2)}, u32[]{:S(2)}) collective-permute-start(bf16[128,2048]{1,0:T(8,128)(2,1)S(1)} %get-tuple-element.92.source), channel_id=1, source_target_pairs={{0,8},{4,12},{8,0},{12,4},{16,24},{20,28},{24,16},{28,20},{1,9},{5... | collective-permute-start | bytes 1572872 | tf_op jit(solution)/shard_map/ppermute | solution.py:35
  91.5 5.8 %collective-permute-start.9 = (bf16[128,2048]{1,0:T(8,128)(2,1)S(1)}, bf16[128,2048]{1,0:T(8,128)(2,1)S(1)}, u32[]{:S(2)}, u32[]{:S(2)}) collective-permute-start(bf16[128,2048]{1,0:T(8,128)(2,1)S(1)} %get-tuple-element.92.source), channel_id=1, source_target_pairs={{0,16},{4,20},{8,24},{12,28},{16,0},{20,4},{24,8},{28,12},{1,17},{... | collective-permute-start | bytes 1572872 | tf_op jit(solution)/shard_map/ppermute | solution.py:35
  98.1 7.5 %collective-permute-done.14.refs_2_ = bf16[96,2048]{1,0:T(8,128)(2,1)S(1)} collective-permute-done((bf16[96,2048]{1,0:T(8,128)(2,1)S(1)}, bf16[96,2048]{1,0:T(8,128)(2,1)S(1)}, u32[]{:S(2)}, u32[]{:S(2)}) %collective-permute-start.14) | collective-permute-done | bytes 393248 | tf_op jit(solution)/shard_map/ppermute | solution.py:35
  105.8 8.0 %collective-permute-done.10.source = bf16[128,2048]{1,0:T(8,128)(2,1)S(1)} collective-permute-done((bf16[128,2048]{1,0:T(8,128)(2,1)S(1)}, bf16[128,2048]{1,0:T(8,128)(2,1)S(1)}, u32[]{:S(2)}, u32[]{:S(2)}) %collective-permute-start.10) | collective-permute-done | bytes 524320 | tf_op jit(solution)/shard_map/ppermute | solution.py:35
  115.0 2.2 collective-permute-start.18
  118.5 1.6 collective-permute-done.9.source
  120.2 2.4 collective-permute-start.22
  122.6 5.5 %collective-permute-done.18.refs_3_ = bf16[96,2048]{1,0:T(8,128)(2,1)S(1)} collective-permute-done((bf16[96,2048]{1,0:T(8,128)(2,1)S(1)}, bf16[96,2048]{1,0:T(8,128)(2,1)S(1)}, u32[]{:S(2)}, u32[]{:S(2)}) %collective-permute-start.18) | collective-permute-done | bytes 393248 | tf_op jit(solution)/shard_map/ppermute | solution.py:35
  128.1 6.0 %collective-permute-done.15.refs_2_ = bf16[96,2048]{1,0:T(8,128)(2,1)S(1)} collective-permute-done((bf16[96,2048]{1,0:T(8,128)(2,1)S(1)}, bf16[96,2048]{1,0:T(8,128)(2,1)S(1)}, u32[]{:S(2)}, u32[]{:S(2)}) %collective-permute-start.15) | collective-permute-done | bytes 393248 | tf_op jit(solution)/shard_map/ppermute | solution.py:35
  135.4 1.6 collective-permute-start.13
  140.1 3.9 %expert.7 = (bf16[192,2048]{1,0:T(8,128)(2,1)S(1)}, bf16[192,2048]{1,0:T(8,128)(2,1)S(1)}) custom-call(bf16[96,2048]{1,0:T(8,128)(2,1)S(1)} %get-tuple-element.115.refs_0_, bf16[96,2048]{1,0:T(8,128)(2,1)S(1)} %collective-permute-done.11.refs_1_, bf16[96,2048]{1,0:T(8,128)(2,1)S(1)} %collective-permute-done.14.refs_2_, ...), custom_call_target="tpu_custom_call" | custom-call | flops 1000 | bytes 1000 | tf_op jit(solution)/shard_map/expert/pallas_call | solution.py:272
  144.1 12.1 %collective-permute-done.19.refs_3_ = bf16[96,2048]{1,0:T(8,128)(2,1)S(1)} collective-permute-done((bf16[96,2048]{1,0:T(8,128)(2,1)S(1)}, bf16[96,2048]{1,0:T(8,128)(2,1)S(1)}, u32[]{:S(2)}, u32[]{:S(2)}) %collective-permute-start.19) | collective-permute-done | bytes 393248 | tf_op jit(solution)/shard_map/ppermute | solution.py:35
  158.7 1.7 collective-permute-start.27
  160.4 3.8 %expert.6 = (bf16[192,2048]{1,0:T(8,128)(2,1)S(1)}, bf16[192,2048]{1,0:T(8,128)(2,1)S(1)}) custom-call(bf16[96,2048]{1,0:T(8,128)(2,1)S(1)} %get-tuple-element.109.refs_0_, bf16[96,2048]{1,0:T(8,128)(2,1)S(1)} %collective-permute-done.12.refs_1_, bf16[96,2048]{1,0:T(8,128)(2,1)S(1)} %collective-permute-done.15.refs_2_, ...), custom_call_target="tpu_custom_call" | custom-call | flops 1000 | bytes 1000 | tf_op jit(solution)/shard_map/expert/pallas_call | solution.py:272
  164.3 12.8 %collective-permute-done.27.refs_3_ = bf16[96,2048]{1,0:T(8,128)(2,1)S(1)} collective-permute-done((bf16[96,2048]{1,0:T(8,128)(2,1)S(1)}, bf16[96,2048]{1,0:T(8,128)(2,1)S(1)}, u32[]{:S(2)}, u32[]{:S(2)}) %collective-permute-start.27) | collective-permute-done | bytes 393248 | tf_op jit(solution)/shard_map/ppermute | solution.py:35
  177.9 4.1 %expert.4 = (bf16[192,2048]{1,0:T(8,128)(2,1)S(1)}, bf16[192,2048]{1,0:T(8,128)(2,1)S(1)}) custom-call(bf16[96,2048]{1,0:T(8,128)(2,1)S(1)} %get-tuple-element.74.refs_0_, bf16[96,2048]{1,0:T(8,128)(2,1)S(1)} %collective-permute-done.13.refs_1_, bf16[96,2048]{1,0:T(8,128)(2,1)S(1)} %collective-permute-done.16.refs_2_, ...), custom_call_target="tpu_custom_call" | custom-call | flops 1000 | bytes 1000 | tf_op jit(solution)/shard_map/expert/pallas_call | solution.py:272
  182.2 3.8 %expert.5 = (bf16[192,2048]{1,0:T(8,128)(2,1)S(1)}, bf16[192,2048]{1,0:T(8,128)(2,1)S(1)}) custom-call(bf16[96,2048]{1,0:T(8,128)(2,1)S(1)} %get-tuple-element.102.refs_0_, bf16[96,2048]{1,0:T(8,128)(2,1)S(1)} %collective-permute-done.23.refs_1_, bf16[96,2048]{1,0:T(8,128)(2,1)S(1)} %collective-permute-done.25.refs_2_, ...), custom_call_target="tpu_custom_call" | custom-call | flops 1000 | bytes 1000 | tf_op jit(solution)/shard_map/expert/pallas_call | solution.py:272
  189.0 1.7 collective-permute-start.28
  190.8 8.1 %collective-permute-done.24.refs_1_ = bf16[96,2048]{1,0:T(8,128)(2,1)S(1)} collective-permute-done((bf16[96,2048]{1,0:T(8,128)(2,1)S(1)}, bf16[96,2048]{1,0:T(8,128)(2,1)S(1)}, u32[]{:S(2)}, u32[]{:S(2)}) %collective-permute-start.24) | collective-permute-done | bytes 393248 | tf_op jit(solution)/shard_map/ppermute | solution.py:35
  200.0 8.0 %collective-permute-done.26.refs_2_ = bf16[96,2048]{1,0:T(8,128)(2,1)S(1)} collective-permute-done((bf16[96,2048]{1,0:T(8,128)(2,1)S(1)}, bf16[96,2048]{1,0:T(8,128)(2,1)S(1)}, u32[]{:S(2)}, u32[]{:S(2)}) %collective-permute-start.26) | collective-permute-done | bytes 393248 | tf_op jit(solution)/shard_map/ppermute | solution.py:35
  210.6 1.5 collective-permute-start.29
  212.1 3.7 %collective-permute-done.32.refs_1_ = bf16[96,2048]{1,0:T(8,128)(2,1)S(1)} collective-permute-done((bf16[96,2048]{1,0:T(8,128)(2,1)S(1)}, bf16[96,2048]{1,0:T(8,128)(2,1)S(1)}, u32[]{:S(2)}, u32[]{:S(2)}) %collective-permute-start.32) | collective-permute-done | bytes 393248 | tf_op jit(solution)/shard_map/ppermute | solution.py:35
  216.9 7.8 %collective-permute-done.33.refs_2_ = bf16[96,2048]{1,0:T(8,128)(2,1)S(1)} collective-permute-done((bf16[96,2048]{1,0:T(8,128)(2,1)S(1)}, bf16[96,2048]{1,0:T(8,128)(2,1)S(1)}, u32[]{:S(2)}, u32[]{:S(2)}) %collective-permute-start.33) | collective-permute-done | bytes 393248 | tf_op jit(solution)/shard_map/ppermute | solution.py:35
  227.4 7.8 %collective-permute-done.29.refs_1_ = bf16[128,2048]{1,0:T(8,128)(2,1)S(1)} collective-permute-done((bf16[128,2048]{1,0:T(8,128)(2,1)S(1)}, bf16[128,2048]{1,0:T(8,128)(2,1)S(1)}, u32[]{:S(2)}, u32[]{:S(2)}) %collective-permute-start.29) | collective-permute-done | bytes 524320 | tf_op jit(solution)/shard_map/ppermute | solution.py:35
  235.1 2.4 collective-permute-start.35
  237.5 3.9 %collective-permute-done.39.refs_2_ = bf16[96,2048]{1,0:T(8,128)(2,1)S(1)} collective-permute-done((bf16[96,2048]{1,0:T(8,128)(2,1)S(1)}, bf16[96,2048]{1,0:T(8,128)(2,1)S(1)}, u32[]{:S(2)}, u32[]{:S(2)}) %collective-permute-start.39) | collective-permute-done | bytes 393248 | tf_op jit(solution)/shard_map/ppermute | solution.py:35
  244.5 1.6 collective-permute-start.46
  246.1 8.5 %collective-permute-done.44.refs_1_ = bf16[96,2048]{1,0:T(8,128)(2,1)S(1)} collective-permute-done((bf16[96,2048]{1,0:T(8,128)(2,1)S(1)}, bf16[96,2048]{1,0:T(8,128)(2,1)S(1)}, u32[]{:S(2)}, u32[]{:S(2)}) %collective-permute-start.44) | collective-permute-done | bytes 393248 | tf_op jit(solution)/shard_map/ppermute | solution.py:35
  254.6 7.3 %collective-permute-done.45.refs_2_ = bf16[96,2048]{1,0:T(8,128)(2,1)S(1)} collective-permute-done((bf16[96,2048]{1,0:T(8,128)(2,1)S(1)}, bf16[96,2048]{1,0:T(8,128)(2,1)S(1)}, u32[]{:S(2)}, u32[]{:S(2)}) %collective-permute-start.45) | collective-permute-done | bytes 393248 | tf_op jit(solution)/shard_map/ppermute | solution.py:35
  (158 shorter events, 39.0 us)
Async XLA Ops:
  6.5 46.6 %all-gather.2.cloned.1.call-start = ((), (), s32[]{:S(2)}) async-start(), calls=%async_computation | async-start | bytes 2433024 | tf_op jit(solution)/shard_map/all_gather | solution.py:340
  12.6 5.7 %collective-permute-start = (bf16[128,256]{1,0:T(8,128)(2,1)}, bf16[128,256]{1,0:T(8,128)(2,1)S(1)}, u32[]{:S(2)}, u32[]{:S(2)}) collective-permute-start(bf16[128,256]{1,0:T(8,128)(2,1)} %get-tuple-element.63), channel_id=1, source_target_pairs={{0,1},{1,0},{2,3},{3,2},{4,5},{5,4},{6,7},{7,6},{8,9},{9,8},{10,11... | collective-permute-start | bytes 196616 | tf_op jit(solution)/shard_map/ppermute | solution.py:35
  15.6 4.5 %collective-permute-start.1 = (bf16[128,256]{1,0:T(8,128)(2,1)}, bf16[128,256]{1,0:T(8,128)(2,1)S(1)}, u32[]{:S(2)}, u32[]{:S(2)}) collective-permute-start(bf16[128,256]{1,0:T(8,128)(2,1)} %get-tuple-element.64), channel_id=1, source_target_pairs={{0,2},{1,3},{2,0},{3,1},{4,6},{5,7},{6,4},{7,5},{8,10},{9,11},{10,... | collective-permute-start | bytes 196616 | tf_op jit(solution)/shard_map/ppermute | solution.py:35
  17.1 5.4 %collective-permute-start.2 = (bf16[128,256]{1,0:T(8,128)(2,1)}, bf16[128,256]{1,0:T(8,128)(2,1)S(1)}, u32[]{:S(2)}, u32[]{:S(2)}) collective-permute-start(bf16[128,256]{1,0:T(8,128)(2,1)} %get-tuple-element.65), channel_id=1, source_target_pairs={{0,3},{1,2},{2,1},{3,0},{4,7},{5,6},{6,5},{7,4},{8,11},{9,10},{10,... | collective-permute-start | bytes 196616 | tf_op jit(solution)/shard_map/ppermute | solution.py:35
  24.0 14.9 %collective-permute-start.3 = (bf16[128,2048]{1,0:T(8,128)(2,1)S(1)}, bf16[128,2048]{1,0:T(8,128)(2,1)S(1)}, u32[]{:S(2)}, u32[]{:S(2)}) collective-permute-start(bf16[128,2048]{1,0:T(8,128)(2,1)S(1)} %copy-done.6), channel_id=1, source_target_pairs={{0,1},{1,0},{2,3},{3,2},{4,5},{5,4},{6,7},{7,6},{8,9},{9,8},{10,11... | collective-permute-start | bytes 1572872 | tf_op jit(solution)/shard_map/ppermute | solution.py:35
  24.6 23.3 %collective-permute-start.4 = (bf16[128,2048]{1,0:T(8,128)(2,1)S(1)}, bf16[128,2048]{1,0:T(8,128)(2,1)S(1)}, u32[]{:S(2)}, u32[]{:S(2)}) collective-permute-start(bf16[128,2048]{1,0:T(8,128)(2,1)S(1)} %copy-done.6), channel_id=1, source_target_pairs={{0,2},{1,3},{2,0},{3,1},{4,6},{5,7},{6,4},{7,5},{8,10},{9,11},{10,... | collective-permute-start | bytes 1572872 | tf_op jit(solution)/shard_map/ppermute | solution.py:35
  24.8 23.0 %collective-permute-start.5 = (bf16[128,2048]{1,0:T(8,128)(2,1)S(1)}, bf16[128,2048]{1,0:T(8,128)(2,1)S(1)}, u32[]{:S(2)}, u32[]{:S(2)}) collective-permute-start(bf16[128,2048]{1,0:T(8,128)(2,1)S(1)} %copy-done.6), channel_id=1, source_target_pairs={{0,3},{1,2},{2,1},{3,0},{4,7},{5,6},{6,5},{7,4},{8,11},{9,10},{10,... | collective-permute-start | bytes 1572872 | tf_op jit(solution)/shard_map/ppermute | solution.py:35
  56.4 15.9 %collective-permute-start.6 = (bf16[128,2048]{1,0:T(8,128)(2,1)S(1)}, bf16[128,2048]{1,0:T(8,128)(2,1)S(1)}, u32[]{:S(2)}, u32[]{:S(2)}) collective-permute-start(bf16[128,2048]{1,0:T(8,128)(2,1)S(1)} %attention.4), channel_id=1, source_target_pairs={{0,3},{1,2},{2,1},{3,0},{4,7},{5,6},{6,5},{7,4},{8,11},{9,10},{10,... | collective-permute-start | bytes 1572872 | tf_op jit(solution)/shard_map/ppermute | solution.py:35
  60.6 22.9 %collective-permute-start.7 = (bf16[128,2048]{1,0:T(8,128)(2,1)S(1)}, bf16[128,2048]{1,0:T(8,128)(2,1)S(1)}, u32[]{:S(2)}, u32[]{:S(2)}) collective-permute-start(bf16[128,2048]{1,0:T(8,128)(2,1)S(1)} %attention.5), channel_id=1, source_target_pairs={{0,1},{1,0},{2,3},{3,2},{4,5},{5,4},{6,7},{7,6},{8,9},{9,8},{10,11... | collective-permute-start | bytes 1572872 | tf_op jit(solution)/shard_map/ppermute | solution.py:35
  62.9 20.6 %collective-permute-start.8 = (bf16[128,2048]{1,0:T(8,128)(2,1)S(1)}, bf16[128,2048]{1,0:T(8,128)(2,1)S(1)}, u32[]{:S(2)}, u32[]{:S(2)}) collective-permute-start(bf16[128,2048]{1,0:T(8,128)(2,1)S(1)} %attention.6), channel_id=1, source_target_pairs={{0,2},{1,3},{2,0},{3,1},{4,6},{5,7},{6,4},{7,5},{8,10},{9,11},{10,... | collective-permute-start | bytes 1572872 | tf_op jit(solution)/shard_map/ppermute | solution.py:35
  85.1 13.0 %collective-permute-start.17 = (bf16[96,2048]{1,0:T(8,128)(2,1)S(1)}, bf16[96,2048]{1,0:T(8,128)(2,1)S(1)}, u32[]{:S(2)}, u32[]{:S(2)}) collective-permute-start(bf16[96,2048]{1,0:T(8,128)(2,1)S(1)} %get-tuple-element.87), channel_id=1, source_target_pairs={{0,3},{1,2},{2,1},{3,0},{4,7},{5,6},{6,5},{7,4},{8,11},{9,10},{10,... | collective-permute-start | bytes 1179656 | tf_op jit(solution)/shard_map/ppermute | solution.py:35
  87.3 18.3 %collective-permute-start.14 = (bf16[96,2048]{1,0:T(8,128)(2,1)S(1)}, bf16[96,2048]{1,0:T(8,128)(2,1)S(1)}, u32[]{:S(2)}, u32[]{:S(2)}) collective-permute-start(bf16[96,2048]{1,0:T(8,128)(2,1)S(1)} %get-tuple-element.82), channel_id=1, source_target_pairs={{0,2},{1,3},{2,0},{3,1},{4,6},{5,7},{6,4},{7,5},{8,10},{9,11},{10,... | collective-permute-start | bytes 1179656 | tf_op jit(solution)/shard_map/ppermute | solution.py:35
  88.1 17.5 %collective-permute-start.11 = (bf16[96,2048]{1,0:T(8,128)(2,1)S(1)}, bf16[96,2048]{1,0:T(8,128)(2,1)S(1)}, u32[]{:S(2)}, u32[]{:S(2)}) collective-permute-start(bf16[96,2048]{1,0:T(8,128)(2,1)S(1)} %get-tuple-element.77), channel_id=1, source_target_pairs={{0,1},{1,0},{2,3},{3,2},{4,5},{5,4},{6,7},{7,6},{8,9},{9,8},{10,11... | collective-permute-start | bytes 1179656 | tf_op jit(solution)/shard_map/ppermute | solution.py:35
  88.7 25.2 %collective-permute-start.10 = (bf16[128,2048]{1,0:T(8,128)(2,1)S(1)}, bf16[128,2048]{1,0:T(8,128)(2,1)S(1)}, u32[]{:S(2)}, u32[]{:S(2)}) collective-permute-start(bf16[128,2048]{1,0:T(8,128)(2,1)S(1)} %get-tuple-element.92.source), channel_id=1, source_target_pairs={{0,8},{4,12},{8,0},{12,4},{16,24},{20,28},{24,16},{28,20},{1,9},{5... | collective-permute-start | bytes 1572872 | tf_op jit(solution)/shard_map/ppermute | solution.py:35
  91.5 28.7 %collective-permute-start.9 = (bf16[128,2048]{1,0:T(8,128)(2,1)S(1)}, bf16[128,2048]{1,0:T(8,128)(2,1)S(1)}, u32[]{:S(2)}, u32[]{:S(2)}) collective-permute-start(bf16[128,2048]{1,0:T(8,128)(2,1)S(1)} %get-tuple-element.92.source), channel_id=1, source_target_pairs={{0,16},{4,20},{8,24},{12,28},{16,0},{20,4},{24,8},{28,12},{1,17},{... | collective-permute-start | bytes 1572872 | tf_op jit(solution)/shard_map/ppermute | solution.py:35
  105.8 34.3 %collective-permute-start.42 = (bf16[192,2048]{1,0:T(8,128)(2,1)S(1)}, bf16[192,2048]{1,0:T(8,128)(2,1)S(1)}, u32[]{:S(2)}, u32[]{:S(2)}) collective-permute-start(bf16[192,2048]{1,0:T(8,128)(2,1)S(1)} %pad_maximum_fusion.3), channel_id=1, source_target_pairs={{0,4},{4,0},{8,12},{12,8},{16,20},{20,16},{24,28},{28,24},{1,5},{5... | collective-permute-start | bytes 2359304 | tf_op jit(solution)/shard_map/ppermute | solution.py:35
  115.0 13.1 %collective-permute-start.18 = (bf16[96,2048]{1,0:T(8,128)(2,1)S(1)}, bf16[96,2048]{1,0:T(8,128)(2,1)S(1)}, u32[]{:S(2)}, u32[]{:S(2)}) collective-permute-start(bf16[96,2048]{1,0:T(8,128)(2,1)S(1)} %get-tuple-element.88), channel_id=1, source_target_pairs={{0,3},{1,2},{2,1},{3,0},{4,7},{5,6},{6,5},{7,4},{8,11},{9,10},{10,... | collective-permute-start | bytes 1179656 | tf_op jit(solution)/shard_map/ppermute | solution.py:35
  117.2 16.8 %collective-permute-start.15 = (bf16[96,2048]{1,0:T(8,128)(2,1)S(1)}, bf16[96,2048]{1,0:T(8,128)(2,1)S(1)}, u32[]{:S(2)}, u32[]{:S(2)}) collective-permute-start(bf16[96,2048]{1,0:T(8,128)(2,1)S(1)} %get-tuple-element.83), channel_id=1, source_target_pairs={{0,2},{1,3},{2,0},{3,1},{4,6},{5,7},{6,4},{7,5},{8,10},{9,11},{10,... | collective-permute-start | bytes 1179656 | tf_op jit(solution)/shard_map/ppermute | solution.py:35
  118.0 16.1 %collective-permute-start.12 = (bf16[96,2048]{1,0:T(8,128)(2,1)S(1)}, bf16[96,2048]{1,0:T(8,128)(2,1)S(1)}, u32[]{:S(2)}, u32[]{:S(2)}) collective-permute-start(bf16[96,2048]{1,0:T(8,128)(2,1)S(1)} %get-tuple-element.78), channel_id=1, source_target_pairs={{0,1},{1,0},{2,3},{3,2},{4,5},{5,4},{6,7},{7,6},{8,9},{9,8},{10,11... | collective-permute-start | bytes 1179656 | tf_op jit(solution)/shard_map/ppermute | solution.py:35
  120.2 17.6 %collective-permute-start.22 = (bf16[128,2048]{1,0:T(8,128)(2,1)S(1)}, bf16[128,2048]{1,0:T(8,128)(2,1)S(1)}, u32[]{:S(2)}, u32[]{:S(2)}) collective-permute-start(bf16[128,2048]{1,0:T(8,128)(2,1)S(1)} %get-tuple-element.92.source), channel_id=1, source_target_pairs={{0,24},{4,28},{8,16},{12,20},{16,8},{20,12},{24,0},{28,4},{1,25},{... | collective-permute-start | bytes 1572872 | tf_op jit(solution)/shard_map/ppermute | solution.py:35
  134.2 24.5 %collective-permute-start.36 = (bf16[192,2048]{1,0:T(8,128)(2,1)S(1)}, bf16[192,2048]{1,0:T(8,128)(2,1)S(1)}, u32[]{:S(2)}, u32[]{:S(2)}) collective-permute-start(bf16[192,2048]{1,0:T(8,128)(2,1)S(1)} %pad_maximum_fusion.2), channel_id=1, source_target_pairs={{0,4},{4,0},{8,12},{12,8},{16,20},{20,16},{24,28},{28,24},{1,5},{5... | collective-permute-start | bytes 2359304 | tf_op jit(solution)/shard_map/ppermute | solution.py:35
  135.4 21.2 %collective-permute-start.13 = (bf16[96,2048]{1,0:T(8,128)(2,1)S(1)}, bf16[96,2048]{1,0:T(8,128)(2,1)S(1)}, u32[]{:S(2)}, u32[]{:S(2)}) collective-permute-start(bf16[96,2048]{1,0:T(8,128)(2,1)S(1)} %get-tuple-element.79), channel_id=1, source_target_pairs={{0,1},{1,0},{2,3},{3,2},{4,5},{5,4},{6,7},{7,6},{8,9},{9,8},{10,11... | collective-permute-start | bytes 1179656 | tf_op jit(solution)/shard_map/ppermute | solution.py:35
  136.9 19.7 %collective-permute-start.16 = (bf16[96,2048]{1,0:T(8,128)(2,1)S(1)}, bf16[96,2048]{1,0:T(8,128)(2,1)S(1)}, u32[]{:S(2)}, u32[]{:S(2)}) collective-permute-start(bf16[96,2048]{1,0:T(8,128)(2,1)S(1)} %get-tuple-element.84), channel_id=1, source_target_pairs={{0,2},{1,3},{2,0},{3,1},{4,6},{5,7},{6,4},{7,5},{8,10},{9,11},{10,... | collective-permute-start | bytes 1179656 | tf_op jit(solution)/shard_map/ppermute | solution.py:35
  137.8 18.4 %collective-permute-start.19 = (bf16[96,2048]{1,0:T(8,128)(2,1)S(1)}, bf16[96,2048]{1,0:T(8,128)(2,1)S(1)}, u32[]{:S(2)}, u32[]{:S(2)}) collective-permute-start(bf16[96,2048]{1,0:T(8,128)(2,1)S(1)} %get-tuple-element.89), channel_id=1, source_target_pairs={{0,3},{1,2},{2,1},{3,0},{4,7},{5,6},{6,5},{7,4},{8,11},{9,10},{10,... | collective-permute-start | bytes 1179656 | tf_op jit(solution)/shard_map/ppermute | solution.py:35
  143.9 33.8 %collective-permute-start.43 = (bf16[192,2048]{1,0:T(8,128)(2,1)S(1)}, bf16[192,2048]{1,0:T(8,128)(2,1)S(1)}, u32[]{:S(2)}, u32[]{:S(2)}) collective-permute-start(bf16[192,2048]{1,0:T(8,128)(2,1)S(1)} %get-tuple-element.117), channel_id=1, source_target_pairs={{0,4},{4,0},{8,12},{12,8},{16,20},{20,16},{24,28},{28,24},{1,5},{5... | collective-permute-start | bytes 2359304 | tf_op jit(solution)/shard_map/ppermute | solution.py:35
  156.7 21.2 %collective-permute-start.20 = (bf16[192,2048]{1,0:T(8,128)(2,1)S(1)}, bf16[192,2048]{1,0:T(8,128)(2,1)S(1)}, u32[]{:S(2)}, u32[]{:S(2)}) collective-permute-start(bf16[192,2048]{1,0:T(8,128)(2,1)S(1)} %pad_maximum_fusion), channel_id=1, source_target_pairs={{0,4},{4,0},{8,12},{12,8},{16,20},{20,16},{24,28},{28,24},{1,5},{5... | collective-permute-start | bytes 2359304 | tf_op jit(solution)/shard_map/ppermute | solution.py:35
  156.8 20.3 %collective-permute-start.23 = (bf16[96,2048]{1,0:T(8,128)(2,1)S(1)}, bf16[96,2048]{1,0:T(8,128)(2,1)S(1)}, u32[]{:S(2)}, u32[]{:S(2)}) collective-permute-start(bf16[96,2048]{1,0:T(8,128)(2,1)S(1)} %get-tuple-element.94), channel_id=1, source_target_pairs={{0,1},{1,0},{2,3},{3,2},{4,5},{5,4},{6,7},{7,6},{8,9},{9,8},{10,11... | collective-permute-start | bytes 1179656 | tf_op jit(solution)/shard_map/ppermute | solution.py:35
  157.4 19.6 %collective-permute-start.25 = (bf16[96,2048]{1,0:T(8,128)(2,1)S(1)}, bf16[96,2048]{1,0:T(8,128)(2,1)S(1)}, u32[]{:S(2)}, u32[]{:S(2)}) collective-permute-start(bf16[96,2048]{1,0:T(8,128)(2,1)S(1)} %get-tuple-element.97), channel_id=1, source_target_pairs={{0,2},{1,3},{2,0},{3,1},{4,6},{5,7},{6,4},{7,5},{8,10},{9,11},{10,... | collective-permute-start | bytes 1179656 | tf_op jit(solution)/shard_map/ppermute | solution.py:35
  158.7 18.4 %collective-permute-start.27 = (bf16[96,2048]{1,0:T(8,128)(2,1)S(1)}, bf16[96,2048]{1,0:T(8,128)(2,1)S(1)}, u32[]{:S(2)}, u32[]{:S(2)}) collective-permute-start(bf16[96,2048]{1,0:T(8,128)(2,1)S(1)} %get-tuple-element.100), channel_id=1, source_target_pairs={{0,3},{1,2},{2,1},{3,0},{4,7},{5,6},{6,5},{7,4},{8,11},{9,10},{10,... | collective-permute-start | bytes 1179656 | tf_op jit(solution)/shard_map/ppermute | solution.py:35
  177.0 9.6 %collective-permute-start.37 = (bf16[192,2048]{1,0:T(8,128)(2,1)S(1)}, bf16[192,2048]{1,0:T(8,128)(2,1)S(1)}, u32[]{:S(2)}, u32[]{:S(2)}) collective-permute-start(bf16[192,2048]{1,0:T(8,128)(2,1)S(1)} %get-tuple-element.111), channel_id=1, source_target_pairs={{0,4},{4,0},{8,12},{12,8},{16,20},{20,16},{24,28},{28,24},{1,5},{5... | collective-permute-start | bytes 2359304 | tf_op jit(solution)/shard_map/ppermute | solution.py:35
  177.2 5.0 %collective-permute-start.30 = (bf16[192,2048]{1,0:T(8,128)(2,1)S(1)}, bf16[192,2048]{1,0:T(8,128)(2,1)S(1)}, u32[]{:S(2)}, u32[]{:S(2)}) collective-permute-start(bf16[192,2048]{1,0:T(8,128)(2,1)S(1)} %pad_maximum_fusion.1), channel_id=1, source_target_pairs={{0,4},{4,0},{8,12},{12,8},{16,20},{20,16},{24,28},{28,24},{1,5},{5... | collective-permute-start | bytes 2359304 | tf_op jit(solution)/shard_map/ppermute | solution.py:35
  182.0 4.8 %collective-permute-start.21 = (bf16[192,2048]{1,0:T(8,128)(2,1)S(1)}, bf16[192,2048]{1,0:T(8,128)(2,1)S(1)}, u32[]{:S(2)}, u32[]{:S(2)}) collective-permute-start(bf16[192,2048]{1,0:T(8,128)(2,1)S(1)} %get-tuple-element.91), channel_id=1, source_target_pairs={{0,4},{4,0},{8,12},{12,8},{16,20},{20,16},{24,28},{28,24},{1,5},{5... | collective-permute-start | bytes 2359304 | tf_op jit(solution)/shard_map/ppermute | solution.py:35
  186.0 4.7 %collective-permute-start.31 = (bf16[192,2048]{1,0:T(8,128)(2,1)S(1)}, bf16[192,2048]{1,0:T(8,128)(2,1)S(1)}, u32[]{:S(2)}, u32[]{:S(2)}) collective-permute-start(bf16[192,2048]{1,0:T(8,128)(2,1)S(1)} %get-tuple-element.104), channel_id=1, source_target_pairs={{0,4},{4,0},{8,12},{12,8},{16,20},{20,16},{24,28},{28,24},{1,5},{5... | collective-permute-start | bytes 2359304 | tf_op jit(solution)/shard_map/ppermute | solution.py:35
  186.9 12.0 %collective-permute-start.24 = (bf16[96,2048]{1,0:T(8,128)(2,1)S(1)}, bf16[96,2048]{1,0:T(8,128)(2,1)S(1)}, u32[]{:S(2)}, u32[]{:S(2)}) collective-permute-start(bf16[96,2048]{1,0:T(8,128)(2,1)S(1)} %pad_maximum_fusion.5), channel_id=1, source_target_pairs={{0,1},{1,0},{2,3},{3,2},{4,5},{5,4},{6,7},{7,6},{8,9},{9,8},{10,11... | collective-permute-start | bytes 1179656 | tf_op jit(solution)/shard_map/ppermute | solution.py:35
  188.1 19.9 %collective-permute-start.26 = (bf16[96,2048]{1,0:T(8,128)(2,1)S(1)}, bf16[96,2048]{1,0:T(8,128)(2,1)S(1)}, u32[]{:S(2)}, u32[]{:S(2)}) collective-permute-start(bf16[96,2048]{1,0:T(8,128)(2,1)S(1)} %pad_maximum_fusion.6), channel_id=1, source_target_pairs={{0,2},{1,3},{2,0},{3,1},{4,6},{5,7},{6,4},{7,5},{8,10},{9,11},{10,... | collective-permute-start | bytes 1179656 | tf_op jit(solution)/shard_map/ppermute | solution.py:35
  189.0 20.0 %collective-permute-start.28 = (bf16[96,2048]{1,0:T(8,128)(2,1)S(1)}, bf16[96,2048]{1,0:T(8,128)(2,1)S(1)}, u32[]{:S(2)}, u32[]{:S(2)}) collective-permute-start(bf16[96,2048]{1,0:T(8,128)(2,1)S(1)} %pad_maximum_fusion.7), channel_id=1, source_target_pairs={{0,3},{1,2},{2,1},{3,0},{4,7},{5,6},{6,5},{7,4},{8,11},{9,10},{10,... | collective-permute-start | bytes 1179656 | tf_op jit(solution)/shard_map/ppermute | solution.py:35
  199.0 16.9 %collective-permute-start.32 = (bf16[96,2048]{1,0:T(8,128)(2,1)S(1)}, bf16[96,2048]{1,0:T(8,128)(2,1)S(1)}, u32[]{:S(2)}, u32[]{:S(2)}) collective-permute-start(bf16[96,2048]{1,0:T(8,128)(2,1)S(1)} %pad_maximum_fusion.9), channel_id=1, source_target_pairs={{0,1},{1,0},{2,3},{3,2},{4,5},{5,4},{6,7},{7,6},{8,9},{9,8},{10,11... | collective-permute-start | bytes 1179656 | tf_op jit(solution)/shard_map/ppermute | solution.py:35
  208.0 16.7 %collective-permute-start.33 = (bf16[96,2048]{1,0:T(8,128)(2,1)S(1)}, bf16[96,2048]{1,0:T(8,128)(2,1)S(1)}, u32[]{:S(2)}, u32[]{:S(2)}) collective-permute-start(bf16[96,2048]{1,0:T(8,128)(2,1)S(1)} %pad_maximum_fusion.10), channel_id=1, source_target_pairs={{0,2},{1,3},{2,0},{3,1},{4,6},{5,7},{6,4},{7,5},{8,10},{9,11},{10,... | collective-permute-start | bytes 1179656 | tf_op jit(solution)/shard_map/ppermute | solution.py:35
  209.0 16.8 %collective-permute-start.34 = (bf16[96,2048]{1,0:T(8,128)(2,1)S(1)}, bf16[96,2048]{1,0:T(8,128)(2,1)S(1)}, u32[]{:S(2)}, u32[]{:S(2)}) collective-permute-start(bf16[96,2048]{1,0:T(8,128)(2,1)S(1)} %pad_maximum_fusion.11), channel_id=1, source_target_pairs={{0,3},{1,2},{2,1},{3,0},{4,7},{5,6},{6,5},{7,4},{8,11},{9,10},{10,... | collective-permute-start | bytes 1179656 | tf_op jit(solution)/shard_map/ppermute | solution.py:35
  210.6 24.6 %collective-permute-start.29 = (bf16[128,2048]{1,0:T(8,128)(2,1)S(1)}, bf16[128,2048]{1,0:T(8,128)(2,1)S(1)}, u32[]{:S(2)}, u32[]{:S(2)}) collective-permute-start(bf16[128,2048]{1,0:T(8,128)(2,1)S(1)} %combine.4), channel_id=1, source_target_pairs={{0,16},{4,20},{8,24},{12,28},{16,0},{20,4},{24,8},{28,12},{1,17},{... | collective-permute-start | bytes 1572872 | tf_op jit(solution)/shard_map/ppermute | solution.py:35
  215.9 21.7 %collective-permute-start.38 = (bf16[96,2048]{1,0:T(8,128)(2,1)S(1)}, bf16[96,2048]{1,0:T(8,128)(2,1)S(1)}, u32[]{:S(2)}, u32[]{:S(2)}) collective-permute-start(bf16[96,2048]{1,0:T(8,128)(2,1)S(1)} %pad_maximum_fusion.13), channel_id=1, source_target_pairs={{0,1},{1,0},{2,3},{3,2},{4,5},{5,4},{6,7},{7,6},{8,9},{9,8},{10,11... | collective-permute-start | bytes 1179656 | tf_op jit(solution)/shard_map/ppermute | solution.py:35
  224.7 16.7 %collective-permute-start.39 = (bf16[96,2048]{1,0:T(8,128)(2,1)S(1)}, bf16[96,2048]{1,0:T(8,128)(2,1)S(1)}, u32[]{:S(2)}, u32[]{:S(2)}) collective-permute-start(bf16[96,2048]{1,0:T(8,128)(2,1)S(1)} %pad_maximum_fusion.14), channel_id=1, source_target_pairs={{0,2},{1,3},{2,0},{3,1},{4,6},{5,7},{6,4},{7,5},{8,10},{9,11},{10,... | collective-permute-start | bytes 1179656 | tf_op jit(solution)/shard_map/ppermute | solution.py:35
  225.8 15.6 %collective-permute-start.40 = (bf16[96,2048]{1,0:T(8,128)(2,1)S(1)}, bf16[96,2048]{1,0:T(8,128)(2,1)S(1)}, u32[]{:S(2)}, u32[]{:S(2)}) collective-permute-start(bf16[96,2048]{1,0:T(8,128)(2,1)S(1)} %pad_maximum_fusion.15), channel_id=1, source_target_pairs={{0,3},{1,2},{2,1},{3,0},{4,7},{5,6},{6,5},{7,4},{8,11},{9,10},{10,... | collective-permute-start | bytes 1179656 | tf_op jit(solution)/shard_map/ppermute | solution.py:35
  235.1 27.9 %collective-permute-start.35 = (bf16[128,2048]{1,0:T(8,128)(2,1)S(1)}, bf16[128,2048]{1,0:T(8,128)(2,1)S(1)}, u32[]{:S(2)}, u32[]{:S(2)}) collective-permute-start(bf16[128,2048]{1,0:T(8,128)(2,1)S(1)} %combine.5), channel_id=1, source_target_pairs={{0,24},{4,28},{8,16},{12,20},{16,8},{20,12},{24,0},{28,4},{1,25},{... | collective-permute-start | bytes 1572872 | tf_op jit(solution)/shard_map/ppermute | solution.py:35
  242.4 20.6 %collective-permute-start.41 = (bf16[128,2048]{1,0:T(8,128)(2,1)S(1)}, bf16[128,2048]{1,0:T(8,128)(2,1)S(1)}, u32[]{:S(2)}, u32[]{:S(2)}) collective-permute-start(bf16[128,2048]{1,0:T(8,128)(2,1)S(1)} %combine.6), channel_id=1, source_target_pairs={{0,8},{4,12},{8,0},{12,4},{16,24},{20,28},{24,16},{28,20},{1,9},{5... | collective-permute-start | bytes 1572872 | tf_op jit(solution)/shard_map/ppermute | solution.py:35
  242.5 12.1 %collective-permute-start.44 = (bf16[96,2048]{1,0:T(8,128)(2,1)S(1)}, bf16[96,2048]{1,0:T(8,128)(2,1)S(1)}, u32[]{:S(2)}, u32[]{:S(2)}) collective-permute-start(bf16[96,2048]{1,0:T(8,128)(2,1)S(1)} %pad_maximum_fusion.17), channel_id=1, source_target_pairs={{0,1},{1,0},{2,3},{3,2},{4,5},{5,4},{6,7},{7,6},{8,9},{9,8},{10,11... | collective-permute-start | bytes 1179656 | tf_op jit(solution)/shard_map/ppermute | solution.py:35
  243.5 18.5 %collective-permute-start.45 = (bf16[96,2048]{1,0:T(8,128)(2,1)S(1)}, bf16[96,2048]{1,0:T(8,128)(2,1)S(1)}, u32[]{:S(2)}, u32[]{:S(2)}) collective-permute-start(bf16[96,2048]{1,0:T(8,128)(2,1)S(1)} %pad_maximum_fusion.18), channel_id=1, source_target_pairs={{0,2},{1,3},{2,0},{3,1},{4,6},{5,7},{6,4},{7,5},{8,10},{9,11},{10,... | collective-permute-start | bytes 1179656 | tf_op jit(solution)/shard_map/ppermute | solution.py:35
  244.5 17.5 %collective-permute-start.46 = (bf16[96,2048]{1,0:T(8,128)(2,1)S(1)}, bf16[96,2048]{1,0:T(8,128)(2,1)S(1)}, u32[]{:S(2)}, u32[]{:S(2)}) collective-permute-start(bf16[96,2048]{1,0:T(8,128)(2,1)S(1)} %pad_maximum_fusion.19), channel_id=1, source_target_pairs={{0,3},{1,2},{2,1},{3,0},{4,7},{5,6},{6,5},{7,4},{8,11},{9,10},{10,... | collective-permute-start | bytes 1179656 | tf_op jit(solution)/shard_map/ppermute | solution.py:35
  (13 other events, 216.8 us)
Sparse Core Ops, SparseCore 0:
  24.1 29.0 all-gather.1

commit v6 on v5

--- a/solution.py
+++ b/solution.py
@@ -197,8 +197,8 @@
     normed[...] = rms_scale(rounded.astype(jnp.float32), gain[...]).astype(jnp.bfloat16)
 
 
-def slot_targets(routing, block, expert):
-    table = routing[block].astype(jnp.float32)
+def slot_targets(table, expert):
+    table = table.astype(jnp.float32)
     rows = table.shape[1] // 2
     named = table[:TOP, :rows] == expert.astype(jnp.float32)
     slot = jnp.max(jnp.where(named, table[:TOP, rows:], -1.0), axis=0, keepdims=True)
@@ -206,58 +206,123 @@
     return slot.astype(jnp.int32), weight * (1.0 / 1024.0)
 
 
-def plane_targets(place, routing, count, distance, group):
-    block, me = place[0], place[1]
-    return [
-        slot_targets(routing, block ^ (2 * group), (block ^ core) * count + (me ^ distance))
-        for core in (0, 1)
-    ]
-
-
-def dispatch_kernel(group, capacity, place, routing, source, *outs):
-    count = len(outs)
-    slots = lax.broadcasted_iota(jnp.int32, (capacity, source.shape[0]), 0)
-    parts = []
-    for distance in range(count):
-        for slot, _ in plane_targets(place, routing, count, distance, group):
-            parts.append(jnp.where(slots == slot, 1.0, 0.0))
-    hot = jnp.concatenate(parts, axis=0).astype(jnp.bfloat16)
-    picked = jnp.dot(hot, source[...], preferred_element_type=jnp.float32).astype(jnp.bfloat16)
-    for distance, out in enumerate(outs):
-        out[...] = picked[2 * distance * capacity : 2 * (distance + 1) * capacity]
-
-
-def combine_kernel(group, capacity, place, routing, *refs):
-    *returned, out = refs
-    count = len(returned)
-    slots = lax.broadcasted_iota(jnp.int32, (capacity, out.shape[0]), 0)
-    parts = []
-    for distance in range(count):
-        for slot, weight in plane_targets(place, routing, count, distance, group):
-            parts.append(jnp.where(slots == slot, weight, 0.0))
-    shares = jnp.concatenate(parts, axis=0).astype(jnp.bfloat16)
-    produced = jnp.concatenate([ref[...] for ref in returned], axis=0)
-    out[...] = lax.dot_general(
-        shares, produced, (((0,), (0,)), ((), ())), preferred_element_type=jnp.float32
-    ).astype(jnp.bfloat16)
-
-
-def expert_kernel(*refs):
-    *came, mate, w_gate, w_up, w_down, own, other, hidden = refs
-    capacity = came[0].shape[0] // 2
-    half = own.shape[0]
-    rows = jnp.concatenate([ref[:capacity, :] for ref in came] + [mate[...]], axis=0)
+def plane_targets(group, place, routing, near, away):
+    block, me, count = place[0], place[1], routing.shape[0]
+    table = routing[near, block ^ (2 * group)]
+    return [slot_targets(table, (block ^ core) * count + (me ^ away)) for core in (0, 1)]
+
+
+def route_order(route):
+    near, away = route
+    return [n ^ a for a in away for n in near]
+
+
+def dispatch_kernel(routes, group, capacity, place, routing, *refs):
+    sources = refs[: sum(len(near) for near, _ in routes)]
+    outs = refs[len(sources) :]
+    rows = sources[0].shape[0]
+    slots = lax.broadcasted_iota(jnp.int32, (capacity, rows), 0)
+    for near, away in routes:
+        some, sources = sources[: len(near)], sources[len(near) :]
+        mine, outs = outs[: len(away)], outs[len(away) :]
+        for at, (n, source) in enumerate(zip(near, some)):
+            parts = []
+            for a in away:
+                for slot, _ in plane_targets(group, place, routing, n, a):
+                    parts.append(jnp.where(slots == slot, 1.0, 0.0))
+            hot = jnp.concatenate(parts, axis=0).astype(jnp.bfloat16)
+            picked = jnp.dot(hot, source[...], preferred_element_type=jnp.float32)
+            picked = picked.astype(jnp.bfloat16)
+            for part in range(2 * len(away)):
+                first = ((part % 2) * len(near) + at) * capacity
+                mine[part // 2][first : first + capacity, :] = picked[
+                    part * capacity : (part + 1) * capacity
+                ]
+
+
+def combine_kernel(routes, group, capacity, place, routing, *refs):
+    arrived = refs[: sum(len(away) + 1 for _, away in routes)]
+    kept, *outs = refs[len(arrived) :]
+    rows, width = kept.shape[0], arrived[0].shape[1]
+    slots = lax.broadcasted_iota(jnp.int32, (capacity, rows), 0)
+    for side, (near, away) in enumerate(routes):
+        some, arrived = arrived[: len(away) + 1], arrived[len(away) + 1 :]
+        for at, n in enumerate(near):
+            shares, produced = [], []
+            for index, a in enumerate(away):
+                for core, (slot, weight) in enumerate(plane_targets(group, place, routing, n, a)):
+                    shares.append(jnp.where(slots == slot, weight, 0.0))
+                    piece = some[index + 1] if index else some[core]
+                    first = ((core if index else 0) * len(near) + at) * capacity
+                    produced.append(piece[first : first + capacity, :])
+            total = lax.dot_general(
+                jnp.concatenate(shares, axis=0).astype(jnp.bfloat16),
+                jnp.concatenate(produced, axis=0),
+                (((0,), (0,)), ((), ())),
+                preferred_element_type=jnp.float32,
+            )
+            if n:
+                outs[0][...] = total.astype(jnp.bfloat16)
+                outs = outs[1:]
+            else:
+                kept[:, side * width : (side + 1) * width] = total
+
+
+def gather_kernel(kept, *refs):
+    *parts, out = refs
+    width = parts[0].shape[1]
+    count = out.shape[1] // width
+    first = 0
+    for side, some in enumerate(split_parts(parts, count)):
+        cols = slice(first, first + width)
+        total = kept[:, cols]
+        for part in some:
+            total = total + part[...].astype(jnp.float32)
+        out[:, cols] = total.astype(out.dtype)
+        first += width
+
+
+def split_parts(parts, count):
+    assert count == 2
+    return parts[:1], parts[1:]
+
+
+def expert_kernel(routes, capacity, *refs):
+    count = sum(len(away) for _, away in routes)
+    came, (mate, w_gate, w_up, w_down) = refs[:count], refs[count : count + 4]
+    own, other = refs[count + 4 : 2 * count + 4], refs[2 * count + 4 : 3 * count + 4]
+    rows_in, hidden = refs[3 * count + 4 :]
+    width = came[0].shape[1]
+    half = rows_in.shape[1] // 2
+    places = []
+    for side, (near, away) in enumerate(routes):
+        base = sum(len(some) for _, some in routes[:side])
+        for at, d in enumerate(route_order((near, away))):
+            places.append((side, base + at // len(near), (at % len(near)) * capacity, d * capacity))
+    for at, (side, piece, first, to) in enumerate(places):
+        rows_in[side, to : to + capacity, :] = came[piece][first : first + capacity, :]
+        to = half + to
+        rows_in[side, to : to + capacity, :] = mate[at * capacity : (at + 1) * capacity, :]
     for first in range(0, hidden.shape[1], 256):
         cols = slice(first, first + 256)
-        gate = jnp.dot(rows, w_gate[:, cols], preferred_element_type=jnp.float32)
-        up = jnp.dot(rows, w_up[:, cols], preferred_element_type=jnp.float32)
+        gate = up = 0.0
+        for side in range(len(routes)):
+            depth = slice(side * width, (side + 1) * width)
+            rows = rows_in[side]
+            gate = gate + jnp.dot(rows, w_gate[depth, cols], preferred_element_type=jnp.float32)
+            up = up + jnp.dot(rows, w_up[depth, cols], preferred_element_type=jnp.float32)
         hidden[:, cols] = (gate / (1.0 + jnp.exp(-gate)) * up).astype(jnp.bfloat16)
-    for first in range(0, w_down.shape[1], 512):
-        cols = slice(first, first + 512)
-        product = jnp.dot(hidden[...], w_down[:, cols], preferred_element_type=jnp.float32)
-        product = product.astype(jnp.bfloat16)
-        own[:, cols] = product[:half]
-        other[:, cols] = product[half:]
+    for side in range(len(routes)):
+        for first in range(0, width, 256):
+            cols = slice(first, first + 256)
+            down = w_down[:, side * width + first : side * width + first + 256]
+            product = jnp.dot(hidden[...], down, preferred_element_type=jnp.float32)
+            product = product.astype(jnp.bfloat16)
+            for where, piece, to, at in places:
+                if where == side:
+                    here = slice(to, to + capacity)
+                    own[piece][here, cols] = product[at : at + capacity]
+                    other[piece][here, cols] = product[half + at : half + at + capacity]
 
 
 def sum_kernel(*refs):
@@ -341,6 +406,7 @@
     sent = tie(tokens, *block_kv[1:])
     pieces = [tokens] + [swap(sent, "exp", d) for d in peers[1:]]
     routing = both.reshape(ctx_count, ctx_rows + 2 * TOP, 2 * HEAD_SIZE)[:, ctx_rows:]
+    routing = jnp.stack([routing] + [swap(routing, "exp", d) for d in peers[1:]], axis=0)
 
     positions = jnp.concatenate(
         [me_ctx * ctx_rows + (me_exp ^ d) * rows + jnp.arange(rows) for d in peers]
@@ -368,7 +434,7 @@
             [bf16((rows, width)) for _ in some],
             [SMEM, VMEM, VMEM, VMEM],
             place,
-            tie(asked, *last),
+            tie(asked, *last, *([routing] if last else [])),
             both,
             w_out,
             name="attention",
@@ -399,62 +465,84 @@
     )
 
     groups = ctx_count // 2
+    low, high = [0, 1], list(range(0, exp_count, 2))
+    routes = [(low, high), (high, low)]
+    half = width // 2
     far = [normed]
     for g in range(1, groups):
         far.append(swap(tie(normed, *([far[g - 1]] if g > 2 else [])), "ctx", 2 * g))
-    in_flight = {d: () for d in peers[1:]}
-
-    def send(array, d):
-        came = swap(tie(array, *in_flight[d]), "exp", d)
-        in_flight[d] = (came,)
+    in_flight = {}
+
+    def send(array, d, kind):
+        came = swap(tie(array, *in_flight.get((kind, d), ())), "exp", d)
+        in_flight[kind, d] = (came,)
         return came
 
     arrived = []
     for g in range(groups):
+        sources = []
+        for side, (near, _) in enumerate(routes):
+            part = far[g][:, side * half : (side + 1) * half]
+            sources += [part] + [send(part, n, "whole") for n in near[1:]]
         outgoing = call(
-            functools.partial(dispatch_kernel, g, capacity),
-            [bf16((2 * capacity, width)) for _ in peers],
-            [SMEM, VMEM, VMEM],
+            functools.partial(dispatch_kernel, routes, g, capacity),
+            [bf16((2 * len(near) * capacity, half)) for near, away in routes for _ in away],
+            [SMEM, VMEM] + [VMEM] * len(sources),
             place,
             routing,
-            far[g],
+            *sources,
             name="dispatch",
         )
-        arrived.append([outgoing[0]] + [send(outgoing[d], d) for d in peers[1:]])
+        onward = [a for _, away in routes for a in away]
+        arrived.append([send(out, a, "picked") if a else out for out, a in zip(outgoing, onward)])
 
     produced = []
-    half = exp_count * capacity
+    slots = exp_count * capacity
     for came in arrived:
-        mate = swap(jnp.concatenate([rows_in[capacity:] for rows_in in came], axis=0), "ctx", 1)
-        own, other = call(
-            expert_kernel,
-            [bf16((half, width)), bf16((half, width))],
-            [VMEM] * (exp_count + 4),
+        mate = jnp.concatenate([part[part.shape[0] // 2 :] for part in came], axis=0)
+        made = call(
+            functools.partial(expert_kernel, routes, capacity),
+            [bf16((len(near) * capacity, half)) for near, away in routes for _ in away] * 2,
+            [VMEM] * (len(came) + 4),
             *came,
-            mate,
+            swap(mate, "ctx", 1),
             w_gate[0],
             w_up[0],
             w_down[0],
             name="expert",
-            scratch=[pltpu.VMEM((2 * half, w_gate.shape[2]), jnp.bfloat16)],
-        )
-        produced.append((own, swap(other, "ctx", 1)))
+            scratch=[
+                pltpu.VMEM((2, 2 * slots, half), jnp.bfloat16),
+                pltpu.VMEM((2 * slots, w_gate.shape[2]), jnp.bfloat16),
+            ],
+        )
+        own, other = made[: len(came)], made[len(came) :]
+        produced.append([(mine, swap(mates, "ctx", 1)) for mine, mates in zip(own, other)])
 
     totals, hop = [], ()
     for g in [*range(2, groups), *(g for g in (1, 0) if g < groups)]:
-        back = []
-        for d in peers:
-            mine = slice(d * capacity, (d + 1) * capacity)
-            back.append(jnp.concatenate([part[mine] for part in produced[g]], axis=0))
-        back = [back[0]] + [send(back[d], d) for d in peers[1:]]
-        total = call(
-            functools.partial(combine_kernel, g, capacity),
-            bf16((rows, width)),
-            [SMEM, VMEM] + [VMEM] * exp_count,
+        back, pieces = [], iter(produced[g])
+        for _, away in routes:
+            for a in away:
+                pair = next(pieces)
+                back += [send(jnp.concatenate(pair, axis=0), a, "picked")] if a else pair
+        onward = [n for near, _ in routes for n in near[1:]]
+        kept, *sums = call(
+            functools.partial(combine_kernel, routes, g, capacity),
+            [jax.ShapeDtypeStruct((rows, width), jnp.float32)] + [bf16((rows, half)) for _ in onward],
+            [SMEM, VMEM] + [VMEM] * len(back),
             place,
             routing,
             *back,
             name="combine",
+        )
+        sums = [send(part, n, "whole") for part, n in zip(sums, onward)]
+        total = call(
+            gather_kernel,
+            bf16((rows, width)),
+            [VMEM] * (1 + len(sums)),
+            kept,
+            *sums,
+            name="gather",
         )
         if g:
             total = swap(tie(total, *(hop if g > 1 else ())), "ctx", 2 * g)

time: 271 us -> 280 us (1.033)
  starting transfers between devices: 54.8 us -> 78.7 us
  waiting for transfers between devices: 153 us -> 139 us
    ppermute x47 -> x70, starting transfers between devices: 54.8 us -> 78.7 us  [swap(): return lax.ppermute(array, axis, pairs)]
    ppermute x47 -> x70, waiting for transfers between devices: 152 us -> 137 us  [swap(): return lax.ppermute(array, axis, pairs)]
    pallas_call x23 -> x27, Pallas kernels: 39.1 us -> 39.5 us  [call(): pl.pallas_call(kernel, out_shape=out_shape, in_specs=specs, out_specs=jax...]
  transfers between devices with their start and end apart: 48 -> 71, of which waited for: 25 -> 35; matrix products, arithmetic and copies ran while one was open for 1% -> 1% of each run, Pallas kernels for 11% -> 11%
where the time goes in v6:
time: 280 us
  waiting for transfers between devices  139 us (50%)
  starting transfers between devices  78.7 us (28%)
  Pallas kernels  39.5 us (14%)
  between operations  14.1 us (5%)
  local copies, waits for them, and re-layouts  5.94 us (2%)
  other arithmetic  3.08 us (1%)
    ppermute x70, waiting for transfers between devices, swap(): return lax.ppermute(array, axis, pairs)  137 us
    ppermute x70, starting transfers between devices, swap(): return lax.ppermute(array, axis, pairs)  78.7 us
    pallas_call x27, Pallas kernels, call(): pl.pallas_call(kernel, out_shape=out_shape, in_specs=specs, out_specs=jax...  39.5 us
  transfers between devices with their start and end apart: 71, of which 35 were waited for; matrix products, arithmetic and copies ran while one was open for 1% of the time, Pallas kernels for 11%

profile of v6, /device:TPU:0, one launch (start us, length us, event | category | flops | bytes accessed | tf_op | source)
XLA Modules:
  0.0 280.2 jit_solution(11342355330453548795)
XLA Ops:
  8.2 4.5 %own_rows.1 = (bf16[128,256]{1,0:T(8,128)(2,1)}, bf16[128,256]{1,0:T(8,128)(2,1)}, bf16[128,256]{1,0:T(8,128)(2,1)}, bf16[128,256]{1,0:T(8,128)(2,1)}, bf16[16,256]{1,0:T(8,128)(2,1)}) custom-call(s32[6]{0:T(128)} %pad_add_fusion.place, s32[8,128]{1,0:T(8,128)} %bitcast.37, s32[8,128]{1,0:T(8,128)} %bitcast.38, bf16[128,2048]{1,0:T(8,128)(2,1)} %tokens.1, ...), custom_call_target="tpu_custom_call" | custom-call | flops 1000 | bytes 1000 | tf_op jit(solution)/shard_map/own_rows/pallas_call | solution.py:337
  12.6 3.0 %collective-permute-start = (bf16[128,256]{1,0:T(8,128)(2,1)}, bf16[128,256]{1,0:T(8,128)(2,1)S(1)}, u32[]{:S(2)}, u32[]{:S(2)}) collective-permute-start(bf16[128,256]{1,0:T(8,128)(2,1)} %get-tuple-element.106), channel_id=1, source_target_pairs={{0,1},{1,0},{2,3},{3,2},{4,5},{5,4},{6,7},{7,6},{8,9},{9,8},{10,11... | collective-permute-start | bytes 196616 | tf_op jit(solution)/shard_map/ppermute | solution.py:35
  18.3 1.8 collective-permute-done.1
  20.1 2.4 collective-permute-done.2
  24.9 2.7 collective-permute-start.5
  28.6 10.4 %collective-permute-done.3.refs_1_ = bf16[128,2048]{1,0:T(8,128)(2,1)S(1)} collective-permute-done((bf16[128,2048]{1,0:T(8,128)(2,1)S(1)}, bf16[128,2048]{1,0:T(8,128)(2,1)S(1)}, u32[]{:S(2)}, u32[]{:S(2)}) %collective-permute-start.3) | collective-permute-done | bytes 524320 | tf_op jit(solution)/shard_map/ppermute | solution.py:35
  38.9 9.0 %collective-permute-done.4.refs_2_ = bf16[128,2048]{1,0:T(8,128)(2,1)S(1)} collective-permute-done((bf16[128,2048]{1,0:T(8,128)(2,1)S(1)}, bf16[128,2048]{1,0:T(8,128)(2,1)S(1)}, u32[]{:S(2)}, u32[]{:S(2)}) %collective-permute-start.4) | collective-permute-done | bytes 524320 | tf_op jit(solution)/shard_map/ppermute | solution.py:35
  47.9 1.6 copy-done.7
  49.5 1.8 queries.1
  51.4 1.7 all-gather.2.cloned.1.call-done.both
  53.2 1.6 copy-done.3
  54.8 1.7 attention.4
  56.5 2.4 collective-permute-start.9
  62.5 11.3 %collective-permute-done.8 = bf16[8,16,256]{2,1,0:T(8,128)(2,1)S(1)} collective-permute-done((bf16[8,16,256]{2,1,0:T(8,128)(2,1)S(1)}, bf16[8,16,256]{2,1,0:T(8,128)(2,1)S(1)}, u32[]{:S(2)}, u32[]{:S(2)}) %collective-permute-start.8) | collective-permute-done | bytes 65568 | tf_op jit(solution)/shard_map/ppermute | solution.py:35
  75.2 1.7 attention.5
  78.4 1.7 attention.6
  81.6 1.9 attention.7.refs_0_
  83.6 8.0 %collective-permute-done.10.refs_1_ = bf16[128,2048]{1,0:T(8,128)(2,1)S(1)} collective-permute-done((bf16[128,2048]{1,0:T(8,128)(2,1)S(1)}, bf16[128,2048]{1,0:T(8,128)(2,1)S(1)}, u32[]{:S(2)}, u32[]{:S(2)}) %collective-permute-start.10) | collective-permute-done | bytes 524320 | tf_op jit(solution)/shard_map/ppermute | solution.py:35
  91.7 2.9 %collective-permute-done.11.partial = bf16[128,2048]{1,0:T(8,128)(2,1)S(1)} collective-permute-done((bf16[128,2048]{1,0:T(8,128)(2,1)S(1)}, bf16[128,2048]{1,0:T(8,128)(2,1)S(1)}, u32[]{:S(2)}, u32[]{:S(2)}) %collective-permute-start.11) | collective-permute-done | bytes 524320 | tf_op jit(solution)/shard_map/ppermute | solution.py:35
  95.0 5.9 %collective-permute-start.13 = (bf16[128,2048]{1,0:T(8,128)(2,1)S(1)}, bf16[128,2048]{1,0:T(8,128)(2,1)S(1)}, u32[]{:S(2)}, u32[]{:S(2)}) collective-permute-start(bf16[128,2048]{1,0:T(8,128)(2,1)S(1)} %get-tuple-element.137), channel_id=1, source_target_pairs={{0,8},{4,12},{8,0},{12,4},{16,24},{20,28},{24,16},{28,20},{1,9},{5... | collective-permute-start | bytes 1572872 | tf_op jit(solution)/shard_map/ppermute | solution.py:35
  103.1 9.5 %collective-permute-start.12 = (bf16[128,2048]{1,0:T(8,128)(2,1)S(1)}, bf16[128,2048]{1,0:T(8,128)(2,1)S(1)}, u32[]{:S(2)}, u32[]{:S(2)}) collective-permute-start(bf16[128,2048]{1,0:T(8,128)(2,1)S(1)} %get-tuple-element.137), channel_id=1, source_target_pairs={{0,16},{4,20},{8,24},{12,28},{16,0},{20,4},{24,8},{28,12},{1,17},{... | collective-permute-start | bytes 1572872 | tf_op jit(solution)/shard_map/ppermute | solution.py:35
  115.7 6.7 %collective-permute-done.13 = bf16[128,2048]{1,0:T(8,128)(2,1)S(1)} collective-permute-done((bf16[128,2048]{1,0:T(8,128)(2,1)S(1)}, bf16[128,2048]{1,0:T(8,128)(2,1)S(1)}, u32[]{:S(2)}, u32[]{:S(2)}) %collective-permute-start.13) | collective-permute-done | bytes 524320 | tf_op jit(solution)/shard_map/ppermute | solution.py:35
  122.5 2.6 collective-permute-start.18
  125.1 10.0 %collective-permute-done.12 = bf16[128,2048]{1,0:T(8,128)(2,1)S(1)} collective-permute-done((bf16[128,2048]{1,0:T(8,128)(2,1)S(1)}, bf16[128,2048]{1,0:T(8,128)(2,1)S(1)}, u32[]{:S(2)}, u32[]{:S(2)}) %collective-permute-start.12) | collective-permute-done | bytes 524320 | tf_op jit(solution)/shard_map/ppermute | solution.py:35
  135.2 3.1 %collective-permute-start.29 = (bf16[128,2048]{1,0:T(8,128)(2,1)S(1)}, bf16[128,2048]{1,0:T(8,128)(2,1)S(1)}, u32[]{:S(2)}, u32[]{:S(2)}) collective-permute-start(bf16[128,2048]{1,0:T(8,128)(2,1)S(1)} %get-tuple-element.137), channel_id=1, source_target_pairs={{0,24},{4,28},{8,16},{12,20},{16,8},{20,12},{24,0},{28,4},{1,25},{... | collective-permute-start | bytes 1572872 | tf_op jit(solution)/shard_map/ppermute | solution.py:35
  139.5 2.0 collective-permute-start.24
  141.7 1.9 collective-permute-start.19
  143.7 10.4 %collective-permute-done.16.refs_1_ = bf16[128,1024]{1,0:T(8,128)(2,1)S(1)} collective-permute-done((bf16[128,1024]{1,0:T(8,128)(2,1)S(1)}, bf16[128,1024]{1,0:T(8,128)(2,1)S(1)}, u32[]{:S(2)}, u32[]{:S(2)}) %collective-permute-start.16) | collective-permute-done | bytes 262176 | tf_op jit(solution)/shard_map/ppermute | solution.py:35
  155.2 1.6 collective-permute-start.25
  159.5 6.6 %collective-permute-done.25.refs_3_ = bf16[192,1024]{1,0:T(8,128)(2,1)S(1)} collective-permute-done((bf16[192,1024]{1,0:T(8,128)(2,1)S(1)}, bf16[192,1024]{1,0:T(8,128)(2,1)S(1)}, u32[]{:S(2)}, u32[]{:S(2)}) %collective-permute-start.25) | collective-permute-done | bytes 393248 | tf_op jit(solution)/shard_map/ppermute | solution.py:35
  167.3 1.6 collective-permute-done.30.refs_1_
  173.0 7.0 %collective-permute-done.36.refs_3_ = bf16[192,1024]{1,0:T(8,128)(2,1)S(1)} collective-permute-done((bf16[192,1024]{1,0:T(8,128)(2,1)S(1)}, bf16[192,1024]{1,0:T(8,128)(2,1)S(1)}, u32[]{:S(2)}, u32[]{:S(2)}) %collective-permute-start.36) | collective-permute-done | bytes 393248 | tf_op jit(solution)/shard_map/ppermute | solution.py:35
  180.6 3.8 %expert.4 = (bf16[96,1024]{1,0:T(8,128)(2,1)S(1)}, bf16[96,1024]{1,0:T(8,128)(2,1)S(1)}, bf16[96,1024]{1,0:T(8,128)(2,1)S(1)}, bf16[96,1024]{1,0:T(8,128)(2,1)S(...) custom-call(bf16[192,1024]{1,0:T(8,128)(2,1)S(1)} %get-tuple-element, ...), custom_call_target="tpu_custom_call" | custom-call | flops 1000 | bytes 1000 | tf_op jit(solution)/shard_map/expert/pallas_call | solution.py:337
  189.3 3.8 %expert.5 = (bf16[96,1024]{1,0:T(8,128)(2,1)S(1)}, bf16[96,1024]{1,0:T(8,128)(2,1)S(1)}, bf16[96,1024]{1,0:T(8,128)(2,1)S(1)}, bf16[96,1024]{1,0:T(8,128)(2,1)S(...) custom-call(bf16[192,1024]{1,0:T(8,128)(2,1)S(1)} %get-tuple-element, ...), custom_call_target="tpu_custom_call" | custom-call | flops 1000 | bytes 1000 | tf_op jit(solution)/shard_map/expert/pallas_call | solution.py:337
  193.3 4.2 %collective-permute-done.33.refs_2_ = bf16[192,1024]{1,0:T(8,128)(2,1)S(1)} collective-permute-done((bf16[192,1024]{1,0:T(8,128)(2,1)S(1)}, bf16[192,1024]{1,0:T(8,128)(2,1)S(1)}, u32[]{:S(2)}, u32[]{:S(2)}) %collective-permute-start.33) | collective-permute-done | bytes 393248 | tf_op jit(solution)/shard_map/ppermute | solution.py:35
  200.3 1.7 collective-permute-start.47
  202.0 4.1 %expert.6 = (bf16[96,1024]{1,0:T(8,128)(2,1)S(1)}, bf16[96,1024]{1,0:T(8,128)(2,1)S(1)}, bf16[96,1024]{1,0:T(8,128)(2,1)S(1)}, bf16[96,1024]{1,0:T(8,128)(2,1)S(...) custom-call(bf16[192,1024]{1,0:T(8,128)(2,1)S(1)} %get-tuple-element, ...), custom_call_target="tpu_custom_call" | custom-call | flops 1000 | bytes 1000 | tf_op jit(solution)/shard_map/expert/pallas_call | solution.py:337
  210.0 2.2 collective-permute-done.47.refs_5_
  213.2 1.7 collective-permute-start.57
  214.9 3.0 %collective-permute-done.38.refs_0_ = bf16[128,1024]{1,0:T(8,128)(2,1)S(1)} collective-permute-done((bf16[128,1024]{1,0:T(8,128)(2,1)S(1)}, bf16[128,1024]{1,0:T(8,128)(2,1)S(1)}, u32[]{:S(2)}, u32[]{:S(2)}) %collective-permute-start.38) | collective-permute-done | bytes 262176 | tf_op jit(solution)/shard_map/ppermute | solution.py:35
  222.2 3.8 %expert.7 = (bf16[96,1024]{1,0:T(8,128)(2,1)S(1)}, bf16[96,1024]{1,0:T(8,128)(2,1)S(1)}, bf16[96,1024]{1,0:T(8,128)(2,1)S(1)}, bf16[96,1024]{1,0:T(8,128)(2,1)S(...) custom-call(bf16[192,1024]{1,0:T(8,128)(2,1)S(1)} %get-tuple-element, ...), custom_call_target="tpu_custom_call" | custom-call | flops 1000 | bytes 1000 | tf_op jit(solution)/shard_map/expert/pallas_call | solution.py:337
  227.7 3.8 %collective-permute-done.48.refs_0_ = bf16[128,1024]{1,0:T(8,128)(2,1)S(1)} collective-permute-done((bf16[128,1024]{1,0:T(8,128)(2,1)S(1)}, bf16[128,1024]{1,0:T(8,128)(2,1)S(1)}, u32[]{:S(2)}, u32[]{:S(2)}) %collective-permute-start.48) | collective-permute-done | bytes 262176 | tf_op jit(solution)/shard_map/ppermute | solution.py:35
  231.6 1.7 collective-permute-start.58
  235.4 8.6 %collective-permute-done.40.refs_1_ = bf16[128,2048]{1,0:T(8,128)(2,1)S(1)} collective-permute-done((bf16[128,2048]{1,0:T(8,128)(2,1)S(1)}, bf16[128,2048]{1,0:T(8,128)(2,1)S(1)}, u32[]{:S(2)}, u32[]{:S(2)}) %collective-permute-start.40) | collective-permute-done | bytes 524320 | tf_op jit(solution)/shard_map/ppermute | solution.py:35
  245.4 2.2 collective-permute-start.50
  250.1 4.9 %collective-permute-done.67.refs_5_ = bf16[192,1024]{1,0:T(8,128)(2,1)S(1)} collective-permute-done((bf16[192,1024]{1,0:T(8,128)(2,1)S(1)}, bf16[192,1024]{1,0:T(8,128)(2,1)S(1)}, u32[]{:S(2)}, u32[]{:S(2)}) %collective-permute-start.67) | collective-permute-done | bytes 393248 | tf_op jit(solution)/shard_map/ppermute | solution.py:35
  258.3 5.2 %collective-permute-done.68.refs_0_ = bf16[128,1024]{1,0:T(8,128)(2,1)S(1)} collective-permute-done((bf16[128,1024]{1,0:T(8,128)(2,1)S(1)}, bf16[128,1024]{1,0:T(8,128)(2,1)S(1)}, u32[]{:S(2)}, u32[]{:S(2)}) %collective-permute-start.68) | collective-permute-done | bytes 262176 | tf_op jit(solution)/shard_map/ppermute | solution.py:35
  264.6 7.5 %collective-permute-done.60.refs_3_ = bf16[128,2048]{1,0:T(8,128)(2,1)S(1)} collective-permute-done((bf16[128,2048]{1,0:T(8,128)(2,1)S(1)}, bf16[128,2048]{1,0:T(8,128)(2,1)S(1)}, u32[]{:S(2)}, u32[]{:S(2)}) %collective-permute-start.60) | collective-permute-done | bytes 524320 | tf_op jit(solution)/shard_map/ppermute | solution.py:35
  (207 shorter events, 62.8 us)
Async XLA Ops:
  6.5 46.6 %all-gather.2.cloned.1.call-start = ((), (), s32[]{:S(2)}) async-start(), calls=%async_computation | async-start | bytes 2433024 | tf_op jit(solution)/shard_map/all_gather | solution.py:405
  24.0 14.9 %collective-permute-start.3 = (bf16[128,2048]{1,0:T(8,128)(2,1)S(1)}, bf16[128,2048]{1,0:T(8,128)(2,1)S(1)}, u32[]{:S(2)}, u32[]{:S(2)}) collective-permute-start(bf16[128,2048]{1,0:T(8,128)(2,1)S(1)} %copy-done.6), channel_id=1, source_target_pairs={{0,1},{1,0},{2,3},{3,2},{4,5},{5,4},{6,7},{7,6},{8,9},{9,8},{10,11... | collective-permute-start | bytes 1572872 | tf_op jit(solution)/shard_map/ppermute | solution.py:35
  24.6 23.3 %collective-permute-start.4 = (bf16[128,2048]{1,0:T(8,128)(2,1)S(1)}, bf16[128,2048]{1,0:T(8,128)(2,1)S(1)}, u32[]{:S(2)}, u32[]{:S(2)}) collective-permute-start(bf16[128,2048]{1,0:T(8,128)(2,1)S(1)} %copy-done.6), channel_id=1, source_target_pairs={{0,2},{1,3},{2,0},{3,1},{4,6},{5,7},{6,4},{7,5},{8,10},{9,11},{10,... | collective-permute-start | bytes 1572872 | tf_op jit(solution)/shard_map/ppermute | solution.py:35
  24.9 23.0 %collective-permute-start.5 = (bf16[128,2048]{1,0:T(8,128)(2,1)S(1)}, bf16[128,2048]{1,0:T(8,128)(2,1)S(1)}, u32[]{:S(2)}, u32[]{:S(2)}) collective-permute-start(bf16[128,2048]{1,0:T(8,128)(2,1)S(1)} %copy-done.6), channel_id=1, source_target_pairs={{0,3},{1,2},{2,1},{3,0},{4,7},{5,6},{6,5},{7,4},{8,11},{9,10},{10,... | collective-permute-start | bytes 1572872 | tf_op jit(solution)/shard_map/ppermute | solution.py:35
  56.5 27.0 %collective-permute-start.9 = (bf16[128,2048]{1,0:T(8,128)(2,1)S(1)}, bf16[128,2048]{1,0:T(8,128)(2,1)S(1)}, u32[]{:S(2)}, u32[]{:S(2)}) collective-permute-start(bf16[128,2048]{1,0:T(8,128)(2,1)S(1)} %attention.4), channel_id=1, source_target_pairs={{0,3},{1,2},{2,1},{3,0},{4,7},{5,6},{6,5},{7,4},{8,11},{9,10},{10,... | collective-permute-start | bytes 1572872 | tf_op jit(solution)/shard_map/ppermute | solution.py:35
  58.9 14.8 %collective-permute-start.8 = (bf16[8,16,256]{2,1,0:T(8,128)(2,1)S(1)}, bf16[8,16,256]{2,1,0:T(8,128)(2,1)S(1)}, u32[]{:S(2)}, u32[]{:S(2)}) collective-permute-start(bf16[8,16,256]{2,1,0:T(8,128)(2,1)S(1)} %get-tuple-element.208), channel_id=1, source_target_pairs={{0,3},{1,2},{2,1},{3,0},{4,7},{5,6},{6,5},{7,4},{8,11},{9,10},{10,... | collective-permute-start | bytes 196616 | tf_op jit(solution)/shard_map/ppermute | solution.py:35
  59.6 15.5 %collective-permute-start.7 = (bf16[8,16,256]{2,1,0:T(8,128)(2,1)S(1)}, bf16[8,16,256]{2,1,0:T(8,128)(2,1)S(1)}, u32[]{:S(2)}, u32[]{:S(2)}) collective-permute-start(bf16[8,16,256]{2,1,0:T(8,128)(2,1)S(1)} %get-tuple-element.208), channel_id=1, source_target_pairs={{0,2},{1,3},{2,0},{3,1},{4,6},{5,7},{6,4},{7,5},{8,10},{9,11},{10,... | collective-permute-start | bytes 196616 | tf_op jit(solution)/shard_map/ppermute | solution.py:35
  61.0 14.1 %collective-permute-start.6 = (bf16[8,16,256]{2,1,0:T(8,128)(2,1)S(1)}, bf16[8,16,256]{2,1,0:T(8,128)(2,1)S(1)}, u32[]{:S(2)}, u32[]{:S(2)}) collective-permute-start(bf16[8,16,256]{2,1,0:T(8,128)(2,1)S(1)} %get-tuple-element.208), channel_id=1, source_target_pairs={{0,1},{1,0},{2,3},{3,2},{4,5},{5,4},{6,7},{7,6},{8,9},{9,8},{10,11... | collective-permute-start | bytes 196616 | tf_op jit(solution)/shard_map/ppermute | solution.py:35
  76.9 14.7 %collective-permute-start.10 = (bf16[128,2048]{1,0:T(8,128)(2,1)S(1)}, bf16[128,2048]{1,0:T(8,128)(2,1)S(1)}, u32[]{:S(2)}, u32[]{:S(2)}) collective-permute-start(bf16[128,2048]{1,0:T(8,128)(2,1)S(1)} %attention.5), channel_id=1, source_target_pairs={{0,1},{1,0},{2,3},{3,2},{4,5},{5,4},{6,7},{7,6},{8,9},{9,8},{10,11... | collective-permute-start | bytes 1572872 | tf_op jit(solution)/shard_map/ppermute | solution.py:35
  80.1 14.5 %collective-permute-start.11 = (bf16[128,2048]{1,0:T(8,128)(2,1)S(1)}, bf16[128,2048]{1,0:T(8,128)(2,1)S(1)}, u32[]{:S(2)}, u32[]{:S(2)}) collective-permute-start(bf16[128,2048]{1,0:T(8,128)(2,1)S(1)} %attention.6), channel_id=1, source_target_pairs={{0,2},{1,3},{2,0},{3,1},{4,6},{5,7},{6,4},{7,5},{8,10},{9,11},{10,... | collective-permute-start | bytes 1572872 | tf_op jit(solution)/shard_map/ppermute | solution.py:35
  95.0 27.4 %collective-permute-start.13 = (bf16[128,2048]{1,0:T(8,128)(2,1)S(1)}, bf16[128,2048]{1,0:T(8,128)(2,1)S(1)}, u32[]{:S(2)}, u32[]{:S(2)}) collective-permute-start(bf16[128,2048]{1,0:T(8,128)(2,1)S(1)} %get-tuple-element.137), channel_id=1, source_target_pairs={{0,8},{4,12},{8,0},{12,4},{16,24},{20,28},{24,16},{28,20},{1,9},{5... | collective-permute-start | bytes 1572872 | tf_op jit(solution)/shard_map/ppermute | solution.py:35
  101.0 11.6 %collective-permute-start.14 = (bf16[128,1024]{1,0:T(8,128)(2,1)S(1)}, bf16[128,1024]{1,0:T(8,128)(2,1)S(1)}, u32[]{:S(2)}, u32[]{:S(2)}) collective-permute-start(bf16[128,1024]{1,0:T(8,128)(2,1)S(1)} %get-tuple-element.212.refs_0_), channel_id=1, source_target_pairs={{0,1},{1,0},{2,3},{3,2},{4,5},{5,4},{6,7},{7,6},{8,9},{9,8},{10,11... | collective-permute-start | bytes 786440 | tf_op jit(solution)/shard_map/ppermute | solution.py:35
  101.6 11.0 %collective-permute-start.17 = (bf16[128,1024]{1,0:T(8,128)(2,1)S(1)}, bf16[128,1024]{1,0:T(8,128)(2,1)S(1)}, u32[]{:S(2)}, u32[]{:S(2)}) collective-permute-start(bf16[128,1024]{1,0:T(8,128)(2,1)S(1)} %get-tuple-element.211.refs_2_), channel_id=1, source_target_pairs={{0,2},{1,3},{2,0},{3,1},{4,6},{5,7},{6,4},{7,5},{8,10},{9,11},{10,... | collective-permute-start | bytes 786440 | tf_op jit(solution)/shard_map/ppermute | solution.py:35
  103.1 32.1 %collective-permute-start.12 = (bf16[128,2048]{1,0:T(8,128)(2,1)S(1)}, bf16[128,2048]{1,0:T(8,128)(2,1)S(1)}, u32[]{:S(2)}, u32[]{:S(2)}) collective-permute-start(bf16[128,2048]{1,0:T(8,128)(2,1)S(1)} %get-tuple-element.137), channel_id=1, source_target_pairs={{0,16},{4,20},{8,24},{12,28},{16,0},{20,4},{24,8},{28,12},{1,17},{... | collective-permute-start | bytes 1572872 | tf_op jit(solution)/shard_map/ppermute | solution.py:35
  113.6 25.8 %collective-permute-start.20 = (bf16[192,1024]{1,0:T(8,128)(2,1)S(1)}, bf16[192,1024]{1,0:T(8,128)(2,1)S(1)}, u32[]{:S(2)}, u32[]{:S(2)}) collective-permute-start(bf16[192,1024]{1,0:T(8,128)(2,1)S(1)} %get-tuple-element.124), channel_id=1, source_target_pairs={{0,2},{1,3},{2,0},{3,1},{4,6},{5,7},{6,4},{7,5},{8,10},{9,11},{10,... | collective-permute-start | bytes 1179656 | tf_op jit(solution)/shard_map/ppermute | solution.py:35
  114.3 25.2 %collective-permute-start.23 = (bf16[192,1024]{1,0:T(8,128)(2,1)S(1)}, bf16[192,1024]{1,0:T(8,128)(2,1)S(1)}, u32[]{:S(2)}, u32[]{:S(2)}) collective-permute-start(bf16[192,1024]{1,0:T(8,128)(2,1)S(1)} %get-tuple-element.130), channel_id=1, source_target_pairs={{0,1},{1,0},{2,3},{3,2},{4,5},{5,4},{6,7},{7,6},{8,9},{9,8},{10,11... | collective-permute-start | bytes 1179656 | tf_op jit(solution)/shard_map/ppermute | solution.py:35
  122.4 15.9 %collective-permute-start.15 = (bf16[128,1024]{1,0:T(8,128)(2,1)S(1)}, bf16[128,1024]{1,0:T(8,128)(2,1)S(1)}, u32[]{:S(2)}, u32[]{:S(2)}) collective-permute-start(bf16[128,1024]{1,0:T(8,128)(2,1)S(1)} %get-tuple-element.117.refs_0_), channel_id=1, source_target_pairs={{0,1},{1,0},{2,3},{3,2},{4,5},{5,4},{6,7},{7,6},{8,9},{9,8},{10,11... | collective-permute-start | bytes 786440 | tf_op jit(solution)/shard_map/ppermute | solution.py:35
  122.5 15.8 %collective-permute-start.18 = (bf16[128,1024]{1,0:T(8,128)(2,1)S(1)}, bf16[128,1024]{1,0:T(8,128)(2,1)S(1)}, u32[]{:S(2)}, u32[]{:S(2)}) collective-permute-start(bf16[128,1024]{1,0:T(8,128)(2,1)S(1)} %get-tuple-element.119.refs_2_), channel_id=1, source_target_pairs={{0,2},{1,3},{2,0},{3,1},{4,6},{5,7},{6,4},{7,5},{8,10},{9,11},{10,... | collective-permute-start | bytes 786440 | tf_op jit(solution)/shard_map/ppermute | solution.py:35
  135.2 23.2 %collective-permute-start.29 = (bf16[128,2048]{1,0:T(8,128)(2,1)S(1)}, bf16[128,2048]{1,0:T(8,128)(2,1)S(1)}, u32[]{:S(2)}, u32[]{:S(2)}) collective-permute-start(bf16[128,2048]{1,0:T(8,128)(2,1)S(1)} %get-tuple-element.137), channel_id=1, source_target_pairs={{0,24},{4,28},{8,16},{12,20},{16,8},{20,12},{24,0},{28,4},{1,25},{... | collective-permute-start | bytes 1572872 | tf_op jit(solution)/shard_map/ppermute | solution.py:35
  139.4 15.8 %collective-permute-start.21 = (bf16[192,1024]{1,0:T(8,128)(2,1)S(1)}, bf16[192,1024]{1,0:T(8,128)(2,1)S(1)}, u32[]{:S(2)}, u32[]{:S(2)}) collective-permute-start(bf16[192,1024]{1,0:T(8,128)(2,1)S(1)} %get-tuple-element.125), channel_id=1, source_target_pairs={{0,2},{1,3},{2,0},{3,1},{4,6},{5,7},{6,4},{7,5},{8,10},{9,11},{10,... | collective-permute-start | bytes 1179656 | tf_op jit(solution)/shard_map/ppermute | solution.py:35
  139.5 15.7 %collective-permute-start.24 = (bf16[192,1024]{1,0:T(8,128)(2,1)S(1)}, bf16[192,1024]{1,0:T(8,128)(2,1)S(1)}, u32[]{:S(2)}, u32[]{:S(2)}) collective-permute-start(bf16[192,1024]{1,0:T(8,128)(2,1)S(1)} %get-tuple-element.131), channel_id=1, source_target_pairs={{0,1},{1,0},{2,3},{3,2},{4,5},{5,4},{6,7},{7,6},{8,9},{9,8},{10,11... | collective-permute-start | bytes 1179656 | tf_op jit(solution)/shard_map/ppermute | solution.py:35
  141.5 12.6 %collective-permute-start.16 = (bf16[128,1024]{1,0:T(8,128)(2,1)S(1)}, bf16[128,1024]{1,0:T(8,128)(2,1)S(1)}, u32[]{:S(2)}, u32[]{:S(2)}) collective-permute-start(bf16[128,1024]{1,0:T(8,128)(2,1)S(1)} %get-tuple-element.118.refs_0_), channel_id=1, source_target_pairs={{0,1},{1,0},{2,3},{3,2},{4,5},{5,4},{6,7},{7,6},{8,9},{9,8},{10,11... | collective-permute-start | bytes 786440 | tf_op jit(solution)/shard_map/ppermute | solution.py:35
  141.7 12.4 %collective-permute-start.19 = (bf16[128,1024]{1,0:T(8,128)(2,1)S(1)}, bf16[128,1024]{1,0:T(8,128)(2,1)S(1)}, u32[]{:S(2)}, u32[]{:S(2)}) collective-permute-start(bf16[128,1024]{1,0:T(8,128)(2,1)S(1)} %get-tuple-element.120.refs_2_), channel_id=1, source_target_pairs={{0,2},{1,3},{2,0},{3,1},{4,6},{5,7},{6,4},{7,5},{8,10},{9,11},{10,... | collective-permute-start | bytes 786440 | tf_op jit(solution)/shard_map/ppermute | solution.py:35
  155.2 10.8 %collective-permute-start.25 = (bf16[192,1024]{1,0:T(8,128)(2,1)S(1)}, bf16[192,1024]{1,0:T(8,128)(2,1)S(1)}, u32[]{:S(2)}, u32[]{:S(2)}) collective-permute-start(bf16[192,1024]{1,0:T(8,128)(2,1)S(1)} %get-tuple-element.132), channel_id=1, source_target_pairs={{0,1},{1,0},{2,3},{3,2},{4,5},{5,4},{6,7},{7,6},{8,9},{9,8},{10,11... | collective-permute-start | bytes 1179656 | tf_op jit(solution)/shard_map/ppermute | solution.py:35
  156.8 10.3 %collective-permute-start.22 = (bf16[192,1024]{1,0:T(8,128)(2,1)S(1)}, bf16[192,1024]{1,0:T(8,128)(2,1)S(1)}, u32[]{:S(2)}, u32[]{:S(2)}) collective-permute-start(bf16[192,1024]{1,0:T(8,128)(2,1)S(1)} %get-tuple-element.126), channel_id=1, source_target_pairs={{0,2},{1,3},{2,0},{3,1},{4,6},{5,7},{6,4},{7,5},{8,10},{9,11},{10,... | collective-permute-start | bytes 1179656 | tf_op jit(solution)/shard_map/ppermute | solution.py:35
  158.4 10.5 %collective-permute-start.30 = (bf16[128,1024]{1,0:T(8,128)(2,1)S(1)}, bf16[128,1024]{1,0:T(8,128)(2,1)S(1)}, u32[]{:S(2)}, u32[]{:S(2)}) collective-permute-start(bf16[128,1024]{1,0:T(8,128)(2,1)S(1)} %get-tuple-element.138.refs_0_), channel_id=1, source_target_pairs={{0,1},{1,0},{2,3},{3,2},{4,5},{5,4},{6,7},{7,6},{8,9},{9,8},{10,11... | collective-permute-start | bytes 786440 | tf_op jit(solution)/shard_map/ppermute | solution.py:35
  159.0 10.9 %collective-permute-start.31 = (bf16[128,1024]{1,0:T(8,128)(2,1)S(1)}, bf16[128,1024]{1,0:T(8,128)(2,1)S(1)}, u32[]{:S(2)}, u32[]{:S(2)}) collective-permute-start(bf16[128,1024]{1,0:T(8,128)(2,1)S(1)} %get-tuple-element.139.refs_2_), channel_id=1, source_target_pairs={{0,2},{1,3},{2,0},{3,1},{4,6},{5,7},{6,4},{7,5},{8,10},{9,11},{10,... | collective-permute-start | bytes 786440 | tf_op jit(solution)/shard_map/ppermute | solution.py:35
  167.2 13.3 %collective-permute-start.26 = (bf16[384,1024]{1,0:T(8,128)(2,1)S(1)}, bf16[384,1024]{1,0:T(8,128)(2,1)S(1)}, u32[]{:S(2)}, u32[]{:S(2)}) collective-permute-start(bf16[384,1024]{1,0:T(8,128)(2,1)S(1)} %pad_maximum_fusion), channel_id=1, source_target_pairs={{0,4},{4,0},{8,12},{12,8},{16,20},{20,16},{24,28},{28,24},{1,5},{5... | collective-permute-start | bytes 2359304 | tf_op jit(solution)/shard_map/ppermute | solution.py:35
  185.2 15.1 %collective-permute-start.51 = (bf16[384,1024]{1,0:T(8,128)(2,1)S(1)}, bf16[384,1024]{1,0:T(8,128)(2,1)S(1)}, u32[]{:S(2)}, u32[]{:S(2)}) collective-permute-start(bf16[384,1024]{1,0:T(8,128)(2,1)S(1)} %pad_maximum_fusion.2), channel_id=1, source_target_pairs={{0,4},{4,0},{8,12},{12,8},{16,20},{20,16},{24,28},{28,24},{1,5},{5... | collective-permute-start | bytes 2359304 | tf_op jit(solution)/shard_map/ppermute | solution.py:35
  186.1 11.5 %collective-permute-start.33 = (bf16[192,1024]{1,0:T(8,128)(2,1)S(1)}, bf16[192,1024]{1,0:T(8,128)(2,1)S(1)}, u32[]{:S(2)}, u32[]{:S(2)}) collective-permute-start(bf16[192,1024]{1,0:T(8,128)(2,1)S(1)} %pad_maximum_fusion.4), channel_id=1, source_target_pairs={{0,2},{1,3},{2,0},{3,1},{4,6},{5,7},{6,4},{7,5},{8,10},{9,11},{10,... | collective-permute-start | bytes 1179656 | tf_op jit(solution)/shard_map/ppermute | solution.py:35
  187.4 20.4 %collective-permute-start.61 = (bf16[384,1024]{1,0:T(8,128)(2,1)S(1)}, bf16[384,1024]{1,0:T(8,128)(2,1)S(1)}, u32[]{:S(2)}, u32[]{:S(2)}) collective-permute-start(bf16[384,1024]{1,0:T(8,128)(2,1)S(1)} %pad_maximum_fusion.3), channel_id=1, source_target_pairs={{0,4},{4,0},{8,12},{12,8},{16,20},{20,16},{24,28},{28,24},{1,5},{5... | collective-permute-start | bytes 2359304 | tf_op jit(solution)/shard_map/ppermute | solution.py:35
  187.9 11.2 %collective-permute-start.37 = (bf16[192,1024]{1,0:T(8,128)(2,1)S(1)}, bf16[192,1024]{1,0:T(8,128)(2,1)S(1)}, u32[]{:S(2)}, u32[]{:S(2)}) collective-permute-start(bf16[192,1024]{1,0:T(8,128)(2,1)S(1)} %pad_maximum_fusion.5), channel_id=1, source_target_pairs={{0,1},{1,0},{2,3},{3,2},{4,5},{5,4},{6,7},{7,6},{8,9},{9,8},{10,11... | collective-permute-start | bytes 1179656 | tf_op jit(solution)/shard_map/ppermute | solution.py:35
  199.1 10.3 %collective-permute-start.44 = (bf16[192,1024]{1,0:T(8,128)(2,1)S(1)}, bf16[192,1024]{1,0:T(8,128)(2,1)S(1)}, u32[]{:S(2)}, u32[]{:S(2)}) collective-permute-start(bf16[192,1024]{1,0:T(8,128)(2,1)S(1)} %pad_maximum_fusion.6), channel_id=1, source_target_pairs={{0,2},{1,3},{2,0},{3,1},{4,6},{5,7},{6,4},{7,5},{8,10},{9,11},{10,... | collective-permute-start | bytes 1179656 | tf_op jit(solution)/shard_map/ppermute | solution.py:35
  200.3 12.0 %collective-permute-start.47 = (bf16[192,1024]{1,0:T(8,128)(2,1)S(1)}, bf16[192,1024]{1,0:T(8,128)(2,1)S(1)}, u32[]{:S(2)}, u32[]{:S(2)}) collective-permute-start(bf16[192,1024]{1,0:T(8,128)(2,1)S(1)} %pad_maximum_fusion.7), channel_id=1, source_target_pairs={{0,1},{1,0},{2,3},{3,2},{4,5},{5,4},{6,7},{7,6},{8,9},{9,8},{10,11... | collective-permute-start | bytes 1179656 | tf_op jit(solution)/shard_map/ppermute | solution.py:35
  207.7 10.2 %collective-permute-start.38 = (bf16[128,1024]{1,0:T(8,128)(2,1)S(1)}, bf16[128,1024]{1,0:T(8,128)(2,1)S(1)}, u32[]{:S(2)}, u32[]{:S(2)}) collective-permute-start(bf16[128,1024]{1,0:T(8,128)(2,1)S(1)} %get-tuple-element.152), channel_id=1, source_target_pairs={{0,1},{1,0},{2,3},{3,2},{4,5},{5,4},{6,7},{7,6},{8,9},{9,8},{10,11... | collective-permute-start | bytes 786440 | tf_op jit(solution)/shard_map/ppermute | solution.py:35
  208.2 9.7 %collective-permute-start.39 = (bf16[128,1024]{1,0:T(8,128)(2,1)S(1)}, bf16[128,1024]{1,0:T(8,128)(2,1)S(1)}, u32[]{:S(2)}, u32[]{:S(2)}) collective-permute-start(bf16[128,1024]{1,0:T(8,128)(2,1)S(1)} %get-tuple-element.154), channel_id=1, source_target_pairs={{0,2},{1,3},{2,0},{3,1},{4,6},{5,7},{6,4},{7,5},{8,10},{9,11},{10,... | collective-permute-start | bytes 786440 | tf_op jit(solution)/shard_map/ppermute | solution.py:35
  212.3 13.8 %collective-permute-start.54 = (bf16[192,1024]{1,0:T(8,128)(2,1)S(1)}, bf16[192,1024]{1,0:T(8,128)(2,1)S(1)}, u32[]{:S(2)}, u32[]{:S(2)}) collective-permute-start(bf16[192,1024]{1,0:T(8,128)(2,1)S(1)} %pad_maximum_fusion.8), channel_id=1, source_target_pairs={{0,2},{1,3},{2,0},{3,1},{4,6},{5,7},{6,4},{7,5},{8,10},{9,11},{10,... | collective-permute-start | bytes 1179656 | tf_op jit(solution)/shard_map/ppermute | solution.py:35
  213.2 13.1 %collective-permute-start.57 = (bf16[192,1024]{1,0:T(8,128)(2,1)S(1)}, bf16[192,1024]{1,0:T(8,128)(2,1)S(1)}, u32[]{:S(2)}, u32[]{:S(2)}) collective-permute-start(bf16[192,1024]{1,0:T(8,128)(2,1)S(1)} %pad_maximum_fusion.9), channel_id=1, source_target_pairs={{0,1},{1,0},{2,3},{3,2},{4,5},{5,4},{6,7},{7,6},{8,9},{9,8},{10,11... | collective-permute-start | bytes 1179656 | tf_op jit(solution)/shard_map/ppermute | solution.py:35
  218.5 25.4 %collective-permute-start.40 = (bf16[128,2048]{1,0:T(8,128)(2,1)S(1)}, bf16[128,2048]{1,0:T(8,128)(2,1)S(1)}, u32[]{:S(2)}, u32[]{:S(2)}) collective-permute-start(bf16[128,2048]{1,0:T(8,128)(2,1)S(1)} %gather.4), channel_id=1, source_target_pairs={{0,16},{4,20},{8,24},{12,28},{16,0},{20,4},{24,8},{28,12},{1,17},{... | collective-permute-start | bytes 1572872 | tf_op jit(solution)/shard_map/ppermute | solution.py:35
  219.9 11.7 %collective-permute-start.48 = (bf16[128,1024]{1,0:T(8,128)(2,1)S(1)}, bf16[128,1024]{1,0:T(8,128)(2,1)S(1)}, u32[]{:S(2)}, u32[]{:S(2)}) collective-permute-start(bf16[128,1024]{1,0:T(8,128)(2,1)S(1)} %get-tuple-element.169), channel_id=1, source_target_pairs={{0,1},{1,0},{2,3},{3,2},{4,5},{5,4},{6,7},{7,6},{8,9},{9,8},{10,11... | collective-permute-start | bytes 786440 | tf_op jit(solution)/shard_map/ppermute | solution.py:35
  221.4 10.2 %collective-permute-start.49 = (bf16[128,1024]{1,0:T(8,128)(2,1)S(1)}, bf16[128,1024]{1,0:T(8,128)(2,1)S(1)}, u32[]{:S(2)}, u32[]{:S(2)}) collective-permute-start(bf16[128,1024]{1,0:T(8,128)(2,1)S(1)} %get-tuple-element.171), channel_id=1, source_target_pairs={{0,2},{1,3},{2,0},{3,1},{4,6},{5,7},{6,4},{7,5},{8,10},{9,11},{10,... | collective-permute-start | bytes 786440 | tf_op jit(solution)/shard_map/ppermute | solution.py:35
  231.6 16.2 %collective-permute-start.62 = (bf16[96,1024]{1,0:T(8,128)(2,1)S(1)}, bf16[96,1024]{1,0:T(8,128)(2,1)S(1)}, u32[]{:S(2)}, u32[]{:S(2)}) collective-permute-start(bf16[96,1024]{1,0:T(8,128)(2,1)S(1)} %get-tuple-element.193), channel_id=1, source_target_pairs={{0,4},{4,0},{8,12},{12,8},{16,20},{20,16},{24,28},{28,24},{1,5},{5... | collective-permute-start | bytes 589832 | tf_op jit(solution)/shard_map/ppermute | solution.py:35
  231.6 13.8 %collective-permute-start.58 = (bf16[128,1024]{1,0:T(8,128)(2,1)S(1)}, bf16[128,1024]{1,0:T(8,128)(2,1)S(1)}, u32[]{:S(2)}, u32[]{:S(2)}) collective-permute-start(bf16[128,1024]{1,0:T(8,128)(2,1)S(1)} %get-tuple-element.187), channel_id=1, source_target_pairs={{0,1},{1,0},{2,3},{3,2},{4,5},{5,4},{6,7},{7,6},{8,9},{9,8},{10,11... | collective-permute-start | bytes 786440 | tf_op jit(solution)/shard_map/ppermute | solution.py:35
  233.2 14.4 %collective-permute-start.59 = (bf16[128,1024]{1,0:T(8,128)(2,1)S(1)}, bf16[128,1024]{1,0:T(8,128)(2,1)S(1)}, u32[]{:S(2)}, u32[]{:S(2)}) collective-permute-start(bf16[128,1024]{1,0:T(8,128)(2,1)S(1)} %get-tuple-element.189), channel_id=1, source_target_pairs={{0,2},{1,3},{2,0},{3,1},{4,6},{5,7},{6,4},{7,5},{8,10},{9,11},{10,... | collective-permute-start | bytes 786440 | tf_op jit(solution)/shard_map/ppermute | solution.py:35
  234.1 15.9 %collective-permute-start.64 = (bf16[192,1024]{1,0:T(8,128)(2,1)S(1)}, bf16[192,1024]{1,0:T(8,128)(2,1)S(1)}, u32[]{:S(2)}, u32[]{:S(2)}) collective-permute-start(bf16[192,1024]{1,0:T(8,128)(2,1)S(1)} %pad_maximum_fusion.10), channel_id=1, source_target_pairs={{0,2},{1,3},{2,0},{3,1},{4,6},{5,7},{6,4},{7,5},{8,10},{9,11},{10,... | collective-permute-start | bytes 1179656 | tf_op jit(solution)/shard_map/ppermute | solution.py:35
  243.9 11.0 %collective-permute-start.67 = (bf16[192,1024]{1,0:T(8,128)(2,1)S(1)}, bf16[192,1024]{1,0:T(8,128)(2,1)S(1)}, u32[]{:S(2)}, u32[]{:S(2)}) collective-permute-start(bf16[192,1024]{1,0:T(8,128)(2,1)S(1)} %pad_maximum_fusion.11), channel_id=1, source_target_pairs={{0,1},{1,0},{2,3},{3,2},{4,5},{5,4},{6,7},{7,6},{8,9},{9,8},{10,11... | collective-permute-start | bytes 1179656 | tf_op jit(solution)/shard_map/ppermute | solution.py:35
  245.4 19.3 %collective-permute-start.50 = (bf16[128,2048]{1,0:T(8,128)(2,1)S(1)}, bf16[128,2048]{1,0:T(8,128)(2,1)S(1)}, u32[]{:S(2)}, u32[]{:S(2)}) collective-permute-start(bf16[128,2048]{1,0:T(8,128)(2,1)S(1)} %gather.5), channel_id=1, source_target_pairs={{0,24},{4,28},{8,16},{12,20},{16,8},{20,12},{24,0},{28,4},{1,25},{... | collective-permute-start | bytes 1572872 | tf_op jit(solution)/shard_map/ppermute | solution.py:35
  247.7 24.5 %collective-permute-start.60 = (bf16[128,2048]{1,0:T(8,128)(2,1)S(1)}, bf16[128,2048]{1,0:T(8,128)(2,1)S(1)}, u32[]{:S(2)}, u32[]{:S(2)}) collective-permute-start(bf16[128,2048]{1,0:T(8,128)(2,1)S(1)} %gather.6), channel_id=1, source_target_pairs={{0,8},{4,12},{8,0},{12,4},{16,24},{20,28},{24,16},{28,20},{1,9},{5... | collective-permute-start | bytes 1572872 | tf_op jit(solution)/shard_map/ppermute | solution.py:35
  (42 other events, 393.7 us)
Sparse Core Ops, SparseCore 0:
  24.1 29.0 all-gather.1

commit v7 on v6

--- a/solution.py
+++ b/solution.py
@@ -72,8 +72,8 @@
 
 
 def own_rows_kernel(experts, heads_dev, place, *refs):
-    peers = len(refs) - 20
-    sources, outs, table, targets, sems = refs[:9], refs[9:-11], refs[-11], refs[-10:-1], refs[-1]
+    peers = len(refs) - 19
+    sources, outs, targets, sems = refs[:9], refs[9:-10], refs[-10:-1], refs[-1]
     copies = load_all(list(zip(sources, targets)), sems)
     ids, shares, tokens, gain, key_weight, value_weight, k_gain, cosine, sine = targets
     copies[0].wait()
@@ -98,8 +98,9 @@
     ]
     slots = jnp.concatenate(slots, axis=0)
     left = jnp.concatenate([chosen_ids, shares[...]], axis=0).astype(jnp.float32)
-    table[:, :rows] = left.astype(jnp.bfloat16)
-    table[:, rows:] = jnp.concatenate([slots, jnp.zeros_like(slots)], axis=0).astype(jnp.bfloat16)
+    right = jnp.concatenate([slots, jnp.zeros_like(slots)], axis=0)
+    for out in outs:
+        out[rows:, :] = jnp.concatenate([left, right], axis=1).astype(jnp.bfloat16)
     for copy in copies[2:]:
         copy.wait()
     normed = rms_scale(tokens[...].astype(jnp.float32), gain[...]).astype(jnp.bfloat16)
@@ -115,7 +116,7 @@
 
             @pl.when(asked == head)
             def _(out=outs[distance], pair=pair):
-                out[...] = pair
+                out[:rows, :] = pair
 
 
 def query_kernel(*refs):
@@ -138,7 +139,7 @@
     heads = w_out.shape[0] // HEAD_SIZE
     width = heads * rows
     span = rows * (place.shape[0] - 2)
-    stride = span + 2 * TOP
+    stride = span + 2 * TOP * (place.shape[0] - 2)
     scale = HEAD_SIZE ** (-0.5) * LOG2E
 
     def step(first, states, masked):
@@ -207,8 +208,8 @@
 
 
 def plane_targets(group, place, routing, near, away):
-    block, me, count = place[0], place[1], routing.shape[0]
-    table = routing[near, block ^ (2 * group)]
+    block, me, count = place[0], place[1], routing.shape[1]
+    table = routing[block ^ (2 * group), near]
     return [slot_targets(table, (block ^ core) * count + (me ^ away)) for core in (0, 1)]
 
 
@@ -268,23 +269,18 @@
                 kept[:, side * width : (side + 1) * width] = total
 
 
-def gather_kernel(kept, *refs):
+def gather_kernel(counts, kept, *refs):
     *parts, out = refs
-    width = parts[0].shape[1]
-    count = out.shape[1] // width
-    first = 0
-    for side, some in enumerate(split_parts(parts, count)):
-        cols = slice(first, first + width)
+    width = out.shape[1] // len(counts)
+    for side, count in enumerate(counts):
+        cols = slice(side * width, (side + 1) * width)
         total = kept[:, cols]
-        for part in some:
+        for part in parts[:count]:
             total = total + part[...].astype(jnp.float32)
+        parts = parts[count:]
+        for part in parts[sum(counts[side + 1 :]) :]:
+            total = total + part[:, cols].astype(jnp.float32)
         out[:, cols] = total.astype(out.dtype)
-        first += width
-
-
-def split_parts(parts, count):
-    assert count == 2
-    return parts[:1], parts[1:]
 
 
 def expert_kernel(routes, capacity, *refs):
@@ -391,9 +387,9 @@
         cosine,
         sine,
     ]
-    *own_kv, table = call(
+    own_kv = call(
         functools.partial(own_rows_kernel, experts, heads_dev),
-        [bf16((rows, 2 * HEAD_SIZE)) for _ in peers] + [bf16((2 * TOP, 2 * rows))],
+        [bf16((rows + 2 * TOP, 2 * HEAD_SIZE)) for _ in peers],
         [SMEM] + [ANY] * 9,
         place,
         *own_args,
@@ -402,11 +398,12 @@
         limit=60,
     )
     block_kv = [own_kv[0]] + [swap(own_kv[d], "exp", d) for d in peers[1:]]
-    both = lax.all_gather(jnp.concatenate(block_kv + [table], axis=0), "ctx", axis=0, tiled=True)
+    both = [part[:rows] for part in block_kv] + [part[rows:] for part in block_kv]
+    both = lax.all_gather(jnp.concatenate(both, axis=0), "ctx", axis=0, tiled=True)
     sent = tie(tokens, *block_kv[1:])
     pieces = [tokens] + [swap(sent, "exp", d) for d in peers[1:]]
-    routing = both.reshape(ctx_count, ctx_rows + 2 * TOP, 2 * HEAD_SIZE)[:, ctx_rows:]
-    routing = jnp.stack([routing] + [swap(routing, "exp", d) for d in peers[1:]], axis=0)
+    routing = both.reshape(ctx_count, -1, 2 * HEAD_SIZE)[:, ctx_rows:]
+    routing = routing.reshape(ctx_count, exp_count, 2 * TOP, 2 * HEAD_SIZE)
 
     positions = jnp.concatenate(
         [me_ctx * ctx_rows + (me_exp ^ d) * rows + jnp.arange(rows) for d in peers]
@@ -434,7 +431,7 @@
             [bf16((rows, width)) for _ in some],
             [SMEM, VMEM, VMEM, VMEM],
             place,
-            tie(asked, *last, *([routing] if last else [])),
+            tie(asked, *last),
             both,
             w_out,
             name="attention",
@@ -470,7 +467,7 @@
     half = width // 2
     far = [normed]
     for g in range(1, groups):
-        far.append(swap(tie(normed, *([far[g - 1]] if g > 2 else [])), "ctx", 2 * g))
+        far.append(swap(far[g & (g - 1)], "ctx", 2 * (g & -g)))
     in_flight = {}
 
     def send(array, d, kind):
@@ -518,8 +515,8 @@
         own, other = made[: len(came)], made[len(came) :]
         produced.append([(mine, swap(mates, "ctx", 1)) for mine, mates in zip(own, other)])
 
-    totals, hop = [], ()
-    for g in [*range(2, groups), *(g for g in (1, 0) if g < groups)]:
+    passing = [[] for _ in range(groups)]
+    for g in reversed(range(groups)):
         back, pieces = [], iter(produced[g])
         for _, away in routes:
             for a in away:
@@ -537,29 +534,26 @@
         )
         sums = [send(part, n, "whole") for part, n in zip(sums, onward)]
         total = call(
-            gather_kernel,
-            bf16((rows, width)),
-            [VMEM] * (1 + len(sums)),
+            functools.partial(gather_kernel, [len(near) - 1 for near, _ in routes]),
+            bf16((rows, width)) if g else jax.ShapeDtypeStruct((rows, width), jnp.float32),
+            [VMEM] * (1 + len(sums) + (len(passing[g]) if g else 0)),
             kept,
             *sums,
+            *(passing[g] if g else []),
             name="gather",
         )
         if g:
-            total = swap(tie(total, *(hop if g > 1 else ())), "ctx", 2 * g)
-            hop = (total,)
-        totals.append(total)
+            passing[g & (g - 1)].append(swap(total, "ctx", 2 * (g & -g)))
     early = call(
         sum_kernel,
         jax.ShapeDtypeStruct((rows, width), jnp.float32),
-        [VMEM] * groups,
+        [VMEM] * (1 + len(passing[0])),
         residual,
-        *totals[:-1],
+        *passing[0],
         name="add",
         flops=10_000_000_000,
     )
-    return call(
-        sum_kernel, bf16((rows, width)), [VMEM] * 2, early, totals[-1], name="add"
-    )
+    return call(sum_kernel, bf16((rows, width)), [VMEM] * 2, early, total, name="add")
 
 
 def solution(mesh):

time: 280 us -> 264 us (0.943)
  starting transfers between devices: 78.7 us -> 63.1 us
    ppermute x70 -> x67, starting transfers between devices: 78.7 us -> 63.1 us  [swap(): return lax.ppermute(array, axis, pairs)]
    ppermute x70 -> x67, waiting for transfers between devices: 137 us -> 133 us  [swap(): return lax.ppermute(array, axis, pairs)]
    unnamed x38 -> x49, local copies, waits for them, and re-layouts: 4.84 us -> 6.38 us
  transfers between devices with their start and end apart: 71 -> 68, of which waited for: 35 -> 30; matrix products, arithmetic and copies ran while one was open for 1% -> 1% of each run, Pallas kernels for 11% -> 12%
where the time goes in v7:
time: 264 us; the launch traced here: 263 us
  waiting for transfers between devices  137 us (52%)
  starting transfers between devices  63.1 us (24%)
  Pallas kernels  39.6 us (15%)
  between operations  14.1 us (5%)
  local copies, waits for them, and re-layouts  6.77 us (3%)
  other arithmetic  3.06 us (1%)
    ppermute x67, waiting for transfers between devices, swap(): return lax.ppermute(array, axis, pairs)  133 us
    ppermute x67, starting transfers between devices, swap(): return lax.ppermute(array, axis, pairs)  63.1 us
    pallas_call x27, Pallas kernels, call(): pl.pallas_call(kernel, out_shape=out_shape, in_specs=specs, out_specs=jax...  39.6 us
    unnamed x49, local copies, waits for them, and re-layouts  6.38 us
  transfers between devices with their start and end apart: 68, of which 30 were waited for; matrix products, arithmetic and copies ran while one was open for 1% of the time, Pallas kernels for 12%

profile of v7, /device:TPU:0, one launch (start us, length us, event | category | flops | bytes accessed | tf_op | source)
XLA Modules:
  0.0 263.5 jit_solution(385167061978966383)
XLA Ops:
  8.2 4.5 %own_rows.1 = (bf16[144,256]{1,0:T(8,128)(2,1)}, bf16[144,256]{1,0:T(8,128)(2,1)}, bf16[144,256]{1,0:T(8,128)(2,1)}, bf16[144,256]{1,0:T(8,128)(2,1)}) custom-call(s32[6]{0:T(128)} %pad_add_fusion.place, s32[8,128]{1,0:T(8,128)} %bitcast.38, s32[8,128]{1,0:T(8,128)} %bitcast.39, bf16[128,2048]{1,0:T(8,128)(2,1)} %tokens.1, f32[1,2048]{1,0:T(1,128)} %bitcast.34, ...), custom_call_target="tpu_custom_call" | custom-call | flops 1000 | bytes 1000 | tf_op jit(solution)/shard_map/own_rows/pallas_call | solution.py:333
  12.7 3.0 %collective-permute-start = (bf16[144,256]{1,0:T(8,128)(2,1)}, bf16[144,256]{1,0:T(8,128)(2,1)S(1)}, u32[]{:S(2)}, u32[]{:S(2)}) collective-permute-start(bf16[144,256]{1,0:T(8,128)(2,1)} %get-tuple-element.103), channel_id=1, source_target_pairs={{0,1},{1,0},{2,3},{3,2},{4,5},{5,4},{6,7},{7,6},{8,9},{9,8},{10,11... | collective-permute-start | bytes 221192 | tf_op jit(solution)/shard_map/ppermute | solution.py:35
  15.7 1.5 collective-permute-start.1
  18.5 1.7 collective-permute-done.1
  20.3 2.4 collective-permute-done.2
  25.2 2.5 collective-permute-start.5
  28.7 10.4 %collective-permute-done.3.refs_1_ = bf16[128,2048]{1,0:T(8,128)(2,1)S(1)} collective-permute-done((bf16[128,2048]{1,0:T(8,128)(2,1)S(1)}, bf16[128,2048]{1,0:T(8,128)(2,1)S(1)}, u32[]{:S(2)}, u32[]{:S(2)}) %collective-permute-start.3) | collective-permute-done | bytes 524320 | tf_op jit(solution)/shard_map/ppermute | solution.py:35
  39.0 9.1 %collective-permute-done.4.refs_2_ = bf16[128,2048]{1,0:T(8,128)(2,1)S(1)} collective-permute-done((bf16[128,2048]{1,0:T(8,128)(2,1)S(1)}, bf16[128,2048]{1,0:T(8,128)(2,1)S(1)}, u32[]{:S(2)}, u32[]{:S(2)}) %collective-permute-start.4) | collective-permute-done | bytes 524320 | tf_op jit(solution)/shard_map/ppermute | solution.py:35
  48.1 1.6 copy-done.7
  49.8 1.8 queries.1
  51.7 3.6 %all-gather.2.cloned.1.call-done.both = bf16[4608,256]{1,0:T(8,128)(2,1)} async-done(((bf16[576,256]{1,0:T(8,128)(2,1)}), bf16[4608,256]{1,0:T(8,128)(2,1)}) %all-gather.2.cloned.1.call-update) | async-done | bytes 2359312 | tf_op jit(solution)/shard_map/all_gather | solution.py:402
  55.3 1.7 copy-done.3
  56.9 1.7 attention.4
  58.6 2.4 collective-permute-start.6
  61.1 1.7 attention.5
  63.4 1.7 attention.6
  65.8 1.9 attention.7.refs_0_
  67.7 6.8 %collective-permute-done.6.refs_1_ = bf16[128,2048]{1,0:T(8,128)(2,1)S(1)} collective-permute-done((bf16[128,2048]{1,0:T(8,128)(2,1)S(1)}, bf16[128,2048]{1,0:T(8,128)(2,1)S(1)}, u32[]{:S(2)}, u32[]{:S(2)}) %collective-permute-start.6) | collective-permute-done | bytes 524320 | tf_op jit(solution)/shard_map/ppermute | solution.py:35
  74.6 11.0 %collective-permute-done.7.refs_1_ = bf16[128,2048]{1,0:T(8,128)(2,1)S(1)} collective-permute-done((bf16[128,2048]{1,0:T(8,128)(2,1)S(1)}, bf16[128,2048]{1,0:T(8,128)(2,1)S(1)}, u32[]{:S(2)}, u32[]{:S(2)}) %collective-permute-start.7) | collective-permute-done | bytes 524320 | tf_op jit(solution)/shard_map/ppermute | solution.py:35
  86.2 2.5 collective-permute-start.10
  88.8 1.5 collective-permute-start.11
  91.5 5.2 %collective-permute-start.9 = (bf16[128,2048]{1,0:T(8,128)(2,1)S(1)}, bf16[128,2048]{1,0:T(8,128)(2,1)S(1)}, u32[]{:S(2)}, u32[]{:S(2)}) collective-permute-start(bf16[128,2048]{1,0:T(8,128)(2,1)S(1)} %get-tuple-element.112), channel_id=1, source_target_pairs={{0,16},{4,20},{8,24},{12,28},{16,0},{20,4},{24,8},{28,12},{1,17},{... | collective-permute-start | bytes 1572872 | tf_op jit(solution)/shard_map/ppermute | solution.py:35
  101.0 9.4 %collective-permute-done.10 = bf16[128,2048]{1,0:T(8,128)(2,1)S(1)} collective-permute-done((bf16[128,2048]{1,0:T(8,128)(2,1)S(1)}, bf16[128,2048]{1,0:T(8,128)(2,1)S(1)}, u32[]{:S(2)}, u32[]{:S(2)}) %collective-permute-start.10) | collective-permute-done | bytes 524320 | tf_op jit(solution)/shard_map/ppermute | solution.py:35
  110.4 2.4 collective-permute-start.12
  113.1 6.7 %collective-permute-done.9 = bf16[128,2048]{1,0:T(8,128)(2,1)S(1)} collective-permute-done((bf16[128,2048]{1,0:T(8,128)(2,1)S(1)}, bf16[128,2048]{1,0:T(8,128)(2,1)S(1)}, u32[]{:S(2)}, u32[]{:S(2)}) %collective-permute-start.9) | collective-permute-done | bytes 524320 | tf_op jit(solution)/shard_map/ppermute | solution.py:35
  123.1 1.5 collective-permute-start.13
  125.7 12.4 %collective-permute-done.13.refs_1_ = bf16[128,1024]{1,0:T(8,128)(2,1)S(1)} collective-permute-done((bf16[128,1024]{1,0:T(8,128)(2,1)S(1)}, bf16[128,1024]{1,0:T(8,128)(2,1)S(1)}, u32[]{:S(2)}, u32[]{:S(2)}) %collective-permute-start.13) | collective-permute-done | bytes 262176 | tf_op jit(solution)/shard_map/ppermute | solution.py:35
  143.5 10.8 %collective-permute-done.27.refs_1_ = bf16[128,1024]{1,0:T(8,128)(2,1)S(1)} collective-permute-done((bf16[128,1024]{1,0:T(8,128)(2,1)S(1)}, bf16[128,1024]{1,0:T(8,128)(2,1)S(1)}, u32[]{:S(2)}, u32[]{:S(2)}) %collective-permute-start.27) | collective-permute-done | bytes 262176 | tf_op jit(solution)/shard_map/ppermute | solution.py:35
  157.5 5.8 %collective-permute-done.30.refs_3_ = bf16[192,1024]{1,0:T(8,128)(2,1)S(1)} collective-permute-done((bf16[192,1024]{1,0:T(8,128)(2,1)S(1)}, bf16[192,1024]{1,0:T(8,128)(2,1)S(1)}, u32[]{:S(2)}, u32[]{:S(2)}) %collective-permute-start.30) | collective-permute-done | bytes 393248 | tf_op jit(solution)/shard_map/ppermute | solution.py:35
  167.0 3.8 %expert.5 = (bf16[96,1024]{1,0:T(8,128)(2,1)S(1)}, bf16[96,1024]{1,0:T(8,128)(2,1)S(1)}, bf16[96,1024]{1,0:T(8,128)(2,1)S(1)}, bf16[96,1024]{1,0:T(8,128)(2,1)S(...) custom-call(bf16[192,1024]{1,0:T(8,128)(2,1)S(1)} %get-tuple-element, ...), custom_call_target="tpu_custom_call" | custom-call | flops 1000 | bytes 1000 | tf_op jit(solution)/shard_map/expert/pallas_call | solution.py:333
  172.4 1.5 collective-permute-start.33
  173.9 3.8 %expert.4 = (bf16[96,1024]{1,0:T(8,128)(2,1)S(1)}, bf16[96,1024]{1,0:T(8,128)(2,1)S(1)}, bf16[96,1024]{1,0:T(8,128)(2,1)S(1)}, bf16[96,1024]{1,0:T(8,128)(2,1)S(...) custom-call(bf16[192,1024]{1,0:T(8,128)(2,1)S(1)} %get-tuple-element, ...), custom_call_target="tpu_custom_call" | custom-call | flops 1000 | bytes 1000 | tf_op jit(solution)/shard_map/expert/pallas_call | solution.py:333
  178.0 1.5 collective-permute-start.38
  179.7 4.2 %collective-permute-done.33.refs_2_ = bf16[192,1024]{1,0:T(8,128)(2,1)S(1)} collective-permute-done((bf16[192,1024]{1,0:T(8,128)(2,1)S(1)}, bf16[192,1024]{1,0:T(8,128)(2,1)S(1)}, u32[]{:S(2)}, u32[]{:S(2)}) %collective-permute-start.33) | collective-permute-done | bytes 393248 | tf_op jit(solution)/shard_map/ppermute | solution.py:35
  185.4 4.1 %collective-permute-done.38.refs_5_ = bf16[192,1024]{1,0:T(8,128)(2,1)S(1)} collective-permute-done((bf16[192,1024]{1,0:T(8,128)(2,1)S(1)}, bf16[192,1024]{1,0:T(8,128)(2,1)S(1)}, u32[]{:S(2)}, u32[]{:S(2)}) %collective-permute-start.38) | collective-permute-done | bytes 393248 | tf_op jit(solution)/shard_map/ppermute | solution.py:35
  189.5 1.5 collective-permute-start.39
  191.1 4.1 %expert.6 = (bf16[96,1024]{1,0:T(8,128)(2,1)S(1)}, bf16[96,1024]{1,0:T(8,128)(2,1)S(1)}, bf16[96,1024]{1,0:T(8,128)(2,1)S(1)}, bf16[96,1024]{1,0:T(8,128)(2,1)S(...) custom-call(bf16[192,1024]{1,0:T(8,128)(2,1)S(1)} %get-tuple-element, ...), custom_call_target="tpu_custom_call" | custom-call | flops 1000 | bytes 1000 | tf_op jit(solution)/shard_map/expert/pallas_call | solution.py:333
  198.7 2.9 %collective-permute-done.39.refs_5_ = bf16[192,1024]{1,0:T(8,128)(2,1)S(1)} collective-permute-done((bf16[192,1024]{1,0:T(8,128)(2,1)S(1)}, bf16[192,1024]{1,0:T(8,128)(2,1)S(1)}, u32[]{:S(2)}, u32[]{:S(2)}) %collective-permute-start.39) | collective-permute-done | bytes 393248 | tf_op jit(solution)/shard_map/ppermute | solution.py:35
  203.6 3.5 %collective-permute-done.42.refs_0_ = bf16[128,1024]{1,0:T(8,128)(2,1)S(1)} collective-permute-done((bf16[128,1024]{1,0:T(8,128)(2,1)S(1)}, bf16[128,1024]{1,0:T(8,128)(2,1)S(1)}, u32[]{:S(2)}, u32[]{:S(2)}) %collective-permute-start.42) | collective-permute-done | bytes 262176 | tf_op jit(solution)/shard_map/ppermute | solution.py:35
  207.8 1.5 collective-permute-start.46
  212.4 3.8 %expert.7 = (bf16[96,1024]{1,0:T(8,128)(2,1)S(1)}, bf16[96,1024]{1,0:T(8,128)(2,1)S(1)}, bf16[96,1024]{1,0:T(8,128)(2,1)S(1)}, bf16[96,1024]{1,0:T(8,128)(2,1)S(...) custom-call(bf16[192,1024]{1,0:T(8,128)(2,1)S(1)} %get-tuple-element, ...), custom_call_target="tpu_custom_call" | custom-call | flops 1000 | bytes 1000 | tf_op jit(solution)/shard_map/expert/pallas_call | solution.py:333
  217.9 2.9 %collective-permute-done.43.refs_0_ = bf16[128,1024]{1,0:T(8,128)(2,1)S(1)} collective-permute-done((bf16[128,1024]{1,0:T(8,128)(2,1)S(1)}, bf16[128,1024]{1,0:T(8,128)(2,1)S(1)}, u32[]{:S(2)}, u32[]{:S(2)}) %collective-permute-start.43) | collective-permute-done | bytes 262176 | tf_op jit(solution)/shard_map/ppermute | solution.py:35
  222.9 1.5 collective-permute-start.61
  225.2 4.7 %collective-permute-done.55.refs_0_ = bf16[128,1024]{1,0:T(8,128)(2,1)S(1)} collective-permute-done((bf16[128,1024]{1,0:T(8,128)(2,1)S(1)}, bf16[128,1024]{1,0:T(8,128)(2,1)S(1)}, u32[]{:S(2)}, u32[]{:S(2)}) %collective-permute-start.55) | collective-permute-done | bytes 262176 | tf_op jit(solution)/shard_map/ppermute | solution.py:35
  229.9 2.4 collective-permute-start.47
  234.5 4.6 %collective-permute-done.61.refs_2_ = bf16[192,1024]{1,0:T(8,128)(2,1)S(1)} collective-permute-done((bf16[192,1024]{1,0:T(8,128)(2,1)S(1)}, bf16[192,1024]{1,0:T(8,128)(2,1)S(1)}, u32[]{:S(2)}, u32[]{:S(2)}) %collective-permute-start.61) | collective-permute-done | bytes 393248 | tf_op jit(solution)/shard_map/ppermute | solution.py:35
  241.4 6.4 %collective-permute-done.65.refs_0_ = bf16[128,1024]{1,0:T(8,128)(2,1)S(1)} collective-permute-done((bf16[128,1024]{1,0:T(8,128)(2,1)S(1)}, bf16[128,1024]{1,0:T(8,128)(2,1)S(1)}, u32[]{:S(2)}, u32[]{:S(2)}) %collective-permute-start.65) | collective-permute-done | bytes 262176 | tf_op jit(solution)/shard_map/ppermute | solution.py:35
  248.3 7.0 %collective-permute-done.47.refs_1_ = bf16[128,2048]{1,0:T(8,128)(2,1)S(1)} collective-permute-done((bf16[128,2048]{1,0:T(8,128)(2,1)S(1)}, bf16[128,2048]{1,0:T(8,128)(2,1)S(1)}, u32[]{:S(2)}, u32[]{:S(2)}) %collective-permute-start.47) | collective-permute-done | bytes 524320 | tf_op jit(solution)/shard_map/ppermute | solution.py:35
  (213 shorter events, 54.1 us)
Async XLA Ops:
  6.5 48.7 %all-gather.2.cloned.1.call-start = ((), (), s32[]{:S(2)}) async-start(), calls=%async_computation | async-start | bytes 2654208 | tf_op jit(solution)/shard_map/all_gather | solution.py:402
  24.1 14.9 %collective-permute-start.3 = (bf16[128,2048]{1,0:T(8,128)(2,1)S(1)}, bf16[128,2048]{1,0:T(8,128)(2,1)S(1)}, u32[]{:S(2)}, u32[]{:S(2)}) collective-permute-start(bf16[128,2048]{1,0:T(8,128)(2,1)S(1)} %copy-done.6), channel_id=1, source_target_pairs={{0,1},{1,0},{2,3},{3,2},{4,5},{5,4},{6,7},{7,6},{8,9},{9,8},{10,11... | collective-permute-start | bytes 1572872 | tf_op jit(solution)/shard_map/ppermute | solution.py:35
  24.7 23.4 %collective-permute-start.4 = (bf16[128,2048]{1,0:T(8,128)(2,1)S(1)}, bf16[128,2048]{1,0:T(8,128)(2,1)S(1)}, u32[]{:S(2)}, u32[]{:S(2)}) collective-permute-start(bf16[128,2048]{1,0:T(8,128)(2,1)S(1)} %copy-done.6), channel_id=1, source_target_pairs={{0,2},{1,3},{2,0},{3,1},{4,6},{5,7},{6,4},{7,5},{8,10},{9,11},{10,... | collective-permute-start | bytes 1572872 | tf_op jit(solution)/shard_map/ppermute | solution.py:35
  25.2 22.9 %collective-permute-start.5 = (bf16[128,2048]{1,0:T(8,128)(2,1)S(1)}, bf16[128,2048]{1,0:T(8,128)(2,1)S(1)}, u32[]{:S(2)}, u32[]{:S(2)}) collective-permute-start(bf16[128,2048]{1,0:T(8,128)(2,1)S(1)} %copy-done.6), channel_id=1, source_target_pairs={{0,3},{1,2},{2,1},{3,0},{4,7},{5,6},{6,5},{7,4},{8,11},{9,10},{10,... | collective-permute-start | bytes 1572872 | tf_op jit(solution)/shard_map/ppermute | solution.py:35
  58.6 15.9 %collective-permute-start.6 = (bf16[128,2048]{1,0:T(8,128)(2,1)S(1)}, bf16[128,2048]{1,0:T(8,128)(2,1)S(1)}, u32[]{:S(2)}, u32[]{:S(2)}) collective-permute-start(bf16[128,2048]{1,0:T(8,128)(2,1)S(1)} %attention.4), channel_id=1, source_target_pairs={{0,3},{1,2},{2,1},{3,0},{4,7},{5,6},{6,5},{7,4},{8,11},{9,10},{10,... | collective-permute-start | bytes 1572872 | tf_op jit(solution)/shard_map/ppermute | solution.py:35
  62.8 22.9 %collective-permute-start.7 = (bf16[128,2048]{1,0:T(8,128)(2,1)S(1)}, bf16[128,2048]{1,0:T(8,128)(2,1)S(1)}, u32[]{:S(2)}, u32[]{:S(2)}) collective-permute-start(bf16[128,2048]{1,0:T(8,128)(2,1)S(1)} %attention.5), channel_id=1, source_target_pairs={{0,1},{1,0},{2,3},{3,2},{4,5},{5,4},{6,7},{7,6},{8,9},{9,8},{10,11... | collective-permute-start | bytes 1572872 | tf_op jit(solution)/shard_map/ppermute | solution.py:35
  65.1 20.7 %collective-permute-start.8 = (bf16[128,2048]{1,0:T(8,128)(2,1)S(1)}, bf16[128,2048]{1,0:T(8,128)(2,1)S(1)}, u32[]{:S(2)}, u32[]{:S(2)}) collective-permute-start(bf16[128,2048]{1,0:T(8,128)(2,1)S(1)} %attention.6), channel_id=1, source_target_pairs={{0,2},{1,3},{2,0},{3,1},{4,6},{5,7},{6,4},{7,5},{8,10},{9,11},{10,... | collective-permute-start | bytes 1572872 | tf_op jit(solution)/shard_map/ppermute | solution.py:35
  86.2 24.2 %collective-permute-start.10 = (bf16[128,2048]{1,0:T(8,128)(2,1)S(1)}, bf16[128,2048]{1,0:T(8,128)(2,1)S(1)}, u32[]{:S(2)}, u32[]{:S(2)}) collective-permute-start(bf16[128,2048]{1,0:T(8,128)(2,1)S(1)} %get-tuple-element.112), channel_id=1, source_target_pairs={{0,8},{4,12},{8,0},{12,4},{16,24},{20,28},{24,16},{28,20},{1,9},{5... | collective-permute-start | bytes 1572872 | tf_op jit(solution)/shard_map/ppermute | solution.py:35
  88.8 8.1 %collective-permute-start.11 = (bf16[128,1024]{1,0:T(8,128)(2,1)S(1)}, bf16[128,1024]{1,0:T(8,128)(2,1)S(1)}, u32[]{:S(2)}, u32[]{:S(2)}) collective-permute-start(bf16[128,1024]{1,0:T(8,128)(2,1)S(1)} %get-tuple-element.204.refs_0_), channel_id=1, source_target_pairs={{0,1},{1,0},{2,3},{3,2},{4,5},{5,4},{6,7},{7,6},{8,9},{9,8},{10,11... | collective-permute-start | bytes 786440 | tf_op jit(solution)/shard_map/ppermute | solution.py:35
  90.3 7.8 %collective-permute-start.14 = (bf16[128,1024]{1,0:T(8,128)(2,1)S(1)}, bf16[128,1024]{1,0:T(8,128)(2,1)S(1)}, u32[]{:S(2)}, u32[]{:S(2)}) collective-permute-start(bf16[128,1024]{1,0:T(8,128)(2,1)S(1)} %get-tuple-element.203.refs_2_), channel_id=1, source_target_pairs={{0,2},{1,3},{2,0},{3,1},{4,6},{5,7},{6,4},{7,5},{8,10},{9,11},{10,... | collective-permute-start | bytes 786440 | tf_op jit(solution)/shard_map/ppermute | solution.py:35
  91.5 28.4 %collective-permute-start.9 = (bf16[128,2048]{1,0:T(8,128)(2,1)S(1)}, bf16[128,2048]{1,0:T(8,128)(2,1)S(1)}, u32[]{:S(2)}, u32[]{:S(2)}) collective-permute-start(bf16[128,2048]{1,0:T(8,128)(2,1)S(1)} %get-tuple-element.112), channel_id=1, source_target_pairs={{0,16},{4,20},{8,24},{12,28},{16,0},{20,4},{24,8},{28,12},{1,17},{... | collective-permute-start | bytes 1572872 | tf_op jit(solution)/shard_map/ppermute | solution.py:35
  99.2 22.3 %collective-permute-start.17 = (bf16[192,1024]{1,0:T(8,128)(2,1)S(1)}, bf16[192,1024]{1,0:T(8,128)(2,1)S(1)}, u32[]{:S(2)}, u32[]{:S(2)}) collective-permute-start(bf16[192,1024]{1,0:T(8,128)(2,1)S(1)} %get-tuple-element.120), channel_id=1, source_target_pairs={{0,2},{1,3},{2,0},{3,1},{4,6},{5,7},{6,4},{7,5},{8,10},{9,11},{10,... | collective-permute-start | bytes 1179656 | tf_op jit(solution)/shard_map/ppermute | solution.py:35
  100.4 22.1 %collective-permute-start.20 = (bf16[192,1024]{1,0:T(8,128)(2,1)S(1)}, bf16[192,1024]{1,0:T(8,128)(2,1)S(1)}, u32[]{:S(2)}, u32[]{:S(2)}) collective-permute-start(bf16[192,1024]{1,0:T(8,128)(2,1)S(1)} %get-tuple-element.126), channel_id=1, source_target_pairs={{0,1},{1,0},{2,3},{3,2},{4,5},{5,4},{6,7},{7,6},{8,9},{9,8},{10,11... | collective-permute-start | bytes 1179656 | tf_op jit(solution)/shard_map/ppermute | solution.py:35
  110.4 9.4 %collective-permute-start.12 = (bf16[128,1024]{1,0:T(8,128)(2,1)S(1)}, bf16[128,1024]{1,0:T(8,128)(2,1)S(1)}, u32[]{:S(2)}, u32[]{:S(2)}) collective-permute-start(bf16[128,1024]{1,0:T(8,128)(2,1)S(1)} %get-tuple-element.113.refs_0_), channel_id=1, source_target_pairs={{0,1},{1,0},{2,3},{3,2},{4,5},{5,4},{6,7},{7,6},{8,9},{9,8},{10,11... | collective-permute-start | bytes 786440 | tf_op jit(solution)/shard_map/ppermute | solution.py:35
  119.9 20.7 %collective-permute-start.26 = (bf16[128,2048]{1,0:T(8,128)(2,1)S(1)}, bf16[128,2048]{1,0:T(8,128)(2,1)S(1)}, u32[]{:S(2)}, u32[]{:S(2)}) collective-permute-start(bf16[128,2048]{1,0:T(8,128)(2,1)S(1)} %collective-permute-done.9), channel_id=1, source_target_pairs={{0,8},{4,12},{8,0},{12,4},{16,24},{20,28},{24,16},{28,20},{1,9},{5... | collective-permute-start | bytes 1572872 | tf_op jit(solution)/shard_map/ppermute | solution.py:35
  121.5 17.8 %collective-permute-start.18 = (bf16[192,1024]{1,0:T(8,128)(2,1)S(1)}, bf16[192,1024]{1,0:T(8,128)(2,1)S(1)}, u32[]{:S(2)}, u32[]{:S(2)}) collective-permute-start(bf16[192,1024]{1,0:T(8,128)(2,1)S(1)} %get-tuple-element.121), channel_id=1, source_target_pairs={{0,2},{1,3},{2,0},{3,1},{4,6},{5,7},{6,4},{7,5},{8,10},{9,11},{10,... | collective-permute-start | bytes 1179656 | tf_op jit(solution)/shard_map/ppermute | solution.py:35
  122.5 17.3 %collective-permute-start.21 = (bf16[192,1024]{1,0:T(8,128)(2,1)S(1)}, bf16[192,1024]{1,0:T(8,128)(2,1)S(1)}, u32[]{:S(2)}, u32[]{:S(2)}) collective-permute-start(bf16[192,1024]{1,0:T(8,128)(2,1)S(1)} %get-tuple-element.127), channel_id=1, source_target_pairs={{0,1},{1,0},{2,3},{3,2},{4,5},{5,4},{6,7},{7,6},{8,9},{9,8},{10,11... | collective-permute-start | bytes 1179656 | tf_op jit(solution)/shard_map/ppermute | solution.py:35
  123.1 15.0 %collective-permute-start.13 = (bf16[128,1024]{1,0:T(8,128)(2,1)S(1)}, bf16[128,1024]{1,0:T(8,128)(2,1)S(1)}, u32[]{:S(2)}, u32[]{:S(2)}) collective-permute-start(bf16[128,1024]{1,0:T(8,128)(2,1)S(1)} %get-tuple-element.114.refs_0_), channel_id=1, source_target_pairs={{0,1},{1,0},{2,3},{3,2},{4,5},{5,4},{6,7},{7,6},{8,9},{9,8},{10,11... | collective-permute-start | bytes 786440 | tf_op jit(solution)/shard_map/ppermute | solution.py:35
  124.7 13.4 %collective-permute-start.16 = (bf16[128,1024]{1,0:T(8,128)(2,1)S(1)}, bf16[128,1024]{1,0:T(8,128)(2,1)S(1)}, u32[]{:S(2)}, u32[]{:S(2)}) collective-permute-start(bf16[128,1024]{1,0:T(8,128)(2,1)S(1)} %get-tuple-element.116.refs_2_), channel_id=1, source_target_pairs={{0,2},{1,3},{2,0},{3,1},{4,6},{5,7},{6,4},{7,5},{8,10},{9,11},{10,... | collective-permute-start | bytes 786440 | tf_op jit(solution)/shard_map/ppermute | solution.py:35
  139.2 16.1 %collective-permute-start.19 = (bf16[192,1024]{1,0:T(8,128)(2,1)S(1)}, bf16[192,1024]{1,0:T(8,128)(2,1)S(1)}, u32[]{:S(2)}, u32[]{:S(2)}) collective-permute-start(bf16[192,1024]{1,0:T(8,128)(2,1)S(1)} %get-tuple-element.122), channel_id=1, source_target_pairs={{0,2},{1,3},{2,0},{3,1},{4,6},{5,7},{6,4},{7,5},{8,10},{9,11},{10,... | collective-permute-start | bytes 1179656 | tf_op jit(solution)/shard_map/ppermute | solution.py:35
  139.9 15.5 %collective-permute-start.22 = (bf16[192,1024]{1,0:T(8,128)(2,1)S(1)}, bf16[192,1024]{1,0:T(8,128)(2,1)S(1)}, u32[]{:S(2)}, u32[]{:S(2)}) collective-permute-start(bf16[192,1024]{1,0:T(8,128)(2,1)S(1)} %get-tuple-element.128), channel_id=1, source_target_pairs={{0,1},{1,0},{2,3},{3,2},{4,5},{5,4},{6,7},{7,6},{8,9},{9,8},{10,11... | collective-permute-start | bytes 1179656 | tf_op jit(solution)/shard_map/ppermute | solution.py:35
  140.6 13.6 %collective-permute-start.27 = (bf16[128,1024]{1,0:T(8,128)(2,1)S(1)}, bf16[128,1024]{1,0:T(8,128)(2,1)S(1)}, u32[]{:S(2)}, u32[]{:S(2)}) collective-permute-start(bf16[128,1024]{1,0:T(8,128)(2,1)S(1)} %get-tuple-element.133.refs_0_), channel_id=1, source_target_pairs={{0,1},{1,0},{2,3},{3,2},{4,5},{5,4},{6,7},{7,6},{8,9},{9,8},{10,11... | collective-permute-start | bytes 786440 | tf_op jit(solution)/shard_map/ppermute | solution.py:35
  142.0 12.2 %collective-permute-start.28 = (bf16[128,1024]{1,0:T(8,128)(2,1)S(1)}, bf16[128,1024]{1,0:T(8,128)(2,1)S(1)}, u32[]{:S(2)}, u32[]{:S(2)}) collective-permute-start(bf16[128,1024]{1,0:T(8,128)(2,1)S(1)} %get-tuple-element.134.refs_2_), channel_id=1, source_target_pairs={{0,2},{1,3},{2,0},{3,1},{4,6},{5,7},{6,4},{7,5},{8,10},{9,11},{10,... | collective-permute-start | bytes 786440 | tf_op jit(solution)/shard_map/ppermute | solution.py:35
  155.4 7.9 %collective-permute-start.30 = (bf16[192,1024]{1,0:T(8,128)(2,1)S(1)}, bf16[192,1024]{1,0:T(8,128)(2,1)S(1)}, u32[]{:S(2)}, u32[]{:S(2)}) collective-permute-start(bf16[192,1024]{1,0:T(8,128)(2,1)S(1)} %get-tuple-element.140), channel_id=1, source_target_pairs={{0,1},{1,0},{2,3},{3,2},{4,5},{5,4},{6,7},{7,6},{8,9},{9,8},{10,11... | collective-permute-start | bytes 1179656 | tf_op jit(solution)/shard_map/ppermute | solution.py:35
  156.0 7.8 %collective-permute-start.29 = (bf16[192,1024]{1,0:T(8,128)(2,1)S(1)}, bf16[192,1024]{1,0:T(8,128)(2,1)S(1)}, u32[]{:S(2)}, u32[]{:S(2)}) collective-permute-start(bf16[192,1024]{1,0:T(8,128)(2,1)S(1)} %get-tuple-element.137), channel_id=1, source_target_pairs={{0,2},{1,3},{2,0},{3,1},{4,6},{5,7},{6,4},{7,5},{8,10},{9,11},{10,... | collective-permute-start | bytes 1179656 | tf_op jit(solution)/shard_map/ppermute | solution.py:35
  164.1 9.8 %collective-permute-start.23 = (bf16[384,1024]{1,0:T(8,128)(2,1)S(1)}, bf16[384,1024]{1,0:T(8,128)(2,1)S(1)}, u32[]{:S(2)}, u32[]{:S(2)}) collective-permute-start(bf16[384,1024]{1,0:T(8,128)(2,1)S(1)} %pad_maximum_fusion), channel_id=1, source_target_pairs={{0,4},{4,0},{8,12},{12,8},{16,20},{20,16},{24,28},{28,24},{1,5},{5... | collective-permute-start | bytes 2359304 | tf_op jit(solution)/shard_map/ppermute | solution.py:35
  171.4 18.2 %collective-permute-start.48 = (bf16[384,1024]{1,0:T(8,128)(2,1)S(1)}, bf16[384,1024]{1,0:T(8,128)(2,1)S(1)}, u32[]{:S(2)}, u32[]{:S(2)}) collective-permute-start(bf16[384,1024]{1,0:T(8,128)(2,1)S(1)} %pad_maximum_fusion.2), channel_id=1, source_target_pairs={{0,4},{4,0},{8,12},{12,8},{16,20},{20,16},{24,28},{28,24},{1,5},{5... | collective-permute-start | bytes 2359304 | tf_op jit(solution)/shard_map/ppermute | solution.py:35
  172.0 24.8 %collective-permute-start.58 = (bf16[384,1024]{1,0:T(8,128)(2,1)S(1)}, bf16[384,1024]{1,0:T(8,128)(2,1)S(1)}, u32[]{:S(2)}, u32[]{:S(2)}) collective-permute-start(bf16[384,1024]{1,0:T(8,128)(2,1)S(1)} %pad_maximum_fusion.3), channel_id=1, source_target_pairs={{0,4},{4,0},{8,12},{12,8},{16,20},{20,16},{24,28},{28,24},{1,5},{5... | collective-permute-start | bytes 2359304 | tf_op jit(solution)/shard_map/ppermute | solution.py:35
  172.4 11.5 %collective-permute-start.33 = (bf16[192,1024]{1,0:T(8,128)(2,1)S(1)}, bf16[192,1024]{1,0:T(8,128)(2,1)S(1)}, u32[]{:S(2)}, u32[]{:S(2)}) collective-permute-start(bf16[192,1024]{1,0:T(8,128)(2,1)S(1)} %pad_maximum_fusion.5), channel_id=1, source_target_pairs={{0,2},{1,3},{2,0},{3,1},{4,6},{5,7},{6,4},{7,5},{8,10},{9,11},{10,... | collective-permute-start | bytes 1179656 | tf_op jit(solution)/shard_map/ppermute | solution.py:35
  178.0 11.5 %collective-permute-start.38 = (bf16[192,1024]{1,0:T(8,128)(2,1)S(1)}, bf16[192,1024]{1,0:T(8,128)(2,1)S(1)}, u32[]{:S(2)}, u32[]{:S(2)}) collective-permute-start(bf16[192,1024]{1,0:T(8,128)(2,1)S(1)} %pad_maximum_fusion.7), channel_id=1, source_target_pairs={{0,1},{1,0},{2,3},{3,2},{4,5},{5,4},{6,7},{7,6},{8,9},{9,8},{10,11... | collective-permute-start | bytes 1179656 | tf_op jit(solution)/shard_map/ppermute | solution.py:35
  183.9 11.3 %collective-permute-start.40 = (bf16[96,1024]{1,0:T(8,128)(2,1)S(1)}, bf16[96,1024]{1,0:T(8,128)(2,1)S(1)}, u32[]{:S(2)}, u32[]{:S(2)}) collective-permute-start(bf16[96,1024]{1,0:T(8,128)(2,1)S(1)} %get-tuple-element.156), channel_id=1, source_target_pairs={{0,4},{4,0},{8,12},{12,8},{16,20},{20,16},{24,28},{28,24},{1,5},{5... | collective-permute-start | bytes 589832 | tf_op jit(solution)/shard_map/ppermute | solution.py:35
  183.9 14.1 %collective-permute-start.34 = (bf16[192,1024]{1,0:T(8,128)(2,1)S(1)}, bf16[192,1024]{1,0:T(8,128)(2,1)S(1)}, u32[]{:S(2)}, u32[]{:S(2)}) collective-permute-start(bf16[192,1024]{1,0:T(8,128)(2,1)S(1)} %pad_maximum_fusion.4), channel_id=1, source_target_pairs={{0,2},{1,3},{2,0},{3,1},{4,6},{5,7},{6,4},{7,5},{8,10},{9,11},{10,... | collective-permute-start | bytes 1179656 | tf_op jit(solution)/shard_map/ppermute | solution.py:35
  189.5 12.0 %collective-permute-start.39 = (bf16[192,1024]{1,0:T(8,128)(2,1)S(1)}, bf16[192,1024]{1,0:T(8,128)(2,1)S(1)}, u32[]{:S(2)}, u32[]{:S(2)}) collective-permute-start(bf16[192,1024]{1,0:T(8,128)(2,1)S(1)} %pad_maximum_fusion.6), channel_id=1, source_target_pairs={{0,1},{1,0},{2,3},{3,2},{4,5},{5,4},{6,7},{7,6},{8,9},{9,8},{10,11... | collective-permute-start | bytes 1179656 | tf_op jit(solution)/shard_map/ppermute | solution.py:35
  196.8 10.3 %collective-permute-start.42 = (bf16[128,1024]{1,0:T(8,128)(2,1)S(1)}, bf16[128,1024]{1,0:T(8,128)(2,1)S(1)}, u32[]{:S(2)}, u32[]{:S(2)}) collective-permute-start(bf16[128,1024]{1,0:T(8,128)(2,1)S(1)} %get-tuple-element.160), channel_id=1, source_target_pairs={{0,1},{1,0},{2,3},{3,2},{4,5},{5,4},{6,7},{7,6},{8,9},{9,8},{10,11... | collective-permute-start | bytes 786440 | tf_op jit(solution)/shard_map/ppermute | solution.py:35
  197.4 9.7 %collective-permute-start.44 = (bf16[128,1024]{1,0:T(8,128)(2,1)S(1)}, bf16[128,1024]{1,0:T(8,128)(2,1)S(1)}, u32[]{:S(2)}, u32[]{:S(2)}) collective-permute-start(bf16[128,1024]{1,0:T(8,128)(2,1)S(1)} %get-tuple-element.164), channel_id=1, source_target_pairs={{0,2},{1,3},{2,0},{3,1},{4,6},{5,7},{6,4},{7,5},{8,10},{9,11},{10,... | collective-permute-start | bytes 786440 | tf_op jit(solution)/shard_map/ppermute | solution.py:35
  198.1 9.7 %collective-permute-start.35 = (bf16[96,1024]{1,0:T(8,128)(2,1)S(1)}, bf16[96,1024]{1,0:T(8,128)(2,1)S(1)}, u32[]{:S(2)}, u32[]{:S(2)}) collective-permute-start(bf16[96,1024]{1,0:T(8,128)(2,1)S(1)} %get-tuple-element.146), channel_id=1, source_target_pairs={{0,4},{4,0},{8,12},{12,8},{16,20},{20,16},{24,28},{28,24},{1,5},{5... | collective-permute-start | bytes 589832 | tf_op jit(solution)/shard_map/ppermute | solution.py:35
  201.5 14.8 %collective-permute-start.51 = (bf16[192,1024]{1,0:T(8,128)(2,1)S(1)}, bf16[192,1024]{1,0:T(8,128)(2,1)S(1)}, u32[]{:S(2)}, u32[]{:S(2)}) collective-permute-start(bf16[192,1024]{1,0:T(8,128)(2,1)S(1)} %pad_maximum_fusion.8), channel_id=1, source_target_pairs={{0,2},{1,3},{2,0},{3,1},{4,6},{5,7},{6,4},{7,5},{8,10},{9,11},{10,... | collective-permute-start | bytes 1179656 | tf_op jit(solution)/shard_map/ppermute | solution.py:35
  202.2 14.2 %collective-permute-start.54 = (bf16[192,1024]{1,0:T(8,128)(2,1)S(1)}, bf16[192,1024]{1,0:T(8,128)(2,1)S(1)}, u32[]{:S(2)}, u32[]{:S(2)}) collective-permute-start(bf16[192,1024]{1,0:T(8,128)(2,1)S(1)} %pad_maximum_fusion.9), channel_id=1, source_target_pairs={{0,1},{1,0},{2,3},{3,2},{4,5},{5,4},{6,7},{7,6},{8,9},{9,8},{10,11... | collective-permute-start | bytes 1179656 | tf_op jit(solution)/shard_map/ppermute | solution.py:35
  207.8 16.7 %collective-permute-start.46 = (bf16[128,2048]{1,0:T(8,128)(2,1)S(1)}, bf16[128,2048]{1,0:T(8,128)(2,1)S(1)}, u32[]{:S(2)}, u32[]{:S(2)}) collective-permute-start(bf16[128,2048]{1,0:T(8,128)(2,1)S(1)} %gather.4), channel_id=1, source_target_pairs={{0,8},{4,12},{8,0},{12,4},{16,24},{20,28},{24,16},{28,20},{1,9},{5... | collective-permute-start | bytes 1572872 | tf_op jit(solution)/shard_map/ppermute | solution.py:35
  210.4 10.4 %collective-permute-start.43 = (bf16[128,1024]{1,0:T(8,128)(2,1)S(1)}, bf16[128,1024]{1,0:T(8,128)(2,1)S(1)}, u32[]{:S(2)}, u32[]{:S(2)}) collective-permute-start(bf16[128,1024]{1,0:T(8,128)(2,1)S(1)} %get-tuple-element.161), channel_id=1, source_target_pairs={{0,1},{1,0},{2,3},{3,2},{4,5},{5,4},{6,7},{7,6},{8,9},{9,8},{10,11... | collective-permute-start | bytes 786440 | tf_op jit(solution)/shard_map/ppermute | solution.py:35
  211.9 8.9 %collective-permute-start.45 = (bf16[128,1024]{1,0:T(8,128)(2,1)S(1)}, bf16[128,1024]{1,0:T(8,128)(2,1)S(1)}, u32[]{:S(2)}, u32[]{:S(2)}) collective-permute-start(bf16[128,1024]{1,0:T(8,128)(2,1)S(1)} %get-tuple-element.165), channel_id=1, source_target_pairs={{0,2},{1,3},{2,0},{3,1},{4,6},{5,7},{6,4},{7,5},{8,10},{9,11},{10,... | collective-permute-start | bytes 786440 | tf_op jit(solution)/shard_map/ppermute | solution.py:35
  220.8 12.3 %collective-permute-start.59 = (bf16[96,1024]{1,0:T(8,128)(2,1)S(1)}, bf16[96,1024]{1,0:T(8,128)(2,1)S(1)}, u32[]{:S(2)}, u32[]{:S(2)}) collective-permute-start(bf16[96,1024]{1,0:T(8,128)(2,1)S(1)} %get-tuple-element.187), channel_id=1, source_target_pairs={{0,4},{4,0},{8,12},{12,8},{16,20},{20,16},{24,28},{28,24},{1,5},{5... | collective-permute-start | bytes 589832 | tf_op jit(solution)/shard_map/ppermute | solution.py:35
  220.8 9.1 %collective-permute-start.55 = (bf16[128,1024]{1,0:T(8,128)(2,1)S(1)}, bf16[128,1024]{1,0:T(8,128)(2,1)S(1)}, u32[]{:S(2)}, u32[]{:S(2)}) collective-permute-start(bf16[128,1024]{1,0:T(8,128)(2,1)S(1)} %get-tuple-element.181), channel_id=1, source_target_pairs={{0,1},{1,0},{2,3},{3,2},{4,5},{5,4},{6,7},{7,6},{8,9},{9,8},{10,11... | collective-permute-start | bytes 786440 | tf_op jit(solution)/shard_map/ppermute | solution.py:35
  222.3 10.0 %collective-permute-start.56 = (bf16[128,1024]{1,0:T(8,128)(2,1)S(1)}, bf16[128,1024]{1,0:T(8,128)(2,1)S(1)}, u32[]{:S(2)}, u32[]{:S(2)}) collective-permute-start(bf16[128,1024]{1,0:T(8,128)(2,1)S(1)} %get-tuple-element.183), channel_id=1, source_target_pairs={{0,2},{1,3},{2,0},{3,1},{4,6},{5,7},{6,4},{7,5},{8,10},{9,11},{10,... | collective-permute-start | bytes 786440 | tf_op jit(solution)/shard_map/ppermute | solution.py:35
  222.9 16.2 %collective-permute-start.61 = (bf16[192,1024]{1,0:T(8,128)(2,1)S(1)}, bf16[192,1024]{1,0:T(8,128)(2,1)S(1)}, u32[]{:S(2)}, u32[]{:S(2)}) collective-permute-start(bf16[192,1024]{1,0:T(8,128)(2,1)S(1)} %pad_maximum_fusion.10), channel_id=1, source_target_pairs={{0,2},{1,3},{2,0},{3,1},{4,6},{5,7},{6,4},{7,5},{8,10},{9,11},{10,... | collective-permute-start | bytes 1179656 | tf_op jit(solution)/shard_map/ppermute | solution.py:35
  224.4 14.7 %collective-permute-start.64 = (bf16[192,1024]{1,0:T(8,128)(2,1)S(1)}, bf16[192,1024]{1,0:T(8,128)(2,1)S(1)}, u32[]{:S(2)}, u32[]{:S(2)}) collective-permute-start(bf16[192,1024]{1,0:T(8,128)(2,1)S(1)} %pad_maximum_fusion.11), channel_id=1, source_target_pairs={{0,1},{1,0},{2,3},{3,2},{4,5},{5,4},{6,7},{7,6},{8,9},{9,8},{10,11... | collective-permute-start | bytes 1179656 | tf_op jit(solution)/shard_map/ppermute | solution.py:35
  229.9 25.4 %collective-permute-start.47 = (bf16[128,2048]{1,0:T(8,128)(2,1)S(1)}, bf16[128,2048]{1,0:T(8,128)(2,1)S(1)}, u32[]{:S(2)}, u32[]{:S(2)}) collective-permute-start(bf16[128,2048]{1,0:T(8,128)(2,1)S(1)} %gather.5), channel_id=1, source_target_pairs={{0,16},{4,20},{8,24},{12,28},{16,0},{20,4},{24,8},{28,12},{1,17},{... | collective-permute-start | bytes 1572872 | tf_op jit(solution)/shard_map/ppermute | solution.py:35
  232.4 23.2 %collective-permute-start.57 = (bf16[128,2048]{1,0:T(8,128)(2,1)S(1)}, bf16[128,2048]{1,0:T(8,128)(2,1)S(1)}, u32[]{:S(2)}, u32[]{:S(2)}) collective-permute-start(bf16[128,2048]{1,0:T(8,128)(2,1)S(1)} %gather.6), channel_id=1, source_target_pairs={{0,8},{4,12},{8,0},{12,4},{16,24},{20,28},{24,16},{28,20},{1,9},{5... | collective-permute-start | bytes 1572872 | tf_op jit(solution)/shard_map/ppermute | solution.py:35
  (45 other events, 412.3 us)
Sparse Core Ops, SparseCore 0:
  24.2 30.9 all-gather.1

commit v8 on v7

--- a/solution.py
+++ b/solution.py
@@ -481,6 +481,7 @@
         for side, (near, _) in enumerate(routes):
             part = far[g][:, side * half : (side + 1) * half]
             sources += [part] + [send(part, n, "whole") for n in near[1:]]
+        last_sources = sources
         outgoing = call(
             functools.partial(dispatch_kernel, routes, g, capacity),
             [bf16((2 * len(near) * capacity, half)) for near, away in routes for _ in away],
@@ -491,18 +492,25 @@
             name="dispatch",
         )
         onward = [a for _, away in routes for a in away]
-        arrived.append([send(out, a, "picked") if a else out for out, a in zip(outgoing, onward)])
-
-    produced = []
+        ahead = far[g + 1 : g + 2] if g > 1 else []
+        arrived.append(
+            [send(tie(out, *ahead), a, "picked") if a else out for out, a in zip(outgoing, onward)]
+        )
+
+    produced, mates_before = [], ()
     slots = exp_count * capacity
-    for came in arrived:
+    for g, came in enumerate(arrived):
+        ahead = last_sources if g == groups - 2 else ()
+        done = [mates for pair in produced[groups - 2 :] for _, mates in pair]
         mate = jnp.concatenate([part[part.shape[0] // 2 :] for part in came], axis=0)
+        mate = swap(tie(mate, *ahead, *done, *mates_before), "ctx", 1)
+        mates_before = (mate,)
         made = call(
             functools.partial(expert_kernel, routes, capacity),
             [bf16((len(near) * capacity, half)) for near, away in routes for _ in away] * 2,
             [VMEM] * (len(came) + 4),
             *came,
-            swap(mate, "ctx", 1),
+            mate,
             w_gate[0],
             w_up[0],
             w_down[0],
@@ -515,8 +523,8 @@
         own, other = made[: len(came)], made[len(came) :]
         produced.append([(mine, swap(mates, "ctx", 1)) for mine, mates in zip(own, other)])
 
-    passing = [[] for _ in range(groups)]
-    for g in reversed(range(groups)):
+    totals, hop = [], ()
+    for g in [*range(2, groups), *(g for g in (1, 0) if g < groups)]:
         back, pieces = [], iter(produced[g])
         for _, away in routes:
             for a in away:
@@ -536,20 +544,21 @@
         total = call(
             functools.partial(gather_kernel, [len(near) - 1 for near, _ in routes]),
             bf16((rows, width)) if g else jax.ShapeDtypeStruct((rows, width), jnp.float32),
-            [VMEM] * (1 + len(sums) + (len(passing[g]) if g else 0)),
+            [VMEM] * (1 + len(sums)),
             kept,
             *sums,
-            *(passing[g] if g else []),
             name="gather",
         )
         if g:
-            passing[g & (g - 1)].append(swap(total, "ctx", 2 * (g & -g)))
+            total = swap(tie(total, *(hop if g > 1 else ())), "ctx", 2 * g)
+            hop = (total,)
+            totals.append(total)
     early = call(
         sum_kernel,
         jax.ShapeDtypeStruct((rows, width), jnp.float32),
-        [VMEM] * (1 + len(passing[0])),
+        [VMEM] * groups,
         residual,
-        *passing[0],
+        *totals,
         name="add",
         flops=10_000_000_000,
     )

time: 264 us -> 270 us (1.023)
  waiting for transfers between devices: 137 us -> 153 us
  starting transfers between devices: 63.1 us -> 54.1 us
    ppermute x67, waiting for transfers between devices: 133 us -> 150 us  [swap(): return lax.ppermute(array, axis, pairs)]
    ppermute x67, starting transfers between devices: 63.1 us -> 54.1 us  [swap(): return lax.ppermute(array, axis, pairs)]
    unnamed x49 -> x33, local copies, waits for them, and re-layouts: 6.38 us -> 5.6 us
  transfers between devices with their start and end apart: 68 -> 68, of which waited for: 30 -> 37; matrix products, arithmetic and copies ran while one was open for 1% -> 1% of each run, Pallas kernels for 12% -> 12%
where the time goes in v8:
time: 270 us
  waiting for transfers between devices  153 us (57%)
  starting transfers between devices  54.1 us (20%)
  Pallas kernels  39.6 us (15%)
  between operations  14.1 us (5%)
  local copies, waits for them, and re-layouts  6.03 us (2%)
  other arithmetic  3.07 us (1%)
    ppermute x67, waiting for transfers between devices, swap(): return lax.ppermute(array, axis, pairs)  150 us
    ppermute x67, starting transfers between devices, swap(): return lax.ppermute(array, axis, pairs)  54.1 us
    pallas_call x27, Pallas kernels, call(): pl.pallas_call(kernel, out_shape=out_shape, in_specs=specs, out_specs=jax...  39.6 us
    unnamed x33, local copies, waits for them, and re-layouts  5.6 us
  transfers between devices with their start and end apart: 68, of which 37 were waited for; matrix products, arithmetic and copies ran while one was open for 1% of the time, Pallas kernels for 12%

profile of v8, /device:TPU:0, one launch (start us, length us, event | category | flops | bytes accessed | tf_op | source)
XLA Modules:
  0.0 270.0 jit_solution(8616943586931180928)
XLA Ops:
  8.2 4.5 %own_rows.1 = (bf16[144,256]{1,0:T(8,128)(2,1)}, bf16[144,256]{1,0:T(8,128)(2,1)}, bf16[144,256]{1,0:T(8,128)(2,1)}, bf16[144,256]{1,0:T(8,128)(2,1)}) custom-call(s32[6]{0:T(128)} %pad_add_fusion.place, s32[8,128]{1,0:T(8,128)} %bitcast.38, s32[8,128]{1,0:T(8,128)} %bitcast.39, bf16[128,2048]{1,0:T(8,128)(2,1)} %tokens.1, f32[1,2048]{1,0:T(1,128)} %bitcast.34, ...), custom_call_target="tpu_custom_call" | custom-call | flops 1000 | bytes 1000 | tf_op jit(solution)/shard_map/own_rows/pallas_call | solution.py:333
  12.7 3.0 %collective-permute-start = (bf16[144,256]{1,0:T(8,128)(2,1)}, bf16[144,256]{1,0:T(8,128)(2,1)S(1)}, u32[]{:S(2)}, u32[]{:S(2)}) collective-permute-start(bf16[144,256]{1,0:T(8,128)(2,1)} %get-tuple-element.109), channel_id=1, source_target_pairs={{0,1},{1,0},{2,3},{3,2},{4,5},{5,4},{6,7},{7,6},{8,9},{9,8},{10,11... | collective-permute-start | bytes 221192 | tf_op jit(solution)/shard_map/ppermute | solution.py:35
  15.7 1.5 collective-permute-start.1
  18.5 1.7 collective-permute-done.1
  20.3 2.4 collective-permute-done.2
  24.6 1.6 collective-permute-start.4
  26.2 1.5 collective-permute-start.3
  28.7 11.3 %collective-permute-done.5.refs_3_ = bf16[128,2048]{1,0:T(8,128)(2,1)S(1)} collective-permute-done((bf16[128,2048]{1,0:T(8,128)(2,1)S(1)}, bf16[128,2048]{1,0:T(8,128)(2,1)S(1)}, u32[]{:S(2)}, u32[]{:S(2)}) %collective-permute-start.5) | collective-permute-done | bytes 524320 | tf_op jit(solution)/shard_map/ppermute | solution.py:35
  40.0 8.2 %collective-permute-done.4.refs_2_ = bf16[128,2048]{1,0:T(8,128)(2,1)S(1)} collective-permute-done((bf16[128,2048]{1,0:T(8,128)(2,1)S(1)}, bf16[128,2048]{1,0:T(8,128)(2,1)S(1)}, u32[]{:S(2)}, u32[]{:S(2)}) %collective-permute-start.4) | collective-permute-done | bytes 524320 | tf_op jit(solution)/shard_map/ppermute | solution.py:35
  48.2 1.6 copy-done.7
  49.8 1.8 queries.1
  51.7 3.5 %all-gather.2.cloned.1.call-done.both = bf16[4608,256]{1,0:T(8,128)(2,1)} async-done(((bf16[576,256]{1,0:T(8,128)(2,1)}), bf16[4608,256]{1,0:T(8,128)(2,1)}) %all-gather.2.cloned.1.call-update) | async-done | bytes 2359312 | tf_op jit(solution)/shard_map/all_gather | solution.py:402
  55.3 1.7 copy-done.3
  56.9 1.7 attention.4
  58.6 2.4 collective-permute-start.6
  61.1 1.7 attention.5
  63.4 1.7 attention.6
  65.8 1.9 attention.7.refs_0_
  67.7 6.8 %collective-permute-done.6.refs_1_ = bf16[128,2048]{1,0:T(8,128)(2,1)S(1)} collective-permute-done((bf16[128,2048]{1,0:T(8,128)(2,1)S(1)}, bf16[128,2048]{1,0:T(8,128)(2,1)S(1)}, u32[]{:S(2)}, u32[]{:S(2)}) %collective-permute-start.6) | collective-permute-done | bytes 524320 | tf_op jit(solution)/shard_map/ppermute | solution.py:35
  74.6 11.0 %collective-permute-done.7.refs_1_ = bf16[128,2048]{1,0:T(8,128)(2,1)S(1)} collective-permute-done((bf16[128,2048]{1,0:T(8,128)(2,1)S(1)}, bf16[128,2048]{1,0:T(8,128)(2,1)S(1)}, u32[]{:S(2)}, u32[]{:S(2)}) %collective-permute-start.7) | collective-permute-done | bytes 524320 | tf_op jit(solution)/shard_map/ppermute | solution.py:35
  86.2 2.5 collective-permute-start.10
  91.5 5.4 %collective-permute-done.14.refs_3_ = bf16[128,1024]{1,0:T(8,128)(2,1)S(1)} collective-permute-done((bf16[128,1024]{1,0:T(8,128)(2,1)S(1)}, bf16[128,1024]{1,0:T(8,128)(2,1)S(1)}, u32[]{:S(2)}, u32[]{:S(2)}) %collective-permute-start.14) | collective-permute-done | bytes 262176 | tf_op jit(solution)/shard_map/ppermute | solution.py:35
  101.3 6.4 %collective-permute-start.9 = (bf16[128,2048]{1,0:T(8,128)(2,1)S(1)}, bf16[128,2048]{1,0:T(8,128)(2,1)S(1)}, u32[]{:S(2)}, u32[]{:S(2)}) collective-permute-start(bf16[128,2048]{1,0:T(8,128)(2,1)S(1)} %get-tuple-element.118), channel_id=1, source_target_pairs={{0,16},{4,20},{8,24},{12,28},{16,0},{20,4},{24,8},{28,12},{1,17},{... | collective-permute-start | bytes 1572872 | tf_op jit(solution)/shard_map/ppermute | solution.py:35
  109.7 5.1 %collective-permute-done.12.refs_1_ = bf16[128,1024]{1,0:T(8,128)(2,1)S(1)} collective-permute-done((bf16[128,1024]{1,0:T(8,128)(2,1)S(1)}, bf16[128,1024]{1,0:T(8,128)(2,1)S(1)}, u32[]{:S(2)}, u32[]{:S(2)}) %collective-permute-start.12) | collective-permute-done | bytes 262176 | tf_op jit(solution)/shard_map/ppermute | solution.py:35
  118.7 11.0 %collective-permute-done.9 = bf16[128,2048]{1,0:T(8,128)(2,1)S(1)} collective-permute-done((bf16[128,2048]{1,0:T(8,128)(2,1)S(1)}, bf16[128,2048]{1,0:T(8,128)(2,1)S(1)}, u32[]{:S(2)}, u32[]{:S(2)}) %collective-permute-start.9) | collective-permute-done | bytes 524320 | tf_op jit(solution)/shard_map/ppermute | solution.py:35
  131.2 6.7 %collective-permute-done.13.refs_1_ = bf16[128,1024]{1,0:T(8,128)(2,1)S(1)} collective-permute-done((bf16[128,1024]{1,0:T(8,128)(2,1)S(1)}, bf16[128,1024]{1,0:T(8,128)(2,1)S(1)}, u32[]{:S(2)}, u32[]{:S(2)}) %collective-permute-start.13) | collective-permute-done | bytes 262176 | tf_op jit(solution)/shard_map/ppermute | solution.py:35
  139.1 4.3 %collective-permute-done.17 = bf16[128,2048]{1,0:T(8,128)(2,1)S(1)} collective-permute-done((bf16[128,2048]{1,0:T(8,128)(2,1)S(1)}, bf16[128,2048]{1,0:T(8,128)(2,1)S(1)}, u32[]{:S(2)}, u32[]{:S(2)}) %collective-permute-start.17) | collective-permute-done | bytes 524320 | tf_op jit(solution)/shard_map/ppermute | solution.py:35
  144.2 2.0 collective-permute-start.24
  147.6 7.9 %collective-permute-done.20.refs_1_ = bf16[192,1024]{1,0:T(8,128)(2,1)S(1)} collective-permute-done((bf16[192,1024]{1,0:T(8,128)(2,1)S(1)}, bf16[192,1024]{1,0:T(8,128)(2,1)S(1)}, u32[]{:S(2)}, u32[]{:S(2)}) %collective-permute-start.20) | collective-permute-done | bytes 393248 | tf_op jit(solution)/shard_map/ppermute | solution.py:35
  156.1 3.3 %collective-permute-done.24.refs_1_ = bf16[128,1024]{1,0:T(8,128)(2,1)S(1)} collective-permute-done((bf16[128,1024]{1,0:T(8,128)(2,1)S(1)}, bf16[128,1024]{1,0:T(8,128)(2,1)S(1)}, u32[]{:S(2)}, u32[]{:S(2)}) %collective-permute-start.24) | collective-permute-done | bytes 262176 | tf_op jit(solution)/shard_map/ppermute | solution.py:35
  162.4 3.8 %expert.4 = (bf16[96,1024]{1,0:T(8,128)(2,1)S(1)}, bf16[96,1024]{1,0:T(8,128)(2,1)S(1)}, bf16[96,1024]{1,0:T(8,128)(2,1)S(1)}, bf16[96,1024]{1,0:T(8,128)(2,1)S(...) custom-call(bf16[192,1024]{1,0:T(8,128)(2,1)S(1)} %get-tuple-element, ...), custom_call_target="tpu_custom_call" | custom-call | flops 1000 | bytes 1000 | tf_op jit(solution)/shard_map/expert/pallas_call | solution.py:333
  166.9 5.3 %collective-permute-done.35.refs_3_ = bf16[192,1024]{1,0:T(8,128)(2,1)S(1)} collective-permute-done((bf16[192,1024]{1,0:T(8,128)(2,1)S(1)}, bf16[192,1024]{1,0:T(8,128)(2,1)S(1)}, u32[]{:S(2)}, u32[]{:S(2)}) %collective-permute-start.35) | collective-permute-done | bytes 393248 | tf_op jit(solution)/shard_map/ppermute | solution.py:35
  174.2 1.7 collective-permute-done.40.refs_4_
  175.9 3.8 %expert.5 = (bf16[96,1024]{1,0:T(8,128)(2,1)S(1)}, bf16[96,1024]{1,0:T(8,128)(2,1)S(1)}, bf16[96,1024]{1,0:T(8,128)(2,1)S(1)}, bf16[96,1024]{1,0:T(8,128)(2,1)S(...) custom-call(bf16[192,1024]{1,0:T(8,128)(2,1)S(1)} %get-tuple-element, ...), custom_call_target="tpu_custom_call" | custom-call | flops 1000 | bytes 1000 | tf_op jit(solution)/shard_map/expert/pallas_call | solution.py:333
  180.0 1.5 collective-permute-start.32
  181.6 3.6 %collective-permute-done.36.refs_5_ = bf16[192,1024]{1,0:T(8,128)(2,1)S(1)} collective-permute-done((bf16[192,1024]{1,0:T(8,128)(2,1)S(1)}, bf16[192,1024]{1,0:T(8,128)(2,1)S(1)}, u32[]{:S(2)}, u32[]{:S(2)}) %collective-permute-start.36) | collective-permute-done | bytes 393248 | tf_op jit(solution)/shard_map/ppermute | solution.py:35
  185.7 5.7 %collective-permute-done.32.refs_2_ = bf16[192,1024]{1,0:T(8,128)(2,1)S(1)} collective-permute-done((bf16[192,1024]{1,0:T(8,128)(2,1)S(1)}, bf16[192,1024]{1,0:T(8,128)(2,1)S(1)}, u32[]{:S(2)}, u32[]{:S(2)}) %collective-permute-start.32) | collective-permute-done | bytes 393248 | tf_op jit(solution)/shard_map/ppermute | solution.py:35
  192.8 4.1 %expert.6 = (bf16[96,1024]{1,0:T(8,128)(2,1)S(1)}, bf16[96,1024]{1,0:T(8,128)(2,1)S(1)}, bf16[96,1024]{1,0:T(8,128)(2,1)S(1)}, bf16[96,1024]{1,0:T(8,128)(2,1)S(...) custom-call(bf16[192,1024]{1,0:T(8,128)(2,1)S(1)} %get-tuple-element, ...), custom_call_target="tpu_custom_call" | custom-call | flops 1000 | bytes 1000 | tf_op jit(solution)/shard_map/expert/pallas_call | solution.py:333
  200.3 2.3 collective-permute-done.43.refs_2_
  203.1 4.5 %collective-permute-done.38.refs_1_ = bf16[128,1024]{1,0:T(8,128)(2,1)S(1)} collective-permute-done((bf16[128,1024]{1,0:T(8,128)(2,1)S(1)}, bf16[128,1024]{1,0:T(8,128)(2,1)S(1)}, u32[]{:S(2)}, u32[]{:S(2)}) %collective-permute-start.38) | collective-permute-done | bytes 262176 | tf_op jit(solution)/shard_map/ppermute | solution.py:35
  212.2 3.8 %expert.7 = (bf16[96,1024]{1,0:T(8,128)(2,1)S(1)}, bf16[96,1024]{1,0:T(8,128)(2,1)S(1)}, bf16[96,1024]{1,0:T(8,128)(2,1)S(1)}, bf16[96,1024]{1,0:T(8,128)(2,1)S(...) custom-call(bf16[192,1024]{1,0:T(8,128)(2,1)S(1)} %get-tuple-element, ...), custom_call_target="tpu_custom_call" | custom-call | flops 1000 | bytes 1000 | tf_op jit(solution)/shard_map/expert/pallas_call | solution.py:333
  216.8 2.8 %collective-permute-done.52.refs_2_ = bf16[192,1024]{1,0:T(8,128)(2,1)S(1)} collective-permute-done((bf16[192,1024]{1,0:T(8,128)(2,1)S(1)}, bf16[192,1024]{1,0:T(8,128)(2,1)S(1)}, u32[]{:S(2)}, u32[]{:S(2)}) %collective-permute-start.52) | collective-permute-done | bytes 393248 | tf_op jit(solution)/shard_map/ppermute | solution.py:35
  221.3 2.4 collective-permute-done.48.refs_1_
  224.9 1.6 collective-permute-start.64
  226.5 9.3 %collective-permute-done.39.refs_1_ = bf16[128,2048]{1,0:T(8,128)(2,1)S(1)} collective-permute-done((bf16[128,2048]{1,0:T(8,128)(2,1)S(1)}, bf16[128,2048]{1,0:T(8,128)(2,1)S(1)}, u32[]{:S(2)}, u32[]{:S(2)}) %collective-permute-start.39) | collective-permute-done | bytes 524320 | tf_op jit(solution)/shard_map/ppermute | solution.py:35
  239.5 7.2 %collective-permute-done.61.refs_2_ = bf16[192,1024]{1,0:T(8,128)(2,1)S(1)} collective-permute-done((bf16[192,1024]{1,0:T(8,128)(2,1)S(1)}, bf16[192,1024]{1,0:T(8,128)(2,1)S(1)}, u32[]{:S(2)}, u32[]{:S(2)}) %collective-permute-start.61) | collective-permute-done | bytes 393248 | tf_op jit(solution)/shard_map/ppermute | solution.py:35
  249.1 6.1 %collective-permute-done.66.refs_1_ = bf16[128,1024]{1,0:T(8,128)(2,1)S(1)} collective-permute-done((bf16[128,1024]{1,0:T(8,128)(2,1)S(1)}, bf16[128,1024]{1,0:T(8,128)(2,1)S(1)}, u32[]{:S(2)}, u32[]{:S(2)}) %collective-permute-start.66) | collective-permute-done | bytes 262176 | tf_op jit(solution)/shard_map/ppermute | solution.py:35
  255.8 6.3 %collective-permute-done.58.refs_3_ = bf16[128,2048]{1,0:T(8,128)(2,1)S(1)} collective-permute-done((bf16[128,2048]{1,0:T(8,128)(2,1)S(1)}, bf16[128,2048]{1,0:T(8,128)(2,1)S(1)}, u32[]{:S(2)}, u32[]{:S(2)}) %collective-permute-start.58) | collective-permute-done | bytes 524320 | tf_op jit(solution)/shard_map/ppermute | solution.py:35
  (193 shorter events, 54.0 us)
Async XLA Ops:
  6.5 48.7 %all-gather.2.cloned.1.call-start = ((), (), s32[]{:S(2)}) async-start(), calls=%async_computation | async-start | bytes 2654208 | tf_op jit(solution)/shard_map/all_gather | solution.py:402
  24.1 15.8 %collective-permute-start.5 = (bf16[128,2048]{1,0:T(8,128)(2,1)S(1)}, bf16[128,2048]{1,0:T(8,128)(2,1)S(1)}, u32[]{:S(2)}, u32[]{:S(2)}) collective-permute-start(bf16[128,2048]{1,0:T(8,128)(2,1)S(1)} %copy-done.6), channel_id=1, source_target_pairs={{0,3},{1,2},{2,1},{3,0},{4,7},{5,6},{6,5},{7,4},{8,11},{9,10},{10,... | collective-permute-start | bytes 1572872 | tf_op jit(solution)/shard_map/ppermute | solution.py:35
  24.6 23.5 %collective-permute-start.4 = (bf16[128,2048]{1,0:T(8,128)(2,1)S(1)}, bf16[128,2048]{1,0:T(8,128)(2,1)S(1)}, u32[]{:S(2)}, u32[]{:S(2)}) collective-permute-start(bf16[128,2048]{1,0:T(8,128)(2,1)S(1)} %copy-done.6), channel_id=1, source_target_pairs={{0,2},{1,3},{2,0},{3,1},{4,6},{5,7},{6,4},{7,5},{8,10},{9,11},{10,... | collective-permute-start | bytes 1572872 | tf_op jit(solution)/shard_map/ppermute | solution.py:35
  26.2 22.0 %collective-permute-start.3 = (bf16[128,2048]{1,0:T(8,128)(2,1)S(1)}, bf16[128,2048]{1,0:T(8,128)(2,1)S(1)}, u32[]{:S(2)}, u32[]{:S(2)}) collective-permute-start(bf16[128,2048]{1,0:T(8,128)(2,1)S(1)} %copy-done.6), channel_id=1, source_target_pairs={{0,1},{1,0},{2,3},{3,2},{4,5},{5,4},{6,7},{7,6},{8,9},{9,8},{10,11... | collective-permute-start | bytes 1572872 | tf_op jit(solution)/shard_map/ppermute | solution.py:35
  58.6 15.9 %collective-permute-start.6 = (bf16[128,2048]{1,0:T(8,128)(2,1)S(1)}, bf16[128,2048]{1,0:T(8,128)(2,1)S(1)}, u32[]{:S(2)}, u32[]{:S(2)}) collective-permute-start(bf16[128,2048]{1,0:T(8,128)(2,1)S(1)} %attention.4), channel_id=1, source_target_pairs={{0,3},{1,2},{2,1},{3,0},{4,7},{5,6},{6,5},{7,4},{8,11},{9,10},{10,... | collective-permute-start | bytes 1572872 | tf_op jit(solution)/shard_map/ppermute | solution.py:35
  62.8 22.9 %collective-permute-start.7 = (bf16[128,2048]{1,0:T(8,128)(2,1)S(1)}, bf16[128,2048]{1,0:T(8,128)(2,1)S(1)}, u32[]{:S(2)}, u32[]{:S(2)}) collective-permute-start(bf16[128,2048]{1,0:T(8,128)(2,1)S(1)} %attention.5), channel_id=1, source_target_pairs={{0,1},{1,0},{2,3},{3,2},{4,5},{5,4},{6,7},{7,6},{8,9},{9,8},{10,11... | collective-permute-start | bytes 1572872 | tf_op jit(solution)/shard_map/ppermute | solution.py:35
  65.2 20.7 %collective-permute-start.8 = (bf16[128,2048]{1,0:T(8,128)(2,1)S(1)}, bf16[128,2048]{1,0:T(8,128)(2,1)S(1)}, u32[]{:S(2)}, u32[]{:S(2)}) collective-permute-start(bf16[128,2048]{1,0:T(8,128)(2,1)S(1)} %attention.6), channel_id=1, source_target_pairs={{0,2},{1,3},{2,0},{3,1},{4,6},{5,7},{6,4},{7,5},{8,10},{9,11},{10,... | collective-permute-start | bytes 1572872 | tf_op jit(solution)/shard_map/ppermute | solution.py:35
  86.2 21.4 %collective-permute-start.10 = (bf16[128,2048]{1,0:T(8,128)(2,1)S(1)}, bf16[128,2048]{1,0:T(8,128)(2,1)S(1)}, u32[]{:S(2)}, u32[]{:S(2)}) collective-permute-start(bf16[128,2048]{1,0:T(8,128)(2,1)S(1)} %get-tuple-element.118), channel_id=1, source_target_pairs={{0,8},{4,12},{8,0},{12,4},{16,24},{20,28},{24,16},{28,20},{1,9},{5... | collective-permute-start | bytes 1572872 | tf_op jit(solution)/shard_map/ppermute | solution.py:35
  88.8 8.1 %collective-permute-start.14 = (bf16[128,1024]{1,0:T(8,128)(2,1)S(1)}, bf16[128,1024]{1,0:T(8,128)(2,1)S(1)}, u32[]{:S(2)}, u32[]{:S(2)}) collective-permute-start(bf16[128,1024]{1,0:T(8,128)(2,1)S(1)} %get-tuple-element.215.refs_2_), channel_id=1, source_target_pairs={{0,2},{1,3},{2,0},{3,1},{4,6},{5,7},{6,4},{7,5},{8,10},{9,11},{10,... | collective-permute-start | bytes 786440 | tf_op jit(solution)/shard_map/ppermute | solution.py:35
  90.0 7.8 %collective-permute-start.11 = (bf16[128,1024]{1,0:T(8,128)(2,1)S(1)}, bf16[128,1024]{1,0:T(8,128)(2,1)S(1)}, u32[]{:S(2)}, u32[]{:S(2)}) collective-permute-start(bf16[128,1024]{1,0:T(8,128)(2,1)S(1)} %get-tuple-element.216.refs_0_), channel_id=1, source_target_pairs={{0,1},{1,0},{2,3},{3,2},{4,5},{5,4},{6,7},{7,6},{8,9},{9,8},{10,11... | collective-permute-start | bytes 786440 | tf_op jit(solution)/shard_map/ppermute | solution.py:35
  98.9 10.1 %collective-permute-start.18 = (bf16[192,1024]{1,0:T(8,128)(2,1)S(1)}, bf16[192,1024]{1,0:T(8,128)(2,1)S(1)}, u32[]{:S(2)}, u32[]{:S(2)}) collective-permute-start(bf16[192,1024]{1,0:T(8,128)(2,1)S(1)} %get-tuple-element.127), channel_id=1, source_target_pairs={{0,2},{1,3},{2,0},{3,1},{4,6},{5,7},{6,4},{7,5},{8,10},{9,11},{10,... | collective-permute-start | bytes 1179656 | tf_op jit(solution)/shard_map/ppermute | solution.py:35
  99.8 9.7 %collective-permute-start.21 = (bf16[192,1024]{1,0:T(8,128)(2,1)S(1)}, bf16[192,1024]{1,0:T(8,128)(2,1)S(1)}, u32[]{:S(2)}, u32[]{:S(2)}) collective-permute-start(bf16[192,1024]{1,0:T(8,128)(2,1)S(1)} %get-tuple-element.134), channel_id=1, source_target_pairs={{0,1},{1,0},{2,3},{3,2},{4,5},{5,4},{6,7},{7,6},{8,9},{9,8},{10,11... | collective-permute-start | bytes 1179656 | tf_op jit(solution)/shard_map/ppermute | solution.py:35
  101.3 28.4 %collective-permute-start.9 = (bf16[128,2048]{1,0:T(8,128)(2,1)S(1)}, bf16[128,2048]{1,0:T(8,128)(2,1)S(1)}, u32[]{:S(2)}, u32[]{:S(2)}) collective-permute-start(bf16[128,2048]{1,0:T(8,128)(2,1)S(1)} %get-tuple-element.118), channel_id=1, source_target_pairs={{0,16},{4,20},{8,24},{12,28},{16,0},{20,4},{24,8},{28,12},{1,17},{... | collective-permute-start | bytes 1572872 | tf_op jit(solution)/shard_map/ppermute | solution.py:35
  109.6 21.5 %collective-permute-start.26 = (bf16[384,1024]{1,0:T(8,128)(2,1)S(1)}, bf16[384,1024]{1,0:T(8,128)(2,1)S(1)}, u32[]{:S(2)}, u32[]{:S(2)}) collective-permute-start(bf16[384,1024]{1,0:T(8,128)(2,1)S(1)} %pad_maximum_fusion.2), channel_id=1, source_target_pairs={{0,4},{4,0},{8,12},{12,8},{16,20},{20,16},{24,28},{28,24},{1,5},{5... | collective-permute-start | bytes 2359304 | tf_op jit(solution)/shard_map/ppermute | solution.py:35
  115.9 14.4 %collective-permute-start.19 = (bf16[192,1024]{1,0:T(8,128)(2,1)S(1)}, bf16[192,1024]{1,0:T(8,128)(2,1)S(1)}, u32[]{:S(2)}, u32[]{:S(2)}) collective-permute-start(bf16[192,1024]{1,0:T(8,128)(2,1)S(1)} %get-tuple-element.128), channel_id=1, source_target_pairs={{0,2},{1,3},{2,0},{3,1},{4,6},{5,7},{6,4},{7,5},{8,10},{9,11},{10,... | collective-permute-start | bytes 1179656 | tf_op jit(solution)/shard_map/ppermute | solution.py:35
  117.2 13.9 %collective-permute-start.22 = (bf16[192,1024]{1,0:T(8,128)(2,1)S(1)}, bf16[192,1024]{1,0:T(8,128)(2,1)S(1)}, u32[]{:S(2)}, u32[]{:S(2)}) collective-permute-start(bf16[192,1024]{1,0:T(8,128)(2,1)S(1)} %get-tuple-element.135), channel_id=1, source_target_pairs={{0,1},{1,0},{2,3},{3,2},{4,5},{5,4},{6,7},{7,6},{8,9},{9,8},{10,11... | collective-permute-start | bytes 1179656 | tf_op jit(solution)/shard_map/ppermute | solution.py:35
  129.6 13.8 %collective-permute-start.17 = (bf16[128,2048]{1,0:T(8,128)(2,1)S(1)}, bf16[128,2048]{1,0:T(8,128)(2,1)S(1)}, u32[]{:S(2)}, u32[]{:S(2)}) collective-permute-start(bf16[128,2048]{1,0:T(8,128)(2,1)S(1)} %collective-permute-done.9), channel_id=1, source_target_pairs={{0,8},{4,12},{8,0},{12,4},{16,24},{20,28},{24,16},{28,20},{1,9},{5... | collective-permute-start | bytes 1572872 | tf_op jit(solution)/shard_map/ppermute | solution.py:35
  129.6 8.2 %collective-permute-start.13 = (bf16[128,1024]{1,0:T(8,128)(2,1)S(1)}, bf16[128,1024]{1,0:T(8,128)(2,1)S(1)}, u32[]{:S(2)}, u32[]{:S(2)}) collective-permute-start(bf16[128,1024]{1,0:T(8,128)(2,1)S(1)} %get-tuple-element.120.refs_0_), channel_id=1, source_target_pairs={{0,1},{1,0},{2,3},{3,2},{4,5},{5,4},{6,7},{7,6},{8,9},{9,8},{10,11... | collective-permute-start | bytes 786440 | tf_op jit(solution)/shard_map/ppermute | solution.py:35
  130.3 7.7 %collective-permute-start.16 = (bf16[128,1024]{1,0:T(8,128)(2,1)S(1)}, bf16[128,1024]{1,0:T(8,128)(2,1)S(1)}, u32[]{:S(2)}, u32[]{:S(2)}) collective-permute-start(bf16[128,1024]{1,0:T(8,128)(2,1)S(1)} %get-tuple-element.122.refs_2_), channel_id=1, source_target_pairs={{0,2},{1,3},{2,0},{3,1},{4,6},{5,7},{6,4},{7,5},{8,10},{9,11},{10,... | collective-permute-start | bytes 786440 | tf_op jit(solution)/shard_map/ppermute | solution.py:35
  131.1 28.3 %collective-permute-start.27 = (bf16[384,1024]{1,0:T(8,128)(2,1)S(1)}, bf16[384,1024]{1,0:T(8,128)(2,1)S(1)}, u32[]{:S(2)}, u32[]{:S(2)}) collective-permute-start(bf16[384,1024]{1,0:T(8,128)(2,1)S(1)} %pad_maximum_fusion.1), channel_id=1, source_target_pairs={{0,4},{4,0},{8,12},{12,8},{16,20},{20,16},{24,28},{28,24},{1,5},{5... | collective-permute-start | bytes 2359304 | tf_op jit(solution)/shard_map/ppermute | solution.py:35
  143.4 12.1 %collective-permute-start.20 = (bf16[192,1024]{1,0:T(8,128)(2,1)S(1)}, bf16[192,1024]{1,0:T(8,128)(2,1)S(1)}, u32[]{:S(2)}, u32[]{:S(2)}) collective-permute-start(bf16[192,1024]{1,0:T(8,128)(2,1)S(1)} %get-tuple-element.129), channel_id=1, source_target_pairs={{0,2},{1,3},{2,0},{3,1},{4,6},{5,7},{6,4},{7,5},{8,10},{9,11},{10,... | collective-permute-start | bytes 1179656 | tf_op jit(solution)/shard_map/ppermute | solution.py:35
  144.0 12.1 %collective-permute-start.23 = (bf16[192,1024]{1,0:T(8,128)(2,1)S(1)}, bf16[192,1024]{1,0:T(8,128)(2,1)S(1)}, u32[]{:S(2)}, u32[]{:S(2)}) collective-permute-start(bf16[192,1024]{1,0:T(8,128)(2,1)S(1)} %get-tuple-element.136), channel_id=1, source_target_pairs={{0,1},{1,0},{2,3},{3,2},{4,5},{5,4},{6,7},{7,6},{8,9},{9,8},{10,11... | collective-permute-start | bytes 1179656 | tf_op jit(solution)/shard_map/ppermute | solution.py:35
  144.2 15.3 %collective-permute-start.24 = (bf16[128,1024]{1,0:T(8,128)(2,1)S(1)}, bf16[128,1024]{1,0:T(8,128)(2,1)S(1)}, u32[]{:S(2)}, u32[]{:S(2)}) collective-permute-start(bf16[128,1024]{1,0:T(8,128)(2,1)S(1)} %get-tuple-element.137.refs_0_), channel_id=1, source_target_pairs={{0,1},{1,0},{2,3},{3,2},{4,5},{5,4},{6,7},{7,6},{8,9},{9,8},{10,11... | collective-permute-start | bytes 786440 | tf_op jit(solution)/shard_map/ppermute | solution.py:35
  146.1 13.3 %collective-permute-start.25 = (bf16[128,1024]{1,0:T(8,128)(2,1)S(1)}, bf16[128,1024]{1,0:T(8,128)(2,1)S(1)}, u32[]{:S(2)}, u32[]{:S(2)}) collective-permute-start(bf16[128,1024]{1,0:T(8,128)(2,1)S(1)} %get-tuple-element.138.refs_2_), channel_id=1, source_target_pairs={{0,2},{1,3},{2,0},{3,1},{4,6},{5,7},{6,4},{7,5},{8,10},{9,11},{10,... | collective-permute-start | bytes 786440 | tf_op jit(solution)/shard_map/ppermute | solution.py:35
  160.6 11.6 %collective-permute-start.35 = (bf16[192,1024]{1,0:T(8,128)(2,1)S(1)}, bf16[192,1024]{1,0:T(8,128)(2,1)S(1)}, u32[]{:S(2)}, u32[]{:S(2)}) collective-permute-start(bf16[192,1024]{1,0:T(8,128)(2,1)S(1)} %get-tuple-element.157), channel_id=1, source_target_pairs={{0,1},{1,0},{2,3},{3,2},{4,5},{5,4},{6,7},{7,6},{8,9},{9,8},{10,11... | collective-permute-start | bytes 1179656 | tf_op jit(solution)/shard_map/ppermute | solution.py:35
  160.9 11.3 %collective-permute-start.31 = (bf16[192,1024]{1,0:T(8,128)(2,1)S(1)}, bf16[192,1024]{1,0:T(8,128)(2,1)S(1)}, u32[]{:S(2)}, u32[]{:S(2)}) collective-permute-start(bf16[192,1024]{1,0:T(8,128)(2,1)S(1)} %get-tuple-element.150), channel_id=1, source_target_pairs={{0,2},{1,3},{2,0},{3,1},{4,6},{5,7},{6,4},{7,5},{8,10},{9,11},{10,... | collective-permute-start | bytes 1179656 | tf_op jit(solution)/shard_map/ppermute | solution.py:35
  173.8 11.5 %collective-permute-start.36 = (bf16[192,1024]{1,0:T(8,128)(2,1)S(1)}, bf16[192,1024]{1,0:T(8,128)(2,1)S(1)}, u32[]{:S(2)}, u32[]{:S(2)}) collective-permute-start(bf16[192,1024]{1,0:T(8,128)(2,1)S(1)} %pad_maximum_fusion.5), channel_id=1, source_target_pairs={{0,1},{1,0},{2,3},{3,2},{4,5},{5,4},{6,7},{7,6},{8,9},{9,8},{10,11... | collective-permute-start | bytes 1179656 | tf_op jit(solution)/shard_map/ppermute | solution.py:35
  180.0 11.5 %collective-permute-start.32 = (bf16[192,1024]{1,0:T(8,128)(2,1)S(1)}, bf16[192,1024]{1,0:T(8,128)(2,1)S(1)}, u32[]{:S(2)}, u32[]{:S(2)}) collective-permute-start(bf16[192,1024]{1,0:T(8,128)(2,1)S(1)} %pad_maximum_fusion.4), channel_id=1, source_target_pairs={{0,2},{1,3},{2,0},{3,1},{4,6},{5,7},{6,4},{7,5},{8,10},{9,11},{10,... | collective-permute-start | bytes 1179656 | tf_op jit(solution)/shard_map/ppermute | solution.py:35
  185.2 14.5 %collective-permute-start.46 = (bf16[192,1024]{1,0:T(8,128)(2,1)S(1)}, bf16[192,1024]{1,0:T(8,128)(2,1)S(1)}, u32[]{:S(2)}, u32[]{:S(2)}) collective-permute-start(bf16[192,1024]{1,0:T(8,128)(2,1)S(1)} %pad_maximum_fusion.7), channel_id=1, source_target_pairs={{0,1},{1,0},{2,3},{3,2},{4,5},{5,4},{6,7},{7,6},{8,9},{9,8},{10,11... | collective-permute-start | bytes 1179656 | tf_op jit(solution)/shard_map/ppermute | solution.py:35
  191.4 11.2 %collective-permute-start.43 = (bf16[192,1024]{1,0:T(8,128)(2,1)S(1)}, bf16[192,1024]{1,0:T(8,128)(2,1)S(1)}, u32[]{:S(2)}, u32[]{:S(2)}) collective-permute-start(bf16[192,1024]{1,0:T(8,128)(2,1)S(1)} %pad_maximum_fusion.6), channel_id=1, source_target_pairs={{0,2},{1,3},{2,0},{3,1},{4,6},{5,7},{6,4},{7,5},{8,10},{9,11},{10,... | collective-permute-start | bytes 1179656 | tf_op jit(solution)/shard_map/ppermute | solution.py:35
  198.5 9.1 %collective-permute-start.38 = (bf16[128,1024]{1,0:T(8,128)(2,1)S(1)}, bf16[128,1024]{1,0:T(8,128)(2,1)S(1)}, u32[]{:S(2)}, u32[]{:S(2)}) collective-permute-start(bf16[128,1024]{1,0:T(8,128)(2,1)S(1)} %get-tuple-element.163), channel_id=1, source_target_pairs={{0,2},{1,3},{2,0},{3,1},{4,6},{5,7},{6,4},{7,5},{8,10},{9,11},{10,... | collective-permute-start | bytes 786440 | tf_op jit(solution)/shard_map/ppermute | solution.py:35
  199.2 9.9 %collective-permute-start.37 = (bf16[128,1024]{1,0:T(8,128)(2,1)S(1)}, bf16[128,1024]{1,0:T(8,128)(2,1)S(1)}, u32[]{:S(2)}, u32[]{:S(2)}) collective-permute-start(bf16[128,1024]{1,0:T(8,128)(2,1)S(1)} %get-tuple-element.161), channel_id=1, source_target_pairs={{0,1},{1,0},{2,3},{3,2},{4,5},{5,4},{6,7},{7,6},{8,9},{9,8},{10,11... | collective-permute-start | bytes 786440 | tf_op jit(solution)/shard_map/ppermute | solution.py:35
  199.7 9.4 %collective-permute-start.41 = (bf16[96,1024]{1,0:T(8,128)(2,1)S(1)}, bf16[96,1024]{1,0:T(8,128)(2,1)S(1)}, u32[]{:S(2)}, u32[]{:S(2)}) collective-permute-start(bf16[96,1024]{1,0:T(8,128)(2,1)S(1)} %get-tuple-element.168), channel_id=1, source_target_pairs={{0,4},{4,0},{8,12},{12,8},{16,20},{20,16},{24,28},{28,24},{1,5},{5... | collective-permute-start | bytes 589832 | tf_op jit(solution)/shard_map/ppermute | solution.py:35
  199.7 9.9 %collective-permute-start.44 = (bf16[96,1024]{1,0:T(8,128)(2,1)S(1)}, bf16[96,1024]{1,0:T(8,128)(2,1)S(1)}, u32[]{:S(2)}, u32[]{:S(2)}) collective-permute-start(bf16[96,1024]{1,0:T(8,128)(2,1)S(1)} %get-tuple-element.173), channel_id=1, source_target_pairs={{0,4},{4,0},{8,12},{12,8},{16,20},{20,16},{24,28},{28,24},{1,5},{5... | collective-permute-start | bytes 589832 | tf_op jit(solution)/shard_map/ppermute | solution.py:35
  202.7 14.2 %collective-permute-start.55 = (bf16[192,1024]{1,0:T(8,128)(2,1)S(1)}, bf16[192,1024]{1,0:T(8,128)(2,1)S(1)}, u32[]{:S(2)}, u32[]{:S(2)}) collective-permute-start(bf16[192,1024]{1,0:T(8,128)(2,1)S(1)} %pad_maximum_fusion.9), channel_id=1, source_target_pairs={{0,1},{1,0},{2,3},{3,2},{4,5},{5,4},{6,7},{7,6},{8,9},{9,8},{10,11... | collective-permute-start | bytes 1179656 | tf_op jit(solution)/shard_map/ppermute | solution.py:35
  207.6 12.1 %collective-permute-start.52 = (bf16[192,1024]{1,0:T(8,128)(2,1)S(1)}, bf16[192,1024]{1,0:T(8,128)(2,1)S(1)}, u32[]{:S(2)}, u32[]{:S(2)}) collective-permute-start(bf16[192,1024]{1,0:T(8,128)(2,1)S(1)} %pad_maximum_fusion.8), channel_id=1, source_target_pairs={{0,2},{1,3},{2,0},{3,1},{4,6},{5,7},{6,4},{7,5},{8,10},{9,11},{10,... | collective-permute-start | bytes 1179656 | tf_op jit(solution)/shard_map/ppermute | solution.py:35
  209.7 26.1 %collective-permute-start.39 = (bf16[128,2048]{1,0:T(8,128)(2,1)S(1)}, bf16[128,2048]{1,0:T(8,128)(2,1)S(1)}, u32[]{:S(2)}, u32[]{:S(2)}) collective-permute-start(bf16[128,2048]{1,0:T(8,128)(2,1)S(1)} %gather.4), channel_id=1, source_target_pairs={{0,16},{4,20},{8,24},{12,28},{16,0},{20,4},{24,8},{28,12},{1,17},{... | collective-permute-start | bytes 1572872 | tf_op jit(solution)/shard_map/ppermute | solution.py:35
  210.8 10.4 %collective-permute-start.47 = (bf16[128,1024]{1,0:T(8,128)(2,1)S(1)}, bf16[128,1024]{1,0:T(8,128)(2,1)S(1)}, u32[]{:S(2)}, u32[]{:S(2)}) collective-permute-start(bf16[128,1024]{1,0:T(8,128)(2,1)S(1)} %get-tuple-element.179), channel_id=1, source_target_pairs={{0,1},{1,0},{2,3},{3,2},{4,5},{5,4},{6,7},{7,6},{8,9},{9,8},{10,11... | collective-permute-start | bytes 786440 | tf_op jit(solution)/shard_map/ppermute | solution.py:35
  211.4 12.3 %collective-permute-start.48 = (bf16[128,1024]{1,0:T(8,128)(2,1)S(1)}, bf16[128,1024]{1,0:T(8,128)(2,1)S(1)}, u32[]{:S(2)}, u32[]{:S(2)}) collective-permute-start(bf16[128,1024]{1,0:T(8,128)(2,1)S(1)} %get-tuple-element.181), channel_id=1, source_target_pairs={{0,2},{1,3},{2,0},{3,1},{4,6},{5,7},{6,4},{7,5},{8,10},{9,11},{10,... | collective-permute-start | bytes 786440 | tf_op jit(solution)/shard_map/ppermute | solution.py:35
  216.8 7.5 %collective-permute-start.60 = (bf16[96,1024]{1,0:T(8,128)(2,1)S(1)}, bf16[96,1024]{1,0:T(8,128)(2,1)S(1)}, u32[]{:S(2)}, u32[]{:S(2)}) collective-permute-start(bf16[96,1024]{1,0:T(8,128)(2,1)S(1)} %get-tuple-element.201), channel_id=1, source_target_pairs={{0,4},{4,0},{8,12},{12,8},{16,20},{20,16},{24,28},{28,24},{1,5},{5... | collective-permute-start | bytes 589832 | tf_op jit(solution)/shard_map/ppermute | solution.py:35
  221.3 16.5 %collective-permute-start.59 = (bf16[96,1024]{1,0:T(8,128)(2,1)S(1)}, bf16[96,1024]{1,0:T(8,128)(2,1)S(1)}, u32[]{:S(2)}, u32[]{:S(2)}) collective-permute-start(bf16[96,1024]{1,0:T(8,128)(2,1)S(1)} %get-tuple-element.199), channel_id=1, source_target_pairs={{0,4},{4,0},{8,12},{12,8},{16,20},{20,16},{24,28},{28,24},{1,5},{5... | collective-permute-start | bytes 589832 | tf_op jit(solution)/shard_map/ppermute | solution.py:35
  223.7 12.9 %collective-permute-start.57 = (bf16[128,1024]{1,0:T(8,128)(2,1)S(1)}, bf16[128,1024]{1,0:T(8,128)(2,1)S(1)}, u32[]{:S(2)}, u32[]{:S(2)}) collective-permute-start(bf16[128,1024]{1,0:T(8,128)(2,1)S(1)} %get-tuple-element.197), channel_id=1, source_target_pairs={{0,2},{1,3},{2,0},{3,1},{4,6},{5,7},{6,4},{7,5},{8,10},{9,11},{10,... | collective-permute-start | bytes 786440 | tf_op jit(solution)/shard_map/ppermute | solution.py:35
  224.3 13.3 %collective-permute-start.56 = (bf16[128,1024]{1,0:T(8,128)(2,1)S(1)}, bf16[128,1024]{1,0:T(8,128)(2,1)S(1)}, u32[]{:S(2)}, u32[]{:S(2)}) collective-permute-start(bf16[128,1024]{1,0:T(8,128)(2,1)S(1)} %get-tuple-element.195), channel_id=1, source_target_pairs={{0,1},{1,0},{2,3},{3,2},{4,5},{5,4},{6,7},{7,6},{8,9},{9,8},{10,11... | collective-permute-start | bytes 786440 | tf_op jit(solution)/shard_map/ppermute | solution.py:35
  224.9 14.6 %collective-permute-start.64 = (bf16[192,1024]{1,0:T(8,128)(2,1)S(1)}, bf16[192,1024]{1,0:T(8,128)(2,1)S(1)}, u32[]{:S(2)}, u32[]{:S(2)}) collective-permute-start(bf16[192,1024]{1,0:T(8,128)(2,1)S(1)} %pad_maximum_fusion.11), channel_id=1, source_target_pairs={{0,1},{1,0},{2,3},{3,2},{4,5},{5,4},{6,7},{7,6},{8,9},{9,8},{10,11... | collective-permute-start | bytes 1179656 | tf_op jit(solution)/shard_map/ppermute | solution.py:35
  235.8 11.0 %collective-permute-start.61 = (bf16[192,1024]{1,0:T(8,128)(2,1)S(1)}, bf16[192,1024]{1,0:T(8,128)(2,1)S(1)}, u32[]{:S(2)}, u32[]{:S(2)}) collective-permute-start(bf16[192,1024]{1,0:T(8,128)(2,1)S(1)} %pad_maximum_fusion.10), channel_id=1, source_target_pairs={{0,2},{1,3},{2,0},{3,1},{4,6},{5,7},{6,4},{7,5},{8,10},{9,11},{10,... | collective-permute-start | bytes 1179656 | tf_op jit(solution)/shard_map/ppermute | solution.py:35
  236.6 19.2 %collective-permute-start.49 = (bf16[128,2048]{1,0:T(8,128)(2,1)S(1)}, bf16[128,2048]{1,0:T(8,128)(2,1)S(1)}, u32[]{:S(2)}, u32[]{:S(2)}) collective-permute-start(bf16[128,2048]{1,0:T(8,128)(2,1)S(1)} %gather.5), channel_id=1, source_target_pairs={{0,24},{4,28},{8,16},{12,20},{16,8},{20,12},{24,0},{28,4},{1,25},{... | collective-permute-start | bytes 1572872 | tf_op jit(solution)/shard_map/ppermute | solution.py:35
  237.7 24.3 %collective-permute-start.58 = (bf16[128,2048]{1,0:T(8,128)(2,1)S(1)}, bf16[128,2048]{1,0:T(8,128)(2,1)S(1)}, u32[]{:S(2)}, u32[]{:S(2)}) collective-permute-start(bf16[128,2048]{1,0:T(8,128)(2,1)S(1)} %gather.6), channel_id=1, source_target_pairs={{0,8},{4,12},{8,0},{12,4},{16,24},{20,28},{24,16},{28,20},{1,9},{5... | collective-permute-start | bytes 1572872 | tf_op jit(solution)/shard_map/ppermute | solution.py:35
  247.8 7.4 %collective-permute-start.66 = (bf16[128,1024]{1,0:T(8,128)(2,1)S(1)}, bf16[128,1024]{1,0:T(8,128)(2,1)S(1)}, u32[]{:S(2)}, u32[]{:S(2)}) collective-permute-start(bf16[128,1024]{1,0:T(8,128)(2,1)S(1)} %get-tuple-element.212), channel_id=1, source_target_pairs={{0,2},{1,3},{2,0},{3,1},{4,6},{5,7},{6,4},{7,5},{8,10},{9,11},{10,... | collective-permute-start | bytes 786440 | tf_op jit(solution)/shard_map/ppermute | solution.py:35
  (33 other events, 270.3 us)
Sparse Core Ops, SparseCore 0:
  24.2 30.9 all-gather.1

commit v9 on v8

--- a/solution.py
+++ b/solution.py
@@ -242,19 +242,22 @@
 
 
 def combine_kernel(routes, group, capacity, place, routing, *refs):
-    arrived = refs[: sum(len(away) + 1 for _, away in routes)]
-    kept, *outs = refs[len(arrived) :]
-    rows, width = kept.shape[0], arrived[0].shape[1]
+    count = sum(len(away) for _, away in routes)
+    arrived, other, (kept, *outs) = refs[:count], refs[count], refs[count + 1 :]
+    rows, width = kept.shape[0], other.shape[1]
     slots = lax.broadcasted_iota(jnp.int32, (capacity, rows), 0)
+    base = 0
     for side, (near, away) in enumerate(routes):
-        some, arrived = arrived[: len(away) + 1], arrived[len(away) + 1 :]
+        some, arrived = arrived[: len(away)], arrived[len(away) :]
         for at, n in enumerate(near):
             shares, produced = [], []
             for index, a in enumerate(away):
                 for core, (slot, weight) in enumerate(plane_targets(group, place, routing, n, a)):
                     shares.append(jnp.where(slots == slot, weight, 0.0))
-                    piece = some[index + 1] if index else some[core]
-                    first = ((core if index else 0) * len(near) + at) * capacity
+                    first = at * capacity
+                    if core:
+                        first += base + index * len(near) * capacity
+                    piece = other if core else some[index]
                     produced.append(piece[first : first + capacity, :])
             total = lax.dot_general(
                 jnp.concatenate(shares, axis=0).astype(jnp.bfloat16),
@@ -267,6 +270,7 @@
                 outs = outs[1:]
             else:
                 kept[:, side * width : (side + 1) * width] = total
+        base += len(near) * len(away) * capacity
 
 
 def gather_kernel(counts, kept, *refs):
@@ -286,8 +290,8 @@
 def expert_kernel(routes, capacity, *refs):
     count = sum(len(away) for _, away in routes)
     came, (mate, w_gate, w_up, w_down) = refs[:count], refs[count : count + 4]
-    own, other = refs[count + 4 : 2 * count + 4], refs[2 * count + 4 : 3 * count + 4]
-    rows_in, hidden = refs[3 * count + 4 :]
+    outs = refs[count + 4 : 2 * count + 4]
+    rows_in, hidden = refs[2 * count + 4 :]
     width = came[0].shape[1]
     half = rows_in.shape[1] // 2
     places = []
@@ -316,9 +320,10 @@
             product = product.astype(jnp.bfloat16)
             for where, piece, to, at in places:
                 if where == side:
-                    here = slice(to, to + capacity)
-                    own[piece][here, cols] = product[at : at + capacity]
-                    other[piece][here, cols] = product[half + at : half + at + capacity]
+                    out = outs[piece]
+                    out[to : to + capacity, cols] = product[at : at + capacity]
+                    to += out.shape[0] // 2
+                    out[to : to + capacity, cols] = product[half + at : half + at + capacity]
 
 
 def sum_kernel(*refs):
@@ -481,7 +486,6 @@
         for side, (near, _) in enumerate(routes):
             part = far[g][:, side * half : (side + 1) * half]
             sources += [part] + [send(part, n, "whole") for n in near[1:]]
-        last_sources = sources
         outgoing = call(
             functools.partial(dispatch_kernel, routes, g, capacity),
             [bf16((2 * len(near) * capacity, half)) for near, away in routes for _ in away],
@@ -492,44 +496,39 @@
             name="dispatch",
         )
         onward = [a for _, away in routes for a in away]
-        ahead = far[g + 1 : g + 2] if g > 1 else []
-        arrived.append(
-            [send(tie(out, *ahead), a, "picked") if a else out for out, a in zip(outgoing, onward)]
-        )
-
-    produced, mates_before = [], ()
+        arrived.append([send(out, a, "picked") if a else out for out, a in zip(outgoing, onward)])
+
+    def to_mate(parts, *others):
+        halves = [part[part.shape[0] // 2 :] for part in parts]
+        return swap(tie(jnp.concatenate(halves, axis=0), *others), "ctx", 1)
+
+    produced = []
     slots = exp_count * capacity
     for g, came in enumerate(arrived):
-        ahead = last_sources if g == groups - 2 else ()
-        done = [mates for pair in produced[groups - 2 :] for _, mates in pair]
-        mate = jnp.concatenate([part[part.shape[0] // 2 :] for part in came], axis=0)
-        mate = swap(tie(mate, *ahead, *done, *mates_before), "ctx", 1)
-        mates_before = (mate,)
-        made = call(
-            functools.partial(expert_kernel, routes, capacity),
-            [bf16((len(near) * capacity, half)) for near, away in routes for _ in away] * 2,
-            [VMEM] * (len(came) + 4),
-            *came,
-            mate,
-            w_gate[0],
-            w_up[0],
-            w_down[0],
-            name="expert",
-            scratch=[
-                pltpu.VMEM((2, 2 * slots, half), jnp.bfloat16),
-                pltpu.VMEM((2 * slots, w_gate.shape[2]), jnp.bfloat16),
-            ],
-        )
-        own, other = made[: len(came)], made[len(came) :]
-        produced.append([(mine, swap(mates, "ctx", 1)) for mine, mates in zip(own, other)])
+        ready = produced if g >= groups - 2 else []
+        produced.append(
+            call(
+                functools.partial(expert_kernel, routes, capacity),
+                [bf16((2 * len(near) * capacity, half)) for near, away in routes for _ in away],
+                [VMEM] * (len(came) + 4),
+                *came,
+                to_mate(came, *[made[0] for made in ready]),
+                w_gate[0],
+                w_up[0],
+                w_down[0],
+                name="expert",
+                scratch=[
+                    pltpu.VMEM((2, 2 * slots, half), jnp.bfloat16),
+                    pltpu.VMEM((2 * slots, w_gate.shape[2]), jnp.bfloat16),
+                ],
+            )
+        )
 
     totals, hop = [], ()
+    onward_picked = [a for _, away in routes for a in away]
     for g in [*range(2, groups), *(g for g in (1, 0) if g < groups)]:
-        back, pieces = [], iter(produced[g])
-        for _, away in routes:
-            for a in away:
-                pair = next(pieces)
-                back += [send(jnp.concatenate(pair, axis=0), a, "picked")] if a else pair
+        back = [send(p, a, "picked") if a else p for p, a in zip(produced[g], onward_picked)]
+        back.append(to_mate(back))
         onward = [n for near, _ in routes for n in near[1:]]
         kept, *sums = call(
             functools.partial(combine_kernel, routes, g, capacity),

time: 270 us -> 288 us (1.067)
  waiting for transfers between devices: 153 us -> 166 us
  starting transfers between devices: 54.1 us -> 57.8 us
    ppermute x67 -> x55, waiting for transfers between devices: 150 us -> 163 us  [swap(): return lax.ppermute(array, axis, pairs)]
    ppermute x67 -> x55, starting transfers between devices: 54.1 us -> 57.8 us  [swap(): return lax.ppermute(array, axis, pairs)]
  transfers between devices with their start and end apart: 68 -> 56, of which waited for: 37 -> 33; matrix products, arithmetic and copies ran while one was open for 1% -> 1% of each run, Pallas kernels for 12% -> 8%
where the time goes in v9:
time: 288 us; the launch traced here: 287 us
  waiting for transfers between devices  166 us (58%)
  starting transfers between devices  57.8 us (20%)
  Pallas kernels  39.7 us (14%)
  between operations  14.2 us (5%)
  local copies, waits for them, and re-layouts  6.26 us (2%)
  other arithmetic  3.07 us (1%)
    ppermute x55, waiting for transfers between devices, swap(): return lax.ppermute(array, axis, pairs)  163 us
    ppermute x55, starting transfers between devices, swap(): return lax.ppermute(array, axis, pairs)  57.8 us
    pallas_call x27, Pallas kernels, call(): pl.pallas_call(kernel, out_shape=out_shape, in_specs=specs, out_specs=jax...  39.7 us
  transfers between devices with their start and end apart: 56, of which 33 were waited for; matrix products, arithmetic and copies ran while one was open for 1% of the time, Pallas kernels for 8%

profile of v9, /device:TPU:0, one launch (start us, length us, event | category | flops | bytes accessed | tf_op | source)
XLA Modules:
  0.0 287.4 jit_solution(1179437059624511749)
XLA Ops:
  8.2 4.5 %own_rows.1 = (bf16[144,256]{1,0:T(8,128)(2,1)}, bf16[144,256]{1,0:T(8,128)(2,1)}, bf16[144,256]{1,0:T(8,128)(2,1)}, bf16[144,256]{1,0:T(8,128)(2,1)}) custom-call(s32[6]{0:T(128)} %pad_add_fusion.place, s32[8,128]{1,0:T(8,128)} %bitcast.38, s32[8,128]{1,0:T(8,128)} %bitcast.39, bf16[128,2048]{1,0:T(8,128)(2,1)} %tokens.1, f32[1,2048]{1,0:T(1,128)} %bitcast.34, ...), custom_call_target="tpu_custom_call" | custom-call | flops 1000 | bytes 1000 | tf_op jit(solution)/shard_map/own_rows/pallas_call | solution.py:338
  12.7 3.0 %collective-permute-start = (bf16[144,256]{1,0:T(8,128)(2,1)}, bf16[144,256]{1,0:T(8,128)(2,1)S(1)}, u32[]{:S(2)}, u32[]{:S(2)}) collective-permute-start(bf16[144,256]{1,0:T(8,128)(2,1)} %get-tuple-element.90), channel_id=1, source_target_pairs={{0,1},{1,0},{2,3},{3,2},{4,5},{5,4},{6,7},{7,6},{8,9},{9,8},{10,11... | collective-permute-start | bytes 221192 | tf_op jit(solution)/shard_map/ppermute | solution.py:35
  18.5 1.7 collective-permute-done.1
  20.3 2.4 collective-permute-done.2
  25.2 2.5 collective-permute-start.5
  28.7 10.4 %collective-permute-done.3.refs_1_ = bf16[128,2048]{1,0:T(8,128)(2,1)S(1)} collective-permute-done((bf16[128,2048]{1,0:T(8,128)(2,1)S(1)}, bf16[128,2048]{1,0:T(8,128)(2,1)S(1)}, u32[]{:S(2)}, u32[]{:S(2)}) %collective-permute-start.3) | collective-permute-done | bytes 524320 | tf_op jit(solution)/shard_map/ppermute | solution.py:35
  39.1 9.1 %collective-permute-done.4.refs_2_ = bf16[128,2048]{1,0:T(8,128)(2,1)S(1)} collective-permute-done((bf16[128,2048]{1,0:T(8,128)(2,1)S(1)}, bf16[128,2048]{1,0:T(8,128)(2,1)S(1)}, u32[]{:S(2)}, u32[]{:S(2)}) %collective-permute-start.4) | collective-permute-done | bytes 524320 | tf_op jit(solution)/shard_map/ppermute | solution.py:35
  48.1 1.6 copy-done.7
  49.8 1.8 queries.1
  51.7 3.6 %all-gather.2.cloned.1.call-done.both = bf16[4608,256]{1,0:T(8,128)(2,1)} async-done(((bf16[576,256]{1,0:T(8,128)(2,1)}), bf16[4608,256]{1,0:T(8,128)(2,1)}) %all-gather.2.cloned.1.call-update) | async-done | bytes 2359312 | tf_op jit(solution)/shard_map/all_gather | solution.py:407
  55.3 1.7 copy-done.3
  56.9 1.7 attention.4
  58.6 2.4 collective-permute-start.6
  61.1 1.7 attention.5
  63.4 1.7 attention.6
  65.8 1.9 attention.7.refs_0_
  67.7 6.8 %collective-permute-done.6.refs_1_ = bf16[128,2048]{1,0:T(8,128)(2,1)S(1)} collective-permute-done((bf16[128,2048]{1,0:T(8,128)(2,1)S(1)}, bf16[128,2048]{1,0:T(8,128)(2,1)S(1)}, u32[]{:S(2)}, u32[]{:S(2)}) %collective-permute-start.6) | collective-permute-done | bytes 524320 | tf_op jit(solution)/shard_map/ppermute | solution.py:35
  74.6 11.0 %collective-permute-done.7.refs_1_ = bf16[128,2048]{1,0:T(8,128)(2,1)S(1)} collective-permute-done((bf16[128,2048]{1,0:T(8,128)(2,1)S(1)}, bf16[128,2048]{1,0:T(8,128)(2,1)S(1)}, u32[]{:S(2)}, u32[]{:S(2)}) %collective-permute-start.7) | collective-permute-done | bytes 524320 | tf_op jit(solution)/shard_map/ppermute | solution.py:35
  86.2 2.5 collective-permute-start.10
  91.5 5.2 %collective-permute-start.9 = (bf16[128,2048]{1,0:T(8,128)(2,1)S(1)}, bf16[128,2048]{1,0:T(8,128)(2,1)S(1)}, u32[]{:S(2)}, u32[]{:S(2)}) collective-permute-start(bf16[128,2048]{1,0:T(8,128)(2,1)S(1)} %get-tuple-element.99), channel_id=1, source_target_pairs={{0,16},{4,20},{8,24},{12,28},{16,0},{20,4},{24,8},{28,12},{1,17},{... | collective-permute-start | bytes 1572872 | tf_op jit(solution)/shard_map/ppermute | solution.py:35
  101.0 9.4 %collective-permute-done.10 = bf16[128,2048]{1,0:T(8,128)(2,1)S(1)} collective-permute-done((bf16[128,2048]{1,0:T(8,128)(2,1)S(1)}, bf16[128,2048]{1,0:T(8,128)(2,1)S(1)}, u32[]{:S(2)}, u32[]{:S(2)}) %collective-permute-start.10) | collective-permute-done | bytes 524320 | tf_op jit(solution)/shard_map/ppermute | solution.py:35
  110.4 2.4 collective-permute-start.12
  113.1 5.7 %collective-permute-done.12.refs_1_ = bf16[128,1024]{1,0:T(8,128)(2,1)S(1)} collective-permute-done((bf16[128,1024]{1,0:T(8,128)(2,1)S(1)}, bf16[128,1024]{1,0:T(8,128)(2,1)S(1)}, u32[]{:S(2)}, u32[]{:S(2)}) %collective-permute-start.12) | collective-permute-done | bytes 262176 | tf_op jit(solution)/shard_map/ppermute | solution.py:35
  122.6 1.7 collective-permute-start.13
  124.3 9.2 %collective-permute-done.21.refs_3_ = bf16[192,1024]{1,0:T(8,128)(2,1)S(1)} collective-permute-done((bf16[192,1024]{1,0:T(8,128)(2,1)S(1)}, bf16[192,1024]{1,0:T(8,128)(2,1)S(1)}, u32[]{:S(2)}, u32[]{:S(2)}) %collective-permute-start.21) | collective-permute-done | bytes 393248 | tf_op jit(solution)/shard_map/ppermute | solution.py:35
  134.1 2.4 collective-permute-done.13.refs_1_
  136.5 4.2 %collective-permute-done.16.refs_3_ = bf16[128,1024]{1,0:T(8,128)(2,1)S(1)} collective-permute-done((bf16[128,1024]{1,0:T(8,128)(2,1)S(1)}, bf16[128,1024]{1,0:T(8,128)(2,1)S(1)}, u32[]{:S(2)}, u32[]{:S(2)}) %collective-permute-start.16) | collective-permute-done | bytes 262176 | tf_op jit(solution)/shard_map/ppermute | solution.py:35
  142.1 2.0 collective-permute-start.27
  144.1 2.0 collective-permute-start.28
  146.1 3.9 %expert.4 = (bf16[192,1024]{1,0:T(8,128)(2,1)S(1)}, bf16[192,1024]{1,0:T(8,128)(2,1)S(1)}, bf16[192,1024]{1,0:T(8,128)(2,1)S(1)}, bf16[192,1024]{1,0:T(8,128)(2,1)S(1)}) custom-call(bf16[192,1024]{1,0:T(8,128)(2,1)S(1)} %get-tuple-element.116.refs_0_, bf16[192,1024]{1,0:T(8,128)(2,1)S(1)} %collective-permute-done.17.refs_1_, ...), custom_call_target="tpu_custom_call" | custom-call | flops 1000 | bytes 1000 | tf_op jit(solution)/shard_map/expert/pallas_call | solution.py:338
  151.2 3.9 %expert.5 = (bf16[192,1024]{1,0:T(8,128)(2,1)S(1)}, bf16[192,1024]{1,0:T(8,128)(2,1)S(1)}, bf16[192,1024]{1,0:T(8,128)(2,1)S(1)}, bf16[192,1024]{1,0:T(8,128)(2,1)S(1)}) custom-call(bf16[192,1024]{1,0:T(8,128)(2,1)S(1)} %get-tuple-element.119.refs_0_, bf16[192,1024]{1,0:T(8,128)(2,1)S(1)} %collective-permute-done.18.refs_1_, ...), custom_call_target="tpu_custom_call" | custom-call | flops 1000 | bytes 1000 | tf_op jit(solution)/shard_map/expert/pallas_call | solution.py:338
  158.3 9.6 %collective-permute-done.31.refs_3_ = bf16[192,1024]{1,0:T(8,128)(2,1)S(1)} collective-permute-done((bf16[192,1024]{1,0:T(8,128)(2,1)S(1)}, bf16[192,1024]{1,0:T(8,128)(2,1)S(1)}, u32[]{:S(2)}, u32[]{:S(2)}) %collective-permute-start.31) | collective-permute-done | bytes 393248 | tf_op jit(solution)/shard_map/ppermute | solution.py:35
  168.2 4.1 %expert.6 = (bf16[192,1024]{1,0:T(8,128)(2,1)S(1)}, bf16[192,1024]{1,0:T(8,128)(2,1)S(1)}, bf16[192,1024]{1,0:T(8,128)(2,1)S(1)}, bf16[192,1024]{1,0:T(8,128)(2,1)S(1)}) custom-call(bf16[192,1024]{1,0:T(8,128)(2,1)S(1)} %get-tuple-element.104.refs_0_, bf16[192,1024]{1,0:T(8,128)(2,1)S(1)} %collective-permute-done.19.refs_1_, ...), custom_call_target="tpu_custom_call" | custom-call | flops 1000 | bytes 1000 | tf_op jit(solution)/shard_map/expert/pallas_call | solution.py:338
  172.4 1.6 collective-permute-start.32
  174.4 9.6 %collective-permute-done.32.refs_3_ = bf16[192,1024]{1,0:T(8,128)(2,1)S(1)} collective-permute-done((bf16[192,1024]{1,0:T(8,128)(2,1)S(1)}, bf16[192,1024]{1,0:T(8,128)(2,1)S(1)}, u32[]{:S(2)}, u32[]{:S(2)}) %collective-permute-start.32) | collective-permute-done | bytes 393248 | tf_op jit(solution)/shard_map/ppermute | solution.py:35
  185.2 3.9 %expert.7 = (bf16[192,1024]{1,0:T(8,128)(2,1)S(1)}, bf16[192,1024]{1,0:T(8,128)(2,1)S(1)}, bf16[192,1024]{1,0:T(8,128)(2,1)S(1)}, bf16[192,1024]{1,0:T(8,128)(2,1)S(1)}) custom-call(bf16[192,1024]{1,0:T(8,128)(2,1)S(1)} %get-tuple-element.140.refs_0_, bf16[192,1024]{1,0:T(8,128)(2,1)S(1)} %collective-permute-done.29.refs_1_, ...), custom_call_target="tpu_custom_call" | custom-call | flops 1000 | bytes 1000 | tf_op jit(solution)/shard_map/expert/pallas_call | solution.py:338
  191.2 8.3 %collective-permute-done.38.refs_1_ = bf16[192,1024]{1,0:T(8,128)(2,1)S(1)} collective-permute-done((bf16[192,1024]{1,0:T(8,128)(2,1)S(1)}, bf16[192,1024]{1,0:T(8,128)(2,1)S(1)}, u32[]{:S(2)}, u32[]{:S(2)}) %collective-permute-start.38) | collective-permute-done | bytes 393248 | tf_op jit(solution)/shard_map/ppermute | solution.py:35
  203.3 5.6 %collective-permute-done.44.refs_1_ = bf16[192,1024]{1,0:T(8,128)(2,1)S(1)} collective-permute-done((bf16[192,1024]{1,0:T(8,128)(2,1)S(1)}, bf16[192,1024]{1,0:T(8,128)(2,1)S(1)}, u32[]{:S(2)}, u32[]{:S(2)}) %collective-permute-start.44) | collective-permute-done | bytes 393248 | tf_op jit(solution)/shard_map/ppermute | solution.py:35
  209.6 2.5 collective-permute-done.45.refs_3_
  213.6 4.0 %collective-permute-done.34.refs_0_ = bf16[128,1024]{1,0:T(8,128)(2,1)S(1)} collective-permute-done((bf16[128,1024]{1,0:T(8,128)(2,1)S(1)}, bf16[128,1024]{1,0:T(8,128)(2,1)S(1)}, u32[]{:S(2)}, u32[]{:S(2)}) %collective-permute-start.34) | collective-permute-done | bytes 262176 | tf_op jit(solution)/shard_map/ppermute | solution.py:35
  219.2 4.8 %collective-permute-done.35.refs_1_ = bf16[128,1024]{1,0:T(8,128)(2,1)S(1)} collective-permute-done((bf16[128,1024]{1,0:T(8,128)(2,1)S(1)}, bf16[128,1024]{1,0:T(8,128)(2,1)S(1)}, u32[]{:S(2)}, u32[]{:S(2)}) %collective-permute-start.35) | collective-permute-done | bytes 262176 | tf_op jit(solution)/shard_map/ppermute | solution.py:35
  230.4 3.7 %collective-permute-done.41.refs_0_ = bf16[128,1024]{1,0:T(8,128)(2,1)S(1)} collective-permute-done((bf16[128,1024]{1,0:T(8,128)(2,1)S(1)}, bf16[128,1024]{1,0:T(8,128)(2,1)S(1)}, u32[]{:S(2)}, u32[]{:S(2)}) %collective-permute-start.41) | collective-permute-done | bytes 262176 | tf_op jit(solution)/shard_map/ppermute | solution.py:35
  237.6 15.4 %collective-permute-done.36.refs_1_ = bf16[128,2048]{1,0:T(8,128)(2,1)S(1)} collective-permute-done((bf16[128,2048]{1,0:T(8,128)(2,1)S(1)}, bf16[128,2048]{1,0:T(8,128)(2,1)S(1)}, u32[]{:S(2)}, u32[]{:S(2)}) %collective-permute-start.36) | collective-permute-done | bytes 524320 | tf_op jit(solution)/shard_map/ppermute | solution.py:35
  253.0 2.3 collective-permute-start.43
  257.4 1.7 collective-permute-start.54
  259.1 5.4 %collective-permute-done.53.refs_0_ = bf16[128,1024]{1,0:T(8,128)(2,1)S(1)} collective-permute-done((bf16[128,1024]{1,0:T(8,128)(2,1)S(1)}, bf16[128,1024]{1,0:T(8,128)(2,1)S(1)}, u32[]{:S(2)}, u32[]{:S(2)}) %collective-permute-start.53) | collective-permute-done | bytes 262176 | tf_op jit(solution)/shard_map/ppermute | solution.py:35
  265.2 4.4 %collective-permute-done.43.refs_2_ = bf16[128,2048]{1,0:T(8,128)(2,1)S(1)} collective-permute-done((bf16[128,2048]{1,0:T(8,128)(2,1)S(1)}, bf16[128,2048]{1,0:T(8,128)(2,1)S(1)}, u32[]{:S(2)}, u32[]{:S(2)}) %collective-permute-start.43) | collective-permute-done | bytes 524320 | tf_op jit(solution)/shard_map/ppermute | solution.py:35
  269.7 9.8 %collective-permute-done.49.refs_3_ = bf16[128,2048]{1,0:T(8,128)(2,1)S(1)} collective-permute-done((bf16[128,2048]{1,0:T(8,128)(2,1)S(1)}, bf16[128,2048]{1,0:T(8,128)(2,1)S(1)}, u32[]{:S(2)}, u32[]{:S(2)}) %collective-permute-start.49) | collective-permute-done | bytes 524320 | tf_op jit(solution)/shard_map/ppermute | solution.py:35
  (181 shorter events, 52.5 us)
Async XLA Ops:
  6.5 48.7 %all-gather.2.cloned.1.call-start = ((), (), s32[]{:S(2)}) async-start(), calls=%async_computation | async-start | bytes 2654208 | tf_op jit(solution)/shard_map/all_gather | solution.py:407
  24.1 14.9 %collective-permute-start.3 = (bf16[128,2048]{1,0:T(8,128)(2,1)S(1)}, bf16[128,2048]{1,0:T(8,128)(2,1)S(1)}, u32[]{:S(2)}, u32[]{:S(2)}) collective-permute-start(bf16[128,2048]{1,0:T(8,128)(2,1)S(1)} %copy-done.6), channel_id=1, source_target_pairs={{0,1},{1,0},{2,3},{3,2},{4,5},{5,4},{6,7},{7,6},{8,9},{9,8},{10,11... | collective-permute-start | bytes 1572872 | tf_op jit(solution)/shard_map/ppermute | solution.py:35
  24.7 23.4 %collective-permute-start.4 = (bf16[128,2048]{1,0:T(8,128)(2,1)S(1)}, bf16[128,2048]{1,0:T(8,128)(2,1)S(1)}, u32[]{:S(2)}, u32[]{:S(2)}) collective-permute-start(bf16[128,2048]{1,0:T(8,128)(2,1)S(1)} %copy-done.6), channel_id=1, source_target_pairs={{0,2},{1,3},{2,0},{3,1},{4,6},{5,7},{6,4},{7,5},{8,10},{9,11},{10,... | collective-permute-start | bytes 1572872 | tf_op jit(solution)/shard_map/ppermute | solution.py:35
  25.2 22.9 %collective-permute-start.5 = (bf16[128,2048]{1,0:T(8,128)(2,1)S(1)}, bf16[128,2048]{1,0:T(8,128)(2,1)S(1)}, u32[]{:S(2)}, u32[]{:S(2)}) collective-permute-start(bf16[128,2048]{1,0:T(8,128)(2,1)S(1)} %copy-done.6), channel_id=1, source_target_pairs={{0,3},{1,2},{2,1},{3,0},{4,7},{5,6},{6,5},{7,4},{8,11},{9,10},{10,... | collective-permute-start | bytes 1572872 | tf_op jit(solution)/shard_map/ppermute | solution.py:35
  58.6 15.9 %collective-permute-start.6 = (bf16[128,2048]{1,0:T(8,128)(2,1)S(1)}, bf16[128,2048]{1,0:T(8,128)(2,1)S(1)}, u32[]{:S(2)}, u32[]{:S(2)}) collective-permute-start(bf16[128,2048]{1,0:T(8,128)(2,1)S(1)} %attention.4), channel_id=1, source_target_pairs={{0,3},{1,2},{2,1},{3,0},{4,7},{5,6},{6,5},{7,4},{8,11},{9,10},{10,... | collective-permute-start | bytes 1572872 | tf_op jit(solution)/shard_map/ppermute | solution.py:35
  62.8 22.9 %collective-permute-start.7 = (bf16[128,2048]{1,0:T(8,128)(2,1)S(1)}, bf16[128,2048]{1,0:T(8,128)(2,1)S(1)}, u32[]{:S(2)}, u32[]{:S(2)}) collective-permute-start(bf16[128,2048]{1,0:T(8,128)(2,1)S(1)} %attention.5), channel_id=1, source_target_pairs={{0,1},{1,0},{2,3},{3,2},{4,5},{5,4},{6,7},{7,6},{8,9},{9,8},{10,11... | collective-permute-start | bytes 1572872 | tf_op jit(solution)/shard_map/ppermute | solution.py:35
  65.2 20.7 %collective-permute-start.8 = (bf16[128,2048]{1,0:T(8,128)(2,1)S(1)}, bf16[128,2048]{1,0:T(8,128)(2,1)S(1)}, u32[]{:S(2)}, u32[]{:S(2)}) collective-permute-start(bf16[128,2048]{1,0:T(8,128)(2,1)S(1)} %attention.6), channel_id=1, source_target_pairs={{0,2},{1,3},{2,0},{3,1},{4,6},{5,7},{6,4},{7,5},{8,10},{9,11},{10,... | collective-permute-start | bytes 1572872 | tf_op jit(solution)/shard_map/ppermute | solution.py:35
  86.2 24.2 %collective-permute-start.10 = (bf16[128,2048]{1,0:T(8,128)(2,1)S(1)}, bf16[128,2048]{1,0:T(8,128)(2,1)S(1)}, u32[]{:S(2)}, u32[]{:S(2)}) collective-permute-start(bf16[128,2048]{1,0:T(8,128)(2,1)S(1)} %get-tuple-element.99), channel_id=1, source_target_pairs={{0,8},{4,12},{8,0},{12,4},{16,24},{20,28},{24,16},{28,20},{1,9},{5... | collective-permute-start | bytes 1572872 | tf_op jit(solution)/shard_map/ppermute | solution.py:35
  88.8 8.1 %collective-permute-start.11 = (bf16[128,1024]{1,0:T(8,128)(2,1)S(1)}, bf16[128,1024]{1,0:T(8,128)(2,1)S(1)}, u32[]{:S(2)}, u32[]{:S(2)}) collective-permute-start(bf16[128,1024]{1,0:T(8,128)(2,1)S(1)} %get-tuple-element.178.refs_0_), channel_id=1, source_target_pairs={{0,1},{1,0},{2,3},{3,2},{4,5},{5,4},{6,7},{7,6},{8,9},{9,8},{10,11... | collective-permute-start | bytes 786440 | tf_op jit(solution)/shard_map/ppermute | solution.py:35
  91.5 30.7 %collective-permute-start.9 = (bf16[128,2048]{1,0:T(8,128)(2,1)S(1)}, bf16[128,2048]{1,0:T(8,128)(2,1)S(1)}, u32[]{:S(2)}, u32[]{:S(2)}) collective-permute-start(bf16[128,2048]{1,0:T(8,128)(2,1)S(1)} %get-tuple-element.99), channel_id=1, source_target_pairs={{0,16},{4,20},{8,24},{12,28},{16,0},{20,4},{24,8},{28,12},{1,17},{... | collective-permute-start | bytes 1572872 | tf_op jit(solution)/shard_map/ppermute | solution.py:35
  99.2 22.7 %collective-permute-start.17 = (bf16[192,1024]{1,0:T(8,128)(2,1)S(1)}, bf16[192,1024]{1,0:T(8,128)(2,1)S(1)}, u32[]{:S(2)}, u32[]{:S(2)}) collective-permute-start(bf16[192,1024]{1,0:T(8,128)(2,1)S(1)} %get-tuple-element.107), channel_id=1, source_target_pairs={{0,2},{1,3},{2,0},{3,1},{4,6},{5,7},{6,4},{7,5},{8,10},{9,11},{10,... | collective-permute-start | bytes 1179656 | tf_op jit(solution)/shard_map/ppermute | solution.py:35
  100.4 21.0 %collective-permute-start.20 = (bf16[192,1024]{1,0:T(8,128)(2,1)S(1)}, bf16[192,1024]{1,0:T(8,128)(2,1)S(1)}, u32[]{:S(2)}, u32[]{:S(2)}) collective-permute-start(bf16[192,1024]{1,0:T(8,128)(2,1)S(1)} %get-tuple-element.113), channel_id=1, source_target_pairs={{0,1},{1,0},{2,3},{3,2},{4,5},{5,4},{6,7},{7,6},{8,9},{9,8},{10,11... | collective-permute-start | bytes 1179656 | tf_op jit(solution)/shard_map/ppermute | solution.py:35
  110.4 8.4 %collective-permute-start.12 = (bf16[128,1024]{1,0:T(8,128)(2,1)S(1)}, bf16[128,1024]{1,0:T(8,128)(2,1)S(1)}, u32[]{:S(2)}, u32[]{:S(2)}) collective-permute-start(bf16[128,1024]{1,0:T(8,128)(2,1)S(1)} %get-tuple-element.100.refs_0_), channel_id=1, source_target_pairs={{0,1},{1,0},{2,3},{3,2},{4,5},{5,4},{6,7},{7,6},{8,9},{9,8},{10,11... | collective-permute-start | bytes 786440 | tf_op jit(solution)/shard_map/ppermute | solution.py:35
  121.4 12.1 %collective-permute-start.21 = (bf16[192,1024]{1,0:T(8,128)(2,1)S(1)}, bf16[192,1024]{1,0:T(8,128)(2,1)S(1)}, u32[]{:S(2)}, u32[]{:S(2)}) collective-permute-start(bf16[192,1024]{1,0:T(8,128)(2,1)S(1)} %get-tuple-element.114), channel_id=1, source_target_pairs={{0,1},{1,0},{2,3},{3,2},{4,5},{5,4},{6,7},{7,6},{8,9},{9,8},{10,11... | collective-permute-start | bytes 1179656 | tf_op jit(solution)/shard_map/ppermute | solution.py:35
  121.9 12.0 %collective-permute-start.18 = (bf16[192,1024]{1,0:T(8,128)(2,1)S(1)}, bf16[192,1024]{1,0:T(8,128)(2,1)S(1)}, u32[]{:S(2)}, u32[]{:S(2)}) collective-permute-start(bf16[192,1024]{1,0:T(8,128)(2,1)S(1)} %get-tuple-element.108), channel_id=1, source_target_pairs={{0,2},{1,3},{2,0},{3,1},{4,6},{5,7},{6,4},{7,5},{8,10},{9,11},{10,... | collective-permute-start | bytes 1179656 | tf_op jit(solution)/shard_map/ppermute | solution.py:35
  122.3 19.7 %collective-permute-start.26 = (bf16[128,2048]{1,0:T(8,128)(2,1)S(1)}, bf16[128,2048]{1,0:T(8,128)(2,1)S(1)}, u32[]{:S(2)}, u32[]{:S(2)}) collective-permute-start(bf16[128,2048]{1,0:T(8,128)(2,1)S(1)} %collective-permute-done.9), channel_id=1, source_target_pairs={{0,8},{4,12},{8,0},{12,4},{16,24},{20,28},{24,16},{28,20},{1,9},{5... | collective-permute-start | bytes 1572872 | tf_op jit(solution)/shard_map/ppermute | solution.py:35
  122.5 21.6 %collective-permute-start.23 = (bf16[384,1024]{1,0:T(8,128)(2,1)S(1)}, bf16[384,1024]{1,0:T(8,128)(2,1)S(1)}, u32[]{:S(2)}, u32[]{:S(2)}) collective-permute-start(bf16[384,1024]{1,0:T(8,128)(2,1)S(1)} %pad_maximum_fusion.1), channel_id=1, source_target_pairs={{0,4},{4,0},{8,12},{12,8},{16,20},{20,16},{24,28},{28,24},{1,5},{5... | collective-permute-start | bytes 2359304 | tf_op jit(solution)/shard_map/ppermute | solution.py:35
  122.6 14.0 %collective-permute-start.13 = (bf16[128,1024]{1,0:T(8,128)(2,1)S(1)}, bf16[128,1024]{1,0:T(8,128)(2,1)S(1)}, u32[]{:S(2)}, u32[]{:S(2)}) collective-permute-start(bf16[128,1024]{1,0:T(8,128)(2,1)S(1)} %get-tuple-element.101.refs_0_), channel_id=1, source_target_pairs={{0,1},{1,0},{2,3},{3,2},{4,5},{5,4},{6,7},{7,6},{8,9},{9,8},{10,11... | collective-permute-start | bytes 786440 | tf_op jit(solution)/shard_map/ppermute | solution.py:35
  134.0 17.2 %collective-permute-start.24 = (bf16[384,1024]{1,0:T(8,128)(2,1)S(1)}, bf16[384,1024]{1,0:T(8,128)(2,1)S(1)}, u32[]{:S(2)}, u32[]{:S(2)}) collective-permute-start(bf16[384,1024]{1,0:T(8,128)(2,1)S(1)} %pad_maximum_fusion.2), channel_id=1, source_target_pairs={{0,4},{4,0},{8,12},{12,8},{16,20},{20,16},{24,28},{28,24},{1,5},{5... | collective-permute-start | bytes 2359304 | tf_op jit(solution)/shard_map/ppermute | solution.py:35
  141.8 8.2 %collective-permute-start.22 = (bf16[192,1024]{1,0:T(8,128)(2,1)S(1)}, bf16[192,1024]{1,0:T(8,128)(2,1)S(1)}, u32[]{:S(2)}, u32[]{:S(2)}) collective-permute-start(bf16[192,1024]{1,0:T(8,128)(2,1)S(1)} %get-tuple-element.115), channel_id=1, source_target_pairs={{0,1},{1,0},{2,3},{3,2},{4,5},{5,4},{6,7},{7,6},{8,9},{9,8},{10,11... | collective-permute-start | bytes 1179656 | tf_op jit(solution)/shard_map/ppermute | solution.py:35
  141.9 9.3 %collective-permute-start.19 = (bf16[192,1024]{1,0:T(8,128)(2,1)S(1)}, bf16[192,1024]{1,0:T(8,128)(2,1)S(1)}, u32[]{:S(2)}, u32[]{:S(2)}) collective-permute-start(bf16[192,1024]{1,0:T(8,128)(2,1)S(1)} %get-tuple-element.109), channel_id=1, source_target_pairs={{0,2},{1,3},{2,0},{3,1},{4,6},{5,7},{6,4},{7,5},{8,10},{9,11},{10,... | collective-permute-start | bytes 1179656 | tf_op jit(solution)/shard_map/ppermute | solution.py:35
  142.1 13.1 %collective-permute-start.27 = (bf16[128,1024]{1,0:T(8,128)(2,1)S(1)}, bf16[128,1024]{1,0:T(8,128)(2,1)S(1)}, u32[]{:S(2)}, u32[]{:S(2)}) collective-permute-start(bf16[128,1024]{1,0:T(8,128)(2,1)S(1)} %get-tuple-element.125.refs_0_), channel_id=1, source_target_pairs={{0,1},{1,0},{2,3},{3,2},{4,5},{5,4},{6,7},{7,6},{8,9},{9,8},{10,11... | collective-permute-start | bytes 786440 | tf_op jit(solution)/shard_map/ppermute | solution.py:35
  144.1 11.2 %collective-permute-start.28 = (bf16[128,1024]{1,0:T(8,128)(2,1)S(1)}, bf16[128,1024]{1,0:T(8,128)(2,1)S(1)}, u32[]{:S(2)}, u32[]{:S(2)}) collective-permute-start(bf16[128,1024]{1,0:T(8,128)(2,1)S(1)} %get-tuple-element.126.refs_2_), channel_id=1, source_target_pairs={{0,2},{1,3},{2,0},{3,1},{4,6},{5,7},{6,4},{7,5},{8,10},{9,11},{10,... | collective-permute-start | bytes 786440 | tf_op jit(solution)/shard_map/ppermute | solution.py:35
  155.1 13.1 %collective-permute-start.25 = (bf16[384,1024]{1,0:T(8,128)(2,1)S(1)}, bf16[384,1024]{1,0:T(8,128)(2,1)S(1)}, u32[]{:S(2)}, u32[]{:S(2)}) collective-permute-start(bf16[384,1024]{1,0:T(8,128)(2,1)S(1)} %pad_maximum_fusion), channel_id=1, source_target_pairs={{0,4},{4,0},{8,12},{12,8},{16,20},{20,16},{24,28},{28,24},{1,5},{5... | collective-permute-start | bytes 2359304 | tf_op jit(solution)/shard_map/ppermute | solution.py:35
  156.3 11.6 %collective-permute-start.31 = (bf16[192,1024]{1,0:T(8,128)(2,1)S(1)}, bf16[192,1024]{1,0:T(8,128)(2,1)S(1)}, u32[]{:S(2)}, u32[]{:S(2)}) collective-permute-start(bf16[192,1024]{1,0:T(8,128)(2,1)S(1)} %get-tuple-element.133), channel_id=1, source_target_pairs={{0,1},{1,0},{2,3},{3,2},{4,5},{5,4},{6,7},{7,6},{8,9},{9,8},{10,11... | collective-permute-start | bytes 1179656 | tf_op jit(solution)/shard_map/ppermute | solution.py:35
  156.9 11.2 %collective-permute-start.29 = (bf16[192,1024]{1,0:T(8,128)(2,1)S(1)}, bf16[192,1024]{1,0:T(8,128)(2,1)S(1)}, u32[]{:S(2)}, u32[]{:S(2)}) collective-permute-start(bf16[192,1024]{1,0:T(8,128)(2,1)S(1)} %get-tuple-element.128), channel_id=1, source_target_pairs={{0,2},{1,3},{2,0},{3,1},{4,6},{5,7},{6,4},{7,5},{8,10},{9,11},{10,... | collective-permute-start | bytes 1179656 | tf_op jit(solution)/shard_map/ppermute | solution.py:35
  172.3 12.9 %collective-permute-start.37 = (bf16[384,1024]{1,0:T(8,128)(2,1)S(1)}, bf16[384,1024]{1,0:T(8,128)(2,1)S(1)}, u32[]{:S(2)}, u32[]{:S(2)}) collective-permute-start(bf16[384,1024]{1,0:T(8,128)(2,1)S(1)} %pad_maximum_fusion.4), channel_id=1, source_target_pairs={{0,4},{4,0},{8,12},{12,8},{16,20},{20,16},{24,28},{28,24},{1,5},{5... | collective-permute-start | bytes 2359304 | tf_op jit(solution)/shard_map/ppermute | solution.py:35
  172.4 11.5 %collective-permute-start.32 = (bf16[192,1024]{1,0:T(8,128)(2,1)S(1)}, bf16[192,1024]{1,0:T(8,128)(2,1)S(1)}, u32[]{:S(2)}, u32[]{:S(2)}) collective-permute-start(bf16[192,1024]{1,0:T(8,128)(2,1)S(1)} %get-tuple-element.134), channel_id=1, source_target_pairs={{0,1},{1,0},{2,3},{3,2},{4,5},{5,4},{6,7},{7,6},{8,9},{9,8},{10,11... | collective-permute-start | bytes 1179656 | tf_op jit(solution)/shard_map/ppermute | solution.py:35
  174.0 11.2 %collective-permute-start.30 = (bf16[192,1024]{1,0:T(8,128)(2,1)S(1)}, bf16[192,1024]{1,0:T(8,128)(2,1)S(1)}, u32[]{:S(2)}, u32[]{:S(2)}) collective-permute-start(bf16[192,1024]{1,0:T(8,128)(2,1)S(1)} %get-tuple-element.129), channel_id=1, source_target_pairs={{0,2},{1,3},{2,0},{3,1},{4,6},{5,7},{6,4},{7,5},{8,10},{9,11},{10,... | collective-permute-start | bytes 1179656 | tf_op jit(solution)/shard_map/ppermute | solution.py:35
  189.1 10.4 %collective-permute-start.38 = (bf16[192,1024]{1,0:T(8,128)(2,1)S(1)}, bf16[192,1024]{1,0:T(8,128)(2,1)S(1)}, u32[]{:S(2)}, u32[]{:S(2)}) collective-permute-start(bf16[192,1024]{1,0:T(8,128)(2,1)S(1)} %get-tuple-element.145), channel_id=1, source_target_pairs={{0,2},{1,3},{2,0},{3,1},{4,6},{5,7},{6,4},{7,5},{8,10},{9,11},{10,... | collective-permute-start | bytes 1179656 | tf_op jit(solution)/shard_map/ppermute | solution.py:35
  189.5 10.5 %collective-permute-start.39 = (bf16[192,1024]{1,0:T(8,128)(2,1)S(1)}, bf16[192,1024]{1,0:T(8,128)(2,1)S(1)}, u32[]{:S(2)}, u32[]{:S(2)}) collective-permute-start(bf16[192,1024]{1,0:T(8,128)(2,1)S(1)} %get-tuple-element.148), channel_id=1, source_target_pairs={{0,1},{1,0},{2,3},{3,2},{4,5},{5,4},{6,7},{7,6},{8,9},{9,8},{10,11... | collective-permute-start | bytes 1179656 | tf_op jit(solution)/shard_map/ppermute | solution.py:35
  191.1 10.5 %collective-permute-start.33 = (bf16[384,1024]{1,0:T(8,128)(2,1)S(1)}, bf16[384,1024]{1,0:T(8,128)(2,1)S(1)}, u32[]{:S(2)}, u32[]{:S(2)}) collective-permute-start(bf16[384,1024]{1,0:T(8,128)(2,1)S(1)} %pad_maximum_fusion.3), channel_id=1, source_target_pairs={{0,4},{4,0},{8,12},{12,8},{16,20},{20,16},{24,28},{28,24},{1,5},{5... | collective-permute-start | bytes 2359304 | tf_op jit(solution)/shard_map/ppermute | solution.py:35
  199.5 9.4 %collective-permute-start.44 = (bf16[192,1024]{1,0:T(8,128)(2,1)S(1)}, bf16[192,1024]{1,0:T(8,128)(2,1)S(1)}, u32[]{:S(2)}, u32[]{:S(2)}) collective-permute-start(bf16[192,1024]{1,0:T(8,128)(2,1)S(1)} %get-tuple-element.156), channel_id=1, source_target_pairs={{0,2},{1,3},{2,0},{3,1},{4,6},{5,7},{6,4},{7,5},{8,10},{9,11},{10,... | collective-permute-start | bytes 1179656 | tf_op jit(solution)/shard_map/ppermute | solution.py:35
  200.0 12.1 %collective-permute-start.45 = (bf16[192,1024]{1,0:T(8,128)(2,1)S(1)}, bf16[192,1024]{1,0:T(8,128)(2,1)S(1)}, u32[]{:S(2)}, u32[]{:S(2)}) collective-permute-start(bf16[192,1024]{1,0:T(8,128)(2,1)S(1)} %get-tuple-element.159), channel_id=1, source_target_pairs={{0,1},{1,0},{2,3},{3,2},{4,5},{5,4},{6,7},{7,6},{8,9},{9,8},{10,11... | collective-permute-start | bytes 1179656 | tf_op jit(solution)/shard_map/ppermute | solution.py:35
  201.5 22.6 %collective-permute-start.40 = (bf16[384,1024]{1,0:T(8,128)(2,1)S(1)}, bf16[384,1024]{1,0:T(8,128)(2,1)S(1)}, u32[]{:S(2)}, u32[]{:S(2)}) collective-permute-start(bf16[384,1024]{1,0:T(8,128)(2,1)S(1)} %pad_maximum_fusion.5), channel_id=1, source_target_pairs={{0,4},{4,0},{8,12},{12,8},{16,20},{20,16},{24,28},{28,24},{1,5},{5... | collective-permute-start | bytes 2359304 | tf_op jit(solution)/shard_map/ppermute | solution.py:35
  202.6 15.0 %collective-permute-start.34 = (bf16[128,1024]{1,0:T(8,128)(2,1)S(1)}, bf16[128,1024]{1,0:T(8,128)(2,1)S(1)}, u32[]{:S(2)}, u32[]{:S(2)}) collective-permute-start(bf16[128,1024]{1,0:T(8,128)(2,1)S(1)} %get-tuple-element.137), channel_id=1, source_target_pairs={{0,1},{1,0},{2,3},{3,2},{4,5},{5,4},{6,7},{7,6},{8,9},{9,8},{10,11... | collective-permute-start | bytes 786440 | tf_op jit(solution)/shard_map/ppermute | solution.py:35
  208.9 16.3 %collective-permute-start.50 = (bf16[192,1024]{1,0:T(8,128)(2,1)S(1)}, bf16[192,1024]{1,0:T(8,128)(2,1)S(1)}, u32[]{:S(2)}, u32[]{:S(2)}) collective-permute-start(bf16[192,1024]{1,0:T(8,128)(2,1)S(1)} %get-tuple-element.166), channel_id=1, source_target_pairs={{0,2},{1,3},{2,0},{3,1},{4,6},{5,7},{6,4},{7,5},{8,10},{9,11},{10,... | collective-permute-start | bytes 1179656 | tf_op jit(solution)/shard_map/ppermute | solution.py:35
  212.0 13.1 %collective-permute-start.51 = (bf16[192,1024]{1,0:T(8,128)(2,1)S(1)}, bf16[192,1024]{1,0:T(8,128)(2,1)S(1)}, u32[]{:S(2)}, u32[]{:S(2)}) collective-permute-start(bf16[192,1024]{1,0:T(8,128)(2,1)S(1)} %get-tuple-element.169), channel_id=1, source_target_pairs={{0,1},{1,0},{2,3},{3,2},{4,5},{5,4},{6,7},{7,6},{8,9},{9,8},{10,11... | collective-permute-start | bytes 1179656 | tf_op jit(solution)/shard_map/ppermute | solution.py:35
  213.5 15.9 %collective-permute-start.46 = (bf16[384,1024]{1,0:T(8,128)(2,1)S(1)}, bf16[384,1024]{1,0:T(8,128)(2,1)S(1)}, u32[]{:S(2)}, u32[]{:S(2)}) collective-permute-start(bf16[384,1024]{1,0:T(8,128)(2,1)S(1)} %pad_maximum_fusion.6), channel_id=1, source_target_pairs={{0,4},{4,0},{8,12},{12,8},{16,20},{20,16},{24,28},{28,24},{1,5},{5... | collective-permute-start | bytes 2359304 | tf_op jit(solution)/shard_map/ppermute | solution.py:35
  225.3 30.1 %collective-permute-start.52 = (bf16[384,1024]{1,0:T(8,128)(2,1)S(1)}, bf16[384,1024]{1,0:T(8,128)(2,1)S(1)}, u32[]{:S(2)}, u32[]{:S(2)}) collective-permute-start(bf16[384,1024]{1,0:T(8,128)(2,1)S(1)} %pad_maximum_fusion.7), channel_id=1, source_target_pairs={{0,4},{4,0},{8,12},{12,8},{16,20},{20,16},{24,28},{28,24},{1,5},{5... | collective-permute-start | bytes 2359304 | tf_op jit(solution)/shard_map/ppermute | solution.py:35
  225.4 8.7 %collective-permute-start.41 = (bf16[128,1024]{1,0:T(8,128)(2,1)S(1)}, bf16[128,1024]{1,0:T(8,128)(2,1)S(1)}, u32[]{:S(2)}, u32[]{:S(2)}) collective-permute-start(bf16[128,1024]{1,0:T(8,128)(2,1)S(1)} %get-tuple-element.151), channel_id=1, source_target_pairs={{0,1},{1,0},{2,3},{3,2},{4,5},{5,4},{6,7},{7,6},{8,9},{9,8},{10,11... | collective-permute-start | bytes 786440 | tf_op jit(solution)/shard_map/ppermute | solution.py:35
  226.8 26.1 %collective-permute-start.36 = (bf16[128,2048]{1,0:T(8,128)(2,1)S(1)}, bf16[128,2048]{1,0:T(8,128)(2,1)S(1)}, u32[]{:S(2)}, u32[]{:S(2)}) collective-permute-start(bf16[128,2048]{1,0:T(8,128)(2,1)S(1)} %gather.4), channel_id=1, source_target_pairs={{0,16},{4,20},{8,24},{12,28},{16,0},{20,4},{24,8},{28,12},{1,17},{... | collective-permute-start | bytes 1572872 | tf_op jit(solution)/shard_map/ppermute | solution.py:35
  228.2 8.1 %collective-permute-start.42 = (bf16[128,1024]{1,0:T(8,128)(2,1)S(1)}, bf16[128,1024]{1,0:T(8,128)(2,1)S(1)}, u32[]{:S(2)}, u32[]{:S(2)}) collective-permute-start(bf16[128,1024]{1,0:T(8,128)(2,1)S(1)} %get-tuple-element.153), channel_id=1, source_target_pairs={{0,2},{1,3},{2,0},{3,1},{4,6},{5,7},{6,4},{7,5},{8,10},{9,11},{10,... | collective-permute-start | bytes 786440 | tf_op jit(solution)/shard_map/ppermute | solution.py:35
  234.1 21.2 %collective-permute-start.47 = (bf16[128,1024]{1,0:T(8,128)(2,1)S(1)}, bf16[128,1024]{1,0:T(8,128)(2,1)S(1)}, u32[]{:S(2)}, u32[]{:S(2)}) collective-permute-start(bf16[128,1024]{1,0:T(8,128)(2,1)S(1)} %get-tuple-element.162), channel_id=1, source_target_pairs={{0,1},{1,0},{2,3},{3,2},{4,5},{5,4},{6,7},{7,6},{8,9},{9,8},{10,11... | collective-permute-start | bytes 786440 | tf_op jit(solution)/shard_map/ppermute | solution.py:35
  236.3 18.9 %collective-permute-start.48 = (bf16[128,1024]{1,0:T(8,128)(2,1)S(1)}, bf16[128,1024]{1,0:T(8,128)(2,1)S(1)}, u32[]{:S(2)}, u32[]{:S(2)}) collective-permute-start(bf16[128,1024]{1,0:T(8,128)(2,1)S(1)} %get-tuple-element.164), channel_id=1, source_target_pairs={{0,2},{1,3},{2,0},{3,1},{4,6},{5,7},{6,4},{7,5},{8,10},{9,11},{10,... | collective-permute-start | bytes 786440 | tf_op jit(solution)/shard_map/ppermute | solution.py:35
  253.0 16.7 %collective-permute-start.43 = (bf16[128,2048]{1,0:T(8,128)(2,1)S(1)}, bf16[128,2048]{1,0:T(8,128)(2,1)S(1)}, u32[]{:S(2)}, u32[]{:S(2)}) collective-permute-start(bf16[128,2048]{1,0:T(8,128)(2,1)S(1)} %gather.5), channel_id=1, source_target_pairs={{0,24},{4,28},{8,16},{12,20},{16,8},{20,12},{24,0},{28,4},{1,25},{... | collective-permute-start | bytes 1572872 | tf_op jit(solution)/shard_map/ppermute | solution.py:35
  255.4 24.1 %collective-permute-start.49 = (bf16[128,2048]{1,0:T(8,128)(2,1)S(1)}, bf16[128,2048]{1,0:T(8,128)(2,1)S(1)}, u32[]{:S(2)}, u32[]{:S(2)}) collective-permute-start(bf16[128,2048]{1,0:T(8,128)(2,1)S(1)} %gather.6), channel_id=1, source_target_pairs={{0,8},{4,12},{8,0},{12,4},{16,24},{20,28},{24,16},{28,20},{1,9},{5... | collective-permute-start | bytes 1572872 | tf_op jit(solution)/shard_map/ppermute | solution.py:35
  256.5 8.0 %collective-permute-start.53 = (bf16[128,1024]{1,0:T(8,128)(2,1)S(1)}, bf16[128,1024]{1,0:T(8,128)(2,1)S(1)}, u32[]{:S(2)}, u32[]{:S(2)}) collective-permute-start(bf16[128,1024]{1,0:T(8,128)(2,1)S(1)} %get-tuple-element.172), channel_id=1, source_target_pairs={{0,1},{1,0},{2,3},{3,2},{4,5},{5,4},{6,7},{7,6},{8,9},{9,8},{10,11... | collective-permute-start | bytes 786440 | tf_op jit(solution)/shard_map/ppermute | solution.py:35
  (21 other events, 234.3 us)
Sparse Core Ops, SparseCore 0:
  24.2 30.9 all-gather.1

commit v10 on v9

--- a/solution.py
+++ b/solution.py
@@ -505,7 +505,7 @@
     produced = []
     slots = exp_count * capacity
     for g, came in enumerate(arrived):
-        ready = produced if g >= groups - 2 else []
+        ready = produced if g == groups - 2 else []
         produced.append(
             call(
                 functools.partial(expert_kernel, routes, capacity),
@@ -524,9 +524,9 @@
             )
         )
 
-    totals, hop = [], ()
+    passing = [[] for _ in range(groups)]
     onward_picked = [a for _, away in routes for a in away]
-    for g in [*range(2, groups), *(g for g in (1, 0) if g < groups)]:
+    for g in reversed(range(groups)):
         back = [send(p, a, "picked") if a else p for p, a in zip(produced[g], onward_picked)]
         back.append(to_mate(back))
         onward = [n for near, _ in routes for n in near[1:]]
@@ -543,21 +543,20 @@
         total = call(
             functools.partial(gather_kernel, [len(near) - 1 for near, _ in routes]),
             bf16((rows, width)) if g else jax.ShapeDtypeStruct((rows, width), jnp.float32),
-            [VMEM] * (1 + len(sums)),
+            [VMEM] * (1 + len(sums) + (len(passing[g]) if g else 0)),
             kept,
             *sums,
+            *(passing[g] if g else []),
             name="gather",
         )
         if g:
-            total = swap(tie(total, *(hop if g > 1 else ())), "ctx", 2 * g)
-            hop = (total,)
-            totals.append(total)
+            passing[g & (g - 1)].append(swap(total, "ctx", 2 * (g & -g)))
     early = call(
         sum_kernel,
         jax.ShapeDtypeStruct((rows, width), jnp.float32),
-        [VMEM] * groups,
+        [VMEM] * (1 + len(passing[0])),
         residual,
-        *totals,
+        *passing[0],
         name="add",
         flops=10_000_000_000,
     )

time: 288 us -> 279 us (0.969)
  waiting for transfers between devices: 166 us -> 154 us
    ppermute x55, waiting for transfers between devices: 163 us -> 150 us  [swap(): return lax.ppermute(array, axis, pairs)]
    unnamed x33 -> x37, local copies, waits for them, and re-layouts: 5.6 us -> 6.48 us
  transfers between devices with their start and end apart: 56 -> 56, of which waited for: 33 -> 31; matrix products, arithmetic and copies ran while one was open for 1% -> 1% of each run, Pallas kernels for 8% -> 12%
where the time goes in v10:
time: 279 us; the launch traced here: 278 us
  waiting for transfers between devices  154 us (55%)
  starting transfers between devices  60.2 us (22%)
  Pallas kernels  39.7 us (14%)
  between operations  14.2 us (5%)
  local copies, waits for them, and re-layouts  7.14 us (3%)
  other arithmetic  3.03 us (1%)
    ppermute x55, waiting for transfers between devices, swap(): return lax.ppermute(array, axis, pairs)  150 us
    ppermute x55, starting transfers between devices, swap(): return lax.ppermute(array, axis, pairs)  60.2 us
    pallas_call x27, Pallas kernels, call(): pl.pallas_call(kernel, out_shape=out_shape, in_specs=specs, out_specs=jax...  39.7 us
    unnamed x37, local copies, waits for them, and re-layouts  6.48 us
  transfers between devices with their start and end apart: 56, of which 31 were waited for; matrix products, arithmetic and copies ran while one was open for 1% of the time, Pallas kernels for 12%

profile of v10, /device:TPU:0, one launch (start us, length us, event | category | flops | bytes accessed | tf_op | source)
XLA Modules:
  0.0 278.3 jit_solution(14758397280275008389)
XLA Ops:
  8.2 4.5 %own_rows.1 = (bf16[144,256]{1,0:T(8,128)(2,1)}, bf16[144,256]{1,0:T(8,128)(2,1)}, bf16[144,256]{1,0:T(8,128)(2,1)}, bf16[144,256]{1,0:T(8,128)(2,1)}) custom-call(s32[6]{0:T(128)} %pad_add_fusion.place, s32[8,128]{1,0:T(8,128)} %bitcast.38, s32[8,128]{1,0:T(8,128)} %bitcast.39, bf16[128,2048]{1,0:T(8,128)(2,1)} %tokens.1, f32[1,2048]{1,0:T(1,128)} %bitcast.34, ...), custom_call_target="tpu_custom_call" | custom-call | flops 1000 | bytes 1000 | tf_op jit(solution)/shard_map/own_rows/pallas_call | solution.py:338
  12.6 3.0 %collective-permute-start = (bf16[144,256]{1,0:T(8,128)(2,1)}, bf16[144,256]{1,0:T(8,128)(2,1)S(1)}, u32[]{:S(2)}, u32[]{:S(2)}) collective-permute-start(bf16[144,256]{1,0:T(8,128)(2,1)} %get-tuple-element.88), channel_id=1, source_target_pairs={{0,1},{1,0},{2,3},{3,2},{4,5},{5,4},{6,7},{7,6},{8,9},{9,8},{10,11... | collective-permute-start | bytes 221192 | tf_op jit(solution)/shard_map/ppermute | solution.py:35
  15.6 1.5 collective-permute-start.1
  18.5 1.7 collective-permute-done.1
  20.2 2.4 collective-permute-done.2
  25.2 2.5 collective-permute-start.5
  28.7 10.4 %collective-permute-done.3.refs_1_ = bf16[128,2048]{1,0:T(8,128)(2,1)S(1)} collective-permute-done((bf16[128,2048]{1,0:T(8,128)(2,1)S(1)}, bf16[128,2048]{1,0:T(8,128)(2,1)S(1)}, u32[]{:S(2)}, u32[]{:S(2)}) %collective-permute-start.3) | collective-permute-done | bytes 524320 | tf_op jit(solution)/shard_map/ppermute | solution.py:35
  39.0 9.1 %collective-permute-done.4.refs_2_ = bf16[128,2048]{1,0:T(8,128)(2,1)S(1)} collective-permute-done((bf16[128,2048]{1,0:T(8,128)(2,1)S(1)}, bf16[128,2048]{1,0:T(8,128)(2,1)S(1)}, u32[]{:S(2)}, u32[]{:S(2)}) %collective-permute-start.4) | collective-permute-done | bytes 524320 | tf_op jit(solution)/shard_map/ppermute | solution.py:35
  48.1 1.6 copy-done.7
  49.7 1.9 queries.1
  51.6 3.6 %all-gather.2.cloned.1.call-done.both = bf16[4608,256]{1,0:T(8,128)(2,1)} async-done(((bf16[576,256]{1,0:T(8,128)(2,1)}), bf16[4608,256]{1,0:T(8,128)(2,1)}) %all-gather.2.cloned.1.call-update) | async-done | bytes 2359312 | tf_op jit(solution)/shard_map/all_gather | solution.py:407
  55.2 1.7 copy-done.3
  56.9 1.7 attention.4
  58.6 2.4 collective-permute-start.6
  61.0 1.7 attention.5
  63.4 1.7 attention.6
  65.7 1.9 attention.7.refs_0_
  67.6 6.8 %collective-permute-done.6.refs_1_ = bf16[128,2048]{1,0:T(8,128)(2,1)S(1)} collective-permute-done((bf16[128,2048]{1,0:T(8,128)(2,1)S(1)}, bf16[128,2048]{1,0:T(8,128)(2,1)S(1)}, u32[]{:S(2)}, u32[]{:S(2)}) %collective-permute-start.6) | collective-permute-done | bytes 524320 | tf_op jit(solution)/shard_map/ppermute | solution.py:35
  74.6 11.0 %collective-permute-done.7.refs_1_ = bf16[128,2048]{1,0:T(8,128)(2,1)S(1)} collective-permute-done((bf16[128,2048]{1,0:T(8,128)(2,1)S(1)}, bf16[128,2048]{1,0:T(8,128)(2,1)S(1)}, u32[]{:S(2)}, u32[]{:S(2)}) %collective-permute-start.7) | collective-permute-done | bytes 524320 | tf_op jit(solution)/shard_map/ppermute | solution.py:35
  86.2 2.5 collective-permute-start.10
  90.0 1.5 collective-permute-start.11
  91.5 5.2 %collective-permute-start.9 = (bf16[128,2048]{1,0:T(8,128)(2,1)S(1)}, bf16[128,2048]{1,0:T(8,128)(2,1)S(1)}, u32[]{:S(2)}, u32[]{:S(2)}) collective-permute-start(bf16[128,2048]{1,0:T(8,128)(2,1)S(1)} %get-tuple-element.97), channel_id=1, source_target_pairs={{0,16},{4,20},{8,24},{12,28},{16,0},{20,4},{24,8},{28,12},{1,17},{... | collective-permute-start | bytes 1572872 | tf_op jit(solution)/shard_map/ppermute | solution.py:35
  98.9 1.5 collective-permute-start.20
  101.2 9.1 %collective-permute-done.10 = bf16[128,2048]{1,0:T(8,128)(2,1)S(1)} collective-permute-done((bf16[128,2048]{1,0:T(8,128)(2,1)S(1)}, bf16[128,2048]{1,0:T(8,128)(2,1)S(1)}, u32[]{:S(2)}, u32[]{:S(2)}) %collective-permute-start.10) | collective-permute-done | bytes 524320 | tf_op jit(solution)/shard_map/ppermute | solution.py:35
  110.8 2.3 collective-permute-start.12
  113.1 6.7 %collective-permute-done.9 = bf16[128,2048]{1,0:T(8,128)(2,1)S(1)} collective-permute-done((bf16[128,2048]{1,0:T(8,128)(2,1)S(1)}, bf16[128,2048]{1,0:T(8,128)(2,1)S(1)}, u32[]{:S(2)}, u32[]{:S(2)}) %collective-permute-start.9) | collective-permute-done | bytes 524320 | tf_op jit(solution)/shard_map/ppermute | solution.py:35
  121.8 1.7 collective-permute-start.18
  125.2 12.1 %collective-permute-done.16.refs_3_ = bf16[128,1024]{1,0:T(8,128)(2,1)S(1)} collective-permute-done((bf16[128,1024]{1,0:T(8,128)(2,1)S(1)}, bf16[128,1024]{1,0:T(8,128)(2,1)S(1)}, u32[]{:S(2)}, u32[]{:S(2)}) %collective-permute-start.16) | collective-permute-done | bytes 262176 | tf_op jit(solution)/shard_map/ppermute | solution.py:35
  139.8 1.5 collective-permute-start.19
  143.0 11.2 %collective-permute-done.28.refs_3_ = bf16[128,1024]{1,0:T(8,128)(2,1)S(1)} collective-permute-done((bf16[128,1024]{1,0:T(8,128)(2,1)S(1)}, bf16[128,1024]{1,0:T(8,128)(2,1)S(1)}, u32[]{:S(2)}, u32[]{:S(2)}) %collective-permute-start.28) | collective-permute-done | bytes 262176 | tf_op jit(solution)/shard_map/ppermute | solution.py:35
  157.6 5.6 %collective-permute-done.30.refs_3_ = bf16[192,1024]{1,0:T(8,128)(2,1)S(1)} collective-permute-done((bf16[192,1024]{1,0:T(8,128)(2,1)S(1)}, bf16[192,1024]{1,0:T(8,128)(2,1)S(1)}, u32[]{:S(2)}, u32[]{:S(2)}) %collective-permute-start.30) | collective-permute-done | bytes 393248 | tf_op jit(solution)/shard_map/ppermute | solution.py:35
  164.0 3.9 %expert.4 = (bf16[192,1024]{1,0:T(8,128)(2,1)S(1)}, bf16[192,1024]{1,0:T(8,128)(2,1)S(1)}, bf16[192,1024]{1,0:T(8,128)(2,1)S(1)}, bf16[192,1024]{1,0:T(8,128)(2,1)S(1)}) custom-call(bf16[192,1024]{1,0:T(8,128)(2,1)S(1)} %get-tuple-element.114.refs_0_, bf16[192,1024]{1,0:T(8,128)(2,1)S(1)} %collective-permute-done.17.refs_1_, ...), custom_call_target="tpu_custom_call" | custom-call | flops 1000 | bytes 1000 | tf_op jit(solution)/shard_map/expert/pallas_call | solution.py:338
  168.9 3.9 %expert.5 = (bf16[192,1024]{1,0:T(8,128)(2,1)S(1)}, bf16[192,1024]{1,0:T(8,128)(2,1)S(1)}, bf16[192,1024]{1,0:T(8,128)(2,1)S(1)}, bf16[192,1024]{1,0:T(8,128)(2,1)S(1)}) custom-call(bf16[192,1024]{1,0:T(8,128)(2,1)S(1)} %get-tuple-element.117.refs_0_, bf16[192,1024]{1,0:T(8,128)(2,1)S(1)} %collective-permute-done.18.refs_1_, ...), custom_call_target="tpu_custom_call" | custom-call | flops 1000 | bytes 1000 | tf_op jit(solution)/shard_map/expert/pallas_call | solution.py:338
  173.3 4.1 %expert.7 = (bf16[192,1024]{1,0:T(8,128)(2,1)S(1)}, bf16[192,1024]{1,0:T(8,128)(2,1)S(1)}, bf16[192,1024]{1,0:T(8,128)(2,1)S(1)}, bf16[192,1024]{1,0:T(8,128)(2,1)S(1)}) custom-call(bf16[192,1024]{1,0:T(8,128)(2,1)S(1)} %get-tuple-element.125.refs_0_, bf16[192,1024]{1,0:T(8,128)(2,1)S(1)} %collective-permute-done.29.refs_1_, ...), custom_call_target="tpu_custom_call" | custom-call | flops 1000 | bytes 1000 | tf_op jit(solution)/shard_map/expert/pallas_call | solution.py:338
  177.4 1.5 collective-permute-start.34
  178.9 1.5 collective-permute-start.32
  180.4 3.9 %expert.6 = (bf16[192,1024]{1,0:T(8,128)(2,1)S(1)}, bf16[192,1024]{1,0:T(8,128)(2,1)S(1)}, bf16[192,1024]{1,0:T(8,128)(2,1)S(1)}, bf16[192,1024]{1,0:T(8,128)(2,1)S(1)}) custom-call(bf16[192,1024]{1,0:T(8,128)(2,1)S(1)} %get-tuple-element.102.refs_0_, bf16[192,1024]{1,0:T(8,128)(2,1)S(1)} %collective-permute-done.19.refs_1_, ...), custom_call_target="tpu_custom_call" | custom-call | flops 1000 | bytes 1000 | tf_op jit(solution)/shard_map/expert/pallas_call | solution.py:338
  184.3 4.3 %collective-permute-done.34.refs_3_ = bf16[192,1024]{1,0:T(8,128)(2,1)S(1)} collective-permute-done((bf16[192,1024]{1,0:T(8,128)(2,1)S(1)}, bf16[192,1024]{1,0:T(8,128)(2,1)S(1)}, u32[]{:S(2)}, u32[]{:S(2)}) %collective-permute-start.34) | collective-permute-done | bytes 393248 | tf_op jit(solution)/shard_map/ppermute | solution.py:35
  191.9 9.5 %collective-permute-done.35.refs_3_ = bf16[192,1024]{1,0:T(8,128)(2,1)S(1)} collective-permute-done((bf16[192,1024]{1,0:T(8,128)(2,1)S(1)}, bf16[192,1024]{1,0:T(8,128)(2,1)S(1)}, u32[]{:S(2)}, u32[]{:S(2)}) %collective-permute-start.35) | collective-permute-done | bytes 393248 | tf_op jit(solution)/shard_map/ppermute | solution.py:35
  205.4 6.7 %collective-permute-done.45.refs_3_ = bf16[192,1024]{1,0:T(8,128)(2,1)S(1)} collective-permute-done((bf16[192,1024]{1,0:T(8,128)(2,1)S(1)}, bf16[192,1024]{1,0:T(8,128)(2,1)S(1)}, u32[]{:S(2)}, u32[]{:S(2)}) %collective-permute-start.45) | collective-permute-done | bytes 393248 | tf_op jit(solution)/shard_map/ppermute | solution.py:35
  215.6 4.0 %collective-permute-done.40.refs_1_ = bf16[128,1024]{1,0:T(8,128)(2,1)S(1)} collective-permute-done((bf16[128,1024]{1,0:T(8,128)(2,1)S(1)}, bf16[128,1024]{1,0:T(8,128)(2,1)S(1)}, u32[]{:S(2)}, u32[]{:S(2)}) %collective-permute-start.40) | collective-permute-done | bytes 262176 | tf_op jit(solution)/shard_map/ppermute | solution.py:35
  221.1 6.3 %collective-permute-done.38.refs_0_ = bf16[128,1024]{1,0:T(8,128)(2,1)S(1)} collective-permute-done((bf16[128,1024]{1,0:T(8,128)(2,1)S(1)}, bf16[128,1024]{1,0:T(8,128)(2,1)S(1)}, u32[]{:S(2)}, u32[]{:S(2)}) %collective-permute-start.38) | collective-permute-done | bytes 262176 | tf_op jit(solution)/shard_map/ppermute | solution.py:35
  228.8 1.5 collective-permute-start.41
  233.4 4.2 %collective-permute-done.41.refs_1_ = bf16[128,1024]{1,0:T(8,128)(2,1)S(1)} collective-permute-done((bf16[128,1024]{1,0:T(8,128)(2,1)S(1)}, bf16[128,1024]{1,0:T(8,128)(2,1)S(1)}, u32[]{:S(2)}, u32[]{:S(2)}) %collective-permute-start.41) | collective-permute-done | bytes 262176 | tf_op jit(solution)/shard_map/ppermute | solution.py:35
  240.5 3.9 %collective-permute-done.42.refs_2_ = bf16[128,2048]{1,0:T(8,128)(2,1)S(1)} collective-permute-done((bf16[128,2048]{1,0:T(8,128)(2,1)S(1)}, bf16[128,2048]{1,0:T(8,128)(2,1)S(1)}, u32[]{:S(2)}, u32[]{:S(2)}) %collective-permute-start.42) | collective-permute-done | bytes 524320 | tf_op jit(solution)/shard_map/ppermute | solution.py:35
  244.5 2.4 collective-permute-start.43
  250.6 5.2 %collective-permute-done.54.refs_1_ = bf16[128,1024]{1,0:T(8,128)(2,1)S(1)} collective-permute-done((bf16[128,1024]{1,0:T(8,128)(2,1)S(1)}, bf16[128,1024]{1,0:T(8,128)(2,1)S(1)}, u32[]{:S(2)}, u32[]{:S(2)}) %collective-permute-start.54) | collective-permute-done | bytes 262176 | tf_op jit(solution)/shard_map/ppermute | solution.py:35
  256.4 13.6 %collective-permute-done.43.refs_1_ = bf16[128,2048]{1,0:T(8,128)(2,1)S(1)} collective-permute-done((bf16[128,2048]{1,0:T(8,128)(2,1)S(1)}, bf16[128,2048]{1,0:T(8,128)(2,1)S(1)}, u32[]{:S(2)}, u32[]{:S(2)}) %collective-permute-start.43) | collective-permute-done | bytes 524320 | tf_op jit(solution)/shard_map/ppermute | solution.py:35
  (186 shorter events, 51.8 us)
Async XLA Ops:
  6.5 48.7 %all-gather.2.cloned.1.call-start = ((), (), s32[]{:S(2)}) async-start(), calls=%async_computation | async-start | bytes 2654208 | tf_op jit(solution)/shard_map/all_gather | solution.py:407
  24.1 14.9 %collective-permute-start.3 = (bf16[128,2048]{1,0:T(8,128)(2,1)S(1)}, bf16[128,2048]{1,0:T(8,128)(2,1)S(1)}, u32[]{:S(2)}, u32[]{:S(2)}) collective-permute-start(bf16[128,2048]{1,0:T(8,128)(2,1)S(1)} %copy-done.6), channel_id=1, source_target_pairs={{0,1},{1,0},{2,3},{3,2},{4,5},{5,4},{6,7},{7,6},{8,9},{9,8},{10,11... | collective-permute-start | bytes 1572872 | tf_op jit(solution)/shard_map/ppermute | solution.py:35
  24.7 23.4 %collective-permute-start.4 = (bf16[128,2048]{1,0:T(8,128)(2,1)S(1)}, bf16[128,2048]{1,0:T(8,128)(2,1)S(1)}, u32[]{:S(2)}, u32[]{:S(2)}) collective-permute-start(bf16[128,2048]{1,0:T(8,128)(2,1)S(1)} %copy-done.6), channel_id=1, source_target_pairs={{0,2},{1,3},{2,0},{3,1},{4,6},{5,7},{6,4},{7,5},{8,10},{9,11},{10,... | collective-permute-start | bytes 1572872 | tf_op jit(solution)/shard_map/ppermute | solution.py:35
  25.2 22.9 %collective-permute-start.5 = (bf16[128,2048]{1,0:T(8,128)(2,1)S(1)}, bf16[128,2048]{1,0:T(8,128)(2,1)S(1)}, u32[]{:S(2)}, u32[]{:S(2)}) collective-permute-start(bf16[128,2048]{1,0:T(8,128)(2,1)S(1)} %copy-done.6), channel_id=1, source_target_pairs={{0,3},{1,2},{2,1},{3,0},{4,7},{5,6},{6,5},{7,4},{8,11},{9,10},{10,... | collective-permute-start | bytes 1572872 | tf_op jit(solution)/shard_map/ppermute | solution.py:35
  58.6 15.9 %collective-permute-start.6 = (bf16[128,2048]{1,0:T(8,128)(2,1)S(1)}, bf16[128,2048]{1,0:T(8,128)(2,1)S(1)}, u32[]{:S(2)}, u32[]{:S(2)}) collective-permute-start(bf16[128,2048]{1,0:T(8,128)(2,1)S(1)} %attention.4), channel_id=1, source_target_pairs={{0,3},{1,2},{2,1},{3,0},{4,7},{5,6},{6,5},{7,4},{8,11},{9,10},{10,... | collective-permute-start | bytes 1572872 | tf_op jit(solution)/shard_map/ppermute | solution.py:35
  62.8 22.9 %collective-permute-start.7 = (bf16[128,2048]{1,0:T(8,128)(2,1)S(1)}, bf16[128,2048]{1,0:T(8,128)(2,1)S(1)}, u32[]{:S(2)}, u32[]{:S(2)}) collective-permute-start(bf16[128,2048]{1,0:T(8,128)(2,1)S(1)} %attention.5), channel_id=1, source_target_pairs={{0,1},{1,0},{2,3},{3,2},{4,5},{5,4},{6,7},{7,6},{8,9},{9,8},{10,11... | collective-permute-start | bytes 1572872 | tf_op jit(solution)/shard_map/ppermute | solution.py:35
  65.1 20.7 %collective-permute-start.8 = (bf16[128,2048]{1,0:T(8,128)(2,1)S(1)}, bf16[128,2048]{1,0:T(8,128)(2,1)S(1)}, u32[]{:S(2)}, u32[]{:S(2)}) collective-permute-start(bf16[128,2048]{1,0:T(8,128)(2,1)S(1)} %attention.6), channel_id=1, source_target_pairs={{0,2},{1,3},{2,0},{3,1},{4,6},{5,7},{6,4},{7,5},{8,10},{9,11},{10,... | collective-permute-start | bytes 1572872 | tf_op jit(solution)/shard_map/ppermute | solution.py:35
  86.2 24.2 %collective-permute-start.10 = (bf16[128,2048]{1,0:T(8,128)(2,1)S(1)}, bf16[128,2048]{1,0:T(8,128)(2,1)S(1)}, u32[]{:S(2)}, u32[]{:S(2)}) collective-permute-start(bf16[128,2048]{1,0:T(8,128)(2,1)S(1)} %get-tuple-element.97), channel_id=1, source_target_pairs={{0,8},{4,12},{8,0},{12,4},{16,24},{20,28},{24,16},{28,20},{1,9},{5... | collective-permute-start | bytes 1572872 | tf_op jit(solution)/shard_map/ppermute | solution.py:35
  88.8 8.1 %collective-permute-start.14 = (bf16[128,1024]{1,0:T(8,128)(2,1)S(1)}, bf16[128,1024]{1,0:T(8,128)(2,1)S(1)}, u32[]{:S(2)}, u32[]{:S(2)}) collective-permute-start(bf16[128,1024]{1,0:T(8,128)(2,1)S(1)} %get-tuple-element.173.refs_2_), channel_id=1, source_target_pairs={{0,2},{1,3},{2,0},{3,1},{4,6},{5,7},{6,4},{7,5},{8,10},{9,11},{10,... | collective-permute-start | bytes 786440 | tf_op jit(solution)/shard_map/ppermute | solution.py:35
  91.5 28.4 %collective-permute-start.9 = (bf16[128,2048]{1,0:T(8,128)(2,1)S(1)}, bf16[128,2048]{1,0:T(8,128)(2,1)S(1)}, u32[]{:S(2)}, u32[]{:S(2)}) collective-permute-start(bf16[128,2048]{1,0:T(8,128)(2,1)S(1)} %get-tuple-element.97), channel_id=1, source_target_pairs={{0,16},{4,20},{8,24},{12,28},{16,0},{20,4},{24,8},{28,12},{1,17},{... | collective-permute-start | bytes 1572872 | tf_op jit(solution)/shard_map/ppermute | solution.py:35
  98.9 22.1 %collective-permute-start.20 = (bf16[192,1024]{1,0:T(8,128)(2,1)S(1)}, bf16[192,1024]{1,0:T(8,128)(2,1)S(1)}, u32[]{:S(2)}, u32[]{:S(2)}) collective-permute-start(bf16[192,1024]{1,0:T(8,128)(2,1)S(1)} %get-tuple-element.111), channel_id=1, source_target_pairs={{0,1},{1,0},{2,3},{3,2},{4,5},{5,4},{6,7},{7,6},{8,9},{9,8},{10,11... | collective-permute-start | bytes 1179656 | tf_op jit(solution)/shard_map/ppermute | solution.py:35
  100.4 21.4 %collective-permute-start.17 = (bf16[192,1024]{1,0:T(8,128)(2,1)S(1)}, bf16[192,1024]{1,0:T(8,128)(2,1)S(1)}, u32[]{:S(2)}, u32[]{:S(2)}) collective-permute-start(bf16[192,1024]{1,0:T(8,128)(2,1)S(1)} %get-tuple-element.105), channel_id=1, source_target_pairs={{0,2},{1,3},{2,0},{3,1},{4,6},{5,7},{6,4},{7,5},{8,10},{9,11},{10,... | collective-permute-start | bytes 1179656 | tf_op jit(solution)/shard_map/ppermute | solution.py:35
  110.4 9.4 %collective-permute-start.15 = (bf16[128,1024]{1,0:T(8,128)(2,1)S(1)}, bf16[128,1024]{1,0:T(8,128)(2,1)S(1)}, u32[]{:S(2)}, u32[]{:S(2)}) collective-permute-start(bf16[128,1024]{1,0:T(8,128)(2,1)S(1)} %get-tuple-element.100.refs_2_), channel_id=1, source_target_pairs={{0,2},{1,3},{2,0},{3,1},{4,6},{5,7},{6,4},{7,5},{8,10},{9,11},{10,... | collective-permute-start | bytes 786440 | tf_op jit(solution)/shard_map/ppermute | solution.py:35
  110.8 9.1 %collective-permute-start.12 = (bf16[128,1024]{1,0:T(8,128)(2,1)S(1)}, bf16[128,1024]{1,0:T(8,128)(2,1)S(1)}, u32[]{:S(2)}, u32[]{:S(2)}) collective-permute-start(bf16[128,1024]{1,0:T(8,128)(2,1)S(1)} %get-tuple-element.98.refs_0_), channel_id=1, source_target_pairs={{0,1},{1,0},{2,3},{3,2},{4,5},{5,4},{6,7},{7,6},{8,9},{9,8},{10,11... | collective-permute-start | bytes 786440 | tf_op jit(solution)/shard_map/ppermute | solution.py:35
  119.8 21.5 %collective-permute-start.26 = (bf16[128,2048]{1,0:T(8,128)(2,1)S(1)}, bf16[128,2048]{1,0:T(8,128)(2,1)S(1)}, u32[]{:S(2)}, u32[]{:S(2)}) collective-permute-start(bf16[128,2048]{1,0:T(8,128)(2,1)S(1)} %collective-permute-done.9), channel_id=1, source_target_pairs={{0,8},{4,12},{8,0},{12,4},{16,24},{20,28},{24,16},{28,20},{1,9},{5... | collective-permute-start | bytes 1572872 | tf_op jit(solution)/shard_map/ppermute | solution.py:35
  121.0 17.5 %collective-permute-start.21 = (bf16[192,1024]{1,0:T(8,128)(2,1)S(1)}, bf16[192,1024]{1,0:T(8,128)(2,1)S(1)}, u32[]{:S(2)}, u32[]{:S(2)}) collective-permute-start(bf16[192,1024]{1,0:T(8,128)(2,1)S(1)} %get-tuple-element.112), channel_id=1, source_target_pairs={{0,1},{1,0},{2,3},{3,2},{4,5},{5,4},{6,7},{7,6},{8,9},{9,8},{10,11... | collective-permute-start | bytes 1179656 | tf_op jit(solution)/shard_map/ppermute | solution.py:35
  121.8 18.0 %collective-permute-start.18 = (bf16[192,1024]{1,0:T(8,128)(2,1)S(1)}, bf16[192,1024]{1,0:T(8,128)(2,1)S(1)}, u32[]{:S(2)}, u32[]{:S(2)}) collective-permute-start(bf16[192,1024]{1,0:T(8,128)(2,1)S(1)} %get-tuple-element.106), channel_id=1, source_target_pairs={{0,2},{1,3},{2,0},{3,1},{4,6},{5,7},{6,4},{7,5},{8,10},{9,11},{10,... | collective-permute-start | bytes 1179656 | tf_op jit(solution)/shard_map/ppermute | solution.py:35
  123.5 13.8 %collective-permute-start.16 = (bf16[128,1024]{1,0:T(8,128)(2,1)S(1)}, bf16[128,1024]{1,0:T(8,128)(2,1)S(1)}, u32[]{:S(2)}, u32[]{:S(2)}) collective-permute-start(bf16[128,1024]{1,0:T(8,128)(2,1)S(1)} %get-tuple-element.101.refs_2_), channel_id=1, source_target_pairs={{0,2},{1,3},{2,0},{3,1},{4,6},{5,7},{6,4},{7,5},{8,10},{9,11},{10,... | collective-permute-start | bytes 786440 | tf_op jit(solution)/shard_map/ppermute | solution.py:35
  124.0 13.4 %collective-permute-start.13 = (bf16[128,1024]{1,0:T(8,128)(2,1)S(1)}, bf16[128,1024]{1,0:T(8,128)(2,1)S(1)}, u32[]{:S(2)}, u32[]{:S(2)}) collective-permute-start(bf16[128,1024]{1,0:T(8,128)(2,1)S(1)} %get-tuple-element.99.refs_0_), channel_id=1, source_target_pairs={{0,1},{1,0},{2,3},{3,2},{4,5},{5,4},{6,7},{7,6},{8,9},{9,8},{10,11... | collective-permute-start | bytes 786440 | tf_op jit(solution)/shard_map/ppermute | solution.py:35
  138.4 16.9 %collective-permute-start.22 = (bf16[192,1024]{1,0:T(8,128)(2,1)S(1)}, bf16[192,1024]{1,0:T(8,128)(2,1)S(1)}, u32[]{:S(2)}, u32[]{:S(2)}) collective-permute-start(bf16[192,1024]{1,0:T(8,128)(2,1)S(1)} %get-tuple-element.113), channel_id=1, source_target_pairs={{0,1},{1,0},{2,3},{3,2},{4,5},{5,4},{6,7},{7,6},{8,9},{9,8},{10,11... | collective-permute-start | bytes 1179656 | tf_op jit(solution)/shard_map/ppermute | solution.py:35
  139.8 16.2 %collective-permute-start.19 = (bf16[192,1024]{1,0:T(8,128)(2,1)S(1)}, bf16[192,1024]{1,0:T(8,128)(2,1)S(1)}, u32[]{:S(2)}, u32[]{:S(2)}) collective-permute-start(bf16[192,1024]{1,0:T(8,128)(2,1)S(1)} %get-tuple-element.107), channel_id=1, source_target_pairs={{0,2},{1,3},{2,0},{3,1},{4,6},{5,7},{6,4},{7,5},{8,10},{9,11},{10,... | collective-permute-start | bytes 1179656 | tf_op jit(solution)/shard_map/ppermute | solution.py:35
  141.3 12.9 %collective-permute-start.28 = (bf16[128,1024]{1,0:T(8,128)(2,1)S(1)}, bf16[128,1024]{1,0:T(8,128)(2,1)S(1)}, u32[]{:S(2)}, u32[]{:S(2)}) collective-permute-start(bf16[128,1024]{1,0:T(8,128)(2,1)S(1)} %get-tuple-element.124.refs_2_), channel_id=1, source_target_pairs={{0,2},{1,3},{2,0},{3,1},{4,6},{5,7},{6,4},{7,5},{8,10},{9,11},{10,... | collective-permute-start | bytes 786440 | tf_op jit(solution)/shard_map/ppermute | solution.py:35
  142.0 12.3 %collective-permute-start.27 = (bf16[128,1024]{1,0:T(8,128)(2,1)S(1)}, bf16[128,1024]{1,0:T(8,128)(2,1)S(1)}, u32[]{:S(2)}, u32[]{:S(2)}) collective-permute-start(bf16[128,1024]{1,0:T(8,128)(2,1)S(1)} %get-tuple-element.123.refs_0_), channel_id=1, source_target_pairs={{0,1},{1,0},{2,3},{3,2},{4,5},{5,4},{6,7},{7,6},{8,9},{9,8},{10,11... | collective-permute-start | bytes 786440 | tf_op jit(solution)/shard_map/ppermute | solution.py:35
  142.8 21.2 %collective-permute-start.23 = (bf16[384,1024]{1,0:T(8,128)(2,1)S(1)}, bf16[384,1024]{1,0:T(8,128)(2,1)S(1)}, u32[]{:S(2)}, u32[]{:S(2)}) collective-permute-start(bf16[384,1024]{1,0:T(8,128)(2,1)S(1)} %pad_maximum_fusion.1), channel_id=1, source_target_pairs={{0,4},{4,0},{8,12},{12,8},{16,20},{20,16},{24,28},{28,24},{1,5},{5... | collective-permute-start | bytes 2359304 | tf_op jit(solution)/shard_map/ppermute | solution.py:35
  155.3 7.9 %collective-permute-start.30 = (bf16[192,1024]{1,0:T(8,128)(2,1)S(1)}, bf16[192,1024]{1,0:T(8,128)(2,1)S(1)}, u32[]{:S(2)}, u32[]{:S(2)}) collective-permute-start(bf16[192,1024]{1,0:T(8,128)(2,1)S(1)} %get-tuple-element.130), channel_id=1, source_target_pairs={{0,1},{1,0},{2,3},{3,2},{4,5},{5,4},{6,7},{7,6},{8,9},{9,8},{10,11... | collective-permute-start | bytes 1179656 | tf_op jit(solution)/shard_map/ppermute | solution.py:35
  156.0 7.8 %collective-permute-start.29 = (bf16[192,1024]{1,0:T(8,128)(2,1)S(1)}, bf16[192,1024]{1,0:T(8,128)(2,1)S(1)}, u32[]{:S(2)}, u32[]{:S(2)}) collective-permute-start(bf16[192,1024]{1,0:T(8,128)(2,1)S(1)} %get-tuple-element.127), channel_id=1, source_target_pairs={{0,2},{1,3},{2,0},{3,1},{4,6},{5,7},{6,4},{7,5},{8,10},{9,11},{10,... | collective-permute-start | bytes 1179656 | tf_op jit(solution)/shard_map/ppermute | solution.py:35
  157.5 10.6 %collective-permute-start.24 = (bf16[384,1024]{1,0:T(8,128)(2,1)S(1)}, bf16[384,1024]{1,0:T(8,128)(2,1)S(1)}, u32[]{:S(2)}, u32[]{:S(2)}) collective-permute-start(bf16[384,1024]{1,0:T(8,128)(2,1)S(1)} %pad_maximum_fusion.2), channel_id=1, source_target_pairs={{0,4},{4,0},{8,12},{12,8},{16,20},{20,16},{24,28},{28,24},{1,5},{5... | collective-permute-start | bytes 2359304 | tf_op jit(solution)/shard_map/ppermute | solution.py:35
  163.9 9.5 %collective-permute-start.31 = (bf16[384,1024]{1,0:T(8,128)(2,1)S(1)}, bf16[384,1024]{1,0:T(8,128)(2,1)S(1)}, u32[]{:S(2)}, u32[]{:S(2)}) collective-permute-start(bf16[384,1024]{1,0:T(8,128)(2,1)S(1)} %pad_maximum_fusion.3), channel_id=1, source_target_pairs={{0,4},{4,0},{8,12},{12,8},{16,20},{20,16},{24,28},{28,24},{1,5},{5... | collective-permute-start | bytes 2359304 | tf_op jit(solution)/shard_map/ppermute | solution.py:35
  177.4 11.1 %collective-permute-start.34 = (bf16[192,1024]{1,0:T(8,128)(2,1)S(1)}, bf16[192,1024]{1,0:T(8,128)(2,1)S(1)}, u32[]{:S(2)}, u32[]{:S(2)}) collective-permute-start(bf16[192,1024]{1,0:T(8,128)(2,1)S(1)} %get-tuple-element.137), channel_id=1, source_target_pairs={{0,1},{1,0},{2,3},{3,2},{4,5},{5,4},{6,7},{7,6},{8,9},{9,8},{10,11... | collective-permute-start | bytes 1179656 | tf_op jit(solution)/shard_map/ppermute | solution.py:35
  178.9 10.8 %collective-permute-start.32 = (bf16[192,1024]{1,0:T(8,128)(2,1)S(1)}, bf16[192,1024]{1,0:T(8,128)(2,1)S(1)}, u32[]{:S(2)}, u32[]{:S(2)}) collective-permute-start(bf16[192,1024]{1,0:T(8,128)(2,1)S(1)} %get-tuple-element.132), channel_id=1, source_target_pairs={{0,2},{1,3},{2,0},{3,1},{4,6},{5,7},{6,4},{7,5},{8,10},{9,11},{10,... | collective-permute-start | bytes 1179656 | tf_op jit(solution)/shard_map/ppermute | solution.py:35
  189.8 13.9 %collective-permute-start.37 = (bf16[384,1024]{1,0:T(8,128)(2,1)S(1)}, bf16[384,1024]{1,0:T(8,128)(2,1)S(1)}, u32[]{:S(2)}, u32[]{:S(2)}) collective-permute-start(bf16[384,1024]{1,0:T(8,128)(2,1)S(1)} %pad_maximum_fusion.5), channel_id=1, source_target_pairs={{0,4},{4,0},{8,12},{12,8},{16,20},{20,16},{24,28},{28,24},{1,5},{5... | collective-permute-start | bytes 2359304 | tf_op jit(solution)/shard_map/ppermute | solution.py:35
  189.8 11.5 %collective-permute-start.35 = (bf16[192,1024]{1,0:T(8,128)(2,1)S(1)}, bf16[192,1024]{1,0:T(8,128)(2,1)S(1)}, u32[]{:S(2)}, u32[]{:S(2)}) collective-permute-start(bf16[192,1024]{1,0:T(8,128)(2,1)S(1)} %get-tuple-element.138), channel_id=1, source_target_pairs={{0,1},{1,0},{2,3},{3,2},{4,5},{5,4},{6,7},{7,6},{8,9},{9,8},{10,11... | collective-permute-start | bytes 1179656 | tf_op jit(solution)/shard_map/ppermute | solution.py:35
  190.5 11.5 %collective-permute-start.33 = (bf16[192,1024]{1,0:T(8,128)(2,1)S(1)}, bf16[192,1024]{1,0:T(8,128)(2,1)S(1)}, u32[]{:S(2)}, u32[]{:S(2)}) collective-permute-start(bf16[192,1024]{1,0:T(8,128)(2,1)S(1)} %get-tuple-element.133), channel_id=1, source_target_pairs={{0,2},{1,3},{2,0},{3,1},{4,6},{5,7},{6,4},{7,5},{8,10},{9,11},{10,... | collective-permute-start | bytes 1179656 | tf_op jit(solution)/shard_map/ppermute | solution.py:35
  201.4 10.7 %collective-permute-start.45 = (bf16[192,1024]{1,0:T(8,128)(2,1)S(1)}, bf16[192,1024]{1,0:T(8,128)(2,1)S(1)}, u32[]{:S(2)}, u32[]{:S(2)}) collective-permute-start(bf16[192,1024]{1,0:T(8,128)(2,1)S(1)} %get-tuple-element.155), channel_id=1, source_target_pairs={{0,1},{1,0},{2,3},{3,2},{4,5},{5,4},{6,7},{7,6},{8,9},{9,8},{10,11... | collective-permute-start | bytes 1179656 | tf_op jit(solution)/shard_map/ppermute | solution.py:35
  202.0 12.1 %collective-permute-start.44 = (bf16[192,1024]{1,0:T(8,128)(2,1)S(1)}, bf16[192,1024]{1,0:T(8,128)(2,1)S(1)}, u32[]{:S(2)}, u32[]{:S(2)}) collective-permute-start(bf16[192,1024]{1,0:T(8,128)(2,1)S(1)} %get-tuple-element.152), channel_id=1, source_target_pairs={{0,2},{1,3},{2,0},{3,1},{4,6},{5,7},{6,4},{7,5},{8,10},{9,11},{10,... | collective-permute-start | bytes 1179656 | tf_op jit(solution)/shard_map/ppermute | solution.py:35
  203.5 24.2 %collective-permute-start.36 = (bf16[384,1024]{1,0:T(8,128)(2,1)S(1)}, bf16[384,1024]{1,0:T(8,128)(2,1)S(1)}, u32[]{:S(2)}, u32[]{:S(2)}) collective-permute-start(bf16[384,1024]{1,0:T(8,128)(2,1)S(1)} %pad_maximum_fusion.4), channel_id=1, source_target_pairs={{0,4},{4,0},{8,12},{12,8},{16,20},{20,16},{24,28},{28,24},{1,5},{5... | collective-permute-start | bytes 2359304 | tf_op jit(solution)/shard_map/ppermute | solution.py:35
  204.7 15.0 %collective-permute-start.40 = (bf16[128,1024]{1,0:T(8,128)(2,1)S(1)}, bf16[128,1024]{1,0:T(8,128)(2,1)S(1)}, u32[]{:S(2)}, u32[]{:S(2)}) collective-permute-start(bf16[128,1024]{1,0:T(8,128)(2,1)S(1)} %get-tuple-element.148), channel_id=1, source_target_pairs={{0,2},{1,3},{2,0},{3,1},{4,6},{5,7},{6,4},{7,5},{8,10},{9,11},{10,... | collective-permute-start | bytes 786440 | tf_op jit(solution)/shard_map/ppermute | solution.py:35
  212.0 15.5 %collective-permute-start.51 = (bf16[192,1024]{1,0:T(8,128)(2,1)S(1)}, bf16[192,1024]{1,0:T(8,128)(2,1)S(1)}, u32[]{:S(2)}, u32[]{:S(2)}) collective-permute-start(bf16[192,1024]{1,0:T(8,128)(2,1)S(1)} %get-tuple-element.165), channel_id=1, source_target_pairs={{0,1},{1,0},{2,3},{3,2},{4,5},{5,4},{6,7},{7,6},{8,9},{9,8},{10,11... | collective-permute-start | bytes 1179656 | tf_op jit(solution)/shard_map/ppermute | solution.py:35
  214.0 13.6 %collective-permute-start.50 = (bf16[192,1024]{1,0:T(8,128)(2,1)S(1)}, bf16[192,1024]{1,0:T(8,128)(2,1)S(1)}, u32[]{:S(2)}, u32[]{:S(2)}) collective-permute-start(bf16[192,1024]{1,0:T(8,128)(2,1)S(1)} %get-tuple-element.162), channel_id=1, source_target_pairs={{0,2},{1,3},{2,0},{3,1},{4,6},{5,7},{6,4},{7,5},{8,10},{9,11},{10,... | collective-permute-start | bytes 1179656 | tf_op jit(solution)/shard_map/ppermute | solution.py:35
  215.5 16.8 %collective-permute-start.46 = (bf16[384,1024]{1,0:T(8,128)(2,1)S(1)}, bf16[384,1024]{1,0:T(8,128)(2,1)S(1)}, u32[]{:S(2)}, u32[]{:S(2)}) collective-permute-start(bf16[384,1024]{1,0:T(8,128)(2,1)S(1)} %pad_maximum_fusion.6), channel_id=1, source_target_pairs={{0,4},{4,0},{8,12},{12,8},{16,20},{20,16},{24,28},{28,24},{1,5},{5... | collective-permute-start | bytes 2359304 | tf_op jit(solution)/shard_map/ppermute | solution.py:35
  219.6 7.8 %collective-permute-start.38 = (bf16[128,1024]{1,0:T(8,128)(2,1)S(1)}, bf16[128,1024]{1,0:T(8,128)(2,1)S(1)}, u32[]{:S(2)}, u32[]{:S(2)}) collective-permute-start(bf16[128,1024]{1,0:T(8,128)(2,1)S(1)} %get-tuple-element.144), channel_id=1, source_target_pairs={{0,1},{1,0},{2,3},{3,2},{4,5},{5,4},{6,7},{7,6},{8,9},{9,8},{10,11... | collective-permute-start | bytes 786440 | tf_op jit(solution)/shard_map/ppermute | solution.py:35
  227.7 20.6 %collective-permute-start.52 = (bf16[384,1024]{1,0:T(8,128)(2,1)S(1)}, bf16[384,1024]{1,0:T(8,128)(2,1)S(1)}, u32[]{:S(2)}, u32[]{:S(2)}) collective-permute-start(bf16[384,1024]{1,0:T(8,128)(2,1)S(1)} %pad_maximum_fusion.7), channel_id=1, source_target_pairs={{0,4},{4,0},{8,12},{12,8},{16,20},{20,16},{24,28},{28,24},{1,5},{5... | collective-permute-start | bytes 2359304 | tf_op jit(solution)/shard_map/ppermute | solution.py:35
  228.8 8.8 %collective-permute-start.41 = (bf16[128,1024]{1,0:T(8,128)(2,1)S(1)}, bf16[128,1024]{1,0:T(8,128)(2,1)S(1)}, u32[]{:S(2)}, u32[]{:S(2)}) collective-permute-start(bf16[128,1024]{1,0:T(8,128)(2,1)S(1)} %get-tuple-element.149), channel_id=1, source_target_pairs={{0,2},{1,3},{2,0},{3,1},{4,6},{5,7},{6,4},{7,5},{8,10},{9,11},{10,... | collective-permute-start | bytes 786440 | tf_op jit(solution)/shard_map/ppermute | solution.py:35
  230.3 14.0 %collective-permute-start.42 = (bf16[128,2048]{1,0:T(8,128)(2,1)S(1)}, bf16[128,2048]{1,0:T(8,128)(2,1)S(1)}, u32[]{:S(2)}, u32[]{:S(2)}) collective-permute-start(bf16[128,2048]{1,0:T(8,128)(2,1)S(1)} %gather.4), channel_id=1, source_target_pairs={{0,8},{4,12},{8,0},{12,4},{16,24},{20,28},{24,16},{28,20},{1,9},{5... | collective-permute-start | bytes 1572872 | tf_op jit(solution)/shard_map/ppermute | solution.py:35
  231.8 8.1 %collective-permute-start.39 = (bf16[128,1024]{1,0:T(8,128)(2,1)S(1)}, bf16[128,1024]{1,0:T(8,128)(2,1)S(1)}, u32[]{:S(2)}, u32[]{:S(2)}) collective-permute-start(bf16[128,1024]{1,0:T(8,128)(2,1)S(1)} %get-tuple-element.145), channel_id=1, source_target_pairs={{0,1},{1,0},{2,3},{3,2},{4,5},{5,4},{6,7},{7,6},{8,9},{9,8},{10,11... | collective-permute-start | bytes 786440 | tf_op jit(solution)/shard_map/ppermute | solution.py:35
  237.6 9.4 %collective-permute-start.48 = (bf16[128,1024]{1,0:T(8,128)(2,1)S(1)}, bf16[128,1024]{1,0:T(8,128)(2,1)S(1)}, u32[]{:S(2)}, u32[]{:S(2)}) collective-permute-start(bf16[128,1024]{1,0:T(8,128)(2,1)S(1)} %get-tuple-element.160), channel_id=1, source_target_pairs={{0,2},{1,3},{2,0},{3,1},{4,6},{5,7},{6,4},{7,5},{8,10},{9,11},{10,... | collective-permute-start | bytes 786440 | tf_op jit(solution)/shard_map/ppermute | solution.py:35
  244.5 25.5 %collective-permute-start.43 = (bf16[128,2048]{1,0:T(8,128)(2,1)S(1)}, bf16[128,2048]{1,0:T(8,128)(2,1)S(1)}, u32[]{:S(2)}, u32[]{:S(2)}) collective-permute-start(bf16[128,2048]{1,0:T(8,128)(2,1)S(1)} %gather.5), channel_id=1, source_target_pairs={{0,16},{4,20},{8,24},{12,28},{16,0},{20,4},{24,8},{28,12},{1,17},{... | collective-permute-start | bytes 1572872 | tf_op jit(solution)/shard_map/ppermute | solution.py:35
  247.3 23.1 %collective-permute-start.49 = (bf16[128,2048]{1,0:T(8,128)(2,1)S(1)}, bf16[128,2048]{1,0:T(8,128)(2,1)S(1)}, u32[]{:S(2)}, u32[]{:S(2)}) collective-permute-start(bf16[128,2048]{1,0:T(8,128)(2,1)S(1)} %gather.6), channel_id=1, source_target_pairs={{0,8},{4,12},{8,0},{12,4},{16,24},{20,28},{24,16},{28,20},{1,9},{5... | collective-permute-start | bytes 1572872 | tf_op jit(solution)/shard_map/ppermute | solution.py:35
  (24 other events, 233.2 us)
Sparse Core Ops, SparseCore 0:
  24.2 30.9 all-gather.1

commit v11 on v7

--- a/solution.py
+++ b/solution.py
@@ -178,9 +178,14 @@
         for _ in distances
     )
     states = step(pl.multiple_of(block * stride, 2 * TOP), states, True)
-    states = lax.fori_loop(
-        0, block, lambda i, s: step(pl.multiple_of(i * stride, 2 * TOP), s, False), states
-    )
+
+    def blocks(first, count, states):
+        for at in range(count):
+            states = step(pl.multiple_of((first + at) * stride, 2 * TOP), states, False)
+        return states
+
+    states = lax.fori_loop(0, block // 2, lambda i, s: blocks(2 * i, 2, s), states)
+    states = lax.fori_loop(0, block % 2, lambda i, s: blocks(block - 1, 1, s), states)
     for (_, total, mixed), out in zip(states, outs):
         attended = (mixed / total).astype(jnp.bfloat16)
         attended = jnp.concatenate(
@@ -241,53 +246,28 @@
                 ]
 
 
-def combine_kernel(routes, group, capacity, place, routing, *refs):
-    arrived = refs[: sum(len(away) + 1 for _, away in routes)]
-    kept, *outs = refs[len(arrived) :]
-    rows, width = kept.shape[0], arrived[0].shape[1]
-    slots = lax.broadcasted_iota(jnp.int32, (capacity, rows), 0)
-    for side, (near, away) in enumerate(routes):
-        some, arrived = arrived[: len(away) + 1], arrived[len(away) + 1 :]
-        for at, n in enumerate(near):
-            shares, produced = [], []
-            for index, a in enumerate(away):
-                for core, (slot, weight) in enumerate(plane_targets(group, place, routing, n, a)):
-                    shares.append(jnp.where(slots == slot, weight, 0.0))
-                    piece = some[index + 1] if index else some[core]
-                    first = ((core if index else 0) * len(near) + at) * capacity
-                    produced.append(piece[first : first + capacity, :])
-            total = lax.dot_general(
-                jnp.concatenate(shares, axis=0).astype(jnp.bfloat16),
-                jnp.concatenate(produced, axis=0),
-                (((0,), (0,)), ((), ())),
-                preferred_element_type=jnp.float32,
-            )
-            if n:
-                outs[0][...] = total.astype(jnp.bfloat16)
-                outs = outs[1:]
-            else:
-                kept[:, side * width : (side + 1) * width] = total
-
-
-def gather_kernel(counts, kept, *refs):
-    *parts, out = refs
-    width = out.shape[1] // len(counts)
-    for side, count in enumerate(counts):
-        cols = slice(side * width, (side + 1) * width)
-        total = kept[:, cols]
-        for part in parts[:count]:
-            total = total + part[...].astype(jnp.float32)
-        parts = parts[count:]
-        for part in parts[sum(counts[side + 1 :]) :]:
-            total = total + part[:, cols].astype(jnp.float32)
-        out[:, cols] = total.astype(out.dtype)
+def combine_kernel(group, capacity, place, routing, *refs):
+    count = routing.shape[1]
+    returned, passing, out = refs[:count], refs[count:-1], refs[-1]
+    slots = lax.broadcasted_iota(jnp.int32, (capacity, out.shape[0]), 0)
+    parts = []
+    for distance in range(len(returned)):
+        for slot, weight in plane_targets(group, place, routing, 0, distance):
+            parts.append(jnp.where(slots == slot, weight, 0.0))
+    shares = jnp.concatenate(parts, axis=0).astype(jnp.bfloat16)
+    produced = jnp.concatenate([ref[...] for ref in returned], axis=0)
+    total = lax.dot_general(
+        shares, produced, (((0,), (0,)), ((), ())), preferred_element_type=jnp.float32
+    )
+    for part in passing:
+        total = total + part[...].astype(jnp.float32)
+    out[...] = total.astype(out.dtype)
 
 
 def expert_kernel(routes, capacity, *refs):
     count = sum(len(away) for _, away in routes)
     came, (mate, w_gate, w_up, w_down) = refs[:count], refs[count : count + 4]
-    own, other = refs[count + 4 : 2 * count + 4], refs[2 * count + 4 : 3 * count + 4]
-    rows_in, hidden = refs[3 * count + 4 :]
+    own, other, rows_in, hidden = refs[count + 4 :]
     width = came[0].shape[1]
     half = rows_in.shape[1] // 2
     places = []
@@ -310,15 +290,12 @@
         hidden[:, cols] = (gate / (1.0 + jnp.exp(-gate)) * up).astype(jnp.bfloat16)
     for side in range(len(routes)):
         for first in range(0, width, 256):
-            cols = slice(first, first + 256)
             down = w_down[:, side * width + first : side * width + first + 256]
             product = jnp.dot(hidden[...], down, preferred_element_type=jnp.float32)
             product = product.astype(jnp.bfloat16)
-            for where, piece, to, at in places:
-                if where == side:
-                    here = slice(to, to + capacity)
-                    own[piece][here, cols] = product[at : at + capacity]
-                    other[piece][here, cols] = product[half + at : half + at + capacity]
+            cols = slice(side * width + first, side * width + first + 256)
+            own[:, cols] = product[:half]
+            other[:, cols] = product[half:]
 
 
 def sum_kernel(*refs):
@@ -467,7 +444,8 @@
     half = width // 2
     far = [normed]
     for g in range(1, groups):
-        far.append(swap(far[g & (g - 1)], "ctx", 2 * (g & -g)))
+        first = tie(far[g & (g - 1)], *(far[1:] if g == 2 else []))
+        far.append(swap(first, "ctx", 2 * (g & -g)))
     in_flight = {}
 
     def send(array, d, kind):
@@ -486,7 +464,7 @@
             [bf16((2 * len(near) * capacity, half)) for near, away in routes for _ in away],
             [SMEM, VMEM] + [VMEM] * len(sources),
             place,
-            routing,
+            tie(routing, *[part for came in arrived[-1:] for part in came]),
             *sources,
             name="dispatch",
         )
@@ -497,9 +475,9 @@
     slots = exp_count * capacity
     for came in arrived:
         mate = jnp.concatenate([part[part.shape[0] // 2 :] for part in came], axis=0)
-        made = call(
+        own, other = call(
             functools.partial(expert_kernel, routes, capacity),
-            [bf16((len(near) * capacity, half)) for near, away in routes for _ in away] * 2,
+            [bf16((slots, width)), bf16((slots, width))],
             [VMEM] * (len(came) + 4),
             *came,
             swap(mate, "ctx", 1),
@@ -512,35 +490,24 @@
                 pltpu.VMEM((2 * slots, w_gate.shape[2]), jnp.bfloat16),
             ],
         )
-        own, other = made[: len(came)], made[len(came) :]
-        produced.append([(mine, swap(mates, "ctx", 1)) for mine, mates in zip(own, other)])
-
-    passing = [[] for _ in range(groups)]
-    for g in reversed(range(groups)):
-        back, pieces = [], iter(produced[g])
-        for _, away in routes:
-            for a in away:
-                pair = next(pieces)
-                back += [send(jnp.concatenate(pair, axis=0), a, "picked")] if a else pair
-        onward = [n for near, _ in routes for n in near[1:]]
-        kept, *sums = call(
-            functools.partial(combine_kernel, routes, g, capacity),
-            [jax.ShapeDtypeStruct((rows, width), jnp.float32)] + [bf16((rows, half)) for _ in onward],
-            [SMEM, VMEM] + [VMEM] * len(back),
+        produced.append((own, swap(other, "ctx", 1)))
+
+    passing, in_flight = [[] for _ in range(groups)], {}
+    for g in [*range(1, min(2, groups)), *reversed(range(2, groups)), 0]:
+        back = []
+        for d in peers:
+            mine = slice(d * capacity, (d + 1) * capacity)
+            back.append(jnp.concatenate([part[mine] for part in produced[g]], axis=0))
+        back = [back[0]] + [send(back[d], d, "back") for d in peers[1:]]
+        total = call(
+            functools.partial(combine_kernel, g, capacity),
+            bf16((rows, width)) if g else jax.ShapeDtypeStruct((rows, width), jnp.float32),
+            [SMEM, VMEM] + [VMEM] * (exp_count + (len(passing[g]) if g else 0)),
             place,
             routing,
             *back,
+            *(passing[g] if g else []),
             name="combine",
-        )
-        sums = [send(part, n, "whole") for part, n in zip(sums, onward)]
-        total = call(
-            functools.partial(gather_kernel, [len(near) - 1 for near, _ in routes]),
-            bf16((rows, width)) if g else jax.ShapeDtypeStruct((rows, width), jnp.float32),
-            [VMEM] * (1 + len(sums) + (len(passing[g]) if g else 0)),
-            kept,
-            *sums,
-            *(passing[g] if g else []),
-            name="gather",
         )
         if g:
             passing[g & (g - 1)].append(swap(total, "ctx", 2 * (g & -g)))

time: 264 us -> 272 us (1.030)
  waiting for transfers between devices: 137 us -> 151 us
  starting transfers between devices: 63.1 us -> 56.6 us
    ppermute x67 -> x51, waiting for transfers between devices: 133 us -> 147 us  [swap(): return lax.ppermute(array, axis, pairs)]
    ppermute x67 -> x51, starting transfers between devices: 63.1 us -> 56.6 us  [swap(): return lax.ppermute(array, axis, pairs)]
    pallas_call x27 -> x23, Pallas kernels: 39.6 us -> 39.4 us  [call(): pl.pallas_call(kernel, out_shape=out_shape, in_specs=specs, out_specs=jax...]
    unnamed x49 -> x33, local copies, waits for them, and re-layouts: 6.38 us -> 6.58 us
  transfers between devices with their start and end apart: 68 -> 52, of which waited for: 30 -> 33; matrix products, arithmetic and copies ran while one was open for 1% -> 1% of each run, Pallas kernels for 12% -> 11%
where the time goes in v11:
time: 272 us
  waiting for transfers between devices  151 us (56%)
  starting transfers between devices  56.6 us (21%)
  Pallas kernels  39.4 us (14%)
  between operations  14.1 us (5%)
  local copies, waits for them, and re-layouts  7.55 us (3%)
  other arithmetic  3.3 us (1%)
    ppermute x51, waiting for transfers between devices, swap(): return lax.ppermute(array, axis, pairs)  147 us
    ppermute x51, starting transfers between devices, swap(): return lax.ppermute(array, axis, pairs)  56.6 us
    pallas_call x23, Pallas kernels, call(): pl.pallas_call(kernel, out_shape=out_shape, in_specs=specs, out_specs=jax...  39.4 us
    unnamed x33, local copies, waits for them, and re-layouts  6.58 us
  transfers between devices with their start and end apart: 52, of which 33 were waited for; matrix products, arithmetic and copies ran while one was open for 1% of the time, Pallas kernels for 11%

profile of v11, /device:TPU:0, one launch (start us, length us, event | category | flops | bytes accessed | tf_op | source)
XLA Modules:
  0.0 271.7 jit_solution(9402883809366872121)
XLA Ops:
  8.2 4.5 %own_rows.1 = (bf16[144,256]{1,0:T(8,128)(2,1)}, bf16[144,256]{1,0:T(8,128)(2,1)}, bf16[144,256]{1,0:T(8,128)(2,1)}, bf16[144,256]{1,0:T(8,128)(2,1)}) custom-call(s32[6]{0:T(128)} %pad_add_fusion.place, s32[8,128]{1,0:T(8,128)} %bitcast.38, s32[8,128]{1,0:T(8,128)} %bitcast.39, bf16[128,2048]{1,0:T(8,128)(2,1)} %tokens.1, f32[1,2048]{1,0:T(1,128)} %bitcast.34, ...), custom_call_target="tpu_custom_call" | custom-call | flops 1000 | bytes 1000 | tf_op jit(solution)/shard_map/own_rows/pallas_call | solution.py:310
  12.7 3.0 %collective-permute-start = (bf16[144,256]{1,0:T(8,128)(2,1)}, bf16[144,256]{1,0:T(8,128)(2,1)S(1)}, u32[]{:S(2)}, u32[]{:S(2)}) collective-permute-start(bf16[144,256]{1,0:T(8,128)(2,1)} %get-tuple-element.64), channel_id=1, source_target_pairs={{0,1},{1,0},{2,3},{3,2},{4,5},{5,4},{6,7},{7,6},{8,9},{9,8},{10,11... | collective-permute-start | bytes 221192 | tf_op jit(solution)/shard_map/ppermute | solution.py:35
  15.7 1.5 collective-permute-start.1
  18.5 1.7 collective-permute-done.1
  20.3 2.4 collective-permute-done.2
  25.2 2.5 collective-permute-start.5
  28.7 10.4 %collective-permute-done.3.refs_1_ = bf16[128,2048]{1,0:T(8,128)(2,1)S(1)} collective-permute-done((bf16[128,2048]{1,0:T(8,128)(2,1)S(1)}, bf16[128,2048]{1,0:T(8,128)(2,1)S(1)}, u32[]{:S(2)}, u32[]{:S(2)}) %collective-permute-start.3) | collective-permute-done | bytes 524320 | tf_op jit(solution)/shard_map/ppermute | solution.py:35
  39.1 9.1 %collective-permute-done.4.refs_2_ = bf16[128,2048]{1,0:T(8,128)(2,1)S(1)} collective-permute-done((bf16[128,2048]{1,0:T(8,128)(2,1)S(1)}, bf16[128,2048]{1,0:T(8,128)(2,1)S(1)}, u32[]{:S(2)}, u32[]{:S(2)}) %collective-permute-start.4) | collective-permute-done | bytes 524320 | tf_op jit(solution)/shard_map/ppermute | solution.py:35
  48.1 1.6 copy-done.7
  49.8 1.8 queries.1
  51.7 3.6 %all-gather.2.cloned.1.call-done.both = bf16[4608,256]{1,0:T(8,128)(2,1)} async-done(((bf16[576,256]{1,0:T(8,128)(2,1)}), bf16[4608,256]{1,0:T(8,128)(2,1)}) %all-gather.2.cloned.1.call-update) | async-done | bytes 2359312 | tf_op jit(solution)/shard_map/all_gather | solution.py:379
  55.3 1.7 copy-done.3
  56.9 1.7 attention.4
  58.7 2.4 collective-permute-start.6
  61.1 1.7 attention.5
  63.5 1.9 attention.6
  66.0 1.7 attention.7.refs_0_
  67.8 6.8 %collective-permute-done.6.refs_1_ = bf16[128,2048]{1,0:T(8,128)(2,1)S(1)} collective-permute-done((bf16[128,2048]{1,0:T(8,128)(2,1)S(1)}, bf16[128,2048]{1,0:T(8,128)(2,1)S(1)}, u32[]{:S(2)}, u32[]{:S(2)}) %collective-permute-start.6) | collective-permute-done | bytes 524320 | tf_op jit(solution)/shard_map/ppermute | solution.py:35
  74.7 11.0 %collective-permute-done.7.refs_1_ = bf16[128,2048]{1,0:T(8,128)(2,1)S(1)} collective-permute-done((bf16[128,2048]{1,0:T(8,128)(2,1)S(1)}, bf16[128,2048]{1,0:T(8,128)(2,1)S(1)}, u32[]{:S(2)}, u32[]{:S(2)}) %collective-permute-start.7) | collective-permute-done | bytes 524320 | tf_op jit(solution)/shard_map/ppermute | solution.py:35
  86.3 2.3 collective-permute-start.13
  91.4 5.3 %collective-permute-done.10.refs_3_ = bf16[128,1024]{1,0:T(8,128)(2,1)S(1)} collective-permute-done((bf16[128,1024]{1,0:T(8,128)(2,1)S(1)}, bf16[128,1024]{1,0:T(8,128)(2,1)S(1)}, u32[]{:S(2)}, u32[]{:S(2)}) %collective-permute-start.10) | collective-permute-done | bytes 262176 | tf_op jit(solution)/shard_map/ppermute | solution.py:35
  103.6 4.4 %collective-permute-start.24 = (bf16[128,2048]{1,0:T(8,128)(2,1)S(1)}, bf16[128,2048]{1,0:T(8,128)(2,1)S(1)}, u32[]{:S(2)}, u32[]{:S(2)}) collective-permute-start(bf16[128,2048]{1,0:T(8,128)(2,1)S(1)} %get-tuple-element.90), channel_id=1, source_target_pairs={{0,16},{4,20},{8,24},{12,28},{16,0},{20,4},{24,8},{28,12},{1,17},{... | collective-permute-start | bytes 1572872 | tf_op jit(solution)/shard_map/ppermute | solution.py:35
  108.0 2.8 %collective-permute-done.11.refs_1_ = bf16[192,1024]{1,0:T(8,128)(2,1)S(1)} collective-permute-done((bf16[192,1024]{1,0:T(8,128)(2,1)S(1)}, bf16[192,1024]{1,0:T(8,128)(2,1)S(1)}, u32[]{:S(2)}, u32[]{:S(2)}) %collective-permute-start.11) | collective-permute-done | bytes 393248 | tf_op jit(solution)/shard_map/ppermute | solution.py:35
  111.7 2.4 collective-permute-done.15.refs_3_
  115.7 1.5 collective-permute-start.17
  118.7 12.2 %collective-permute-done.24 = bf16[128,2048]{1,0:T(8,128)(2,1)S(1)} collective-permute-done((bf16[128,2048]{1,0:T(8,128)(2,1)S(1)}, bf16[128,2048]{1,0:T(8,128)(2,1)S(1)}, u32[]{:S(2)}, u32[]{:S(2)}) %collective-permute-start.24) | collective-permute-done | bytes 524320 | tf_op jit(solution)/shard_map/ppermute | solution.py:35
  133.8 5.9 %collective-permute-done.26.refs_3_ = bf16[128,1024]{1,0:T(8,128)(2,1)S(1)} collective-permute-done((bf16[128,1024]{1,0:T(8,128)(2,1)S(1)}, bf16[128,1024]{1,0:T(8,128)(2,1)S(1)}, u32[]{:S(2)}, u32[]{:S(2)}) %collective-permute-start.26) | collective-permute-done | bytes 262176 | tf_op jit(solution)/shard_map/ppermute | solution.py:35
  144.5 3.9 %expert.7 = (bf16[192,2048]{1,0:T(8,128)(2,1)S(1)}, bf16[192,2048]{1,0:T(8,128)(2,1)S(1)}) custom-call(bf16[192,1024]{1,0:T(8,128)(2,1)S(1)} %get-tuple-element.74.refs_0_, bf16[192,1024]{1,0:T(8,128)(2,1)S(1)} %collective-permute-done.11.refs_1_, bf16[192,1024]{1,0:T(8,128)(2,1)S(1)} %get-tuple-element.76.refs_2_, ...), custom_call_target="tpu_custom_call" | custom-call | flops 1000 | bytes 1000 | tf_op jit(solution)/shard_map/expert/pallas_call | solution.py:310
  149.2 2.3 collective-permute-done.28.refs_3_
  152.2 2.6 collective-permute-done.27.refs_1_
  155.0 5.0 %collective-permute-done.33.refs_3_ = bf16[128,1024]{1,0:T(8,128)(2,1)S(1)} collective-permute-done((bf16[128,1024]{1,0:T(8,128)(2,1)S(1)}, bf16[128,1024]{1,0:T(8,128)(2,1)S(1)}, u32[]{:S(2)}, u32[]{:S(2)}) %collective-permute-start.33) | collective-permute-done | bytes 262176 | tf_op jit(solution)/shard_map/ppermute | solution.py:35
  163.2 3.9 %expert.4 = (bf16[192,2048]{1,0:T(8,128)(2,1)S(1)}, bf16[192,2048]{1,0:T(8,128)(2,1)S(1)}) custom-call(bf16[192,1024]{1,0:T(8,128)(2,1)S(1)} %get-tuple-element.81.refs_0_, bf16[192,1024]{1,0:T(8,128)(2,1)S(1)} %collective-permute-done.16.refs_1_, bf16[192,1024]{1,0:T(8,128)(2,1)S(1)} %get-tuple-element.84.refs_2_, ...), custom_call_target="tpu_custom_call" | custom-call | flops 1000 | bytes 1000 | tf_op jit(solution)/shard_map/expert/pallas_call | solution.py:310
  167.2 4.6 %collective-permute-done.35.refs_3_ = bf16[192,1024]{1,0:T(8,128)(2,1)S(1)} collective-permute-done((bf16[192,1024]{1,0:T(8,128)(2,1)S(1)}, bf16[192,1024]{1,0:T(8,128)(2,1)S(1)}, u32[]{:S(2)}, u32[]{:S(2)}) %collective-permute-start.35) | collective-permute-done | bytes 393248 | tf_op jit(solution)/shard_map/ppermute | solution.py:35
  173.2 4.1 %expert.5 = (bf16[192,2048]{1,0:T(8,128)(2,1)S(1)}, bf16[192,2048]{1,0:T(8,128)(2,1)S(1)}) custom-call(bf16[192,1024]{1,0:T(8,128)(2,1)S(1)} %get-tuple-element.93.refs_0_, bf16[192,1024]{1,0:T(8,128)(2,1)S(1)} %collective-permute-done.27.refs_1_, bf16[192,1024]{1,0:T(8,128)(2,1)S(1)} %get-tuple-element.96.refs_2_, ...), custom_call_target="tpu_custom_call" | custom-call | flops 1000 | bytes 1000 | tf_op jit(solution)/shard_map/expert/pallas_call | solution.py:310
  181.9 3.9 %expert.6 = (bf16[192,2048]{1,0:T(8,128)(2,1)S(1)}, bf16[192,2048]{1,0:T(8,128)(2,1)S(1)}) custom-call(bf16[192,1024]{1,0:T(8,128)(2,1)S(1)} %get-tuple-element.104.refs_0_, bf16[192,1024]{1,0:T(8,128)(2,1)S(1)} %collective-permute-done.34.refs_1_, bf16[192,1024]{1,0:T(8,128)(2,1)S(1)} %get-tuple-element.107.refs_2_, ...), custom_call_target="tpu_custom_call" | custom-call | flops 1000 | bytes 1000 | tf_op jit(solution)/shard_map/expert/pallas_call | solution.py:310
  186.0 2.1 collective-permute-done.37
  188.2 2.9 %collective-permute-done.22.refs_3_ = bf16[96,2048]{1,0:T(8,128)(2,1)S(1)} collective-permute-done((bf16[96,2048]{1,0:T(8,128)(2,1)S(1)}, bf16[96,2048]{1,0:T(8,128)(2,1)S(1)}, u32[]{:S(2)}, u32[]{:S(2)}) %collective-permute-start.22) | collective-permute-done | bytes 393248 | tf_op jit(solution)/shard_map/ppermute | solution.py:35
  191.7 6.8 %collective-permute-done.21.refs_2_ = bf16[96,2048]{1,0:T(8,128)(2,1)S(1)} collective-permute-done((bf16[96,2048]{1,0:T(8,128)(2,1)S(1)}, bf16[96,2048]{1,0:T(8,128)(2,1)S(1)}, u32[]{:S(2)}, u32[]{:S(2)}) %collective-permute-start.21) | collective-permute-done | bytes 393248 | tf_op jit(solution)/shard_map/ppermute | solution.py:35
  198.5 1.5 collective-permute-start.40
  200.8 7.2 %collective-permute-done.42.refs_3_ = bf16[96,2048]{1,0:T(8,128)(2,1)S(1)} collective-permute-done((bf16[96,2048]{1,0:T(8,128)(2,1)S(1)}, bf16[96,2048]{1,0:T(8,128)(2,1)S(1)}, u32[]{:S(2)}, u32[]{:S(2)}) %collective-permute-start.42) | collective-permute-done | bytes 393248 | tf_op jit(solution)/shard_map/ppermute | solution.py:35
  208.0 7.4 %collective-permute-done.40.refs_2_ = bf16[96,2048]{1,0:T(8,128)(2,1)S(1)} collective-permute-done((bf16[96,2048]{1,0:T(8,128)(2,1)S(1)}, bf16[96,2048]{1,0:T(8,128)(2,1)S(1)}, u32[]{:S(2)}, u32[]{:S(2)}) %collective-permute-start.40) | collective-permute-done | bytes 393248 | tf_op jit(solution)/shard_map/ppermute | solution.py:35
  221.5 1.8 collective-permute-start.23
  223.3 6.5 %collective-permute-done.43.refs_3_ = bf16[96,2048]{1,0:T(8,128)(2,1)S(1)} collective-permute-done((bf16[96,2048]{1,0:T(8,128)(2,1)S(1)}, bf16[96,2048]{1,0:T(8,128)(2,1)S(1)}, u32[]{:S(2)}, u32[]{:S(2)}) %collective-permute-start.43) | collective-permute-done | bytes 393248 | tf_op jit(solution)/shard_map/ppermute | solution.py:35
  229.8 6.6 %collective-permute-done.41.refs_2_ = bf16[96,2048]{1,0:T(8,128)(2,1)S(1)} collective-permute-done((bf16[96,2048]{1,0:T(8,128)(2,1)S(1)}, bf16[96,2048]{1,0:T(8,128)(2,1)S(1)}, u32[]{:S(2)}, u32[]{:S(2)}) %collective-permute-start.41) | collective-permute-done | bytes 393248 | tf_op jit(solution)/shard_map/ppermute | solution.py:35
  237.5 3.5 %collective-permute-start.45 = (bf16[128,2048]{1,0:T(8,128)(2,1)S(1)}, bf16[128,2048]{1,0:T(8,128)(2,1)S(1)}, u32[]{:S(2)}, u32[]{:S(2)}) collective-permute-start(bf16[128,2048]{1,0:T(8,128)(2,1)S(1)} %combine.6), channel_id=1, source_target_pairs={{0,16},{4,20},{8,24},{12,28},{16,0},{20,4},{24,8},{28,12},{1,17},{... | collective-permute-start | bytes 1572872 | tf_op jit(solution)/shard_map/ppermute | solution.py:35
  244.6 9.5 %collective-permute-done.50.refs_3_ = bf16[96,2048]{1,0:T(8,128)(2,1)S(1)} collective-permute-done((bf16[96,2048]{1,0:T(8,128)(2,1)S(1)}, bf16[96,2048]{1,0:T(8,128)(2,1)S(1)}, u32[]{:S(2)}, u32[]{:S(2)}) %collective-permute-start.50) | collective-permute-done | bytes 393248 | tf_op jit(solution)/shard_map/ppermute | solution.py:35
  254.1 6.5 %collective-permute-done.49.refs_2_ = bf16[96,2048]{1,0:T(8,128)(2,1)S(1)} collective-permute-done((bf16[96,2048]{1,0:T(8,128)(2,1)S(1)}, bf16[96,2048]{1,0:T(8,128)(2,1)S(1)}, u32[]{:S(2)}, u32[]{:S(2)}) %collective-permute-start.49) | collective-permute-done | bytes 393248 | tf_op jit(solution)/shard_map/ppermute | solution.py:35
  261.9 1.8 collective-permute-done.45.refs_2_
  (173 shorter events, 55.3 us)
Async XLA Ops:
  6.5 48.7 %all-gather.2.cloned.1.call-start = ((), (), s32[]{:S(2)}) async-start(), calls=%async_computation | async-start | bytes 2654208 | tf_op jit(solution)/shard_map/all_gather | solution.py:379
  24.1 14.9 %collective-permute-start.3 = (bf16[128,2048]{1,0:T(8,128)(2,1)S(1)}, bf16[128,2048]{1,0:T(8,128)(2,1)S(1)}, u32[]{:S(2)}, u32[]{:S(2)}) collective-permute-start(bf16[128,2048]{1,0:T(8,128)(2,1)S(1)} %copy-done.6), channel_id=1, source_target_pairs={{0,1},{1,0},{2,3},{3,2},{4,5},{5,4},{6,7},{7,6},{8,9},{9,8},{10,11... | collective-permute-start | bytes 1572872 | tf_op jit(solution)/shard_map/ppermute | solution.py:35
  24.7 23.4 %collective-permute-start.4 = (bf16[128,2048]{1,0:T(8,128)(2,1)S(1)}, bf16[128,2048]{1,0:T(8,128)(2,1)S(1)}, u32[]{:S(2)}, u32[]{:S(2)}) collective-permute-start(bf16[128,2048]{1,0:T(8,128)(2,1)S(1)} %copy-done.6), channel_id=1, source_target_pairs={{0,2},{1,3},{2,0},{3,1},{4,6},{5,7},{6,4},{7,5},{8,10},{9,11},{10,... | collective-permute-start | bytes 1572872 | tf_op jit(solution)/shard_map/ppermute | solution.py:35
  25.2 22.9 %collective-permute-start.5 = (bf16[128,2048]{1,0:T(8,128)(2,1)S(1)}, bf16[128,2048]{1,0:T(8,128)(2,1)S(1)}, u32[]{:S(2)}, u32[]{:S(2)}) collective-permute-start(bf16[128,2048]{1,0:T(8,128)(2,1)S(1)} %copy-done.6), channel_id=1, source_target_pairs={{0,3},{1,2},{2,1},{3,0},{4,7},{5,6},{6,5},{7,4},{8,11},{9,10},{10,... | collective-permute-start | bytes 1572872 | tf_op jit(solution)/shard_map/ppermute | solution.py:35
  58.7 15.9 %collective-permute-start.6 = (bf16[128,2048]{1,0:T(8,128)(2,1)S(1)}, bf16[128,2048]{1,0:T(8,128)(2,1)S(1)}, u32[]{:S(2)}, u32[]{:S(2)}) collective-permute-start(bf16[128,2048]{1,0:T(8,128)(2,1)S(1)} %attention.4), channel_id=1, source_target_pairs={{0,3},{1,2},{2,1},{3,0},{4,7},{5,6},{6,5},{7,4},{8,11},{9,10},{10,... | collective-permute-start | bytes 1572872 | tf_op jit(solution)/shard_map/ppermute | solution.py:35
  62.9 22.9 %collective-permute-start.7 = (bf16[128,2048]{1,0:T(8,128)(2,1)S(1)}, bf16[128,2048]{1,0:T(8,128)(2,1)S(1)}, u32[]{:S(2)}, u32[]{:S(2)}) collective-permute-start(bf16[128,2048]{1,0:T(8,128)(2,1)S(1)} %attention.5), channel_id=1, source_target_pairs={{0,1},{1,0},{2,3},{3,2},{4,5},{5,4},{6,7},{7,6},{8,9},{9,8},{10,11... | collective-permute-start | bytes 1572872 | tf_op jit(solution)/shard_map/ppermute | solution.py:35
  65.4 20.5 %collective-permute-start.8 = (bf16[128,2048]{1,0:T(8,128)(2,1)S(1)}, bf16[128,2048]{1,0:T(8,128)(2,1)S(1)}, u32[]{:S(2)}, u32[]{:S(2)}) collective-permute-start(bf16[128,2048]{1,0:T(8,128)(2,1)S(1)} %attention.6), channel_id=1, source_target_pairs={{0,2},{1,3},{2,0},{3,1},{4,6},{5,7},{6,4},{7,5},{8,10},{9,11},{10,... | collective-permute-start | bytes 1572872 | tf_op jit(solution)/shard_map/ppermute | solution.py:35
  86.3 14.9 %collective-permute-start.13 = (bf16[128,2048]{1,0:T(8,128)(2,1)S(1)}, bf16[128,2048]{1,0:T(8,128)(2,1)S(1)}, u32[]{:S(2)}, u32[]{:S(2)}) collective-permute-start(bf16[128,2048]{1,0:T(8,128)(2,1)S(1)} %get-tuple-element.90), channel_id=1, source_target_pairs={{0,8},{4,12},{8,0},{12,4},{16,24},{20,28},{24,16},{28,20},{1,9},{5... | collective-permute-start | bytes 1572872 | tf_op jit(solution)/shard_map/ppermute | solution.py:35
  88.6 8.1 %collective-permute-start.10 = (bf16[128,1024]{1,0:T(8,128)(2,1)S(1)}, bf16[128,1024]{1,0:T(8,128)(2,1)S(1)}, u32[]{:S(2)}, u32[]{:S(2)}) collective-permute-start(bf16[128,1024]{1,0:T(8,128)(2,1)S(1)} %get-tuple-element.161.refs_2_), channel_id=1, source_target_pairs={{0,2},{1,3},{2,0},{3,1},{4,6},{5,7},{6,4},{7,5},{8,10},{9,11},{10,... | collective-permute-start | bytes 786440 | tf_op jit(solution)/shard_map/ppermute | solution.py:35
  89.9 7.8 %collective-permute-start.9 = (bf16[128,1024]{1,0:T(8,128)(2,1)S(1)}, bf16[128,1024]{1,0:T(8,128)(2,1)S(1)}, u32[]{:S(2)}, u32[]{:S(2)}) collective-permute-start(bf16[128,1024]{1,0:T(8,128)(2,1)S(1)} %get-tuple-element.162.refs_0_), channel_id=1, source_target_pairs={{0,1},{1,0},{2,3},{3,2},{4,5},{5,4},{6,7},{7,6},{8,9},{9,8},{10,11... | collective-permute-start | bytes 786440 | tf_op jit(solution)/shard_map/ppermute | solution.py:35
  98.7 12.1 %collective-permute-start.11 = (bf16[192,1024]{1,0:T(8,128)(2,1)S(1)}, bf16[192,1024]{1,0:T(8,128)(2,1)S(1)}, u32[]{:S(2)}, u32[]{:S(2)}) collective-permute-start(bf16[192,1024]{1,0:T(8,128)(2,1)S(1)} %get-tuple-element.75), channel_id=1, source_target_pairs={{0,2},{1,3},{2,0},{3,1},{4,6},{5,7},{6,4},{7,5},{8,10},{9,11},{10,... | collective-permute-start | bytes 1179656 | tf_op jit(solution)/shard_map/ppermute | solution.py:35
  99.6 12.1 %collective-permute-start.12 = (bf16[192,1024]{1,0:T(8,128)(2,1)S(1)}, bf16[192,1024]{1,0:T(8,128)(2,1)S(1)}, u32[]{:S(2)}, u32[]{:S(2)}) collective-permute-start(bf16[192,1024]{1,0:T(8,128)(2,1)S(1)} %get-tuple-element.77), channel_id=1, source_target_pairs={{0,1},{1,0},{2,3},{3,2},{4,5},{5,4},{6,7},{7,6},{8,9},{9,8},{10,11... | collective-permute-start | bytes 1179656 | tf_op jit(solution)/shard_map/ppermute | solution.py:35
  101.2 12.9 %collective-permute-start.15 = (bf16[128,1024]{1,0:T(8,128)(2,1)S(1)}, bf16[128,1024]{1,0:T(8,128)(2,1)S(1)}, u32[]{:S(2)}, u32[]{:S(2)}) collective-permute-start(bf16[128,1024]{1,0:T(8,128)(2,1)S(1)} %get-tuple-element.80.refs_2_), channel_id=1, source_target_pairs={{0,2},{1,3},{2,0},{3,1},{4,6},{5,7},{6,4},{7,5},{8,10},{9,11},{10,... | collective-permute-start | bytes 786440 | tf_op jit(solution)/shard_map/ppermute | solution.py:35
  102.4 12.2 %collective-permute-start.14 = (bf16[128,1024]{1,0:T(8,128)(2,1)S(1)}, bf16[128,1024]{1,0:T(8,128)(2,1)S(1)}, u32[]{:S(2)}, u32[]{:S(2)}) collective-permute-start(bf16[128,1024]{1,0:T(8,128)(2,1)S(1)} %get-tuple-element.79.refs_0_), channel_id=1, source_target_pairs={{0,1},{1,0},{2,3},{3,2},{4,5},{5,4},{6,7},{7,6},{8,9},{9,8},{10,11... | collective-permute-start | bytes 786440 | tf_op jit(solution)/shard_map/ppermute | solution.py:35
  103.6 27.3 %collective-permute-start.24 = (bf16[128,2048]{1,0:T(8,128)(2,1)S(1)}, bf16[128,2048]{1,0:T(8,128)(2,1)S(1)}, u32[]{:S(2)}, u32[]{:S(2)}) collective-permute-start(bf16[128,2048]{1,0:T(8,128)(2,1)S(1)} %get-tuple-element.90), channel_id=1, source_target_pairs={{0,16},{4,20},{8,24},{12,28},{16,0},{20,4},{24,8},{28,12},{1,17},{... | collective-permute-start | bytes 1572872 | tf_op jit(solution)/shard_map/ppermute | solution.py:35
  115.7 17.4 %collective-permute-start.17 = (bf16[192,1024]{1,0:T(8,128)(2,1)S(1)}, bf16[192,1024]{1,0:T(8,128)(2,1)S(1)}, u32[]{:S(2)}, u32[]{:S(2)}) collective-permute-start(bf16[192,1024]{1,0:T(8,128)(2,1)S(1)} %get-tuple-element.86), channel_id=1, source_target_pairs={{0,1},{1,0},{2,3},{3,2},{4,5},{5,4},{6,7},{7,6},{8,9},{9,8},{10,11... | collective-permute-start | bytes 1179656 | tf_op jit(solution)/shard_map/ppermute | solution.py:35
  117.3 26.2 %collective-permute-start.46 = (bf16[384,1024]{1,0:T(8,128)(2,1)S(1)}, bf16[384,1024]{1,0:T(8,128)(2,1)S(1)}, u32[]{:S(2)}, u32[]{:S(2)}) collective-permute-start(bf16[384,1024]{1,0:T(8,128)(2,1)S(1)} %pad_maximum_fusion.3), channel_id=1, source_target_pairs={{0,4},{4,0},{8,12},{12,8},{16,20},{20,16},{24,28},{28,24},{1,5},{5... | collective-permute-start | bytes 2359304 | tf_op jit(solution)/shard_map/ppermute | solution.py:35
  117.4 16.3 %collective-permute-start.16 = (bf16[192,1024]{1,0:T(8,128)(2,1)S(1)}, bf16[192,1024]{1,0:T(8,128)(2,1)S(1)}, u32[]{:S(2)}, u32[]{:S(2)}) collective-permute-start(bf16[192,1024]{1,0:T(8,128)(2,1)S(1)} %get-tuple-element.83), channel_id=1, source_target_pairs={{0,2},{1,3},{2,0},{3,1},{4,6},{5,7},{6,4},{7,5},{8,10},{9,11},{10,... | collective-permute-start | bytes 1179656 | tf_op jit(solution)/shard_map/ppermute | solution.py:35
  130.9 17.6 %collective-permute-start.31 = (bf16[128,2048]{1,0:T(8,128)(2,1)S(1)}, bf16[128,2048]{1,0:T(8,128)(2,1)S(1)}, u32[]{:S(2)}, u32[]{:S(2)}) collective-permute-start(bf16[128,2048]{1,0:T(8,128)(2,1)S(1)} %collective-permute-done.24), channel_id=1, source_target_pairs={{0,8},{4,12},{8,0},{12,4},{16,24},{20,28},{24,16},{28,20},{1,9},{5... | collective-permute-start | bytes 1572872 | tf_op jit(solution)/shard_map/ppermute | solution.py:35
  131.6 8.0 %collective-permute-start.26 = (bf16[128,1024]{1,0:T(8,128)(2,1)S(1)}, bf16[128,1024]{1,0:T(8,128)(2,1)S(1)}, u32[]{:S(2)}, u32[]{:S(2)}) collective-permute-start(bf16[128,1024]{1,0:T(8,128)(2,1)S(1)} %get-tuple-element.92.refs_2_), channel_id=1, source_target_pairs={{0,2},{1,3},{2,0},{3,1},{4,6},{5,7},{6,4},{7,5},{8,10},{9,11},{10,... | collective-permute-start | bytes 786440 | tf_op jit(solution)/shard_map/ppermute | solution.py:35
  133.1 7.7 %collective-permute-start.25 = (bf16[128,1024]{1,0:T(8,128)(2,1)S(1)}, bf16[128,1024]{1,0:T(8,128)(2,1)S(1)}, u32[]{:S(2)}, u32[]{:S(2)}) collective-permute-start(bf16[128,1024]{1,0:T(8,128)(2,1)S(1)} %get-tuple-element.91.refs_0_), channel_id=1, source_target_pairs={{0,1},{1,0},{2,3},{3,2},{4,5},{5,4},{6,7},{7,6},{8,9},{9,8},{10,11... | collective-permute-start | bytes 786440 | tf_op jit(solution)/shard_map/ppermute | solution.py:35
  141.9 9.6 %collective-permute-start.28 = (bf16[192,1024]{1,0:T(8,128)(2,1)S(1)}, bf16[192,1024]{1,0:T(8,128)(2,1)S(1)}, u32[]{:S(2)}, u32[]{:S(2)}) collective-permute-start(bf16[192,1024]{1,0:T(8,128)(2,1)S(1)} %get-tuple-element.98), channel_id=1, source_target_pairs={{0,1},{1,0},{2,3},{3,2},{4,5},{5,4},{6,7},{7,6},{8,9},{9,8},{10,11... | collective-permute-start | bytes 1179656 | tf_op jit(solution)/shard_map/ppermute | solution.py:35
  142.7 20.5 %collective-permute-start.18 = (bf16[384,1024]{1,0:T(8,128)(2,1)S(1)}, bf16[384,1024]{1,0:T(8,128)(2,1)S(1)}, u32[]{:S(2)}, u32[]{:S(2)}) collective-permute-start(bf16[384,1024]{1,0:T(8,128)(2,1)S(1)} %pad_maximum_fusion), channel_id=1, source_target_pairs={{0,4},{4,0},{8,12},{12,8},{16,20},{20,16},{24,28},{28,24},{1,5},{5... | collective-permute-start | bytes 2359304 | tf_op jit(solution)/shard_map/ppermute | solution.py:35
  142.8 12.0 %collective-permute-start.27 = (bf16[192,1024]{1,0:T(8,128)(2,1)S(1)}, bf16[192,1024]{1,0:T(8,128)(2,1)S(1)}, u32[]{:S(2)}, u32[]{:S(2)}) collective-permute-start(bf16[192,1024]{1,0:T(8,128)(2,1)S(1)} %get-tuple-element.95), channel_id=1, source_target_pairs={{0,2},{1,3},{2,0},{3,1},{4,6},{5,7},{6,4},{7,5},{8,10},{9,11},{10,... | collective-permute-start | bytes 1179656 | tf_op jit(solution)/shard_map/ppermute | solution.py:35
  148.4 24.7 %collective-permute-start.47 = (bf16[192,2048]{1,0:T(8,128)(2,1)S(1)}, bf16[192,2048]{1,0:T(8,128)(2,1)S(1)}, u32[]{:S(2)}, u32[]{:S(2)}) collective-permute-start(bf16[192,2048]{1,0:T(8,128)(2,1)S(1)} %get-tuple-element.119), channel_id=1, source_target_pairs={{0,4},{4,0},{8,12},{12,8},{16,20},{20,16},{24,28},{28,24},{1,5},{5... | collective-permute-start | bytes 2359304 | tf_op jit(solution)/shard_map/ppermute | solution.py:35
  148.5 11.5 %collective-permute-start.33 = (bf16[128,1024]{1,0:T(8,128)(2,1)S(1)}, bf16[128,1024]{1,0:T(8,128)(2,1)S(1)}, u32[]{:S(2)}, u32[]{:S(2)}) collective-permute-start(bf16[128,1024]{1,0:T(8,128)(2,1)S(1)} %get-tuple-element.103.refs_2_), channel_id=1, source_target_pairs={{0,2},{1,3},{2,0},{3,1},{4,6},{5,7},{6,4},{7,5},{8,10},{9,11},{10,... | collective-permute-start | bytes 786440 | tf_op jit(solution)/shard_map/ppermute | solution.py:35
  151.5 8.5 %collective-permute-start.32 = (bf16[128,1024]{1,0:T(8,128)(2,1)S(1)}, bf16[128,1024]{1,0:T(8,128)(2,1)S(1)}, u32[]{:S(2)}, u32[]{:S(2)}) collective-permute-start(bf16[128,1024]{1,0:T(8,128)(2,1)S(1)} %get-tuple-element.102.refs_0_), channel_id=1, source_target_pairs={{0,1},{1,0},{2,3},{3,2},{4,5},{5,4},{6,7},{7,6},{8,9},{9,8},{10,11... | collective-permute-start | bytes 786440 | tf_op jit(solution)/shard_map/ppermute | solution.py:35
  154.9 18.3 %collective-permute-start.29 = (bf16[384,1024]{1,0:T(8,128)(2,1)S(1)}, bf16[384,1024]{1,0:T(8,128)(2,1)S(1)}, u32[]{:S(2)}, u32[]{:S(2)}) collective-permute-start(bf16[384,1024]{1,0:T(8,128)(2,1)S(1)} %pad_maximum_fusion.1), channel_id=1, source_target_pairs={{0,4},{4,0},{8,12},{12,8},{16,20},{20,16},{24,28},{28,24},{1,5},{5... | collective-permute-start | bytes 2359304 | tf_op jit(solution)/shard_map/ppermute | solution.py:35
  161.1 10.7 %collective-permute-start.35 = (bf16[192,1024]{1,0:T(8,128)(2,1)S(1)}, bf16[192,1024]{1,0:T(8,128)(2,1)S(1)}, u32[]{:S(2)}, u32[]{:S(2)}) collective-permute-start(bf16[192,1024]{1,0:T(8,128)(2,1)S(1)} %get-tuple-element.109), channel_id=1, source_target_pairs={{0,1},{1,0},{2,3},{3,2},{4,5},{5,4},{6,7},{7,6},{8,9},{9,8},{10,11... | collective-permute-start | bytes 1179656 | tf_op jit(solution)/shard_map/ppermute | solution.py:35
  162.6 10.4 %collective-permute-start.34 = (bf16[192,1024]{1,0:T(8,128)(2,1)S(1)}, bf16[192,1024]{1,0:T(8,128)(2,1)S(1)}, u32[]{:S(2)}, u32[]{:S(2)}) collective-permute-start(bf16[192,1024]{1,0:T(8,128)(2,1)S(1)} %get-tuple-element.106), channel_id=1, source_target_pairs={{0,2},{1,3},{2,0},{3,1},{4,6},{5,7},{6,4},{7,5},{8,10},{9,11},{10,... | collective-permute-start | bytes 1179656 | tf_op jit(solution)/shard_map/ppermute | solution.py:35
  167.1 10.9 %collective-permute-start.19 = (bf16[192,2048]{1,0:T(8,128)(2,1)S(1)}, bf16[192,2048]{1,0:T(8,128)(2,1)S(1)}, u32[]{:S(2)}, u32[]{:S(2)}) collective-permute-start(bf16[192,2048]{1,0:T(8,128)(2,1)S(1)} %get-tuple-element.88), channel_id=1, source_target_pairs={{0,4},{4,0},{8,12},{12,8},{16,20},{20,16},{24,28},{28,24},{1,5},{5... | collective-permute-start | bytes 2359304 | tf_op jit(solution)/shard_map/ppermute | solution.py:35
  173.0 8.9 %collective-permute-start.36 = (bf16[384,1024]{1,0:T(8,128)(2,1)S(1)}, bf16[384,1024]{1,0:T(8,128)(2,1)S(1)}, u32[]{:S(2)}, u32[]{:S(2)}) collective-permute-start(bf16[384,1024]{1,0:T(8,128)(2,1)S(1)} %pad_maximum_fusion.2), channel_id=1, source_target_pairs={{0,4},{4,0},{8,12},{12,8},{16,20},{20,16},{24,28},{28,24},{1,5},{5... | collective-permute-start | bytes 2359304 | tf_op jit(solution)/shard_map/ppermute | solution.py:35
  177.4 8.6 %collective-permute-start.30 = (bf16[192,2048]{1,0:T(8,128)(2,1)S(1)}, bf16[192,2048]{1,0:T(8,128)(2,1)S(1)}, u32[]{:S(2)}, u32[]{:S(2)}) collective-permute-start(bf16[192,2048]{1,0:T(8,128)(2,1)S(1)} %get-tuple-element.100), channel_id=1, source_target_pairs={{0,4},{4,0},{8,12},{12,8},{16,20},{20,16},{24,28},{28,24},{1,5},{5... | collective-permute-start | bytes 2359304 | tf_op jit(solution)/shard_map/ppermute | solution.py:35
  178.1 13.0 %collective-permute-start.22 = (bf16[96,2048]{1,0:T(8,128)(2,1)S(1)}, bf16[96,2048]{1,0:T(8,128)(2,1)S(1)}, u32[]{:S(2)}, u32[]{:S(2)}) collective-permute-start(bf16[96,2048]{1,0:T(8,128)(2,1)S(1)} %pad_maximum_fusion.7), channel_id=1, source_target_pairs={{0,3},{1,2},{2,1},{3,0},{4,7},{5,6},{6,5},{7,4},{8,11},{9,10},{10,... | collective-permute-start | bytes 1179656 | tf_op jit(solution)/shard_map/ppermute | solution.py:35
  178.8 19.7 %collective-permute-start.21 = (bf16[96,2048]{1,0:T(8,128)(2,1)S(1)}, bf16[96,2048]{1,0:T(8,128)(2,1)S(1)}, u32[]{:S(2)}, u32[]{:S(2)}) collective-permute-start(bf16[96,2048]{1,0:T(8,128)(2,1)S(1)} %pad_maximum_fusion.6), channel_id=1, source_target_pairs={{0,2},{1,3},{2,0},{3,1},{4,6},{5,7},{6,4},{7,5},{8,10},{9,11},{10,... | collective-permute-start | bytes 1179656 | tf_op jit(solution)/shard_map/ppermute | solution.py:35
  180.4 19.7 %collective-permute-start.20 = (bf16[96,2048]{1,0:T(8,128)(2,1)S(1)}, bf16[96,2048]{1,0:T(8,128)(2,1)S(1)}, u32[]{:S(2)}, u32[]{:S(2)}) collective-permute-start(bf16[96,2048]{1,0:T(8,128)(2,1)S(1)} %pad_maximum_fusion.5), channel_id=1, source_target_pairs={{0,1},{1,0},{2,3},{3,2},{4,5},{5,4},{6,7},{7,6},{8,9},{9,8},{10,11... | collective-permute-start | bytes 1179656 | tf_op jit(solution)/shard_map/ppermute | solution.py:35
  191.1 16.9 %collective-permute-start.42 = (bf16[96,2048]{1,0:T(8,128)(2,1)S(1)}, bf16[96,2048]{1,0:T(8,128)(2,1)S(1)}, u32[]{:S(2)}, u32[]{:S(2)}) collective-permute-start(bf16[96,2048]{1,0:T(8,128)(2,1)S(1)} %pad_maximum_fusion.14), channel_id=1, source_target_pairs={{0,3},{1,2},{2,1},{3,0},{4,7},{5,6},{6,5},{7,4},{8,11},{9,10},{10,... | collective-permute-start | bytes 1179656 | tf_op jit(solution)/shard_map/ppermute | solution.py:35
  198.5 16.9 %collective-permute-start.40 = (bf16[96,2048]{1,0:T(8,128)(2,1)S(1)}, bf16[96,2048]{1,0:T(8,128)(2,1)S(1)}, u32[]{:S(2)}, u32[]{:S(2)}) collective-permute-start(bf16[96,2048]{1,0:T(8,128)(2,1)S(1)} %pad_maximum_fusion.12), channel_id=1, source_target_pairs={{0,2},{1,3},{2,0},{3,1},{4,6},{5,7},{6,4},{7,5},{8,10},{9,11},{10,... | collective-permute-start | bytes 1179656 | tf_op jit(solution)/shard_map/ppermute | solution.py:35
  200.1 15.4 %collective-permute-start.38 = (bf16[96,2048]{1,0:T(8,128)(2,1)S(1)}, bf16[96,2048]{1,0:T(8,128)(2,1)S(1)}, u32[]{:S(2)}, u32[]{:S(2)}) collective-permute-start(bf16[96,2048]{1,0:T(8,128)(2,1)S(1)} %pad_maximum_fusion.10), channel_id=1, source_target_pairs={{0,1},{1,0},{2,3},{3,2},{4,5},{5,4},{6,7},{7,6},{8,9},{9,8},{10,11... | collective-permute-start | bytes 1179656 | tf_op jit(solution)/shard_map/ppermute | solution.py:35
  216.5 20.0 %collective-permute-start.44 = (bf16[128,2048]{1,0:T(8,128)(2,1)S(1)}, bf16[128,2048]{1,0:T(8,128)(2,1)S(1)}, u32[]{:S(2)}, u32[]{:S(2)}) collective-permute-start(bf16[128,2048]{1,0:T(8,128)(2,1)S(1)} %combine.5), channel_id=1, source_target_pairs={{0,8},{4,12},{8,0},{12,4},{16,24},{20,28},{24,16},{28,20},{1,9},{5... | collective-permute-start | bytes 1572872 | tf_op jit(solution)/shard_map/ppermute | solution.py:35
  216.9 13.0 %collective-permute-start.43 = (bf16[96,2048]{1,0:T(8,128)(2,1)S(1)}, bf16[96,2048]{1,0:T(8,128)(2,1)S(1)}, u32[]{:S(2)}, u32[]{:S(2)}) collective-permute-start(bf16[96,2048]{1,0:T(8,128)(2,1)S(1)} %pad_maximum_fusion.13), channel_id=1, source_target_pairs={{0,3},{1,2},{2,1},{3,0},{4,7},{5,6},{6,5},{7,4},{8,11},{9,10},{10,... | collective-permute-start | bytes 1179656 | tf_op jit(solution)/shard_map/ppermute | solution.py:35
  217.6 18.9 %collective-permute-start.41 = (bf16[96,2048]{1,0:T(8,128)(2,1)S(1)}, bf16[96,2048]{1,0:T(8,128)(2,1)S(1)}, u32[]{:S(2)}, u32[]{:S(2)}) collective-permute-start(bf16[96,2048]{1,0:T(8,128)(2,1)S(1)} %pad_maximum_fusion.11), channel_id=1, source_target_pairs={{0,2},{1,3},{2,0},{3,1},{4,6},{5,7},{6,4},{7,5},{8,10},{9,11},{10,... | collective-permute-start | bytes 1179656 | tf_op jit(solution)/shard_map/ppermute | solution.py:35
  219.0 17.5 %collective-permute-start.39 = (bf16[96,2048]{1,0:T(8,128)(2,1)S(1)}, bf16[96,2048]{1,0:T(8,128)(2,1)S(1)}, u32[]{:S(2)}, u32[]{:S(2)}) collective-permute-start(bf16[96,2048]{1,0:T(8,128)(2,1)S(1)} %pad_maximum_fusion.9), channel_id=1, source_target_pairs={{0,1},{1,0},{2,3},{3,2},{4,5},{5,4},{6,7},{7,6},{8,9},{9,8},{10,11... | collective-permute-start | bytes 1179656 | tf_op jit(solution)/shard_map/ppermute | solution.py:35
  221.5 40.4 %collective-permute-start.23 = (bf16[128,2048]{1,0:T(8,128)(2,1)S(1)}, bf16[128,2048]{1,0:T(8,128)(2,1)S(1)}, u32[]{:S(2)}, u32[]{:S(2)}) collective-permute-start(bf16[128,2048]{1,0:T(8,128)(2,1)S(1)} %combine.4), channel_id=1, source_target_pairs={{0,8},{4,12},{8,0},{12,4},{16,24},{20,28},{24,16},{28,20},{1,9},{5... | collective-permute-start | bytes 1572872 | tf_op jit(solution)/shard_map/ppermute | solution.py:35
  237.5 26.3 %collective-permute-start.45 = (bf16[128,2048]{1,0:T(8,128)(2,1)S(1)}, bf16[128,2048]{1,0:T(8,128)(2,1)S(1)}, u32[]{:S(2)}, u32[]{:S(2)}) collective-permute-start(bf16[128,2048]{1,0:T(8,128)(2,1)S(1)} %combine.6), channel_id=1, source_target_pairs={{0,16},{4,20},{8,24},{12,28},{16,0},{20,4},{24,8},{28,12},{1,17},{... | collective-permute-start | bytes 1572872 | tf_op jit(solution)/shard_map/ppermute | solution.py:35
  241.0 13.1 %collective-permute-start.50 = (bf16[96,2048]{1,0:T(8,128)(2,1)S(1)}, bf16[96,2048]{1,0:T(8,128)(2,1)S(1)}, u32[]{:S(2)}, u32[]{:S(2)}) collective-permute-start(bf16[96,2048]{1,0:T(8,128)(2,1)S(1)} %pad_maximum_fusion.19), channel_id=1, source_target_pairs={{0,3},{1,2},{2,1},{3,0},{4,7},{5,6},{6,5},{7,4},{8,11},{9,10},{10,... | collective-permute-start | bytes 1179656 | tf_op jit(solution)/shard_map/ppermute | solution.py:35
  242.3 18.3 %collective-permute-start.49 = (bf16[96,2048]{1,0:T(8,128)(2,1)S(1)}, bf16[96,2048]{1,0:T(8,128)(2,1)S(1)}, u32[]{:S(2)}, u32[]{:S(2)}) collective-permute-start(bf16[96,2048]{1,0:T(8,128)(2,1)S(1)} %pad_maximum_fusion.18), channel_id=1, source_target_pairs={{0,2},{1,3},{2,0},{3,1},{4,6},{5,7},{6,4},{7,5},{8,10},{9,11},{10,... | collective-permute-start | bytes 1179656 | tf_op jit(solution)/shard_map/ppermute | solution.py:35
  243.7 17.2 %collective-permute-start.48 = (bf16[96,2048]{1,0:T(8,128)(2,1)S(1)}, bf16[96,2048]{1,0:T(8,128)(2,1)S(1)}, u32[]{:S(2)}, u32[]{:S(2)}) collective-permute-start(bf16[96,2048]{1,0:T(8,128)(2,1)S(1)} %pad_maximum_fusion.17), channel_id=1, source_target_pairs={{0,1},{1,0},{2,3},{3,2},{4,5},{5,4},{6,7},{7,6},{8,9},{9,8},{10,11... | collective-permute-start | bytes 1179656 | tf_op jit(solution)/shard_map/ppermute | solution.py:35
  (17 other events, 188.4 us)
Sparse Core Ops, SparseCore 0:
  24.2 30.9 all-gather.1

commit v12 on v11

--- a/solution.py
+++ b/solution.py
@@ -247,8 +247,7 @@
 
 
 def combine_kernel(group, capacity, place, routing, *refs):
-    count = routing.shape[1]
-    returned, passing, out = refs[:count], refs[count:-1], refs[-1]
+    *returned, out = refs
     slots = lax.broadcasted_iota(jnp.int32, (capacity, out.shape[0]), 0)
     parts = []
     for distance in range(len(returned)):
@@ -256,12 +255,9 @@
             parts.append(jnp.where(slots == slot, weight, 0.0))
     shares = jnp.concatenate(parts, axis=0).astype(jnp.bfloat16)
     produced = jnp.concatenate([ref[...] for ref in returned], axis=0)
-    total = lax.dot_general(
+    out[...] = lax.dot_general(
         shares, produced, (((0,), (0,)), ((), ())), preferred_element_type=jnp.float32
-    )
-    for part in passing:
-        total = total + part[...].astype(jnp.float32)
-    out[...] = total.astype(out.dtype)
+    ).astype(jnp.bfloat16)
 
 
 def expert_kernel(routes, capacity, *refs):
@@ -442,10 +438,7 @@
     low, high = [0, 1], list(range(0, exp_count, 2))
     routes = [(low, high), (high, low)]
     half = width // 2
-    far = [normed]
-    for g in range(1, groups):
-        first = tie(far[g & (g - 1)], *(far[1:] if g == 2 else []))
-        far.append(swap(first, "ctx", 2 * (g & -g)))
+    far = [normed] + [swap(normed, "ctx", 2 * g) for g in (1, 2) if g < groups]
     in_flight = {}
 
     def send(array, d, kind):
@@ -459,12 +452,16 @@
         for side, (near, _) in enumerate(routes):
             part = far[g][:, side * half : (side + 1) * half]
             sources += [part] + [send(part, n, "whole") for n in near[1:]]
+        ahead = g + 2
+        if g and ahead < groups:
+            first = far[ahead & (ahead - 1)]
+            far.append(swap(tie(first, *sources), "ctx", 2 * (ahead & -ahead)))
         outgoing = call(
             functools.partial(dispatch_kernel, routes, g, capacity),
             [bf16((2 * len(near) * capacity, half)) for near, away in routes for _ in away],
             [SMEM, VMEM] + [VMEM] * len(sources),
             place,
-            tie(routing, *[part for came in arrived[-1:] for part in came]),
+            routing,
             *sources,
             name="dispatch",
         )
@@ -473,14 +470,14 @@
 
     produced = []
     slots = exp_count * capacity
-    for came in arrived:
+    for g, came in enumerate(arrived):
         mate = jnp.concatenate([part[part.shape[0] // 2 :] for part in came], axis=0)
         own, other = call(
             functools.partial(expert_kernel, routes, capacity),
             [bf16((slots, width)), bf16((slots, width))],
             [VMEM] * (len(came) + 4),
             *came,
-            swap(mate, "ctx", 1),
+            swap(tie(mate, *(produced[-1][1] if g == groups - 1 else ())), "ctx", 1),
             w_gate[0],
             w_up[0],
             w_down[0],
@@ -490,37 +487,43 @@
                 pltpu.VMEM((2 * slots, w_gate.shape[2]), jnp.bfloat16),
             ],
         )
-        produced.append((own, swap(other, "ctx", 1)))
-
-    passing, in_flight = [[] for _ in range(groups)], {}
-    for g in [*range(1, min(2, groups)), *reversed(range(2, groups)), 0]:
+        ours = [slice(d * capacity, (d + 1) * capacity) for d in peers]
+        if g == groups - 2:
+            mates = [swap(other[mine], "ctx", 1) for mine in ours]
+        else:
+            mates = swap(other, "ctx", 1)
+            mates = [mates[mine] for mine in ours]
+        produced.append(([own[mine] for mine in ours], mates))
+
+    totals, hop, in_flight = [], (), {}
+    for g in [*range(2, groups), *(g for g in (1, 0) if g < groups)]:
         back = []
         for d in peers:
-            mine = slice(d * capacity, (d + 1) * capacity)
-            back.append(jnp.concatenate([part[mine] for part in produced[g]], axis=0))
+            back.append(jnp.concatenate([part[d] for part in produced[g]], axis=0))
         back = [back[0]] + [send(back[d], d, "back") for d in peers[1:]]
         total = call(
             functools.partial(combine_kernel, g, capacity),
-            bf16((rows, width)) if g else jax.ShapeDtypeStruct((rows, width), jnp.float32),
-            [SMEM, VMEM] + [VMEM] * (exp_count + (len(passing[g]) if g else 0)),
+            bf16((rows, width)),
+            [SMEM, VMEM] + [VMEM] * exp_count,
             place,
             routing,
             *back,
-            *(passing[g] if g else []),
             name="combine",
         )
         if g:
-            passing[g & (g - 1)].append(swap(total, "ctx", 2 * (g & -g)))
+            total = swap(tie(total, *(hop if g > 1 else ())), "ctx", 2 * g)
+            hop = (total,)
+        totals.append(total)
     early = call(
         sum_kernel,
         jax.ShapeDtypeStruct((rows, width), jnp.float32),
-        [VMEM] * (1 + len(passing[0])),
+        [VMEM] * groups,
         residual,
-        *passing[0],
+        *totals[:-1],
         name="add",
         flops=10_000_000_000,
     )
-    return call(sum_kernel, bf16((rows, width)), [VMEM] * 2, early, total, name="add")
+    return call(sum_kernel, bf16((rows, width)), [VMEM] * 2, early, totals[-1], name="add")
 
 
 def solution(mesh):

time: 272 us -> 263 us (0.967)
  waiting for transfers between devices: 151 us -> 140 us
  starting transfers between devices: 56.6 us -> 60 us
    ppermute x51 -> x54, waiting for transfers between devices: 147 us -> 136 us  [swap(): return lax.ppermute(array, axis, pairs)]
    ppermute x51 -> x54, starting transfers between devices: 56.6 us -> 60 us  [swap(): return lax.ppermute(array, axis, pairs)]
  transfers between devices with their start and end apart: 52 -> 55, of which waited for: 33 -> 33; matrix products, arithmetic and copies ran while one was open for 1% -> 1% of each run, Pallas kernels for 11% -> 12%
where the time goes in v12:
time: 263 us
  waiting for transfers between devices  140 us (53%)
  starting transfers between devices  60 us (23%)
  Pallas kernels  39.4 us (15%)
  between operations  14.2 us (5%)
  local copies, waits for them, and re-layouts  6.58 us (3%)
  other arithmetic  3.24 us (1%)
    ppermute x54, waiting for transfers between devices, swap(): return lax.ppermute(array, axis, pairs)  136 us
    ppermute x54, starting transfers between devices, swap(): return lax.ppermute(array, axis, pairs)  60 us
    pallas_call x23, Pallas kernels, call(): pl.pallas_call(kernel, out_shape=out_shape, in_specs=specs, out_specs=jax...  39.4 us
    unnamed x33, local copies, waits for them, and re-layouts  5.6 us
  transfers between devices with their start and end apart: 55, of which 33 were waited for; matrix products, arithmetic and copies ran while one was open for 1% of the time, Pallas kernels for 12%

profile of v12, /device:TPU:0, one launch (start us, length us, event | category | flops | bytes accessed | tf_op | source)
XLA Modules:
  0.0 263.1 jit_solution(14493499016866210862)
XLA Ops:
  8.1 4.5 %own_rows.1 = (bf16[144,256]{1,0:T(8,128)(2,1)}, bf16[144,256]{1,0:T(8,128)(2,1)}, bf16[144,256]{1,0:T(8,128)(2,1)}, bf16[144,256]{1,0:T(8,128)(2,1)}) custom-call(s32[6]{0:T(128)} %pad_add_fusion.place, s32[8,128]{1,0:T(8,128)} %bitcast.38, s32[8,128]{1,0:T(8,128)} %bitcast.39, bf16[128,2048]{1,0:T(8,128)(2,1)} %tokens.1, f32[1,2048]{1,0:T(1,128)} %bitcast.34, ...), custom_call_target="tpu_custom_call" | custom-call | flops 1000 | bytes 1000 | tf_op jit(solution)/shard_map/own_rows/pallas_call | solution.py:306
  12.6 3.0 %collective-permute-start = (bf16[144,256]{1,0:T(8,128)(2,1)}, bf16[144,256]{1,0:T(8,128)(2,1)S(1)}, u32[]{:S(2)}, u32[]{:S(2)}) collective-permute-start(bf16[144,256]{1,0:T(8,128)(2,1)} %get-tuple-element.63), channel_id=1, source_target_pairs={{0,1},{1,0},{2,3},{3,2},{4,5},{5,4},{6,7},{7,6},{8,9},{9,8},{10,11... | collective-permute-start | bytes 221192 | tf_op jit(solution)/shard_map/ppermute | solution.py:35
  18.5 1.7 collective-permute-done.1
  20.2 2.4 collective-permute-done.2
  25.1 2.5 collective-permute-start.5
  28.6 10.4 %collective-permute-done.3.refs_1_ = bf16[128,2048]{1,0:T(8,128)(2,1)S(1)} collective-permute-done((bf16[128,2048]{1,0:T(8,128)(2,1)S(1)}, bf16[128,2048]{1,0:T(8,128)(2,1)S(1)}, u32[]{:S(2)}, u32[]{:S(2)}) %collective-permute-start.3) | collective-permute-done | bytes 524320 | tf_op jit(solution)/shard_map/ppermute | solution.py:35
  39.0 9.1 %collective-permute-done.4.refs_2_ = bf16[128,2048]{1,0:T(8,128)(2,1)S(1)} collective-permute-done((bf16[128,2048]{1,0:T(8,128)(2,1)S(1)}, bf16[128,2048]{1,0:T(8,128)(2,1)S(1)}, u32[]{:S(2)}, u32[]{:S(2)}) %collective-permute-start.4) | collective-permute-done | bytes 524320 | tf_op jit(solution)/shard_map/ppermute | solution.py:35
  49.7 1.8 queries.1
  51.6 3.6 %all-gather.2.cloned.1.call-done.both = bf16[4608,256]{1,0:T(8,128)(2,1)} async-done(((bf16[576,256]{1,0:T(8,128)(2,1)}), bf16[4608,256]{1,0:T(8,128)(2,1)}) %all-gather.2.cloned.1.call-update) | async-done | bytes 2359312 | tf_op jit(solution)/shard_map/all_gather | solution.py:375
  55.2 1.7 copy-done.3
  56.9 1.7 attention.4
  58.6 2.4 collective-permute-start.6
  61.1 1.7 attention.5
  63.4 1.9 attention.6
  66.0 1.7 attention.7.refs_0_
  67.7 6.7 %collective-permute-done.6.refs_1_ = bf16[128,2048]{1,0:T(8,128)(2,1)S(1)} collective-permute-done((bf16[128,2048]{1,0:T(8,128)(2,1)S(1)}, bf16[128,2048]{1,0:T(8,128)(2,1)S(1)}, u32[]{:S(2)}, u32[]{:S(2)}) %collective-permute-start.6) | collective-permute-done | bytes 524320 | tf_op jit(solution)/shard_map/ppermute | solution.py:35
  74.6 11.0 %collective-permute-done.7.refs_1_ = bf16[128,2048]{1,0:T(8,128)(2,1)S(1)} collective-permute-done((bf16[128,2048]{1,0:T(8,128)(2,1)S(1)}, bf16[128,2048]{1,0:T(8,128)(2,1)S(1)}, u32[]{:S(2)}, u32[]{:S(2)}) %collective-permute-start.7) | collective-permute-done | bytes 524320 | tf_op jit(solution)/shard_map/ppermute | solution.py:35
  86.2 2.3 collective-permute-start.10
  91.3 3.9 %collective-permute-start.9 = (bf16[128,2048]{1,0:T(8,128)(2,1)S(1)}, bf16[128,2048]{1,0:T(8,128)(2,1)S(1)}, u32[]{:S(2)}, u32[]{:S(2)}) collective-permute-start(bf16[128,2048]{1,0:T(8,128)(2,1)S(1)} %get-tuple-element.72), channel_id=1, source_target_pairs={{0,16},{4,20},{8,24},{12,28},{16,0},{20,4},{24,8},{28,12},{1,17},{... | collective-permute-start | bytes 1572872 | tf_op jit(solution)/shard_map/ppermute | solution.py:35
  100.8 9.4 %collective-permute-done.10 = bf16[128,2048]{1,0:T(8,128)(2,1)S(1)} collective-permute-done((bf16[128,2048]{1,0:T(8,128)(2,1)S(1)}, bf16[128,2048]{1,0:T(8,128)(2,1)S(1)}, u32[]{:S(2)}, u32[]{:S(2)}) %collective-permute-start.10) | collective-permute-done | bytes 524320 | tf_op jit(solution)/shard_map/ppermute | solution.py:35
  110.2 2.4 collective-permute-start.12
  112.9 5.5 %collective-permute-done.9 = bf16[128,2048]{1,0:T(8,128)(2,1)S(1)} collective-permute-done((bf16[128,2048]{1,0:T(8,128)(2,1)S(1)}, bf16[128,2048]{1,0:T(8,128)(2,1)S(1)}, u32[]{:S(2)}, u32[]{:S(2)}) %collective-permute-start.9) | collective-permute-done | bytes 524320 | tf_op jit(solution)/shard_map/ppermute | solution.py:35
  118.6 1.7 collective-permute-start.13
  123.4 4.0 %collective-permute-done.13.refs_1_ = bf16[128,1024]{1,0:T(8,128)(2,1)S(1)} collective-permute-done((bf16[128,1024]{1,0:T(8,128)(2,1)S(1)}, bf16[128,1024]{1,0:T(8,128)(2,1)S(1)}, u32[]{:S(2)}, u32[]{:S(2)}) %collective-permute-start.13) | collective-permute-done | bytes 262176 | tf_op jit(solution)/shard_map/ppermute | solution.py:35
  128.7 10.1 %collective-permute-done.16.refs_3_ = bf16[128,1024]{1,0:T(8,128)(2,1)S(1)} collective-permute-done((bf16[128,1024]{1,0:T(8,128)(2,1)S(1)}, bf16[128,1024]{1,0:T(8,128)(2,1)S(1)}, u32[]{:S(2)}, u32[]{:S(2)}) %collective-permute-start.16) | collective-permute-done | bytes 262176 | tf_op jit(solution)/shard_map/ppermute | solution.py:35
  142.5 1.7 collective-permute-start.34
  144.4 3.9 %expert.7 = (bf16[192,2048]{1,0:T(8,128)(2,1)S(1)}, bf16[192,2048]{1,0:T(8,128)(2,1)S(1)}) custom-call(bf16[192,1024]{1,0:T(8,128)(2,1)S(1)} %get-tuple-element.114.refs_0_, bf16[192,1024]{1,0:T(8,128)(2,1)S(1)} %collective-permute-done.17.refs_1_, bf16[192,1024]{1,0:T(8,128)(2,1)S(1)} %get-tuple-element.115.refs_2_, ...), custom_call_target="tpu_custom_call" | custom-call | flops 1000 | bytes 1000 | tf_op jit(solution)/shard_map/expert/pallas_call | solution.py:306
  148.3 8.1 %collective-permute-done.33.refs_1_ = bf16[128,1024]{1,0:T(8,128)(2,1)S(1)} collective-permute-done((bf16[128,1024]{1,0:T(8,128)(2,1)S(1)}, bf16[128,1024]{1,0:T(8,128)(2,1)S(1)}, u32[]{:S(2)}, u32[]{:S(2)}) %collective-permute-start.33) | collective-permute-done | bytes 262176 | tf_op jit(solution)/shard_map/ppermute | solution.py:35
  157.6 1.7 collective-permute-start.35
  159.9 3.9 %expert.6 = (bf16[192,2048]{1,0:T(8,128)(2,1)S(1)}, bf16[192,2048]{1,0:T(8,128)(2,1)S(1)}) custom-call(bf16[192,1024]{1,0:T(8,128)(2,1)S(1)} %get-tuple-element.107.refs_0_, bf16[192,1024]{1,0:T(8,128)(2,1)S(1)} %collective-permute-done.18.refs_1_, bf16[192,1024]{1,0:T(8,128)(2,1)S(1)} %get-tuple-element.108.refs_2_, ...), custom_call_target="tpu_custom_call" | custom-call | flops 1000 | bytes 1000 | tf_op jit(solution)/shard_map/expert/pallas_call | solution.py:306
  164.3 6.2 %collective-permute-done.36.refs_3_ = bf16[192,1024]{1,0:T(8,128)(2,1)S(1)} collective-permute-done((bf16[192,1024]{1,0:T(8,128)(2,1)S(1)}, bf16[192,1024]{1,0:T(8,128)(2,1)S(1)}, u32[]{:S(2)}, u32[]{:S(2)}) %collective-permute-start.36) | collective-permute-done | bytes 393248 | tf_op jit(solution)/shard_map/ppermute | solution.py:35
  170.9 4.1 %expert.4 = (bf16[192,2048]{1,0:T(8,128)(2,1)S(1)}, bf16[192,2048]{1,0:T(8,128)(2,1)S(1)}) custom-call(bf16[192,1024]{1,0:T(8,128)(2,1)S(1)} %get-tuple-element.77.refs_0_, bf16[192,1024]{1,0:T(8,128)(2,1)S(1)} %collective-permute-done.19.refs_1_, bf16[192,1024]{1,0:T(8,128)(2,1)S(1)} %get-tuple-element.83.refs_2_, ...), custom_call_target="tpu_custom_call" | custom-call | flops 1000 | bytes 1000 | tf_op jit(solution)/shard_map/expert/pallas_call | solution.py:306
  179.6 1.8 collective-permute-start.30
  181.5 3.9 %expert.5 = (bf16[192,2048]{1,0:T(8,128)(2,1)S(1)}, bf16[192,2048]{1,0:T(8,128)(2,1)S(1)}) custom-call(bf16[192,1024]{1,0:T(8,128)(2,1)S(1)} %get-tuple-element.94.refs_0_, bf16[192,1024]{1,0:T(8,128)(2,1)S(1)} %collective-permute-done.35.refs_1_, bf16[192,1024]{1,0:T(8,128)(2,1)S(1)} %get-tuple-element.97.refs_2_, ...), custom_call_target="tpu_custom_call" | custom-call | flops 1000 | bytes 1000 | tf_op jit(solution)/shard_map/expert/pallas_call | solution.py:306
  185.6 2.1 collective-permute-done.38
  187.8 1.9 collective-permute-done.26.refs_1_
  190.0 7.5 %collective-permute-done.28.refs_2_ = bf16[96,2048]{1,0:T(8,128)(2,1)S(1)} collective-permute-done((bf16[96,2048]{1,0:T(8,128)(2,1)S(1)}, bf16[96,2048]{1,0:T(8,128)(2,1)S(1)}, u32[]{:S(2)}, u32[]{:S(2)}) %collective-permute-start.28) | collective-permute-done | bytes 393248 | tf_op jit(solution)/shard_map/ppermute | solution.py:35
  198.0 3.4 %collective-permute-start.41 = (bf16[96,2048]{1,0:T(8,128)(2,1)S(1)}, bf16[96,2048]{1,0:T(8,128)(2,1)S(1)}, u32[]{:S(2)}, u32[]{:S(2)}) collective-permute-start(bf16[96,2048]{1,0:T(8,128)(2,1)S(1)} %pad_maximum_fusion.11), channel_id=1, source_target_pairs={{0,3},{1,2},{2,1},{3,0},{4,7},{5,6},{6,5},{7,4},{8,11},{9,10},{10,... | collective-permute-start | bytes 1179656 | tf_op jit(solution)/shard_map/ppermute | solution.py:35
  202.5 3.3 %collective-permute-start.31 = (bf16[128,2048]{1,0:T(8,128)(2,1)S(1)}, bf16[128,2048]{1,0:T(8,128)(2,1)S(1)}, u32[]{:S(2)}, u32[]{:S(2)}) collective-permute-start(bf16[128,2048]{1,0:T(8,128)(2,1)S(1)} %combine.4), channel_id=1, source_target_pairs={{0,16},{4,20},{8,24},{12,28},{16,0},{20,4},{24,8},{28,12},{1,17},{... | collective-permute-start | bytes 1572872 | tf_op jit(solution)/shard_map/ppermute | solution.py:35
  206.9 7.4 %collective-permute-done.40.refs_2_ = bf16[96,2048]{1,0:T(8,128)(2,1)S(1)} collective-permute-done((bf16[96,2048]{1,0:T(8,128)(2,1)S(1)}, bf16[96,2048]{1,0:T(8,128)(2,1)S(1)}, u32[]{:S(2)}, u32[]{:S(2)}) %collective-permute-start.40) | collective-permute-done | bytes 393248 | tf_op jit(solution)/shard_map/ppermute | solution.py:35
  214.9 3.2 %collective-permute-start.47 = (bf16[96,2048]{1,0:T(8,128)(2,1)S(1)}, bf16[96,2048]{1,0:T(8,128)(2,1)S(1)}, u32[]{:S(2)}, u32[]{:S(2)}) collective-permute-start(bf16[96,2048]{1,0:T(8,128)(2,1)S(1)} %pad_maximum_fusion.15), channel_id=1, source_target_pairs={{0,3},{1,2},{2,1},{3,0},{4,7},{5,6},{6,5},{7,4},{8,11},{9,10},{10,... | collective-permute-start | bytes 1179656 | tf_op jit(solution)/shard_map/ppermute | solution.py:35
  219.2 7.2 %collective-permute-done.31.refs_1_ = bf16[128,2048]{1,0:T(8,128)(2,1)S(1)} collective-permute-done((bf16[128,2048]{1,0:T(8,128)(2,1)S(1)}, bf16[128,2048]{1,0:T(8,128)(2,1)S(1)}, u32[]{:S(2)}, u32[]{:S(2)}) %collective-permute-start.31) | collective-permute-done | bytes 524320 | tf_op jit(solution)/shard_map/ppermute | solution.py:35
  226.5 1.7 collective-permute-start.42
  228.2 3.1 %collective-permute-done.46.refs_2_ = bf16[96,2048]{1,0:T(8,128)(2,1)S(1)} collective-permute-done((bf16[96,2048]{1,0:T(8,128)(2,1)S(1)}, bf16[96,2048]{1,0:T(8,128)(2,1)S(1)}, u32[]{:S(2)}, u32[]{:S(2)}) %collective-permute-start.46) | collective-permute-done | bytes 393248 | tf_op jit(solution)/shard_map/ppermute | solution.py:35
  232.3 2.1 collective-permute-start.48
  234.5 1.8 collective-permute-start.51
  238.1 8.5 %collective-permute-done.51.refs_1_ = bf16[96,2048]{1,0:T(8,128)(2,1)S(1)} collective-permute-done((bf16[96,2048]{1,0:T(8,128)(2,1)S(1)}, bf16[96,2048]{1,0:T(8,128)(2,1)S(1)}, u32[]{:S(2)}, u32[]{:S(2)}) %collective-permute-start.51) | collective-permute-done | bytes 393248 | tf_op jit(solution)/shard_map/ppermute | solution.py:35
  247.5 6.6 %collective-permute-done.53.refs_3_ = bf16[96,2048]{1,0:T(8,128)(2,1)S(1)} collective-permute-done((bf16[96,2048]{1,0:T(8,128)(2,1)S(1)}, bf16[96,2048]{1,0:T(8,128)(2,1)S(1)}, u32[]{:S(2)}, u32[]{:S(2)}) %collective-permute-start.53) | collective-permute-done | bytes 393248 | tf_op jit(solution)/shard_map/ppermute | solution.py:35
  (179 shorter events, 46.5 us)
Async XLA Ops:
  6.5 48.7 %all-gather.2.cloned.1.call-start = ((), (), s32[]{:S(2)}) async-start(), calls=%async_computation | async-start | bytes 2654208 | tf_op jit(solution)/shard_map/all_gather | solution.py:375
  12.6 5.9 %collective-permute-start = (bf16[144,256]{1,0:T(8,128)(2,1)}, bf16[144,256]{1,0:T(8,128)(2,1)S(1)}, u32[]{:S(2)}, u32[]{:S(2)}) collective-permute-start(bf16[144,256]{1,0:T(8,128)(2,1)} %get-tuple-element.63), channel_id=1, source_target_pairs={{0,1},{1,0},{2,3},{3,2},{4,5},{5,4},{6,7},{7,6},{8,9},{9,8},{10,11... | collective-permute-start | bytes 221192 | tf_op jit(solution)/shard_map/ppermute | solution.py:35
  17.1 5.5 %collective-permute-start.2 = (bf16[144,256]{1,0:T(8,128)(2,1)}, bf16[144,256]{1,0:T(8,128)(2,1)S(1)}, u32[]{:S(2)}, u32[]{:S(2)}) collective-permute-start(bf16[144,256]{1,0:T(8,128)(2,1)} %get-tuple-element.65), channel_id=1, source_target_pairs={{0,3},{1,2},{2,1},{3,0},{4,7},{5,6},{6,5},{7,4},{8,11},{9,10},{10,... | collective-permute-start | bytes 221192 | tf_op jit(solution)/shard_map/ppermute | solution.py:35
  24.1 14.9 %collective-permute-start.3 = (bf16[128,2048]{1,0:T(8,128)(2,1)S(1)}, bf16[128,2048]{1,0:T(8,128)(2,1)S(1)}, u32[]{:S(2)}, u32[]{:S(2)}) collective-permute-start(bf16[128,2048]{1,0:T(8,128)(2,1)S(1)} %copy-done.6), channel_id=1, source_target_pairs={{0,1},{1,0},{2,3},{3,2},{4,5},{5,4},{6,7},{7,6},{8,9},{9,8},{10,11... | collective-permute-start | bytes 1572872 | tf_op jit(solution)/shard_map/ppermute | solution.py:35
  24.7 23.4 %collective-permute-start.4 = (bf16[128,2048]{1,0:T(8,128)(2,1)S(1)}, bf16[128,2048]{1,0:T(8,128)(2,1)S(1)}, u32[]{:S(2)}, u32[]{:S(2)}) collective-permute-start(bf16[128,2048]{1,0:T(8,128)(2,1)S(1)} %copy-done.6), channel_id=1, source_target_pairs={{0,2},{1,3},{2,0},{3,1},{4,6},{5,7},{6,4},{7,5},{8,10},{9,11},{10,... | collective-permute-start | bytes 1572872 | tf_op jit(solution)/shard_map/ppermute | solution.py:35
  25.1 22.9 %collective-permute-start.5 = (bf16[128,2048]{1,0:T(8,128)(2,1)S(1)}, bf16[128,2048]{1,0:T(8,128)(2,1)S(1)}, u32[]{:S(2)}, u32[]{:S(2)}) collective-permute-start(bf16[128,2048]{1,0:T(8,128)(2,1)S(1)} %copy-done.6), channel_id=1, source_target_pairs={{0,3},{1,2},{2,1},{3,0},{4,7},{5,6},{6,5},{7,4},{8,11},{9,10},{10,... | collective-permute-start | bytes 1572872 | tf_op jit(solution)/shard_map/ppermute | solution.py:35
  58.6 15.9 %collective-permute-start.6 = (bf16[128,2048]{1,0:T(8,128)(2,1)S(1)}, bf16[128,2048]{1,0:T(8,128)(2,1)S(1)}, u32[]{:S(2)}, u32[]{:S(2)}) collective-permute-start(bf16[128,2048]{1,0:T(8,128)(2,1)S(1)} %attention.4), channel_id=1, source_target_pairs={{0,3},{1,2},{2,1},{3,0},{4,7},{5,6},{6,5},{7,4},{8,11},{9,10},{10,... | collective-permute-start | bytes 1572872 | tf_op jit(solution)/shard_map/ppermute | solution.py:35
  62.8 22.9 %collective-permute-start.7 = (bf16[128,2048]{1,0:T(8,128)(2,1)S(1)}, bf16[128,2048]{1,0:T(8,128)(2,1)S(1)}, u32[]{:S(2)}, u32[]{:S(2)}) collective-permute-start(bf16[128,2048]{1,0:T(8,128)(2,1)S(1)} %attention.5), channel_id=1, source_target_pairs={{0,1},{1,0},{2,3},{3,2},{4,5},{5,4},{6,7},{7,6},{8,9},{9,8},{10,11... | collective-permute-start | bytes 1572872 | tf_op jit(solution)/shard_map/ppermute | solution.py:35
  65.4 20.5 %collective-permute-start.8 = (bf16[128,2048]{1,0:T(8,128)(2,1)S(1)}, bf16[128,2048]{1,0:T(8,128)(2,1)S(1)}, u32[]{:S(2)}, u32[]{:S(2)}) collective-permute-start(bf16[128,2048]{1,0:T(8,128)(2,1)S(1)} %attention.6), channel_id=1, source_target_pairs={{0,2},{1,3},{2,0},{3,1},{4,6},{5,7},{6,4},{7,5},{8,10},{9,11},{10,... | collective-permute-start | bytes 1572872 | tf_op jit(solution)/shard_map/ppermute | solution.py:35
  86.2 24.0 %collective-permute-start.10 = (bf16[128,2048]{1,0:T(8,128)(2,1)S(1)}, bf16[128,2048]{1,0:T(8,128)(2,1)S(1)}, u32[]{:S(2)}, u32[]{:S(2)}) collective-permute-start(bf16[128,2048]{1,0:T(8,128)(2,1)S(1)} %get-tuple-element.72), channel_id=1, source_target_pairs={{0,8},{4,12},{8,0},{12,4},{16,24},{20,28},{24,16},{28,20},{1,9},{5... | collective-permute-start | bytes 1572872 | tf_op jit(solution)/shard_map/ppermute | solution.py:35
  88.6 8.1 %collective-permute-start.11 = (bf16[128,1024]{1,0:T(8,128)(2,1)S(1)}, bf16[128,1024]{1,0:T(8,128)(2,1)S(1)}, u32[]{:S(2)}, u32[]{:S(2)}) collective-permute-start(bf16[128,1024]{1,0:T(8,128)(2,1)S(1)} %get-tuple-element.156.refs_0_), channel_id=1, source_target_pairs={{0,1},{1,0},{2,3},{3,2},{4,5},{5,4},{6,7},{7,6},{8,9},{9,8},{10,11... | collective-permute-start | bytes 786440 | tf_op jit(solution)/shard_map/ppermute | solution.py:35
  90.1 7.8 %collective-permute-start.14 = (bf16[128,1024]{1,0:T(8,128)(2,1)S(1)}, bf16[128,1024]{1,0:T(8,128)(2,1)S(1)}, u32[]{:S(2)}, u32[]{:S(2)}) collective-permute-start(bf16[128,1024]{1,0:T(8,128)(2,1)S(1)} %get-tuple-element.155.refs_2_), channel_id=1, source_target_pairs={{0,2},{1,3},{2,0},{3,1},{4,6},{5,7},{6,4},{7,5},{8,10},{9,11},{10,... | collective-permute-start | bytes 786440 | tf_op jit(solution)/shard_map/ppermute | solution.py:35
  91.3 27.1 %collective-permute-start.9 = (bf16[128,2048]{1,0:T(8,128)(2,1)S(1)}, bf16[128,2048]{1,0:T(8,128)(2,1)S(1)}, u32[]{:S(2)}, u32[]{:S(2)}) collective-permute-start(bf16[128,2048]{1,0:T(8,128)(2,1)S(1)} %get-tuple-element.72), channel_id=1, source_target_pairs={{0,16},{4,20},{8,24},{12,28},{16,0},{20,4},{24,8},{28,12},{1,17},{... | collective-permute-start | bytes 1572872 | tf_op jit(solution)/shard_map/ppermute | solution.py:35
  99.0 19.5 %collective-permute-start.17 = (bf16[192,1024]{1,0:T(8,128)(2,1)S(1)}, bf16[192,1024]{1,0:T(8,128)(2,1)S(1)}, u32[]{:S(2)}, u32[]{:S(2)}) collective-permute-start(bf16[192,1024]{1,0:T(8,128)(2,1)S(1)} %get-tuple-element.80), channel_id=1, source_target_pairs={{0,2},{1,3},{2,0},{3,1},{4,6},{5,7},{6,4},{7,5},{8,10},{9,11},{10,... | collective-permute-start | bytes 1179656 | tf_op jit(solution)/shard_map/ppermute | solution.py:35
  100.2 18.2 %collective-permute-start.20 = (bf16[192,1024]{1,0:T(8,128)(2,1)S(1)}, bf16[192,1024]{1,0:T(8,128)(2,1)S(1)}, u32[]{:S(2)}, u32[]{:S(2)}) collective-permute-start(bf16[192,1024]{1,0:T(8,128)(2,1)S(1)} %get-tuple-element.86), channel_id=1, source_target_pairs={{0,1},{1,0},{2,3},{3,2},{4,5},{5,4},{6,7},{7,6},{8,9},{9,8},{10,11... | collective-permute-start | bytes 1179656 | tf_op jit(solution)/shard_map/ppermute | solution.py:35
  110.2 8.4 %collective-permute-start.12 = (bf16[128,1024]{1,0:T(8,128)(2,1)S(1)}, bf16[128,1024]{1,0:T(8,128)(2,1)S(1)}, u32[]{:S(2)}, u32[]{:S(2)}) collective-permute-start(bf16[128,1024]{1,0:T(8,128)(2,1)S(1)} %get-tuple-element.73.refs_0_), channel_id=1, source_target_pairs={{0,1},{1,0},{2,3},{3,2},{4,5},{5,4},{6,7},{7,6},{8,9},{9,8},{10,11... | collective-permute-start | bytes 786440 | tf_op jit(solution)/shard_map/ppermute | solution.py:35
  112.6 7.8 %collective-permute-start.15 = (bf16[128,1024]{1,0:T(8,128)(2,1)S(1)}, bf16[128,1024]{1,0:T(8,128)(2,1)S(1)}, u32[]{:S(2)}, u32[]{:S(2)}) collective-permute-start(bf16[128,1024]{1,0:T(8,128)(2,1)S(1)} %get-tuple-element.75.refs_2_), channel_id=1, source_target_pairs={{0,2},{1,3},{2,0},{3,1},{4,6},{5,7},{6,4},{7,5},{8,10},{9,11},{10,... | collective-permute-start | bytes 786440 | tf_op jit(solution)/shard_map/ppermute | solution.py:35
  118.6 8.7 %collective-permute-start.13 = (bf16[128,1024]{1,0:T(8,128)(2,1)S(1)}, bf16[128,1024]{1,0:T(8,128)(2,1)S(1)}, u32[]{:S(2)}, u32[]{:S(2)}) collective-permute-start(bf16[128,1024]{1,0:T(8,128)(2,1)S(1)} %get-tuple-element.74.refs_0_), channel_id=1, source_target_pairs={{0,1},{1,0},{2,3},{3,2},{4,5},{5,4},{6,7},{7,6},{8,9},{9,8},{10,11... | collective-permute-start | bytes 786440 | tf_op jit(solution)/shard_map/ppermute | solution.py:35
  120.4 21.4 %collective-permute-start.32 = (bf16[128,2048]{1,0:T(8,128)(2,1)S(1)}, bf16[128,2048]{1,0:T(8,128)(2,1)S(1)}, u32[]{:S(2)}, u32[]{:S(2)}) collective-permute-start(bf16[128,2048]{1,0:T(8,128)(2,1)S(1)} %collective-permute-done.9), channel_id=1, source_target_pairs={{0,8},{4,12},{8,0},{12,4},{16,24},{20,28},{24,16},{28,20},{1,9},{5... | collective-permute-start | bytes 1572872 | tf_op jit(solution)/shard_map/ppermute | solution.py:35
  120.4 23.8 %collective-permute-start.49 = (bf16[384,1024]{1,0:T(8,128)(2,1)S(1)}, bf16[384,1024]{1,0:T(8,128)(2,1)S(1)}, u32[]{:S(2)}, u32[]{:S(2)}) collective-permute-start(bf16[384,1024]{1,0:T(8,128)(2,1)S(1)} %pad_maximum_fusion.3), channel_id=1, source_target_pairs={{0,4},{4,0},{8,12},{12,8},{16,20},{20,16},{24,28},{28,24},{1,5},{5... | collective-permute-start | bytes 2359304 | tf_op jit(solution)/shard_map/ppermute | solution.py:35
  121.6 18.3 %collective-permute-start.18 = (bf16[192,1024]{1,0:T(8,128)(2,1)S(1)}, bf16[192,1024]{1,0:T(8,128)(2,1)S(1)}, u32[]{:S(2)}, u32[]{:S(2)}) collective-permute-start(bf16[192,1024]{1,0:T(8,128)(2,1)S(1)} %get-tuple-element.81), channel_id=1, source_target_pairs={{0,2},{1,3},{2,0},{3,1},{4,6},{5,7},{6,4},{7,5},{8,10},{9,11},{10,... | collective-permute-start | bytes 1179656 | tf_op jit(solution)/shard_map/ppermute | solution.py:35
  122.0 18.3 %collective-permute-start.21 = (bf16[192,1024]{1,0:T(8,128)(2,1)S(1)}, bf16[192,1024]{1,0:T(8,128)(2,1)S(1)}, u32[]{:S(2)}, u32[]{:S(2)}) collective-permute-start(bf16[192,1024]{1,0:T(8,128)(2,1)S(1)} %get-tuple-element.87), channel_id=1, source_target_pairs={{0,1},{1,0},{2,3},{3,2},{4,5},{5,4},{6,7},{7,6},{8,9},{9,8},{10,11... | collective-permute-start | bytes 1179656 | tf_op jit(solution)/shard_map/ppermute | solution.py:35
  127.4 11.4 %collective-permute-start.16 = (bf16[128,1024]{1,0:T(8,128)(2,1)S(1)}, bf16[128,1024]{1,0:T(8,128)(2,1)S(1)}, u32[]{:S(2)}, u32[]{:S(2)}) collective-permute-start(bf16[128,1024]{1,0:T(8,128)(2,1)S(1)} %get-tuple-element.76.refs_2_), channel_id=1, source_target_pairs={{0,2},{1,3},{2,0},{3,1},{4,6},{5,7},{6,4},{7,5},{8,10},{9,11},{10,... | collective-permute-start | bytes 786440 | tf_op jit(solution)/shard_map/ppermute | solution.py:35
  139.9 17.6 %collective-permute-start.19 = (bf16[192,1024]{1,0:T(8,128)(2,1)S(1)}, bf16[192,1024]{1,0:T(8,128)(2,1)S(1)}, u32[]{:S(2)}, u32[]{:S(2)}) collective-permute-start(bf16[192,1024]{1,0:T(8,128)(2,1)S(1)} %get-tuple-element.82), channel_id=1, source_target_pairs={{0,2},{1,3},{2,0},{3,1},{4,6},{5,7},{6,4},{7,5},{8,10},{9,11},{10,... | collective-permute-start | bytes 1179656 | tf_op jit(solution)/shard_map/ppermute | solution.py:35
  140.3 19.0 %collective-permute-start.22 = (bf16[192,1024]{1,0:T(8,128)(2,1)S(1)}, bf16[192,1024]{1,0:T(8,128)(2,1)S(1)}, u32[]{:S(2)}, u32[]{:S(2)}) collective-permute-start(bf16[192,1024]{1,0:T(8,128)(2,1)S(1)} %get-tuple-element.88), channel_id=1, source_target_pairs={{0,1},{1,0},{2,3},{3,2},{4,5},{5,4},{6,7},{7,6},{8,9},{9,8},{10,11... | collective-permute-start | bytes 1179656 | tf_op jit(solution)/shard_map/ppermute | solution.py:35
  141.8 14.6 %collective-permute-start.33 = (bf16[128,1024]{1,0:T(8,128)(2,1)S(1)}, bf16[128,1024]{1,0:T(8,128)(2,1)S(1)}, u32[]{:S(2)}, u32[]{:S(2)}) collective-permute-start(bf16[128,1024]{1,0:T(8,128)(2,1)S(1)} %get-tuple-element.92.refs_0_), channel_id=1, source_target_pairs={{0,1},{1,0},{2,3},{3,2},{4,5},{5,4},{6,7},{7,6},{8,9},{9,8},{10,11... | collective-permute-start | bytes 786440 | tf_op jit(solution)/shard_map/ppermute | solution.py:35
  142.5 13.9 %collective-permute-start.34 = (bf16[128,1024]{1,0:T(8,128)(2,1)S(1)}, bf16[128,1024]{1,0:T(8,128)(2,1)S(1)}, u32[]{:S(2)}, u32[]{:S(2)}) collective-permute-start(bf16[128,1024]{1,0:T(8,128)(2,1)S(1)} %get-tuple-element.93.refs_2_), channel_id=1, source_target_pairs={{0,2},{1,3},{2,0},{3,1},{4,6},{5,7},{6,4},{7,5},{8,10},{9,11},{10,... | collective-permute-start | bytes 786440 | tf_op jit(solution)/shard_map/ppermute | solution.py:35
  144.3 15.6 %collective-permute-start.43 = (bf16[384,1024]{1,0:T(8,128)(2,1)S(1)}, bf16[384,1024]{1,0:T(8,128)(2,1)S(1)}, u32[]{:S(2)}, u32[]{:S(2)}) collective-permute-start(bf16[384,1024]{1,0:T(8,128)(2,1)S(1)} %pad_maximum_fusion.2), channel_id=1, source_target_pairs={{0,4},{4,0},{8,12},{12,8},{16,20},{20,16},{24,28},{28,24},{1,5},{5... | collective-permute-start | bytes 2359304 | tf_op jit(solution)/shard_map/ppermute | solution.py:35
  156.4 14.3 %collective-permute-start.50 = (bf16[192,2048]{1,0:T(8,128)(2,1)S(1)}, bf16[192,2048]{1,0:T(8,128)(2,1)S(1)}, u32[]{:S(2)}, u32[]{:S(2)}) collective-permute-start(bf16[192,2048]{1,0:T(8,128)(2,1)S(1)} %get-tuple-element.117), channel_id=1, source_target_pairs={{0,4},{4,0},{8,12},{12,8},{16,20},{20,16},{24,28},{28,24},{1,5},{5... | collective-permute-start | bytes 2359304 | tf_op jit(solution)/shard_map/ppermute | solution.py:35
  157.6 13.0 %collective-permute-start.35 = (bf16[192,1024]{1,0:T(8,128)(2,1)S(1)}, bf16[192,1024]{1,0:T(8,128)(2,1)S(1)}, u32[]{:S(2)}, u32[]{:S(2)}) collective-permute-start(bf16[192,1024]{1,0:T(8,128)(2,1)S(1)} %get-tuple-element.96), channel_id=1, source_target_pairs={{0,2},{1,3},{2,0},{3,1},{4,6},{5,7},{6,4},{7,5},{8,10},{9,11},{10,... | collective-permute-start | bytes 1179656 | tf_op jit(solution)/shard_map/ppermute | solution.py:35
  159.3 11.3 %collective-permute-start.36 = (bf16[192,1024]{1,0:T(8,128)(2,1)S(1)}, bf16[192,1024]{1,0:T(8,128)(2,1)S(1)}, u32[]{:S(2)}, u32[]{:S(2)}) collective-permute-start(bf16[192,1024]{1,0:T(8,128)(2,1)S(1)} %get-tuple-element.99), channel_id=1, source_target_pairs={{0,1},{1,0},{2,3},{3,2},{4,5},{5,4},{6,7},{7,6},{8,9},{9,8},{10,11... | collective-permute-start | bytes 1179656 | tf_op jit(solution)/shard_map/ppermute | solution.py:35
  159.8 11.1 %collective-permute-start.23 = (bf16[384,1024]{1,0:T(8,128)(2,1)S(1)}, bf16[384,1024]{1,0:T(8,128)(2,1)S(1)}, u32[]{:S(2)}, u32[]{:S(2)}) collective-permute-start(bf16[384,1024]{1,0:T(8,128)(2,1)S(1)} %pad_maximum_fusion), channel_id=1, source_target_pairs={{0,4},{4,0},{8,12},{12,8},{16,20},{20,16},{24,28},{28,24},{1,5},{5... | collective-permute-start | bytes 2359304 | tf_op jit(solution)/shard_map/ppermute | solution.py:35
  163.8 21.7 %collective-permute-start.44 = (bf16[192,2048]{1,0:T(8,128)(2,1)S(1)}, bf16[192,2048]{1,0:T(8,128)(2,1)S(1)}, u32[]{:S(2)}, u32[]{:S(2)}) collective-permute-start(bf16[192,2048]{1,0:T(8,128)(2,1)S(1)} %get-tuple-element.110), channel_id=1, source_target_pairs={{0,4},{4,0},{8,12},{12,8},{16,20},{20,16},{24,28},{28,24},{1,5},{5... | collective-permute-start | bytes 2359304 | tf_op jit(solution)/shard_map/ppermute | solution.py:35
  177.7 12.0 %collective-permute-start.26 = (bf16[96,2048]{1,0:T(8,128)(2,1)S(1)}, bf16[96,2048]{1,0:T(8,128)(2,1)S(1)}, u32[]{:S(2)}, u32[]{:S(2)}) collective-permute-start(bf16[96,2048]{1,0:T(8,128)(2,1)S(1)} %pad_maximum_fusion.5), channel_id=1, source_target_pairs={{0,1},{1,0},{2,3},{3,2},{4,5},{5,4},{6,7},{7,6},{8,9},{9,8},{10,11... | collective-permute-start | bytes 1179656 | tf_op jit(solution)/shard_map/ppermute | solution.py:35
  178.1 19.4 %collective-permute-start.28 = (bf16[96,2048]{1,0:T(8,128)(2,1)S(1)}, bf16[96,2048]{1,0:T(8,128)(2,1)S(1)}, u32[]{:S(2)}, u32[]{:S(2)}) collective-permute-start(bf16[96,2048]{1,0:T(8,128)(2,1)S(1)} %pad_maximum_fusion.6), channel_id=1, source_target_pairs={{0,2},{1,3},{2,0},{3,1},{4,6},{5,7},{6,4},{7,5},{8,10},{9,11},{10,... | collective-permute-start | bytes 1179656 | tf_op jit(solution)/shard_map/ppermute | solution.py:35
  179.6 18.4 %collective-permute-start.30 = (bf16[96,2048]{1,0:T(8,128)(2,1)S(1)}, bf16[96,2048]{1,0:T(8,128)(2,1)S(1)}, u32[]{:S(2)}, u32[]{:S(2)}) collective-permute-start(bf16[96,2048]{1,0:T(8,128)(2,1)S(1)} %pad_maximum_fusion.7), channel_id=1, source_target_pairs={{0,3},{1,2},{2,1},{3,0},{4,7},{5,6},{6,5},{7,4},{8,11},{9,10},{10,... | collective-permute-start | bytes 1179656 | tf_op jit(solution)/shard_map/ppermute | solution.py:35
  189.7 16.9 %collective-permute-start.39 = (bf16[96,2048]{1,0:T(8,128)(2,1)S(1)}, bf16[96,2048]{1,0:T(8,128)(2,1)S(1)}, u32[]{:S(2)}, u32[]{:S(2)}) collective-permute-start(bf16[96,2048]{1,0:T(8,128)(2,1)S(1)} %pad_maximum_fusion.9), channel_id=1, source_target_pairs={{0,1},{1,0},{2,3},{3,2},{4,5},{5,4},{6,7},{7,6},{8,9},{9,8},{10,11... | collective-permute-start | bytes 1179656 | tf_op jit(solution)/shard_map/ppermute | solution.py:35
  197.5 16.7 %collective-permute-start.40 = (bf16[96,2048]{1,0:T(8,128)(2,1)S(1)}, bf16[96,2048]{1,0:T(8,128)(2,1)S(1)}, u32[]{:S(2)}, u32[]{:S(2)}) collective-permute-start(bf16[96,2048]{1,0:T(8,128)(2,1)S(1)} %pad_maximum_fusion.10), channel_id=1, source_target_pairs={{0,2},{1,3},{2,0},{3,1},{4,6},{5,7},{6,4},{7,5},{8,10},{9,11},{10,... | collective-permute-start | bytes 1179656 | tf_op jit(solution)/shard_map/ppermute | solution.py:35
  198.0 16.9 %collective-permute-start.41 = (bf16[96,2048]{1,0:T(8,128)(2,1)S(1)}, bf16[96,2048]{1,0:T(8,128)(2,1)S(1)}, u32[]{:S(2)}, u32[]{:S(2)}) collective-permute-start(bf16[96,2048]{1,0:T(8,128)(2,1)S(1)} %pad_maximum_fusion.11), channel_id=1, source_target_pairs={{0,3},{1,2},{2,1},{3,0},{4,7},{5,6},{6,5},{7,4},{8,11},{9,10},{10,... | collective-permute-start | bytes 1179656 | tf_op jit(solution)/shard_map/ppermute | solution.py:35
  202.5 24.0 %collective-permute-start.31 = (bf16[128,2048]{1,0:T(8,128)(2,1)S(1)}, bf16[128,2048]{1,0:T(8,128)(2,1)S(1)}, u32[]{:S(2)}, u32[]{:S(2)}) collective-permute-start(bf16[128,2048]{1,0:T(8,128)(2,1)S(1)} %combine.4), channel_id=1, source_target_pairs={{0,16},{4,20},{8,24},{12,28},{16,0},{20,4},{24,8},{28,12},{1,17},{... | collective-permute-start | bytes 1572872 | tf_op jit(solution)/shard_map/ppermute | solution.py:35
  206.6 21.6 %collective-permute-start.45 = (bf16[96,2048]{1,0:T(8,128)(2,1)S(1)}, bf16[96,2048]{1,0:T(8,128)(2,1)S(1)}, u32[]{:S(2)}, u32[]{:S(2)}) collective-permute-start(bf16[96,2048]{1,0:T(8,128)(2,1)S(1)} %pad_maximum_fusion.13), channel_id=1, source_target_pairs={{0,1},{1,0},{2,3},{3,2},{4,5},{5,4},{6,7},{7,6},{8,9},{9,8},{10,11... | collective-permute-start | bytes 1179656 | tf_op jit(solution)/shard_map/ppermute | solution.py:35
  214.2 17.1 %collective-permute-start.46 = (bf16[96,2048]{1,0:T(8,128)(2,1)S(1)}, bf16[96,2048]{1,0:T(8,128)(2,1)S(1)}, u32[]{:S(2)}, u32[]{:S(2)}) collective-permute-start(bf16[96,2048]{1,0:T(8,128)(2,1)S(1)} %pad_maximum_fusion.14), channel_id=1, source_target_pairs={{0,2},{1,3},{2,0},{3,1},{4,6},{5,7},{6,4},{7,5},{8,10},{9,11},{10,... | collective-permute-start | bytes 1179656 | tf_op jit(solution)/shard_map/ppermute | solution.py:35
  214.9 16.4 %collective-permute-start.47 = (bf16[96,2048]{1,0:T(8,128)(2,1)S(1)}, bf16[96,2048]{1,0:T(8,128)(2,1)S(1)}, u32[]{:S(2)}, u32[]{:S(2)}) collective-permute-start(bf16[96,2048]{1,0:T(8,128)(2,1)S(1)} %pad_maximum_fusion.15), channel_id=1, source_target_pairs={{0,3},{1,2},{2,1},{3,0},{4,7},{5,6},{6,5},{7,4},{8,11},{9,10},{10,... | collective-permute-start | bytes 1179656 | tf_op jit(solution)/shard_map/ppermute | solution.py:35
  226.5 28.6 %collective-permute-start.42 = (bf16[128,2048]{1,0:T(8,128)(2,1)S(1)}, bf16[128,2048]{1,0:T(8,128)(2,1)S(1)}, u32[]{:S(2)}, u32[]{:S(2)}) collective-permute-start(bf16[128,2048]{1,0:T(8,128)(2,1)S(1)} %combine.5), channel_id=1, source_target_pairs={{0,24},{4,28},{8,16},{12,20},{16,8},{20,12},{24,0},{28,4},{1,25},{... | collective-permute-start | bytes 1572872 | tf_op jit(solution)/shard_map/ppermute | solution.py:35
  232.3 22.8 %collective-permute-start.48 = (bf16[128,2048]{1,0:T(8,128)(2,1)S(1)}, bf16[128,2048]{1,0:T(8,128)(2,1)S(1)}, u32[]{:S(2)}, u32[]{:S(2)}) collective-permute-start(bf16[128,2048]{1,0:T(8,128)(2,1)S(1)} %combine.6), channel_id=1, source_target_pairs={{0,8},{4,12},{8,0},{12,4},{16,24},{20,28},{24,16},{28,20},{1,9},{5... | collective-permute-start | bytes 1572872 | tf_op jit(solution)/shard_map/ppermute | solution.py:35
  234.5 12.1 %collective-permute-start.51 = (bf16[96,2048]{1,0:T(8,128)(2,1)S(1)}, bf16[96,2048]{1,0:T(8,128)(2,1)S(1)}, u32[]{:S(2)}, u32[]{:S(2)}) collective-permute-start(bf16[96,2048]{1,0:T(8,128)(2,1)S(1)} %pad_maximum_fusion.17), channel_id=1, source_target_pairs={{0,1},{1,0},{2,3},{3,2},{4,5},{5,4},{6,7},{7,6},{8,9},{9,8},{10,11... | collective-permute-start | bytes 1179656 | tf_op jit(solution)/shard_map/ppermute | solution.py:35
  236.3 11.2 %collective-permute-start.52 = (bf16[96,2048]{1,0:T(8,128)(2,1)S(1)}, bf16[96,2048]{1,0:T(8,128)(2,1)S(1)}, u32[]{:S(2)}, u32[]{:S(2)}) collective-permute-start(bf16[96,2048]{1,0:T(8,128)(2,1)S(1)} %pad_maximum_fusion.18), channel_id=1, source_target_pairs={{0,2},{1,3},{2,0},{3,1},{4,6},{5,7},{6,4},{7,5},{8,10},{9,11},{10,... | collective-permute-start | bytes 1179656 | tf_op jit(solution)/shard_map/ppermute | solution.py:35
  236.6 17.4 %collective-permute-start.53 = (bf16[96,2048]{1,0:T(8,128)(2,1)S(1)}, bf16[96,2048]{1,0:T(8,128)(2,1)S(1)}, u32[]{:S(2)}, u32[]{:S(2)}) collective-permute-start(bf16[96,2048]{1,0:T(8,128)(2,1)S(1)} %pad_maximum_fusion.19), channel_id=1, source_target_pairs={{0,3},{1,2},{2,1},{3,0},{4,7},{5,6},{6,5},{7,4},{8,11},{9,10},{10,... | collective-permute-start | bytes 1179656 | tf_op jit(solution)/shard_map/ppermute | solution.py:35
  (20 other events, 186.3 us)
Sparse Core Ops, SparseCore 0:
  24.2 30.9 all-gather.1

commit v13 on v12

--- a/solution.py
+++ b/solution.py
@@ -471,13 +471,17 @@
     produced = []
     slots = exp_count * capacity
     for g, came in enumerate(arrived):
-        mate = jnp.concatenate([part[part.shape[0] // 2 :] for part in came], axis=0)
+        halves = [part[part.shape[0] // 2 :] for part in came]
+        if g == groups - 1 and g:
+            count = len(halves)
+            halves = lax.optimization_barrier((*halves, *produced[-1][1]))[:count]
+        mate = jnp.concatenate(halves, axis=0)
         own, other = call(
             functools.partial(expert_kernel, routes, capacity),
             [bf16((slots, width)), bf16((slots, width))],
             [VMEM] * (len(came) + 4),
             *came,
-            swap(tie(mate, *(produced[-1][1] if g == groups - 1 else ())), "ctx", 1),
+            swap(mate, "ctx", 1),
             w_gate[0],
             w_up[0],
             w_down[0],
@@ -495,7 +499,7 @@
             mates = [mates[mine] for mine in ours]
         produced.append(([own[mine] for mine in ours], mates))
 
-    totals, hop, in_flight = [], (), {}
+    totals, in_flight = [], {}
     for g in [*range(2, groups), *(g for g in (1, 0) if g < groups)]:
         back = []
         for d in peers:
@@ -511,18 +515,19 @@
             name="combine",
         )
         if g:
-            total = swap(tie(total, *(hop if g > 1 else ())), "ctx", 2 * g)
-            hop = (total,)
+            total = swap(total, "ctx", 2 * g)
         totals.append(total)
-    early = call(
-        sum_kernel,
-        jax.ShapeDtypeStruct((rows, width), jnp.float32),
-        [VMEM] * groups,
-        residual,
-        *totals[:-1],
-        name="add",
-        flops=10_000_000_000,
-    )
+    early = residual
+    for total in totals[:-1]:
+        early = call(
+            sum_kernel,
+            jax.ShapeDtypeStruct((rows, width), jnp.float32),
+            [VMEM] * 2,
+            early,
+            total,
+            name="add",
+            flops=3_000_000_000,
+        )
     return call(sum_kernel, bf16((rows, width)), [VMEM] * 2, early, totals[-1], name="add")
 
 

time: 263 us -> 262 us (level)
    unnamed x33 -> x41, local copies, waits for them, and re-layouts: 5.6 us -> 6.71 us
    pallas_call x23 -> x25, Pallas kernels: 39.4 us -> 39.4 us  [call(): pl.pallas_call(kernel, out_shape=out_shape, in_specs=specs, out_specs=jax...]
where the time goes in v13:
time: 262 us
  waiting for transfers between devices  138 us (53%)
  starting transfers between devices  59.6 us (23%)
  Pallas kernels  39.4 us (15%)
  between operations  14.2 us (5%)
  local copies, waits for them, and re-layouts  7.67 us (3%)
  other arithmetic  3.19 us (1%)
    ppermute x54, waiting for transfers between devices, swap(): return lax.ppermute(array, axis, pairs)  134 us
    ppermute x54, starting transfers between devices, swap(): return lax.ppermute(array, axis, pairs)  59.6 us
    pallas_call x25, Pallas kernels, call(): pl.pallas_call(kernel, out_shape=out_shape, in_specs=specs, out_specs=jax...  39.4 us
    unnamed x41, local copies, waits for them, and re-layouts  6.71 us
  transfers between devices with their start and end apart: 55, of which 33 were waited for; matrix products, arithmetic and copies ran while one was open for 1% of the time, Pallas kernels for 12%

profile of v13, /device:TPU:0, one launch (start us, length us, event | category | flops | bytes accessed | tf_op | source)
XLA Modules:
  0.0 261.9 jit_solution(4061585551849326814)
XLA Ops:
  8.1 4.5 %own_rows.1 = (bf16[144,256]{1,0:T(8,128)(2,1)}, bf16[144,256]{1,0:T(8,128)(2,1)}, bf16[144,256]{1,0:T(8,128)(2,1)}, bf16[144,256]{1,0:T(8,128)(2,1)}) custom-call(s32[6]{0:T(128)} %pad_add_fusion.place, s32[8,128]{1,0:T(8,128)} %bitcast.38, s32[8,128]{1,0:T(8,128)} %bitcast.39, bf16[128,2048]{1,0:T(8,128)(2,1)} %tokens.1, f32[1,2048]{1,0:T(1,128)} %bitcast.34, ...), custom_call_target="tpu_custom_call" | custom-call | flops 1000 | bytes 1000 | tf_op jit(solution)/shard_map/own_rows/pallas_call | solution.py:306
  12.6 3.0 %collective-permute-start = (bf16[144,256]{1,0:T(8,128)(2,1)}, bf16[144,256]{1,0:T(8,128)(2,1)S(1)}, u32[]{:S(2)}, u32[]{:S(2)}) collective-permute-start(bf16[144,256]{1,0:T(8,128)(2,1)} %get-tuple-element.65), channel_id=1, source_target_pairs={{0,1},{1,0},{2,3},{3,2},{4,5},{5,4},{6,7},{7,6},{8,9},{9,8},{10,11... | collective-permute-start | bytes 221192 | tf_op jit(solution)/shard_map/ppermute | solution.py:35
  18.4 1.7 collective-permute-done.1
  20.2 2.4 collective-permute-done.2
  25.1 2.5 collective-permute-start.5
  28.6 10.4 %collective-permute-done.3.refs_1_ = bf16[128,2048]{1,0:T(8,128)(2,1)S(1)} collective-permute-done((bf16[128,2048]{1,0:T(8,128)(2,1)S(1)}, bf16[128,2048]{1,0:T(8,128)(2,1)S(1)}, u32[]{:S(2)}, u32[]{:S(2)}) %collective-permute-start.3) | collective-permute-done | bytes 524320 | tf_op jit(solution)/shard_map/ppermute | solution.py:35
  39.0 9.1 %collective-permute-done.4.refs_2_ = bf16[128,2048]{1,0:T(8,128)(2,1)S(1)} collective-permute-done((bf16[128,2048]{1,0:T(8,128)(2,1)S(1)}, bf16[128,2048]{1,0:T(8,128)(2,1)S(1)}, u32[]{:S(2)}, u32[]{:S(2)}) %collective-permute-start.4) | collective-permute-done | bytes 524320 | tf_op jit(solution)/shard_map/ppermute | solution.py:35
  49.7 1.8 queries.1
  51.6 3.6 %all-gather.2.cloned.1.call-done.both = bf16[4608,256]{1,0:T(8,128)(2,1)} async-done(((bf16[576,256]{1,0:T(8,128)(2,1)}), bf16[4608,256]{1,0:T(8,128)(2,1)}) %all-gather.2.cloned.1.call-update) | async-done | bytes 2359312 | tf_op jit(solution)/shard_map/all_gather | solution.py:375
  55.2 1.7 copy-done.3
  56.8 1.7 attention.4
  58.6 2.4 collective-permute-start.6
  61.0 1.7 attention.5
  63.4 1.9 attention.6
  65.9 1.7 attention.7.refs_0_
  67.7 6.8 %collective-permute-done.6.refs_1_ = bf16[128,2048]{1,0:T(8,128)(2,1)S(1)} collective-permute-done((bf16[128,2048]{1,0:T(8,128)(2,1)S(1)}, bf16[128,2048]{1,0:T(8,128)(2,1)S(1)}, u32[]{:S(2)}, u32[]{:S(2)}) %collective-permute-start.6) | collective-permute-done | bytes 524320 | tf_op jit(solution)/shard_map/ppermute | solution.py:35
  74.6 11.0 %collective-permute-done.7.refs_1_ = bf16[128,2048]{1,0:T(8,128)(2,1)S(1)} collective-permute-done((bf16[128,2048]{1,0:T(8,128)(2,1)S(1)}, bf16[128,2048]{1,0:T(8,128)(2,1)S(1)}, u32[]{:S(2)}, u32[]{:S(2)}) %collective-permute-start.7) | collective-permute-done | bytes 524320 | tf_op jit(solution)/shard_map/ppermute | solution.py:35
  86.2 2.3 collective-permute-start.10
  91.3 3.9 %collective-permute-start.9 = (bf16[128,2048]{1,0:T(8,128)(2,1)S(1)}, bf16[128,2048]{1,0:T(8,128)(2,1)S(1)}, u32[]{:S(2)}, u32[]{:S(2)}) collective-permute-start(bf16[128,2048]{1,0:T(8,128)(2,1)S(1)} %get-tuple-element.74), channel_id=1, source_target_pairs={{0,16},{4,20},{8,24},{12,28},{16,0},{20,4},{24,8},{28,12},{1,17},{... | collective-permute-start | bytes 1572872 | tf_op jit(solution)/shard_map/ppermute | solution.py:35
  100.7 9.4 %collective-permute-done.10 = bf16[128,2048]{1,0:T(8,128)(2,1)S(1)} collective-permute-done((bf16[128,2048]{1,0:T(8,128)(2,1)S(1)}, bf16[128,2048]{1,0:T(8,128)(2,1)S(1)}, u32[]{:S(2)}, u32[]{:S(2)}) %collective-permute-start.10) | collective-permute-done | bytes 524320 | tf_op jit(solution)/shard_map/ppermute | solution.py:35
  110.5 2.3 collective-permute-start.12
  112.9 5.5 %collective-permute-done.9 = bf16[128,2048]{1,0:T(8,128)(2,1)S(1)} collective-permute-done((bf16[128,2048]{1,0:T(8,128)(2,1)S(1)}, bf16[128,2048]{1,0:T(8,128)(2,1)S(1)}, u32[]{:S(2)}, u32[]{:S(2)}) %collective-permute-start.9) | collective-permute-done | bytes 524320 | tf_op jit(solution)/shard_map/ppermute | solution.py:35
  118.7 1.7 collective-permute-start.16
  121.6 1.8 collective-permute-start.21
  123.7 2.5 collective-permute-done.16.refs_3_
  126.3 1.7 collective-permute-start.13
  128.0 10.8 %collective-permute-done.13.refs_1_ = bf16[128,1024]{1,0:T(8,128)(2,1)S(1)} collective-permute-done((bf16[128,1024]{1,0:T(8,128)(2,1)S(1)}, bf16[128,1024]{1,0:T(8,128)(2,1)S(1)}, u32[]{:S(2)}, u32[]{:S(2)}) %collective-permute-start.13) | collective-permute-done | bytes 262176 | tf_op jit(solution)/shard_map/ppermute | solution.py:35
  139.9 1.8 collective-permute-start.22
  142.2 1.7 collective-permute-start.34
  144.4 3.9 %expert.7 = (bf16[192,2048]{1,0:T(8,128)(2,1)S(1)}, bf16[192,2048]{1,0:T(8,128)(2,1)S(1)}) custom-call(bf16[192,1024]{1,0:T(8,128)(2,1)S(1)} %get-tuple-element.118.refs_0_, bf16[192,1024]{1,0:T(8,128)(2,1)S(1)} %collective-permute-done.17.refs_1_, bf16[192,1024]{1,0:T(8,128)(2,1)S(1)} %get-tuple-element.119.refs_2_, ...), custom_call_target="tpu_custom_call" | custom-call | flops 1000 | bytes 1000 | tf_op jit(solution)/shard_map/expert/pallas_call | solution.py:306
  148.3 9.5 %collective-permute-done.34.refs_3_ = bf16[128,1024]{1,0:T(8,128)(2,1)S(1)} collective-permute-done((bf16[128,1024]{1,0:T(8,128)(2,1)S(1)}, bf16[128,1024]{1,0:T(8,128)(2,1)S(1)}, u32[]{:S(2)}, u32[]{:S(2)}) %collective-permute-start.34) | collective-permute-done | bytes 262176 | tf_op jit(solution)/shard_map/ppermute | solution.py:35
  160.0 3.9 %expert.6 = (bf16[192,2048]{1,0:T(8,128)(2,1)S(1)}, bf16[192,2048]{1,0:T(8,128)(2,1)S(1)}) custom-call(bf16[192,1024]{1,0:T(8,128)(2,1)S(1)} %get-tuple-element.111.refs_0_, bf16[192,1024]{1,0:T(8,128)(2,1)S(1)} %collective-permute-done.18.refs_1_, bf16[192,1024]{1,0:T(8,128)(2,1)S(1)} %get-tuple-element.112.refs_2_, ...), custom_call_target="tpu_custom_call" | custom-call | flops 1000 | bytes 1000 | tf_op jit(solution)/shard_map/expert/pallas_call | solution.py:306
  164.4 6.0 %collective-permute-done.36.refs_3_ = bf16[192,1024]{1,0:T(8,128)(2,1)S(1)} collective-permute-done((bf16[192,1024]{1,0:T(8,128)(2,1)S(1)}, bf16[192,1024]{1,0:T(8,128)(2,1)S(1)}, u32[]{:S(2)}, u32[]{:S(2)}) %collective-permute-start.36) | collective-permute-done | bytes 393248 | tf_op jit(solution)/shard_map/ppermute | solution.py:35
  171.4 4.1 %expert.4 = (bf16[192,2048]{1,0:T(8,128)(2,1)S(1)}, bf16[192,2048]{1,0:T(8,128)(2,1)S(1)}) custom-call(bf16[192,1024]{1,0:T(8,128)(2,1)S(1)} %get-tuple-element.79.refs_0_, bf16[192,1024]{1,0:T(8,128)(2,1)S(1)} %collective-permute-done.19.refs_1_, bf16[192,1024]{1,0:T(8,128)(2,1)S(1)} %get-tuple-element.85.refs_2_, ...), custom_call_target="tpu_custom_call" | custom-call | flops 1000 | bytes 1000 | tf_op jit(solution)/shard_map/expert/pallas_call | solution.py:306
  179.9 1.7 collective-permute-start.28
  182.7 3.9 %expert.5 = (bf16[192,2048]{1,0:T(8,128)(2,1)S(1)}, bf16[192,2048]{1,0:T(8,128)(2,1)S(1)}) custom-call(bf16[192,1024]{1,0:T(8,128)(2,1)S(1)} %get-tuple-element.96.refs_0_, bf16[192,1024]{1,0:T(8,128)(2,1)S(1)} %copy-done.11, bf16[192,1024]{1,0:T(8,128)(2,1)S(1)} %get-tuple-element.99.refs_2_, bf16[192,1024]{1,0:T(8,128)(2,1)S(1)} %copy-done.9, ...), custom_call_target="tpu_custom_call" | custom-call | flops 1000 | bytes 1000 | tf_op jit(solution)/shard_map/expert/pallas_call | solution.py:306
  186.8 2.1 collective-permute-done.38
  189.1 2.3 collective-permute-done.30.refs_3_
  192.8 6.8 %collective-permute-done.28.refs_2_ = bf16[96,2048]{1,0:T(8,128)(2,1)S(1)} collective-permute-done((bf16[96,2048]{1,0:T(8,128)(2,1)S(1)}, bf16[96,2048]{1,0:T(8,128)(2,1)S(1)}, u32[]{:S(2)}, u32[]{:S(2)}) %collective-permute-start.28) | collective-permute-done | bytes 393248 | tf_op jit(solution)/shard_map/ppermute | solution.py:35
  200.1 1.7 collective-permute-start.39
  202.8 3.8 %collective-permute-start.31 = (bf16[128,2048]{1,0:T(8,128)(2,1)S(1)}, bf16[128,2048]{1,0:T(8,128)(2,1)S(1)}, u32[]{:S(2)}, u32[]{:S(2)}) collective-permute-start(bf16[128,2048]{1,0:T(8,128)(2,1)S(1)} %combine.4), channel_id=1, source_target_pairs={{0,16},{4,20},{8,24},{12,28},{16,0},{20,4},{24,8},{28,12},{1,17},{... | collective-permute-start | bytes 1572872 | tf_op jit(solution)/shard_map/ppermute | solution.py:35
  209.7 6.9 %collective-permute-done.40.refs_2_ = bf16[96,2048]{1,0:T(8,128)(2,1)S(1)} collective-permute-done((bf16[96,2048]{1,0:T(8,128)(2,1)S(1)}, bf16[96,2048]{1,0:T(8,128)(2,1)S(1)}, u32[]{:S(2)}, u32[]{:S(2)}) %collective-permute-start.40) | collective-permute-done | bytes 393248 | tf_op jit(solution)/shard_map/ppermute | solution.py:35
  219.6 3.3 %collective-permute-start.42 = (bf16[128,2048]{1,0:T(8,128)(2,1)S(1)}, bf16[128,2048]{1,0:T(8,128)(2,1)S(1)}, u32[]{:S(2)}, u32[]{:S(2)}) collective-permute-start(bf16[128,2048]{1,0:T(8,128)(2,1)S(1)} %combine.5), channel_id=1, source_target_pairs={{0,24},{4,28},{8,16},{12,20},{16,8},{20,12},{24,0},{28,4},{1,25},{... | collective-permute-start | bytes 1572872 | tf_op jit(solution)/shard_map/ppermute | solution.py:35
  222.9 2.2 collective-permute-done.47.refs_3_
  226.6 6.9 %collective-permute-done.46.refs_2_ = bf16[96,2048]{1,0:T(8,128)(2,1)S(1)} collective-permute-done((bf16[96,2048]{1,0:T(8,128)(2,1)S(1)}, bf16[96,2048]{1,0:T(8,128)(2,1)S(1)}, u32[]{:S(2)}, u32[]{:S(2)}) %collective-permute-start.46) | collective-permute-done | bytes 393248 | tf_op jit(solution)/shard_map/ppermute | solution.py:35
  236.5 4.6 %collective-permute-done.31.refs_1_ = bf16[128,2048]{1,0:T(8,128)(2,1)S(1)} collective-permute-done((bf16[128,2048]{1,0:T(8,128)(2,1)S(1)}, bf16[128,2048]{1,0:T(8,128)(2,1)S(1)}, u32[]{:S(2)}, u32[]{:S(2)}) %collective-permute-start.31) | collective-permute-done | bytes 524320 | tf_op jit(solution)/shard_map/ppermute | solution.py:35
  242.0 7.7 %collective-permute-done.52.refs_2_ = bf16[96,2048]{1,0:T(8,128)(2,1)S(1)} collective-permute-done((bf16[96,2048]{1,0:T(8,128)(2,1)S(1)}, bf16[96,2048]{1,0:T(8,128)(2,1)S(1)}, u32[]{:S(2)}, u32[]{:S(2)}) %collective-permute-start.52) | collective-permute-done | bytes 393248 | tf_op jit(solution)/shard_map/ppermute | solution.py:35
  250.8 3.3 %collective-permute-done.48.refs_1_ = bf16[128,2048]{1,0:T(8,128)(2,1)S(1)} collective-permute-done((bf16[128,2048]{1,0:T(8,128)(2,1)S(1)}, bf16[128,2048]{1,0:T(8,128)(2,1)S(1)}, u32[]{:S(2)}, u32[]{:S(2)}) %collective-permute-start.48) | collective-permute-done | bytes 524320 | tf_op jit(solution)/shard_map/ppermute | solution.py:35
  (191 shorter events, 50.0 us)
Async XLA Ops:
  6.5 48.6 %all-gather.2.cloned.1.call-start = ((), (), s32[]{:S(2)}) async-start(), calls=%async_computation | async-start | bytes 2654208 | tf_op jit(solution)/shard_map/all_gather | solution.py:375
  12.6 5.9 %collective-permute-start = (bf16[144,256]{1,0:T(8,128)(2,1)}, bf16[144,256]{1,0:T(8,128)(2,1)S(1)}, u32[]{:S(2)}, u32[]{:S(2)}) collective-permute-start(bf16[144,256]{1,0:T(8,128)(2,1)} %get-tuple-element.65), channel_id=1, source_target_pairs={{0,1},{1,0},{2,3},{3,2},{4,5},{5,4},{6,7},{7,6},{8,9},{9,8},{10,11... | collective-permute-start | bytes 221192 | tf_op jit(solution)/shard_map/ppermute | solution.py:35
  17.1 5.5 %collective-permute-start.2 = (bf16[144,256]{1,0:T(8,128)(2,1)}, bf16[144,256]{1,0:T(8,128)(2,1)S(1)}, u32[]{:S(2)}, u32[]{:S(2)}) collective-permute-start(bf16[144,256]{1,0:T(8,128)(2,1)} %get-tuple-element.67), channel_id=1, source_target_pairs={{0,3},{1,2},{2,1},{3,0},{4,7},{5,6},{6,5},{7,4},{8,11},{9,10},{10,... | collective-permute-start | bytes 221192 | tf_op jit(solution)/shard_map/ppermute | solution.py:35
  24.0 14.9 %collective-permute-start.3 = (bf16[128,2048]{1,0:T(8,128)(2,1)S(1)}, bf16[128,2048]{1,0:T(8,128)(2,1)S(1)}, u32[]{:S(2)}, u32[]{:S(2)}) collective-permute-start(bf16[128,2048]{1,0:T(8,128)(2,1)S(1)} %copy-done.6), channel_id=1, source_target_pairs={{0,1},{1,0},{2,3},{3,2},{4,5},{5,4},{6,7},{7,6},{8,9},{9,8},{10,11... | collective-permute-start | bytes 1572872 | tf_op jit(solution)/shard_map/ppermute | solution.py:35
  24.6 23.4 %collective-permute-start.4 = (bf16[128,2048]{1,0:T(8,128)(2,1)S(1)}, bf16[128,2048]{1,0:T(8,128)(2,1)S(1)}, u32[]{:S(2)}, u32[]{:S(2)}) collective-permute-start(bf16[128,2048]{1,0:T(8,128)(2,1)S(1)} %copy-done.6), channel_id=1, source_target_pairs={{0,2},{1,3},{2,0},{3,1},{4,6},{5,7},{6,4},{7,5},{8,10},{9,11},{10,... | collective-permute-start | bytes 1572872 | tf_op jit(solution)/shard_map/ppermute | solution.py:35
  25.1 22.9 %collective-permute-start.5 = (bf16[128,2048]{1,0:T(8,128)(2,1)S(1)}, bf16[128,2048]{1,0:T(8,128)(2,1)S(1)}, u32[]{:S(2)}, u32[]{:S(2)}) collective-permute-start(bf16[128,2048]{1,0:T(8,128)(2,1)S(1)} %copy-done.6), channel_id=1, source_target_pairs={{0,3},{1,2},{2,1},{3,0},{4,7},{5,6},{6,5},{7,4},{8,11},{9,10},{10,... | collective-permute-start | bytes 1572872 | tf_op jit(solution)/shard_map/ppermute | solution.py:35
  58.6 15.9 %collective-permute-start.6 = (bf16[128,2048]{1,0:T(8,128)(2,1)S(1)}, bf16[128,2048]{1,0:T(8,128)(2,1)S(1)}, u32[]{:S(2)}, u32[]{:S(2)}) collective-permute-start(bf16[128,2048]{1,0:T(8,128)(2,1)S(1)} %attention.4), channel_id=1, source_target_pairs={{0,3},{1,2},{2,1},{3,0},{4,7},{5,6},{6,5},{7,4},{8,11},{9,10},{10,... | collective-permute-start | bytes 1572872 | tf_op jit(solution)/shard_map/ppermute | solution.py:35
  62.8 22.9 %collective-permute-start.7 = (bf16[128,2048]{1,0:T(8,128)(2,1)S(1)}, bf16[128,2048]{1,0:T(8,128)(2,1)S(1)}, u32[]{:S(2)}, u32[]{:S(2)}) collective-permute-start(bf16[128,2048]{1,0:T(8,128)(2,1)S(1)} %attention.5), channel_id=1, source_target_pairs={{0,1},{1,0},{2,3},{3,2},{4,5},{5,4},{6,7},{7,6},{8,9},{9,8},{10,11... | collective-permute-start | bytes 1572872 | tf_op jit(solution)/shard_map/ppermute | solution.py:35
  65.3 20.5 %collective-permute-start.8 = (bf16[128,2048]{1,0:T(8,128)(2,1)S(1)}, bf16[128,2048]{1,0:T(8,128)(2,1)S(1)}, u32[]{:S(2)}, u32[]{:S(2)}) collective-permute-start(bf16[128,2048]{1,0:T(8,128)(2,1)S(1)} %attention.6), channel_id=1, source_target_pairs={{0,2},{1,3},{2,0},{3,1},{4,6},{5,7},{6,4},{7,5},{8,10},{9,11},{10,... | collective-permute-start | bytes 1572872 | tf_op jit(solution)/shard_map/ppermute | solution.py:35
  86.2 23.9 %collective-permute-start.10 = (bf16[128,2048]{1,0:T(8,128)(2,1)S(1)}, bf16[128,2048]{1,0:T(8,128)(2,1)S(1)}, u32[]{:S(2)}, u32[]{:S(2)}) collective-permute-start(bf16[128,2048]{1,0:T(8,128)(2,1)S(1)} %get-tuple-element.74), channel_id=1, source_target_pairs={{0,8},{4,12},{8,0},{12,4},{16,24},{20,28},{24,16},{28,20},{1,9},{5... | collective-permute-start | bytes 1572872 | tf_op jit(solution)/shard_map/ppermute | solution.py:35
  88.5 8.1 %collective-permute-start.11 = (bf16[128,1024]{1,0:T(8,128)(2,1)S(1)}, bf16[128,1024]{1,0:T(8,128)(2,1)S(1)}, u32[]{:S(2)}, u32[]{:S(2)}) collective-permute-start(bf16[128,1024]{1,0:T(8,128)(2,1)S(1)} %get-tuple-element.160.refs_0_), channel_id=1, source_target_pairs={{0,1},{1,0},{2,3},{3,2},{4,5},{5,4},{6,7},{7,6},{8,9},{9,8},{10,11... | collective-permute-start | bytes 786440 | tf_op jit(solution)/shard_map/ppermute | solution.py:35
  90.1 7.8 %collective-permute-start.14 = (bf16[128,1024]{1,0:T(8,128)(2,1)S(1)}, bf16[128,1024]{1,0:T(8,128)(2,1)S(1)}, u32[]{:S(2)}, u32[]{:S(2)}) collective-permute-start(bf16[128,1024]{1,0:T(8,128)(2,1)S(1)} %get-tuple-element.159.refs_2_), channel_id=1, source_target_pairs={{0,2},{1,3},{2,0},{3,1},{4,6},{5,7},{6,4},{7,5},{8,10},{9,11},{10,... | collective-permute-start | bytes 786440 | tf_op jit(solution)/shard_map/ppermute | solution.py:35
  91.3 27.1 %collective-permute-start.9 = (bf16[128,2048]{1,0:T(8,128)(2,1)S(1)}, bf16[128,2048]{1,0:T(8,128)(2,1)S(1)}, u32[]{:S(2)}, u32[]{:S(2)}) collective-permute-start(bf16[128,2048]{1,0:T(8,128)(2,1)S(1)} %get-tuple-element.74), channel_id=1, source_target_pairs={{0,16},{4,20},{8,24},{12,28},{16,0},{20,4},{24,8},{28,12},{1,17},{... | collective-permute-start | bytes 1572872 | tf_op jit(solution)/shard_map/ppermute | solution.py:35
  98.9 19.5 %collective-permute-start.17 = (bf16[192,1024]{1,0:T(8,128)(2,1)S(1)}, bf16[192,1024]{1,0:T(8,128)(2,1)S(1)}, u32[]{:S(2)}, u32[]{:S(2)}) collective-permute-start(bf16[192,1024]{1,0:T(8,128)(2,1)S(1)} %get-tuple-element.82), channel_id=1, source_target_pairs={{0,2},{1,3},{2,0},{3,1},{4,6},{5,7},{6,4},{7,5},{8,10},{9,11},{10,... | collective-permute-start | bytes 1179656 | tf_op jit(solution)/shard_map/ppermute | solution.py:35
  100.2 18.3 %collective-permute-start.20 = (bf16[192,1024]{1,0:T(8,128)(2,1)S(1)}, bf16[192,1024]{1,0:T(8,128)(2,1)S(1)}, u32[]{:S(2)}, u32[]{:S(2)}) collective-permute-start(bf16[192,1024]{1,0:T(8,128)(2,1)S(1)} %get-tuple-element.88), channel_id=1, source_target_pairs={{0,1},{1,0},{2,3},{3,2},{4,5},{5,4},{6,7},{7,6},{8,9},{9,8},{10,11... | collective-permute-start | bytes 1179656 | tf_op jit(solution)/shard_map/ppermute | solution.py:35
  110.1 8.4 %collective-permute-start.15 = (bf16[128,1024]{1,0:T(8,128)(2,1)S(1)}, bf16[128,1024]{1,0:T(8,128)(2,1)S(1)}, u32[]{:S(2)}, u32[]{:S(2)}) collective-permute-start(bf16[128,1024]{1,0:T(8,128)(2,1)S(1)} %get-tuple-element.77.refs_2_), channel_id=1, source_target_pairs={{0,2},{1,3},{2,0},{3,1},{4,6},{5,7},{6,4},{7,5},{8,10},{9,11},{10,... | collective-permute-start | bytes 786440 | tf_op jit(solution)/shard_map/ppermute | solution.py:35
  110.5 8.1 %collective-permute-start.12 = (bf16[128,1024]{1,0:T(8,128)(2,1)S(1)}, bf16[128,1024]{1,0:T(8,128)(2,1)S(1)}, u32[]{:S(2)}, u32[]{:S(2)}) collective-permute-start(bf16[128,1024]{1,0:T(8,128)(2,1)S(1)} %get-tuple-element.75.refs_0_), channel_id=1, source_target_pairs={{0,1},{1,0},{2,3},{3,2},{4,5},{5,4},{6,7},{7,6},{8,9},{9,8},{10,11... | collective-permute-start | bytes 786440 | tf_op jit(solution)/shard_map/ppermute | solution.py:35
  118.7 23.4 %collective-permute-start.32 = (bf16[128,2048]{1,0:T(8,128)(2,1)S(1)}, bf16[128,2048]{1,0:T(8,128)(2,1)S(1)}, u32[]{:S(2)}, u32[]{:S(2)}) collective-permute-start(bf16[128,2048]{1,0:T(8,128)(2,1)S(1)} %collective-permute-done.9), channel_id=1, source_target_pairs={{0,8},{4,12},{8,0},{12,4},{16,24},{20,28},{24,16},{28,20},{1,9},{5... | collective-permute-start | bytes 1572872 | tf_op jit(solution)/shard_map/ppermute | solution.py:35
  118.7 7.6 %collective-permute-start.16 = (bf16[128,1024]{1,0:T(8,128)(2,1)S(1)}, bf16[128,1024]{1,0:T(8,128)(2,1)S(1)}, u32[]{:S(2)}, u32[]{:S(2)}) collective-permute-start(bf16[128,1024]{1,0:T(8,128)(2,1)S(1)} %get-tuple-element.78.refs_2_), channel_id=1, source_target_pairs={{0,2},{1,3},{2,0},{3,1},{4,6},{5,7},{6,4},{7,5},{8,10},{9,11},{10,... | collective-permute-start | bytes 786440 | tf_op jit(solution)/shard_map/ppermute | solution.py:35
  120.4 23.8 %collective-permute-start.49 = (bf16[384,1024]{1,0:T(8,128)(2,1)S(1)}, bf16[384,1024]{1,0:T(8,128)(2,1)S(1)}, u32[]{:S(2)}, u32[]{:S(2)}) collective-permute-start(bf16[384,1024]{1,0:T(8,128)(2,1)S(1)} %pad_maximum_fusion.3), channel_id=1, source_target_pairs={{0,4},{4,0},{8,12},{12,8},{16,20},{20,16},{24,28},{28,24},{1,5},{5... | collective-permute-start | bytes 2359304 | tf_op jit(solution)/shard_map/ppermute | solution.py:35
  121.6 18.3 %collective-permute-start.21 = (bf16[192,1024]{1,0:T(8,128)(2,1)S(1)}, bf16[192,1024]{1,0:T(8,128)(2,1)S(1)}, u32[]{:S(2)}, u32[]{:S(2)}) collective-permute-start(bf16[192,1024]{1,0:T(8,128)(2,1)S(1)} %get-tuple-element.89), channel_id=1, source_target_pairs={{0,1},{1,0},{2,3},{3,2},{4,5},{5,4},{6,7},{7,6},{8,9},{9,8},{10,11... | collective-permute-start | bytes 1179656 | tf_op jit(solution)/shard_map/ppermute | solution.py:35
  123.4 18.3 %collective-permute-start.18 = (bf16[192,1024]{1,0:T(8,128)(2,1)S(1)}, bf16[192,1024]{1,0:T(8,128)(2,1)S(1)}, u32[]{:S(2)}, u32[]{:S(2)}) collective-permute-start(bf16[192,1024]{1,0:T(8,128)(2,1)S(1)} %get-tuple-element.83), channel_id=1, source_target_pairs={{0,2},{1,3},{2,0},{3,1},{4,6},{5,7},{6,4},{7,5},{8,10},{9,11},{10,... | collective-permute-start | bytes 1179656 | tf_op jit(solution)/shard_map/ppermute | solution.py:35
  126.3 12.5 %collective-permute-start.13 = (bf16[128,1024]{1,0:T(8,128)(2,1)S(1)}, bf16[128,1024]{1,0:T(8,128)(2,1)S(1)}, u32[]{:S(2)}, u32[]{:S(2)}) collective-permute-start(bf16[128,1024]{1,0:T(8,128)(2,1)S(1)} %get-tuple-element.76.refs_0_), channel_id=1, source_target_pairs={{0,1},{1,0},{2,3},{3,2},{4,5},{5,4},{6,7},{7,6},{8,9},{9,8},{10,11... | collective-permute-start | bytes 786440 | tf_op jit(solution)/shard_map/ppermute | solution.py:35
  139.9 19.0 %collective-permute-start.22 = (bf16[192,1024]{1,0:T(8,128)(2,1)S(1)}, bf16[192,1024]{1,0:T(8,128)(2,1)S(1)}, u32[]{:S(2)}, u32[]{:S(2)}) collective-permute-start(bf16[192,1024]{1,0:T(8,128)(2,1)S(1)} %get-tuple-element.90), channel_id=1, source_target_pairs={{0,1},{1,0},{2,3},{3,2},{4,5},{5,4},{6,7},{7,6},{8,9},{9,8},{10,11... | collective-permute-start | bytes 1179656 | tf_op jit(solution)/shard_map/ppermute | solution.py:35
  141.7 17.6 %collective-permute-start.19 = (bf16[192,1024]{1,0:T(8,128)(2,1)S(1)}, bf16[192,1024]{1,0:T(8,128)(2,1)S(1)}, u32[]{:S(2)}, u32[]{:S(2)}) collective-permute-start(bf16[192,1024]{1,0:T(8,128)(2,1)S(1)} %get-tuple-element.84), channel_id=1, source_target_pairs={{0,2},{1,3},{2,0},{3,1},{4,6},{5,7},{6,4},{7,5},{8,10},{9,11},{10,... | collective-permute-start | bytes 1179656 | tf_op jit(solution)/shard_map/ppermute | solution.py:35
  142.2 15.6 %collective-permute-start.34 = (bf16[128,1024]{1,0:T(8,128)(2,1)S(1)}, bf16[128,1024]{1,0:T(8,128)(2,1)S(1)}, u32[]{:S(2)}, u32[]{:S(2)}) collective-permute-start(bf16[128,1024]{1,0:T(8,128)(2,1)S(1)} %get-tuple-element.95.refs_2_), channel_id=1, source_target_pairs={{0,2},{1,3},{2,0},{3,1},{4,6},{5,7},{6,4},{7,5},{8,10},{9,11},{10,... | collective-permute-start | bytes 786440 | tf_op jit(solution)/shard_map/ppermute | solution.py:35
  143.9 13.9 %collective-permute-start.33 = (bf16[128,1024]{1,0:T(8,128)(2,1)S(1)}, bf16[128,1024]{1,0:T(8,128)(2,1)S(1)}, u32[]{:S(2)}, u32[]{:S(2)}) collective-permute-start(bf16[128,1024]{1,0:T(8,128)(2,1)S(1)} %get-tuple-element.94.refs_0_), channel_id=1, source_target_pairs={{0,1},{1,0},{2,3},{3,2},{4,5},{5,4},{6,7},{7,6},{8,9},{9,8},{10,11... | collective-permute-start | bytes 786440 | tf_op jit(solution)/shard_map/ppermute | solution.py:35
  144.2 15.8 %collective-permute-start.43 = (bf16[384,1024]{1,0:T(8,128)(2,1)S(1)}, bf16[384,1024]{1,0:T(8,128)(2,1)S(1)}, u32[]{:S(2)}, u32[]{:S(2)}) collective-permute-start(bf16[384,1024]{1,0:T(8,128)(2,1)S(1)} %pad_maximum_fusion.2), channel_id=1, source_target_pairs={{0,4},{4,0},{8,12},{12,8},{16,20},{20,16},{24,28},{28,24},{1,5},{5... | collective-permute-start | bytes 2359304 | tf_op jit(solution)/shard_map/ppermute | solution.py:35
  157.8 12.9 %collective-permute-start.50 = (bf16[192,2048]{1,0:T(8,128)(2,1)S(1)}, bf16[192,2048]{1,0:T(8,128)(2,1)S(1)}, u32[]{:S(2)}, u32[]{:S(2)}) collective-permute-start(bf16[192,2048]{1,0:T(8,128)(2,1)S(1)} %get-tuple-element.121), channel_id=1, source_target_pairs={{0,4},{4,0},{8,12},{12,8},{16,20},{20,16},{24,28},{28,24},{1,5},{5... | collective-permute-start | bytes 2359304 | tf_op jit(solution)/shard_map/ppermute | solution.py:35
  158.9 11.6 %collective-permute-start.36 = (bf16[192,1024]{1,0:T(8,128)(2,1)S(1)}, bf16[192,1024]{1,0:T(8,128)(2,1)S(1)}, u32[]{:S(2)}, u32[]{:S(2)}) collective-permute-start(bf16[192,1024]{1,0:T(8,128)(2,1)S(1)} %get-tuple-element.101), channel_id=1, source_target_pairs={{0,1},{1,0},{2,3},{3,2},{4,5},{5,4},{6,7},{7,6},{8,9},{9,8},{10,11... | collective-permute-start | bytes 1179656 | tf_op jit(solution)/shard_map/ppermute | solution.py:35
  159.3 11.3 %collective-permute-start.35 = (bf16[192,1024]{1,0:T(8,128)(2,1)S(1)}, bf16[192,1024]{1,0:T(8,128)(2,1)S(1)}, u32[]{:S(2)}, u32[]{:S(2)}) collective-permute-start(bf16[192,1024]{1,0:T(8,128)(2,1)S(1)} %get-tuple-element.98), channel_id=1, source_target_pairs={{0,2},{1,3},{2,0},{3,1},{4,6},{5,7},{6,4},{7,5},{8,10},{9,11},{10,... | collective-permute-start | bytes 1179656 | tf_op jit(solution)/shard_map/ppermute | solution.py:35
  159.9 11.5 %collective-permute-start.23 = (bf16[384,1024]{1,0:T(8,128)(2,1)S(1)}, bf16[384,1024]{1,0:T(8,128)(2,1)S(1)}, u32[]{:S(2)}, u32[]{:S(2)}) collective-permute-start(bf16[384,1024]{1,0:T(8,128)(2,1)S(1)} %pad_maximum_fusion), channel_id=1, source_target_pairs={{0,4},{4,0},{8,12},{12,8},{16,20},{20,16},{24,28},{28,24},{1,5},{5... | collective-permute-start | bytes 2359304 | tf_op jit(solution)/shard_map/ppermute | solution.py:35
  163.9 18.3 %collective-permute-start.44 = (bf16[192,2048]{1,0:T(8,128)(2,1)S(1)}, bf16[192,2048]{1,0:T(8,128)(2,1)S(1)}, u32[]{:S(2)}, u32[]{:S(2)}) collective-permute-start(bf16[192,2048]{1,0:T(8,128)(2,1)S(1)} %get-tuple-element.114), channel_id=1, source_target_pairs={{0,4},{4,0},{8,12},{12,8},{16,20},{20,16},{24,28},{28,24},{1,5},{5... | collective-permute-start | bytes 2359304 | tf_op jit(solution)/shard_map/ppermute | solution.py:35
  178.4 13.0 %collective-permute-start.30 = (bf16[96,2048]{1,0:T(8,128)(2,1)S(1)}, bf16[96,2048]{1,0:T(8,128)(2,1)S(1)}, u32[]{:S(2)}, u32[]{:S(2)}) collective-permute-start(bf16[96,2048]{1,0:T(8,128)(2,1)S(1)} %pad_maximum_fusion.7), channel_id=1, source_target_pairs={{0,3},{1,2},{2,1},{3,0},{4,7},{5,6},{6,5},{7,4},{8,11},{9,10},{10,... | collective-permute-start | bytes 1179656 | tf_op jit(solution)/shard_map/ppermute | solution.py:35
  179.9 19.7 %collective-permute-start.28 = (bf16[96,2048]{1,0:T(8,128)(2,1)S(1)}, bf16[96,2048]{1,0:T(8,128)(2,1)S(1)}, u32[]{:S(2)}, u32[]{:S(2)}) collective-permute-start(bf16[96,2048]{1,0:T(8,128)(2,1)S(1)} %pad_maximum_fusion.6), channel_id=1, source_target_pairs={{0,2},{1,3},{2,0},{3,1},{4,6},{5,7},{6,4},{7,5},{8,10},{9,11},{10,... | collective-permute-start | bytes 1179656 | tf_op jit(solution)/shard_map/ppermute | solution.py:35
  181.7 18.4 %collective-permute-start.26 = (bf16[96,2048]{1,0:T(8,128)(2,1)S(1)}, bf16[96,2048]{1,0:T(8,128)(2,1)S(1)}, u32[]{:S(2)}, u32[]{:S(2)}) collective-permute-start(bf16[96,2048]{1,0:T(8,128)(2,1)S(1)} %pad_maximum_fusion.5), channel_id=1, source_target_pairs={{0,1},{1,0},{2,3},{3,2},{4,5},{5,4},{6,7},{7,6},{8,9},{9,8},{10,11... | collective-permute-start | bytes 1179656 | tf_op jit(solution)/shard_map/ppermute | solution.py:35
  191.3 16.9 %collective-permute-start.41 = (bf16[96,2048]{1,0:T(8,128)(2,1)S(1)}, bf16[96,2048]{1,0:T(8,128)(2,1)S(1)}, u32[]{:S(2)}, u32[]{:S(2)}) collective-permute-start(bf16[96,2048]{1,0:T(8,128)(2,1)S(1)} %pad_maximum_fusion.11), channel_id=1, source_target_pairs={{0,3},{1,2},{2,1},{3,0},{4,7},{5,6},{6,5},{7,4},{8,11},{9,10},{10,... | collective-permute-start | bytes 1179656 | tf_op jit(solution)/shard_map/ppermute | solution.py:35
  199.7 16.9 %collective-permute-start.40 = (bf16[96,2048]{1,0:T(8,128)(2,1)S(1)}, bf16[96,2048]{1,0:T(8,128)(2,1)S(1)}, u32[]{:S(2)}, u32[]{:S(2)}) collective-permute-start(bf16[96,2048]{1,0:T(8,128)(2,1)S(1)} %pad_maximum_fusion.10), channel_id=1, source_target_pairs={{0,2},{1,3},{2,0},{3,1},{4,6},{5,7},{6,4},{7,5},{8,10},{9,11},{10,... | collective-permute-start | bytes 1179656 | tf_op jit(solution)/shard_map/ppermute | solution.py:35
  200.1 16.9 %collective-permute-start.39 = (bf16[96,2048]{1,0:T(8,128)(2,1)S(1)}, bf16[96,2048]{1,0:T(8,128)(2,1)S(1)}, u32[]{:S(2)}, u32[]{:S(2)}) collective-permute-start(bf16[96,2048]{1,0:T(8,128)(2,1)S(1)} %pad_maximum_fusion.9), channel_id=1, source_target_pairs={{0,1},{1,0},{2,3},{3,2},{4,5},{5,4},{6,7},{7,6},{8,9},{9,8},{10,11... | collective-permute-start | bytes 1179656 | tf_op jit(solution)/shard_map/ppermute | solution.py:35
  202.8 38.2 %collective-permute-start.31 = (bf16[128,2048]{1,0:T(8,128)(2,1)S(1)}, bf16[128,2048]{1,0:T(8,128)(2,1)S(1)}, u32[]{:S(2)}, u32[]{:S(2)}) collective-permute-start(bf16[128,2048]{1,0:T(8,128)(2,1)S(1)} %combine.4), channel_id=1, source_target_pairs={{0,16},{4,20},{8,24},{12,28},{16,0},{20,4},{24,8},{28,12},{1,17},{... | collective-permute-start | bytes 1572872 | tf_op jit(solution)/shard_map/ppermute | solution.py:35
  208.2 16.9 %collective-permute-start.47 = (bf16[96,2048]{1,0:T(8,128)(2,1)S(1)}, bf16[96,2048]{1,0:T(8,128)(2,1)S(1)}, u32[]{:S(2)}, u32[]{:S(2)}) collective-permute-start(bf16[96,2048]{1,0:T(8,128)(2,1)S(1)} %pad_maximum_fusion.15), channel_id=1, source_target_pairs={{0,3},{1,2},{2,1},{3,0},{4,7},{5,6},{6,5},{7,4},{8,11},{9,10},{10,... | collective-permute-start | bytes 1179656 | tf_op jit(solution)/shard_map/ppermute | solution.py:35
  216.6 16.9 %collective-permute-start.46 = (bf16[96,2048]{1,0:T(8,128)(2,1)S(1)}, bf16[96,2048]{1,0:T(8,128)(2,1)S(1)}, u32[]{:S(2)}, u32[]{:S(2)}) collective-permute-start(bf16[96,2048]{1,0:T(8,128)(2,1)S(1)} %pad_maximum_fusion.14), channel_id=1, source_target_pairs={{0,2},{1,3},{2,0},{3,1},{4,6},{5,7},{6,4},{7,5},{8,10},{9,11},{10,... | collective-permute-start | bytes 1179656 | tf_op jit(solution)/shard_map/ppermute | solution.py:35
  216.9 16.9 %collective-permute-start.45 = (bf16[96,2048]{1,0:T(8,128)(2,1)S(1)}, bf16[96,2048]{1,0:T(8,128)(2,1)S(1)}, u32[]{:S(2)}, u32[]{:S(2)}) collective-permute-start(bf16[96,2048]{1,0:T(8,128)(2,1)S(1)} %pad_maximum_fusion.13), channel_id=1, source_target_pairs={{0,1},{1,0},{2,3},{3,2},{4,5},{5,4},{6,7},{7,6},{8,9},{9,8},{10,11... | collective-permute-start | bytes 1179656 | tf_op jit(solution)/shard_map/ppermute | solution.py:35
  219.6 22.0 %collective-permute-start.42 = (bf16[128,2048]{1,0:T(8,128)(2,1)S(1)}, bf16[128,2048]{1,0:T(8,128)(2,1)S(1)}, u32[]{:S(2)}, u32[]{:S(2)}) collective-permute-start(bf16[128,2048]{1,0:T(8,128)(2,1)S(1)} %combine.5), channel_id=1, source_target_pairs={{0,24},{4,28},{8,16},{12,20},{16,8},{20,12},{24,0},{28,4},{1,25},{... | collective-permute-start | bytes 1572872 | tf_op jit(solution)/shard_map/ppermute | solution.py:35
  225.1 16.9 %collective-permute-start.53 = (bf16[96,2048]{1,0:T(8,128)(2,1)S(1)}, bf16[96,2048]{1,0:T(8,128)(2,1)S(1)}, u32[]{:S(2)}, u32[]{:S(2)}) collective-permute-start(bf16[96,2048]{1,0:T(8,128)(2,1)S(1)} %pad_maximum_fusion.19), channel_id=1, source_target_pairs={{0,3},{1,2},{2,1},{3,0},{4,7},{5,6},{6,5},{7,4},{8,11},{9,10},{10,... | collective-permute-start | bytes 1179656 | tf_op jit(solution)/shard_map/ppermute | solution.py:35
  233.5 16.3 %collective-permute-start.52 = (bf16[96,2048]{1,0:T(8,128)(2,1)S(1)}, bf16[96,2048]{1,0:T(8,128)(2,1)S(1)}, u32[]{:S(2)}, u32[]{:S(2)}) collective-permute-start(bf16[96,2048]{1,0:T(8,128)(2,1)S(1)} %pad_maximum_fusion.18), channel_id=1, source_target_pairs={{0,2},{1,3},{2,0},{3,1},{4,6},{5,7},{6,4},{7,5},{8,10},{9,11},{10,... | collective-permute-start | bytes 1179656 | tf_op jit(solution)/shard_map/ppermute | solution.py:35
  233.8 15.9 %collective-permute-start.51 = (bf16[96,2048]{1,0:T(8,128)(2,1)S(1)}, bf16[96,2048]{1,0:T(8,128)(2,1)S(1)}, u32[]{:S(2)}, u32[]{:S(2)}) collective-permute-start(bf16[96,2048]{1,0:T(8,128)(2,1)S(1)} %pad_maximum_fusion.17), channel_id=1, source_target_pairs={{0,1},{1,0},{2,3},{3,2},{4,5},{5,4},{6,7},{7,6},{8,9},{9,8},{10,11... | collective-permute-start | bytes 1179656 | tf_op jit(solution)/shard_map/ppermute | solution.py:35
  241.1 13.0 %collective-permute-start.48 = (bf16[128,2048]{1,0:T(8,128)(2,1)S(1)}, bf16[128,2048]{1,0:T(8,128)(2,1)S(1)}, u32[]{:S(2)}, u32[]{:S(2)}) collective-permute-start(bf16[128,2048]{1,0:T(8,128)(2,1)S(1)} %combine.6), channel_id=1, source_target_pairs={{0,8},{4,12},{8,0},{12,4},{16,24},{20,28},{24,16},{28,20},{1,9},{5... | collective-permute-start | bytes 1572872 | tf_op jit(solution)/shard_map/ppermute | solution.py:35
  (26 other events, 195.2 us)
Sparse Core Ops, SparseCore 0:
  24.1 30.9 all-gather.1

commit v14 on v13

--- a/solution.py
+++ b/solution.py
@@ -294,6 +294,15 @@
             other[:, cols] = product[half:]
 
 
+def halves_kernel(*refs):
+    *parts, out = refs
+    first = 0
+    for part in parts:
+        count = part.shape[0] // 2
+        out[first : first + count, :] = part[count:, :]
+        first += count
+
+
 def sum_kernel(*refs):
     *parts, out = refs
     total = parts[0][...].astype(jnp.float32)
@@ -471,11 +480,16 @@
     produced = []
     slots = exp_count * capacity
     for g, came in enumerate(arrived):
-        halves = [part[part.shape[0] // 2 :] for part in came]
+        parts = came
         if g == groups - 1 and g:
-            count = len(halves)
-            halves = lax.optimization_barrier((*halves, *produced[-1][1]))[:count]
-        mate = jnp.concatenate(halves, axis=0)
+            parts = lax.optimization_barrier((*came, *produced[-1][1]))[: len(came)]
+        mate = call(
+            halves_kernel,
+            bf16((2 * slots, half)),
+            [VMEM] * len(parts),
+            *parts,
+            name="halves",
+        )
         own, other = call(
             functools.partial(expert_kernel, routes, capacity),
             [bf16((slots, width)), bf16((slots, width))],

time: 262 us -> 251 us (0.958)
  waiting for transfers between devices: 138 us -> 124 us
  starting transfers between devices: 59.6 us -> 63.4 us
    ppermute x54, waiting for transfers between devices: 134 us -> 120 us  [swap(): return lax.ppermute(array, axis, pairs)]
    ppermute x54, starting transfers between devices: 59.6 us -> 63.4 us  [swap(): return lax.ppermute(array, axis, pairs)]
    unnamed x41 -> x33, local copies, waits for them, and re-layouts: 6.71 us -> 5.6 us
    pallas_call x25 -> x29, Pallas kernels: 39.4 us -> 39.5 us  [call(): pl.pallas_call(kernel, out_shape=out_shape, in_specs=specs, out_specs=jax...]
  transfers between devices with their start and end apart: 55 -> 55, of which waited for: 33 -> 32; matrix products, arithmetic and copies ran while one was open for 1% -> 1% of each run, Pallas kernels for 12% -> 13%
where the time goes in v14:
time: 251 us; the launch traced here: 250 us
  waiting for transfers between devices  124 us (49%)
  starting transfers between devices  63.4 us (25%)
  Pallas kernels  39.5 us (16%)
  between operations  14 us (6%)
  local copies, waits for them, and re-layouts  6.35 us (3%)
  other arithmetic  3.03 us (1%)
    ppermute x54, waiting for transfers between devices, swap(): return lax.ppermute(array, axis, pairs)  120 us
    ppermute x54, starting transfers between devices, swap(): return lax.ppermute(array, axis, pairs)  63.4 us
    pallas_call x29, Pallas kernels, call(): pl.pallas_call(kernel, out_shape=out_shape, in_specs=specs, out_specs=jax...  39.5 us
    unnamed x33, local copies, waits for them, and re-layouts  5.6 us
  transfers between devices with their start and end apart: 55, of which 32 were waited for; matrix products, arithmetic and copies ran while one was open for 1% of the time, Pallas kernels for 13%

profile of v14, /device:TPU:0, one launch (start us, length us, event | category | flops | bytes accessed | tf_op | source)
XLA Modules:
  0.0 250.4 jit_solution(12628558285000060992)
XLA Ops:
  8.1 4.3 %own_rows.1 = (bf16[144,256]{1,0:T(8,128)(2,1)}, bf16[144,256]{1,0:T(8,128)(2,1)}, bf16[144,256]{1,0:T(8,128)(2,1)}, bf16[144,256]{1,0:T(8,128)(2,1)}) custom-call(s32[6]{0:T(128)} %pad_add_fusion.place, s32[8,128]{1,0:T(8,128)} %bitcast.38, s32[8,128]{1,0:T(8,128)} %bitcast.39, bf16[128,2048]{1,0:T(8,128)(2,1)} %tokens.1, f32[1,2048]{1,0:T(1,128)} %bitcast.34, ...), custom_call_target="tpu_custom_call" | custom-call | flops 1000 | bytes 1000 | tf_op jit(solution)/shard_map/own_rows/pallas_call | solution.py:315
  12.5 3.0 %collective-permute-start = (bf16[144,256]{1,0:T(8,128)(2,1)}, bf16[144,256]{1,0:T(8,128)(2,1)S(1)}, u32[]{:S(2)}, u32[]{:S(2)}) collective-permute-start(bf16[144,256]{1,0:T(8,128)(2,1)} %get-tuple-element.65), channel_id=1, source_target_pairs={{0,1},{1,0},{2,3},{3,2},{4,5},{5,4},{6,7},{7,6},{8,9},{9,8},{10,11... | collective-permute-start | bytes 221192 | tf_op jit(solution)/shard_map/ppermute | solution.py:35
  18.3 1.7 collective-permute-done.1
  20.1 2.4 collective-permute-done.2
  25.0 2.5 collective-permute-start.5
  28.5 10.4 %collective-permute-done.3.refs_1_ = bf16[128,2048]{1,0:T(8,128)(2,1)S(1)} collective-permute-done((bf16[128,2048]{1,0:T(8,128)(2,1)S(1)}, bf16[128,2048]{1,0:T(8,128)(2,1)S(1)}, u32[]{:S(2)}, u32[]{:S(2)}) %collective-permute-start.3) | collective-permute-done | bytes 524320 | tf_op jit(solution)/shard_map/ppermute | solution.py:35
  38.9 9.1 %collective-permute-done.4.refs_2_ = bf16[128,2048]{1,0:T(8,128)(2,1)S(1)} collective-permute-done((bf16[128,2048]{1,0:T(8,128)(2,1)S(1)}, bf16[128,2048]{1,0:T(8,128)(2,1)S(1)}, u32[]{:S(2)}, u32[]{:S(2)}) %collective-permute-start.4) | collective-permute-done | bytes 524320 | tf_op jit(solution)/shard_map/ppermute | solution.py:35
  48.0 1.6 copy-done.7
  49.6 1.8 queries.1
  51.5 3.6 %all-gather.2.cloned.1.call-done.both = bf16[4608,256]{1,0:T(8,128)(2,1)} async-done(((bf16[576,256]{1,0:T(8,128)(2,1)}), bf16[4608,256]{1,0:T(8,128)(2,1)}) %all-gather.2.cloned.1.call-update) | async-done | bytes 2359312 | tf_op jit(solution)/shard_map/all_gather | solution.py:384
  55.1 1.7 copy-done.3
  56.7 1.7 attention.4
  58.5 2.4 collective-permute-start.6
  60.9 1.7 attention.5
  63.3 1.9 attention.6
  65.9 1.7 attention.7.refs_0_
  67.6 6.7 %collective-permute-done.6.refs_1_ = bf16[128,2048]{1,0:T(8,128)(2,1)S(1)} collective-permute-done((bf16[128,2048]{1,0:T(8,128)(2,1)S(1)}, bf16[128,2048]{1,0:T(8,128)(2,1)S(1)}, u32[]{:S(2)}, u32[]{:S(2)}) %collective-permute-start.6) | collective-permute-done | bytes 524320 | tf_op jit(solution)/shard_map/ppermute | solution.py:35
  74.5 11.0 %collective-permute-done.7.refs_1_ = bf16[128,2048]{1,0:T(8,128)(2,1)S(1)} collective-permute-done((bf16[128,2048]{1,0:T(8,128)(2,1)S(1)}, bf16[128,2048]{1,0:T(8,128)(2,1)S(1)}, u32[]{:S(2)}, u32[]{:S(2)}) %collective-permute-start.7) | collective-permute-done | bytes 524320 | tf_op jit(solution)/shard_map/ppermute | solution.py:35
  86.1 2.3 collective-permute-start.10
  91.2 3.9 %collective-permute-start.9 = (bf16[128,2048]{1,0:T(8,128)(2,1)S(1)}, bf16[128,2048]{1,0:T(8,128)(2,1)S(1)}, u32[]{:S(2)}, u32[]{:S(2)}) collective-permute-start(bf16[128,2048]{1,0:T(8,128)(2,1)S(1)} %get-tuple-element.74), channel_id=1, source_target_pairs={{0,16},{4,20},{8,24},{12,28},{16,0},{20,4},{24,8},{28,12},{1,17},{... | collective-permute-start | bytes 1572872 | tf_op jit(solution)/shard_map/ppermute | solution.py:35
  100.7 9.3 %collective-permute-done.10 = bf16[128,2048]{1,0:T(8,128)(2,1)S(1)} collective-permute-done((bf16[128,2048]{1,0:T(8,128)(2,1)S(1)}, bf16[128,2048]{1,0:T(8,128)(2,1)S(1)}, u32[]{:S(2)}, u32[]{:S(2)}) %collective-permute-start.10) | collective-permute-done | bytes 524320 | tf_op jit(solution)/shard_map/ppermute | solution.py:35
  110.4 2.4 collective-permute-start.12
  112.8 5.5 %collective-permute-done.9 = bf16[128,2048]{1,0:T(8,128)(2,1)S(1)} collective-permute-done((bf16[128,2048]{1,0:T(8,128)(2,1)S(1)}, bf16[128,2048]{1,0:T(8,128)(2,1)S(1)}, u32[]{:S(2)}, u32[]{:S(2)}) %collective-permute-start.9) | collective-permute-done | bytes 524320 | tf_op jit(solution)/shard_map/ppermute | solution.py:35
  119.7 1.8 collective-permute-start.21
  121.5 1.7 collective-permute-start.18
  123.8 6.0 %collective-permute-done.21.refs_3_ = bf16[192,1024]{1,0:T(8,128)(2,1)S(1)} collective-permute-done((bf16[192,1024]{1,0:T(8,128)(2,1)S(1)}, bf16[192,1024]{1,0:T(8,128)(2,1)S(1)}, u32[]{:S(2)}, u32[]{:S(2)}) %collective-permute-start.21) | collective-permute-done | bytes 393248 | tf_op jit(solution)/shard_map/ppermute | solution.py:35
  131.2 2.4 collective-permute-done.18.refs_1_
  133.8 2.7 %collective-permute-done.16.refs_3_ = bf16[128,1024]{1,0:T(8,128)(2,1)S(1)} collective-permute-done((bf16[128,1024]{1,0:T(8,128)(2,1)S(1)}, bf16[128,1024]{1,0:T(8,128)(2,1)S(1)}, u32[]{:S(2)}, u32[]{:S(2)}) %collective-permute-start.16) | collective-permute-done | bytes 262176 | tf_op jit(solution)/shard_map/ppermute | solution.py:35
  141.8 3.9 %expert.7 = (bf16[192,2048]{1,0:T(8,128)(2,1)S(1)}, bf16[192,2048]{1,0:T(8,128)(2,1)S(1)}) custom-call(bf16[192,1024]{1,0:T(8,128)(2,1)S(1)} %get-tuple-element.118.refs_0_, bf16[192,1024]{1,0:T(8,128)(2,1)S(1)} %collective-permute-done.17.refs_1_, bf16[192,1024]{1,0:T(8,128)(2,1)S(1)} %get-tuple-element.119.refs_2_, ...), custom_call_target="tpu_custom_call" | custom-call | flops 1000 | bytes 1000 | tf_op jit(solution)/shard_map/expert/pallas_call | solution.py:315
  145.9 7.6 %collective-permute-done.33.refs_1_ = bf16[128,1024]{1,0:T(8,128)(2,1)S(1)} collective-permute-done((bf16[128,1024]{1,0:T(8,128)(2,1)S(1)}, bf16[128,1024]{1,0:T(8,128)(2,1)S(1)}, u32[]{:S(2)}, u32[]{:S(2)}) %collective-permute-start.33) | collective-permute-done | bytes 262176 | tf_op jit(solution)/shard_map/ppermute | solution.py:35
  156.0 3.9 %expert.6 = (bf16[192,2048]{1,0:T(8,128)(2,1)S(1)}, bf16[192,2048]{1,0:T(8,128)(2,1)S(1)}) custom-call(bf16[192,1024]{1,0:T(8,128)(2,1)S(1)} %get-tuple-element.111.refs_0_, bf16[192,1024]{1,0:T(8,128)(2,1)S(1)} %collective-permute-done.18.refs_1_, bf16[192,1024]{1,0:T(8,128)(2,1)S(1)} %get-tuple-element.112.refs_2_, ...), custom_call_target="tpu_custom_call" | custom-call | flops 1000 | bytes 1000 | tf_op jit(solution)/shard_map/expert/pallas_call | solution.py:315
  160.1 4.1 %expert.4 = (bf16[192,2048]{1,0:T(8,128)(2,1)S(1)}, bf16[192,2048]{1,0:T(8,128)(2,1)S(1)}) custom-call(bf16[192,1024]{1,0:T(8,128)(2,1)S(1)} %get-tuple-element.79.refs_0_, bf16[192,1024]{1,0:T(8,128)(2,1)S(1)} %collective-permute-done.19.refs_1_, bf16[192,1024]{1,0:T(8,128)(2,1)S(1)} %get-tuple-element.85.refs_2_, ...), custom_call_target="tpu_custom_call" | custom-call | flops 1000 | bytes 1000 | tf_op jit(solution)/shard_map/expert/pallas_call | solution.py:315
  167.3 2.3 collective-permute-start.30
  171.2 3.9 %expert.5 = (bf16[192,2048]{1,0:T(8,128)(2,1)S(1)}, bf16[192,2048]{1,0:T(8,128)(2,1)S(1)}) custom-call(bf16[192,1024]{1,0:T(8,128)(2,1)S(1)} %get-tuple-element.102.refs_0_, bf16[192,1024]{1,0:T(8,128)(2,1)S(1)} %collective-permute-done.35.refs_1_, bf16[192,1024]{1,0:T(8,128)(2,1)S(1)} %get-tuple-element.104.refs_2_, ...), custom_call_target="tpu_custom_call" | custom-call | flops 1000 | bytes 1000 | tf_op jit(solution)/shard_map/expert/pallas_call | solution.py:315
  175.3 2.1 collective-permute-done.38
  177.5 2.7 %collective-permute-done.30.refs_3_ = bf16[96,2048]{1,0:T(8,128)(2,1)S(1)} collective-permute-done((bf16[96,2048]{1,0:T(8,128)(2,1)S(1)}, bf16[96,2048]{1,0:T(8,128)(2,1)S(1)}, u32[]{:S(2)}, u32[]{:S(2)}) %collective-permute-start.30) | collective-permute-done | bytes 393248 | tf_op jit(solution)/shard_map/ppermute | solution.py:35
  180.3 2.3 collective-permute-start.41
  182.6 6.0 %collective-permute-done.28.refs_2_ = bf16[96,2048]{1,0:T(8,128)(2,1)S(1)} collective-permute-done((bf16[96,2048]{1,0:T(8,128)(2,1)S(1)}, bf16[96,2048]{1,0:T(8,128)(2,1)S(1)}, u32[]{:S(2)}, u32[]{:S(2)}) %collective-permute-start.28) | collective-permute-done | bytes 393248 | tf_op jit(solution)/shard_map/ppermute | solution.py:35
  191.8 3.2 %collective-permute-start.31 = (bf16[128,2048]{1,0:T(8,128)(2,1)S(1)}, bf16[128,2048]{1,0:T(8,128)(2,1)S(1)}, u32[]{:S(2)}, u32[]{:S(2)}) collective-permute-start(bf16[128,2048]{1,0:T(8,128)(2,1)S(1)} %combine.4), channel_id=1, source_target_pairs={{0,16},{4,20},{8,24},{12,28},{16,0},{20,4},{24,8},{28,12},{1,17},{... | collective-permute-start | bytes 1572872 | tf_op jit(solution)/shard_map/ppermute | solution.py:35
  195.0 2.2 collective-permute-done.41.refs_3_
  197.2 2.3 collective-permute-start.47
  199.4 6.1 %collective-permute-done.40.refs_2_ = bf16[96,2048]{1,0:T(8,128)(2,1)S(1)} collective-permute-done((bf16[96,2048]{1,0:T(8,128)(2,1)S(1)}, bf16[96,2048]{1,0:T(8,128)(2,1)S(1)}, u32[]{:S(2)}, u32[]{:S(2)}) %collective-permute-start.40) | collective-permute-done | bytes 393248 | tf_op jit(solution)/shard_map/ppermute | solution.py:35
  209.4 3.4 %collective-permute-start.42 = (bf16[128,2048]{1,0:T(8,128)(2,1)S(1)}, bf16[128,2048]{1,0:T(8,128)(2,1)S(1)}, u32[]{:S(2)}, u32[]{:S(2)}) collective-permute-start(bf16[128,2048]{1,0:T(8,128)(2,1)S(1)} %combine.5), channel_id=1, source_target_pairs={{0,24},{4,28},{8,16},{12,20},{16,8},{20,12},{24,0},{28,4},{1,25},{... | collective-permute-start | bytes 1572872 | tf_op jit(solution)/shard_map/ppermute | solution.py:35
  214.0 2.3 collective-permute-start.53
  216.3 6.1 %collective-permute-done.46.refs_2_ = bf16[96,2048]{1,0:T(8,128)(2,1)S(1)} collective-permute-done((bf16[96,2048]{1,0:T(8,128)(2,1)S(1)}, bf16[96,2048]{1,0:T(8,128)(2,1)S(1)}, u32[]{:S(2)}, u32[]{:S(2)}) %collective-permute-start.46) | collective-permute-done | bytes 393248 | tf_op jit(solution)/shard_map/ppermute | solution.py:35
  226.3 3.2 %collective-permute-done.31.refs_1_ = bf16[128,2048]{1,0:T(8,128)(2,1)S(1)} collective-permute-done((bf16[128,2048]{1,0:T(8,128)(2,1)S(1)}, bf16[128,2048]{1,0:T(8,128)(2,1)S(1)}, u32[]{:S(2)}, u32[]{:S(2)}) %collective-permute-start.31) | collective-permute-done | bytes 524320 | tf_op jit(solution)/shard_map/ppermute | solution.py:35
  230.9 7.7 %collective-permute-done.52.refs_2_ = bf16[96,2048]{1,0:T(8,128)(2,1)S(1)} collective-permute-done((bf16[96,2048]{1,0:T(8,128)(2,1)S(1)}, bf16[96,2048]{1,0:T(8,128)(2,1)S(1)}, u32[]{:S(2)}, u32[]{:S(2)}) %collective-permute-start.52) | collective-permute-done | bytes 393248 | tf_op jit(solution)/shard_map/ppermute | solution.py:35
  239.7 2.9 %collective-permute-done.48.refs_1_ = bf16[128,2048]{1,0:T(8,128)(2,1)S(1)} collective-permute-done((bf16[128,2048]{1,0:T(8,128)(2,1)S(1)}, bf16[128,2048]{1,0:T(8,128)(2,1)S(1)}, u32[]{:S(2)}, u32[]{:S(2)}) %collective-permute-start.48) | collective-permute-done | bytes 524320 | tf_op jit(solution)/shard_map/ppermute | solution.py:35
  (165 shorter events, 50.8 us)
Async XLA Ops:
  6.5 48.5 %all-gather.2.cloned.1.call-start = ((), (), s32[]{:S(2)}) async-start(), calls=%async_computation | async-start | bytes 2654208 | tf_op jit(solution)/shard_map/all_gather | solution.py:384
  12.5 5.8 %collective-permute-start = (bf16[144,256]{1,0:T(8,128)(2,1)}, bf16[144,256]{1,0:T(8,128)(2,1)S(1)}, u32[]{:S(2)}, u32[]{:S(2)}) collective-permute-start(bf16[144,256]{1,0:T(8,128)(2,1)} %get-tuple-element.65), channel_id=1, source_target_pairs={{0,1},{1,0},{2,3},{3,2},{4,5},{5,4},{6,7},{7,6},{8,9},{9,8},{10,11... | collective-permute-start | bytes 221192 | tf_op jit(solution)/shard_map/ppermute | solution.py:35
  15.5 4.6 %collective-permute-start.1 = (bf16[144,256]{1,0:T(8,128)(2,1)}, bf16[144,256]{1,0:T(8,128)(2,1)S(1)}, u32[]{:S(2)}, u32[]{:S(2)}) collective-permute-start(bf16[144,256]{1,0:T(8,128)(2,1)} %get-tuple-element.66), channel_id=1, source_target_pairs={{0,2},{1,3},{2,0},{3,1},{4,6},{5,7},{6,4},{7,5},{8,10},{9,11},{10,... | collective-permute-start | bytes 221192 | tf_op jit(solution)/shard_map/ppermute | solution.py:35
  17.0 5.5 %collective-permute-start.2 = (bf16[144,256]{1,0:T(8,128)(2,1)}, bf16[144,256]{1,0:T(8,128)(2,1)S(1)}, u32[]{:S(2)}, u32[]{:S(2)}) collective-permute-start(bf16[144,256]{1,0:T(8,128)(2,1)} %get-tuple-element.67), channel_id=1, source_target_pairs={{0,3},{1,2},{2,1},{3,0},{4,7},{5,6},{6,5},{7,4},{8,11},{9,10},{10,... | collective-permute-start | bytes 221192 | tf_op jit(solution)/shard_map/ppermute | solution.py:35
  23.9 14.9 %collective-permute-start.3 = (bf16[128,2048]{1,0:T(8,128)(2,1)S(1)}, bf16[128,2048]{1,0:T(8,128)(2,1)S(1)}, u32[]{:S(2)}, u32[]{:S(2)}) collective-permute-start(bf16[128,2048]{1,0:T(8,128)(2,1)S(1)} %copy-done.6), channel_id=1, source_target_pairs={{0,1},{1,0},{2,3},{3,2},{4,5},{5,4},{6,7},{7,6},{8,9},{9,8},{10,11... | collective-permute-start | bytes 1572872 | tf_op jit(solution)/shard_map/ppermute | solution.py:35
  24.5 23.4 %collective-permute-start.4 = (bf16[128,2048]{1,0:T(8,128)(2,1)S(1)}, bf16[128,2048]{1,0:T(8,128)(2,1)S(1)}, u32[]{:S(2)}, u32[]{:S(2)}) collective-permute-start(bf16[128,2048]{1,0:T(8,128)(2,1)S(1)} %copy-done.6), channel_id=1, source_target_pairs={{0,2},{1,3},{2,0},{3,1},{4,6},{5,7},{6,4},{7,5},{8,10},{9,11},{10,... | collective-permute-start | bytes 1572872 | tf_op jit(solution)/shard_map/ppermute | solution.py:35
  25.0 22.9 %collective-permute-start.5 = (bf16[128,2048]{1,0:T(8,128)(2,1)S(1)}, bf16[128,2048]{1,0:T(8,128)(2,1)S(1)}, u32[]{:S(2)}, u32[]{:S(2)}) collective-permute-start(bf16[128,2048]{1,0:T(8,128)(2,1)S(1)} %copy-done.6), channel_id=1, source_target_pairs={{0,3},{1,2},{2,1},{3,0},{4,7},{5,6},{6,5},{7,4},{8,11},{9,10},{10,... | collective-permute-start | bytes 1572872 | tf_op jit(solution)/shard_map/ppermute | solution.py:35
  58.5 15.9 %collective-permute-start.6 = (bf16[128,2048]{1,0:T(8,128)(2,1)S(1)}, bf16[128,2048]{1,0:T(8,128)(2,1)S(1)}, u32[]{:S(2)}, u32[]{:S(2)}) collective-permute-start(bf16[128,2048]{1,0:T(8,128)(2,1)S(1)} %attention.4), channel_id=1, source_target_pairs={{0,3},{1,2},{2,1},{3,0},{4,7},{5,6},{6,5},{7,4},{8,11},{9,10},{10,... | collective-permute-start | bytes 1572872 | tf_op jit(solution)/shard_map/ppermute | solution.py:35
  62.7 22.9 %collective-permute-start.7 = (bf16[128,2048]{1,0:T(8,128)(2,1)S(1)}, bf16[128,2048]{1,0:T(8,128)(2,1)S(1)}, u32[]{:S(2)}, u32[]{:S(2)}) collective-permute-start(bf16[128,2048]{1,0:T(8,128)(2,1)S(1)} %attention.5), channel_id=1, source_target_pairs={{0,1},{1,0},{2,3},{3,2},{4,5},{5,4},{6,7},{7,6},{8,9},{9,8},{10,11... | collective-permute-start | bytes 1572872 | tf_op jit(solution)/shard_map/ppermute | solution.py:35
  65.2 20.4 %collective-permute-start.8 = (bf16[128,2048]{1,0:T(8,128)(2,1)S(1)}, bf16[128,2048]{1,0:T(8,128)(2,1)S(1)}, u32[]{:S(2)}, u32[]{:S(2)}) collective-permute-start(bf16[128,2048]{1,0:T(8,128)(2,1)S(1)} %attention.6), channel_id=1, source_target_pairs={{0,2},{1,3},{2,0},{3,1},{4,6},{5,7},{6,4},{7,5},{8,10},{9,11},{10,... | collective-permute-start | bytes 1572872 | tf_op jit(solution)/shard_map/ppermute | solution.py:35
  86.1 23.9 %collective-permute-start.10 = (bf16[128,2048]{1,0:T(8,128)(2,1)S(1)}, bf16[128,2048]{1,0:T(8,128)(2,1)S(1)}, u32[]{:S(2)}, u32[]{:S(2)}) collective-permute-start(bf16[128,2048]{1,0:T(8,128)(2,1)S(1)} %get-tuple-element.74), channel_id=1, source_target_pairs={{0,8},{4,12},{8,0},{12,4},{16,24},{20,28},{24,16},{28,20},{1,9},{5... | collective-permute-start | bytes 1572872 | tf_op jit(solution)/shard_map/ppermute | solution.py:35
  88.4 8.1 %collective-permute-start.11 = (bf16[128,1024]{1,0:T(8,128)(2,1)S(1)}, bf16[128,1024]{1,0:T(8,128)(2,1)S(1)}, u32[]{:S(2)}, u32[]{:S(2)}) collective-permute-start(bf16[128,1024]{1,0:T(8,128)(2,1)S(1)} %get-tuple-element.160.refs_0_), channel_id=1, source_target_pairs={{0,1},{1,0},{2,3},{3,2},{4,5},{5,4},{6,7},{7,6},{8,9},{9,8},{10,11... | collective-permute-start | bytes 786440 | tf_op jit(solution)/shard_map/ppermute | solution.py:35
  90.0 7.8 %collective-permute-start.14 = (bf16[128,1024]{1,0:T(8,128)(2,1)S(1)}, bf16[128,1024]{1,0:T(8,128)(2,1)S(1)}, u32[]{:S(2)}, u32[]{:S(2)}) collective-permute-start(bf16[128,1024]{1,0:T(8,128)(2,1)S(1)} %get-tuple-element.159.refs_2_), channel_id=1, source_target_pairs={{0,2},{1,3},{2,0},{3,1},{4,6},{5,7},{6,4},{7,5},{8,10},{9,11},{10,... | collective-permute-start | bytes 786440 | tf_op jit(solution)/shard_map/ppermute | solution.py:35
  91.2 27.2 %collective-permute-start.9 = (bf16[128,2048]{1,0:T(8,128)(2,1)S(1)}, bf16[128,2048]{1,0:T(8,128)(2,1)S(1)}, u32[]{:S(2)}, u32[]{:S(2)}) collective-permute-start(bf16[128,2048]{1,0:T(8,128)(2,1)S(1)} %get-tuple-element.74), channel_id=1, source_target_pairs={{0,16},{4,20},{8,24},{12,28},{16,0},{20,4},{24,8},{28,12},{1,17},{... | collective-permute-start | bytes 1572872 | tf_op jit(solution)/shard_map/ppermute | solution.py:35
  98.9 22.7 %collective-permute-start.17 = (bf16[192,1024]{1,0:T(8,128)(2,1)S(1)}, bf16[192,1024]{1,0:T(8,128)(2,1)S(1)}, u32[]{:S(2)}, u32[]{:S(2)}) collective-permute-start(bf16[192,1024]{1,0:T(8,128)(2,1)S(1)} %get-tuple-element.82), channel_id=1, source_target_pairs={{0,2},{1,3},{2,0},{3,1},{4,6},{5,7},{6,4},{7,5},{8,10},{9,11},{10,... | collective-permute-start | bytes 1179656 | tf_op jit(solution)/shard_map/ppermute | solution.py:35
  100.1 19.6 %collective-permute-start.20 = (bf16[192,1024]{1,0:T(8,128)(2,1)S(1)}, bf16[192,1024]{1,0:T(8,128)(2,1)S(1)}, u32[]{:S(2)}, u32[]{:S(2)}) collective-permute-start(bf16[192,1024]{1,0:T(8,128)(2,1)S(1)} %get-tuple-element.88), channel_id=1, source_target_pairs={{0,1},{1,0},{2,3},{3,2},{4,5},{5,4},{6,7},{7,6},{8,9},{9,8},{10,11... | collective-permute-start | bytes 1179656 | tf_op jit(solution)/shard_map/ppermute | solution.py:35
  110.0 8.3 %collective-permute-start.15 = (bf16[128,1024]{1,0:T(8,128)(2,1)S(1)}, bf16[128,1024]{1,0:T(8,128)(2,1)S(1)}, u32[]{:S(2)}, u32[]{:S(2)}) collective-permute-start(bf16[128,1024]{1,0:T(8,128)(2,1)S(1)} %get-tuple-element.77.refs_2_), channel_id=1, source_target_pairs={{0,2},{1,3},{2,0},{3,1},{4,6},{5,7},{6,4},{7,5},{8,10},{9,11},{10,... | collective-permute-start | bytes 786440 | tf_op jit(solution)/shard_map/ppermute | solution.py:35
  110.4 8.2 %collective-permute-start.12 = (bf16[128,1024]{1,0:T(8,128)(2,1)S(1)}, bf16[128,1024]{1,0:T(8,128)(2,1)S(1)}, u32[]{:S(2)}, u32[]{:S(2)}) collective-permute-start(bf16[128,1024]{1,0:T(8,128)(2,1)S(1)} %get-tuple-element.75.refs_0_), channel_id=1, source_target_pairs={{0,1},{1,0},{2,3},{3,2},{4,5},{5,4},{6,7},{7,6},{8,9},{9,8},{10,11... | collective-permute-start | bytes 786440 | tf_op jit(solution)/shard_map/ppermute | solution.py:35
  118.6 15.1 %collective-permute-start.32 = (bf16[128,2048]{1,0:T(8,128)(2,1)S(1)}, bf16[128,2048]{1,0:T(8,128)(2,1)S(1)}, u32[]{:S(2)}, u32[]{:S(2)}) collective-permute-start(bf16[128,2048]{1,0:T(8,128)(2,1)S(1)} %collective-permute-done.9), channel_id=1, source_target_pairs={{0,8},{4,12},{8,0},{12,4},{16,24},{20,28},{24,16},{28,20},{1,9},{5... | collective-permute-start | bytes 1572872 | tf_op jit(solution)/shard_map/ppermute | solution.py:35
  119.7 10.1 %collective-permute-start.21 = (bf16[192,1024]{1,0:T(8,128)(2,1)S(1)}, bf16[192,1024]{1,0:T(8,128)(2,1)S(1)}, u32[]{:S(2)}, u32[]{:S(2)}) collective-permute-start(bf16[192,1024]{1,0:T(8,128)(2,1)S(1)} %get-tuple-element.89), channel_id=1, source_target_pairs={{0,1},{1,0},{2,3},{3,2},{4,5},{5,4},{6,7},{7,6},{8,9},{9,8},{10,11... | collective-permute-start | bytes 1179656 | tf_op jit(solution)/shard_map/ppermute | solution.py:35
  121.5 12.1 %collective-permute-start.18 = (bf16[192,1024]{1,0:T(8,128)(2,1)S(1)}, bf16[192,1024]{1,0:T(8,128)(2,1)S(1)}, u32[]{:S(2)}, u32[]{:S(2)}) collective-permute-start(bf16[192,1024]{1,0:T(8,128)(2,1)S(1)} %get-tuple-element.83), channel_id=1, source_target_pairs={{0,2},{1,3},{2,0},{3,1},{4,6},{5,7},{6,4},{7,5},{8,10},{9,11},{10,... | collective-permute-start | bytes 1179656 | tf_op jit(solution)/shard_map/ppermute | solution.py:35
  123.3 17.2 %collective-permute-start.49 = (bf16[384,1024]{1,0:T(8,128)(2,1)S(1)}, bf16[384,1024]{1,0:T(8,128)(2,1)S(1)}, u32[]{:S(2)}, u32[]{:S(2)}) collective-permute-start(bf16[384,1024]{1,0:T(8,128)(2,1)S(1)} %halves.7), channel_id=1, source_target_pairs={{0,4},{4,0},{8,12},{12,8},{16,20},{20,16},{24,28},{28,24},{1,5},{5... | collective-permute-start | bytes 2359304 | tf_op jit(solution)/shard_map/ppermute | solution.py:35
  123.4 13.1 %collective-permute-start.16 = (bf16[128,1024]{1,0:T(8,128)(2,1)S(1)}, bf16[128,1024]{1,0:T(8,128)(2,1)S(1)}, u32[]{:S(2)}, u32[]{:S(2)}) collective-permute-start(bf16[128,1024]{1,0:T(8,128)(2,1)S(1)} %get-tuple-element.78.refs_2_), channel_id=1, source_target_pairs={{0,2},{1,3},{2,0},{3,1},{4,6},{5,7},{6,4},{7,5},{8,10},{9,11},{10,... | collective-permute-start | bytes 786440 | tf_op jit(solution)/shard_map/ppermute | solution.py:35
  129.9 8.1 %collective-permute-start.13 = (bf16[128,1024]{1,0:T(8,128)(2,1)S(1)}, bf16[128,1024]{1,0:T(8,128)(2,1)S(1)}, u32[]{:S(2)}, u32[]{:S(2)}) collective-permute-start(bf16[128,1024]{1,0:T(8,128)(2,1)S(1)} %get-tuple-element.76.refs_0_), channel_id=1, source_target_pairs={{0,1},{1,0},{2,3},{3,2},{4,5},{5,4},{6,7},{7,6},{8,9},{9,8},{10,11... | collective-permute-start | bytes 786440 | tf_op jit(solution)/shard_map/ppermute | solution.py:35
  133.7 22.3 %collective-permute-start.43 = (bf16[384,1024]{1,0:T(8,128)(2,1)S(1)}, bf16[384,1024]{1,0:T(8,128)(2,1)S(1)}, u32[]{:S(2)}, u32[]{:S(2)}) collective-permute-start(bf16[384,1024]{1,0:T(8,128)(2,1)S(1)} %halves.6), channel_id=1, source_target_pairs={{0,4},{4,0},{8,12},{12,8},{16,20},{20,16},{24,28},{28,24},{1,5},{5... | collective-permute-start | bytes 2359304 | tf_op jit(solution)/shard_map/ppermute | solution.py:35
  136.5 9.2 %collective-permute-start.34 = (bf16[128,1024]{1,0:T(8,128)(2,1)S(1)}, bf16[128,1024]{1,0:T(8,128)(2,1)S(1)}, u32[]{:S(2)}, u32[]{:S(2)}) collective-permute-start(bf16[128,1024]{1,0:T(8,128)(2,1)S(1)} %get-tuple-element.95.refs_2_), channel_id=1, source_target_pairs={{0,2},{1,3},{2,0},{3,1},{4,6},{5,7},{6,4},{7,5},{8,10},{9,11},{10,... | collective-permute-start | bytes 786440 | tf_op jit(solution)/shard_map/ppermute | solution.py:35
  139.1 15.5 %collective-permute-start.22 = (bf16[192,1024]{1,0:T(8,128)(2,1)S(1)}, bf16[192,1024]{1,0:T(8,128)(2,1)S(1)}, u32[]{:S(2)}, u32[]{:S(2)}) collective-permute-start(bf16[192,1024]{1,0:T(8,128)(2,1)S(1)} %get-tuple-element.90), channel_id=1, source_target_pairs={{0,1},{1,0},{2,3},{3,2},{4,5},{5,4},{6,7},{7,6},{8,9},{9,8},{10,11... | collective-permute-start | bytes 1179656 | tf_op jit(solution)/shard_map/ppermute | solution.py:35
  139.9 15.2 %collective-permute-start.19 = (bf16[192,1024]{1,0:T(8,128)(2,1)S(1)}, bf16[192,1024]{1,0:T(8,128)(2,1)S(1)}, u32[]{:S(2)}, u32[]{:S(2)}) collective-permute-start(bf16[192,1024]{1,0:T(8,128)(2,1)S(1)} %get-tuple-element.84), channel_id=1, source_target_pairs={{0,2},{1,3},{2,0},{3,1},{4,6},{5,7},{6,4},{7,5},{8,10},{9,11},{10,... | collective-permute-start | bytes 1179656 | tf_op jit(solution)/shard_map/ppermute | solution.py:35
  140.4 13.0 %collective-permute-start.33 = (bf16[128,1024]{1,0:T(8,128)(2,1)S(1)}, bf16[128,1024]{1,0:T(8,128)(2,1)S(1)}, u32[]{:S(2)}, u32[]{:S(2)}) collective-permute-start(bf16[128,1024]{1,0:T(8,128)(2,1)S(1)} %get-tuple-element.94.refs_0_), channel_id=1, source_target_pairs={{0,1},{1,0},{2,3},{3,2},{4,5},{5,4},{6,7},{7,6},{8,9},{9,8},{10,11... | collective-permute-start | bytes 786440 | tf_op jit(solution)/shard_map/ppermute | solution.py:35
  145.8 14.2 %collective-permute-start.50 = (bf16[192,2048]{1,0:T(8,128)(2,1)S(1)}, bf16[192,2048]{1,0:T(8,128)(2,1)S(1)}, u32[]{:S(2)}, u32[]{:S(2)}) collective-permute-start(bf16[192,2048]{1,0:T(8,128)(2,1)S(1)} %get-tuple-element.121), channel_id=1, source_target_pairs={{0,4},{4,0},{8,12},{12,8},{16,20},{20,16},{24,28},{28,24},{1,5},{5... | collective-permute-start | bytes 2359304 | tf_op jit(solution)/shard_map/ppermute | solution.py:35
  154.6 10.8 %collective-permute-start.36 = (bf16[192,1024]{1,0:T(8,128)(2,1)S(1)}, bf16[192,1024]{1,0:T(8,128)(2,1)S(1)}, u32[]{:S(2)}, u32[]{:S(2)}) collective-permute-start(bf16[192,1024]{1,0:T(8,128)(2,1)S(1)} %get-tuple-element.101), channel_id=1, source_target_pairs={{0,1},{1,0},{2,3},{3,2},{4,5},{5,4},{6,7},{7,6},{8,9},{9,8},{10,11... | collective-permute-start | bytes 1179656 | tf_op jit(solution)/shard_map/ppermute | solution.py:35
  155.1 10.4 %collective-permute-start.35 = (bf16[192,1024]{1,0:T(8,128)(2,1)S(1)}, bf16[192,1024]{1,0:T(8,128)(2,1)S(1)}, u32[]{:S(2)}, u32[]{:S(2)}) collective-permute-start(bf16[192,1024]{1,0:T(8,128)(2,1)S(1)} %get-tuple-element.98), channel_id=1, source_target_pairs={{0,2},{1,3},{2,0},{3,1},{4,6},{5,7},{6,4},{7,5},{8,10},{9,11},{10,... | collective-permute-start | bytes 1179656 | tf_op jit(solution)/shard_map/ppermute | solution.py:35
  165.5 5.5 %collective-permute-start.44 = (bf16[192,2048]{1,0:T(8,128)(2,1)S(1)}, bf16[192,2048]{1,0:T(8,128)(2,1)S(1)}, u32[]{:S(2)}, u32[]{:S(2)}) collective-permute-start(bf16[192,2048]{1,0:T(8,128)(2,1)S(1)} %get-tuple-element.114), channel_id=1, source_target_pairs={{0,4},{4,0},{8,12},{12,8},{16,20},{20,16},{24,28},{28,24},{1,5},{5... | collective-permute-start | bytes 2359304 | tf_op jit(solution)/shard_map/ppermute | solution.py:35
  167.3 13.0 %collective-permute-start.30 = (bf16[96,2048]{1,0:T(8,128)(2,1)S(1)}, bf16[96,2048]{1,0:T(8,128)(2,1)S(1)}, u32[]{:S(2)}, u32[]{:S(2)}) collective-permute-start(bf16[96,2048]{1,0:T(8,128)(2,1)S(1)} %pad_maximum_fusion.3), channel_id=1, source_target_pairs={{0,3},{1,2},{2,1},{3,0},{4,7},{5,6},{6,5},{7,4},{8,11},{9,10},{10,... | collective-permute-start | bytes 1179656 | tf_op jit(solution)/shard_map/ppermute | solution.py:35
  169.7 18.9 %collective-permute-start.28 = (bf16[96,2048]{1,0:T(8,128)(2,1)S(1)}, bf16[96,2048]{1,0:T(8,128)(2,1)S(1)}, u32[]{:S(2)}, u32[]{:S(2)}) collective-permute-start(bf16[96,2048]{1,0:T(8,128)(2,1)S(1)} %pad_maximum_fusion.2), channel_id=1, source_target_pairs={{0,2},{1,3},{2,0},{3,1},{4,6},{5,7},{6,4},{7,5},{8,10},{9,11},{10,... | collective-permute-start | bytes 1179656 | tf_op jit(solution)/shard_map/ppermute | solution.py:35
  170.2 19.7 %collective-permute-start.26 = (bf16[96,2048]{1,0:T(8,128)(2,1)S(1)}, bf16[96,2048]{1,0:T(8,128)(2,1)S(1)}, u32[]{:S(2)}, u32[]{:S(2)}) collective-permute-start(bf16[96,2048]{1,0:T(8,128)(2,1)S(1)} %pad_maximum_fusion.1), channel_id=1, source_target_pairs={{0,1},{1,0},{2,3},{3,2},{4,5},{5,4},{6,7},{7,6},{8,9},{9,8},{10,11... | collective-permute-start | bytes 1179656 | tf_op jit(solution)/shard_map/ppermute | solution.py:35
  180.3 16.9 %collective-permute-start.41 = (bf16[96,2048]{1,0:T(8,128)(2,1)S(1)}, bf16[96,2048]{1,0:T(8,128)(2,1)S(1)}, u32[]{:S(2)}, u32[]{:S(2)}) collective-permute-start(bf16[96,2048]{1,0:T(8,128)(2,1)S(1)} %pad_maximum_fusion.7), channel_id=1, source_target_pairs={{0,3},{1,2},{2,1},{3,0},{4,7},{5,6},{6,5},{7,4},{8,11},{9,10},{10,... | collective-permute-start | bytes 1179656 | tf_op jit(solution)/shard_map/ppermute | solution.py:35
  188.6 16.9 %collective-permute-start.40 = (bf16[96,2048]{1,0:T(8,128)(2,1)S(1)}, bf16[96,2048]{1,0:T(8,128)(2,1)S(1)}, u32[]{:S(2)}, u32[]{:S(2)}) collective-permute-start(bf16[96,2048]{1,0:T(8,128)(2,1)S(1)} %pad_maximum_fusion.6), channel_id=1, source_target_pairs={{0,2},{1,3},{2,0},{3,1},{4,6},{5,7},{6,4},{7,5},{8,10},{9,11},{10,... | collective-permute-start | bytes 1179656 | tf_op jit(solution)/shard_map/ppermute | solution.py:35
  189.9 16.9 %collective-permute-start.39 = (bf16[96,2048]{1,0:T(8,128)(2,1)S(1)}, bf16[96,2048]{1,0:T(8,128)(2,1)S(1)}, u32[]{:S(2)}, u32[]{:S(2)}) collective-permute-start(bf16[96,2048]{1,0:T(8,128)(2,1)S(1)} %pad_maximum_fusion.5), channel_id=1, source_target_pairs={{0,1},{1,0},{2,3},{3,2},{4,5},{5,4},{6,7},{7,6},{8,9},{9,8},{10,11... | collective-permute-start | bytes 1179656 | tf_op jit(solution)/shard_map/ppermute | solution.py:35
  191.8 37.7 %collective-permute-start.31 = (bf16[128,2048]{1,0:T(8,128)(2,1)S(1)}, bf16[128,2048]{1,0:T(8,128)(2,1)S(1)}, u32[]{:S(2)}, u32[]{:S(2)}) collective-permute-start(bf16[128,2048]{1,0:T(8,128)(2,1)S(1)} %combine.4), channel_id=1, source_target_pairs={{0,16},{4,20},{8,24},{12,28},{16,0},{20,4},{24,8},{28,12},{1,17},{... | collective-permute-start | bytes 1572872 | tf_op jit(solution)/shard_map/ppermute | solution.py:35
  197.2 16.9 %collective-permute-start.47 = (bf16[96,2048]{1,0:T(8,128)(2,1)S(1)}, bf16[96,2048]{1,0:T(8,128)(2,1)S(1)}, u32[]{:S(2)}, u32[]{:S(2)}) collective-permute-start(bf16[96,2048]{1,0:T(8,128)(2,1)S(1)} %pad_maximum_fusion.11), channel_id=1, source_target_pairs={{0,3},{1,2},{2,1},{3,0},{4,7},{5,6},{6,5},{7,4},{8,11},{9,10},{10,... | collective-permute-start | bytes 1179656 | tf_op jit(solution)/shard_map/ppermute | solution.py:35
  205.5 16.9 %collective-permute-start.46 = (bf16[96,2048]{1,0:T(8,128)(2,1)S(1)}, bf16[96,2048]{1,0:T(8,128)(2,1)S(1)}, u32[]{:S(2)}, u32[]{:S(2)}) collective-permute-start(bf16[96,2048]{1,0:T(8,128)(2,1)S(1)} %pad_maximum_fusion.10), channel_id=1, source_target_pairs={{0,2},{1,3},{2,0},{3,1},{4,6},{5,7},{6,4},{7,5},{8,10},{9,11},{10,... | collective-permute-start | bytes 1179656 | tf_op jit(solution)/shard_map/ppermute | solution.py:35
  206.8 16.9 %collective-permute-start.45 = (bf16[96,2048]{1,0:T(8,128)(2,1)S(1)}, bf16[96,2048]{1,0:T(8,128)(2,1)S(1)}, u32[]{:S(2)}, u32[]{:S(2)}) collective-permute-start(bf16[96,2048]{1,0:T(8,128)(2,1)S(1)} %pad_maximum_fusion.9), channel_id=1, source_target_pairs={{0,1},{1,0},{2,3},{3,2},{4,5},{5,4},{6,7},{7,6},{8,9},{9,8},{10,11... | collective-permute-start | bytes 1179656 | tf_op jit(solution)/shard_map/ppermute | solution.py:35
  209.4 20.7 %collective-permute-start.42 = (bf16[128,2048]{1,0:T(8,128)(2,1)S(1)}, bf16[128,2048]{1,0:T(8,128)(2,1)S(1)}, u32[]{:S(2)}, u32[]{:S(2)}) collective-permute-start(bf16[128,2048]{1,0:T(8,128)(2,1)S(1)} %combine.5), channel_id=1, source_target_pairs={{0,24},{4,28},{8,16},{12,20},{16,8},{20,12},{24,0},{28,4},{1,25},{... | collective-permute-start | bytes 1572872 | tf_op jit(solution)/shard_map/ppermute | solution.py:35
  214.0 16.9 %collective-permute-start.53 = (bf16[96,2048]{1,0:T(8,128)(2,1)S(1)}, bf16[96,2048]{1,0:T(8,128)(2,1)S(1)}, u32[]{:S(2)}, u32[]{:S(2)}) collective-permute-start(bf16[96,2048]{1,0:T(8,128)(2,1)S(1)} %pad_maximum_fusion.15), channel_id=1, source_target_pairs={{0,3},{1,2},{2,1},{3,0},{4,7},{5,6},{6,5},{7,4},{8,11},{9,10},{10,... | collective-permute-start | bytes 1179656 | tf_op jit(solution)/shard_map/ppermute | solution.py:35
  222.4 16.2 %collective-permute-start.52 = (bf16[96,2048]{1,0:T(8,128)(2,1)S(1)}, bf16[96,2048]{1,0:T(8,128)(2,1)S(1)}, u32[]{:S(2)}, u32[]{:S(2)}) collective-permute-start(bf16[96,2048]{1,0:T(8,128)(2,1)S(1)} %pad_maximum_fusion.14), channel_id=1, source_target_pairs={{0,2},{1,3},{2,0},{3,1},{4,6},{5,7},{6,4},{7,5},{8,10},{9,11},{10,... | collective-permute-start | bytes 1179656 | tf_op jit(solution)/shard_map/ppermute | solution.py:35
  223.7 14.9 %collective-permute-start.51 = (bf16[96,2048]{1,0:T(8,128)(2,1)S(1)}, bf16[96,2048]{1,0:T(8,128)(2,1)S(1)}, u32[]{:S(2)}, u32[]{:S(2)}) collective-permute-start(bf16[96,2048]{1,0:T(8,128)(2,1)S(1)} %pad_maximum_fusion.13), channel_id=1, source_target_pairs={{0,1},{1,0},{2,3},{3,2},{4,5},{5,4},{6,7},{7,6},{8,9},{9,8},{10,11... | collective-permute-start | bytes 1179656 | tf_op jit(solution)/shard_map/ppermute | solution.py:35
  229.5 13.1 %collective-permute-start.48 = (bf16[128,2048]{1,0:T(8,128)(2,1)S(1)}, bf16[128,2048]{1,0:T(8,128)(2,1)S(1)}, u32[]{:S(2)}, u32[]{:S(2)}) collective-permute-start(bf16[128,2048]{1,0:T(8,128)(2,1)S(1)} %combine.6), channel_id=1, source_target_pairs={{0,8},{4,12},{8,0},{12,4},{16,24},{20,28},{24,16},{28,20},{1,9},{5... | collective-permute-start | bytes 1572872 | tf_op jit(solution)/shard_map/ppermute | solution.py:35
  (20 other events, 206.9 us)
Sparse Core Ops, SparseCore 0:
  24.0 30.9 all-gather.1

commit v15 on v14

--- a/solution.py
+++ b/solution.py
@@ -247,17 +247,21 @@
 
 
 def combine_kernel(group, capacity, place, routing, *refs):
-    *returned, out = refs
+    count = routing.shape[1]
+    returned, others, out = refs[:count], refs[count:-1], refs[-1]
     slots = lax.broadcasted_iota(jnp.int32, (capacity, out.shape[0]), 0)
     parts = []
-    for distance in range(len(returned)):
+    for distance in range(count):
         for slot, weight in plane_targets(group, place, routing, 0, distance):
             parts.append(jnp.where(slots == slot, weight, 0.0))
     shares = jnp.concatenate(parts, axis=0).astype(jnp.bfloat16)
     produced = jnp.concatenate([ref[...] for ref in returned], axis=0)
-    out[...] = lax.dot_general(
+    total = lax.dot_general(
         shares, produced, (((0,), (0,)), ((), ())), preferred_element_type=jnp.float32
-    ).astype(jnp.bfloat16)
+    )
+    for other in others:
+        total = total + other[...]
+    out[...] = total.astype(jnp.bfloat16)
 
 
 def expert_kernel(routes, capacity, *refs):
@@ -519,30 +523,32 @@
         for d in peers:
             back.append(jnp.concatenate([part[d] for part in produced[g]], axis=0))
         back = [back[0]] + [send(back[d], d, "back") for d in peers[1:]]
+        early = [] if g else [residual]
+        for total in [] if g else totals:
+            early = [
+                call(
+                    sum_kernel,
+                    jax.ShapeDtypeStruct((rows, width), jnp.float32),
+                    [VMEM] * 2,
+                    *early,
+                    total,
+                    name="add",
+                    flops=1_500_000_000,
+                )
+            ]
         total = call(
             functools.partial(combine_kernel, g, capacity),
             bf16((rows, width)),
-            [SMEM, VMEM] + [VMEM] * exp_count,
+            [SMEM, VMEM] + [VMEM] * (exp_count + len(early)),
             place,
             routing,
             *back,
+            *early,
             name="combine",
         )
         if g:
-            total = swap(total, "ctx", 2 * g)
-        totals.append(total)
-    early = residual
-    for total in totals[:-1]:
-        early = call(
-            sum_kernel,
-            jax.ShapeDtypeStruct((rows, width), jnp.float32),
-            [VMEM] * 2,
-            early,
-            total,
-            name="add",
-            flops=3_000_000_000,
-        )
-    return call(sum_kernel, bf16((rows, width)), [VMEM] * 2, early, totals[-1], name="add")
+            totals.append(swap(total, "ctx", 2 * g))
+    return total
 
 
 def solution(mesh):

time: 251 us -> 254 us (1.012)
  waiting for transfers between devices: 124 us -> 127 us
    ppermute x54, waiting for transfers between devices: 120 us -> 123 us  [swap(): return lax.ppermute(array, axis, pairs)]
    pallas_call x29 -> x28, Pallas kernels: 39.5 us -> 39.5 us  [call(): pl.pallas_call(kernel, out_shape=out_shape, in_specs=specs, out_specs=jax...]
  transfers between devices with their start and end apart: 55 -> 55, of which waited for: 32 -> 33; matrix products, arithmetic and copies ran while one was open for 1% -> 1% of each run, Pallas kernels for 13% -> 12%
where the time goes in v15:
time: 254 us
  waiting for transfers between devices  127 us (50%)
  starting transfers between devices  63.8 us (25%)
  Pallas kernels  39.5 us (16%)
  between operations  14 us (6%)
  local copies, waits for them, and re-layouts  6.35 us (2%)
  other arithmetic  3.04 us (1%)
    ppermute x54, waiting for transfers between devices, swap(): return lax.ppermute(array, axis, pairs)  123 us
    ppermute x54, starting transfers between devices, swap(): return lax.ppermute(array, axis, pairs)  63.8 us
    pallas_call x28, Pallas kernels, call(): pl.pallas_call(kernel, out_shape=out_shape, in_specs=specs, out_specs=jax...  39.5 us
    unnamed x33, local copies, waits for them, and re-layouts  5.6 us
  transfers between devices with their start and end apart: 55, of which 33 were waited for; matrix products, arithmetic and copies ran while one was open for 1% of the time, Pallas kernels for 12%

profile of v15, /device:TPU:0, one launch (start us, length us, event | category | flops | bytes accessed | tf_op | source)
XLA Modules:
  0.0 253.8 jit_solution(7097725896494781411)
XLA Ops:
  8.1 4.3 %own_rows.1 = (bf16[144,256]{1,0:T(8,128)(2,1)}, bf16[144,256]{1,0:T(8,128)(2,1)}, bf16[144,256]{1,0:T(8,128)(2,1)}, bf16[144,256]{1,0:T(8,128)(2,1)}) custom-call(s32[6]{0:T(128)} %pad_add_fusion.place, s32[8,128]{1,0:T(8,128)} %bitcast.38, s32[8,128]{1,0:T(8,128)} %bitcast.39, bf16[128,2048]{1,0:T(8,128)(2,1)} %tokens.1, f32[1,2048]{1,0:T(1,128)} %bitcast.34, ...), custom_call_target="tpu_custom_call" | custom-call | flops 1000 | bytes 1000 | tf_op jit(solution)/shard_map/own_rows/pallas_call | solution.py:319
  12.5 3.0 %collective-permute-start = (bf16[144,256]{1,0:T(8,128)(2,1)}, bf16[144,256]{1,0:T(8,128)(2,1)S(1)}, u32[]{:S(2)}, u32[]{:S(2)}) collective-permute-start(bf16[144,256]{1,0:T(8,128)(2,1)} %get-tuple-element.66), channel_id=1, source_target_pairs={{0,1},{1,0},{2,3},{3,2},{4,5},{5,4},{6,7},{7,6},{8,9},{9,8},{10,11... | collective-permute-start | bytes 221192 | tf_op jit(solution)/shard_map/ppermute | solution.py:35
  18.3 1.7 collective-permute-done.1
  20.1 2.4 collective-permute-done.2
  25.0 2.5 collective-permute-start.5
  28.5 10.4 %collective-permute-done.3.refs_1_ = bf16[128,2048]{1,0:T(8,128)(2,1)S(1)} collective-permute-done((bf16[128,2048]{1,0:T(8,128)(2,1)S(1)}, bf16[128,2048]{1,0:T(8,128)(2,1)S(1)}, u32[]{:S(2)}, u32[]{:S(2)}) %collective-permute-start.3) | collective-permute-done | bytes 524320 | tf_op jit(solution)/shard_map/ppermute | solution.py:35
  38.9 9.1 %collective-permute-done.4.refs_2_ = bf16[128,2048]{1,0:T(8,128)(2,1)S(1)} collective-permute-done((bf16[128,2048]{1,0:T(8,128)(2,1)S(1)}, bf16[128,2048]{1,0:T(8,128)(2,1)S(1)}, u32[]{:S(2)}, u32[]{:S(2)}) %collective-permute-start.4) | collective-permute-done | bytes 524320 | tf_op jit(solution)/shard_map/ppermute | solution.py:35
  48.0 1.6 copy-done.7
  49.6 1.8 queries.1
  51.5 3.6 %all-gather.2.cloned.1.call-done.both = bf16[4608,256]{1,0:T(8,128)(2,1)} async-done(((bf16[576,256]{1,0:T(8,128)(2,1)}), bf16[4608,256]{1,0:T(8,128)(2,1)}) %all-gather.2.cloned.1.call-update) | async-done | bytes 2359312 | tf_op jit(solution)/shard_map/all_gather | solution.py:388
  55.1 1.7 copy-done.3
  56.7 1.7 attention.4
  58.5 2.4 collective-permute-start.6
  60.9 1.7 attention.5
  63.3 1.9 attention.6
  65.9 1.7 attention.7.refs_0_
  67.6 6.7 %collective-permute-done.6.refs_1_ = bf16[128,2048]{1,0:T(8,128)(2,1)S(1)} collective-permute-done((bf16[128,2048]{1,0:T(8,128)(2,1)S(1)}, bf16[128,2048]{1,0:T(8,128)(2,1)S(1)}, u32[]{:S(2)}, u32[]{:S(2)}) %collective-permute-start.6) | collective-permute-done | bytes 524320 | tf_op jit(solution)/shard_map/ppermute | solution.py:35
  74.5 11.0 %collective-permute-done.7.refs_1_ = bf16[128,2048]{1,0:T(8,128)(2,1)S(1)} collective-permute-done((bf16[128,2048]{1,0:T(8,128)(2,1)S(1)}, bf16[128,2048]{1,0:T(8,128)(2,1)S(1)}, u32[]{:S(2)}, u32[]{:S(2)}) %collective-permute-start.7) | collective-permute-done | bytes 524320 | tf_op jit(solution)/shard_map/ppermute | solution.py:35
  86.1 2.3 collective-permute-start.15
  88.4 1.5 collective-permute-start.9
  91.2 3.9 %collective-permute-start.22 = (bf16[128,2048]{1,0:T(8,128)(2,1)S(1)}, bf16[128,2048]{1,0:T(8,128)(2,1)S(1)}, u32[]{:S(2)}, u32[]{:S(2)}) collective-permute-start(bf16[128,2048]{1,0:T(8,128)(2,1)S(1)} %get-tuple-element.73), channel_id=1, source_target_pairs={{0,16},{4,20},{8,24},{12,28},{16,0},{20,4},{24,8},{28,12},{1,17},{... | collective-permute-start | bytes 1572872 | tf_op jit(solution)/shard_map/ppermute | solution.py:35
  100.7 9.3 %collective-permute-done.15 = bf16[128,2048]{1,0:T(8,128)(2,1)S(1)} collective-permute-done((bf16[128,2048]{1,0:T(8,128)(2,1)S(1)}, bf16[128,2048]{1,0:T(8,128)(2,1)S(1)}, u32[]{:S(2)}, u32[]{:S(2)}) %collective-permute-start.15) | collective-permute-done | bytes 524320 | tf_op jit(solution)/shard_map/ppermute | solution.py:35
  110.0 2.4 collective-permute-start.16
  112.8 5.5 %collective-permute-done.22 = bf16[128,2048]{1,0:T(8,128)(2,1)S(1)} collective-permute-done((bf16[128,2048]{1,0:T(8,128)(2,1)S(1)}, bf16[128,2048]{1,0:T(8,128)(2,1)S(1)}, u32[]{:S(2)}, u32[]{:S(2)}) %collective-permute-start.22) | collective-permute-done | bytes 524320 | tf_op jit(solution)/shard_map/ppermute | solution.py:35
  122.1 1.7 collective-permute-start.24
  123.8 6.8 %collective-permute-done.18.refs_1_ = bf16[192,1024]{1,0:T(8,128)(2,1)S(1)} collective-permute-done((bf16[192,1024]{1,0:T(8,128)(2,1)S(1)}, bf16[192,1024]{1,0:T(8,128)(2,1)S(1)}, u32[]{:S(2)}, u32[]{:S(2)}) %collective-permute-start.18) | collective-permute-done | bytes 393248 | tf_op jit(solution)/shard_map/ppermute | solution.py:35
  131.3 2.2 collective-permute-done.19.refs_3_
  133.8 2.9 %collective-permute-done.24.refs_1_ = bf16[128,1024]{1,0:T(8,128)(2,1)S(1)} collective-permute-done((bf16[128,1024]{1,0:T(8,128)(2,1)S(1)}, bf16[128,1024]{1,0:T(8,128)(2,1)S(1)}, u32[]{:S(2)}, u32[]{:S(2)}) %collective-permute-start.24) | collective-permute-done | bytes 262176 | tf_op jit(solution)/shard_map/ppermute | solution.py:35
  141.9 3.9 %expert.4 = (bf16[192,2048]{1,0:T(8,128)(2,1)S(1)}, bf16[192,2048]{1,0:T(8,128)(2,1)S(1)}) custom-call(bf16[192,1024]{1,0:T(8,128)(2,1)S(1)} %get-tuple-element.74.refs_0_, bf16[192,1024]{1,0:T(8,128)(2,1)S(1)} %collective-permute-done.11.refs_1_, bf16[192,1024]{1,0:T(8,128)(2,1)S(1)} %get-tuple-element.76.refs_2_, ...), custom_call_target="tpu_custom_call" | custom-call | flops 1000 | bytes 1000 | tf_op jit(solution)/shard_map/expert/pallas_call | solution.py:319
  146.0 6.6 %collective-permute-done.27.refs_3_ = bf16[128,1024]{1,0:T(8,128)(2,1)S(1)} collective-permute-done((bf16[128,1024]{1,0:T(8,128)(2,1)S(1)}, bf16[128,1024]{1,0:T(8,128)(2,1)S(1)}, u32[]{:S(2)}, u32[]{:S(2)}) %collective-permute-start.27) | collective-permute-done | bytes 262176 | tf_op jit(solution)/shard_map/ppermute | solution.py:35
  155.1 1.6 collective-permute-start.31
  156.8 3.9 %expert.5 = (bf16[192,2048]{1,0:T(8,128)(2,1)S(1)}, bf16[192,2048]{1,0:T(8,128)(2,1)S(1)}) custom-call(bf16[192,1024]{1,0:T(8,128)(2,1)S(1)} %get-tuple-element.82.refs_0_, bf16[192,1024]{1,0:T(8,128)(2,1)S(1)} %collective-permute-done.18.refs_1_, bf16[192,1024]{1,0:T(8,128)(2,1)S(1)} %get-tuple-element.85.refs_2_, ...), custom_call_target="tpu_custom_call" | custom-call | flops 1000 | bytes 1000 | tf_op jit(solution)/shard_map/expert/pallas_call | solution.py:319
  160.9 4.1 %expert.6 = (bf16[192,2048]{1,0:T(8,128)(2,1)S(1)}, bf16[192,2048]{1,0:T(8,128)(2,1)S(1)}) custom-call(bf16[192,1024]{1,0:T(8,128)(2,1)S(1)} %get-tuple-element.105.refs_0_, bf16[192,1024]{1,0:T(8,128)(2,1)S(1)} %collective-permute-done.28.refs_1_, bf16[192,1024]{1,0:T(8,128)(2,1)S(1)} %get-tuple-element.106.refs_2_, ...), custom_call_target="tpu_custom_call" | custom-call | flops 1000 | bytes 1000 | tf_op jit(solution)/shard_map/expert/pallas_call | solution.py:319
  169.4 2.4 collective-permute-start.47
  171.9 3.9 %expert.7 = (bf16[192,2048]{1,0:T(8,128)(2,1)S(1)}, bf16[192,2048]{1,0:T(8,128)(2,1)S(1)}) custom-call(bf16[192,1024]{1,0:T(8,128)(2,1)S(1)} %get-tuple-element.108.refs_0_, bf16[192,1024]{1,0:T(8,128)(2,1)S(1)} %collective-permute-done.29.refs_1_, bf16[192,1024]{1,0:T(8,128)(2,1)S(1)} %get-tuple-element.110.refs_2_, ...), custom_call_target="tpu_custom_call" | custom-call | flops 1000 | bytes 1000 | tf_op jit(solution)/shard_map/expert/pallas_call | solution.py:319
  176.0 2.1 collective-permute-done.38
  178.2 1.9 collective-permute-done.39.refs_1_
  180.6 7.6 %collective-permute-done.43.refs_2_ = bf16[96,2048]{1,0:T(8,128)(2,1)S(1)} collective-permute-done((bf16[96,2048]{1,0:T(8,128)(2,1)S(1)}, bf16[96,2048]{1,0:T(8,128)(2,1)S(1)}, u32[]{:S(2)}, u32[]{:S(2)}) %collective-permute-start.43) | collective-permute-done | bytes 393248 | tf_op jit(solution)/shard_map/ppermute | solution.py:35
  188.5 2.8 %collective-permute-start.48 = (bf16[96,2048]{1,0:T(8,128)(2,1)S(1)}, bf16[96,2048]{1,0:T(8,128)(2,1)S(1)}, u32[]{:S(2)}, u32[]{:S(2)}) collective-permute-start(bf16[96,2048]{1,0:T(8,128)(2,1)S(1)} %pad_maximum_fusion.11), channel_id=1, source_target_pairs={{0,3},{1,2},{2,1},{3,0},{4,7},{5,6},{6,5},{7,4},{8,11},{9,10},{10,... | collective-permute-start | bytes 1179656 | tf_op jit(solution)/shard_map/ppermute | solution.py:35
  192.3 3.8 %collective-permute-start.51 = (bf16[128,2048]{1,0:T(8,128)(2,1)S(1)}, bf16[128,2048]{1,0:T(8,128)(2,1)S(1)}, u32[]{:S(2)}, u32[]{:S(2)}) collective-permute-start(bf16[128,2048]{1,0:T(8,128)(2,1)S(1)} %combine.4), channel_id=1, source_target_pairs={{0,16},{4,20},{8,24},{12,28},{16,0},{20,4},{24,8},{28,12},{1,17},{... | collective-permute-start | bytes 1572872 | tf_op jit(solution)/shard_map/ppermute | solution.py:35
  197.5 7.5 %collective-permute-done.44.refs_2_ = bf16[96,2048]{1,0:T(8,128)(2,1)S(1)} collective-permute-done((bf16[96,2048]{1,0:T(8,128)(2,1)S(1)}, bf16[96,2048]{1,0:T(8,128)(2,1)S(1)}, u32[]{:S(2)}, u32[]{:S(2)}) %collective-permute-start.44) | collective-permute-done | bytes 393248 | tf_op jit(solution)/shard_map/ppermute | solution.py:35
  205.3 5.9 %collective-permute-start.49 = (bf16[96,2048]{1,0:T(8,128)(2,1)S(1)}, bf16[96,2048]{1,0:T(8,128)(2,1)S(1)}, u32[]{:S(2)}, u32[]{:S(2)}) collective-permute-start(bf16[96,2048]{1,0:T(8,128)(2,1)S(1)} %pad_maximum_fusion.10), channel_id=1, source_target_pairs={{0,3},{1,2},{2,1},{3,0},{4,7},{5,6},{6,5},{7,4},{8,11},{9,10},{10,... | collective-permute-start | bytes 1179656 | tf_op jit(solution)/shard_map/ppermute | solution.py:35
  213.9 7.9 %collective-permute-done.45.refs_2_ = bf16[96,2048]{1,0:T(8,128)(2,1)S(1)} collective-permute-done((bf16[96,2048]{1,0:T(8,128)(2,1)S(1)}, bf16[96,2048]{1,0:T(8,128)(2,1)S(1)}, u32[]{:S(2)}, u32[]{:S(2)}) %collective-permute-start.45) | collective-permute-done | bytes 393248 | tf_op jit(solution)/shard_map/ppermute | solution.py:35
  222.9 2.0 collective-permute-start.53
  224.9 4.0 %collective-permute-start.42 = (bf16[96,2048]{1,0:T(8,128)(2,1)S(1)}, bf16[96,2048]{1,0:T(8,128)(2,1)S(1)}, u32[]{:S(2)}, u32[]{:S(2)}) collective-permute-start(bf16[96,2048]{1,0:T(8,128)(2,1)S(1)} %pad_maximum_fusion.1), channel_id=1, source_target_pairs={{0,1},{1,0},{2,3},{3,2},{4,5},{5,4},{6,7},{7,6},{8,9},{9,8},{10,11... | collective-permute-start | bytes 1179656 | tf_op jit(solution)/shard_map/ppermute | solution.py:35
  230.7 9.4 %collective-permute-done.53.refs_1_ = bf16[128,2048]{1,0:T(8,128)(2,1)S(1)} collective-permute-done((bf16[128,2048]{1,0:T(8,128)(2,1)S(1)}, bf16[128,2048]{1,0:T(8,128)(2,1)S(1)}, u32[]{:S(2)}, u32[]{:S(2)}) %collective-permute-start.53) | collective-permute-done | bytes 524320 | tf_op jit(solution)/shard_map/ppermute | solution.py:35
  240.2 5.0 %collective-permute-done.46.refs_2_ = bf16[96,2048]{1,0:T(8,128)(2,1)S(1)} collective-permute-done((bf16[96,2048]{1,0:T(8,128)(2,1)S(1)}, bf16[96,2048]{1,0:T(8,128)(2,1)S(1)}, u32[]{:S(2)}, u32[]{:S(2)}) %collective-permute-start.46) | collective-permute-done | bytes 393248 | tf_op jit(solution)/shard_map/ppermute | solution.py:35
  245.1 1.8 combine.7
  (164 shorter events, 43.8 us)
Async XLA Ops:
  6.5 48.5 %all-gather.2.cloned.1.call-start = ((), (), s32[]{:S(2)}) async-start(), calls=%async_computation | async-start | bytes 2654208 | tf_op jit(solution)/shard_map/all_gather | solution.py:388
  12.5 5.8 %collective-permute-start = (bf16[144,256]{1,0:T(8,128)(2,1)}, bf16[144,256]{1,0:T(8,128)(2,1)S(1)}, u32[]{:S(2)}, u32[]{:S(2)}) collective-permute-start(bf16[144,256]{1,0:T(8,128)(2,1)} %get-tuple-element.66), channel_id=1, source_target_pairs={{0,1},{1,0},{2,3},{3,2},{4,5},{5,4},{6,7},{7,6},{8,9},{9,8},{10,11... | collective-permute-start | bytes 221192 | tf_op jit(solution)/shard_map/ppermute | solution.py:35
  15.5 4.6 %collective-permute-start.1 = (bf16[144,256]{1,0:T(8,128)(2,1)}, bf16[144,256]{1,0:T(8,128)(2,1)S(1)}, u32[]{:S(2)}, u32[]{:S(2)}) collective-permute-start(bf16[144,256]{1,0:T(8,128)(2,1)} %get-tuple-element.67), channel_id=1, source_target_pairs={{0,2},{1,3},{2,0},{3,1},{4,6},{5,7},{6,4},{7,5},{8,10},{9,11},{10,... | collective-permute-start | bytes 221192 | tf_op jit(solution)/shard_map/ppermute | solution.py:35
  17.0 5.5 %collective-permute-start.2 = (bf16[144,256]{1,0:T(8,128)(2,1)}, bf16[144,256]{1,0:T(8,128)(2,1)S(1)}, u32[]{:S(2)}, u32[]{:S(2)}) collective-permute-start(bf16[144,256]{1,0:T(8,128)(2,1)} %get-tuple-element.68), channel_id=1, source_target_pairs={{0,3},{1,2},{2,1},{3,0},{4,7},{5,6},{6,5},{7,4},{8,11},{9,10},{10,... | collective-permute-start | bytes 221192 | tf_op jit(solution)/shard_map/ppermute | solution.py:35
  23.9 14.9 %collective-permute-start.3 = (bf16[128,2048]{1,0:T(8,128)(2,1)S(1)}, bf16[128,2048]{1,0:T(8,128)(2,1)S(1)}, u32[]{:S(2)}, u32[]{:S(2)}) collective-permute-start(bf16[128,2048]{1,0:T(8,128)(2,1)S(1)} %copy-done.6), channel_id=1, source_target_pairs={{0,1},{1,0},{2,3},{3,2},{4,5},{5,4},{6,7},{7,6},{8,9},{9,8},{10,11... | collective-permute-start | bytes 1572872 | tf_op jit(solution)/shard_map/ppermute | solution.py:35
  24.5 23.4 %collective-permute-start.4 = (bf16[128,2048]{1,0:T(8,128)(2,1)S(1)}, bf16[128,2048]{1,0:T(8,128)(2,1)S(1)}, u32[]{:S(2)}, u32[]{:S(2)}) collective-permute-start(bf16[128,2048]{1,0:T(8,128)(2,1)S(1)} %copy-done.6), channel_id=1, source_target_pairs={{0,2},{1,3},{2,0},{3,1},{4,6},{5,7},{6,4},{7,5},{8,10},{9,11},{10,... | collective-permute-start | bytes 1572872 | tf_op jit(solution)/shard_map/ppermute | solution.py:35
  25.0 22.9 %collective-permute-start.5 = (bf16[128,2048]{1,0:T(8,128)(2,1)S(1)}, bf16[128,2048]{1,0:T(8,128)(2,1)S(1)}, u32[]{:S(2)}, u32[]{:S(2)}) collective-permute-start(bf16[128,2048]{1,0:T(8,128)(2,1)S(1)} %copy-done.6), channel_id=1, source_target_pairs={{0,3},{1,2},{2,1},{3,0},{4,7},{5,6},{6,5},{7,4},{8,11},{9,10},{10,... | collective-permute-start | bytes 1572872 | tf_op jit(solution)/shard_map/ppermute | solution.py:35
  58.5 15.9 %collective-permute-start.6 = (bf16[128,2048]{1,0:T(8,128)(2,1)S(1)}, bf16[128,2048]{1,0:T(8,128)(2,1)S(1)}, u32[]{:S(2)}, u32[]{:S(2)}) collective-permute-start(bf16[128,2048]{1,0:T(8,128)(2,1)S(1)} %attention.4), channel_id=1, source_target_pairs={{0,3},{1,2},{2,1},{3,0},{4,7},{5,6},{6,5},{7,4},{8,11},{9,10},{10,... | collective-permute-start | bytes 1572872 | tf_op jit(solution)/shard_map/ppermute | solution.py:35
  62.7 22.9 %collective-permute-start.7 = (bf16[128,2048]{1,0:T(8,128)(2,1)S(1)}, bf16[128,2048]{1,0:T(8,128)(2,1)S(1)}, u32[]{:S(2)}, u32[]{:S(2)}) collective-permute-start(bf16[128,2048]{1,0:T(8,128)(2,1)S(1)} %attention.5), channel_id=1, source_target_pairs={{0,1},{1,0},{2,3},{3,2},{4,5},{5,4},{6,7},{7,6},{8,9},{9,8},{10,11... | collective-permute-start | bytes 1572872 | tf_op jit(solution)/shard_map/ppermute | solution.py:35
  65.2 20.4 %collective-permute-start.8 = (bf16[128,2048]{1,0:T(8,128)(2,1)S(1)}, bf16[128,2048]{1,0:T(8,128)(2,1)S(1)}, u32[]{:S(2)}, u32[]{:S(2)}) collective-permute-start(bf16[128,2048]{1,0:T(8,128)(2,1)S(1)} %attention.6), channel_id=1, source_target_pairs={{0,2},{1,3},{2,0},{3,1},{4,6},{5,7},{6,4},{7,5},{8,10},{9,11},{10,... | collective-permute-start | bytes 1572872 | tf_op jit(solution)/shard_map/ppermute | solution.py:35
  86.1 23.9 %collective-permute-start.15 = (bf16[128,2048]{1,0:T(8,128)(2,1)S(1)}, bf16[128,2048]{1,0:T(8,128)(2,1)S(1)}, u32[]{:S(2)}, u32[]{:S(2)}) collective-permute-start(bf16[128,2048]{1,0:T(8,128)(2,1)S(1)} %get-tuple-element.73), channel_id=1, source_target_pairs={{0,8},{4,12},{8,0},{12,4},{16,24},{20,28},{24,16},{28,20},{1,9},{5... | collective-permute-start | bytes 1572872 | tf_op jit(solution)/shard_map/ppermute | solution.py:35
  88.4 8.1 %collective-permute-start.9 = (bf16[128,1024]{1,0:T(8,128)(2,1)S(1)}, bf16[128,1024]{1,0:T(8,128)(2,1)S(1)}, u32[]{:S(2)}, u32[]{:S(2)}) collective-permute-start(bf16[128,1024]{1,0:T(8,128)(2,1)S(1)} %get-tuple-element.164.refs_0_), channel_id=1, source_target_pairs={{0,1},{1,0},{2,3},{3,2},{4,5},{5,4},{6,7},{7,6},{8,9},{9,8},{10,11... | collective-permute-start | bytes 786440 | tf_op jit(solution)/shard_map/ppermute | solution.py:35
  90.0 7.8 %collective-permute-start.10 = (bf16[128,1024]{1,0:T(8,128)(2,1)S(1)}, bf16[128,1024]{1,0:T(8,128)(2,1)S(1)}, u32[]{:S(2)}, u32[]{:S(2)}) collective-permute-start(bf16[128,1024]{1,0:T(8,128)(2,1)S(1)} %get-tuple-element.163.refs_2_), channel_id=1, source_target_pairs={{0,2},{1,3},{2,0},{3,1},{4,6},{5,7},{6,4},{7,5},{8,10},{9,11},{10,... | collective-permute-start | bytes 786440 | tf_op jit(solution)/shard_map/ppermute | solution.py:35
  91.2 27.2 %collective-permute-start.22 = (bf16[128,2048]{1,0:T(8,128)(2,1)S(1)}, bf16[128,2048]{1,0:T(8,128)(2,1)S(1)}, u32[]{:S(2)}, u32[]{:S(2)}) collective-permute-start(bf16[128,2048]{1,0:T(8,128)(2,1)S(1)} %get-tuple-element.73), channel_id=1, source_target_pairs={{0,16},{4,20},{8,24},{12,28},{16,0},{20,4},{24,8},{28,12},{1,17},{... | collective-permute-start | bytes 1572872 | tf_op jit(solution)/shard_map/ppermute | solution.py:35
  98.9 22.3 %collective-permute-start.11 = (bf16[192,1024]{1,0:T(8,128)(2,1)S(1)}, bf16[192,1024]{1,0:T(8,128)(2,1)S(1)}, u32[]{:S(2)}, u32[]{:S(2)}) collective-permute-start(bf16[192,1024]{1,0:T(8,128)(2,1)S(1)} %get-tuple-element.75), channel_id=1, source_target_pairs={{0,2},{1,3},{2,0},{3,1},{4,6},{5,7},{6,4},{7,5},{8,10},{9,11},{10,... | collective-permute-start | bytes 1179656 | tf_op jit(solution)/shard_map/ppermute | solution.py:35
  100.1 21.4 %collective-permute-start.12 = (bf16[192,1024]{1,0:T(8,128)(2,1)S(1)}, bf16[192,1024]{1,0:T(8,128)(2,1)S(1)}, u32[]{:S(2)}, u32[]{:S(2)}) collective-permute-start(bf16[192,1024]{1,0:T(8,128)(2,1)S(1)} %get-tuple-element.77), channel_id=1, source_target_pairs={{0,1},{1,0},{2,3},{3,2},{4,5},{5,4},{6,7},{7,6},{8,9},{9,8},{10,11... | collective-permute-start | bytes 1179656 | tf_op jit(solution)/shard_map/ppermute | solution.py:35
  110.0 8.5 %collective-permute-start.16 = (bf16[128,1024]{1,0:T(8,128)(2,1)S(1)}, bf16[128,1024]{1,0:T(8,128)(2,1)S(1)}, u32[]{:S(2)}, u32[]{:S(2)}) collective-permute-start(bf16[128,1024]{1,0:T(8,128)(2,1)S(1)} %get-tuple-element.80.refs_0_), channel_id=1, source_target_pairs={{0,1},{1,0},{2,3},{3,2},{4,5},{5,4},{6,7},{7,6},{8,9},{9,8},{10,11... | collective-permute-start | bytes 786440 | tf_op jit(solution)/shard_map/ppermute | solution.py:35
  112.5 7.5 %collective-permute-start.17 = (bf16[128,1024]{1,0:T(8,128)(2,1)S(1)}, bf16[128,1024]{1,0:T(8,128)(2,1)S(1)}, u32[]{:S(2)}, u32[]{:S(2)}) collective-permute-start(bf16[128,1024]{1,0:T(8,128)(2,1)S(1)} %get-tuple-element.81.refs_2_), channel_id=1, source_target_pairs={{0,2},{1,3},{2,0},{3,1},{4,6},{5,7},{6,4},{7,5},{8,10},{9,11},{10,... | collective-permute-start | bytes 786440 | tf_op jit(solution)/shard_map/ppermute | solution.py:35
  120.0 13.7 %collective-permute-start.23 = (bf16[128,2048]{1,0:T(8,128)(2,1)S(1)}, bf16[128,2048]{1,0:T(8,128)(2,1)S(1)}, u32[]{:S(2)}, u32[]{:S(2)}) collective-permute-start(bf16[128,2048]{1,0:T(8,128)(2,1)S(1)} %collective-permute-done.22), channel_id=1, source_target_pairs={{0,8},{4,12},{8,0},{12,4},{16,24},{20,28},{24,16},{28,20},{1,9},{5... | collective-permute-start | bytes 1572872 | tf_op jit(solution)/shard_map/ppermute | solution.py:35
  121.1 9.5 %collective-permute-start.18 = (bf16[192,1024]{1,0:T(8,128)(2,1)S(1)}, bf16[192,1024]{1,0:T(8,128)(2,1)S(1)}, u32[]{:S(2)}, u32[]{:S(2)}) collective-permute-start(bf16[192,1024]{1,0:T(8,128)(2,1)S(1)} %get-tuple-element.84), channel_id=1, source_target_pairs={{0,2},{1,3},{2,0},{3,1},{4,6},{5,7},{6,4},{7,5},{8,10},{9,11},{10,... | collective-permute-start | bytes 1179656 | tf_op jit(solution)/shard_map/ppermute | solution.py:35
  121.5 12.1 %collective-permute-start.19 = (bf16[192,1024]{1,0:T(8,128)(2,1)S(1)}, bf16[192,1024]{1,0:T(8,128)(2,1)S(1)}, u32[]{:S(2)}, u32[]{:S(2)}) collective-permute-start(bf16[192,1024]{1,0:T(8,128)(2,1)S(1)} %get-tuple-element.87), channel_id=1, source_target_pairs={{0,1},{1,0},{2,3},{3,2},{4,5},{5,4},{6,7},{7,6},{8,9},{9,8},{10,11... | collective-permute-start | bytes 1179656 | tf_op jit(solution)/shard_map/ppermute | solution.py:35
  121.9 19.2 %collective-permute-start.13 = (bf16[384,1024]{1,0:T(8,128)(2,1)S(1)}, bf16[384,1024]{1,0:T(8,128)(2,1)S(1)}, u32[]{:S(2)}, u32[]{:S(2)}) collective-permute-start(bf16[384,1024]{1,0:T(8,128)(2,1)S(1)} %halves.4), channel_id=1, source_target_pairs={{0,4},{4,0},{8,12},{12,8},{16,20},{20,16},{24,28},{28,24},{1,5},{5... | collective-permute-start | bytes 2359304 | tf_op jit(solution)/shard_map/ppermute | solution.py:35
  122.1 14.6 %collective-permute-start.24 = (bf16[128,1024]{1,0:T(8,128)(2,1)S(1)}, bf16[128,1024]{1,0:T(8,128)(2,1)S(1)}, u32[]{:S(2)}, u32[]{:S(2)}) collective-permute-start(bf16[128,1024]{1,0:T(8,128)(2,1)S(1)} %get-tuple-element.91.refs_0_), channel_id=1, source_target_pairs={{0,1},{1,0},{2,3},{3,2},{4,5},{5,4},{6,7},{7,6},{8,9},{9,8},{10,11... | collective-permute-start | bytes 786440 | tf_op jit(solution)/shard_map/ppermute | solution.py:35
  130.6 6.6 %collective-permute-start.26 = (bf16[128,1024]{1,0:T(8,128)(2,1)S(1)}, bf16[128,1024]{1,0:T(8,128)(2,1)S(1)}, u32[]{:S(2)}, u32[]{:S(2)}) collective-permute-start(bf16[128,1024]{1,0:T(8,128)(2,1)S(1)} %get-tuple-element.93.refs_2_), channel_id=1, source_target_pairs={{0,2},{1,3},{2,0},{3,1},{4,6},{5,7},{6,4},{7,5},{8,10},{9,11},{10,... | collective-permute-start | bytes 786440 | tf_op jit(solution)/shard_map/ppermute | solution.py:35
  133.6 23.1 %collective-permute-start.20 = (bf16[384,1024]{1,0:T(8,128)(2,1)S(1)}, bf16[384,1024]{1,0:T(8,128)(2,1)S(1)}, u32[]{:S(2)}, u32[]{:S(2)}) collective-permute-start(bf16[384,1024]{1,0:T(8,128)(2,1)S(1)} %halves.5), channel_id=1, source_target_pairs={{0,4},{4,0},{8,12},{12,8},{16,20},{20,16},{24,28},{28,24},{1,5},{5... | collective-permute-start | bytes 2359304 | tf_op jit(solution)/shard_map/ppermute | solution.py:35
  136.7 9.2 %collective-permute-start.25 = (bf16[128,1024]{1,0:T(8,128)(2,1)S(1)}, bf16[128,1024]{1,0:T(8,128)(2,1)S(1)}, u32[]{:S(2)}, u32[]{:S(2)}) collective-permute-start(bf16[128,1024]{1,0:T(8,128)(2,1)S(1)} %get-tuple-element.92.refs_0_), channel_id=1, source_target_pairs={{0,1},{1,0},{2,3},{3,2},{4,5},{5,4},{6,7},{7,6},{8,9},{9,8},{10,11... | collective-permute-start | bytes 786440 | tf_op jit(solution)/shard_map/ppermute | solution.py:35
  138.3 15.3 %collective-permute-start.28 = (bf16[192,1024]{1,0:T(8,128)(2,1)S(1)}, bf16[192,1024]{1,0:T(8,128)(2,1)S(1)}, u32[]{:S(2)}, u32[]{:S(2)}) collective-permute-start(bf16[192,1024]{1,0:T(8,128)(2,1)S(1)} %get-tuple-element.98), channel_id=1, source_target_pairs={{0,2},{1,3},{2,0},{3,1},{4,6},{5,7},{6,4},{7,5},{8,10},{9,11},{10,... | collective-permute-start | bytes 1179656 | tf_op jit(solution)/shard_map/ppermute | solution.py:35
  139.8 15.3 %collective-permute-start.30 = (bf16[192,1024]{1,0:T(8,128)(2,1)S(1)}, bf16[192,1024]{1,0:T(8,128)(2,1)S(1)}, u32[]{:S(2)}, u32[]{:S(2)}) collective-permute-start(bf16[192,1024]{1,0:T(8,128)(2,1)S(1)} %get-tuple-element.103), channel_id=1, source_target_pairs={{0,1},{1,0},{2,3},{3,2},{4,5},{5,4},{6,7},{7,6},{8,9},{9,8},{10,11... | collective-permute-start | bytes 1179656 | tf_op jit(solution)/shard_map/ppermute | solution.py:35
  141.2 11.4 %collective-permute-start.27 = (bf16[128,1024]{1,0:T(8,128)(2,1)S(1)}, bf16[128,1024]{1,0:T(8,128)(2,1)S(1)}, u32[]{:S(2)}, u32[]{:S(2)}) collective-permute-start(bf16[128,1024]{1,0:T(8,128)(2,1)S(1)} %get-tuple-element.94.refs_2_), channel_id=1, source_target_pairs={{0,2},{1,3},{2,0},{3,1},{4,6},{5,7},{6,4},{7,5},{8,10},{9,11},{10,... | collective-permute-start | bytes 786440 | tf_op jit(solution)/shard_map/ppermute | solution.py:35
  145.9 14.8 %collective-permute-start.14 = (bf16[192,2048]{1,0:T(8,128)(2,1)S(1)}, bf16[192,2048]{1,0:T(8,128)(2,1)S(1)}, u32[]{:S(2)}, u32[]{:S(2)}) collective-permute-start(bf16[192,2048]{1,0:T(8,128)(2,1)S(1)} %get-tuple-element.79), channel_id=1, source_target_pairs={{0,4},{4,0},{8,12},{12,8},{16,20},{20,16},{24,28},{28,24},{1,5},{5... | collective-permute-start | bytes 2359304 | tf_op jit(solution)/shard_map/ppermute | solution.py:35
  153.7 12.5 %collective-permute-start.29 = (bf16[192,1024]{1,0:T(8,128)(2,1)S(1)}, bf16[192,1024]{1,0:T(8,128)(2,1)S(1)}, u32[]{:S(2)}, u32[]{:S(2)}) collective-permute-start(bf16[192,1024]{1,0:T(8,128)(2,1)S(1)} %get-tuple-element.99), channel_id=1, source_target_pairs={{0,2},{1,3},{2,0},{3,1},{4,6},{5,7},{6,4},{7,5},{8,10},{9,11},{10,... | collective-permute-start | bytes 1179656 | tf_op jit(solution)/shard_map/ppermute | solution.py:35
  155.1 11.2 %collective-permute-start.31 = (bf16[192,1024]{1,0:T(8,128)(2,1)S(1)}, bf16[192,1024]{1,0:T(8,128)(2,1)S(1)}, u32[]{:S(2)}, u32[]{:S(2)}) collective-permute-start(bf16[192,1024]{1,0:T(8,128)(2,1)S(1)} %get-tuple-element.104), channel_id=1, source_target_pairs={{0,1},{1,0},{2,3},{3,2},{4,5},{5,4},{6,7},{7,6},{8,9},{9,8},{10,11... | collective-permute-start | bytes 1179656 | tf_op jit(solution)/shard_map/ppermute | solution.py:35
  166.3 9.5 %collective-permute-start.21 = (bf16[192,2048]{1,0:T(8,128)(2,1)S(1)}, bf16[192,2048]{1,0:T(8,128)(2,1)S(1)}, u32[]{:S(2)}, u32[]{:S(2)}) collective-permute-start(bf16[192,2048]{1,0:T(8,128)(2,1)S(1)} %get-tuple-element.89), channel_id=1, source_target_pairs={{0,4},{4,0},{8,12},{12,8},{16,20},{20,16},{24,28},{28,24},{1,5},{5... | collective-permute-start | bytes 2359304 | tf_op jit(solution)/shard_map/ppermute | solution.py:35
  168.1 12.0 %collective-permute-start.39 = (bf16[96,2048]{1,0:T(8,128)(2,1)S(1)}, bf16[96,2048]{1,0:T(8,128)(2,1)S(1)}, u32[]{:S(2)}, u32[]{:S(2)}) collective-permute-start(bf16[96,2048]{1,0:T(8,128)(2,1)S(1)} %pad_maximum_fusion.4), channel_id=1, source_target_pairs={{0,1},{1,0},{2,3},{3,2},{4,5},{5,4},{6,7},{7,6},{8,9},{9,8},{10,11... | collective-permute-start | bytes 1179656 | tf_op jit(solution)/shard_map/ppermute | solution.py:35
  168.6 19.6 %collective-permute-start.43 = (bf16[96,2048]{1,0:T(8,128)(2,1)S(1)}, bf16[96,2048]{1,0:T(8,128)(2,1)S(1)}, u32[]{:S(2)}, u32[]{:S(2)}) collective-permute-start(bf16[96,2048]{1,0:T(8,128)(2,1)S(1)} %pad_maximum_fusion.8), channel_id=1, source_target_pairs={{0,2},{1,3},{2,0},{3,1},{4,6},{5,7},{6,4},{7,5},{8,10},{9,11},{10,... | collective-permute-start | bytes 1179656 | tf_op jit(solution)/shard_map/ppermute | solution.py:35
  169.4 19.0 %collective-permute-start.47 = (bf16[96,2048]{1,0:T(8,128)(2,1)S(1)}, bf16[96,2048]{1,0:T(8,128)(2,1)S(1)}, u32[]{:S(2)}, u32[]{:S(2)}) collective-permute-start(bf16[96,2048]{1,0:T(8,128)(2,1)S(1)} %pad_maximum_fusion.12), channel_id=1, source_target_pairs={{0,3},{1,2},{2,1},{3,0},{4,7},{5,6},{6,5},{7,4},{8,11},{9,10},{10,... | collective-permute-start | bytes 1179656 | tf_op jit(solution)/shard_map/ppermute | solution.py:35
  180.1 16.9 %collective-permute-start.40 = (bf16[96,2048]{1,0:T(8,128)(2,1)S(1)}, bf16[96,2048]{1,0:T(8,128)(2,1)S(1)}, u32[]{:S(2)}, u32[]{:S(2)}) collective-permute-start(bf16[96,2048]{1,0:T(8,128)(2,1)S(1)} %pad_maximum_fusion.3), channel_id=1, source_target_pairs={{0,1},{1,0},{2,3},{3,2},{4,5},{5,4},{6,7},{7,6},{8,9},{9,8},{10,11... | collective-permute-start | bytes 1179656 | tf_op jit(solution)/shard_map/ppermute | solution.py:35
  188.2 16.7 %collective-permute-start.44 = (bf16[96,2048]{1,0:T(8,128)(2,1)S(1)}, bf16[96,2048]{1,0:T(8,128)(2,1)S(1)}, u32[]{:S(2)}, u32[]{:S(2)}) collective-permute-start(bf16[96,2048]{1,0:T(8,128)(2,1)S(1)} %pad_maximum_fusion.7), channel_id=1, source_target_pairs={{0,2},{1,3},{2,0},{3,1},{4,6},{5,7},{6,4},{7,5},{8,10},{9,11},{10,... | collective-permute-start | bytes 1179656 | tf_op jit(solution)/shard_map/ppermute | solution.py:35
  188.5 16.9 %collective-permute-start.48 = (bf16[96,2048]{1,0:T(8,128)(2,1)S(1)}, bf16[96,2048]{1,0:T(8,128)(2,1)S(1)}, u32[]{:S(2)}, u32[]{:S(2)}) collective-permute-start(bf16[96,2048]{1,0:T(8,128)(2,1)S(1)} %pad_maximum_fusion.11), channel_id=1, source_target_pairs={{0,3},{1,2},{2,1},{3,0},{4,7},{5,6},{6,5},{7,4},{8,11},{9,10},{10,... | collective-permute-start | bytes 1179656 | tf_op jit(solution)/shard_map/ppermute | solution.py:35
  192.3 36.9 %collective-permute-start.51 = (bf16[128,2048]{1,0:T(8,128)(2,1)S(1)}, bf16[128,2048]{1,0:T(8,128)(2,1)S(1)}, u32[]{:S(2)}, u32[]{:S(2)}) collective-permute-start(bf16[128,2048]{1,0:T(8,128)(2,1)S(1)} %combine.4), channel_id=1, source_target_pairs={{0,16},{4,20},{8,24},{12,28},{16,0},{20,4},{24,8},{28,12},{1,17},{... | collective-permute-start | bytes 1572872 | tf_op jit(solution)/shard_map/ppermute | solution.py:35
  197.0 16.9 %collective-permute-start.41 = (bf16[96,2048]{1,0:T(8,128)(2,1)S(1)}, bf16[96,2048]{1,0:T(8,128)(2,1)S(1)}, u32[]{:S(2)}, u32[]{:S(2)}) collective-permute-start(bf16[96,2048]{1,0:T(8,128)(2,1)S(1)} %pad_maximum_fusion.2), channel_id=1, source_target_pairs={{0,1},{1,0},{2,3},{3,2},{4,5},{5,4},{6,7},{7,6},{8,9},{9,8},{10,11... | collective-permute-start | bytes 1179656 | tf_op jit(solution)/shard_map/ppermute | solution.py:35
  204.9 16.9 %collective-permute-start.45 = (bf16[96,2048]{1,0:T(8,128)(2,1)S(1)}, bf16[96,2048]{1,0:T(8,128)(2,1)S(1)}, u32[]{:S(2)}, u32[]{:S(2)}) collective-permute-start(bf16[96,2048]{1,0:T(8,128)(2,1)S(1)} %pad_maximum_fusion.6), channel_id=1, source_target_pairs={{0,2},{1,3},{2,0},{3,1},{4,6},{5,7},{6,4},{7,5},{8,10},{9,11},{10,... | collective-permute-start | bytes 1179656 | tf_op jit(solution)/shard_map/ppermute | solution.py:35
  205.3 16.5 %collective-permute-start.49 = (bf16[96,2048]{1,0:T(8,128)(2,1)S(1)}, bf16[96,2048]{1,0:T(8,128)(2,1)S(1)}, u32[]{:S(2)}, u32[]{:S(2)}) collective-permute-start(bf16[96,2048]{1,0:T(8,128)(2,1)S(1)} %pad_maximum_fusion.10), channel_id=1, source_target_pairs={{0,3},{1,2},{2,1},{3,0},{4,7},{5,6},{6,5},{7,4},{8,11},{9,10},{10,... | collective-permute-start | bytes 1179656 | tf_op jit(solution)/shard_map/ppermute | solution.py:35
  212.4 18.2 %collective-permute-start.52 = (bf16[128,2048]{1,0:T(8,128)(2,1)S(1)}, bf16[128,2048]{1,0:T(8,128)(2,1)S(1)}, u32[]{:S(2)}, u32[]{:S(2)}) collective-permute-start(bf16[128,2048]{1,0:T(8,128)(2,1)S(1)} %combine.5), channel_id=1, source_target_pairs={{0,24},{4,28},{8,16},{12,20},{16,8},{20,12},{24,0},{28,4},{1,25},{... | collective-permute-start | bytes 1572872 | tf_op jit(solution)/shard_map/ppermute | solution.py:35
  222.9 17.2 %collective-permute-start.53 = (bf16[128,2048]{1,0:T(8,128)(2,1)S(1)}, bf16[128,2048]{1,0:T(8,128)(2,1)S(1)}, u32[]{:S(2)}, u32[]{:S(2)}) collective-permute-start(bf16[128,2048]{1,0:T(8,128)(2,1)S(1)} %combine.6), channel_id=1, source_target_pairs={{0,8},{4,12},{8,0},{12,4},{16,24},{20,28},{24,16},{28,20},{1,9},{5... | collective-permute-start | bytes 1572872 | tf_op jit(solution)/shard_map/ppermute | solution.py:35
  224.9 15.2 %collective-permute-start.42 = (bf16[96,2048]{1,0:T(8,128)(2,1)S(1)}, bf16[96,2048]{1,0:T(8,128)(2,1)S(1)}, u32[]{:S(2)}, u32[]{:S(2)}) collective-permute-start(bf16[96,2048]{1,0:T(8,128)(2,1)S(1)} %pad_maximum_fusion.1), channel_id=1, source_target_pairs={{0,1},{1,0},{2,3},{3,2},{4,5},{5,4},{6,7},{7,6},{8,9},{9,8},{10,11... | collective-permute-start | bytes 1179656 | tf_op jit(solution)/shard_map/ppermute | solution.py:35
  228.9 16.2 %collective-permute-start.46 = (bf16[96,2048]{1,0:T(8,128)(2,1)S(1)}, bf16[96,2048]{1,0:T(8,128)(2,1)S(1)}, u32[]{:S(2)}, u32[]{:S(2)}) collective-permute-start(bf16[96,2048]{1,0:T(8,128)(2,1)S(1)} %pad_maximum_fusion.5), channel_id=1, source_target_pairs={{0,2},{1,3},{2,0},{3,1},{4,6},{5,7},{6,4},{7,5},{8,10},{9,11},{10,... | collective-permute-start | bytes 1179656 | tf_op jit(solution)/shard_map/ppermute | solution.py:35
  229.2 15.9 %collective-permute-start.50 = (bf16[96,2048]{1,0:T(8,128)(2,1)S(1)}, bf16[96,2048]{1,0:T(8,128)(2,1)S(1)}, u32[]{:S(2)}, u32[]{:S(2)}) collective-permute-start(bf16[96,2048]{1,0:T(8,128)(2,1)S(1)} %pad_maximum_fusion.9), channel_id=1, source_target_pairs={{0,3},{1,2},{2,1},{3,0},{4,7},{5,6},{6,5},{7,4},{8,11},{9,10},{10,... | collective-permute-start | bytes 1179656 | tf_op jit(solution)/shard_map/ppermute | solution.py:35
  (20 other events, 208.5 us)
Sparse Core Ops, SparseCore 0:
  24.0 30.9 all-gather.1
